TPU v7x, 32 devices: a whole 2x2x4 slice. The times are simulated.
32 devices in a mesh: member: 4 (over z), band: 8 (over y, x, core).
Axes of the slice: x: 2, y: 2, z: 4, core: 2. Of those that a mesh axis runs over, the one named last changes fastest.
Arguments:
- hidden: bfloat16 [8, 512, 1024], P('member', 'band'), may hold values from -6 to 6
- queries: bfloat16 [2048, 1024], P('band'), may hold values from -6 to 6
- kv_weight: bfloat16 [1024, 2048], replicated, may hold values from -0.1875 to 0.1875
- out_weight: bfloat16 [1024, 1024], replicated, may hold values from -0.1875 to 0.1875
- head_projection: bfloat16 [1024, 100], replicated, may hold values from -0.1875 to 0.1875
- initial_state: float32 [100, 2048], P(None, 'band'), may hold values from -6 to 6
- truth: float32 [100, 2048], P(None, 'band'), may hold values from -8 to 8
- latitude_weight: float32 [2048], P('band'), may hold values from 0.1 to 2
- channel_loss_weight: float32 [100], replicated, may hold values from 0.3 to 3
- sources: int32 [3, 2048], P(None, 'band'), may hold values from 0 to 127, as said below
- halo_rows: int32 [16, 32], P('band'), may hold values from 0 to 63, as said below
Outputs:
- hidden_grad: float32 [8, 512, 1024], P('member', 'band')
- kv_grad: float32 [1024, 2048], P(('member', 'band'))
- out_grad: float32 [1024, 1024], P(('member', 'band'))
- head_grad: float32 [1024, 100], P(('member', 'band'))
Inputs may be any that keep to these rules, and one draw needn't show every extreme that they name: sources[e, t] names a row of the extended list of point t's band: rows below 64 are the band's own nodes, the next 32 those received from the band below, the last 32 those from the band above; the 3 rows of one point are distinct; the first band names no row from below and the last band none from above. `halo_rows`: rows 2 b and 2 b + 1 list the nodes of band b sent to the band below and to the band above; each node of a band stands once in the two rows together.
All inputs are finite; a program needn't handle non-finite values.
Results may differ from a plain program's by a relative error of at most 0.019.
Values may be sent and summed in bfloat16 or wider, within the bound.
No kernel may reach another device: no remote copies, remote signals or barrier semaphores. Data moves between devices by JAX's collectives and lax.ppermute only.
A program may use at most 128 MiB of HBM per device.

v0:
```python
import jax
import jax.numpy as jnp
from jax import lax
from jax.sharding import PartitionSpec as P

HEAD_DIM = 64


ALPHA = 0.95
SOFTENING = 0.5


def padded(cells, sides, width):
    for axis, dim in sides:
        count = lax.axis_size(axis)
        ends = count - 1
        head = lax.slice_in_dim(cells, 0, width, axis=dim)
        tail = lax.slice_in_dim(cells, cells.shape[dim] - width, cells.shape[dim], axis=dim)
        cells = jnp.concatenate(
            [
                lax.ppermute(tail, axis, [(i, (i + 1) % count) for i in range(ends)]),
                cells,
                lax.ppermute(head, axis, [((i + 1) % count, i) for i in range(ends)]),
            ],
            axis=dim,
        )
    return cells


def ensemble_terms(local_rows, whole_ensemble, truth_part, lat_part, channel_loss_weight):
    members = whole_ensemble.shape[0]
    score_weight = channel_loss_weight[:, None] * lat_part[None, :]
    spread = (1.0 - (1.0 - ALPHA) / members) / (members * (members - 1))
    member_differences = local_rows[:, None] - whole_ensemble[None]
    gap_root = jnp.sqrt(member_differences * member_differences + SOFTENING * SOFTENING)
    slope_sum = jnp.sum(member_differences / gap_root, axis=1)
    truth_gap = local_rows - truth_part[None]
    truth_root = jnp.sqrt(truth_gap * truth_gap + SOFTENING * SOFTENING)
    return score_weight[None] * (truth_gap / truth_root / members - spread * slope_sum)


def shards(
    hidden,
    queries,
    kv_weight,
    out_weight,
    head_projection,
    initial_state,
    truth,
    latitude_weight,
    channel_loss_weight,
    sources,
    halo_rows,
):
    mem_count, node_count, model_width = hidden.shape
    grid_count = queries.shape[0]
    edge_count = sources.shape[0]
    head_count = model_width // HEAD_DIM
    score_scale = HEAD_DIM ** (-0.5)
    rim_size = halo_rows.shape[1]
    picked = jnp.stack([hidden[:, halo_rows[0]], hidden[:, halo_rows[1]]], axis=0)
    rim_rows = padded(picked, (("band", 0),), 1)
    extended_nodes = jnp.concatenate([hidden, rim_rows[0], rim_rows[3]], axis=1)
    ext_count = extended_nodes.shape[1]
    flat_ext = extended_nodes.reshape(mem_count * ext_count, model_width)
    key_value = jnp.dot(flat_ext, kv_weight, preferred_element_type=jnp.float32).astype(
        jnp.bfloat16
    )
    key_value = key_value.reshape(mem_count, ext_count, 2 * model_width)
    query_heads = queries.reshape(grid_count, head_count, HEAD_DIM)
    stored = []
    predictions = []
    for ensemble_member in range(mem_count):
        edge_rows = key_value[ensemble_member][sources]
        edge_keys = edge_rows[..., :model_width].reshape(
            edge_count, grid_count, head_count, HEAD_DIM
        )
        edge_messages = edge_rows[..., model_width:].reshape(
            edge_count, grid_count, head_count, HEAD_DIM
        )
        scores = (
            jnp.einsum("kthd,thd->kth", edge_keys, query_heads, preferred_element_type=jnp.float32)
            * score_scale
        )
        gate_activations = jax.nn.sigmoid(scores)
        gate_lowprecision = gate_activations.astype(jnp.bfloat16)
        combined_nodes = jnp.einsum(
            "kth,kthd->thd", gate_lowprecision, edge_messages, preferred_element_type=jnp.float32
        )
        combined_nodes = combined_nodes.reshape(grid_count, model_width).astype(jnp.bfloat16)
        updated = queries.astype(jnp.float32) + jnp.dot(
            combined_nodes, out_weight, preferred_element_type=jnp.float32
        )
        updated_lowprecision = updated.astype(jnp.bfloat16)
        prediction = initial_state + lax.dot_general(
            head_projection,
            updated_lowprecision,
            (((0,), (1,)), ((), ())),
            preferred_element_type=jnp.float32,
        )
        predictions.append(prediction)
        stored.append(
            (
                edge_messages,
                gate_activations,
                gate_lowprecision,
                combined_nodes,
                updated_lowprecision,
            )
        )
    local_prediction = jnp.stack(predictions, axis=0)
    whole_ensemble = lax.all_gather(local_prediction, "member", axis=0, tiled=True)
    loss_grad = ensemble_terms(
        local_prediction, whole_ensemble, truth, latitude_weight, channel_loss_weight
    )
    grad_rounded = loss_grad.astype(jnp.bfloat16)
    head_sum = jnp.zeros((model_width, head_projection.shape[1]), jnp.float32)
    out_sum = jnp.zeros((model_width, model_width), jnp.float32)
    node_grads = []
    for ensemble_member in range(mem_count):
        edge_messages, gate_activations, gate_lowprecision, combined_nodes, updated_lowprecision = (
            stored[ensemble_member]
        )
        member_grad = grad_rounded[ensemble_member]
        head_sum = head_sum + lax.dot_general(
            updated_lowprecision,
            member_grad,
            (((0,), (1,)), ((), ())),
            preferred_element_type=jnp.float32,
        )
        update_grad = lax.dot_general(
            member_grad,
            head_projection,
            (((0,), (1,)), ((), ())),
            preferred_element_type=jnp.float32,
        ).astype(jnp.bfloat16)
        out_sum = out_sum + lax.dot_general(
            combined_nodes,
            update_grad,
            (((0,), (0,)), ((), ())),
            preferred_element_type=jnp.float32,
        )
        merged_grad = lax.dot_general(
            update_grad, out_weight, (((1,), (1,)), ((), ())), preferred_element_type=jnp.float32
        ).astype(jnp.bfloat16)
        merged_grad = merged_grad.reshape(grid_count, head_count, HEAD_DIM)
        gate_grad = jnp.einsum(
            "thd,kthd->kth", merged_grad, edge_messages, preferred_element_type=jnp.float32
        )
        score_grad = gate_grad * gate_activations * (1.0 - gate_activations) * score_scale
        value_grad = (
            gate_lowprecision.astype(jnp.float32)[..., None] * merged_grad.astype(jnp.float32)[None]
        )
        key_grad = score_grad[..., None] * query_heads.astype(jnp.float32)[None]
        edge_grad = jnp.concatenate(
            [
                key_grad.reshape(edge_count, grid_count, model_width),
                value_grad.reshape(edge_count, grid_count, model_width),
            ],
            axis=-1,
        )
        node_sum = jax.ops.segment_sum(
            edge_grad.reshape(edge_count * grid_count, 2 * model_width),
            sources.reshape(-1),
            num_segments=ext_count,
        )
        node_grads.append(node_sum.astype(jnp.bfloat16))
    flat_node = jnp.stack(node_grads, axis=0).reshape(mem_count * ext_count, 2 * model_width)
    extended_grad = lax.dot_general(
        flat_node, kv_weight, (((1,), (1,)), ((), ())), preferred_element_type=jnp.float32
    )
    extended_grad = extended_grad.reshape(mem_count, ext_count, model_width)
    back_rows = jnp.stack(
        [
            extended_grad[:, node_count : node_count + rim_size],
            extended_grad[:, node_count + rim_size :],
        ],
        axis=0,
    )
    returned = padded(back_rows.astype(jnp.bfloat16), (("band", 0),), 1).astype(back_rows.dtype)
    hidden_grad = (
        extended_grad[:, :node_count]
        .at[:, halo_rows[0]]
        .add(returned[0])
        .at[:, halo_rows[1]]
        .add(returned[3])
    )
    devices = lax.axis_size("member") * lax.axis_size("band")
    kv_total = lax.psum_scatter(
        lax.dot_general(
            flat_ext, flat_node, (((0,), (0,)), ((), ())), preferred_element_type=jnp.float32
        ),
        ("member", "band"),
        scatter_dimension=0,
        tiled=True,
    )
    out_total, head_total = (
        lax.psum_scatter(out_sum, ("member", "band"), scatter_dimension=0, tiled=True),
        lax.psum_scatter(head_sum, ("member", "band"), scatter_dimension=0, tiled=True),
    )
    return (hidden_grad, kv_total / devices, out_total / devices, head_total / devices)


def solution(mesh):
    placed = (
        P("member", "band", None),
        P("band", None),
        P(),
        P(),
        P(),
        P(None, "band"),
        P(None, "band"),
        P("band"),
        P(),
        P(None, "band"),
        P("band", None),
    )
    return jax.shard_map(
        shards,
        mesh=mesh,
        in_specs=placed,
        out_specs=(
            P("member", "band", None),
            P(("member", "band"), None),
            P(("member", "band"), None),
            P(("member", "band"), None),
        ),
        check_vma=False,
    )
```

profile of v0, /device:TPU:0, one launch (start us, length us, event | category | flops | bytes accessed | tf_op | source)
XLA Modules:
  0.0 524.2 jit_solution(7752691691131780779)
XLA Ops:
  8.2 2.0 gather_fusion
  11.2 3.2 collective-permute-start
  14.3 1.9 gather_fusion.1
  20.3 2.4 collective-permute-done.1
  22.7 1.7 pad_maximum_fusion.3
  25.2 3.4 convolution_convert_fusion
  28.7 4.3 gather_fusion.2
  33.1 4.1 fusion.40
  37.2 2.6 copy.121
  39.8 4.3 gather_fusion.3
  44.1 4.2 fusion.41
  48.3 2.7 copy.122
  51.0 3.0 multiply_reduce_fusion.5
  54.0 2.6 copy.120
  56.7 2.7 copy.123
  59.4 1.9 multiply_reduce_fusion.4
  63.9 19.8 %all_gather.3 = f32[8,100,256]{2,1,0:T(8,128)S(1)} all-gather(f32[2,100,256]{2,1,0:T(8,128)S(1)} %pad_maximum_fusion.4), channel_id=1, replica_groups=mesh['member'=4,'band'=8] {'member'}, dimensions={0}, use_global_device_ids=true | all-gather | bytes 1024000 | tf_op jit(solution)/shard_map/all_gather | solution.py:112
  88.6 1.8 fusion.46
  90.5 2.7 convolution_add_fusion
  94.4 1.9 fusion.44
  97.7 1.9 multiply_reduce_fusion.1
  100.3 2.4 copy.132
  102.7 3.8 copy.70
  107.1 2.4 copy.131
  109.5 3.6 copy.69
  113.1 1.7 fusion.43
  115.2 1.9 multiply_reduce_fusion
  117.8 2.5 copy.133
  120.2 3.5 copy.72
  124.3 2.5 copy.134
  126.8 3.7 copy.73
  130.4 4.4 bitcast_multiply_fusion.3
  134.9 2.1 bitcast_multiply_fusion.2
  139.1 3.5 bitcast_multiply_fusion.1
  142.6 16.3 %scatter_custom_fusion = f32[128,2048]{1,0:T(8,128)S(1)} fusion(s32[768]{0:T(1024)S(1)} %reshape.219, f32[768,1024]{1,0:T(8,128)} %bitcast_multiply_fusion.3, f32[]{:T(128)} %constant.38, f32[768,1024]{1,0:T(8,128)} %get-tuple-element.26, f32[]{:T(128)} %constant.9.clone.1), kind=kCustom, calls=%fused_computation.8 | custom fusion | flops 3145728 | bytes 7340040 | tf_op jit(solution)/shard_map/scatter-add | solution.py:162
  158.9 16.7 %scatter_custom_fusion.1 = f32[128,2048]{1,0:T(8,128)} fusion(s32[768]{0:T(1024)S(1)} %reshape.219, f32[768,1024]{1,0:T(8,128)} %bitcast_multiply_fusion.2, f32[]{:T(128)} %constant.38, f32[768,1024]{1,0:T(8,128)} %get-tuple-element.27, f32[]{:T(128)} %constant.9.clone.1), kind=kCustom, calls=%fused_computation.12 | custom fusion | flops 3145728 | bytes 7340040 | tf_op jit(solution)/shard_map/scatter-add | solution.py:162
  175.7 1.5 convert_bitcast_fusion
  177.2 4.6 convolution_bitcast_fusion
  182.9 3.5 fusion.45
  186.4 6.1 %collective-permute-start.2 = (bf16[1,2,32,1024]{3,2,1,0:T(8,128)(2,1)S(1)}, bf16[1,2,32,1024]{3,2,1,0:T(8,128)(2,1)S(1)}, u32[]{:S(2)}, u32[]{:S(2)}) collective-permute-start(bf16[1,2,32,1024]{3,2,1,0:T(8,128)(2,1)S(1)} %get-tuple-element.32), channel_id=1, source_target_pairs={{0,1},{1,2},{2,3},{3,4},{4,5},{5,6},{6,7},{8,9},{9,10},{10,11},{11... | collective-permute-start | bytes 393224 | tf_op jit(solution)/shard_map/ppermute | solution.py:21
  194.3 3.6 collective-permute-done.3
  198.3 2.0 scatter_fusion
  200.3 2.0 scatter_fusion.1
  203.3 26.1 %reduce-scatter.8.cloned.1.call-done = f32[32,100]{1,0:T(8,128)} async-done(((f32[1024,100]{1,0:T(8,128)}), f32[32,100]{1,0:T(8,128)}) %reduce-scatter.8.cloned.1.call-update) | async-done | bytes 12816 | tf_op jit(solution)/shard_map/reduce_scatter | solution.py:199
  230.7 138.1 %reduce-scatter.6.cloned.1.call-done = f32[32,1024]{1,0:T(8,128)} async-done(((f32[1024,1024]{1,0:T(8,128)}), f32[32,1024]{1,0:T(8,128)}) %reduce-scatter.6.cloned.1.call-update) | async-done | bytes 131088 | tf_op jit(solution)/shard_map/reduce_scatter | solution.py:198
  368.8 1.6 broadcast_multiply_fusion.1
  370.3 145.4 %reduce-scatter.4.cloned.1.call-done = f32[32,2048]{1,0:T(8,128)} async-done(((f32[1024,2048]{1,0:T(8,128)}), f32[32,2048]{1,0:T(8,128)}) %reduce-scatter.4.cloned.1.call-update) | async-done | bytes 262160 | tf_op jit(solution)/shard_map/reduce_scatter | solution.py:189
  515.8 1.7 broadcast_multiply_fusion
  (115 shorter events, 27.2 us)
Async XLA Ops:
  7.2 54.1 %copy-start = (bf16[1024,1024]{1,0:T(8,128)(2,1)S(1)}, bf16[1024,1024]{1,0:T(8,128)(2,1)}, u32[]{:S(2)}) copy-start(bf16[1024,1024]{1,0:T(8,128)(2,1)} %param.14) | copy-start | bytes 6291460
  7.2 11.4 %copy-start.6 = (bf16[256,1024]{1,0:T(8,128)(2,1)S(1)}, bf16[256,1024]{1,0:T(8,128)(2,1)}, u32[]{:S(2)}) copy-start(bf16[256,1024]{1,0:T(8,128)(2,1)} %param.12) | copy-start | bytes 1572868
  7.2 222.2 %reduce-scatter.8.cloned.1.call-start = ((), (), s32[]{:S(2)}) async-start(), calls=%async_computation.5 | async-start | bytes 540672 | tf_op jit(solution)/shard_map/reduce_scatter | solution.py:199
  8.1 11.7 %copy-start.25 = (f32[256]{0:T(256)S(1)}, f32[256]{0:T(256)}, u32[]{:S(2)}) copy-start(f32[256]{0:T(256)} %param.18) | copy-start | bytes 3076
  8.1 11.7 %copy-start.26 = (f32[100]{0:T(128)S(1)}, f32[100]{0:T(128)}, u32[]{:S(2)}) copy-start(f32[100]{0:T(128)} %param.19) | copy-start | bytes 1204
  8.1 11.8 %copy-start.24 = (s32[3,256]{1,0:T(4,128)S(1)}, s32[3,256]{1,0:T(4,128)}, u32[]{:S(2)}) copy-start(s32[3,256]{1,0:T(4,128)} %param.20) | copy-start | bytes 9220
  8.2 11.8 %copy-start.1 = (bf16[2,64,1024]{2,1,0:T(8,128)(2,1)S(1)}, bf16[2,64,1024]{2,1,0:T(8,128)(2,1)}, u32[]{:S(2)}) copy-start(bf16[2,64,1024]{2,1,0:T(8,128)(2,1)} %param.11) | copy-start | bytes 786436
  11.2 9.1 %collective-permute-start = (bf16[1,2,32,1024]{2,3,1,0:T(8,128)(2,1)}, bf16[1,2,32,1024]{2,3,1,0:T(8,128)(2,1)}, u32[]{:S(2)}, u32[]{:S(2)}) collective-permute-start(bf16[1,2,32,1024]{2,3,1,0:T(8,128)(2,1)} %bitcast.11), channel_id=1, source_target_pairs={{0,1},{1,2},{2,3},{3,4},{4,5},{5,6},{6,7},{8,9},{9,10},{10,11},{11... | collective-permute-start | bytes 393224 | tf_op jit(solution)/shard_map/ppermute | solution.py:21
  17.3 5.4 %collective-permute-start.1 = (bf16[1,2,32,1024]{2,3,1,0:T(8,128)(2,1)}, bf16[1,2,32,1024]{2,3,1,0:T(8,128)(2,1)}, u32[]{:S(2)}, u32[]{:S(2)}) collective-permute-start(bf16[1,2,32,1024]{2,3,1,0:T(8,128)(2,1)} %bitcast.16), channel_id=1, source_target_pairs={{1,0},{2,1},{3,2},{4,3},{5,4},{6,5},{7,6},{9,8},{10,9},{11,10},{12... | collective-permute-start | bytes 393224 | tf_op jit(solution)/shard_map/ppermute | solution.py:23
  24.4 0.8 copy-start.10
  48.3 2.7 copy-start.17
  56.6 4.7 copy-start.7
  59.4 2.7 copy-start.2
  62.1 1.2 copy-start.19
  62.1 1.2 copy-start.22
  62.5 21.2 %copy-start.8 = (bf16[256,16,64]{0,2,1:T(8,128)(2,1)}, bf16[256,16,64]{0,2,1:T(8,128)(2,1)S(1)}, u32[]{:S(2)}) copy-start(bf16[256,16,64]{0,2,1:T(8,128)(2,1)S(1)} %multiply_reduce_fusion.2) | copy-start | bytes 1572868
  63.3 21.4 %copy-start.23 = (f32[100,256]{1,0:T(8,128)S(1)}, f32[100,256]{1,0:T(8,128)}, u32[]{:S(2)}) copy-start(f32[100,256]{1,0:T(8,128)} %param.17) | copy-start | bytes 307204
  88.5 280.2 %reduce-scatter.6.cloned.1.call-start = ((), (), s32[]{:S(2)}) async-start(), calls=%async_computation.4 | async-start | bytes 4325376 | tf_op jit(solution)/shard_map/reduce_scatter | solution.py:198
  88.6 1.9 copy-start.9
  88.6 1.9 copy-start.12
  93.2 1.2 copy-start.14
  93.2 422.6 %reduce-scatter.4.cloned.1.call-start = ((), (), s32[]{:S(2)}) async-start(), calls=%async_computation.3 | async-start | bytes 8650752 | tf_op jit(solution)/shard_map/reduce_scatter | solution.py:189
  109.5 3.6 copy-start.13
  126.8 3.7 copy-start.15
  130.4 4.5 copy-start.3
  130.4 4.5 copy-start.16
  134.9 3.0 copy-start.4
  134.9 4.0 copy-start.5
  134.9 4.2 copy-start.18
  175.6 1.6 copy-start.11
  175.7 1.5 copy-start.20
  181.9 1.0 copy-start.21
  186.4 7.9 %collective-permute-start.2 = (bf16[1,2,32,1024]{3,2,1,0:T(8,128)(2,1)S(1)}, bf16[1,2,32,1024]{3,2,1,0:T(8,128)(2,1)S(1)}, u32[]{:S(2)}, u32[]{:S(2)}) collective-permute-start(bf16[1,2,32,1024]{3,2,1,0:T(8,128)(2,1)S(1)} %get-tuple-element.32), channel_id=1, source_target_pairs={{0,1},{1,2},{2,3},{3,4},{4,5},{5,6},{6,7},{8,9},{9,10},{10,11},{11... | collective-permute-start | bytes 393224 | tf_op jit(solution)/shard_map/ppermute | solution.py:21
  192.5 5.3 %collective-permute-start.3 = (bf16[1,2,32,1024]{3,2,1,0:T(8,128)(2,1)S(1)}, bf16[1,2,32,1024]{3,2,1,0:T(8,128)(2,1)S(1)}, u32[]{:S(2)}, u32[]{:S(2)}) collective-permute-start(bf16[1,2,32,1024]{3,2,1,0:T(8,128)(2,1)S(1)} %get-tuple-element.33), channel_id=1, source_target_pairs={{1,0},{2,1},{3,2},{4,3},{5,4},{6,5},{7,6},{9,8},{10,9},{11,10},{12... | collective-permute-start | bytes 393224 | tf_op jit(solution)/shard_map/ppermute | solution.py:23
Sparse Core Ops, SparseCore 0:
  88.7 140.6 reduce-scatter.7
  231.7 136.9 reduce-scatter.5
  371.2 144.5 reduce-scatter.3
where the time goes:
time: 533 us; the launch traced here: 524 us
  waiting for transfers between devices  316 us (59%)
  other arithmetic  68.6 us (13%)
  local copies, waits for them, and re-layouts  68.2 us (13%)
  matrix products  25.6 us (5%)
  blocking collectives  19.8 us (4%)
  between operations  14.6 us (3%)
  starting transfers between devices  11.9 us (2%)
    reduce_scatter x1, waiting for transfers between devices, shards(): lax.psum_scatter(lax.dot_general(flat_ext, flat_node, (((0,), (0,)), ((),...  145 us
    reduce_scatter x1, waiting for transfers between devices, shards(): lax.psum_scatter(out_sum, ('member', 'band'), scatter_dimension=0, tiled=...  138 us
    scatter-add x2, other arithmetic, shards(): jax.ops.segment_sum(edge_grad.reshape(edge_count * grid_count, 2 * model_...  33 us
    reduce_scatter x1, waiting for transfers between devices, shards(): lax.psum_scatter(head_sum, ('member', 'band'), scatter_dimension=0, tiled...  26.1 us
    unnamed x67, local copies, waits for them, and re-layouts  25.5 us
    all_gather x1, blocking collectives, shards(): lax.all_gather(local_prediction, 'member', axis=0, tiled=True)  19.8 us
  transfers between devices with their start and end apart: 7, of which 5 were waited for; matrix products, arithmetic and copies ran while one was open for 21% of the time, Pallas kernels for 0%

commit v1 on v0

v1 whole, which is shorter than its diff:
```python
import functools

import jax
import jax.numpy as jnp
from jax import lax
from jax.experimental import pallas as pl
from jax.experimental.pallas import tpu as pltpu
from jax.sharding import PartitionSpec as P

HEAD_DIM = 64
LANES = 128
ALPHA = 0.95
SOFTENING = 0.5
BF = jnp.bfloat16
F32 = jnp.float32
NN = (((1,), (0,)), ((), ()))
NT = (((1,), (1,)), ((), ()))
TN = (((0,), (0,)), ((), ()))


def mm(a, b, dims=NN):
    return lax.dot_general(a, b, dims, preferred_element_type=F32)


def call(body, out_shape, args, scratch=(), flops=0, nbytes=0, limit=40):
    return pl.pallas_call(
        body,
        out_shape=out_shape,
        in_specs=[pl.BlockSpec(memory_space=pltpu.VMEM) for _ in args],
        out_specs=jax.tree.map(lambda _: pl.BlockSpec(memory_space=pltpu.VMEM), out_shape),
        scratch_shapes=list(scratch),
        compiler_params=pltpu.CompilerParams(vmem_limit_bytes=limit * 1024 * 1024),
        cost_estimate=pl.CostEstimate(flops=flops, bytes_accessed=nbytes, transcendentals=0),
    )(*args)


def sds(shape, dtype):
    return jax.ShapeDtypeStruct(shape, dtype)


def one_hot_rows(halo_ref, row, node_count):
    rim = halo_ref.shape[1]
    nodes = lax.broadcasted_iota(jnp.int32, (node_count, rim), 0)
    return (nodes == halo_ref[row : row + 1, :]).astype(F32).astype(BF)


def pick_body(hidden_ref, halo_ref, down_ref, up_ref):
    members, nodes, _ = hidden_ref.shape
    rim = halo_ref.shape[1]
    for row, out_ref in ((0, down_ref), (1, up_ref)):
        hot = one_hot_rows(halo_ref, row, nodes)
        for m in range(members):
            out_ref[m * rim : (m + 1) * rim, :] = mm(hot, hidden_ref[m], TN).astype(BF)


def prepare_body(
    hidden_ref, kvw_ref, wo_ref, hp_ref, q_ref, init_ref, chw_ref, lat_ref,
    kv_ref, pt_ref, p_ref, base_ref, weight_ref, hp_pad,
):
    channels = hp_ref.shape[1]
    hp_pad[...] = jnp.zeros_like(hp_pad)
    hp_pad[:, 0:channels] = hp_ref[...].astype(F32)
    hp = hp_pad[...]
    hp_t = hp.T.astype(BF)
    pt = mm(wo_ref[...], hp.astype(BF))
    pt_ref[...] = pt.astype(BF)
    p_ref[...] = pt.T.astype(BF)
    base_ref[...] = mm(hp_t, q_ref[...], NT)
    base_ref[0:channels, :] = base_ref[0:channels, :] + init_ref[...]
    weight_ref[...] = chw_ref[...] * lat_ref[...]
    kv_ref[...] = mm(hidden_ref[...], kvw_ref[...]).astype(BF)


def split_heads(block):
    low = lax.broadcasted_iota(jnp.int32, block.shape, 1) < HEAD_DIM
    zero = jnp.zeros_like(block)
    return jnp.concatenate([jnp.where(low, block, zero), jnp.where(low, zero, block)], axis=0)


def forward_body(
    below_ref, above_ref, own_ref, kvw_ref, q_ref, src_ref, p_ref,
    kv_ref, gate_ref, slope_ref, merged_ref, part_ref, send_ref,
):
    members, ext, width2 = kv_ref.shape
    width = width2 // 2
    points = q_ref.shape[0]
    nodes = own_ref.shape[0] // members
    rim = below_ref.shape[0] // members
    halo = mm(jnp.concatenate([below_ref[...], above_ref[...]], axis=0), kvw_ref[...]).astype(BF)
    for m in range(members):
        kv_ref[m, 0:nodes, :] = own_ref[m * nodes : (m + 1) * nodes, :]
        kv_ref[m, nodes : nodes + rim, :] = halo[m * rim : (m + 1) * rim]
        kv_ref[m, nodes + rim : ext, :] = halo[(members + m) * rim : (members + m + 1) * rim]
    rows = lax.broadcasted_iota(jnp.int32, (ext, points), 0)
    mask = rows == src_ref[0:1, :]
    for e in range(1, src_ref.shape[0]):
        mask = mask | (rows == src_ref[e : e + 1, :])
    mask = mask.astype(F32)
    mask = jnp.concatenate([mask, mask], axis=0)
    scale = HEAD_DIM ** (-0.5)
    for pair in range(width // LANES):
        cols = slice(pair * LANES, (pair + 1) * LANES)
        vcols = slice(width + pair * LANES, width + (pair + 1) * LANES)
        q = q_ref[:, cols]
        for m in range(members):
            th = jnp.tanh(mm(split_heads(kv_ref[m, :, cols]), q, NT) * (0.5 * scale))
            gate = ((0.5 * th + 0.5) * mask).astype(BF)
            gate_ref[pair, m] = gate
            slope_ref[pair, m] = ((0.25 * scale) * mask * (1.0 - th * th)).astype(BF)
            merged_ref[m, cols, :] = mm(split_heads(kv_ref[m, :, vcols]), gate, TN).astype(BF)
    send_rows = send_ref.shape[1]
    for m in range(members):
        part = mm(p_ref[...], merged_ref[m])
        part_ref[m] = part
        send_ref[m] = part[0:send_rows].astype(BF)


def destination_rows(member, band, n_member, n_band, rw):
    chip, core = band // 2, band % 2
    for rel_core in (1, 0):
        for rel_chip in range(n_band // 2):
            to_band = (chip ^ rel_chip) * 2 + (core ^ rel_core)
            for rel_member in range(n_member):
                yield pl.multiple_of(((member ^ rel_member) * n_band + to_band) * rw, rw)


def reorder(src_ref, n_member, n_band):
    rw = src_ref.shape[0] // (n_member * n_band)
    member, band = lax.axis_index("member"), lax.axis_index("band")
    starts = destination_rows(member, band, n_member, n_band, rw)
    return jnp.concatenate([src_ref[pl.ds(start, rw), :] for start in starts], axis=0)


def transpose_body(n_member, n_band, hidden_ref, below_ref, above_ref, out_ref, turned):
    members, nodes, _ = hidden_ref.shape
    rim = below_ref.shape[0] // members
    parts = []
    for m in range(members):
        parts.append(hidden_ref[m])
        parts.append(below_ref[m * rim : (m + 1) * rim, :])
        parts.append(above_ref[m * rim : (m + 1) * rim, :])
    turned[...] = jnp.concatenate(parts, axis=0).astype(F32).T
    out_ref[...] = reorder(turned, n_member, n_band).astype(BF)


def select_heads(block):
    half = block.shape[0] // 2
    low = lax.broadcasted_iota(jnp.int32, (half, block.shape[1]), 1) < HEAD_DIM
    return jnp.where(low, block[:half], block[half:])


def soft_slope(v):
    return v * lax.rsqrt(v * v + SOFTENING * SOFTENING)


def backward_body(n_member, n_band, n_recv, *refs):
    recv_refs = refs[:n_recv]
    (part_ref, base_ref, truth_ref, weight_ref, pt_ref, merged_ref, gate_ref, slope_ref,
     kv_ref, q_ref, ext_ref, wo_ref) = refs[n_recv : n_recv + 12]
    outs = refs[n_recv + 12 :]
    n_out = n_band
    ng_ref = outs[0]
    part_outs = outs[1 : 1 + n_out]
    grad, turned = outs[1 + n_out :]
    members, ext, width2 = kv_ref.shape
    width = width2 // 2
    channels = truth_ref.shape[0]
    total = members * n_member
    spread = (1.0 - (1.0 - ALPHA) / total) / (total * (total - 1))

    grad[...] = jnp.zeros_like(grad)
    own = [part_ref[m, 0:channels, :] for m in range(members)]
    for m in range(members):
        slopes = jnp.zeros_like(own[m])
        for k in range(members):
            if k != m:
                slopes = slopes + soft_slope(own[m] - own[k])
        for ref in recv_refs:
            for k in range(members):
                slopes = slopes + soft_slope(own[m] - ref[k, 0:channels, :].astype(F32))
        gap = soft_slope(own[m] + base_ref[0:channels, :] - truth_ref[...])
        grad[m, 0:channels, :] = (weight_ref[...] * (gap / total - spread * slopes)).astype(BF)

    merged_t = [mm(pt_ref[...], grad[m]).astype(BF) for m in range(members)]

    for pair in range(width // LANES):
        cols = slice(pair * LANES, (pair + 1) * LANES)
        vcols = slice(width + pair * LANES, width + (pair + 1) * LANES)
        q = q_ref[:, cols]
        for m in range(members):
            dm = merged_t[m][cols]
            dgate = mm(split_heads(kv_ref[m, :, vcols]), dm)
            dscore = (dgate * slope_ref[pair, m].astype(F32)).astype(BF)
            ng_ref[m * ext : (m + 1) * ext, cols] = select_heads(mm(dscore, q)).astype(BF)
            ng_ref[m * ext : (m + 1) * ext, vcols] = select_heads(mm(gate_ref[pair, m], dm, NT)).astype(BF)

    step = 512
    block = part_outs[0].shape[0]
    for start in range(0, width2, step):
        product = mm(ext_ref[...], ng_ref[:, start : start + step]).astype(BF)
        for i, ref in enumerate(part_outs):
            ref[:, start : start + step] = product[i * block : (i + 1) * block]

    m_t = sum(mm(grad[m], merged_ref[m], NT) for m in range(members))
    head_t = sum(mm(grad[m], q_ref[...]) for m in range(members)) + mm(m_t.astype(BF), wo_ref[...])
    turned[...] = jnp.concatenate([m_t, head_t], axis=0).T
    small = reorder(turned, n_member, n_band).astype(BF)
    for i, ref in enumerate(part_outs):
        ref[:, width2:] = small[i * block : (i + 1) * block]


def extended_grad_body(members, nodes, rim, ng_ref, kvw_ref, own_ref, down_ref, up_ref):
    ext = nodes + 2 * rim
    for m in range(members):
        rows = mm(ng_ref[m * ext : (m + 1) * ext, :], kvw_ref[...], NT)
        own_ref[m] = rows[0:nodes]
        down_ref[m * rim : (m + 1) * rim, :] = rows[nodes : nodes + rim].astype(BF)
        up_ref[m * rim : (m + 1) * rim, :] = rows[nodes + rim :].astype(BF)


def hidden_body(own_ref, from_below_ref, from_above_ref, halo_ref, out_ref):
    members, nodes, _ = own_ref.shape
    rim = halo_ref.shape[1]
    low = one_hot_rows(halo_ref, 0, nodes)
    high = one_hot_rows(halo_ref, 1, nodes)
    for m in range(members):
        rows = slice(m * rim, (m + 1) * rim)
        out_ref[m] = own_ref[m] + mm(low, from_below_ref[rows, :]) + mm(high, from_above_ref[rows, :])


def finish_body(devices, *refs):
    parts = refs[:-4]
    hp_ref, kv_ref, out_ref, head_ref = refs[-4:]
    width2 = kv_ref.shape[1]
    channels = hp_ref.shape[1]
    total = parts[0][...].astype(F32)
    for ref in parts[1:]:
        total = total + ref[...].astype(F32)
    total = total * (1.0 / devices)
    kv_ref[...] = total[:, 0:width2]
    m_rows = total[:, width2 : width2 + channels]
    high = m_rows.astype(BF)
    low = (m_rows - high.astype(F32)).astype(BF)
    out_ref[...] = mm(high, hp_ref[...], NT) + mm(low, hp_ref[...], NT)
    head_ref[...] = total[:, width2 + LANES : width2 + LANES + channels]


def add_up(*parts):
    return functools.reduce(lambda a, b: a + b, [p.astype(F32) for p in parts])


def shards(
    n_member, n_band,
    hidden, queries, kv_weight, out_weight, head_projection, initial_state, truth,
    latitude_weight, channel_loss_weight, sources, halo_rows,
):
    members, nodes, width = hidden.shape
    points = queries.shape[0]
    channels = head_projection.shape[1]
    rim = halo_rows.shape[1]
    ext = nodes + 2 * rim
    pairs = width // LANES
    devices = n_member * n_band
    chips = n_band // 2
    rw = width // devices
    send_rows = -(-channels // 16) * 16
    to_above = [(i, i + 1) for i in range(n_band - 1)]
    to_below = [(i + 1, i) for i in range(n_band - 1)]

    down, up = call(
        pick_body, [sds((members * rim, width), BF)] * 2, (hidden, halo_rows), flops=10**7, nbytes=10**6
    )
    below = lax.ppermute(up, "band", to_above)
    above = lax.ppermute(down, "band", to_below)

    own_kv, pt, p, base, weight = call(
        prepare_body,
        [
            sds((members * nodes, 2 * width), BF),
            sds((width, LANES), BF),
            sds((LANES, width), BF),
            sds((LANES, points), F32),
            sds((channels, points), F32),
        ],
        (
            hidden.reshape(members * nodes, width), kv_weight, out_weight, head_projection, queries,
            initial_state, channel_loss_weight[:, None], latitude_weight[None, :],
        ),
        [pltpu.VMEM((width, LANES), F32)],
        flops=10**9, nbytes=8 * 10**6,
    )

    kv, gates, slopes, merged, part, sent = call(
        forward_body,
        [
            sds((members, ext, 2 * width), BF),
            sds((pairs, members, 2 * ext, points), BF),
            sds((pairs, members, 2 * ext, points), BF),
            sds((members, width, points), BF),
            sds((members, LANES, points), F32),
            sds((members, send_rows, points), BF),
        ],
        (below, above, own_kv, kv_weight, queries, sources, p),
        flops=4 * 10**9, nbytes=16 * 10**6,
    )

    received = [
        lax.ppermute(sent, "member", [(i, i ^ s) for i in range(n_member)]) for s in range(1, n_member)
    ]

    ext_t = call(
        functools.partial(transpose_body, n_member, n_band),
        sds((width, members * ext), BF),
        (hidden, below, above),
        [pltpu.VMEM((width, members * ext), F32)],
        flops=10**8, nbytes=2 * 10**6,
    )

    extra = 2 * LANES
    results = call(
        functools.partial(backward_body, n_member, n_band, n_member - 1),
        [sds((members * ext, 2 * width), BF)]
        + [sds((n_member * rw, 2 * width + extra), BF)] * n_band,
        (*received, part, base, truth, weight, pt, merged, gates, slopes, kv, queries, ext_t, out_weight),
        [pltpu.VMEM((members, LANES, points), BF), pltpu.VMEM((width, extra), F32)],
        flops=8 * 10**9, nbytes=24 * 10**6,
    )
    node_grad, send, keep = results[0], results[1 : 1 + chips], results[1 + chips :]

    swap = [(i, i ^ 1) for i in range(n_band)]
    crossed = [None] * chips
    for s in list(range(1, chips)) + [0]:
        crossed[s] = lax.ppermute(send[s], "band", swap)

    own_grad, back_down, back_up = call(
        functools.partial(extended_grad_body, members, nodes, rim),
        [sds((members, nodes, width), F32)] + [sds((members * rim, width), BF)] * 2,
        (node_grad, kv_weight),
        flops=2 * 10**9, nbytes=8 * 10**6,
    )

    gathered = []
    for s in range(1, chips):
        chip_sum = add_up(keep[s], crossed[s]).astype(BF)
        gathered.append(
            lax.ppermute(chip_sum, "band", [(i, ((i // 2) ^ s) * 2 + i % 2) for i in range(n_band)])
        )

    from_above = lax.ppermute(back_down, "band", to_below)
    from_below = lax.ppermute(back_up, "band", to_above)
    hidden_grad = call(
        hidden_body,
        sds((members, nodes, width), F32),
        (own_grad, from_below, from_above, halo_rows),
        flops=10**7, nbytes=2 * 10**6,
    )

    plane = add_up(keep[0], crossed[0], *gathered).astype(BF)
    last = [plane[0:rw]]
    for s in range(1, n_member):
        last.append(
            lax.ppermute(plane[s * rw : (s + 1) * rw], "member", [(i, i ^ s) for i in range(n_member)])
        )
    kv_grad, out_grad, head_grad = call(
        functools.partial(finish_body, devices),
        [sds((rw, 2 * width), F32), sds((rw, width), F32), sds((rw, channels), F32)],
        (*last, head_projection),
        flops=10**7, nbytes=10**6,
    )
    return hidden_grad, kv_grad, out_grad, head_grad


def solution(mesh):
    placed = (
        P("member", "band", None),
        P("band", None),
        P(),
        P(),
        P(),
        P(None, "band"),
        P(None, "band"),
        P("band"),
        P(),
        P(None, "band"),
        P("band", None),
    )
    return jax.shard_map(
        functools.partial(shards, mesh.shape["member"], mesh.shape["band"]),
        mesh=mesh,
        in_specs=placed,
        out_specs=(
            P("member", "band", None),
            P(("member", "band"), None),
            P(("member", "band"), None),
            P(("member", "band"), None),
        ),
        check_vma=False,
    )
```

time: 533 us -> 98.7 us (0.19)
  the two profiles are of different devices: /device:TPU:0 before, /device:TPU:3 now
where the time goes in v1:
time: 98.7 us; the launch traced here: 98.2 us
  waiting for transfers between devices  42 us (43%)
  starting transfers between devices  23.5 us (24%)
  Pallas kernels  19.2 us (19%)
  local copies, waits for them, and re-layouts  11.7 us (12%)
    ppermute x3, waiting for transfers between devices, shards(): lax.ppermute(chip_sum, 'band', [(i, (i // 2 ^ s) * 2 + i % 2) for i in ra...  25.1 us
    pallas_call x8, Pallas kernels, call(): pl.pallas_call(body, out_shape=out_shape, in_specs=[pl.BlockSpec(memory_s...  19.2 us
    unnamed x27, local copies, waits for them, and re-layouts  10.9 us
    ppermute x3, waiting for transfers between devices, shards(): lax.ppermute(sent, 'member', [(i, i ^ s) for i in range(n_member)])  8.65 us
    ppermute x1, waiting for transfers between devices, shards(): from_above = lax.ppermute(back_down, 'band', to_below)  5.25 us
    ppermute x1, starting transfers between devices, shards(): from_below = lax.ppermute(back_up, 'band', to_above)  5.04 us
    ppermute x3, starting transfers between devices, shards(): lax.ppermute(sent, 'member', [(i, i ^ s) for i in range(n_member)])  3.75 us
    ppermute x1, starting transfers between devices, shards(): below = lax.ppermute(up, 'band', to_above)  3.68 us
  transfers between devices with their start and end apart: 17, of which 8 were waited for; matrix products, arithmetic and copies ran while one was open for 2% of the time, Pallas kernels for 6%

profile of v1, /device:TPU:3, one launch (start us, length us, event | category | flops | bytes accessed | tf_op | source)
XLA Modules:
  0.0 98.2 jit_solution(883628641188262626)
XLA Ops:
  0.6 0.0 copy-start.2
  0.6 0.9 copy-done.2
  1.6 0.7 copy-done.8
  2.3 0.3 shard_map.138
  2.5 3.7 %collective-permute-start = (bf16[64,1024]{1,0:T(8,128)(2,1)S(1)}, bf16[64,1024]{1,0:T(8,128)(2,1)S(1)}, u32[]{:S(2)}, u32[]{:S(2)}) collective-permute-start(bf16[64,1024]{1,0:T(8,128)(2,1)S(1)} %get-tuple-element.32), channel_id=1, source_target_pairs={{0,1},{1,2},{2,3},{3,4},{4,5},{5,6},{6,7},{8,9},{9,10},{10,11},{11... | collective-permute-start | bytes 393224 | tf_op jit(solution)/shard_map/ppermute | solution.py:273
  6.2 1.9 %collective-permute-start.1 = (bf16[64,1024]{1,0:T(8,128)(2,1)S(1)}, bf16[64,1024]{1,0:T(8,128)(2,1)S(1)}, u32[]{:S(2)}, u32[]{:S(2)}) collective-permute-start(bf16[64,1024]{1,0:T(8,128)(2,1)S(1)} %get-tuple-element.33), channel_id=1, source_target_pairs={{1,0},{2,1},{3,2},{4,3},{5,4},{6,5},{7,6},{9,8},{10,9},{11,10},{12... | collective-permute-start | bytes 393224 | tf_op jit(solution)/shard_map/ppermute | solution.py:274
  8.1 0.8 copy.16.chw_ref
  8.9 1.1 %copy.15.hp_ref.refs_4_ = bf16[1024,100]{1,0:T(8,128)(2,1)S(1)} copy(bf16[1024,100]{0,1:T(8,128)(2,1)} %param.15) | data formatting | bytes 409600 | tf_op args[4]
  10.0 2.2 %copy-done = bf16[1024,2048]{1,0:T(8,128)(2,1)S(1)} copy-done((bf16[1024,2048]{1,0:T(8,128)(2,1)S(1)}, bf16[1024,2048]{1,0:T(8,128)(2,1)}, u32[]{:S(2)}) %copy-start) | copy-done | bytes 4194328
  12.2 0.9 copy-done.3
  13.2 1.6 %copy-done.4 = bf16[1024,1024]{1,0:T(8,128)(2,1)S(1)} copy-done((bf16[1024,1024]{1,0:T(8,128)(2,1)S(1)}, bf16[1024,1024]{1,0:T(8,128)(2,1)}, u32[]{:S(2)}) %copy-start.4) | copy-done | bytes 2097176
  14.8 1.0 %copy-done.5 = bf16[256,1024]{1,0:T(8,128)(2,1)S(1)} copy-done((bf16[256,1024]{1,0:T(8,128)(2,1)S(1)}, bf16[256,1024]{1,0:T(8,128)(2,1)}, u32[]{:S(2)}) %copy-start.5) | copy-done | bytes 524312
  15.8 0.9 copy-done.7
  16.7 0.7 copy-done.10
  17.4 1.5 %shard_map.139 = (bf16[128,2048]{1,0:T(8,128)(2,1)S(1)}, bf16[1024,128]{1,0:T(8,128)(2,1)S(1)}, bf16[128,1024]{1,0:T(8,128)(2,1)S(1)}, f32[128,256]{1,0:T(8,128)S(1)}, f32[100,256]{1,0:T(8,128)S(1)}) custom-call(bf16[128,1024]{1,0:T(8,128)(2,1)S(1)} %bitcast.3, bf16[1024,2048]{1,0:T(8,128)(2,1)S(1)} %copy-done, bf16[1024,1024]{1,0:T(8,128)(2,1)S(1)} %copy-done.4, ...), custom_call_target="tpu_custom_call" | custom-call | flops 1000000000 | bytes 8000000 | tf_op jit(solution)/shard_map/pallas_call | solution.py:26
  18.9 0.7 copy-done.1
  19.6 0.1 copy-done.6
  19.7 5.0 %shard_map.140 = (bf16[2,128,2048]{2,1,0:T(8,128)(2,1)S(1)}, bf16[8,2,256,256]{3,2,1,0:T(8,128)(2,1)S(1)}, bf16[8,2,256,256]{3,2,1,0:T(8,128)(2,1)S(1)}, bf16[2,...) custom-call(bf16[64,1024]{1,0:T(8,128)(2,1)S(1)} %collective-permute-done.below_ref, ...), custom_call_target="tpu_custom_call" | custom-call | flops 4000000000 | bytes 16000000 | tf_op jit(solution)/shard_map/pallas_call | solution.py:26
  24.6 3.4 %collective-permute-start.4 = (bf16[2,112,256]{2,1,0:T(8,128)(2,1)S(1)}, bf16[2,112,256]{2,1,0:T(8,128)(2,1)S(1)}, u32[]{:S(2)}, u32[]{:S(2)}) collective-permute-start(bf16[2,112,256]{2,1,0:T(8,128)(2,1)S(1)} %get-tuple-element.36), channel_id=1, source_target_pairs={{0,24},{8,16},{16,8},{24,0},{1,25},{9,17},{17,9},{25,1},{2,26},{10... | collective-permute-start | bytes 344072 | tf_op jit(solution)/shard_map/ppermute | solution.py:308
  28.0 0.4 collective-permute-start.2
  28.4 0.3 shard_map.141.refs_13_
  28.7 2.1 %collective-permute-done.4.refs_2_ = bf16[2,112,256]{2,1,0:T(8,128)(2,1)S(1)} collective-permute-done((bf16[2,112,256]{2,1,0:T(8,128)(2,1)S(1)}, bf16[2,112,256]{2,1,0:T(8,128)(2,1)S(1)}, u32[]{:S(2)}, u32[]{:S(2)}) %collective-permute-start.4) | collective-permute-done | bytes 114720 | tf_op jit(solution)/shard_map/ppermute | solution.py:308
  30.8 6.5 %collective-permute-done.3.refs_1_ = bf16[2,112,256]{2,1,0:T(8,128)(2,1)S(1)} collective-permute-done((bf16[2,112,256]{2,1,0:T(8,128)(2,1)S(1)}, bf16[2,112,256]{2,1,0:T(8,128)(2,1)S(1)}, u32[]{:S(2)}, u32[]{:S(2)}) %collective-permute-start.3) | collective-permute-done | bytes 114720 | tf_op jit(solution)/shard_map/ppermute | solution.py:308
  37.3 7.3 %shard_map.142 = (bf16[256,2048]{1,0:T(8,128)(2,1)S(1)}, bf16[128,2304]{1,0:T(8,128)(2,1)S(1)}, bf16[128,2304]{1,0:T(8,128)(2,1)S(1)}, bf16[128,2304]{1,0:T(8,12...) custom-call(bf16[2,112,256]{2,1,0:T(8,128)(2,1)S(1)} %collective-per, ...), custom_call_target="tpu_custom_call" | custom-call | flops 8000000000 | bytes 24000000 | tf_op jit(solution)/shard_map/pallas_call | solution.py:26
  44.6 1.4 %collective-permute-start.8 = (bf16[128,2304]{1,0:T(8,128)(2,1)S(1)}, bf16[128,2304]{1,0:T(8,128)(2,1)S(1)}, u32[]{:S(2)}, u32[]{:S(2)}) collective-permute-start(bf16[128,2304]{1,0:T(8,128)(2,1)S(1)} %get-tuple-element.52), channel_id=1, source_target_pairs={{0,1},{1,0},{2,3},{3,2},{4,5},{5,4},{6,7},{7,6},{8,9},{9,8},{10,11... | collective-permute-start | bytes 1769480 | tf_op jit(solution)/shard_map/ppermute | solution.py:333
  46.0 0.1 collective-permute-start.7
  46.1 0.4 collective-permute-start.10
  46.6 0.1 collective-permute-start.12
  46.6 1.0 %collective-permute-done.8 = bf16[128,2304]{1,0:T(8,128)(2,1)S(1)} collective-permute-done((bf16[128,2304]{1,0:T(8,128)(2,1)S(1)}, bf16[128,2304]{1,0:T(8,128)(2,1)S(1)}, u32[]{:S(2)}, u32[]{:S(2)}) %collective-permute-start.8) | collective-permute-done | bytes 589856 | tf_op jit(solution)/shard_map/ppermute | solution.py:333
  47.7 0.1 add_convert_fusion.3
  47.8 0.1 collective-permute-start.9
  47.9 1.5 %collective-permute-done.10 = bf16[128,2304]{1,0:T(8,128)(2,1)S(1)} collective-permute-done((bf16[128,2304]{1,0:T(8,128)(2,1)S(1)}, bf16[128,2304]{1,0:T(8,128)(2,1)S(1)}, u32[]{:S(2)}, u32[]{:S(2)}) %collective-permute-start.10) | collective-permute-done | bytes 589856 | tf_op jit(solution)/shard_map/ppermute | solution.py:333
  49.4 0.1 add_convert_fusion.2
  49.5 0.2 collective-permute-start.11
  49.7 0.5 collective-permute-done.12
  50.2 0.1 add_convert_fusion.1
  50.3 1.3 %collective-permute-start.13 = (bf16[128,2304]{1,0:T(8,128)(2,1)S(1)}, bf16[128,2304]{1,0:T(8,128)(2,1)S(1)}, u32[]{:S(2)}, u32[]{:S(2)}) collective-permute-start(bf16[128,2304]{1,0:T(8,128)(2,1)S(1)} %add_convert_fusion.1), channel_id=1, source_target_pairs={{0,6},{1,7},{2,4},{3,5},{4,2},{5,3},{6,0},{7,1},{8,14},{9,15},{10,... | collective-permute-start | bytes 1769480 | tf_op jit(solution)/shard_map/ppermute | solution.py:346
  51.6 10.8 %collective-permute-done.9 = bf16[128,2304]{1,0:T(8,128)(2,1)S(1)} collective-permute-done((bf16[128,2304]{1,0:T(8,128)(2,1)S(1)}, bf16[128,2304]{1,0:T(8,128)(2,1)S(1)}, u32[]{:S(2)}, u32[]{:S(2)}) %collective-permute-start.9) | collective-permute-done | bytes 589856 | tf_op jit(solution)/shard_map/ppermute | solution.py:346
  62.4 14.3 %collective-permute-done.11 = bf16[128,2304]{1,0:T(8,128)(2,1)S(1)} collective-permute-done((bf16[128,2304]{1,0:T(8,128)(2,1)S(1)}, bf16[128,2304]{1,0:T(8,128)(2,1)S(1)}, u32[]{:S(2)}, u32[]{:S(2)}) %collective-permute-start.11) | collective-permute-done | bytes 589856 | tf_op jit(solution)/shard_map/ppermute | solution.py:346
  76.8 0.5 add_convert_fusion
  77.4 2.3 %collective-permute-start.16 = (bf16[32,2304]{1,0:T(8,128)(2,1)S(1)}, bf16[32,2304]{1,0:T(8,128)(2,1)S(1)}, u32[]{:S(2)}, u32[]{:S(2)}) collective-permute-start(bf16[32,2304]{1,0:T(8,128)(2,1)S(1)} %get-tuple-element.60), channel_id=1, source_target_pairs={{0,24},{8,16},{16,8},{24,0},{1,25},{9,17},{17,9},{25,1},{2,26},{10... | collective-permute-start | bytes 442376 | tf_op jit(solution)/shard_map/ppermute | solution.py:362
  79.6 1.4 %collective-permute-start.14 = (bf16[32,2304]{1,0:T(8,128)(2,1)S(1)}, bf16[32,2304]{1,0:T(8,128)(2,1)S(1)}, u32[]{:S(2)}, u32[]{:S(2)}) collective-permute-start(bf16[32,2304]{1,0:T(8,128)(2,1)S(1)} %get-tuple-element.62), channel_id=1, source_target_pairs={{0,8},{8,0},{16,24},{24,16},{1,9},{9,1},{17,25},{25,17},{2,10},{10... | collective-permute-start | bytes 442376 | tf_op jit(solution)/shard_map/ppermute | solution.py:362
  81.0 2.9 %shard_map.143 = (f32[2,64,1024]{2,1,0:T(8,128)S(1)}, bf16[64,1024]{1,0:T(8,128)(2,1)S(1)}, bf16[64,1024]{1,0:T(8,128)(2,1)S(1)}) custom-call(bf16[256,2048]{1,0:T(8,128)(2,1)S(1)} %get-tuple-element.45.ng_ref, bf16[1024,2048]{1,0:T(8,128)(2,1)S(1)} %copy-done.1), custom_call_target="tpu_custom_call" | custom-call | flops 2000000000 | bytes 8000000 | tf_op jit(solution)/shard_map/pallas_call | solution.py:26
  83.8 5.0 %collective-permute-start.5 = (bf16[64,1024]{1,0:T(8,128)(2,1)S(1)}, bf16[64,1024]{1,0:T(8,128)(2,1)S(1)}, u32[]{:S(2)}, u32[]{:S(2)}) collective-permute-start(bf16[64,1024]{1,0:T(8,128)(2,1)S(1)} %get-tuple-element.47), channel_id=1, source_target_pairs={{0,1},{1,2},{2,3},{3,4},{4,5},{5,6},{6,7},{8,9},{9,10},{10,11},{11... | collective-permute-start | bytes 393224 | tf_op jit(solution)/shard_map/ppermute | solution.py:350
  88.9 1.9 %collective-permute-start.6 = (bf16[64,1024]{1,0:T(8,128)(2,1)S(1)}, bf16[64,1024]{1,0:T(8,128)(2,1)S(1)}, u32[]{:S(2)}, u32[]{:S(2)}) collective-permute-start(bf16[64,1024]{1,0:T(8,128)(2,1)S(1)} %get-tuple-element.48), channel_id=1, source_target_pairs={{1,0},{2,1},{3,2},{4,3},{5,4},{6,5},{7,6},{9,8},{10,9},{11,10},{12... | collective-permute-start | bytes 393224 | tf_op jit(solution)/shard_map/ppermute | solution.py:349
  90.8 5.2 %collective-permute-done.6.from_above_ref = bf16[64,1024]{1,0:T(8,128)(2,1)S(1)} collective-permute-done((bf16[64,1024]{1,0:T(8,128)(2,1)S(1)}, bf16[64,1024]{1,0:T(8,128)(2,1)S(1)}, u32[]{:S(2)}, u32[]{:S(2)}) %collective-permute-start.6) | collective-permute-done | bytes 131104 | tf_op jit(solution)/shard_map/ppermute | solution.py:349
  96.1 1.1 %shard_map.144 = f32[2,64,1024]{2,1,0:T(8,128)} custom-call(f32[2,64,1024]{2,1,0:T(8,128)S(1)} %get-tuple-element.46.own_ref, bf16[64,1024]{1,0:T(8,128)(2,1)S(1)} %collective-permute-done.5.from_below_ref, bf16[64,1024]{1,0:T(8,128)(2,1)S(1)} %collective-permute-done.6.from_above_ref, s32[2,32]{1,0:T(2,128)S(1)} %copy-done.9), custom_call_target="tpu_custom_call" | custom-call | flops 10000000 | bytes 2000000 | tf_op jit(solution)/shard_map/pallas_call | solution.py:26
  97.2 1.0 %shard_map.145 = (f32[32,2048]{1,0:T(8,128)}, f32[32,1024]{1,0:T(8,128)}, f32[32,100]{1,0:T(8,128)}) custom-call(bf16[32,2304]{1,0:T(8,128)(2,1)S(1)} %get-tuple-element.63.refs_0_, bf16[32,2304]{1,0:T(8,128)(2,1)S(1)} %collective-permute-done.14.refs_1_, bf16[32,2304]{1,0:T(8,128)(2,1)S(1)} %collective-permute-done.15.refs_2_, ...), custom_call_target="tpu_custom_call" | custom-call | flops 10000000 | bytes 1000000 | tf_op jit(solution)/shard_map/pallas_call | solution.py:26
  (27 shorter events, 0.1 us)
Async XLA Ops:
  0.6 1.0 copy-start.2
  1.6 0.7 copy-start.8
  2.5 16.3 %collective-permute-start = (bf16[64,1024]{1,0:T(8,128)(2,1)S(1)}, bf16[64,1024]{1,0:T(8,128)(2,1)S(1)}, u32[]{:S(2)}, u32[]{:S(2)}) collective-permute-start(bf16[64,1024]{1,0:T(8,128)(2,1)S(1)} %get-tuple-element.32), channel_id=1, source_target_pairs={{0,1},{1,2},{2,3},{3,4},{4,5},{5,6},{6,7},{8,9},{9,10},{10,11},{11... | collective-permute-start | bytes 393224 | tf_op jit(solution)/shard_map/ppermute | solution.py:273
  6.2 12.7 %collective-permute-start.1 = (bf16[64,1024]{1,0:T(8,128)(2,1)S(1)}, bf16[64,1024]{1,0:T(8,128)(2,1)S(1)}, u32[]{:S(2)}, u32[]{:S(2)}) collective-permute-start(bf16[64,1024]{1,0:T(8,128)(2,1)S(1)} %get-tuple-element.33), channel_id=1, source_target_pairs={{1,0},{2,1},{3,2},{4,3},{5,4},{6,5},{7,6},{9,8},{10,9},{11,10},{12... | collective-permute-start | bytes 393224 | tf_op jit(solution)/shard_map/ppermute | solution.py:274
  10.0 2.2 %copy-start = (bf16[1024,2048]{1,0:T(8,128)(2,1)S(1)}, bf16[1024,2048]{1,0:T(8,128)(2,1)}, u32[]{:S(2)}) copy-start(bf16[1024,2048]{1,0:T(8,128)(2,1)} %kvw_ref.5) | copy-start | bytes 12582916
  12.2 0.9 copy-start.3
  13.2 1.6 %copy-start.4 = (bf16[1024,1024]{1,0:T(8,128)(2,1)S(1)}, bf16[1024,1024]{1,0:T(8,128)(2,1)}, u32[]{:S(2)}) copy-start(bf16[1024,1024]{1,0:T(8,128)(2,1)} %refs_14_.1) | copy-start | bytes 6291460
  14.8 1.0 %copy-start.5 = (bf16[256,1024]{1,0:T(8,128)(2,1)S(1)}, bf16[256,1024]{1,0:T(8,128)(2,1)}, u32[]{:S(2)}) copy-start(bf16[256,1024]{1,0:T(8,128)(2,1)} %refs_12_.1) | copy-start | bytes 1572868
  15.8 0.9 copy-start.7
  16.7 0.7 copy-start.10
  17.4 2.2 %copy-start.1 = (bf16[1024,2048]{1,0:T(8,128)(2,1)S(1)}, bf16[1024,2048]{1,0:T(8,128)(2,1)}, u32[]{:S(2)}) copy-start(bf16[1024,2048]{1,0:T(8,128)(2,1)} %kvw_ref.5) | copy-start | bytes 12582916
  17.4 2.3 %copy-start.6 = (bf16[256,1024]{1,0:T(8,128)(2,1)S(1)}, bf16[256,1024]{1,0:T(8,128)(2,1)}, u32[]{:S(2)}) copy-start(bf16[256,1024]{1,0:T(8,128)(2,1)} %refs_12_.1) | copy-start | bytes 1572868
  17.4 2.3 %copy-start.12 = (s32[3,256]{1,0:T(4,128)S(1)}, s32[3,256]{1,0:T(4,128)}, u32[]{:S(2)}) copy-start(s32[3,256]{1,0:T(4,128)} %src_ref.1) | copy-start | bytes 9220
  19.7 17.6 %copy-start.11 = (f32[100,256]{1,0:T(8,128)S(1)}, f32[100,256]{1,0:T(8,128)}, u32[]{:S(2)}) copy-start(f32[100,256]{1,0:T(8,128)} %refs_5_.1) | copy-start | bytes 307204
  24.6 6.1 %collective-permute-start.4 = (bf16[2,112,256]{2,1,0:T(8,128)(2,1)S(1)}, bf16[2,112,256]{2,1,0:T(8,128)(2,1)S(1)}, u32[]{:S(2)}, u32[]{:S(2)}) collective-permute-start(bf16[2,112,256]{2,1,0:T(8,128)(2,1)S(1)} %get-tuple-element.36), channel_id=1, source_target_pairs={{0,24},{8,16},{16,8},{24,0},{1,25},{9,17},{17,9},{25,1},{2,26},{10... | collective-permute-start | bytes 344072 | tf_op jit(solution)/shard_map/ppermute | solution.py:308
  28.0 9.3 %collective-permute-start.3 = (bf16[2,112,256]{2,1,0:T(8,128)(2,1)S(1)}, bf16[2,112,256]{2,1,0:T(8,128)(2,1)S(1)}, u32[]{:S(2)}, u32[]{:S(2)}) collective-permute-start(bf16[2,112,256]{2,1,0:T(8,128)(2,1)S(1)} %get-tuple-element.36), channel_id=1, source_target_pairs={{0,16},{8,24},{16,0},{24,8},{1,17},{9,25},{17,1},{25,9},{2,18},{10... | collective-permute-start | bytes 344072 | tf_op jit(solution)/shard_map/ppermute | solution.py:308
  28.0 9.3 %collective-permute-start.2 = (bf16[2,112,256]{2,1,0:T(8,128)(2,1)S(1)}, bf16[2,112,256]{2,1,0:T(8,128)(2,1)S(1)}, u32[]{:S(2)}, u32[]{:S(2)}) collective-permute-start(bf16[2,112,256]{2,1,0:T(8,128)(2,1)S(1)} %get-tuple-element.36), channel_id=1, source_target_pairs={{0,8},{8,0},{16,24},{24,16},{1,9},{9,1},{17,25},{25,17},{2,10},{10... | collective-permute-start | bytes 344072 | tf_op jit(solution)/shard_map/ppermute | solution.py:308
  44.6 3.0 %collective-permute-start.8 = (bf16[128,2304]{1,0:T(8,128)(2,1)S(1)}, bf16[128,2304]{1,0:T(8,128)(2,1)S(1)}, u32[]{:S(2)}, u32[]{:S(2)}) collective-permute-start(bf16[128,2304]{1,0:T(8,128)(2,1)S(1)} %get-tuple-element.52), channel_id=1, source_target_pairs={{0,1},{1,0},{2,3},{3,2},{4,5},{5,4},{6,7},{7,6},{8,9},{9,8},{10,11... | collective-permute-start | bytes 1769480 | tf_op jit(solution)/shard_map/ppermute | solution.py:333
  46.0 5.6 %collective-permute-start.7 = (bf16[128,2304]{1,0:T(8,128)(2,1)S(1)}, bf16[128,2304]{1,0:T(8,128)(2,1)S(1)}, u32[]{:S(2)}, u32[]{:S(2)}) collective-permute-start(bf16[128,2304]{1,0:T(8,128)(2,1)S(1)} %get-tuple-element.50), channel_id=1, source_target_pairs={{0,1},{1,0},{2,3},{3,2},{4,5},{5,4},{6,7},{7,6},{8,9},{9,8},{10,11... | collective-permute-start | bytes 1769480 | tf_op jit(solution)/shard_map/ppermute | solution.py:333
  46.1 3.2 %collective-permute-start.10 = (bf16[128,2304]{1,0:T(8,128)(2,1)S(1)}, bf16[128,2304]{1,0:T(8,128)(2,1)S(1)}, u32[]{:S(2)}, u32[]{:S(2)}) collective-permute-start(bf16[128,2304]{1,0:T(8,128)(2,1)S(1)} %get-tuple-element.54), channel_id=1, source_target_pairs={{0,1},{1,0},{2,3},{3,2},{4,5},{5,4},{6,7},{7,6},{8,9},{9,8},{10,11... | collective-permute-start | bytes 1769480 | tf_op jit(solution)/shard_map/ppermute | solution.py:333
  46.6 3.7 %collective-permute-start.12 = (bf16[128,2304]{1,0:T(8,128)(2,1)S(1)}, bf16[128,2304]{1,0:T(8,128)(2,1)S(1)}, u32[]{:S(2)}, u32[]{:S(2)}) collective-permute-start(bf16[128,2304]{1,0:T(8,128)(2,1)S(1)} %get-tuple-element.56), channel_id=1, source_target_pairs={{0,1},{1,0},{2,3},{3,2},{4,5},{5,4},{6,7},{7,6},{8,9},{9,8},{10,11... | collective-permute-start | bytes 1769480 | tf_op jit(solution)/shard_map/ppermute | solution.py:333
  47.8 14.6 %collective-permute-start.9 = (bf16[128,2304]{1,0:T(8,128)(2,1)S(1)}, bf16[128,2304]{1,0:T(8,128)(2,1)S(1)}, u32[]{:S(2)}, u32[]{:S(2)}) collective-permute-start(bf16[128,2304]{1,0:T(8,128)(2,1)S(1)} %add_convert_fusion.3), channel_id=1, source_target_pairs={{0,2},{1,3},{2,0},{3,1},{4,6},{5,7},{6,4},{7,5},{8,10},{9,11},{10,... | collective-permute-start | bytes 1769480 | tf_op jit(solution)/shard_map/ppermute | solution.py:346
  49.5 27.2 %collective-permute-start.11 = (bf16[128,2304]{1,0:T(8,128)(2,1)S(1)}, bf16[128,2304]{1,0:T(8,128)(2,1)S(1)}, u32[]{:S(2)}, u32[]{:S(2)}) collective-permute-start(bf16[128,2304]{1,0:T(8,128)(2,1)S(1)} %add_convert_fusion.2), channel_id=1, source_target_pairs={{0,4},{1,5},{2,6},{3,7},{4,0},{5,1},{6,2},{7,3},{8,12},{9,13},{10,... | collective-permute-start | bytes 1769480 | tf_op jit(solution)/shard_map/ppermute | solution.py:346
  50.3 26.4 %collective-permute-start.13 = (bf16[128,2304]{1,0:T(8,128)(2,1)S(1)}, bf16[128,2304]{1,0:T(8,128)(2,1)S(1)}, u32[]{:S(2)}, u32[]{:S(2)}) collective-permute-start(bf16[128,2304]{1,0:T(8,128)(2,1)S(1)} %add_convert_fusion.1), channel_id=1, source_target_pairs={{0,6},{1,7},{2,4},{3,5},{4,2},{5,3},{6,0},{7,1},{8,14},{9,15},{10,... | collective-permute-start | bytes 1769480 | tf_op jit(solution)/shard_map/ppermute | solution.py:346
  77.4 19.8 %collective-permute-start.16 = (bf16[32,2304]{1,0:T(8,128)(2,1)S(1)}, bf16[32,2304]{1,0:T(8,128)(2,1)S(1)}, u32[]{:S(2)}, u32[]{:S(2)}) collective-permute-start(bf16[32,2304]{1,0:T(8,128)(2,1)S(1)} %get-tuple-element.60), channel_id=1, source_target_pairs={{0,24},{8,16},{16,8},{24,0},{1,25},{9,17},{17,9},{25,1},{2,26},{10... | collective-permute-start | bytes 442376 | tf_op jit(solution)/shard_map/ppermute | solution.py:362
  79.6 17.5 %collective-permute-start.15 = (bf16[32,2304]{1,0:T(8,128)(2,1)S(1)}, bf16[32,2304]{1,0:T(8,128)(2,1)S(1)}, u32[]{:S(2)}, u32[]{:S(2)}) collective-permute-start(bf16[32,2304]{1,0:T(8,128)(2,1)S(1)} %get-tuple-element.61), channel_id=1, source_target_pairs={{0,16},{8,24},{16,0},{24,8},{1,17},{9,25},{17,1},{25,9},{2,18},{10... | collective-permute-start | bytes 442376 | tf_op jit(solution)/shard_map/ppermute | solution.py:362
  79.6 17.5 %collective-permute-start.14 = (bf16[32,2304]{1,0:T(8,128)(2,1)S(1)}, bf16[32,2304]{1,0:T(8,128)(2,1)S(1)}, u32[]{:S(2)}, u32[]{:S(2)}) collective-permute-start(bf16[32,2304]{1,0:T(8,128)(2,1)S(1)} %get-tuple-element.62), channel_id=1, source_target_pairs={{0,8},{8,0},{16,24},{24,16},{1,9},{9,1},{17,25},{25,17},{2,10},{10... | collective-permute-start | bytes 442376 | tf_op jit(solution)/shard_map/ppermute | solution.py:362
  81.0 15.1 %copy-start.9 = (s32[2,32]{1,0:T(2,128)S(1)}, s32[2,32]{1,0:T(2,128)}, u32[]{:S(2)}) copy-start(s32[2,32]{1,0:T(2,128)} %halo_ref.3) | copy-start | bytes 772
  83.8 7.0 %collective-permute-start.5 = (bf16[64,1024]{1,0:T(8,128)(2,1)S(1)}, bf16[64,1024]{1,0:T(8,128)(2,1)S(1)}, u32[]{:S(2)}, u32[]{:S(2)}) collective-permute-start(bf16[64,1024]{1,0:T(8,128)(2,1)S(1)} %get-tuple-element.47), channel_id=1, source_target_pairs={{0,1},{1,2},{2,3},{3,4},{4,5},{5,6},{6,7},{8,9},{9,10},{10,11},{11... | collective-permute-start | bytes 393224 | tf_op jit(solution)/shard_map/ppermute | solution.py:350
  88.9 7.2 %collective-permute-start.6 = (bf16[64,1024]{1,0:T(8,128)(2,1)S(1)}, bf16[64,1024]{1,0:T(8,128)(2,1)S(1)}, u32[]{:S(2)}, u32[]{:S(2)}) collective-permute-start(bf16[64,1024]{1,0:T(8,128)(2,1)S(1)} %get-tuple-element.48), channel_id=1, source_target_pairs={{1,0},{2,1},{3,2},{4,3},{5,4},{6,5},{7,6},{9,8},{10,9},{11,10},{12... | collective-permute-start | bytes 393224 | tf_op jit(solution)/shard_map/ppermute | solution.py:349

commit v2 on v1

v2 whole, which is shorter than its diff:
```python
import functools

import jax
import jax.numpy as jnp
from jax import lax
from jax.experimental import pallas as pl
from jax.experimental.pallas import tpu as pltpu
from jax.sharding import PartitionSpec as P

HEAD_DIM = 64
LANES = 128
ALPHA = 0.95
SOFTENING = 0.5
BF = jnp.bfloat16
F32 = jnp.float32
NN = (((1,), (0,)), ((), ()))
NT = (((1,), (1,)), ((), ()))
TN = (((0,), (0,)), ((), ()))


def mm(a, b, dims=NN):
    return lax.dot_general(a, b, dims, preferred_element_type=F32)


def call(body, out_shape, args, scratch=(), flops=0, nbytes=0, hbm=(), limit=40):
    return pl.pallas_call(
        body,
        out_shape=out_shape,
        in_specs=[
            pl.BlockSpec(memory_space=pltpu.HBM if i in hbm else pltpu.VMEM) for i in range(len(args))
        ],
        out_specs=jax.tree.map(lambda _: pl.BlockSpec(memory_space=pltpu.VMEM), out_shape),
        scratch_shapes=list(scratch),
        compiler_params=pltpu.CompilerParams(vmem_limit_bytes=limit * 1024 * 1024),
        cost_estimate=pl.CostEstimate(flops=flops, bytes_accessed=nbytes, transcendentals=0),
    )(*args)


def sds(shape, dtype):
    return jax.ShapeDtypeStruct(shape, dtype)


def one_hot_rows(rows, node_count):
    nodes = lax.broadcasted_iota(jnp.int32, (node_count, rows.shape[1]), 0).astype(rows.dtype)
    return (nodes == rows).astype(F32).astype(BF)


def start_copies(pairs, sems):
    copies = [pltpu.make_async_copy(src, dst, sems.at[i]) for i, (src, dst) in enumerate(pairs)]
    for copy in copies:
        copy.start()
    return copies


def pick_body(hidden_hbm, halo_hbm, hidden_ref, halo_ref, down_ref, up_ref, plus_ref, row_ref, sems):
    for copy in start_copies([(hidden_hbm, hidden_ref), (halo_hbm, halo_ref)], sems):
        copy.wait()
    members, nodes, _ = hidden_ref.shape
    rim = halo_ref.shape[1]
    for row, out_ref in ((0, down_ref), (1, up_ref)):
        hot = one_hot_rows(halo_ref[row : row + 1, :], nodes)
        for m in range(members):
            out_ref[m * rim : (m + 1) * rim, :] = mm(hot, hidden_ref[m], TN).astype(BF)
    for m in range(members):
        plus_ref[m * nodes : (m + 1) * nodes, :] = hidden_ref[m]
    row_ref[...] = jnp.zeros_like(row_ref)
    row_ref[0:2, 0:rim] = halo_ref[...].astype(F32)
    plus_ref[members * nodes :, :] = row_ref[...].astype(BF)


def prepare_body(
    hidden_ref, wo_hbm, hp_hbm, q_hbm, kvw_hbm, init_hbm, chw_hbm, lat_hbm, src_hbm, truth_hbm,
    kv_ref, pt_ref, p_ref, base_ref, weight_ref, wo_ref, hp_ref, q_ref, kvw_ref, src_ref, truth_ref,
    init_ref, chw_ref, lat_ref, chw_pad, hp_pad, sems,
):
    channels = hp_ref.shape[0]
    members, nodes, width = hidden_ref.shape
    w, h, q, k, i, c, l, s, t = start_copies(
        [
            (wo_hbm, wo_ref), (hp_hbm, hp_ref), (q_hbm, q_ref), (kvw_hbm, kvw_ref), (init_hbm, init_ref),
            (chw_hbm, chw_ref), (lat_hbm, lat_ref), (src_hbm, src_ref), (truth_hbm, truth_ref),
        ],
        sems,
    )
    hp_pad[...] = jnp.zeros_like(hp_pad)
    h.wait()
    hp_pad[0:channels, :] = hp_ref[...].astype(F32)
    hp_t = hp_pad[...].astype(BF)
    c.wait()
    l.wait()
    chw_pad[:, 0:channels] = jnp.broadcast_to(chw_ref[...], (8, channels))
    column = chw_pad[...].T
    weight_ref[...] = column[0:channels, 0:1] * lat_ref[...]
    q.wait()
    i.wait()
    base_ref[...] = mm(hp_t, q_ref[...], NT)
    base_ref[0:channels, :] = base_ref[0:channels, :] + init_ref[...]
    w.wait()
    p = mm(hp_t, wo_ref[...], NT)
    p_ref[...] = p.astype(BF)
    pt_ref[...] = p.T.astype(BF)
    k.wait()
    for m in range(members):
        kv_ref[m * nodes : (m + 1) * nodes, :] = mm(hidden_ref[m], kvw_ref[...]).astype(BF)
    s.wait()
    t.wait()


def split_heads(block):
    low = lax.broadcasted_iota(jnp.int32, block.shape, 1) < HEAD_DIM
    zero = jnp.zeros_like(block)
    return jnp.concatenate([jnp.where(low, block, zero), jnp.where(low, zero, block)], axis=0)


def forward_body(
    below_ref, above_ref, own_ref, kvw_ref, q_ref, src_ref, p_ref,
    kv_ref, gate_ref, slope_ref, merged_ref, part_ref, send_ref,
):
    members, ext, width2 = kv_ref.shape
    width = width2 // 2
    points = q_ref.shape[0]
    nodes = own_ref.shape[0] // members
    rim = below_ref.shape[0] // members
    halo = mm(jnp.concatenate([below_ref[...], above_ref[...]], axis=0), kvw_ref[...]).astype(BF)
    for m in range(members):
        kv_ref[m, 0:nodes, :] = own_ref[m * nodes : (m + 1) * nodes, :]
        kv_ref[m, nodes : nodes + rim, :] = halo[m * rim : (m + 1) * rim]
        kv_ref[m, nodes + rim : ext, :] = halo[(members + m) * rim : (members + m + 1) * rim]
    rows = lax.broadcasted_iota(jnp.int32, (ext, points), 0)
    mask = rows == src_ref[0:1, :]
    for e in range(1, src_ref.shape[0]):
        mask = mask | (rows == src_ref[e : e + 1, :])
    mask = mask.astype(F32)
    mask = jnp.concatenate([mask, mask], axis=0)
    scale = HEAD_DIM ** (-0.5)
    for pair in range(width // LANES):
        cols = slice(pair * LANES, (pair + 1) * LANES)
        vcols = slice(width + pair * LANES, width + (pair + 1) * LANES)
        q = q_ref[:, cols]
        for m in range(members):
            th = jnp.tanh(mm(split_heads(kv_ref[m, :, cols]), q, NT) * (0.5 * scale))
            gate = ((0.5 * th + 0.5) * mask).astype(BF)
            gate_ref[pair, m] = gate
            slope_ref[pair, m] = ((0.25 * scale) * mask * (1.0 - th * th)).astype(BF)
            merged_ref[m, cols, :] = mm(split_heads(kv_ref[m, :, vcols]), gate, TN).astype(BF)
    send_rows = send_ref.shape[1]
    for m in range(members):
        part = mm(p_ref[...], merged_ref[m])
        part_ref[m] = part
        send_ref[m] = part[0:send_rows].astype(BF)


def plane_body(all_ref, turned_ref, hot_ref):
    bands, nodes2, rim = all_ref.shape[0], turned_ref.shape[1] // all_ref.shape[0], hot_ref.shape[3]
    for band in range(bands):
        rows = all_ref[band, 0:nodes2, :].astype(F32)
        turned_ref[:, band * nodes2 : (band + 1) * nodes2] = rows.T.astype(BF)
        halo = all_ref[band, nodes2:, 0:LANES].astype(F32)
        for side in range(2):
            hot_ref[band, side] = one_hot_rows(halo[side : side + 1, 0:rim], hot_ref.shape[2])


def select_heads(block):
    half = block.shape[0] // 2
    low = lax.broadcasted_iota(jnp.int32, (half, block.shape[1]), 1) < HEAD_DIM
    return jnp.where(low, block[:half], block[half:])


def soft_slope(v):
    return v * lax.rsqrt(v * v + SOFTENING * SOFTENING)


def column_blocks(width, block):
    for pair in range(width // LANES):
        for side in range(2):
            flat = (2 * pair + side) * LANES
            yield pair, side, flat // block, flat % block


def backward_body(n_member, n_band, n_recv, *refs):
    recv_refs = refs[:n_recv]
    (part_ref, base_ref, truth_ref, weight_ref, pt_ref, merged_ref, gate_ref, slope_ref,
     kv_ref, q_ref, wo_ref, ng_ref, small_ref, grad, turned) = refs[n_recv:]
    members, ext, width2 = kv_ref.shape
    width = width2 // 2
    block = ng_ref.shape[2]
    channels = truth_ref.shape[0]
    total = members * n_member
    spread = (1.0 - (1.0 - ALPHA) / total) / (total * (total - 1))

    grad[...] = jnp.zeros_like(grad)
    own = [part_ref[m, 0:channels, :] for m in range(members)]
    for m in range(members):
        slopes = jnp.zeros_like(own[m])
        for k in range(members):
            if k != m:
                slopes = slopes + soft_slope(own[m] - own[k])
        for ref in recv_refs:
            for k in range(members):
                slopes = slopes + soft_slope(own[m] - ref[k, 0:channels, :].astype(F32))
        gap = soft_slope(own[m] + base_ref[0:channels, :] - truth_ref[...])
        grad[m, 0:channels, :] = (weight_ref[...] * (gap / total - spread * slopes)).astype(BF)

    merged_t = [mm(pt_ref[...], grad[m]).astype(BF) for m in range(members)]

    for pair, side, where, offset in column_blocks(width, block):
        cols = slice(pair * LANES, (pair + 1) * LANES)
        vcols = slice(width + pair * LANES, width + (pair + 1) * LANES)
        for m in range(members):
            dm = merged_t[m][cols]
            if side == 0:
                dgate = mm(split_heads(kv_ref[m, :, vcols]), dm)
                dscore = (dgate * slope_ref[pair, m].astype(F32)).astype(BF)
                result = mm(dscore, q_ref[:, cols])
            else:
                result = mm(gate_ref[pair, m], dm, NT)
            rows = slice(m * ext, (m + 1) * ext)
            ng_ref[where, rows, offset : offset + LANES] = select_heads(result).astype(BF)

    m_t = sum(mm(grad[m], merged_ref[m], NT) for m in range(members))
    head_t = sum(mm(grad[m], q_ref[...]) for m in range(members)) + mm(m_t.astype(BF), wo_ref[...])
    turned[...] = jnp.concatenate([m_t, head_t], axis=0).T
    rw = turned.shape[0] // (n_member * n_band)
    for band in range(n_band):
        starts = [(m * n_band + band) * rw for m in range(n_member)]
        small_ref[band] = jnp.concatenate([turned[i : i + rw, :] for i in starts], axis=0).astype(BF)


def block_body(rim, got_ref, turned_ref, hot_ref, out_ref, owned):
    bands, rows, block = got_ref.shape
    nodes = hot_ref.shape[2]
    ext = nodes + 2 * rim
    members = rows // ext
    for band in range(bands):
        for m in range(members):
            at = m * ext
            total = got_ref[band, at : at + nodes, :].astype(F32)
            if band > 0:
                total = total + mm(hot_ref[band, 0], got_ref[band - 1, at + nodes + rim : at + ext, :])
            if band < bands - 1:
                total = total + mm(hot_ref[band, 1], got_ref[band + 1, at + nodes : at + nodes + rim, :])
            first = (band * members + m) * nodes
            owned[first : first + nodes, :] = total.astype(BF)
    out_ref[...] = mm(turned_ref[...], owned[...]).astype(BF)


def extended_grad_body(members, nodes, rim, ng_ref, kvw_ref, own_ref, down_ref, up_ref):
    ext = nodes + 2 * rim
    width = kvw_ref.shape[0]
    block = ng_ref.shape[2]
    places = list(column_blocks(width, block))
    ordered = [p for p in places if p[1] == 0] + [p for p in places if p[1] == 1]
    for m in range(members):
        at = slice(m * ext, (m + 1) * ext)
        grads = jnp.concatenate([ng_ref[w, at, o : o + LANES] for _, _, w, o in ordered], axis=1)
        rows = mm(grads, kvw_ref[...], NT)
        own_ref[m] = rows[0:nodes]
        down_ref[m * rim : (m + 1) * rim, :] = rows[nodes : nodes + rim].astype(BF)
        up_ref[m * rim : (m + 1) * rim, :] = rows[nodes + rim :].astype(BF)


def hidden_body(own_ref, from_below_ref, from_above_ref, halo_ref, out_ref):
    members, nodes, _ = own_ref.shape
    rim = halo_ref.shape[1]
    low = one_hot_rows(halo_ref[0:1, :], nodes)
    high = one_hot_rows(halo_ref[1:2, :], nodes)
    for m in range(members):
        rows = slice(m * rim, (m + 1) * rim)
        out_ref[m] = own_ref[m] + mm(low, from_below_ref[rows, :]) + mm(high, from_above_ref[rows, :])


def finish_body(n_member, n_band, blocks_ref, small_ref, hp_ref, kv_ref, out_ref, head_ref):
    width = kv_ref.shape[1] // 2
    channels = hp_ref.shape[0]
    scale = 1.0 / (n_member * n_band)
    block = blocks_ref.shape[2]
    sums = []
    for band in range(n_band):
        total = blocks_ref[band].astype(F32)
        for m in range(1, n_member):
            total = total + blocks_ref[m * n_band + band].astype(F32)
        sums.append(total * scale)
    for pair, side, where, offset in column_blocks(width, block):
        at = side * width + pair * LANES
        kv_ref[:, at : at + LANES] = sums[where][:, offset : offset + LANES]
    total = small_ref[0].astype(F32)
    for m in range(1, n_member):
        total = total + small_ref[m].astype(F32)
    total = total * scale
    m_rows = total[:, 0:channels]
    high = m_rows.astype(BF)
    low = (m_rows - high.astype(F32)).astype(BF)
    out_ref[...] = mm(high, hp_ref[...]) + mm(low, hp_ref[...])
    head_ref[...] = total[:, LANES : LANES + channels]


def shards(
    n_member, n_band,
    hidden, queries, kv_weight, out_weight, head_projection, initial_state, truth,
    latitude_weight, channel_loss_weight, sources, halo_rows,
):
    members, nodes, width = hidden.shape
    points = queries.shape[0]
    channels = head_projection.shape[1]
    rim = halo_rows.shape[1]
    ext = nodes + 2 * rim
    pairs = width // LANES
    devices = n_member * n_band
    rw = width // devices
    block = 2 * width // n_band
    send_rows = -(-channels // 16) * 16
    to_above = [(i, i + 1) for i in range(n_band - 1)]
    to_below = [(i + 1, i) for i in range(n_band - 1)]

    own_hidden, halo, down, up, plus = call(
        pick_body,
        [sds(hidden.shape, BF), sds(halo_rows.shape, jnp.int32)]
        + [sds((members * rim, width), BF)] * 2
        + [sds((members * nodes + 16, width), BF)],
        (hidden, halo_rows),
        [pltpu.VMEM((16, width), F32), pltpu.SemaphoreType.DMA((2,))],
        flops=10**7, nbytes=10**6, hbm=(0, 1),
    )
    below = lax.ppermute(up, "band", to_above)
    above = lax.ppermute(down, "band", to_below)
    whole_plane = lax.all_gather(plus, "band", axis=0)

    args = (
        own_hidden, out_weight, head_projection.T, queries, kv_weight, initial_state,
        channel_loss_weight[None, :], latitude_weight[None, :], sources, truth,
    )
    own_kv, pt, p, base, weight, wo, hp, q, kvw, src, true = call(
        prepare_body,
        [
            sds((members * nodes, 2 * width), BF),
            sds((width, LANES), BF),
            sds((LANES, width), BF),
            sds((LANES, points), F32),
            sds((channels, points), F32),
        ]
        + [sds(args[i].shape, args[i].dtype) for i in (1, 2, 3, 4, 8, 9)],
        args,
        [
            pltpu.VMEM((channels, points), F32),
            pltpu.VMEM((1, channels), F32),
            pltpu.VMEM((1, points), F32),
            pltpu.VMEM((8, LANES), F32),
            pltpu.VMEM((LANES, width), F32),
            pltpu.SemaphoreType.DMA((9,)),
        ],
        flops=10**9, nbytes=8 * 10**6, hbm=tuple(range(1, 10)),
    )

    kv, gates, slopes, merged, part, sent = call(
        forward_body,
        [
            sds((members, ext, 2 * width), BF),
            sds((pairs, members, 2 * ext, points), BF),
            sds((pairs, members, 2 * ext, points), BF),
            sds((members, width, points), BF),
            sds((members, LANES, points), F32),
            sds((members, send_rows, points), BF),
        ],
        (below, above, own_kv, kvw, q, src, p),
        flops=4 * 10**9, nbytes=16 * 10**6,
    )

    received = [
        lax.ppermute(sent, "member", [(i, i ^ s) for i in range(n_member)]) for s in range(1, n_member)
    ]

    node_grad, small = call(
        functools.partial(backward_body, n_member, n_band, n_member - 1),
        [sds((n_band, members * ext, block), BF), sds((n_band, n_member * rw, 2 * LANES), BF)],
        (*received, part, base, true, weight, pt, merged, gates, slopes, kv, q, wo),
        [pltpu.VMEM((members, LANES, points), BF), pltpu.VMEM((width, 2 * LANES), F32)],
        flops=6 * 10**9, nbytes=24 * 10**6,
    )
    traded = lax.all_to_all(node_grad, "band", 0, 0, tiled=True)
    small = lax.all_to_all(small, "band", 0, 0, tiled=True)

    own_grad, back_down, back_up = call(
        functools.partial(extended_grad_body, members, nodes, rim),
        [sds((members, nodes, width), F32)] + [sds((members * rim, width), BF)] * 2,
        (node_grad, kvw),
        flops=2 * 10**9, nbytes=8 * 10**6,
    )
    from_above = lax.ppermute(back_down, "band", to_below)
    from_below = lax.ppermute(back_up, "band", to_above)

    turned, hot = call(
        plane_body,
        [sds((width, n_band * members * nodes), BF), sds((n_band, 2, nodes, rim), BF)],
        (whole_plane,),
        flops=10**8, nbytes=2 * 10**6,
    )
    kv_part = call(
        functools.partial(block_body, rim),
        sds((width, block), BF),
        (traded, turned, hot),
        [pltpu.VMEM((n_band * members * nodes, block), BF)],
        flops=10**9, nbytes=4 * 10**6,
    )
    blocks = lax.all_to_all(kv_part.reshape(devices, rw, block), ("member", "band"), 0, 0, tiled=True)
    small = jnp.sum(small.astype(F32), axis=0).astype(BF).reshape(n_member, rw, 2 * LANES)
    small = lax.all_to_all(small, "member", 0, 0, tiled=True)

    hidden_grad = call(
        hidden_body,
        sds((members, nodes, width), F32),
        (own_grad, from_below, from_above, halo),
        flops=10**7, nbytes=2 * 10**6,
    )
    kv_grad, out_grad, head_grad = call(
        functools.partial(finish_body, n_member, n_band),
        [sds((rw, 2 * width), F32), sds((rw, width), F32), sds((rw, channels), F32)],
        (blocks, small, hp),
        flops=10**7, nbytes=10**6,
    )
    return hidden_grad, kv_grad, out_grad, head_grad


def solution(mesh):
    placed = (
        P("member", "band", None),
        P("band", None),
        P(),
        P(),
        P(),
        P(None, "band"),
        P(None, "band"),
        P("band"),
        P(),
        P(None, "band"),
        P("band", None),
    )
    return jax.shard_map(
        functools.partial(shards, mesh.shape["member"], mesh.shape["band"]),
        mesh=mesh,
        in_specs=placed,
        out_specs=(
            P("member", "band", None),
            P(("member", "band"), None),
            P(("member", "band"), None),
            P(("member", "band"), None),
        ),
        check_vma=False,
    )
```

time: 98.7 us -> 120 us (1.22)
  the two profiles are of different devices: /device:TPU:3 before, /device:TPU:0 now
where the time goes in v2:
time: 120 us; the launch traced here: 118 us
  waiting for transfers between devices  28.8 us (24%)
  starting transfers between devices  22.5 us (19%)
  Pallas kernels  22.4 us (19%)
  blocking collectives  16.1 us (13%)
  between operations  14.2 us (12%)
  local copies, waits for them, and re-layouts  12.8 us (11%)
    pallas_call x9, Pallas kernels, call(): pl.pallas_call(body, out_shape=out_shape, in_specs=[pl.BlockSpec(memory_s...  22.4 us
    all_to_all x1, blocking collectives, shards(): small = lax.all_to_all(small, 'band', 0, 0, tiled=True)  16.1 us
    all_to_all x1, waiting for transfers between devices, shards(): traded = lax.all_to_all(node_grad, 'band', 0, 0, tiled=True)  14.6 us
    unnamed x26, local copies, waits for them, and re-layouts  12.8 us
    ppermute x3, waiting for transfers between devices, shards(): lax.ppermute(sent, 'member', [(i, i ^ s) for i in range(n_member)])  7.88 us
    ppermute x3, starting transfers between devices, shards(): lax.ppermute(sent, 'member', [(i, i ^ s) for i in range(n_member)])  5.07 us
    all_to_all x1, starting transfers between devices, shards(): small = lax.all_to_all(small, 'member', 0, 0, tiled=True)  4.07 us
    all_to_all x1, starting transfers between devices, shards(): traded = lax.all_to_all(node_grad, 'band', 0, 0, tiled=True)  3.56 us
  transfers between devices with their start and end apart: 11, of which 7 were waited for; matrix products, arithmetic and copies ran while one was open for 1% of the time, Pallas kernels for 17%

profile of v2, /device:TPU:0, one launch (start us, length us, event | category | flops | bytes accessed | tf_op | source)
XLA Modules:
  0.0 117.6 jit_solution(12714675232997366353)
XLA Ops:
  7.2 0.0 all-gather.3.cloned.1.call-start
  7.2 0.9 copy-done.3
  8.2 0.7 copy-done.8
  8.8 0.9 shard_map.138
  9.8 0.0 all-gather.3.cloned.1.call-update
  9.8 2.4 %collective-permute-start = (bf16[64,1024]{1,0:T(8,128)(2,1)S(1)}, bf16[64,1024]{1,0:T(8,128)(2,1)S(1)}, u32[]{:S(2)}, u32[]{:S(2)}) collective-permute-start(bf16[64,1024]{1,0:T(8,128)(2,1)S(1)} %get-tuple-element.36), channel_id=1, source_target_pairs={{0,1},{1,2},{2,3},{3,4},{4,5},{5,6},{6,7},{8,9},{9,10},{10,11},{11... | collective-permute-start | bytes 393224 | tf_op jit(solution)/shard_map/ppermute | solution.py:324
  12.2 1.3 %collective-permute-start.1 = (bf16[64,1024]{1,0:T(8,128)(2,1)S(1)}, bf16[64,1024]{1,0:T(8,128)(2,1)S(1)}, u32[]{:S(2)}, u32[]{:S(2)}) collective-permute-start(bf16[64,1024]{1,0:T(8,128)(2,1)S(1)} %get-tuple-element.37), channel_id=1, source_target_pairs={{1,0},{2,1},{3,2},{4,3},{5,4},{6,5},{7,6},{9,8},{10,9},{11,10},{12... | collective-permute-start | bytes 393224 | tf_op jit(solution)/shard_map/ppermute | solution.py:325
  13.5 0.0 copy-start.1
  13.5 1.6 %copy-done.1 = bf16[1024,1024]{1,0:T(8,128)(2,1)S(1)} copy-done((bf16[1024,1024]{1,0:T(8,128)(2,1)S(1)}, bf16[1024,1024]{1,0:T(8,128)(2,1)}, u32[]{:S(2)}) %copy-start.1) | copy-done | bytes 2097176
  15.1 1.0 copy-done.2
  16.1 0.9 copy-done.4
  17.0 0.9 copy-done.5
  17.9 0.9 copy-done.6
  18.8 0.7 copy-done.7
  19.5 0.7 copy-done.9
  20.2 0.7 copy-done.10
  20.9 4.4 %shard_map.139 = (bf16[128,2048]{1,0:T(8,128)(2,1)S(1)}, bf16[1024,128]{1,0:T(8,128)(2,1)S(1)}, bf16[128,1024]{1,0:T(8,128)(2,1)S(1)}, f32[128,256]{1,0:T(8,128)...) custom-call(bf16[2,64,1024]{2,1,0:T(8,128)(2,1)S(1)} %get-tuple-elem, ...), custom_call_target="tpu_custom_call" | custom-call | flops 1000000000 | bytes 8000000 | tf_op jit(solution)/shard_map/pallas_call | solution.py:26
  25.3 0.0 copy-start.11
  25.3 0.0 collective-permute-done.below_ref
  25.3 0.0 collective-permute-done.1.above_ref
  25.3 5.0 %shard_map.140 = (bf16[2,128,2048]{2,1,0:T(8,128)(2,1)S(1)}, bf16[8,2,256,256]{3,2,1,0:T(8,128)(2,1)S(1)}, bf16[8,2,256,256]{3,2,1,0:T(8,128)(2,1)S(1)}, bf16[2,...) custom-call(bf16[64,1024]{1,0:T(8,128)(2,1)S(1)} %collective-permute-done.below_ref, ...), custom_call_target="tpu_custom_call" | custom-call | flops 4000000000 | bytes 16000000 | tf_op jit(solution)/shard_map/pallas_call | solution.py:26
  30.3 0.0 copy-done.11
  30.3 2.5 %collective-permute-start.2 = (bf16[2,112,256]{2,1,0:T(8,128)(2,1)S(1)}, bf16[2,112,256]{2,1,0:T(8,128)(2,1)S(1)}, u32[]{:S(2)}, u32[]{:S(2)}) collective-permute-start(bf16[2,112,256]{2,1,0:T(8,128)(2,1)S(1)} %get-tuple-element.44), channel_id=1, source_target_pairs={{0,8},{8,0},{16,24},{24,16},{1,9},{9,1},{17,25},{25,17},{2,10},{10... | collective-permute-start | bytes 344072 | tf_op jit(solution)/shard_map/ppermute | solution.py:369
  32.8 2.6 %collective-permute-start.3 = (bf16[2,112,256]{2,1,0:T(8,128)(2,1)S(1)}, bf16[2,112,256]{2,1,0:T(8,128)(2,1)S(1)}, u32[]{:S(2)}, u32[]{:S(2)}) collective-permute-start(bf16[2,112,256]{2,1,0:T(8,128)(2,1)S(1)} %get-tuple-element.44), channel_id=1, source_target_pairs={{0,16},{8,24},{16,0},{24,8},{1,17},{9,25},{17,1},{25,9},{2,18},{10... | collective-permute-start | bytes 344072 | tf_op jit(solution)/shard_map/ppermute | solution.py:369
  35.4 0.0 collective-permute-start.4
  35.4 0.2 collective-permute-done.2.refs_0_
  35.6 4.3 %collective-permute-done.3.refs_1_ = bf16[2,112,256]{2,1,0:T(8,128)(2,1)S(1)} collective-permute-done((bf16[2,112,256]{2,1,0:T(8,128)(2,1)S(1)}, bf16[2,112,256]{2,1,0:T(8,128)(2,1)S(1)}, u32[]{:S(2)}, u32[]{:S(2)}) %collective-permute-start.3) | collective-permute-done | bytes 114720 | tf_op jit(solution)/shard_map/ppermute | solution.py:369
  39.8 3.4 %collective-permute-done.4.refs_2_ = bf16[2,112,256]{2,1,0:T(8,128)(2,1)S(1)} collective-permute-done((bf16[2,112,256]{2,1,0:T(8,128)(2,1)S(1)}, bf16[2,112,256]{2,1,0:T(8,128)(2,1)S(1)}, u32[]{:S(2)}, u32[]{:S(2)}) %collective-permute-start.4) | collective-permute-done | bytes 114720 | tf_op jit(solution)/shard_map/ppermute | solution.py:369
  43.3 3.5 %shard_map.141 = (bf16[8,256,256]{2,1,0:T(8,128)(2,1)}, bf16[8,128,256]{2,1,0:T(8,128)(2,1)S(1)}) custom-call(bf16[2,112,256]{2,1,0:T(8,128)(2,1)S(1)} %collective-permute-done.2.refs_0_, bf16[2,112,256]{2,1,0:T(8,128)(2,1)S(1)} %collective-permute-done.3.refs_1_, bf16[2,112,256]{2,1,0:T(8,128)(2,1)S(1)} %collective-permute-done.4.refs_2_, ...), custom_call_target="tpu_custom_call" | custom-call | flops 6000000000 | bytes 24000000 | tf_op jit(solution)/shard_map/pallas_call | solution.py:26
  46.8 16.1 %all_to_all.20 = bf16[8,128,256]{2,1,0:T(8,128)(2,1)S(1)} all-to-all(bf16[8,128,256]{2,1,0:T(8,128)(2,1)S(1)} %get-tuple-element.63), channel_id=1, replica_groups=mesh['member'=4,'band'=8] {'band'}, dimensions={0} | all-to-all | bytes 1048576 | tf_op jit(solution)/shard_map/all_to_all | solution.py:380
  62.9 3.6 %all-to-all-start = ((bf16[8,256,256]{2,1,0:T(8,128)(2,1)}), bf16[8,256,256]{2,1,0:T(8,128)(2,1)S(1)}, u32[]{:S(2)}, u32[]{:S(2)}) async-start(bf16[8,256,256]{2,1,0:T(8,128)(2,1)} %get-tuple-element.55.ng_ref), calls=%async_computation | async-start | bytes 2097152 | tf_op jit(solution)/shard_map/all_to_all | solution.py:379
  66.5 0.7 reduce_sum.12
  67.2 14.6 %all-to-all-done.got_ref = bf16[8,256,256]{2,1,0:T(8,128)(2,1)S(1)} async-done(((bf16[8,256,256]{2,1,0:T(8,128)(2,1)}), bf16[8,256,256]{2,1,0:T(8,128)(2,1)S(1)}, u32[]{:S(2)}, u32[]{:S(2)}) %all-to-all-start) | async-done | bytes 1048608 | tf_op jit(solution)/shard_map/all_to_all | solution.py:379
  81.8 4.1 %all-to-all-start.3 = ((bf16[4,32,256]{2,1,0:T(8,128)(2,1)}), bf16[4,32,256]{2,1,0:T(8,128)(2,1)S(1)}, u32[]{:S(2)}, u32[]{:S(2)}) async-start(bf16[4,32,256]{2,1,0:T(8,128)(2,1)} %bitcast.5), calls=%async_computation.3 | async-start | bytes 131072 | tf_op jit(solution)/shard_map/all_to_all | solution.py:406
  85.9 1.7 %copy-done = bf16[1152,1024]{1,0:T(8,128)(2,1)S(1)} copy-done((bf16[1152,1024]{1,0:T(8,128)(2,1)S(1)}, bf16[1152,1024]{1,0:T(8,128)(2,1)}, u32[]{:S(2)}) %copy-start) | copy-done | bytes 2359320
  87.6 0.7 shard_map.144
  88.3 1.8 %shard_map.145 = bf16[1024,256]{1,0:T(8,128)(2,1)} custom-call(bf16[8,256,256]{2,1,0:T(8,128)(2,1)S(1)} %all-to-all-done.got_ref, bf16[1024,1024]{1,0:T(8,128)(2,1)S(1)} %get-tuple-element.61.turned_ref, bf16[8,2,64,32]{3,2,1,0:T(8,128)(2,1)S(1)} %get-tuple-element.62.hot_ref), custom_call_target="tpu_custom_call" | custom-call | flops 1000000000 | bytes 4000000 | tf_op jit(solution)/shard_map/pallas_call | solution.py:26
  90.1 1.5 %all-to-all-done.3.small_ref = bf16[4,32,256]{2,1,0:T(8,128)(2,1)S(1)} async-done(((bf16[4,32,256]{2,1,0:T(8,128)(2,1)}), bf16[4,32,256]{2,1,0:T(8,128)(2,1)S(1)}, u32[]{:S(2)}, u32[]{:S(2)}) %all-to-all-start.3) | async-done | bytes 65568 | tf_op jit(solution)/shard_map/all_to_all | solution.py:406
  91.6 2.7 %all-to-all-start.1 = ((bf16[32,32,256]{2,1,0:T(8,128)(2,1)}), bf16[32,32,256]{2,1,0:T(8,128)(2,1)S(1)}, u32[]{:S(2)}, u32[]{:S(2)}) async-start(bf16[32,32,256]{2,1,0:T(8,128)(2,1)} %bitcast.4), calls=%async_computation.1 | async-start | bytes 1048576 | tf_op jit(solution)/shard_map/all_to_all | solution.py:404
  94.3 2.2 %copy-done.12 = bf16[1024,2048]{1,0:T(8,128)(2,1)S(1)} copy-done((bf16[1024,2048]{1,0:T(8,128)(2,1)S(1)}, bf16[1024,2048]{1,0:T(8,128)(2,1)}, u32[]{:S(2)}) %copy-start.12) | copy-done | bytes 4194328
  96.5 4.1 %shard_map.142 = (f32[2,64,1024]{2,1,0:T(8,128)S(1)}, bf16[64,1024]{1,0:T(8,128)(2,1)S(1)}, bf16[64,1024]{1,0:T(8,128)(2,1)S(1)}) custom-call(bf16[8,256,256]{2,1,0:T(8,128)(2,1)} %get-tuple-element.55.ng_ref, bf16[1024,2048]{1,0:T(8,128)(2,1)S(1)} %copy-done.12), custom_call_target="tpu_custom_call" | custom-call | flops 2000000000 | bytes 8000000 | tf_op jit(solution)/shard_map/pallas_call | solution.py:26
  100.5 2.2 %collective-permute-start.5 = (bf16[64,1024]{1,0:T(8,128)(2,1)S(1)}, bf16[64,1024]{1,0:T(8,128)(2,1)S(1)}, u32[]{:S(2)}, u32[]{:S(2)}) collective-permute-start(bf16[64,1024]{1,0:T(8,128)(2,1)S(1)} %get-tuple-element.57), channel_id=1, source_target_pairs={{0,1},{1,2},{2,3},{3,4},{4,5},{5,6},{6,7},{8,9},{9,10},{10,11},{11... | collective-permute-start | bytes 393224 | tf_op jit(solution)/shard_map/ppermute | solution.py:389
  102.7 1.3 %collective-permute-start.6 = (bf16[64,1024]{1,0:T(8,128)(2,1)S(1)}, bf16[64,1024]{1,0:T(8,128)(2,1)S(1)}, u32[]{:S(2)}, u32[]{:S(2)}) collective-permute-start(bf16[64,1024]{1,0:T(8,128)(2,1)S(1)} %get-tuple-element.58), channel_id=1, source_target_pairs={{1,0},{2,1},{3,2},{4,3},{5,4},{6,5},{7,6},{9,8},{10,9},{11,10},{12... | collective-permute-start | bytes 393224 | tf_op jit(solution)/shard_map/ppermute | solution.py:388
  104.0 0.0 collective-permute-done.5.from_below_ref
  104.0 3.1 %collective-permute-done.6.from_above_ref = bf16[64,1024]{1,0:T(8,128)(2,1)S(1)} collective-permute-done((bf16[64,1024]{1,0:T(8,128)(2,1)S(1)}, bf16[64,1024]{1,0:T(8,128)(2,1)S(1)}, u32[]{:S(2)}, u32[]{:S(2)}) %collective-permute-start.6) | collective-permute-done | bytes 131104 | tf_op jit(solution)/shard_map/ppermute | solution.py:388
  107.1 1.1 shard_map.143
  108.2 1.7 %all-to-all-done.1.blocks_ref = bf16[32,32,256]{2,1,0:T(8,128)(2,1)S(1)} async-done(((bf16[32,32,256]{2,1,0:T(8,128)(2,1)}), bf16[32,32,256]{2,1,0:T(8,128)(2,1)S(1)}, u32[]{:S(2)}, u32[]{:S(2)}) %all-to-all-start.1) | async-done | bytes 524320 | tf_op jit(solution)/shard_map/all_to_all | solution.py:404
  109.8 0.9 shard_map.146
  (12 shorter events, 0.0 us)
Async XLA Ops:
  7.2 78.7 %all-gather.3.cloned.1.call-start = ((), (), s32[]{:S(2)}) async-start(), calls=%async_computation.4 | async-start | bytes 2654208 | tf_op jit(solution)/shard_map/all_gather | solution.py:326
  7.2 1.0 copy-start.3
  8.2 0.7 copy-start.8
  9.8 15.5 %collective-permute-start = (bf16[64,1024]{1,0:T(8,128)(2,1)S(1)}, bf16[64,1024]{1,0:T(8,128)(2,1)S(1)}, u32[]{:S(2)}, u32[]{:S(2)}) collective-permute-start(bf16[64,1024]{1,0:T(8,128)(2,1)S(1)} %get-tuple-element.36), channel_id=1, source_target_pairs={{0,1},{1,2},{2,3},{3,4},{4,5},{5,6},{6,7},{8,9},{9,10},{10,11},{11... | collective-permute-start | bytes 393224 | tf_op jit(solution)/shard_map/ppermute | solution.py:324
  12.2 13.1 %collective-permute-start.1 = (bf16[64,1024]{1,0:T(8,128)(2,1)S(1)}, bf16[64,1024]{1,0:T(8,128)(2,1)S(1)}, u32[]{:S(2)}, u32[]{:S(2)}) collective-permute-start(bf16[64,1024]{1,0:T(8,128)(2,1)S(1)} %get-tuple-element.37), channel_id=1, source_target_pairs={{1,0},{2,1},{3,2},{4,3},{5,4},{6,5},{7,6},{9,8},{10,9},{11,10},{12... | collective-permute-start | bytes 393224 | tf_op jit(solution)/shard_map/ppermute | solution.py:325
  13.5 1.6 %copy-start.1 = (bf16[1024,1024]{1,0:T(8,128)(2,1)S(1)}, bf16[1024,1024]{1,0:T(8,128)(2,1)}, u32[]{:S(2)}) copy-start(bf16[1024,1024]{1,0:T(8,128)(2,1)} %wo_hbm.1) | copy-start | bytes 6291460
  15.1 1.0 copy-start.2
  16.1 0.9 copy-start.4
  17.0 0.9 copy-start.5
  17.9 0.9 copy-start.6
  18.8 0.7 copy-start.7
  19.5 0.7 copy-start.9
  20.2 0.7 copy-start.10
  25.3 5.0 %copy-start.11 = (bf16[1024,2048]{1,0:T(8,128)(2,1)}, bf16[1024,2048]{1,0:T(8,128)(2,1)S(1)}, u32[]{:S(2)}) copy-start(bf16[1024,2048]{1,0:T(8,128)(2,1)S(1)} %get-tuple-element.40.kvw_ref) | copy-start | bytes 12582916
  30.3 5.2 %collective-permute-start.2 = (bf16[2,112,256]{2,1,0:T(8,128)(2,1)S(1)}, bf16[2,112,256]{2,1,0:T(8,128)(2,1)S(1)}, u32[]{:S(2)}, u32[]{:S(2)}) collective-permute-start(bf16[2,112,256]{2,1,0:T(8,128)(2,1)S(1)} %get-tuple-element.44), channel_id=1, source_target_pairs={{0,8},{8,0},{16,24},{24,16},{1,9},{9,1},{17,25},{25,17},{2,10},{10... | collective-permute-start | bytes 344072 | tf_op jit(solution)/shard_map/ppermute | solution.py:369
  32.8 7.1 %collective-permute-start.3 = (bf16[2,112,256]{2,1,0:T(8,128)(2,1)S(1)}, bf16[2,112,256]{2,1,0:T(8,128)(2,1)S(1)}, u32[]{:S(2)}, u32[]{:S(2)}) collective-permute-start(bf16[2,112,256]{2,1,0:T(8,128)(2,1)S(1)} %get-tuple-element.44), channel_id=1, source_target_pairs={{0,16},{8,24},{16,0},{24,8},{1,17},{9,25},{17,1},{25,9},{2,18},{10... | collective-permute-start | bytes 344072 | tf_op jit(solution)/shard_map/ppermute | solution.py:369
  35.4 7.9 %collective-permute-start.4 = (bf16[2,112,256]{2,1,0:T(8,128)(2,1)S(1)}, bf16[2,112,256]{2,1,0:T(8,128)(2,1)S(1)}, u32[]{:S(2)}, u32[]{:S(2)}) collective-permute-start(bf16[2,112,256]{2,1,0:T(8,128)(2,1)S(1)} %get-tuple-element.44), channel_id=1, source_target_pairs={{0,24},{8,16},{16,8},{24,0},{1,25},{9,17},{17,9},{25,1},{2,26},{10... | collective-permute-start | bytes 344072 | tf_op jit(solution)/shard_map/ppermute | solution.py:369
  62.9 18.9 %all-to-all-start = ((bf16[8,256,256]{2,1,0:T(8,128)(2,1)}), bf16[8,256,256]{2,1,0:T(8,128)(2,1)S(1)}, u32[]{:S(2)}, u32[]{:S(2)}) async-start(bf16[8,256,256]{2,1,0:T(8,128)(2,1)} %get-tuple-element.55.ng_ref), calls=%async_computation | async-start | bytes 2097152 | tf_op jit(solution)/shard_map/all_to_all | solution.py:379
  81.8 9.8 %all-to-all-start.3 = ((bf16[4,32,256]{2,1,0:T(8,128)(2,1)}), bf16[4,32,256]{2,1,0:T(8,128)(2,1)S(1)}, u32[]{:S(2)}, u32[]{:S(2)}) async-start(bf16[4,32,256]{2,1,0:T(8,128)(2,1)} %bitcast.5), calls=%async_computation.3 | async-start | bytes 131072 | tf_op jit(solution)/shard_map/all_to_all | solution.py:406
  85.9 1.7 %copy-start = (bf16[1152,1024]{1,0:T(8,128)(2,1)S(1)}, bf16[1152,1024]{1,0:T(8,128)(2,1)}, u32[]{:S(2)}) copy-start(bf16[1152,1024]{1,0:T(8,128)(2,1)} %all-gather.3.cloned.1.call-done) | copy-start | bytes 7077892
  91.6 18.2 %all-to-all-start.1 = ((bf16[32,32,256]{2,1,0:T(8,128)(2,1)}), bf16[32,32,256]{2,1,0:T(8,128)(2,1)S(1)}, u32[]{:S(2)}, u32[]{:S(2)}) async-start(bf16[32,32,256]{2,1,0:T(8,128)(2,1)} %bitcast.4), calls=%async_computation.1 | async-start | bytes 1048576 | tf_op jit(solution)/shard_map/all_to_all | solution.py:404
  94.3 2.2 %copy-start.12 = (bf16[1024,2048]{1,0:T(8,128)(2,1)S(1)}, bf16[1024,2048]{1,0:T(8,128)(2,1)}, u32[]{:S(2)}) copy-start(bf16[1024,2048]{1,0:T(8,128)(2,1)} %copy-done.11) | copy-start | bytes 12582916
  100.5 3.5 %collective-permute-start.5 = (bf16[64,1024]{1,0:T(8,128)(2,1)S(1)}, bf16[64,1024]{1,0:T(8,128)(2,1)S(1)}, u32[]{:S(2)}, u32[]{:S(2)}) collective-permute-start(bf16[64,1024]{1,0:T(8,128)(2,1)S(1)} %get-tuple-element.57), channel_id=1, source_target_pairs={{0,1},{1,2},{2,3},{3,4},{4,5},{5,6},{6,7},{8,9},{9,10},{10,11},{11... | collective-permute-start | bytes 393224 | tf_op jit(solution)/shard_map/ppermute | solution.py:389
  102.7 4.4 %collective-permute-start.6 = (bf16[64,1024]{1,0:T(8,128)(2,1)S(1)}, bf16[64,1024]{1,0:T(8,128)(2,1)S(1)}, u32[]{:S(2)}, u32[]{:S(2)}) collective-permute-start(bf16[64,1024]{1,0:T(8,128)(2,1)S(1)} %get-tuple-element.58), channel_id=1, source_target_pairs={{1,0},{2,1},{3,2},{4,3},{5,4},{6,5},{7,6},{9,8},{10,9},{11,10},{12... | collective-permute-start | bytes 393224 | tf_op jit(solution)/shard_map/ppermute | solution.py:388
Sparse Core Ops, SparseCore 0:
  10.5 31.7 all-gather.2

commit v3 on v2

v3 whole, which is shorter than its diff:
```python
import functools

import jax
import jax.numpy as jnp
from jax import lax
from jax.experimental import pallas as pl
from jax.experimental.pallas import tpu as pltpu
from jax.sharding import PartitionSpec as P

HEAD_DIM = 64
LANES = 128
KV_COPIES = 4
ALPHA = 0.95
SOFTENING = 0.5
BF = jnp.bfloat16
F32 = jnp.float32
NN = (((1,), (0,)), ((), ()))
NT = (((1,), (1,)), ((), ()))
TN = (((0,), (0,)), ((), ()))


def mm(a, b, dims=NN):
    return lax.dot_general(a, b, dims, preferred_element_type=F32)


def call(body, out_shape, args, scratch=(), hbm=(), limit=40):
    args = [pltpu.with_memory_space_constraint(x, pltpu.HBM) if i in hbm else x for i, x in enumerate(args)]
    return pl.pallas_call(
        body,
        out_shape=out_shape,
        in_specs=[
            pl.BlockSpec(memory_space=pltpu.HBM if i in hbm else pltpu.VMEM) for i in range(len(args))
        ],
        out_specs=jax.tree.map(lambda _: pl.BlockSpec(memory_space=pltpu.VMEM), out_shape),
        scratch_shapes=list(scratch),
        compiler_params=pltpu.CompilerParams(vmem_limit_bytes=limit * 1024 * 1024),
        cost_estimate=pl.CostEstimate(flops=1, bytes_accessed=1, transcendentals=0),
    )(*args)


def sds(shape, dtype):
    return jax.ShapeDtypeStruct(shape, dtype)


def one_hot_rows(rows, node_count):
    nodes = lax.broadcasted_iota(jnp.int32, (node_count, rows.shape[1]), 0).astype(rows.dtype)
    return (nodes == rows).astype(F32).astype(BF)


def start_copies(pairs, sems):
    copies = [pltpu.make_async_copy(src, dst, sems.at[i]) for i, (src, dst) in enumerate(pairs)]
    for copy in copies:
        copy.start()
    return copies


def pick_body(hidden_hbm, halo_hbm, hidden_ref, halo_ref, down_ref, up_ref, sems):
    for copy in start_copies([(hidden_hbm, hidden_ref), (halo_hbm, halo_ref)], sems):
        copy.wait()
    members, nodes, _ = hidden_ref.shape
    rim = halo_ref.shape[1]
    for row, out_ref in ((0, down_ref), (1, up_ref)):
        hot = one_hot_rows(halo_ref[row : row + 1, :], nodes)
        for m in range(members):
            out_ref[m * rim : (m + 1) * rim, :] = mm(hot, hidden_ref[m], TN).astype(BF)


def prepare_body(
    hidden_ref, wo_hbm, hp_hbm, q_hbm, kvw_hbm, init_hbm, chw_hbm, lat_hbm, src_hbm, truth_hbm,
    kv_ref, pt_ref, p_ref, base_ref, weight_ref, wo_ref, hp_ref, q_ref, kvw_ref, src_ref, truth_ref,
    init_ref, chw_ref, lat_ref, chw_pad, hp_pad, sems,
):
    channels = hp_ref.shape[0]
    members, nodes, width = hidden_ref.shape
    step = kvw_ref.shape[1] // KV_COPIES
    pieces = [slice(j * step, (j + 1) * step) for j in range(KV_COPIES)]
    h, q, i, w, c, l, s, t, *k = start_copies(
        [
            (hp_hbm, hp_ref), (q_hbm, q_ref), (init_hbm, init_ref), (wo_hbm, wo_ref), (chw_hbm, chw_ref),
            (lat_hbm, lat_ref), (src_hbm, src_ref), (truth_hbm, truth_ref),
        ]
        + [(kvw_hbm.at[:, piece], kvw_ref.at[:, piece]) for piece in pieces],
        sems,
    )
    hp_pad[...] = jnp.zeros_like(hp_pad)
    h.wait()
    hp_pad[0:channels, :] = hp_ref[...].astype(F32)
    hp_t = hp_pad[...].astype(BF)
    c.wait()
    l.wait()
    chw_pad[:, 0:channels] = jnp.broadcast_to(chw_ref[...], (8, channels))
    column = chw_pad[...].T
    weight_ref[...] = column[0:channels, 0:1] * lat_ref[...]
    q.wait()
    i.wait()
    base_ref[...] = mm(hp_t, q_ref[...], NT)
    base_ref[0:channels, :] = base_ref[0:channels, :] + init_ref[...]
    w.wait()
    p = mm(hp_t, wo_ref[...], NT)
    p_ref[...] = p.astype(BF)
    pt_ref[...] = p.T.astype(BF)
    hidden = jnp.concatenate([hidden_ref[m] for m in range(members)], axis=0)
    for piece, copy in zip(pieces, k):
        copy.wait()
        kv_ref[:, piece] = mm(hidden, kvw_ref[:, piece]).astype(BF)
    s.wait()
    t.wait()


def split_heads(block):
    low = lax.broadcasted_iota(jnp.int32, block.shape, 1) < HEAD_DIM
    zero = jnp.zeros_like(block)
    return jnp.concatenate([jnp.where(low, block, zero), jnp.where(low, zero, block)], axis=0)


def forward_body(
    below_ref, above_ref, own_ref, kvw_ref, q_ref, src_ref, p_ref,
    kv_ref, gate_ref, slope_ref, merged_ref, part_ref, send_ref,
):
    members, ext, width2 = kv_ref.shape
    width = width2 // 2
    points = q_ref.shape[0]
    nodes = own_ref.shape[0] // members
    rim = below_ref.shape[0] // members
    halo = mm(jnp.concatenate([below_ref[...], above_ref[...]], axis=0), kvw_ref[...]).astype(BF)
    for m in range(members):
        kv_ref[m, 0:nodes, :] = own_ref[m * nodes : (m + 1) * nodes, :]
        kv_ref[m, nodes : nodes + rim, :] = halo[m * rim : (m + 1) * rim]
        kv_ref[m, nodes + rim : ext, :] = halo[(members + m) * rim : (members + m + 1) * rim]
    rows = lax.broadcasted_iota(jnp.int32, (ext, points), 0)
    mask = rows == src_ref[0:1, :]
    for e in range(1, src_ref.shape[0]):
        mask = mask | (rows == src_ref[e : e + 1, :])
    mask = mask.astype(F32)
    mask = jnp.concatenate([mask, mask], axis=0)
    scale = HEAD_DIM ** (-0.5)
    for pair in range(width // LANES):
        cols = slice(pair * LANES, (pair + 1) * LANES)
        vcols = slice(width + pair * LANES, width + (pair + 1) * LANES)
        q = q_ref[:, cols]
        for m in range(members):
            th = jnp.tanh(mm(split_heads(kv_ref[m, :, cols]), q, NT) * (0.5 * scale))
            gate = ((0.5 * th + 0.5) * mask).astype(BF)
            gate_ref[pair, m] = gate
            slope_ref[pair, m] = ((0.25 * scale) * mask * (1.0 - th * th)).astype(BF)
            merged_ref[m, cols, :] = mm(split_heads(kv_ref[m, :, vcols]), gate, TN).astype(BF)
    send_rows = send_ref.shape[1]
    for m in range(members):
        part = mm(p_ref[...], merged_ref[m])
        part_ref[m] = part
        send_ref[m] = part[0:send_rows].astype(BF)


def chip_orders(chips):
    bits = range(chips.bit_length() - 1)
    orders = []
    for order in (list(bits), list(bits)[::-1]):
        orders.append(sorted(range(chips), key=lambda s: [-(s >> bit & 1) for bit in order]))
    return orders


def destination_rows(member, band, n_member, n_band, rw):
    chip, core = band // 2, band % 2
    for rel_core in (1, 0):
        for rel_chip in range(n_band // 2):
            to_band = (chip ^ rel_chip) * 2 + (core ^ rel_core)
            for rel_member in range(n_member):
                yield pl.multiple_of(((member ^ rel_member) * n_band + to_band) * rw, rw)


def reorder(src_ref, n_member, n_band):
    rw = src_ref.shape[0] // (n_member * n_band)
    member, band = lax.axis_index("member"), lax.axis_index("band")
    starts = destination_rows(member, band, n_member, n_band, rw)
    return jnp.concatenate([src_ref[pl.ds(start, rw), :] for start in starts], axis=0)


def store_parts(rows, chips, half, at, out_refs):
    block = rows.shape[0] // (2 * chips)
    for core, ref in enumerate(out_refs):
        for place, chip in enumerate(chip_orders(chips)[half]):
            start = (core * chips + chip) * block
            ref[place * block : (place + 1) * block, at : at + rows.shape[1]] = rows[start : start + block]


def transpose_body(n_member, n_band, hidden_ref, below_ref, above_ref, out_ref, turned):
    members, nodes, _ = hidden_ref.shape
    rim = below_ref.shape[0] // members
    parts = []
    for m in range(members):
        parts.append(hidden_ref[m])
        parts.append(below_ref[m * rim : (m + 1) * rim, :])
        parts.append(above_ref[m * rim : (m + 1) * rim, :])
    turned[...] = jnp.concatenate(parts, axis=0).astype(F32).T
    out_ref[...] = reorder(turned, n_member, n_band).astype(BF)


def select_heads(block):
    half = block.shape[0] // 2
    low = lax.broadcasted_iota(jnp.int32, (half, block.shape[1]), 1) < HEAD_DIM
    return jnp.where(low, block[:half], block[half:])


def soft_slope(v):
    return v * lax.rsqrt(v * v + SOFTENING * SOFTENING)


def kv_products(chips, ext_ref, ng_ref, out_refs):
    step = ng_ref.shape[1] // 2
    for half in range(2):
        product = mm(ext_ref[...], ng_ref[:, half * step : (half + 1) * step]).astype(BF)
        store_parts(product, chips, half, half * (out_refs[0].shape[1] // 2), out_refs)


def value_body(n_member, n_band, *refs):
    recv_refs = refs[: n_member - 1]
    part_ref, base_ref, truth_ref, weight_ref, pt_ref, gate_ref, ext_ref = refs[n_member - 1 : n_member + 6]
    grad_ref, dm_ref, ng_ref, *out_refs = refs[n_member + 6 :]
    members, width, _ = dm_ref.shape
    ext = ng_ref.shape[0] // members
    channels = truth_ref.shape[0]
    total = members * n_member
    spread = (1.0 - (1.0 - ALPHA) / total) / (total * (total - 1))

    grad_ref[...] = jnp.zeros_like(grad_ref)
    own = [part_ref[m, 0:channels, :] for m in range(members)]
    for m in range(members):
        slopes = jnp.zeros_like(own[m])
        for k in range(members):
            if k != m:
                slopes = slopes + soft_slope(own[m] - own[k])
        for ref in recv_refs:
            for k in range(members):
                slopes = slopes + soft_slope(own[m] - ref[k, 0:channels, :].astype(F32))
        gap = soft_slope(own[m] + base_ref[0:channels, :] - truth_ref[...])
        grad_ref[m, 0:channels, :] = (weight_ref[...] * (gap / total - spread * slopes)).astype(BF)
    for m in range(members):
        dm_ref[m] = mm(pt_ref[...], grad_ref[m]).astype(BF)
    for pair in range(width // LANES):
        cols = slice(pair * LANES, (pair + 1) * LANES)
        for m in range(members):
            result = mm(gate_ref[pair, m], dm_ref[m, cols, :], NT)
            ng_ref[m * ext : (m + 1) * ext, cols] = select_heads(result).astype(BF)
    kv_products(n_band // 2, ext_ref, ng_ref, out_refs)


def small_body(n_member, n_band, grad_ref, merged_ref, q_ref, wo_ref, out_ref, turned):
    members = grad_ref.shape[0]
    m_t = sum(mm(grad_ref[m], merged_ref[m], NT) for m in range(members))
    head_t = sum(mm(grad_ref[m], q_ref[...]) for m in range(members)) + mm(m_t.astype(BF), wo_ref[...])
    turned[...] = jnp.concatenate([m_t, head_t], axis=0).T
    out_ref[...] = reorder(turned, n_member, n_band).astype(BF)


def key_body(chips, dm_ref, kv_ref, slope_ref, q_ref, ext_ref, small_ref, ng_ref, *out_refs):
    members, ext, width2 = kv_ref.shape
    width = width2 // 2
    for pair in range(width // LANES):
        cols = slice(pair * LANES, (pair + 1) * LANES)
        vcols = slice(width + pair * LANES, width + (pair + 1) * LANES)
        for m in range(members):
            dgate = mm(split_heads(kv_ref[m, :, vcols]), dm_ref[m, cols, :])
            dscore = (dgate * slope_ref[pair, m].astype(F32)).astype(BF)
            ng_ref[m * ext : (m + 1) * ext, cols] = select_heads(mm(dscore, q_ref[:, cols])).astype(BF)
    kv_products(chips, ext_ref, ng_ref, out_refs)
    half_width = out_refs[0].shape[1] // 2
    for half in range(2):
        part = small_ref[:, half * LANES : (half + 1) * LANES]
        store_parts(part, chips, half, (half + 1) * half_width - LANES, out_refs)


def extended_grad_body(members, nodes, rim, ngk_ref, ngv_ref, kvw_ref, own_ref, down_ref, up_ref):
    ext = nodes + 2 * rim
    width = kvw_ref.shape[0]
    for m in range(members):
        at = slice(m * ext, (m + 1) * ext)
        rows = mm(ngk_ref[at, :], kvw_ref[:, 0:width], NT) + mm(ngv_ref[at, :], kvw_ref[:, width:], NT)
        own_ref[m] = rows[0:nodes]
        down_ref[m * rim : (m + 1) * rim, :] = rows[nodes : nodes + rim].astype(BF)
        up_ref[m * rim : (m + 1) * rim, :] = rows[nodes + rim :].astype(BF)


def hidden_body(own_ref, from_below_ref, from_above_ref, halo_ref, out_ref):
    members, nodes, _ = own_ref.shape
    rim = halo_ref.shape[1]
    low = one_hot_rows(halo_ref[0:1, :], nodes)
    high = one_hot_rows(halo_ref[1:2, :], nodes)
    for m in range(members):
        rows = slice(m * rim, (m + 1) * rim)
        out_ref[m] = own_ref[m] + mm(low, from_below_ref[rows, :]) + mm(high, from_above_ref[rows, :])


def finish_body(devices, n_member, *refs):
    value_refs, key_refs = refs[:n_member], refs[n_member : 2 * n_member]
    hp_ref, kv_ref, out_ref, head_ref = refs[2 * n_member :]
    width = kv_ref.shape[1] // 2
    channels = hp_ref.shape[0]

    def summed(parts):
        total = parts[0][...].astype(F32)
        for ref in parts[1:]:
            total = total + ref[...].astype(F32)
        return total * (1.0 / devices)

    kv_ref[:, width:] = summed(value_refs)
    total = summed(key_refs)
    half = width // 2
    kv_ref[:, 0:half] = total[:, 0:half]
    kv_ref[:, half:width] = total[:, half + LANES : width + LANES]
    m_rows = total[:, half : half + channels]
    high = m_rows.astype(BF)
    low = (m_rows - high.astype(F32)).astype(BF)
    out_ref[...] = mm(high, hp_ref[...]) + mm(low, hp_ref[...])
    head_ref[...] = total[:, width + LANES : width + LANES + channels]


def add_up(*parts):
    return functools.reduce(lambda a, b: a + b, [p.astype(F32) for p in parts])


def swap_cores(send, keep, n_band):
    arrived = lax.ppermute(send, "band", [(i, i ^ 1) for i in range(n_band)])
    half = send.shape[1] // 2
    return [[t[:, i * half : (i + 1) * half] for t in (keep, arrived)] for i in range(2)]


def outgoing_sums(halves):
    return [add_up(*[t[: t.shape[0] // 2] for t in terms]).astype(BF) for terms in halves]


def reduce_plane(halves, outgoing, n_band):
    bits = list(range((n_band // 2).bit_length() - 1))
    orders = (bits, bits[::-1])
    for step in range(len(bits)):
        if step:
            outgoing = outgoing_sums(halves)
        arrived = [
            lax.ppermute(out, "band", [(i, i ^ (2 << order[step])) for i in range(n_band)])
            for out, order in zip(outgoing, orders)
        ]
        halves = [[t[t.shape[0] // 2 :] for t in terms] + [new] for terms, new in zip(halves, arrived)]
    return halves


def plane_sum(halves):
    return jnp.concatenate([add_up(*terms) for terms in halves], axis=1).astype(BF)


def swap_members(plane, n_member):
    rw = plane.shape[0] // n_member
    return [plane[0:rw]] + [
        lax.ppermute(plane[s * rw : (s + 1) * rw], "member", [(i, i ^ s) for i in range(n_member)])
        for s in range(1, n_member)
    ]


def shards(
    n_member, n_band,
    hidden, queries, kv_weight, out_weight, head_projection, initial_state, truth,
    latitude_weight, channel_loss_weight, sources, halo_rows,
):
    members, nodes, width = hidden.shape
    points = queries.shape[0]
    channels = head_projection.shape[1]
    rim = halo_rows.shape[1]
    ext = nodes + 2 * rim
    pairs = width // LANES
    devices = n_member * n_band
    rw = width // devices
    chips = n_band // 2
    send_rows = -(-channels // 16) * 16
    to_above = [(i, i + 1) for i in range(n_band - 1)]
    to_below = [(i + 1, i) for i in range(n_band - 1)]

    own_hidden, halo, down, up = call(
        pick_body,
        [sds(hidden.shape, BF), sds(halo_rows.shape, jnp.int32)] + [sds((members * rim, width), BF)] * 2,
        (hidden, halo_rows),
        [pltpu.SemaphoreType.DMA((2,))],
        hbm=(0, 1),
    )
    below = lax.ppermute(up, "band", to_above)
    above = lax.ppermute(down, "band", to_below)

    args = (
        own_hidden, out_weight, head_projection.T, queries, kv_weight, initial_state,
        channel_loss_weight[None, :], latitude_weight[None, :], sources, truth,
    )
    own_kv, pt, p, base, weight, wo, hp, q, kvw, src, true = call(
        prepare_body,
        [
            sds((members * nodes, 2 * width), BF),
            sds((width, LANES), BF),
            sds((LANES, width), BF),
            sds((LANES, points), F32),
            sds((channels, points), F32),
        ]
        + [sds(args[i].shape, args[i].dtype) for i in (1, 2, 3, 4, 8, 9)],
        args,
        [
            pltpu.VMEM((channels, points), F32),
            pltpu.VMEM((1, channels), F32),
            pltpu.VMEM((1, points), F32),
            pltpu.VMEM((8, LANES), F32),
            pltpu.VMEM((LANES, width), F32),
            pltpu.SemaphoreType.DMA((8 + KV_COPIES,)),
        ],
        hbm=tuple(range(1, 10)),
    )

    kv, gates, slopes, merged, part, sent = call(
        forward_body,
        [
            sds((members, ext, 2 * width), BF),
            sds((pairs, members, 2 * ext, points), BF),
            sds((pairs, members, 2 * ext, points), BF),
            sds((members, width, points), BF),
            sds((members, LANES, points), F32),
            sds((members, send_rows, points), BF),
        ],
        (below, above, own_kv, kvw, q, src, p),
    )

    received = [
        lax.ppermute(sent, "member", [(i, i ^ s) for i in range(n_member)]) for s in range(1, n_member)
    ]

    ext_t = call(
        functools.partial(transpose_body, n_member, n_band),
        sds((width, members * ext), BF),
        (own_hidden, below, above),
        [pltpu.VMEM((width, members * ext), F32)],
    )

    extra = 2 * LANES
    grad, dm, ng_value, send, keep = call(
        functools.partial(value_body, n_member, n_band),
        [sds((members, LANES, points), BF), sds((members, width, points), BF), sds((members * ext, width), BF)]
        + [sds((width // 2, width), BF)] * 2,
        (*received, part, base, true, weight, pt, gates, ext_t),
    )
    small = call(
        functools.partial(small_body, n_member, n_band),
        sds((width, extra), BF),
        (grad, merged, q, wo),
        [pltpu.VMEM((width, extra), F32)],
    )
    value_halves = swap_cores(send, keep, n_band)
    outgoing = outgoing_sums(value_halves)

    outgoing, dm, small = lax.optimization_barrier((outgoing, dm, small))
    value_halves = reduce_plane(value_halves, outgoing, n_band)
    ng_key, send, keep = call(
        functools.partial(key_body, chips),
        [sds((members * ext, width), BF)] + [sds((width // 2, width + extra), BF)] * 2,
        (dm, kv, slopes, q, ext_t, small),
    )
    key_halves = swap_cores(send, keep, n_band)
    outgoing = outgoing_sums(key_halves)

    outgoing, ng_key = lax.optimization_barrier((outgoing, ng_key))
    key_halves = reduce_plane(key_halves, outgoing, n_band)
    own_grad, back_down, back_up = call(
        functools.partial(extended_grad_body, members, nodes, rim),
        [sds((members, nodes, width), F32)] + [sds((members * rim, width), BF)] * 2,
        (ng_key, ng_value, kvw),
    )
    from_above = lax.ppermute(back_down, "band", to_below)
    from_below = lax.ppermute(back_up, "band", to_above)
    hidden_grad = call(
        hidden_body,
        sds((members, nodes, width), F32),
        (own_grad, from_below, from_above, halo),
    )

    last_v = swap_members(plane_sum(value_halves), n_member)
    hidden_grad, key_halves = lax.optimization_barrier((hidden_grad, key_halves))
    last_k = swap_members(plane_sum(key_halves), n_member)

    kv_grad, out_grad, head_grad = call(
        functools.partial(finish_body, devices, n_member),
        [sds((rw, 2 * width), F32), sds((rw, width), F32), sds((rw, channels), F32)],
        (*last_v, *last_k, hp),
    )
    return hidden_grad, kv_grad, out_grad, head_grad


def solution(mesh):
    placed = (
        P("member", "band", None),
        P("band", None),
        P(),
        P(),
        P(),
        P(None, "band"),
        P(None, "band"),
        P("band"),
        P(),
        P(None, "band"),
        P("band", None),
    )
    return jax.shard_map(
        functools.partial(shards, mesh.shape["member"], mesh.shape["band"]),
        mesh=mesh,
        in_specs=placed,
        out_specs=(
            P("member", "band", None),
            P(("member", "band"), None),
            P(("member", "band"), None),
            P(("member", "band"), None),
        ),
        check_vma=False,
    )
```

time: 120 us -> 91.3 us (0.76); the launches traced: 118 us -> 91.1 us
  blocking collectives: 16.1 us -> 0 us
  starting transfers between devices: 22.5 us -> 36.7 us
  between operations: 14.2 us -> 0.85 us
  local copies, waits for them, and re-layouts: 12.8 us -> 0.09 us
  waiting for transfers between devices: 28.8 us -> 31.5 us
  Pallas kernels: 22.4 us -> 21.1 us
    ppermute x0 -> x16, starting transfers between devices: none -> 25.4 us  [the longest x8 15.4 us: reduce_plane(): lax.ppermute(out, 'band', [(i, i ^ 2 << order[step]) for i in range(n_ban...]
    ppermute x0 -> x16, waiting for transfers between devices: none -> 22.3 us  [the longest x8 16.1 us: reduce_plane(): lax.ppermute(out, 'band', [(i, i ^ 2 << order[step]) for i in range(n_ban...]
    all_to_all x3 -> x0, waiting for transfers between devices: 17.9 us -> none  [the longest x1 14.6 us: shards(): traded = lax.all_to_all(node_grad, 'band', 0, 0, tiled=True)]
    all_to_all x1 -> x0, blocking collectives: 16.1 us -> none  [shards(): small = lax.all_to_all(small, 'band', 0, 0, tiled=True)]
    unnamed x26 -> x0, local copies, waits for them, and re-layouts: 12.8 us -> none
    all_to_all x3 -> x0, starting transfers between devices: 10.3 us -> none  [the longest x1 4.07 us: shards(): small = lax.all_to_all(small, 'member', 0, 0, tiled=True)]
    ppermute x1, waiting for transfers between devices: 3.06 us -> 0.01 us  [shards(): from_above = lax.ppermute(back_down, 'band', to_below)]
    pallas_call x9 -> x10, Pallas kernels: 22.4 us -> 21.1 us  [call(): pl.pallas_call(body, out_shape=out_shape, in_specs=[pl.BlockSpec(memory_s...]
  transfers between devices with their start and end apart: 11 -> 23, of which waited for: 7 -> 9; matrix products, arithmetic and copies ran while one was open for 1% -> 1% of each run, Pallas kernels for 17% -> 11%
where the time goes in v3:
time: 91.3 us; the launch traced here: 91.1 us
  starting transfers between devices  36.7 us (40%)
  waiting for transfers between devices  31.5 us (35%)
  Pallas kernels  21.1 us (23%)
    pallas_call x10, Pallas kernels, call(): pl.pallas_call(body, out_shape=out_shape, in_specs=[pl.BlockSpec(memory_s...  21.1 us
    ppermute x8, waiting for transfers between devices, reduce_plane(): lax.ppermute(out, 'band', [(i, i ^ 2 << order[step]) for i in range(n_ban...  16.1 us
    ppermute x8, starting transfers between devices, reduce_plane(): lax.ppermute(out, 'band', [(i, i ^ 2 << order[step]) for i in range(n_ban...  15.4 us
    ppermute x3, waiting for transfers between devices, shards(): lax.ppermute(sent, 'member', [(i, i ^ s) for i in range(n_member)])  9.17 us
    ppermute x6, starting transfers between devices, swap_members(): lax.ppermute(plane[s * rw:(s + 1) * rw], 'member', [(i, i ^ s) for i in r...  8.9 us
    ppermute x3, starting transfers between devices, shards(): lax.ppermute(sent, 'member', [(i, i ^ s) for i in range(n_member)])  5.14 us
    ppermute x6, waiting for transfers between devices, swap_members(): lax.ppermute(plane[s * rw:(s + 1) * rw], 'member', [(i, i ^ s) for i in r...  4.98 us
    ppermute x1, starting transfers between devices, shards(): below = lax.ppermute(up, 'band', to_above)  2.36 us
  transfers between devices with their start and end apart: 23, of which 9 were waited for; matrix products, arithmetic and copies ran while one was open for 1% of the time, Pallas kernels for 11%

profile of v3, /device:TPU:0, one launch (start us, length us, event | category | flops | bytes accessed | tf_op | source)
XLA Modules:
  0.0 91.1 jit_solution(9016311161284044120)
XLA Ops:
  0.6 1.2 %shard_map.138 = (bf16[2,64,1024]{2,1,0:T(8,128)(2,1)S(1)}, s32[2,32]{1,0:T(2,128)S(1)}, bf16[64,1024]{1,0:T(8,128)(2,1)S(1)}, bf16[64,1024]{1,0:T(8,128)(2,1)S(1)}) custom-call(bf16[2,64,1024]{2,1,0:T(8,128)(2,1)} %hidden_hbm.1, s32[2,32]{1,0:T(2,128)} %halo_hbm.1), custom_call_target="tpu_custom_call" | custom-call | flops 1 | bytes 1 | tf_op jit(solution)/shard_map/pallas_call | solution.py:28
  1.9 2.4 %collective-permute-start = (bf16[64,1024]{1,0:T(8,128)(2,1)S(1)}, bf16[64,1024]{1,0:T(8,128)(2,1)S(1)}, u32[]{:S(2)}, u32[]{:S(2)}) collective-permute-start(bf16[64,1024]{1,0:T(8,128)(2,1)S(1)} %get-tuple-element.55), channel_id=1, source_target_pairs={{0,1},{1,2},{2,3},{3,4},{4,5},{5,6},{6,7},{8,9},{9,10},{10,11},{11... | collective-permute-start | bytes 393224 | tf_op jit(solution)/shard_map/ppermute | solution.py:382
  4.2 1.3 %collective-permute-start.1 = (bf16[64,1024]{1,0:T(8,128)(2,1)S(1)}, bf16[64,1024]{1,0:T(8,128)(2,1)S(1)}, u32[]{:S(2)}, u32[]{:S(2)}) collective-permute-start(bf16[64,1024]{1,0:T(8,128)(2,1)S(1)} %get-tuple-element.56), channel_id=1, source_target_pairs={{1,0},{2,1},{3,2},{4,3},{5,4},{6,5},{7,6},{9,8},{10,9},{11,10},{12... | collective-permute-start | bytes 393224 | tf_op jit(solution)/shard_map/ppermute | solution.py:383
  5.5 4.6 %shard_map.139 = (bf16[128,2048]{1,0:T(8,128)(2,1)S(1)}, bf16[1024,128]{1,0:T(8,128)(2,1)S(1)}, bf16[128,1024]{1,0:T(8,128)(2,1)S(1)}, f32[128,256]{1,0:T(8,128)...) custom-call(bf16[2,64,1024]{2,1,0:T(8,128)(2,1)S(1)} %get-tuple-elem, ...), custom_call_target="tpu_custom_call" | custom-call | flops 1 | bytes 1 | tf_op jit(solution)/shard_map/pallas_call | solution.py:28
  10.2 0.0 collective-permute-done.1.above_ref
  10.2 5.0 %shard_map.140 = (bf16[2,128,2048]{2,1,0:T(8,128)(2,1)S(1)}, bf16[8,2,256,256]{3,2,1,0:T(8,128)(2,1)S(1)}, bf16[8,2,256,256]{3,2,1,0:T(8,128)(2,1)S(1)}, bf16[2,...) custom-call(bf16[64,1024]{1,0:T(8,128)(2,1)S(1)} %collective-permute-done.below_ref, ...), custom_call_target="tpu_custom_call" | custom-call | flops 1 | bytes 1 | tf_op jit(solution)/shard_map/pallas_call | solution.py:28
  15.2 4.5 %collective-permute-start.4 = (bf16[2,112,256]{2,1,0:T(8,128)(2,1)S(1)}, bf16[2,112,256]{2,1,0:T(8,128)(2,1)S(1)}, u32[]{:S(2)}, u32[]{:S(2)}) collective-permute-start(bf16[2,112,256]{2,1,0:T(8,128)(2,1)S(1)} %get-tuple-element.63), channel_id=1, source_target_pairs={{0,24},{8,16},{16,8},{24,0},{1,25},{9,17},{17,9},{25,1},{2,26},{10... | collective-permute-start | bytes 344072 | tf_op jit(solution)/shard_map/ppermute | solution.py:425
  19.7 0.0 collective-permute-start.3
  19.7 0.6 collective-permute-start.2
  20.3 0.3 shard_map.141.refs_9_.ext_ref
  20.6 2.0 %collective-permute-done.4.refs_2_ = bf16[2,112,256]{2,1,0:T(8,128)(2,1)S(1)} collective-permute-done((bf16[2,112,256]{2,1,0:T(8,128)(2,1)S(1)}, bf16[2,112,256]{2,1,0:T(8,128)(2,1)S(1)}, u32[]{:S(2)}, u32[]{:S(2)}) %collective-permute-start.4) | collective-permute-done | bytes 114720 | tf_op jit(solution)/shard_map/ppermute | solution.py:425
  22.5 7.2 %collective-permute-done.3.refs_1_ = bf16[2,112,256]{2,1,0:T(8,128)(2,1)S(1)} collective-permute-done((bf16[2,112,256]{2,1,0:T(8,128)(2,1)S(1)}, bf16[2,112,256]{2,1,0:T(8,128)(2,1)S(1)}, u32[]{:S(2)}, u32[]{:S(2)}) %collective-permute-start.3) | collective-permute-done | bytes 114720 | tf_op jit(solution)/shard_map/ppermute | solution.py:425
  29.7 1.9 %shard_map.142 = (bf16[2,128,256]{2,1,0:T(8,128)(2,1)S(1)}, bf16[2,1024,256]{2,1,0:T(8,128)(2,1)S(1)}, bf16[256,1024]{1,0:T(8,128)(2,1)S(1)}, bf16[512,1024]{1,0:T(8,128)(2,1)S(1)}, bf16[512,1024]{1,0:T(8,128)(2,1)S(1)}) custom-call(bf16[2,112,256]{2,1,0:T(8,128)(2,1)S(1)} %collective-permute-done.2.refs_0_, ...), custom_call_target="tpu_custom_call" | custom-call | flops 1 | bytes 1 | tf_op jit(solution)/shard_map/pallas_call | solution.py:28
  31.7 0.6 collective-permute-start.5
  32.3 1.1 %shard_map.143.small_ref = bf16[1024,256]{1,0:T(8,128)(2,1)S(1)} custom-call(bf16[2,128,256]{2,1,0:T(8,128)(2,1)S(1)} %get-tuple-element.73.grad_ref, bf16[2,1024,256]{2,1,0:T(8,128)(2,1)S(1)} %get-tuple-element.74.merged_ref, bf16[256,1024]{1,0:T(8,128)(2,1)S(1)} %get-tuple-element.60.q_ref, bf16[1024,1024]{1,0:T(8,128)(2,1)S(1)} %get-tuple-element.75.wo_ref), custom_call_target="tpu_custom_call" | custom-call | flops 1 | bytes 1 | tf_op jit(solution)/shard_map/pallas_call | solution.py:28
  33.4 1.2 %collective-permute-done.5 = bf16[512,1024]{1,0:T(8,128)(2,1)S(1)} collective-permute-done((bf16[512,1024]{1,0:T(8,128)(2,1)S(1)}, bf16[512,1024]{1,0:T(8,128)(2,1)S(1)}, u32[]{:S(2)}, u32[]{:S(2)}) %collective-permute-start.5) | collective-permute-done | bytes 1048608 | tf_op jit(solution)/shard_map/ppermute | solution.py:322
  34.6 0.1 add_convert_fusion.2
  34.7 2.0 %shard_map.144 = (bf16[256,1024]{1,0:T(8,128)(2,1)S(1)}, bf16[512,1280]{1,0:T(8,128)(2,1)S(1)}, bf16[512,1280]{1,0:T(8,128)(2,1)S(1)}) custom-call(bf16[2,1024,256]{2,1,0:T(8,128)(2,1)S(1)} %get-tuple-element.76.dm_ref, bf16[2,128,2048]{2,1,0:T(8,128)(2,1)S(1)} %get-tuple-element.77.kv_ref, bf16[8,2,256,256]{3,2,1,0:T(8,128)(2,1)S(1)} %get-tuple-element.78.slope_ref, ...), custom_call_target="tpu_custom_call" | custom-call | flops 1 | bytes 1 | tf_op jit(solution)/shard_map/pallas_call | solution.py:28
  36.7 0.4 collective-permute-start.6
  37.1 3.3 %collective-permute-start.15 = (bf16[256,512]{1,0:T(8,128)(2,1)S(1)}, bf16[256,512]{1,0:T(8,128)(2,1)S(1)}, u32[]{:S(2)}, u32[]{:S(2)}) collective-permute-start(bf16[256,512]{1,0:T(8,128)(2,1)S(1)} %get-tuple-element.93), channel_id=1, source_target_pairs={{0,4},{1,5},{2,6},{3,7},{4,0},{5,1},{6,2},{7,3},{8,12},{9,13},{10,... | collective-permute-start | bytes 786440 | tf_op jit(solution)/shard_map/ppermute | solution.py:338
  40.4 0.6 collective-permute-start.13
  41.0 6.2 %collective-permute-done.15 = bf16[256,512]{1,0:T(8,128)(2,1)S(1)} collective-permute-done((bf16[256,512]{1,0:T(8,128)(2,1)S(1)}, bf16[256,512]{1,0:T(8,128)(2,1)S(1)}, u32[]{:S(2)}, u32[]{:S(2)}) %collective-permute-start.15) | collective-permute-done | bytes 262176 | tf_op jit(solution)/shard_map/ppermute | solution.py:338
  47.2 0.1 add_convert_fusion.9
  47.3 2.4 %collective-permute-start.16 = (bf16[128,512]{1,0:T(8,128)(2,1)S(1)}, bf16[128,512]{1,0:T(8,128)(2,1)S(1)}, u32[]{:S(2)}, u32[]{:S(2)}) collective-permute-start(bf16[128,512]{1,0:T(8,128)(2,1)S(1)} %add_convert_fusion.9), channel_id=1, source_target_pairs={{0,2},{1,3},{2,0},{3,1},{4,6},{5,7},{6,4},{7,5},{8,10},{9,11},{10,... | collective-permute-start | bytes 393224 | tf_op jit(solution)/shard_map/ppermute | solution.py:338
  49.7 3.2 %collective-permute-done.16 = bf16[128,512]{1,0:T(8,128)(2,1)S(1)} collective-permute-done((bf16[128,512]{1,0:T(8,128)(2,1)S(1)}, bf16[128,512]{1,0:T(8,128)(2,1)S(1)}, u32[]{:S(2)}, u32[]{:S(2)}) %collective-permute-start.16) | collective-permute-done | bytes 131104 | tf_op jit(solution)/shard_map/ppermute | solution.py:338
  52.9 0.1 add_convert_fusion.8
  53.0 1.2 %collective-permute-start.14 = (bf16[128,512]{1,0:T(8,128)(2,1)S(1)}, bf16[128,512]{1,0:T(8,128)(2,1)S(1)}, u32[]{:S(2)}, u32[]{:S(2)}) collective-permute-start(bf16[128,512]{1,0:T(8,128)(2,1)S(1)} %get-tuple-element.111), channel_id=1, source_target_pairs={{0,4},{1,5},{2,6},{3,7},{4,0},{5,1},{6,2},{7,3},{8,12},{9,13},{10,... | collective-permute-start | bytes 393224 | tf_op jit(solution)/shard_map/ppermute | solution.py:338
  54.2 0.2 add_convert_fusion
  54.4 1.2 %collective-permute-start.9 = (bf16[256,640]{1,0:T(8,128)(2,1)S(1)}, bf16[256,640]{1,0:T(8,128)(2,1)S(1)}, u32[]{:S(2)}, u32[]{:S(2)}) collective-permute-start(bf16[256,640]{1,0:T(8,128)(2,1)S(1)} %get-tuple-element.89), channel_id=1, source_target_pairs={{0,2},{1,3},{2,0},{3,1},{4,6},{5,7},{6,4},{7,5},{8,10},{9,11},{10,... | collective-permute-start | bytes 983048 | tf_op jit(solution)/shard_map/ppermute | solution.py:338
  55.6 1.5 %collective-permute-start.11 = (bf16[256,640]{1,0:T(8,128)(2,1)S(1)}, bf16[256,640]{1,0:T(8,128)(2,1)S(1)}, u32[]{:S(2)}, u32[]{:S(2)}) collective-permute-start(bf16[256,640]{1,0:T(8,128)(2,1)S(1)} %get-tuple-element.90), channel_id=1, source_target_pairs={{0,4},{1,5},{2,6},{3,7},{4,0},{5,1},{6,2},{7,3},{8,12},{9,13},{10,... | collective-permute-start | bytes 983048 | tf_op jit(solution)/shard_map/ppermute | solution.py:338
  57.1 2.4 %collective-permute-done.14 = bf16[128,512]{1,0:T(8,128)(2,1)S(1)} collective-permute-done((bf16[128,512]{1,0:T(8,128)(2,1)S(1)}, bf16[128,512]{1,0:T(8,128)(2,1)S(1)}, u32[]{:S(2)}, u32[]{:S(2)}) %collective-permute-start.14) | collective-permute-done | bytes 131104 | tf_op jit(solution)/shard_map/ppermute | solution.py:338
  59.4 0.1 add_convert_fusion.10
  59.5 2.5 %collective-permute-start.19 = (bf16[32,1024]{1,0:T(8,128)(2,1)S(1)}, bf16[32,1024]{1,0:T(8,128)(2,1)S(1)}, u32[]{:S(2)}, u32[]{:S(2)}) collective-permute-start(bf16[32,1024]{1,0:T(8,128)(2,1)S(1)} %get-tuple-element.122), channel_id=1, source_target_pairs={{0,24},{8,16},{16,8},{24,0},{1,25},{9,17},{17,9},{25,1},{2,26},{10... | collective-permute-start | bytes 196616 | tf_op jit(solution)/shard_map/ppermute | solution.py:352
  62.1 3.0 %shard_map.145 = (f32[2,64,1024]{2,1,0:T(8,128)S(1)}, bf16[64,1024]{1,0:T(8,128)(2,1)S(1)}, bf16[64,1024]{1,0:T(8,128)(2,1)S(1)}) custom-call(bf16[256,1024]{1,0:T(8,128)(2,1)S(1)} %get-tuple-element.83.ngk_ref, bf16[256,1024]{1,0:T(8,128)(2,1)S(1)} %get-tuple-element.84.ngv_ref, bf16[1024,2048]{1,0:T(8,128)(2,1)S(1)} %get-tuple-element.59.kvw_ref), custom_call_target="tpu_custom_call" | custom-call | flops 1 | bytes 1 | tf_op jit(solution)/shard_map/pallas_call | solution.py:28
  65.1 1.3 %collective-permute-start.7 = (bf16[64,1024]{1,0:T(8,128)(2,1)S(1)}, bf16[64,1024]{1,0:T(8,128)(2,1)S(1)}, u32[]{:S(2)}, u32[]{:S(2)}) collective-permute-start(bf16[64,1024]{1,0:T(8,128)(2,1)S(1)} %get-tuple-element.86), channel_id=1, source_target_pairs={{0,1},{1,2},{2,3},{3,4},{4,5},{5,6},{6,7},{8,9},{9,10},{10,11},{11... | collective-permute-start | bytes 393224 | tf_op jit(solution)/shard_map/ppermute | solution.py:469
  66.4 1.3 %collective-permute-start.8 = (bf16[64,1024]{1,0:T(8,128)(2,1)S(1)}, bf16[64,1024]{1,0:T(8,128)(2,1)S(1)}, u32[]{:S(2)}, u32[]{:S(2)}) collective-permute-start(bf16[64,1024]{1,0:T(8,128)(2,1)S(1)} %get-tuple-element.87), channel_id=1, source_target_pairs={{1,0},{2,1},{3,2},{4,3},{5,4},{6,5},{7,6},{9,8},{10,9},{11,10},{12... | collective-permute-start | bytes 393224 | tf_op jit(solution)/shard_map/ppermute | solution.py:468
  67.8 0.1 add_convert_fusion.6
  67.9 4.9 %collective-permute-start.12 = (bf16[128,640]{1,0:T(8,128)(2,1)S(1)}, bf16[128,640]{1,0:T(8,128)(2,1)S(1)}, u32[]{:S(2)}, u32[]{:S(2)}) collective-permute-start(bf16[128,640]{1,0:T(8,128)(2,1)S(1)} %get-tuple-element.106), channel_id=1, source_target_pairs={{0,2},{1,3},{2,0},{3,1},{4,6},{5,7},{6,4},{7,5},{8,10},{9,11},{10,... | collective-permute-start | bytes 491528 | tf_op jit(solution)/shard_map/ppermute | solution.py:338
  72.7 0.4 collective-permute-start.10
  73.2 1.1 %shard_map.146 = f32[2,64,1024]{2,1,0:T(8,128)} custom-call(f32[2,64,1024]{2,1,0:T(8,128)S(1)} %get-tuple-element.85.own_ref, bf16[64,1024]{1,0:T(8,128)(2,1)S(1)} %collective-permute-done.7.from_below_ref, bf16[64,1024]{1,0:T(8,128)(2,1)S(1)} %collective-permute-done.8.from_above_ref, s32[2,32]{1,0:T(2,128)S(1)} %get-tuple-element.88.halo_ref), custom_call_target="tpu_custom_call" | custom-call | flops 1 | bytes 1 | tf_op jit(solution)/shard_map/pallas_call | solution.py:28
  74.3 4.4 %collective-permute-done.12 = bf16[128,640]{1,0:T(8,128)(2,1)S(1)} collective-permute-done((bf16[128,640]{1,0:T(8,128)(2,1)S(1)}, bf16[128,640]{1,0:T(8,128)(2,1)S(1)}, u32[]{:S(2)}, u32[]{:S(2)}) %collective-permute-start.12) | collective-permute-done | bytes 163872 | tf_op jit(solution)/shard_map/ppermute | solution.py:338
  78.6 0.2 add_convert_fusion.4
  78.8 1.4 %collective-permute-start.22 = (bf16[32,1280]{1,0:T(8,128)(2,1)S(1)}, bf16[32,1280]{1,0:T(8,128)(2,1)S(1)}, u32[]{:S(2)}, u32[]{:S(2)}) collective-permute-start(bf16[32,1280]{1,0:T(8,128)(2,1)S(1)} %get-tuple-element.118), channel_id=1, source_target_pairs={{0,24},{8,16},{16,8},{24,0},{1,25},{9,17},{17,9},{25,1},{2,26},{10... | collective-permute-start | bytes 245768 | tf_op jit(solution)/shard_map/ppermute | solution.py:352
  80.3 3.0 %collective-permute-start.21 = (bf16[32,1280]{1,0:T(8,128)(2,1)S(1)}, bf16[32,1280]{1,0:T(8,128)(2,1)S(1)}, u32[]{:S(2)}, u32[]{:S(2)}) collective-permute-start(bf16[32,1280]{1,0:T(8,128)(2,1)S(1)} %get-tuple-element.121), channel_id=1, source_target_pairs={{0,16},{8,24},{16,0},{24,8},{1,17},{9,25},{17,1},{25,9},{2,18},{10... | collective-permute-start | bytes 245768 | tf_op jit(solution)/shard_map/ppermute | solution.py:352
  83.3 1.9 %collective-permute-start.18 = (bf16[32,1024]{1,0:T(8,128)(2,1)S(1)}, bf16[32,1024]{1,0:T(8,128)(2,1)S(1)}, u32[]{:S(2)}, u32[]{:S(2)}) collective-permute-start(bf16[32,1024]{1,0:T(8,128)(2,1)S(1)} %get-tuple-element.125), channel_id=1, source_target_pairs={{0,16},{8,24},{16,0},{24,8},{1,17},{9,25},{17,1},{25,9},{2,18},{10... | collective-permute-start | bytes 196616 | tf_op jit(solution)/shard_map/ppermute | solution.py:352
  85.2 4.3 %collective-permute-done.17.refs_1_ = bf16[32,1024]{1,0:T(8,128)(2,1)S(1)} collective-permute-done((bf16[32,1024]{1,0:T(8,128)(2,1)S(1)}, bf16[32,1024]{1,0:T(8,128)(2,1)S(1)}, u32[]{:S(2)}, u32[]{:S(2)}) %collective-permute-start.17) | collective-permute-done | bytes 65568 | tf_op jit(solution)/shard_map/ppermute | solution.py:352
  89.5 0.7 collective-permute-done.18.refs_2_
  90.2 0.9 %shard_map.147 = (f32[32,2048]{1,0:T(8,128)}, f32[32,1024]{1,0:T(8,128)}, f32[32,100]{1,0:T(8,128)}) custom-call(bf16[32,1024]{1,0:T(8,128)(2,1)S(1)} %get-tuple-element.123.refs_0_, bf16[32,1024]{1,0:T(8,128)(2,1)S(1)} %collective-permute-done.17.refs_1_, bf16[32,1024]{1,0:T(8,128)(2,1)S(1)} %collective-permute-done.18.refs_2_, ...), custom_call_target="tpu_custom_call" | custom-call | flops 1 | bytes 1 | tf_op jit(solution)/shard_map/pallas_call | solution.py:28
  (21 shorter events, 0.2 us)
Async XLA Ops:
  1.9 8.3 %collective-permute-start = (bf16[64,1024]{1,0:T(8,128)(2,1)S(1)}, bf16[64,1024]{1,0:T(8,128)(2,1)S(1)}, u32[]{:S(2)}, u32[]{:S(2)}) collective-permute-start(bf16[64,1024]{1,0:T(8,128)(2,1)S(1)} %get-tuple-element.55), channel_id=1, source_target_pairs={{0,1},{1,2},{2,3},{3,4},{4,5},{5,6},{6,7},{8,9},{9,10},{10,11},{11... | collective-permute-start | bytes 393224 | tf_op jit(solution)/shard_map/ppermute | solution.py:382
  4.2 5.9 %collective-permute-start.1 = (bf16[64,1024]{1,0:T(8,128)(2,1)S(1)}, bf16[64,1024]{1,0:T(8,128)(2,1)S(1)}, u32[]{:S(2)}, u32[]{:S(2)}) collective-permute-start(bf16[64,1024]{1,0:T(8,128)(2,1)S(1)} %get-tuple-element.56), channel_id=1, source_target_pairs={{1,0},{2,1},{3,2},{4,3},{5,4},{6,5},{7,6},{9,8},{10,9},{11,10},{12... | collective-permute-start | bytes 393224 | tf_op jit(solution)/shard_map/ppermute | solution.py:383
  15.2 7.4 %collective-permute-start.4 = (bf16[2,112,256]{2,1,0:T(8,128)(2,1)S(1)}, bf16[2,112,256]{2,1,0:T(8,128)(2,1)S(1)}, u32[]{:S(2)}, u32[]{:S(2)}) collective-permute-start(bf16[2,112,256]{2,1,0:T(8,128)(2,1)S(1)} %get-tuple-element.63), channel_id=1, source_target_pairs={{0,24},{8,16},{16,8},{24,0},{1,25},{9,17},{17,9},{25,1},{2,26},{10... | collective-permute-start | bytes 344072 | tf_op jit(solution)/shard_map/ppermute | solution.py:425
  19.7 10.1 %collective-permute-start.3 = (bf16[2,112,256]{2,1,0:T(8,128)(2,1)S(1)}, bf16[2,112,256]{2,1,0:T(8,128)(2,1)S(1)}, u32[]{:S(2)}, u32[]{:S(2)}) collective-permute-start(bf16[2,112,256]{2,1,0:T(8,128)(2,1)S(1)} %get-tuple-element.63), channel_id=1, source_target_pairs={{0,16},{8,24},{16,0},{24,8},{1,17},{9,25},{17,1},{25,9},{2,18},{10... | collective-permute-start | bytes 344072 | tf_op jit(solution)/shard_map/ppermute | solution.py:425
  19.7 10.1 %collective-permute-start.2 = (bf16[2,112,256]{2,1,0:T(8,128)(2,1)S(1)}, bf16[2,112,256]{2,1,0:T(8,128)(2,1)S(1)}, u32[]{:S(2)}, u32[]{:S(2)}) collective-permute-start(bf16[2,112,256]{2,1,0:T(8,128)(2,1)S(1)} %get-tuple-element.63), channel_id=1, source_target_pairs={{0,8},{8,0},{16,24},{24,16},{1,9},{9,1},{17,25},{25,17},{2,10},{10... | collective-permute-start | bytes 344072 | tf_op jit(solution)/shard_map/ppermute | solution.py:425
  31.7 2.9 %collective-permute-start.5 = (bf16[512,1024]{1,0:T(8,128)(2,1)S(1)}, bf16[512,1024]{1,0:T(8,128)(2,1)S(1)}, u32[]{:S(2)}, u32[]{:S(2)}) collective-permute-start(bf16[512,1024]{1,0:T(8,128)(2,1)S(1)} %get-tuple-element.71), channel_id=1, source_target_pairs={{0,1},{1,0},{2,3},{3,2},{4,5},{5,4},{6,7},{7,6},{8,9},{9,8},{10,11... | collective-permute-start | bytes 3145736 | tf_op jit(solution)/shard_map/ppermute | solution.py:322
  36.7 17.6 %collective-permute-start.6 = (bf16[512,1280]{1,0:T(8,128)(2,1)S(1)}, bf16[512,1280]{1,0:T(8,128)(2,1)S(1)}, u32[]{:S(2)}, u32[]{:S(2)}) collective-permute-start(bf16[512,1280]{1,0:T(8,128)(2,1)S(1)} %get-tuple-element.81), channel_id=1, source_target_pairs={{0,1},{1,0},{2,3},{3,2},{4,5},{5,4},{6,7},{7,6},{8,9},{9,8},{10,11... | collective-permute-start | bytes 3932168 | tf_op jit(solution)/shard_map/ppermute | solution.py:322
  37.1 10.1 %collective-permute-start.15 = (bf16[256,512]{1,0:T(8,128)(2,1)S(1)}, bf16[256,512]{1,0:T(8,128)(2,1)S(1)}, u32[]{:S(2)}, u32[]{:S(2)}) collective-permute-start(bf16[256,512]{1,0:T(8,128)(2,1)S(1)} %get-tuple-element.93), channel_id=1, source_target_pairs={{0,4},{1,5},{2,6},{3,7},{4,0},{5,1},{6,2},{7,3},{8,12},{9,13},{10,... | collective-permute-start | bytes 786440 | tf_op jit(solution)/shard_map/ppermute | solution.py:338
  40.4 9.3 %collective-permute-start.13 = (bf16[256,512]{1,0:T(8,128)(2,1)S(1)}, bf16[256,512]{1,0:T(8,128)(2,1)S(1)}, u32[]{:S(2)}, u32[]{:S(2)}) collective-permute-start(bf16[256,512]{1,0:T(8,128)(2,1)S(1)} %get-tuple-element.92), channel_id=1, source_target_pairs={{0,2},{1,3},{2,0},{3,1},{4,6},{5,7},{6,4},{7,5},{8,10},{9,11},{10,... | collective-permute-start | bytes 786440 | tf_op jit(solution)/shard_map/ppermute | solution.py:338
  47.3 5.6 %collective-permute-start.16 = (bf16[128,512]{1,0:T(8,128)(2,1)S(1)}, bf16[128,512]{1,0:T(8,128)(2,1)S(1)}, u32[]{:S(2)}, u32[]{:S(2)}) collective-permute-start(bf16[128,512]{1,0:T(8,128)(2,1)S(1)} %add_convert_fusion.9), channel_id=1, source_target_pairs={{0,2},{1,3},{2,0},{3,1},{4,6},{5,7},{6,4},{7,5},{8,10},{9,11},{10,... | collective-permute-start | bytes 393224 | tf_op jit(solution)/shard_map/ppermute | solution.py:338
  53.0 6.4 %collective-permute-start.14 = (bf16[128,512]{1,0:T(8,128)(2,1)S(1)}, bf16[128,512]{1,0:T(8,128)(2,1)S(1)}, u32[]{:S(2)}, u32[]{:S(2)}) collective-permute-start(bf16[128,512]{1,0:T(8,128)(2,1)S(1)} %get-tuple-element.111), channel_id=1, source_target_pairs={{0,4},{1,5},{2,6},{3,7},{4,0},{5,1},{6,2},{7,3},{8,12},{9,13},{10,... | collective-permute-start | bytes 393224 | tf_op jit(solution)/shard_map/ppermute | solution.py:338
  54.4 13.3 %collective-permute-start.9 = (bf16[256,640]{1,0:T(8,128)(2,1)S(1)}, bf16[256,640]{1,0:T(8,128)(2,1)S(1)}, u32[]{:S(2)}, u32[]{:S(2)}) collective-permute-start(bf16[256,640]{1,0:T(8,128)(2,1)S(1)} %get-tuple-element.89), channel_id=1, source_target_pairs={{0,2},{1,3},{2,0},{3,1},{4,6},{5,7},{6,4},{7,5},{8,10},{9,11},{10,... | collective-permute-start | bytes 983048 | tf_op jit(solution)/shard_map/ppermute | solution.py:338
  55.6 12.2 %collective-permute-start.11 = (bf16[256,640]{1,0:T(8,128)(2,1)S(1)}, bf16[256,640]{1,0:T(8,128)(2,1)S(1)}, u32[]{:S(2)}, u32[]{:S(2)}) collective-permute-start(bf16[256,640]{1,0:T(8,128)(2,1)S(1)} %get-tuple-element.90), channel_id=1, source_target_pairs={{0,4},{1,5},{2,6},{3,7},{4,0},{5,1},{6,2},{7,3},{8,12},{9,13},{10,... | collective-permute-start | bytes 983048 | tf_op jit(solution)/shard_map/ppermute | solution.py:338
  59.5 23.8 %collective-permute-start.19 = (bf16[32,1024]{1,0:T(8,128)(2,1)S(1)}, bf16[32,1024]{1,0:T(8,128)(2,1)S(1)}, u32[]{:S(2)}, u32[]{:S(2)}) collective-permute-start(bf16[32,1024]{1,0:T(8,128)(2,1)S(1)} %get-tuple-element.122), channel_id=1, source_target_pairs={{0,24},{8,16},{16,8},{24,0},{1,25},{9,17},{17,9},{25,1},{2,26},{10... | collective-permute-start | bytes 196616 | tf_op jit(solution)/shard_map/ppermute | solution.py:352
  65.1 8.0 %collective-permute-start.7 = (bf16[64,1024]{1,0:T(8,128)(2,1)S(1)}, bf16[64,1024]{1,0:T(8,128)(2,1)S(1)}, u32[]{:S(2)}, u32[]{:S(2)}) collective-permute-start(bf16[64,1024]{1,0:T(8,128)(2,1)S(1)} %get-tuple-element.86), channel_id=1, source_target_pairs={{0,1},{1,2},{2,3},{3,4},{4,5},{5,6},{6,7},{8,9},{9,10},{10,11},{11... | collective-permute-start | bytes 393224 | tf_op jit(solution)/shard_map/ppermute | solution.py:469
  66.4 6.7 %collective-permute-start.8 = (bf16[64,1024]{1,0:T(8,128)(2,1)S(1)}, bf16[64,1024]{1,0:T(8,128)(2,1)S(1)}, u32[]{:S(2)}, u32[]{:S(2)}) collective-permute-start(bf16[64,1024]{1,0:T(8,128)(2,1)S(1)} %get-tuple-element.87), channel_id=1, source_target_pairs={{1,0},{2,1},{3,2},{4,3},{5,4},{6,5},{7,6},{9,8},{10,9},{11,10},{12... | collective-permute-start | bytes 393224 | tf_op jit(solution)/shard_map/ppermute | solution.py:468
  67.9 10.7 %collective-permute-start.12 = (bf16[128,640]{1,0:T(8,128)(2,1)S(1)}, bf16[128,640]{1,0:T(8,128)(2,1)S(1)}, u32[]{:S(2)}, u32[]{:S(2)}) collective-permute-start(bf16[128,640]{1,0:T(8,128)(2,1)S(1)} %get-tuple-element.106), channel_id=1, source_target_pairs={{0,2},{1,3},{2,0},{3,1},{4,6},{5,7},{6,4},{7,5},{8,10},{9,11},{10,... | collective-permute-start | bytes 491528 | tf_op jit(solution)/shard_map/ppermute | solution.py:338
  72.7 5.9 %collective-permute-start.10 = (bf16[128,640]{1,0:T(8,128)(2,1)S(1)}, bf16[128,640]{1,0:T(8,128)(2,1)S(1)}, u32[]{:S(2)}, u32[]{:S(2)}) collective-permute-start(bf16[128,640]{1,0:T(8,128)(2,1)S(1)} %get-tuple-element.107), channel_id=1, source_target_pairs={{0,4},{1,5},{2,6},{3,7},{4,0},{5,1},{6,2},{7,3},{8,12},{9,13},{10,... | collective-permute-start | bytes 491528 | tf_op jit(solution)/shard_map/ppermute | solution.py:338
  78.8 11.3 %collective-permute-start.22 = (bf16[32,1280]{1,0:T(8,128)(2,1)S(1)}, bf16[32,1280]{1,0:T(8,128)(2,1)S(1)}, u32[]{:S(2)}, u32[]{:S(2)}) collective-permute-start(bf16[32,1280]{1,0:T(8,128)(2,1)S(1)} %get-tuple-element.118), channel_id=1, source_target_pairs={{0,24},{8,16},{16,8},{24,0},{1,25},{9,17},{17,9},{25,1},{2,26},{10... | collective-permute-start | bytes 245768 | tf_op jit(solution)/shard_map/ppermute | solution.py:352
  80.3 9.9 %collective-permute-start.20 = (bf16[32,1280]{1,0:T(8,128)(2,1)S(1)}, bf16[32,1280]{1,0:T(8,128)(2,1)S(1)}, u32[]{:S(2)}, u32[]{:S(2)}) collective-permute-start(bf16[32,1280]{1,0:T(8,128)(2,1)S(1)} %get-tuple-element.120), channel_id=1, source_target_pairs={{0,8},{8,0},{16,24},{24,16},{1,9},{9,1},{17,25},{25,17},{2,10},{10... | collective-permute-start | bytes 245768 | tf_op jit(solution)/shard_map/ppermute | solution.py:352
  80.3 9.9 %collective-permute-start.21 = (bf16[32,1280]{1,0:T(8,128)(2,1)S(1)}, bf16[32,1280]{1,0:T(8,128)(2,1)S(1)}, u32[]{:S(2)}, u32[]{:S(2)}) collective-permute-start(bf16[32,1280]{1,0:T(8,128)(2,1)S(1)} %get-tuple-element.121), channel_id=1, source_target_pairs={{0,16},{8,24},{16,0},{24,8},{1,17},{9,25},{17,1},{25,9},{2,18},{10... | collective-permute-start | bytes 245768 | tf_op jit(solution)/shard_map/ppermute | solution.py:352
  83.3 6.2 %collective-permute-start.17 = (bf16[32,1024]{1,0:T(8,128)(2,1)S(1)}, bf16[32,1024]{1,0:T(8,128)(2,1)S(1)}, u32[]{:S(2)}, u32[]{:S(2)}) collective-permute-start(bf16[32,1024]{1,0:T(8,128)(2,1)S(1)} %get-tuple-element.124), channel_id=1, source_target_pairs={{0,8},{8,0},{16,24},{24,16},{1,9},{9,1},{17,25},{25,17},{2,10},{10... | collective-permute-start | bytes 196616 | tf_op jit(solution)/shard_map/ppermute | solution.py:352
  83.3 6.9 %collective-permute-start.18 = (bf16[32,1024]{1,0:T(8,128)(2,1)S(1)}, bf16[32,1024]{1,0:T(8,128)(2,1)S(1)}, u32[]{:S(2)}, u32[]{:S(2)}) collective-permute-start(bf16[32,1024]{1,0:T(8,128)(2,1)S(1)} %get-tuple-element.125), channel_id=1, source_target_pairs={{0,16},{8,24},{16,0},{24,8},{1,17},{9,25},{17,1},{25,9},{2,18},{10... | collective-permute-start | bytes 196616 | tf_op jit(solution)/shard_map/ppermute | solution.py:352

commit v4 on v3

v4 whole, which is shorter than its diff:
```python
import functools

import jax
import jax.numpy as jnp
from jax import lax
from jax.experimental import pallas as pl
from jax.experimental.pallas import tpu as pltpu
from jax.sharding import PartitionSpec as P

HEAD_DIM = 64
LANES = 128
GROUPS = 3
ALPHA = 0.95
SOFTENING = 0.5
BF = jnp.bfloat16
F32 = jnp.float32
NN = (((1,), (0,)), ((), ()))
NT = (((1,), (1,)), ((), ()))
TN = (((0,), (0,)), ((), ()))


def mm(a, b, dims=NN):
    return lax.dot_general(a, b, dims, preferred_element_type=F32)


def call(body, out_shape, args, scratch=(), hbm=(), limit=24, flops=1):
    args = [pltpu.with_memory_space_constraint(x, pltpu.HBM) if i in hbm else x for i, x in enumerate(args)]
    return pl.pallas_call(
        body,
        out_shape=out_shape,
        in_specs=[
            pl.BlockSpec(memory_space=pltpu.HBM if i in hbm else pltpu.VMEM) for i in range(len(args))
        ],
        out_specs=jax.tree.map(lambda _: pl.BlockSpec(memory_space=pltpu.VMEM), out_shape),
        scratch_shapes=list(scratch),
        compiler_params=pltpu.CompilerParams(vmem_limit_bytes=limit * 1024 * 1024),
        cost_estimate=pl.CostEstimate(flops=flops, bytes_accessed=1, transcendentals=0),
    )(*args)


def sds(shape, dtype):
    return jax.ShapeDtypeStruct(shape, dtype)


def one_hot_rows(rows, node_count):
    nodes = lax.broadcasted_iota(jnp.int32, (node_count, rows.shape[1]), 0).astype(rows.dtype)
    return (nodes == rows).astype(F32).astype(BF)


def start_copies(pairs, sems):
    copies = [pltpu.make_async_copy(src, dst, sems.at[i]) for i, (src, dst) in enumerate(pairs)]
    for copy in copies:
        copy.start()
    return copies


def pick_body(hidden_hbm, halo_hbm, hidden_ref, halo_ref, down_ref, up_ref, sems):
    for copy in start_copies([(hidden_hbm, hidden_ref), (halo_hbm, halo_ref)], sems):
        copy.wait()
    members, nodes, _ = hidden_ref.shape
    rim = halo_ref.shape[1]
    for row, out_ref in ((0, down_ref), (1, up_ref)):
        hot = one_hot_rows(halo_ref[row : row + 1, :], nodes)
        for m in range(members):
            out_ref[m * rim : (m + 1) * rim, :] = mm(hot, hidden_ref[m], TN).astype(BF)


def prepare_body(
    hidden_ref, wo_ref, hp_ref, q_ref, kvw_ref, init_ref, chw_ref, lat_ref,
    kv_ref, pt_ref, p_ref, base_ref, weight_ref, chw_pad, hp_pad,
):
    channels = hp_ref.shape[0]
    hp_pad[...] = jnp.zeros_like(hp_pad)
    hp_pad[0:channels, :] = hp_ref[...].astype(F32)
    hp_t = hp_pad[...].astype(BF)
    chw_pad[:, 0:channels] = jnp.broadcast_to(chw_ref[...], (8, channels))
    weight_ref[...] = chw_pad[...].T[0:channels, 0:1] * lat_ref[...]
    base_ref[...] = mm(hp_t, q_ref[...], NT)
    base_ref[0:channels, :] = base_ref[0:channels, :] + init_ref[...]
    p = mm(hp_t, wo_ref[...], NT)
    p_ref[...] = p.astype(BF)
    pt_ref[...] = p.T.astype(BF)
    hidden = jnp.concatenate([hidden_ref[m] for m in range(hidden_ref.shape[0])], axis=0)
    kv_ref[...] = mm(hidden, kvw_ref[...]).astype(BF)


def split_heads(block):
    low = lax.broadcasted_iota(jnp.int32, block.shape, 1) < HEAD_DIM
    zero = jnp.zeros_like(block)
    return jnp.concatenate([jnp.where(low, block, zero), jnp.where(low, zero, block)], axis=0)


def forward_body(
    send_rows,
    below_ref, above_ref, own_ref, kvw_ref, q_ref, src_ref, p_ref,
    kv_ref, gate_ref, slope_ref, merged_ref, part_ref, send_ref,
):
    members, ext, width2 = kv_ref.shape
    width = width2 // 2
    points = q_ref.shape[0]
    nodes = own_ref.shape[0] // members
    rim = below_ref.shape[0] // members
    halo = mm(jnp.concatenate([below_ref[...], above_ref[...]], axis=0), kvw_ref[...]).astype(BF)
    for m in range(members):
        kv_ref[m, 0:nodes, :] = own_ref[m * nodes : (m + 1) * nodes, :]
        kv_ref[m, nodes : nodes + rim, :] = halo[m * rim : (m + 1) * rim]
        kv_ref[m, nodes + rim : ext, :] = halo[(members + m) * rim : (members + m + 1) * rim]
    rows = lax.broadcasted_iota(jnp.int32, (ext, points), 0)
    mask = rows == src_ref[0:1, :]
    for e in range(1, src_ref.shape[0]):
        mask = mask | (rows == src_ref[e : e + 1, :])
    mask = mask.astype(F32)
    mask = jnp.concatenate([mask, mask], axis=0)
    scale = HEAD_DIM ** (-0.5)
    for pair in range(width // LANES):
        cols = slice(pair * LANES, (pair + 1) * LANES)
        vcols = slice(width + pair * LANES, width + (pair + 1) * LANES)
        q = q_ref[:, cols]
        for m in range(members):
            th = jnp.tanh(mm(split_heads(kv_ref[m, :, cols]), q, NT) * (0.5 * scale))
            gate = ((0.5 * th + 0.5) * mask).astype(BF)
            gate_ref[pair, m] = gate
            slope_ref[pair, m] = ((0.25 * scale) * mask * (1.0 - th * th)).astype(BF)
            merged_ref[m, cols, :] = mm(split_heads(kv_ref[m, :, vcols]), gate, TN).astype(BF)
    sent = []
    for m in range(members):
        part = mm(p_ref[...], merged_ref[m])
        part_ref[m] = part
        sent.append(part[0:send_rows])
    filler = send_ref.shape[0] - members * send_rows
    if filler:
        sent.append(jnp.zeros((filler, points), F32))
    send_ref[...] = jnp.concatenate(sent, axis=0).astype(BF)


def halving_orders(n_member, n_band):
    chips = [("band", bit) for bit in range(1, n_band.bit_length() - 1)]
    member = [("member", bit) for bit in range(n_member.bit_length() - 1)]
    turn = chips + member[:1]
    return [turn[i:] + turn[:i] for i in range(GROUPS)], member[1:]


def unit_order(order, n_member, n_band):
    def key(unit):
        return [-((2 * unit[0] if axis == "band" else unit[1]) >> bit & 1) for axis, bit in order]

    return sorted([(c, m) for c in range(n_band // 2) for m in range(n_member)], key=key)


def destination_rows(member, band, n_member, n_band, rw):
    chip, core = band // 2, band % 2
    for rel_core in (1, 0):
        for rel_chip in range(n_band // 2):
            to_band = (chip ^ rel_chip) * 2 + (core ^ rel_core)
            for rel_member in range(n_member):
                yield pl.multiple_of(((member ^ rel_member) * n_band + to_band) * rw, rw)


def reorder(src_ref, n_member, n_band):
    rw = src_ref.shape[0] // (n_member * n_band)
    member, band = lax.axis_index("member"), lax.axis_index("band")
    starts = destination_rows(member, band, n_member, n_band, rw)
    return jnp.concatenate([src_ref[pl.ds(start, rw), :] for start in starts], axis=0)


def store_group(rows, group, n_member, n_band, at, out_refs):
    orders, rest = halving_orders(n_member, n_band)
    units = unit_order(orders[group] + rest, n_member, n_band)
    rw = rows.shape[0] // (n_member * n_band)
    for core, ref in enumerate(out_refs):
        starts = [((core * (n_band // 2) + chip) * n_member + member) * rw for chip, member in units]
        ordered = jnp.concatenate([rows[i : i + rw] for i in starts], axis=0)
        ref[:, at : at + rows.shape[1]] = ordered.astype(BF)


def transpose_body(n_member, n_band, hidden_ref, below_ref, above_ref, out_ref, turned):
    members, nodes, _ = hidden_ref.shape
    rim = below_ref.shape[0] // members
    parts = []
    for m in range(members):
        parts.append(hidden_ref[m])
        parts.append(below_ref[m * rim : (m + 1) * rim, :])
        parts.append(above_ref[m * rim : (m + 1) * rim, :])
    turned[...] = jnp.concatenate(parts, axis=0).astype(F32).T
    out_ref[...] = reorder(turned, n_member, n_band).astype(BF)


def select_heads(block):
    half = block.shape[0] // 2
    low = lax.broadcasted_iota(jnp.int32, (half, block.shape[1]), 1) < HEAD_DIM
    return jnp.where(low, block[:half], block[half:])


def soft_slope(v):
    return v * lax.rsqrt(v * v + SOFTENING * SOFTENING)


def value_body(n_member, n_band, *refs):
    recv_refs = refs[: n_member - 1]
    part_ref, base_ref, truth_ref, weight_ref, pt_ref, gate_ref, ext_ref = refs[n_member - 1 : n_member + 6]
    grad_ref, dm_ref, ng_ref, *out_refs = refs[n_member + 6 :]
    group_width = out_refs[0].shape[1]
    members, width, _ = dm_ref.shape
    ext = ng_ref.shape[0] // members
    channels = truth_ref.shape[0]
    total = members * n_member
    spread = (1.0 - (1.0 - ALPHA) / total) / (total * (total - 1))

    grad_ref[...] = jnp.zeros_like(grad_ref)
    own = [part_ref[m, 0:channels, :] for m in range(members)]
    sent_rows = -(-channels // 8) * 8
    others = []
    for ref in recv_refs:
        rows = ref[...].astype(F32)
        others += [rows[k * sent_rows : k * sent_rows + channels] for k in range(members)]
    for m in range(members):
        slopes = jnp.zeros_like(own[m])
        for k in range(members):
            if k != m:
                slopes = slopes + soft_slope(own[m] - own[k])
        for other in others:
            slopes = slopes + soft_slope(own[m] - other)
        gap = soft_slope(own[m] + base_ref[0:channels, :] - truth_ref[...])
        grad_ref[m, 0:channels, :] = (weight_ref[...] * (gap / total - spread * slopes)).astype(BF)
    for m in range(members):
        dm_ref[m] = mm(pt_ref[...], grad_ref[m]).astype(BF)
    for pair in range(width // LANES):
        cols = slice(pair * LANES, (pair + 1) * LANES)
        for m in range(members):
            result = mm(gate_ref[pair, m], dm_ref[m, cols, :], NT)
            ng_ref[m * ext : (m + 1) * ext, cols] = select_heads(result).astype(BF)
    store_group(mm(ext_ref[...], ng_ref[:, 0:group_width]), 0, n_member, n_band, 0, out_refs)


def key_body(
    n_member, n_band, grad_ref, dm_ref, kv_ref, slope_ref, q_ref, merged_ref, wo_ref, ext_ref, ngv_ref,
    ng_ref, *refs
):
    out_refs, turned = refs[:-1], refs[-1]
    members, ext, width2 = kv_ref.shape
    width = width2 // 2
    group_width = out_refs[0].shape[1]
    for pair in range(width // LANES):
        cols = slice(pair * LANES, (pair + 1) * LANES)
        vcols = slice(width + pair * LANES, width + (pair + 1) * LANES)
        for m in range(members):
            dgate = mm(split_heads(kv_ref[m, :, vcols]), dm_ref[m, cols, :])
            dscore = (dgate * slope_ref[pair, m].astype(F32)).astype(BF)
            ng_ref[m * ext : (m + 1) * ext, cols] = select_heads(mm(dscore, q_ref[:, cols])).astype(BF)
    m_t = sum(mm(grad_ref[m], merged_ref[m], NT) for m in range(members))
    head_t = sum(mm(grad_ref[m], q_ref[...]) for m in range(members)) + mm(m_t.astype(BF), wo_ref[...])
    turned[...] = jnp.concatenate([m_t, head_t], axis=0).T
    pieces = [(ngv_ref, group_width, width), (ng_ref, 0, width), (None, 0, 2 * LANES)]
    at = group_width
    for ref, first, last in pieces:
        while first < last:
            group, offset = at // group_width, at % group_width
            take = min(last - first, group_width - offset)
            if ref is None:
                rows = reorder(turned, n_member, n_band)
            else:
                rows = mm(ext_ref[...], ref[:, first : first + take])
            outs = out_refs[2 * (group - 1) : 2 * group]
            store_group(rows, group, n_member, n_band, offset, outs)
            first, at = first + take, at + take


def extended_grad_body(members, nodes, rim, ngk_ref, ngv_ref, kvw_ref, own_ref, down_ref, up_ref):
    ext = nodes + 2 * rim
    width = kvw_ref.shape[0]
    rows = mm(ngk_ref[...], kvw_ref[:, 0:width], NT) + mm(ngv_ref[...], kvw_ref[:, width:], NT)
    for m in range(members):
        at = m * ext
        own_ref[m] = rows[at : at + nodes]
        down_ref[m * rim : (m + 1) * rim, :] = rows[at + nodes : at + nodes + rim].astype(BF)
        up_ref[m * rim : (m + 1) * rim, :] = rows[at + nodes + rim : at + ext].astype(BF)


def hidden_body(own_ref, from_below_ref, from_above_ref, halo_ref, out_ref):
    members, nodes, _ = own_ref.shape
    rim = halo_ref.shape[1]
    low = one_hot_rows(halo_ref[0:1, :], nodes)
    high = one_hot_rows(halo_ref[1:2, :], nodes)
    for m in range(members):
        rows = slice(m * rim, (m + 1) * rim)
        out_ref[m] = own_ref[m] + mm(low, from_below_ref[rows, :]) + mm(high, from_above_ref[rows, :])


def finish_body(devices, own_ref, arrived_ref, hp_ref, kv_ref, out_ref, head_ref):
    width = kv_ref.shape[1] // 2
    channels = hp_ref.shape[0]
    total = (own_ref[...] + arrived_ref[...].astype(F32)) * (1.0 / devices)
    kv_ref[:, width:] = total[:, 0:width]
    kv_ref[:, 0:width] = total[:, width : 2 * width]
    m_rows = total[:, 2 * width : 2 * width + channels]
    high = m_rows.astype(BF)
    low = (m_rows - high.astype(F32)).astype(BF)
    out_ref[...] = mm(high, hp_ref[...]) + mm(low, hp_ref[...])
    head_ref[...] = total[:, 2 * width + LANES : 2 * width + LANES + channels]


def add_up(*parts):
    return functools.reduce(lambda a, b: a + b, [p.astype(F32) for p in parts])


def swap(rows, axis, bit, count):
    return lax.ppermute(rows, axis, [(i, i ^ (1 << bit)) for i in range(count)])


def upper(terms):
    return [t[: t.shape[0] // 2] for t in terms]


def lower(terms):
    return [t[t.shape[0] // 2 :] for t in terms]


def shards(
    n_member, n_band,
    hidden, queries, kv_weight, out_weight, head_projection, initial_state, truth,
    latitude_weight, channel_loss_weight, sources, halo_rows,
):
    members, nodes, width = hidden.shape
    points = queries.shape[0]
    channels = head_projection.shape[1]
    rim = halo_rows.shape[1]
    ext = nodes + 2 * rim
    pairs = width // LANES
    devices = n_member * n_band
    rw = width // devices
    chips = n_band // 2
    send_rows = -(-channels // 8) * 8
    to_above = [(i, i + 1) for i in range(n_band - 1)]
    to_below = [(i + 1, i) for i in range(n_band - 1)]

    own_hidden, halo, down, up = call(
        pick_body,
        [sds(hidden.shape, BF), sds(halo_rows.shape, jnp.int32)] + [sds((members * rim, width), BF)] * 2,
        (hidden, halo_rows),
        [pltpu.SemaphoreType.DMA((2,))],
        hbm=(0, 1),
        flops=10**10,
    )
    below = lax.ppermute(up, "band", to_above)
    above = lax.ppermute(down, "band", to_below)

    hp = head_projection.T
    own_kv, pt, p, base, weight = call(
        prepare_body,
        [
            sds((members * nodes, 2 * width), BF),
            sds((width, LANES), BF),
            sds((LANES, width), BF),
            sds((LANES, points), F32),
            sds((channels, points), F32),
        ],
        (
            own_hidden, out_weight, hp, queries, kv_weight, initial_state,
            channel_loss_weight[None, :], latitude_weight[None, :],
        ),
        [pltpu.VMEM((8, LANES), F32), pltpu.VMEM((LANES, width), F32)],
    )

    kv, gates, slopes, merged, part, sent = call(
        functools.partial(forward_body, send_rows),
        [
            sds((members, ext, 2 * width), BF),
            sds((pairs, members, 2 * ext, points), BF),
            sds((pairs, members, 2 * ext, points), BF),
            sds((members, width, points), BF),
            sds((members, LANES, points), F32),
            sds((-(-members * send_rows // 16) * 16, points), BF),
        ],
        (below, above, own_kv, kv_weight, queries, sources, p),
    )

    received = [
        lax.ppermute(sent, "member", [(i, i ^ s) for i in range(n_member)]) for s in range(1, n_member)
    ]

    ext_t = call(
        functools.partial(transpose_body, n_member, n_band),
        sds((width, members * ext), BF),
        (own_hidden, below, above),
        [pltpu.VMEM((width, members * ext), F32)],
    )

    extra = 2 * LANES
    group_width = (2 * width + extra) // GROUPS
    grad, dm, ng_value, send, keep = call(
        functools.partial(value_body, n_member, n_band),
        [sds((members, LANES, points), BF), sds((members, width, points), BF), sds((members * ext, width), BF)]
        + [sds((width // 2, group_width), BF)] * 2,
        (*received, part, base, truth, weight, pt, gates, ext_t),
    )
    groups = [[keep, swap(send, "band", 0, n_band)]]
    ng_key, *outs = call(
        functools.partial(key_body, n_member, n_band),
        [sds((members * ext, width), BF)] + [sds((width // 2, group_width), BF)] * (2 * (GROUPS - 1)),
        (grad, dm, kv, slopes, queries, merged, out_weight, ext_t, ng_value),
        [pltpu.VMEM((width, extra), F32)],
    )
    for i in range(GROUPS - 1):
        groups.append([outs[2 * i + 1], swap(outs[2 * i], "band", 0, n_band)])

    count = {"member": n_member, "band": n_band}
    turns, rest = halving_orders(n_member, n_band)
    for step in range(len(turns[0])):
        outgoing = [add_up(*upper(terms)).astype(BF) for terms in groups]
        if step == 0:
            outgoing[0], groups[1:] = lax.optimization_barrier((outgoing[0], groups[1:]))
            outgoing[1:] = [add_up(*upper(terms)).astype(BF) for terms in groups[1:]]
            outgoing, ng_key = lax.optimization_barrier((outgoing, ng_key))
            own_grad, back_down, back_up = call(
                functools.partial(extended_grad_body, members, nodes, rim),
                [sds((members, nodes, width), F32)] + [sds((members * rim, width), BF)] * 2,
                (ng_key, ng_value, kv_weight),
            )
            from_above = lax.ppermute(back_down, "band", to_below)
            from_below = lax.ppermute(back_up, "band", to_above)
        arrived = [swap(out, *turn[step], count[turn[step][0]]) for out, turn in zip(outgoing, turns)]
        if step == 0:
            arrived, from_above, from_below = lax.optimization_barrier((arrived, from_above, from_below))
        groups = [lower(terms) + [new] for terms, new in zip(groups, arrived)]
    hidden_grad = call(
        hidden_body,
        sds((members, nodes, width), F32),
        (own_grad, from_below, from_above, halo),
    )
    terms = [jnp.concatenate([add_up(*group) for group in groups], axis=1)]
    for axis, bit in rest:
        arrived = swap(add_up(*upper(terms)).astype(BF), axis, bit, count[axis])
        terms = lower(terms) + [arrived]

    kv_grad, out_grad, head_grad = call(
        functools.partial(finish_body, devices),
        [sds((rw, 2 * width), F32), sds((rw, width), F32), sds((rw, channels), F32)],
        (add_up(*terms[:-1]), terms[-1], hp),
    )
    return hidden_grad, kv_grad, out_grad, head_grad


def solution(mesh):
    placed = (
        P("member", "band", None),
        P("band", None),
        P(),
        P(),
        P(),
        P(None, "band"),
        P(None, "band"),
        P("band"),
        P(),
        P(None, "band"),
        P("band", None),
    )
    return jax.shard_map(
        functools.partial(shards, mesh.shape["member"], mesh.shape["band"]),
        mesh=mesh,
        in_specs=placed,
        out_specs=(
            P("member", "band", None),
            P(("member", "band"), None),
            P(("member", "band"), None),
            P(("member", "band"), None),
        ),
        check_vma=False,
    )
```

time: 91.3 us -> 77 us (0.84)
  starting transfers between devices: 36.7 us -> 29.3 us
  Pallas kernels: 21.1 us -> 15.8 us
  waiting for transfers between devices: 31.5 us -> 29.8 us
    ppermute x16 -> x13, starting transfers between devices: 25.4 us -> 16.7 us  [swap(): return lax.ppermute(rows, axis, [(i, i ^ 1 << bit) for i in range(count)])]
    pallas_call x10 -> x9, Pallas kernels: 21.1 us -> 15.8 us  [call(): pl.pallas_call(body, out_shape=out_shape, in_specs=[pl.BlockSpec(memory_s...]
    ppermute x16 -> x13, waiting for transfers between devices: 22.3 us -> 18.3 us  [swap(): return lax.ppermute(rows, axis, [(i, i ^ 1 << bit) for i in range(count)])]
    ppermute x1, waiting for transfers between devices: 0.01 us -> 2.42 us  [shards(): above = lax.ppermute(down, 'band', to_below)]
    ppermute x1, starting transfers between devices: 1.3 us -> 3.04 us  [shards(): from_below = lax.ppermute(back_up, 'band', to_above)]
    ppermute x3, waiting for transfers between devices: 9.17 us -> 8.15 us  [shards(): lax.ppermute(sent, 'member', [(i, i ^ s) for i in range(n_member)])]
    ppermute x1, waiting for transfers between devices: 0.01 us -> 0.95 us  [shards(): from_below = lax.ppermute(back_up, 'band', to_above)]
  transfers between devices with their start and end apart: 23 -> 20, of which waited for: 9 -> 15; matrix products, arithmetic and copies ran while one was open for 1% -> 1% of each run, Pallas kernels for 11% -> 9%
where the time goes in v4:
time: 77 us; the launch traced here: 76.8 us
  waiting for transfers between devices  29.8 us (39%)
  starting transfers between devices  29.3 us (38%)
  Pallas kernels  15.8 us (21%)
  between operations  0.92 us (1%)
  other arithmetic  0.91 us (1%)
    ppermute x13, waiting for transfers between devices, swap(): return lax.ppermute(rows, axis, [(i, i ^ 1 << bit) for i in range(count)])  18.3 us
    ppermute x13, starting transfers between devices, swap(): return lax.ppermute(rows, axis, [(i, i ^ 1 << bit) for i in range(count)])  16.7 us
    pallas_call x9, Pallas kernels, call(): pl.pallas_call(body, out_shape=out_shape, in_specs=[pl.BlockSpec(memory_s...  15.8 us
    ppermute x3, waiting for transfers between devices, shards(): lax.ppermute(sent, 'member', [(i, i ^ s) for i in range(n_member)])  8.15 us
    ppermute x3, starting transfers between devices, shards(): lax.ppermute(sent, 'member', [(i, i ^ s) for i in range(n_member)])  4.45 us
    ppermute x1, starting transfers between devices, shards(): from_below = lax.ppermute(back_up, 'band', to_above)  3.04 us
    ppermute x1, starting transfers between devices, shards(): below = lax.ppermute(up, 'band', to_above)  2.5 us
    ppermute x1, waiting for transfers between devices, shards(): above = lax.ppermute(down, 'band', to_below)  2.42 us
  transfers between devices with their start and end apart: 20, of which 15 were waited for; matrix products, arithmetic and copies ran while one was open for 1% of the time, Pallas kernels for 9%

profile of v4, /device:TPU:0, one launch (start us, length us, event | category | flops | bytes accessed | tf_op | source)
XLA Modules:
  0.0 76.8 jit_solution(13510156533129722355)
XLA Ops:
  0.7 1.4 %shard_map.138 = (bf16[2,64,1024]{2,1,0:T(8,128)(2,1)S(1)}, s32[2,32]{1,0:T(2,128)S(1)}, bf16[64,1024]{1,0:T(8,128)(2,1)S(1)}, bf16[64,1024]{1,0:T(8,128)(2,1)S(1)}) custom-call(bf16[2,64,1024]{2,1,0:T(8,128)(2,1)} %hidden_hbm.1, s32[2,32]{1,0:T(2,128)} %halo_hbm.1), custom_call_target="tpu_custom_call" | custom-call | flops 10000000000 | bytes 1 | tf_op jit(solution)/shard_map/pallas_call | solution.py:28
  2.1 2.5 %collective-permute-start = (bf16[64,1024]{1,0:T(8,128)(2,1)S(1)}, bf16[64,1024]{1,0:T(8,128)(2,1)S(1)}, u32[]{:S(2)}, u32[]{:S(2)}) collective-permute-start(bf16[64,1024]{1,0:T(8,128)(2,1)S(1)} %get-tuple-element.49), channel_id=1, source_target_pairs={{0,1},{1,2},{2,3},{3,4},{4,5},{5,6},{6,7},{8,9},{9,10},{10,11},{11... | collective-permute-start | bytes 393224 | tf_op jit(solution)/shard_map/ppermute | solution.py:344
  4.6 1.3 %collective-permute-start.1 = (bf16[64,1024]{1,0:T(8,128)(2,1)S(1)}, bf16[64,1024]{1,0:T(8,128)(2,1)S(1)}, u32[]{:S(2)}, u32[]{:S(2)}) collective-permute-start(bf16[64,1024]{1,0:T(8,128)(2,1)S(1)} %get-tuple-element.50), channel_id=1, source_target_pairs={{1,0},{2,1},{3,2},{4,3},{5,4},{6,5},{7,6},{9,8},{10,9},{11,10},{12... | collective-permute-start | bytes 393224 | tf_op jit(solution)/shard_map/ppermute | solution.py:345
  6.0 1.5 %shard_map.139 = (bf16[128,2048]{1,0:T(8,128)(2,1)S(1)}, bf16[1024,128]{1,0:T(8,128)(2,1)S(1)}, bf16[128,1024]{1,0:T(8,128)(2,1)S(1)}, f32[128,256]{1,0:T(8,128)S(1)}, f32[100,256]{1,0:T(8,128)S(1)}) custom-call(bf16[2,64,1024]{2,1,0:T(8,128)(2,1)S(1)} %get-tuple-element.51.hidden_ref, bf16[1024,1024]{1,0:T(8,128)(2,1)S(1)} %copy-done.1, ...), custom_call_target="tpu_custom_call" | custom-call | flops 1 | bytes 1 | tf_op jit(solution)/shard_map/pallas_call | solution.py:28
  7.5 2.4 %collective-permute-done.1.above_ref = bf16[64,1024]{1,0:T(8,128)(2,1)S(1)} collective-permute-done((bf16[64,1024]{1,0:T(8,128)(2,1)S(1)}, bf16[64,1024]{1,0:T(8,128)(2,1)S(1)}, u32[]{:S(2)}, u32[]{:S(2)}) %collective-permute-start.1) | collective-permute-done | bytes 131104 | tf_op jit(solution)/shard_map/ppermute | solution.py:345
  9.9 4.9 %shard_map.140 = (bf16[2,128,2048]{2,1,0:T(8,128)(2,1)S(1)}, bf16[8,2,256,256]{3,2,1,0:T(8,128)(2,1)S(1)}, bf16[8,2,256,256]{3,2,1,0:T(8,128)(2,1)S(1)}, bf16[2,...) custom-call(bf16[64,1024]{1,0:T(8,128)(2,1)S(1)} %collective-permute-done.below_ref, ...), custom_call_target="tpu_custom_call" | custom-call | flops 1 | bytes 1 | tf_op jit(solution)/shard_map/pallas_call | solution.py:28
  14.9 3.7 %collective-permute-start.4 = (bf16[208,256]{1,0:T(8,128)(2,1)S(1)}, bf16[208,256]{1,0:T(8,128)(2,1)S(1)}, u32[]{:S(2)}, u32[]{:S(2)}) collective-permute-start(bf16[208,256]{1,0:T(8,128)(2,1)S(1)} %get-tuple-element.54), channel_id=1, source_target_pairs={{0,24},{8,16},{16,8},{24,0},{1,25},{9,17},{17,9},{25,1},{2,26},{10... | collective-permute-start | bytes 319496 | tf_op jit(solution)/shard_map/ppermute | solution.py:378
  18.5 0.8 %collective-permute-start.2 = (bf16[208,256]{1,0:T(8,128)(2,1)S(1)}, bf16[208,256]{1,0:T(8,128)(2,1)S(1)}, u32[]{:S(2)}, u32[]{:S(2)}) collective-permute-start(bf16[208,256]{1,0:T(8,128)(2,1)S(1)} %get-tuple-element.54), channel_id=1, source_target_pairs={{0,8},{8,0},{16,24},{24,16},{1,9},{9,1},{17,25},{25,17},{2,10},{10... | collective-permute-start | bytes 319496 | tf_op jit(solution)/shard_map/ppermute | solution.py:378
  19.3 0.3 shard_map.141.refs_9_.ext_ref
  19.6 2.0 %collective-permute-done.4.refs_2_ = bf16[208,256]{1,0:T(8,128)(2,1)S(1)} collective-permute-done((bf16[208,256]{1,0:T(8,128)(2,1)S(1)}, bf16[208,256]{1,0:T(8,128)(2,1)S(1)}, u32[]{:S(2)}, u32[]{:S(2)}) %collective-permute-start.4) | collective-permute-done | bytes 106528 | tf_op jit(solution)/shard_map/ppermute | solution.py:378
  21.6 6.2 %collective-permute-done.3.refs_1_ = bf16[208,256]{1,0:T(8,128)(2,1)S(1)} collective-permute-done((bf16[208,256]{1,0:T(8,128)(2,1)S(1)}, bf16[208,256]{1,0:T(8,128)(2,1)S(1)}, u32[]{:S(2)}, u32[]{:S(2)}) %collective-permute-start.3) | collective-permute-done | bytes 106528 | tf_op jit(solution)/shard_map/ppermute | solution.py:378
  27.8 1.8 %shard_map.142 = (bf16[2,128,256]{2,1,0:T(8,128)(2,1)S(1)}, bf16[2,1024,256]{2,1,0:T(8,128)(2,1)S(1)}, bf16[256,1024]{1,0:T(8,128)(2,1)S(1)}, bf16[512,768]{1,0:T(8,128)(2,1)S(1)}, bf16[512,768]{1,0:T(8,128)(2,1)S(1)}) custom-call(bf16[208,256]{1,0:T(8,128)(2,1)S(1)} %collective-permute-done.2.refs_0_, bf16[208,256]{1,0:T(8,128)(2,1)S(1)} %collective-permute-done.3.refs_1_, ...), custom_call_target="tpu_custom_call" | custom-call | flops 1 | bytes 1 | tf_op jit(solution)/shard_map/pallas_call | solution.py:28
  29.5 1.0 %collective-permute-start.5 = (bf16[512,768]{1,0:T(8,128)(2,1)S(1)}, bf16[512,768]{1,0:T(8,128)(2,1)S(1)}, u32[]{:S(2)}, u32[]{:S(2)}) collective-permute-start(bf16[512,768]{1,0:T(8,128)(2,1)S(1)} %get-tuple-element.61), channel_id=1, source_target_pairs={{0,1},{1,0},{2,3},{3,2},{4,5},{5,4},{6,7},{7,6},{8,9},{9,8},{10,11... | collective-permute-start | bytes 2359304 | tf_op jit(solution)/shard_map/ppermute | solution.py:307
  30.5 2.7 %shard_map.143 = (bf16[256,1024]{1,0:T(8,128)(2,1)S(1)}, bf16[512,768]{1,0:T(8,128)(2,1)S(1)}, bf16[512,768]{1,0:T(8,128)(2,1)S(1)}, bf16[512,768]{1,0:T(8,128)(2,1)S(1)}, bf16[512,768]{1,0:T(8,128)(2,1)S(1)}) custom-call(bf16[2,128,256]{2,1,0:T(8,128)(2,1)S(1)} %get-tuple-element.62.grad_ref, bf16[2,1024,256]{2,1,0:T(8,128)(2,1)S(1)} %get-tuple-element.63.dm_ref, ...), custom_call_target="tpu_custom_call" | custom-call | flops 1 | bytes 1 | tf_op jit(solution)/shard_map/pallas_call | solution.py:28
  33.2 0.1 collective-permute-start.6
  33.3 0.5 collective-permute-start.7
  33.8 0.1 add_convert_fusion.2
  33.9 1.7 %collective-permute-done.6 = bf16[512,768]{1,0:T(8,128)(2,1)S(1)} collective-permute-done((bf16[512,768]{1,0:T(8,128)(2,1)S(1)}, bf16[512,768]{1,0:T(8,128)(2,1)S(1)}, u32[]{:S(2)}, u32[]{:S(2)}) %collective-permute-start.6) | collective-permute-done | bytes 786464 | tf_op jit(solution)/shard_map/ppermute | solution.py:307
  35.6 1.1 %collective-permute-done.7 = bf16[512,768]{1,0:T(8,128)(2,1)S(1)} collective-permute-done((bf16[512,768]{1,0:T(8,128)(2,1)S(1)}, bf16[512,768]{1,0:T(8,128)(2,1)S(1)}, u32[]{:S(2)}, u32[]{:S(2)}) %collective-permute-start.7) | collective-permute-done | bytes 786464 | tf_op jit(solution)/shard_map/ppermute | solution.py:307
  36.7 0.2 add_convert_fusion
  36.9 3.2 %collective-permute-start.8 = (bf16[256,768]{1,0:T(8,128)(2,1)S(1)}, bf16[256,768]{1,0:T(8,128)(2,1)S(1)}, u32[]{:S(2)}, u32[]{:S(2)}) collective-permute-start(bf16[256,768]{1,0:T(8,128)(2,1)S(1)} %add_convert_fusion.2), channel_id=1, source_target_pairs={{0,2},{1,3},{2,0},{3,1},{4,6},{5,7},{6,4},{7,5},{8,10},{9,11},{10,... | collective-permute-start | bytes 1179656 | tf_op jit(solution)/shard_map/ppermute | solution.py:307
  40.1 1.2 %collective-permute-start.9 = (bf16[256,768]{1,0:T(8,128)(2,1)S(1)}, bf16[256,768]{1,0:T(8,128)(2,1)S(1)}, u32[]{:S(2)}, u32[]{:S(2)}) collective-permute-start(bf16[256,768]{1,0:T(8,128)(2,1)S(1)} %get-tuple-element.81), channel_id=1, source_target_pairs={{0,4},{1,5},{2,6},{3,7},{4,0},{5,1},{6,2},{7,3},{8,12},{9,13},{10,... | collective-permute-start | bytes 1179656 | tf_op jit(solution)/shard_map/ppermute | solution.py:307
  41.3 0.4 collective-permute-start.10
  41.7 1.3 %shard_map.144 = (f32[2,64,1024]{2,1,0:T(8,128)S(1)}, bf16[64,1024]{1,0:T(8,128)(2,1)S(1)}, bf16[64,1024]{1,0:T(8,128)(2,1)S(1)}) custom-call(bf16[256,1024]{1,0:T(8,128)(2,1)S(1)} %get-tuple-element.78.ngk_ref, bf16[256,1024]{1,0:T(8,128)(2,1)S(1)} %get-tuple-element.67.ngv_ref, bf16[1024,2048]{1,0:T(8,128)(2,1)S(1)} %copy-done), custom_call_target="tpu_custom_call" | custom-call | flops 1 | bytes 1 | tf_op jit(solution)/shard_map/pallas_call | solution.py:28
  43.0 1.3 %collective-permute-start.11 = (bf16[64,1024]{1,0:T(8,128)(2,1)S(1)}, bf16[64,1024]{1,0:T(8,128)(2,1)S(1)}, u32[]{:S(2)}, u32[]{:S(2)}) collective-permute-start(bf16[64,1024]{1,0:T(8,128)(2,1)S(1)} %get-tuple-element.83), channel_id=1, source_target_pairs={{1,0},{2,1},{3,2},{4,3},{5,4},{6,5},{7,6},{9,8},{10,9},{11,10},{12... | collective-permute-start | bytes 393224 | tf_op jit(solution)/shard_map/ppermute | solution.py:419
  44.3 3.0 %collective-permute-start.12 = (bf16[64,1024]{1,0:T(8,128)(2,1)S(1)}, bf16[64,1024]{1,0:T(8,128)(2,1)S(1)}, u32[]{:S(2)}, u32[]{:S(2)}) collective-permute-start(bf16[64,1024]{1,0:T(8,128)(2,1)S(1)} %get-tuple-element.84), channel_id=1, source_target_pairs={{0,1},{1,2},{2,3},{3,4},{4,5},{5,6},{6,7},{8,9},{9,10},{10,11},{11... | collective-permute-start | bytes 393224 | tf_op jit(solution)/shard_map/ppermute | solution.py:420
  47.3 1.0 %collective-permute-done.12.from_below_ref = bf16[64,1024]{1,0:T(8,128)(2,1)S(1)} collective-permute-done((bf16[64,1024]{1,0:T(8,128)(2,1)S(1)}, bf16[64,1024]{1,0:T(8,128)(2,1)S(1)}, u32[]{:S(2)}, u32[]{:S(2)}) %collective-permute-start.12) | collective-permute-done | bytes 131104 | tf_op jit(solution)/shard_map/ppermute | solution.py:420
  48.3 1.2 %collective-permute-done.8 = bf16[256,768]{1,0:T(8,128)(2,1)S(1)} collective-permute-done((bf16[256,768]{1,0:T(8,128)(2,1)S(1)}, bf16[256,768]{1,0:T(8,128)(2,1)S(1)}, u32[]{:S(2)}, u32[]{:S(2)}) %collective-permute-start.8) | collective-permute-done | bytes 393248 | tf_op jit(solution)/shard_map/ppermute | solution.py:307
  49.5 1.5 %collective-permute-done.9 = bf16[256,768]{1,0:T(8,128)(2,1)S(1)} collective-permute-done((bf16[256,768]{1,0:T(8,128)(2,1)S(1)}, bf16[256,768]{1,0:T(8,128)(2,1)S(1)}, u32[]{:S(2)}, u32[]{:S(2)}) %collective-permute-start.9) | collective-permute-done | bytes 393248 | tf_op jit(solution)/shard_map/ppermute | solution.py:307
  50.9 1.4 %collective-permute-done.10 = bf16[256,768]{1,0:T(8,128)(2,1)S(1)} collective-permute-done((bf16[256,768]{1,0:T(8,128)(2,1)S(1)}, bf16[256,768]{1,0:T(8,128)(2,1)S(1)}, u32[]{:S(2)}, u32[]{:S(2)}) %collective-permute-start.10) | collective-permute-done | bytes 393248 | tf_op jit(solution)/shard_map/ppermute | solution.py:307
  52.4 0.1 add_convert_fusion.4
  52.4 0.1 add_convert_fusion.3
  52.5 1.7 %collective-permute-start.17 = (bf16[128,768]{1,0:T(8,128)(2,1)S(1)}, bf16[128,768]{1,0:T(8,128)(2,1)S(1)}, u32[]{:S(2)}, u32[]{:S(2)}) collective-permute-start(bf16[128,768]{1,0:T(8,128)(2,1)S(1)} %add_convert_fusion.3), channel_id=1, source_target_pairs={{0,2},{1,3},{2,0},{3,1},{4,6},{5,7},{6,4},{7,5},{8,10},{9,11},{10,... | collective-permute-start | bytes 589832 | tf_op jit(solution)/shard_map/ppermute | solution.py:307
  54.3 0.7 collective-permute-start.15
  55.0 0.1 add_convert_fusion.5
  55.1 1.6 %collective-permute-start.13 = (bf16[128,768]{1,0:T(8,128)(2,1)S(1)}, bf16[128,768]{1,0:T(8,128)(2,1)S(1)}, u32[]{:S(2)}, u32[]{:S(2)}) collective-permute-start(bf16[128,768]{1,0:T(8,128)(2,1)S(1)} %add_convert_fusion.5), channel_id=1, source_target_pairs={{0,4},{1,5},{2,6},{3,7},{4,0},{5,1},{6,2},{7,3},{8,12},{9,13},{10,... | collective-permute-start | bytes 589832 | tf_op jit(solution)/shard_map/ppermute | solution.py:307
  56.7 3.6 %collective-permute-done.17 = bf16[128,768]{1,0:T(8,128)(2,1)S(1)} collective-permute-done((bf16[128,768]{1,0:T(8,128)(2,1)S(1)}, bf16[128,768]{1,0:T(8,128)(2,1)S(1)}, u32[]{:S(2)}, u32[]{:S(2)}) %collective-permute-start.17) | collective-permute-done | bytes 196640 | tf_op jit(solution)/shard_map/ppermute | solution.py:307
  60.3 1.0 %collective-permute-start.18 = (bf16[64,768]{1,0:T(8,128)(2,1)S(1)}, bf16[64,768]{1,0:T(8,128)(2,1)S(1)}, u32[]{:S(2)}, u32[]{:S(2)}) collective-permute-start(bf16[64,768]{1,0:T(8,128)(2,1)S(1)} %add_convert_fusion.6), channel_id=1, source_target_pairs={{0,4},{1,5},{2,6},{3,7},{4,0},{5,1},{6,2},{7,3},{8,12},{9,13},{10,... | collective-permute-start | bytes 294920 | tf_op jit(solution)/shard_map/ppermute | solution.py:307
  61.3 0.4 collective-permute-done.15
  61.8 0.5 collective-permute-start.16
  62.3 1.9 %collective-permute-start.14 = (bf16[64,768]{1,0:T(8,128)(2,1)S(1)}, bf16[64,768]{1,0:T(8,128)(2,1)S(1)}, u32[]{:S(2)}, u32[]{:S(2)}) collective-permute-start(bf16[64,768]{1,0:T(8,128)(2,1)S(1)} %add_convert_fusion.8), channel_id=1, source_target_pairs={{0,8},{8,0},{16,24},{24,16},{1,9},{9,1},{17,25},{25,17},{2,10},{10... | collective-permute-start | bytes 294920 | tf_op jit(solution)/shard_map/ppermute | solution.py:307
  64.2 0.9 %collective-permute-done.18 = bf16[64,768]{1,0:T(8,128)(2,1)S(1)} collective-permute-done((bf16[64,768]{1,0:T(8,128)(2,1)S(1)}, bf16[64,768]{1,0:T(8,128)(2,1)S(1)}, u32[]{:S(2)}, u32[]{:S(2)}) %collective-permute-start.18) | collective-permute-done | bytes 98336 | tf_op jit(solution)/shard_map/ppermute | solution.py:307
  65.1 1.3 %collective-permute-done.16 = bf16[64,768]{1,0:T(8,128)(2,1)S(1)} collective-permute-done((bf16[64,768]{1,0:T(8,128)(2,1)S(1)}, bf16[64,768]{1,0:T(8,128)(2,1)S(1)}, u32[]{:S(2)}, u32[]{:S(2)}) %collective-permute-start.16) | collective-permute-done | bytes 98336 | tf_op jit(solution)/shard_map/ppermute | solution.py:307
  66.5 0.5 collective-permute-done.14
  67.1 3.0 %collective-permute-start.19 = (bf16[32,2304]{1,0:T(8,128)(2,1)S(1)}, bf16[32,2304]{1,0:T(8,128)(2,1)S(1)}, u32[]{:S(2)}, u32[]{:S(2)}) collective-permute-start(bf16[32,2304]{1,0:T(8,128)(2,1)S(1)} %slice.262), channel_id=1, source_target_pairs={{0,16},{8,24},{16,0},{24,8},{1,17},{9,25},{17,1},{25,9},{2,18},{10... | collective-permute-start | bytes 442376 | tf_op jit(solution)/shard_map/ppermute | solution.py:307
  70.1 1.1 %shard_map.145 = f32[2,64,1024]{2,1,0:T(8,128)} custom-call(f32[2,64,1024]{2,1,0:T(8,128)S(1)} %get-tuple-element.79.own_ref, bf16[64,1024]{1,0:T(8,128)(2,1)S(1)} %collective-permute-done.12.from_below_ref, bf16[64,1024]{1,0:T(8,128)(2,1)S(1)} %collective-permute-done.11.from_above_ref, s32[2,32]{1,0:T(2,128)S(1)} %get-tuple-element.87.halo_ref), custom_call_target="tpu_custom_call" | custom-call | flops 1 | bytes 1 | tf_op jit(solution)/shard_map/pallas_call | solution.py:28
  71.2 4.7 %collective-permute-done.19.arrived_ref = bf16[32,2304]{1,0:T(8,128)(2,1)S(1)} collective-permute-done((bf16[32,2304]{1,0:T(8,128)(2,1)S(1)}, bf16[32,2304]{1,0:T(8,128)(2,1)S(1)}, u32[]{:S(2)}, u32[]{:S(2)}) %collective-permute-start.19) | collective-permute-done | bytes 147488 | tf_op jit(solution)/shard_map/ppermute | solution.py:307
  75.9 0.9 %shard_map.146 = (f32[32,2048]{1,0:T(8,128)}, f32[32,1024]{1,0:T(8,128)}, f32[32,100]{1,0:T(8,128)}) custom-call(f32[32,2304]{1,0:T(8,128)S(1)} %slice.220.own_ref, bf16[32,2304]{1,0:T(8,128)(2,1)S(1)} %collective-permute-done.19.arrived_ref, bf16[100,1024]{1,0:T(8,128)(2,1)S(1)} %bitcast.4), custom_call_target="tpu_custom_call" | custom-call | flops 1 | bytes 1 | tf_op jit(solution)/shard_map/pallas_call | solution.py:28
  (33 shorter events, 0.5 us)
Async XLA Ops:
  0.6 5.3 %copy-start.2 = (bf16[256,1024]{1,0:T(8,128)(2,1)S(1)}, bf16[256,1024]{1,0:T(8,128)(2,1)}, u32[]{:S(2)}) copy-start(bf16[256,1024]{1,0:T(8,128)(2,1)} %q_ref.5) | copy-start | bytes 1572868
  0.6 5.3 %copy-start.1 = (bf16[1024,1024]{1,0:T(8,128)(2,1)S(1)}, bf16[1024,1024]{1,0:T(8,128)(2,1)}, u32[]{:S(2)}) copy-start(bf16[1024,1024]{1,0:T(8,128)(2,1)} %wo_ref.3) | copy-start | bytes 6291460
  0.7 5.3 %copy-start.8 = (f32[100]{0:T(128)S(1)}, f32[100]{0:T(128)}, u32[]{:S(2)}) copy-start(f32[100]{0:T(128)} %param.19) | copy-start | bytes 1204
  0.7 5.3 %copy-start.7 = (f32[256]{0:T(256)S(1)}, f32[256]{0:T(256)}, u32[]{:S(2)}) copy-start(f32[256]{0:T(256)} %param.18) | copy-start | bytes 3076
  0.7 5.3 %copy-start.4 = (f32[100,256]{1,0:T(8,128)S(1)}, f32[100,256]{1,0:T(8,128)}, u32[]{:S(2)}) copy-start(f32[100,256]{1,0:T(8,128)} %init_ref.1) | copy-start | bytes 307204
  0.7 5.3 %copy-start.3 = (bf16[1024,100]{0,1:T(8,128)(2,1)S(1)}, bf16[1024,100]{0,1:T(8,128)(2,1)}, u32[]{:S(2)}) copy-start(bf16[1024,100]{0,1:T(8,128)(2,1)} %param.15) | copy-start | bytes 614404
  0.7 5.3 %copy-start = (bf16[1024,2048]{1,0:T(8,128)(2,1)S(1)}, bf16[1024,2048]{1,0:T(8,128)(2,1)}, u32[]{:S(2)}) copy-start(bf16[1024,2048]{1,0:T(8,128)(2,1)} %kvw_ref.5) | copy-start | bytes 12582916
  2.1 5.4 %collective-permute-start = (bf16[64,1024]{1,0:T(8,128)(2,1)S(1)}, bf16[64,1024]{1,0:T(8,128)(2,1)S(1)}, u32[]{:S(2)}, u32[]{:S(2)}) collective-permute-start(bf16[64,1024]{1,0:T(8,128)(2,1)S(1)} %get-tuple-element.49), channel_id=1, source_target_pairs={{0,1},{1,2},{2,3},{3,4},{4,5},{5,6},{6,7},{8,9},{9,10},{10,11},{11... | collective-permute-start | bytes 393224 | tf_op jit(solution)/shard_map/ppermute | solution.py:344
  4.6 5.3 %collective-permute-start.1 = (bf16[64,1024]{1,0:T(8,128)(2,1)S(1)}, bf16[64,1024]{1,0:T(8,128)(2,1)S(1)}, u32[]{:S(2)}, u32[]{:S(2)}) collective-permute-start(bf16[64,1024]{1,0:T(8,128)(2,1)S(1)} %get-tuple-element.50), channel_id=1, source_target_pairs={{1,0},{2,1},{3,2},{4,3},{5,4},{6,5},{7,6},{9,8},{10,9},{11,10},{12... | collective-permute-start | bytes 393224 | tf_op jit(solution)/shard_map/ppermute | solution.py:345
  6.0 4.0 %copy-start.6 = (s32[3,256]{1,0:T(4,128)S(1)}, s32[3,256]{1,0:T(4,128)}, u32[]{:S(2)}) copy-start(s32[3,256]{1,0:T(4,128)} %src_ref.1) | copy-start | bytes 9220
  9.9 17.8 %copy-start.5 = (f32[100,256]{1,0:T(8,128)S(1)}, f32[100,256]{1,0:T(8,128)}, u32[]{:S(2)}) copy-start(f32[100,256]{1,0:T(8,128)} %refs_5_.1) | copy-start | bytes 307204
  14.9 6.7 %collective-permute-start.4 = (bf16[208,256]{1,0:T(8,128)(2,1)S(1)}, bf16[208,256]{1,0:T(8,128)(2,1)S(1)}, u32[]{:S(2)}, u32[]{:S(2)}) collective-permute-start(bf16[208,256]{1,0:T(8,128)(2,1)S(1)} %get-tuple-element.54), channel_id=1, source_target_pairs={{0,24},{8,16},{16,8},{24,0},{1,25},{9,17},{17,9},{25,1},{2,26},{10... | collective-permute-start | bytes 319496 | tf_op jit(solution)/shard_map/ppermute | solution.py:378
  18.5 9.2 %collective-permute-start.3 = (bf16[208,256]{1,0:T(8,128)(2,1)S(1)}, bf16[208,256]{1,0:T(8,128)(2,1)S(1)}, u32[]{:S(2)}, u32[]{:S(2)}) collective-permute-start(bf16[208,256]{1,0:T(8,128)(2,1)S(1)} %get-tuple-element.54), channel_id=1, source_target_pairs={{0,16},{8,24},{16,0},{24,8},{1,17},{9,25},{17,1},{25,9},{2,18},{10... | collective-permute-start | bytes 319496 | tf_op jit(solution)/shard_map/ppermute | solution.py:378
  18.5 9.2 %collective-permute-start.2 = (bf16[208,256]{1,0:T(8,128)(2,1)S(1)}, bf16[208,256]{1,0:T(8,128)(2,1)S(1)}, u32[]{:S(2)}, u32[]{:S(2)}) collective-permute-start(bf16[208,256]{1,0:T(8,128)(2,1)S(1)} %get-tuple-element.54), channel_id=1, source_target_pairs={{0,8},{8,0},{16,24},{24,16},{1,9},{9,1},{17,25},{25,17},{2,10},{10... | collective-permute-start | bytes 319496 | tf_op jit(solution)/shard_map/ppermute | solution.py:378
  29.5 4.3 %collective-permute-start.5 = (bf16[512,768]{1,0:T(8,128)(2,1)S(1)}, bf16[512,768]{1,0:T(8,128)(2,1)S(1)}, u32[]{:S(2)}, u32[]{:S(2)}) collective-permute-start(bf16[512,768]{1,0:T(8,128)(2,1)S(1)} %get-tuple-element.61), channel_id=1, source_target_pairs={{0,1},{1,0},{2,3},{3,2},{4,5},{5,4},{6,7},{7,6},{8,9},{9,8},{10,11... | collective-permute-start | bytes 2359304 | tf_op jit(solution)/shard_map/ppermute | solution.py:307
  33.2 2.4 %collective-permute-start.6 = (bf16[512,768]{1,0:T(8,128)(2,1)S(1)}, bf16[512,768]{1,0:T(8,128)(2,1)S(1)}, u32[]{:S(2)}, u32[]{:S(2)}) collective-permute-start(bf16[512,768]{1,0:T(8,128)(2,1)S(1)} %get-tuple-element.69), channel_id=1, source_target_pairs={{0,1},{1,0},{2,3},{3,2},{4,5},{5,4},{6,7},{7,6},{8,9},{9,8},{10,11... | collective-permute-start | bytes 2359304 | tf_op jit(solution)/shard_map/ppermute | solution.py:307
  33.3 3.4 %collective-permute-start.7 = (bf16[512,768]{1,0:T(8,128)(2,1)S(1)}, bf16[512,768]{1,0:T(8,128)(2,1)S(1)}, u32[]{:S(2)}, u32[]{:S(2)}) collective-permute-start(bf16[512,768]{1,0:T(8,128)(2,1)S(1)} %get-tuple-element.71), channel_id=1, source_target_pairs={{0,1},{1,0},{2,3},{3,2},{4,5},{5,4},{6,7},{7,6},{8,9},{9,8},{10,11... | collective-permute-start | bytes 2359304 | tf_op jit(solution)/shard_map/ppermute | solution.py:307
  36.9 12.6 %collective-permute-start.8 = (bf16[256,768]{1,0:T(8,128)(2,1)S(1)}, bf16[256,768]{1,0:T(8,128)(2,1)S(1)}, u32[]{:S(2)}, u32[]{:S(2)}) collective-permute-start(bf16[256,768]{1,0:T(8,128)(2,1)S(1)} %add_convert_fusion.2), channel_id=1, source_target_pairs={{0,2},{1,3},{2,0},{3,1},{4,6},{5,7},{6,4},{7,5},{8,10},{9,11},{10,... | collective-permute-start | bytes 1179656 | tf_op jit(solution)/shard_map/ppermute | solution.py:307
  40.1 10.9 %collective-permute-start.9 = (bf16[256,768]{1,0:T(8,128)(2,1)S(1)}, bf16[256,768]{1,0:T(8,128)(2,1)S(1)}, u32[]{:S(2)}, u32[]{:S(2)}) collective-permute-start(bf16[256,768]{1,0:T(8,128)(2,1)S(1)} %get-tuple-element.81), channel_id=1, source_target_pairs={{0,4},{1,5},{2,6},{3,7},{4,0},{5,1},{6,2},{7,3},{8,12},{9,13},{10,... | collective-permute-start | bytes 1179656 | tf_op jit(solution)/shard_map/ppermute | solution.py:307
  41.3 11.1 %collective-permute-start.10 = (bf16[256,768]{1,0:T(8,128)(2,1)S(1)}, bf16[256,768]{1,0:T(8,128)(2,1)S(1)}, u32[]{:S(2)}, u32[]{:S(2)}) collective-permute-start(bf16[256,768]{1,0:T(8,128)(2,1)S(1)} %get-tuple-element.82), channel_id=1, source_target_pairs={{0,8},{8,0},{16,24},{24,16},{1,9},{9,1},{17,25},{25,17},{2,10},{10... | collective-permute-start | bytes 1179656 | tf_op jit(solution)/shard_map/ppermute | solution.py:307
  43.0 4.3 %collective-permute-start.11 = (bf16[64,1024]{1,0:T(8,128)(2,1)S(1)}, bf16[64,1024]{1,0:T(8,128)(2,1)S(1)}, u32[]{:S(2)}, u32[]{:S(2)}) collective-permute-start(bf16[64,1024]{1,0:T(8,128)(2,1)S(1)} %get-tuple-element.83), channel_id=1, source_target_pairs={{1,0},{2,1},{3,2},{4,3},{5,4},{6,5},{7,6},{9,8},{10,9},{11,10},{12... | collective-permute-start | bytes 393224 | tf_op jit(solution)/shard_map/ppermute | solution.py:419
  44.3 4.0 %collective-permute-start.12 = (bf16[64,1024]{1,0:T(8,128)(2,1)S(1)}, bf16[64,1024]{1,0:T(8,128)(2,1)S(1)}, u32[]{:S(2)}, u32[]{:S(2)}) collective-permute-start(bf16[64,1024]{1,0:T(8,128)(2,1)S(1)} %get-tuple-element.84), channel_id=1, source_target_pairs={{0,1},{1,2},{2,3},{3,4},{4,5},{5,6},{6,7},{8,9},{9,10},{10,11},{11... | collective-permute-start | bytes 393224 | tf_op jit(solution)/shard_map/ppermute | solution.py:420
  52.5 7.7 %collective-permute-start.17 = (bf16[128,768]{1,0:T(8,128)(2,1)S(1)}, bf16[128,768]{1,0:T(8,128)(2,1)S(1)}, u32[]{:S(2)}, u32[]{:S(2)}) collective-permute-start(bf16[128,768]{1,0:T(8,128)(2,1)S(1)} %add_convert_fusion.3), channel_id=1, source_target_pairs={{0,2},{1,3},{2,0},{3,1},{4,6},{5,7},{6,4},{7,5},{8,10},{9,11},{10,... | collective-permute-start | bytes 589832 | tf_op jit(solution)/shard_map/ppermute | solution.py:307
  54.3 7.4 %collective-permute-start.15 = (bf16[128,768]{1,0:T(8,128)(2,1)S(1)}, bf16[128,768]{1,0:T(8,128)(2,1)S(1)}, u32[]{:S(2)}, u32[]{:S(2)}) collective-permute-start(bf16[128,768]{1,0:T(8,128)(2,1)S(1)} %add_convert_fusion.4), channel_id=1, source_target_pairs={{0,8},{8,0},{16,24},{24,16},{1,9},{9,1},{17,25},{25,17},{2,10},{10... | collective-permute-start | bytes 589832 | tf_op jit(solution)/shard_map/ppermute | solution.py:307
  55.1 7.2 %collective-permute-start.13 = (bf16[128,768]{1,0:T(8,128)(2,1)S(1)}, bf16[128,768]{1,0:T(8,128)(2,1)S(1)}, u32[]{:S(2)}, u32[]{:S(2)}) collective-permute-start(bf16[128,768]{1,0:T(8,128)(2,1)S(1)} %add_convert_fusion.5), channel_id=1, source_target_pairs={{0,4},{1,5},{2,6},{3,7},{4,0},{5,1},{6,2},{7,3},{8,12},{9,13},{10,... | collective-permute-start | bytes 589832 | tf_op jit(solution)/shard_map/ppermute | solution.py:307
  60.3 4.7 %collective-permute-start.18 = (bf16[64,768]{1,0:T(8,128)(2,1)S(1)}, bf16[64,768]{1,0:T(8,128)(2,1)S(1)}, u32[]{:S(2)}, u32[]{:S(2)}) collective-permute-start(bf16[64,768]{1,0:T(8,128)(2,1)S(1)} %add_convert_fusion.6), channel_id=1, source_target_pairs={{0,4},{1,5},{2,6},{3,7},{4,0},{5,1},{6,2},{7,3},{8,12},{9,13},{10,... | collective-permute-start | bytes 294920 | tf_op jit(solution)/shard_map/ppermute | solution.py:307
  61.8 4.7 %collective-permute-start.16 = (bf16[64,768]{1,0:T(8,128)(2,1)S(1)}, bf16[64,768]{1,0:T(8,128)(2,1)S(1)}, u32[]{:S(2)}, u32[]{:S(2)}) collective-permute-start(bf16[64,768]{1,0:T(8,128)(2,1)S(1)} %add_convert_fusion.7), channel_id=1, source_target_pairs={{0,2},{1,3},{2,0},{3,1},{4,6},{5,7},{6,4},{7,5},{8,10},{9,11},{10,... | collective-permute-start | bytes 294920 | tf_op jit(solution)/shard_map/ppermute | solution.py:307
  62.3 4.7 %collective-permute-start.14 = (bf16[64,768]{1,0:T(8,128)(2,1)S(1)}, bf16[64,768]{1,0:T(8,128)(2,1)S(1)}, u32[]{:S(2)}, u32[]{:S(2)}) collective-permute-start(bf16[64,768]{1,0:T(8,128)(2,1)S(1)} %add_convert_fusion.8), channel_id=1, source_target_pairs={{0,8},{8,0},{16,24},{24,16},{1,9},{9,1},{17,25},{25,17},{2,10},{10... | collective-permute-start | bytes 294920 | tf_op jit(solution)/shard_map/ppermute | solution.py:307
  67.1 8.8 %collective-permute-start.19 = (bf16[32,2304]{1,0:T(8,128)(2,1)S(1)}, bf16[32,2304]{1,0:T(8,128)(2,1)S(1)}, u32[]{:S(2)}, u32[]{:S(2)}) collective-permute-start(bf16[32,2304]{1,0:T(8,128)(2,1)S(1)} %slice.262), channel_id=1, source_target_pairs={{0,16},{8,24},{16,0},{24,8},{1,17},{9,25},{17,1},{25,9},{2,18},{10... | collective-permute-start | bytes 442376 | tf_op jit(solution)/shard_map/ppermute | solution.py:307

commit v5 on v4

--- a/solution.py
+++ b/solution.py
@@ -54,13 +54,19 @@
     return copies
 
 
-def pick_body(hidden_hbm, halo_hbm, hidden_ref, halo_ref, down_ref, up_ref, sems):
+def halo_lists(halo_ref):
+    even = lax.axis_index("band") % 2 == 0
+    down, up = halo_ref[0:1, :], halo_ref[1:2, :]
+    return jnp.where(even, up, down), jnp.where(even, down, up)
+
+
+def pick_body(hidden_hbm, halo_hbm, hidden_ref, halo_ref, mate_ref, other_ref, sems):
     for copy in start_copies([(hidden_hbm, hidden_ref), (halo_hbm, halo_ref)], sems):
         copy.wait()
     members, nodes, _ = hidden_ref.shape
     rim = halo_ref.shape[1]
-    for row, out_ref in ((0, down_ref), (1, up_ref)):
-        hot = one_hot_rows(halo_ref[row : row + 1, :], nodes)
+    for rows, out_ref in zip(halo_lists(halo_ref), (mate_ref, other_ref)):
+        hot = one_hot_rows(rows, nodes)
         for m in range(members):
             out_ref[m * rim : (m + 1) * rim, :] = mm(hot, hidden_ref[m], TN).astype(BF)
 
@@ -92,23 +98,27 @@
 
 def forward_body(
     send_rows,
-    below_ref, above_ref, own_ref, kvw_ref, q_ref, src_ref, p_ref,
+    mate_ref, other_ref, own_ref, kvw_ref, q_ref, src_ref, p_ref,
     kv_ref, gate_ref, slope_ref, merged_ref, part_ref, send_ref,
 ):
     members, ext, width2 = kv_ref.shape
     width = width2 // 2
     points = q_ref.shape[0]
     nodes = own_ref.shape[0] // members
-    rim = below_ref.shape[0] // members
-    halo = mm(jnp.concatenate([below_ref[...], above_ref[...]], axis=0), kvw_ref[...]).astype(BF)
+    rim = mate_ref.shape[0] // members
+    halo = mm(jnp.concatenate([mate_ref[...], other_ref[...]], axis=0), kvw_ref[...]).astype(BF)
     for m in range(members):
         kv_ref[m, 0:nodes, :] = own_ref[m * nodes : (m + 1) * nodes, :]
         kv_ref[m, nodes : nodes + rim, :] = halo[m * rim : (m + 1) * rim]
         kv_ref[m, nodes + rim : ext, :] = halo[(members + m) * rim : (members + m + 1) * rim]
     rows = lax.broadcasted_iota(jnp.int32, (ext, points), 0)
-    mask = rows == src_ref[0:1, :]
-    for e in range(1, src_ref.shape[0]):
-        mask = mask | (rows == src_ref[e : e + 1, :])
+    src = src_ref[...]
+    even = lax.axis_index("band") % 2 == 0
+    shift = jnp.where(src >= nodes + rim, -rim, jnp.where(src >= nodes, rim, 0))
+    src = src + jnp.where(even, shift, 0)
+    mask = rows == src[0:1, :]
+    for e in range(1, src.shape[0]):
+        mask = mask | (rows == src[e : e + 1, :])
     mask = mask.astype(F32)
     mask = jnp.concatenate([mask, mask], axis=0)
     scale = HEAD_DIM ** (-0.5)
@@ -173,14 +183,14 @@
         ref[:, at : at + rows.shape[1]] = ordered.astype(BF)
 
 
-def transpose_body(n_member, n_band, hidden_ref, below_ref, above_ref, out_ref, turned):
+def transpose_body(n_member, n_band, hidden_ref, mate_ref, other_ref, out_ref, turned):
     members, nodes, _ = hidden_ref.shape
-    rim = below_ref.shape[0] // members
+    rim = mate_ref.shape[0] // members
     parts = []
     for m in range(members):
         parts.append(hidden_ref[m])
-        parts.append(below_ref[m * rim : (m + 1) * rim, :])
-        parts.append(above_ref[m * rim : (m + 1) * rim, :])
+        parts.append(mate_ref[m * rim : (m + 1) * rim, :])
+        parts.append(other_ref[m * rim : (m + 1) * rim, :])
     turned[...] = jnp.concatenate(parts, axis=0).astype(F32).T
     out_ref[...] = reorder(turned, n_member, n_band).astype(BF)
 
@@ -265,25 +275,24 @@
             first, at = first + take, at + take
 
 
-def extended_grad_body(members, nodes, rim, ngk_ref, ngv_ref, kvw_ref, own_ref, down_ref, up_ref):
+def extended_grad_body(members, nodes, rim, ngk_ref, ngv_ref, kvw_ref, own_ref, mate_ref, other_ref):
     ext = nodes + 2 * rim
     width = kvw_ref.shape[0]
     rows = mm(ngk_ref[...], kvw_ref[:, 0:width], NT) + mm(ngv_ref[...], kvw_ref[:, width:], NT)
     for m in range(members):
         at = m * ext
         own_ref[m] = rows[at : at + nodes]
-        down_ref[m * rim : (m + 1) * rim, :] = rows[at + nodes : at + nodes + rim].astype(BF)
-        up_ref[m * rim : (m + 1) * rim, :] = rows[at + nodes + rim : at + ext].astype(BF)
-
-
-def hidden_body(own_ref, from_below_ref, from_above_ref, halo_ref, out_ref):
+        mate_ref[m * rim : (m + 1) * rim, :] = rows[at + nodes : at + nodes + rim].astype(BF)
+        other_ref[m * rim : (m + 1) * rim, :] = rows[at + nodes + rim : at + ext].astype(BF)
+
+
+def hidden_body(own_ref, from_mate_ref, from_other_ref, halo_ref, out_ref):
     members, nodes, _ = own_ref.shape
     rim = halo_ref.shape[1]
-    low = one_hot_rows(halo_ref[0:1, :], nodes)
-    high = one_hot_rows(halo_ref[1:2, :], nodes)
+    mate, other = [one_hot_rows(rows, nodes) for rows in halo_lists(halo_ref)]
     for m in range(members):
         rows = slice(m * rim, (m + 1) * rim)
-        out_ref[m] = own_ref[m] + mm(low, from_below_ref[rows, :]) + mm(high, from_above_ref[rows, :])
+        out_ref[m] = own_ref[m] + mm(mate, from_mate_ref[rows, :]) + mm(other, from_other_ref[rows, :])
 
 
 def finish_body(devices, own_ref, arrived_ref, hp_ref, kv_ref, out_ref, head_ref):
@@ -330,10 +339,10 @@
     rw = width // devices
     chips = n_band // 2
     send_rows = -(-channels // 8) * 8
-    to_above = [(i, i + 1) for i in range(n_band - 1)]
-    to_below = [(i + 1, i) for i in range(n_band - 1)]
-
-    own_hidden, halo, down, up = call(
+    mates = [(i, i ^ 1) for i in range(n_band)]
+    others = [(i, i + 1 if i % 2 else i - 1) for i in range(1, n_band - 1)]
+
+    own_hidden, halo, for_mate, for_other = call(
         pick_body,
         [sds(hidden.shape, BF), sds(halo_rows.shape, jnp.int32)] + [sds((members * rim, width), BF)] * 2,
         (hidden, halo_rows),
@@ -341,8 +350,8 @@
         hbm=(0, 1),
         flops=10**10,
     )
-    below = lax.ppermute(up, "band", to_above)
-    above = lax.ppermute(down, "band", to_below)
+    mate = lax.ppermute(for_mate, "band", mates)
+    other = lax.ppermute(for_other, "band", others)
 
     hp = head_projection.T
     own_kv, pt, p, base, weight = call(
@@ -371,7 +380,7 @@
             sds((members, LANES, points), F32),
             sds((-(-members * send_rows // 16) * 16, points), BF),
         ],
-        (below, above, own_kv, kv_weight, queries, sources, p),
+        (mate, other, own_kv, kv_weight, queries, sources, p),
     )
 
     received = [
@@ -381,7 +390,7 @@
     ext_t = call(
         functools.partial(transpose_body, n_member, n_band),
         sds((width, members * ext), BF),
-        (own_hidden, below, above),
+        (own_hidden, mate, other),
         [pltpu.VMEM((width, members * ext), F32)],
     )
 
@@ -411,21 +420,21 @@
             outgoing[0], groups[1:] = lax.optimization_barrier((outgoing[0], groups[1:]))
             outgoing[1:] = [add_up(*upper(terms)).astype(BF) for terms in groups[1:]]
             outgoing, ng_key = lax.optimization_barrier((outgoing, ng_key))
-            own_grad, back_down, back_up = call(
+            own_grad, back_mate, back_other = call(
                 functools.partial(extended_grad_body, members, nodes, rim),
                 [sds((members, nodes, width), F32)] + [sds((members * rim, width), BF)] * 2,
                 (ng_key, ng_value, kv_weight),
             )
-            from_above = lax.ppermute(back_down, "band", to_below)
-            from_below = lax.ppermute(back_up, "band", to_above)
         arrived = [swap(out, *turn[step], count[turn[step][0]]) for out, turn in zip(outgoing, turns)]
         if step == 0:
-            arrived, from_above, from_below = lax.optimization_barrier((arrived, from_above, from_below))
+            arrived, back_mate, back_other = lax.optimization_barrier((arrived, back_mate, back_other))
+            from_mate = lax.ppermute(back_mate, "band", mates)
+            from_other = lax.ppermute(back_other, "band", others)
         groups = [lower(terms) + [new] for terms, new in zip(groups, arrived)]
     hidden_grad = call(
         hidden_body,
         sds((members, nodes, width), F32),
-        (own_grad, from_below, from_above, halo),
+        (own_grad, from_mate, from_other, halo),
     )
     terms = [jnp.concatenate([add_up(*group) for group in groups], axis=1)]
     for axis, bit in rest:

time: 77 us -> 76.3 us (level)
  the two profiles are of different devices: /device:TPU:0 before, /device:TPU:1 now
where the time goes in v5:
time: 76.3 us; the launch traced here: 76.1 us
  waiting for transfers between devices  30.4 us (40%)
  starting transfers between devices  28 us (37%)
  Pallas kernels  15.8 us (21%)
  between operations  0.93 us (1%)
  other arithmetic  0.91 us (1%)
    ppermute x13, waiting for transfers between devices, swap(): return lax.ppermute(rows, axis, [(i, i ^ 1 << bit) for i in range(count)])  18.8 us
    pallas_call x9, Pallas kernels, call(): pl.pallas_call(body, out_shape=out_shape, in_specs=[pl.BlockSpec(memory_s...  15.8 us
    ppermute x13, starting transfers between devices, swap(): return lax.ppermute(rows, axis, [(i, i ^ 1 << bit) for i in range(count)])  10.4 us
    ppermute x1, starting transfers between devices, shards(): from_mate = lax.ppermute(back_mate, 'band', mates)  6.14 us
    ppermute x3, waiting for transfers between devices, shards(): lax.ppermute(sent, 'member', [(i, i ^ s) for i in range(n_member)])  5.19 us
    ppermute x1, waiting for transfers between devices, shards(): from_other = lax.ppermute(back_other, 'band', others)  4.89 us
    ppermute x3, starting transfers between devices, shards(): lax.ppermute(sent, 'member', [(i, i ^ s) for i in range(n_member)])  4.78 us
    ppermute x1, starting transfers between devices, shards(): other = lax.ppermute(for_other, 'band', others)  4.59 us
  transfers between devices with their start and end apart: 20, of which 13 were waited for; matrix products, arithmetic and copies ran while one was open for 1% of the time, Pallas kernels for 9%

profile of v5, /device:TPU:1, one launch (start us, length us, event | category | flops | bytes accessed | tf_op | source)
XLA Modules:
  0.0 76.1 jit_solution(3445882837549399603)
XLA Ops:
  0.7 1.4 %shard_map.138 = (bf16[2,64,1024]{2,1,0:T(8,128)(2,1)S(1)}, s32[2,32]{1,0:T(2,128)S(1)}, bf16[64,1024]{1,0:T(8,128)(2,1)S(1)}, bf16[64,1024]{1,0:T(8,128)(2,1)S(1)}) custom-call(bf16[2,64,1024]{2,1,0:T(8,128)(2,1)} %hidden_hbm.1, s32[2,32]{1,0:T(2,128)} %halo_hbm.1), custom_call_target="tpu_custom_call" | custom-call | flops 10000000000 | bytes 1 | tf_op jit(solution)/shard_map/pallas_call | solution.py:28
  2.1 0.1 collective-permute-start
  2.2 4.6 %collective-permute-start.1 = (bf16[64,1024]{1,0:T(8,128)(2,1)S(1)}, bf16[64,1024]{1,0:T(8,128)(2,1)S(1)}, u32[]{:S(2)}, u32[]{:S(2)}) collective-permute-start(bf16[64,1024]{1,0:T(8,128)(2,1)S(1)} %get-tuple-element.50), channel_id=1, source_target_pairs={{1,2},{2,1},{3,4},{4,3},{5,6},{6,5},{9,10},{10,9},{11,12},{12,11},... | collective-permute-start | bytes 393224 | tf_op jit(solution)/shard_map/ppermute | solution.py:354
  6.9 1.5 %shard_map.139 = (bf16[128,2048]{1,0:T(8,128)(2,1)S(1)}, bf16[1024,128]{1,0:T(8,128)(2,1)S(1)}, bf16[128,1024]{1,0:T(8,128)(2,1)S(1)}, f32[128,256]{1,0:T(8,128)S(1)}, f32[100,256]{1,0:T(8,128)S(1)}) custom-call(bf16[2,64,1024]{2,1,0:T(8,128)(2,1)S(1)} %get-tuple-element.51.hidden_ref, bf16[1024,1024]{1,0:T(8,128)(2,1)S(1)} %copy-done.1, ...), custom_call_target="tpu_custom_call" | custom-call | flops 1 | bytes 1 | tf_op jit(solution)/shard_map/pallas_call | solution.py:28
  8.5 1.5 %collective-permute-done.1.other_ref = bf16[64,1024]{1,0:T(8,128)(2,1)S(1)} collective-permute-done((bf16[64,1024]{1,0:T(8,128)(2,1)S(1)}, bf16[64,1024]{1,0:T(8,128)(2,1)S(1)}, u32[]{:S(2)}, u32[]{:S(2)}) %collective-permute-start.1) | collective-permute-done | bytes 131104 | tf_op jit(solution)/shard_map/ppermute | solution.py:354
  10.0 4.9 %shard_map.140 = (bf16[2,128,2048]{2,1,0:T(8,128)(2,1)S(1)}, bf16[8,2,256,256]{3,2,1,0:T(8,128)(2,1)S(1)}, bf16[8,2,256,256]{3,2,1,0:T(8,128)(2,1)S(1)}, bf16[2,...) custom-call(bf16[64,1024]{1,0:T(8,128)(2,1)S(1)} %collective-permute-done.mate_ref, ...), custom_call_target="tpu_custom_call" | custom-call | flops 1 | bytes 1 | tf_op jit(solution)/shard_map/pallas_call | solution.py:28
  14.9 4.4 %collective-permute-start.4 = (bf16[208,256]{1,0:T(8,128)(2,1)S(1)}, bf16[208,256]{1,0:T(8,128)(2,1)S(1)}, u32[]{:S(2)}, u32[]{:S(2)}) collective-permute-start(bf16[208,256]{1,0:T(8,128)(2,1)S(1)} %get-tuple-element.54), channel_id=1, source_target_pairs={{0,24},{8,16},{16,8},{24,0},{1,25},{9,17},{17,9},{25,1},{2,26},{10... | collective-permute-start | bytes 319496 | tf_op jit(solution)/shard_map/ppermute | solution.py:387
  19.3 0.4 collective-permute-start.2
  19.7 0.3 shard_map.141.refs_9_.ext_ref
  20.0 2.2 %collective-permute-done.4.refs_2_ = bf16[208,256]{1,0:T(8,128)(2,1)S(1)} collective-permute-done((bf16[208,256]{1,0:T(8,128)(2,1)S(1)}, bf16[208,256]{1,0:T(8,128)(2,1)S(1)}, u32[]{:S(2)}, u32[]{:S(2)}) %collective-permute-start.4) | collective-permute-done | bytes 106528 | tf_op jit(solution)/shard_map/ppermute | solution.py:387
  22.2 3.0 %collective-permute-done.3.refs_1_ = bf16[208,256]{1,0:T(8,128)(2,1)S(1)} collective-permute-done((bf16[208,256]{1,0:T(8,128)(2,1)S(1)}, bf16[208,256]{1,0:T(8,128)(2,1)S(1)}, u32[]{:S(2)}, u32[]{:S(2)}) %collective-permute-start.3) | collective-permute-done | bytes 106528 | tf_op jit(solution)/shard_map/ppermute | solution.py:387
  25.1 1.8 %shard_map.142 = (bf16[2,128,256]{2,1,0:T(8,128)(2,1)S(1)}, bf16[2,1024,256]{2,1,0:T(8,128)(2,1)S(1)}, bf16[256,1024]{1,0:T(8,128)(2,1)S(1)}, bf16[512,768]{1,0:T(8,128)(2,1)S(1)}, bf16[512,768]{1,0:T(8,128)(2,1)S(1)}) custom-call(bf16[208,256]{1,0:T(8,128)(2,1)S(1)} %collective-permute-done.2.refs_0_, bf16[208,256]{1,0:T(8,128)(2,1)S(1)} %collective-permute-done.3.refs_1_, ...), custom_call_target="tpu_custom_call" | custom-call | flops 1 | bytes 1 | tf_op jit(solution)/shard_map/pallas_call | solution.py:28
  26.9 0.1 collective-permute-start.5
  27.0 2.7 %shard_map.143 = (bf16[256,1024]{1,0:T(8,128)(2,1)S(1)}, bf16[512,768]{1,0:T(8,128)(2,1)S(1)}, bf16[512,768]{1,0:T(8,128)(2,1)S(1)}, bf16[512,768]{1,0:T(8,128)(2,1)S(1)}, bf16[512,768]{1,0:T(8,128)(2,1)S(1)}) custom-call(bf16[2,128,256]{2,1,0:T(8,128)(2,1)S(1)} %get-tuple-element.62.grad_ref, bf16[2,1024,256]{2,1,0:T(8,128)(2,1)S(1)} %get-tuple-element.63.dm_ref, ...), custom_call_target="tpu_custom_call" | custom-call | flops 1 | bytes 1 | tf_op jit(solution)/shard_map/pallas_call | solution.py:28
  29.7 0.6 collective-permute-start.6
  30.3 0.1 collective-permute-start.7
  30.4 0.1 add_convert_fusion.2
  30.5 1.7 %collective-permute-done.6 = bf16[512,768]{1,0:T(8,128)(2,1)S(1)} collective-permute-done((bf16[512,768]{1,0:T(8,128)(2,1)S(1)}, bf16[512,768]{1,0:T(8,128)(2,1)S(1)}, u32[]{:S(2)}, u32[]{:S(2)}) %collective-permute-start.6) | collective-permute-done | bytes 786464 | tf_op jit(solution)/shard_map/ppermute | solution.py:316
  32.2 1.1 %collective-permute-done.7 = bf16[512,768]{1,0:T(8,128)(2,1)S(1)} collective-permute-done((bf16[512,768]{1,0:T(8,128)(2,1)S(1)}, bf16[512,768]{1,0:T(8,128)(2,1)S(1)}, u32[]{:S(2)}, u32[]{:S(2)}) %collective-permute-start.7) | collective-permute-done | bytes 786464 | tf_op jit(solution)/shard_map/ppermute | solution.py:316
  33.3 0.2 add_convert_fusion
  33.5 4.2 %collective-permute-start.8 = (bf16[256,768]{1,0:T(8,128)(2,1)S(1)}, bf16[256,768]{1,0:T(8,128)(2,1)S(1)}, u32[]{:S(2)}, u32[]{:S(2)}) collective-permute-start(bf16[256,768]{1,0:T(8,128)(2,1)S(1)} %add_convert_fusion.2), channel_id=1, source_target_pairs={{0,2},{1,3},{2,0},{3,1},{4,6},{5,7},{6,4},{7,5},{8,10},{9,11},{10,... | collective-permute-start | bytes 1179656 | tf_op jit(solution)/shard_map/ppermute | solution.py:316
  37.8 0.4 collective-permute-start.9
  38.1 0.1 collective-permute-start.10
  38.2 1.3 %shard_map.144 = (f32[2,64,1024]{2,1,0:T(8,128)S(1)}, bf16[64,1024]{1,0:T(8,128)(2,1)S(1)}, bf16[64,1024]{1,0:T(8,128)(2,1)S(1)}) custom-call(bf16[256,1024]{1,0:T(8,128)(2,1)S(1)} %get-tuple-element.78.ngk_ref, bf16[256,1024]{1,0:T(8,128)(2,1)S(1)} %get-tuple-element.67.ngv_ref, bf16[1024,2048]{1,0:T(8,128)(2,1)S(1)} %copy-done), custom_call_target="tpu_custom_call" | custom-call | flops 1 | bytes 1 | tf_op jit(solution)/shard_map/pallas_call | solution.py:28
  39.5 7.5 %collective-permute-done.8 = bf16[256,768]{1,0:T(8,128)(2,1)S(1)} collective-permute-done((bf16[256,768]{1,0:T(8,128)(2,1)S(1)}, bf16[256,768]{1,0:T(8,128)(2,1)S(1)}, u32[]{:S(2)}, u32[]{:S(2)}) %collective-permute-start.8) | collective-permute-done | bytes 393248 | tf_op jit(solution)/shard_map/ppermute | solution.py:316
  47.0 0.8 %collective-permute-done.9 = bf16[256,768]{1,0:T(8,128)(2,1)S(1)} collective-permute-done((bf16[256,768]{1,0:T(8,128)(2,1)S(1)}, bf16[256,768]{1,0:T(8,128)(2,1)S(1)}, u32[]{:S(2)}, u32[]{:S(2)}) %collective-permute-start.9) | collective-permute-done | bytes 393248 | tf_op jit(solution)/shard_map/ppermute | solution.py:316
  47.8 0.6 collective-permute-done.10
  48.4 0.1 add_convert_fusion.4
  48.5 0.1 add_convert_fusion.3
  48.5 1.1 %collective-permute-start.17 = (bf16[128,768]{1,0:T(8,128)(2,1)S(1)}, bf16[128,768]{1,0:T(8,128)(2,1)S(1)}, u32[]{:S(2)}, u32[]{:S(2)}) collective-permute-start(bf16[128,768]{1,0:T(8,128)(2,1)S(1)} %add_convert_fusion.3), channel_id=1, source_target_pairs={{0,2},{1,3},{2,0},{3,1},{4,6},{5,7},{6,4},{7,5},{8,10},{9,11},{10,... | collective-permute-start | bytes 589832 | tf_op jit(solution)/shard_map/ppermute | solution.py:316
  49.7 0.1 add_convert_fusion.5
  49.8 0.4 collective-permute-start.13
  50.2 3.5 %collective-permute-done.17 = bf16[128,768]{1,0:T(8,128)(2,1)S(1)} collective-permute-done((bf16[128,768]{1,0:T(8,128)(2,1)S(1)}, bf16[128,768]{1,0:T(8,128)(2,1)S(1)}, u32[]{:S(2)}, u32[]{:S(2)}) %collective-permute-start.17) | collective-permute-done | bytes 196640 | tf_op jit(solution)/shard_map/ppermute | solution.py:316
  53.8 0.1 collective-permute-start.18
  53.9 0.6 collective-permute-done.15
  54.5 0.8 %collective-permute-start.16 = (bf16[64,768]{1,0:T(8,128)(2,1)S(1)}, bf16[64,768]{1,0:T(8,128)(2,1)S(1)}, u32[]{:S(2)}, u32[]{:S(2)}) collective-permute-start(bf16[64,768]{1,0:T(8,128)(2,1)S(1)} %add_convert_fusion.7), channel_id=1, source_target_pairs={{0,2},{1,3},{2,0},{3,1},{4,6},{5,7},{6,4},{7,5},{8,10},{9,11},{10,... | collective-permute-start | bytes 294920 | tf_op jit(solution)/shard_map/ppermute | solution.py:316
  55.4 0.8 %collective-permute-start.14 = (bf16[64,768]{1,0:T(8,128)(2,1)S(1)}, bf16[64,768]{1,0:T(8,128)(2,1)S(1)}, u32[]{:S(2)}, u32[]{:S(2)}) collective-permute-start(bf16[64,768]{1,0:T(8,128)(2,1)S(1)} %add_convert_fusion.8), channel_id=1, source_target_pairs={{0,8},{8,0},{16,24},{24,16},{1,9},{9,1},{17,25},{25,17},{2,10},{10... | collective-permute-start | bytes 294920 | tf_op jit(solution)/shard_map/ppermute | solution.py:316
  56.2 1.8 %collective-permute-done.18 = bf16[64,768]{1,0:T(8,128)(2,1)S(1)} collective-permute-done((bf16[64,768]{1,0:T(8,128)(2,1)S(1)}, bf16[64,768]{1,0:T(8,128)(2,1)S(1)}, u32[]{:S(2)}, u32[]{:S(2)}) %collective-permute-start.18) | collective-permute-done | bytes 98336 | tf_op jit(solution)/shard_map/ppermute | solution.py:316
  58.1 0.1 convert_add_fusion
  58.1 0.1 convert_add_fusion.1
  58.2 1.0 %collective-permute-done.14 = bf16[64,768]{1,0:T(8,128)(2,1)S(1)} collective-permute-done((bf16[64,768]{1,0:T(8,128)(2,1)S(1)}, bf16[64,768]{1,0:T(8,128)(2,1)S(1)}, u32[]{:S(2)}, u32[]{:S(2)}) %collective-permute-start.14) | collective-permute-done | bytes 98336 | tf_op jit(solution)/shard_map/ppermute | solution.py:316
  59.3 0.1 convert_add_fusion.2
  59.4 1.8 %collective-permute-start.19 = (bf16[32,2304]{1,0:T(8,128)(2,1)S(1)}, bf16[32,2304]{1,0:T(8,128)(2,1)S(1)}, u32[]{:S(2)}, u32[]{:S(2)}) collective-permute-start(bf16[32,2304]{1,0:T(8,128)(2,1)S(1)} %slice.262), channel_id=1, source_target_pairs={{0,16},{8,24},{16,0},{24,8},{1,17},{9,25},{17,1},{25,9},{2,18},{10... | collective-permute-start | bytes 442376 | tf_op jit(solution)/shard_map/ppermute | solution.py:316
  61.2 6.1 %collective-permute-start.11 = (bf16[64,1024]{1,0:T(8,128)(2,1)S(1)}, bf16[64,1024]{1,0:T(8,128)(2,1)S(1)}, u32[]{:S(2)}, u32[]{:S(2)}) collective-permute-start(bf16[64,1024]{1,0:T(8,128)(2,1)S(1)} %get-tuple-element.85), channel_id=1, source_target_pairs={{0,1},{1,0},{2,3},{3,2},{4,5},{5,4},{6,7},{7,6},{8,9},{9,8},{10,11... | collective-permute-start | bytes 393224 | tf_op jit(solution)/shard_map/ppermute | solution.py:431
  67.3 1.9 %collective-permute-start.12 = (bf16[64,1024]{1,0:T(8,128)(2,1)S(1)}, bf16[64,1024]{1,0:T(8,128)(2,1)S(1)}, u32[]{:S(2)}, u32[]{:S(2)}) collective-permute-start(bf16[64,1024]{1,0:T(8,128)(2,1)S(1)} %get-tuple-element.86), channel_id=1, source_target_pairs={{1,2},{2,1},{3,4},{4,3},{5,6},{6,5},{9,10},{10,9},{11,12},{12,11},... | collective-permute-start | bytes 393224 | tf_op jit(solution)/shard_map/ppermute | solution.py:432
  69.2 4.9 %collective-permute-done.12.from_other_ref = bf16[64,1024]{1,0:T(8,128)(2,1)S(1)} collective-permute-done((bf16[64,1024]{1,0:T(8,128)(2,1)S(1)}, bf16[64,1024]{1,0:T(8,128)(2,1)S(1)}, u32[]{:S(2)}, u32[]{:S(2)}) %collective-permute-start.12) | collective-permute-done | bytes 131104 | tf_op jit(solution)/shard_map/ppermute | solution.py:432
  74.1 1.1 %shard_map.145 = f32[2,64,1024]{2,1,0:T(8,128)} custom-call(f32[2,64,1024]{2,1,0:T(8,128)S(1)} %get-tuple-element.79.own_ref, bf16[64,1024]{1,0:T(8,128)(2,1)S(1)} %collective-permute-done.11.from_mate_ref, bf16[64,1024]{1,0:T(8,128)(2,1)S(1)} %collective-permute-done.12.from_other_ref, s32[2,32]{1,0:T(2,128)S(1)} %get-tuple-element.87.halo_ref), custom_call_target="tpu_custom_call" | custom-call | flops 1 | bytes 1 | tf_op jit(solution)/shard_map/pallas_call | solution.py:28
  75.2 0.9 %shard_map.146 = (f32[32,2048]{1,0:T(8,128)}, f32[32,1024]{1,0:T(8,128)}, f32[32,100]{1,0:T(8,128)}) custom-call(f32[32,2304]{1,0:T(8,128)S(1)} %slice.220.own_ref, bf16[32,2304]{1,0:T(8,128)(2,1)S(1)} %collective-permute-done.19.arrived_ref, bf16[100,1024]{1,0:T(8,128)(2,1)S(1)} %bitcast.4), custom_call_target="tpu_custom_call" | custom-call | flops 1 | bytes 1 | tf_op jit(solution)/shard_map/pallas_call | solution.py:28
  (33 shorter events, 0.3 us)
Async XLA Ops:
  0.6 6.2 %copy-start.2 = (bf16[256,1024]{1,0:T(8,128)(2,1)S(1)}, bf16[256,1024]{1,0:T(8,128)(2,1)}, u32[]{:S(2)}) copy-start(bf16[256,1024]{1,0:T(8,128)(2,1)} %q_ref.5) | copy-start | bytes 1572868
  0.6 6.2 %copy-start.1 = (bf16[1024,1024]{1,0:T(8,128)(2,1)S(1)}, bf16[1024,1024]{1,0:T(8,128)(2,1)}, u32[]{:S(2)}) copy-start(bf16[1024,1024]{1,0:T(8,128)(2,1)} %wo_ref.3) | copy-start | bytes 6291460
  0.7 6.2 %copy-start.8 = (f32[100]{0:T(128)S(1)}, f32[100]{0:T(128)}, u32[]{:S(2)}) copy-start(f32[100]{0:T(128)} %param.19) | copy-start | bytes 1204
  0.7 6.2 %copy-start.7 = (f32[256]{0:T(256)S(1)}, f32[256]{0:T(256)}, u32[]{:S(2)}) copy-start(f32[256]{0:T(256)} %param.18) | copy-start | bytes 3076
  0.7 6.2 %copy-start.4 = (f32[100,256]{1,0:T(8,128)S(1)}, f32[100,256]{1,0:T(8,128)}, u32[]{:S(2)}) copy-start(f32[100,256]{1,0:T(8,128)} %init_ref.1) | copy-start | bytes 307204
  0.7 6.2 %copy-start.3 = (bf16[1024,100]{0,1:T(8,128)(2,1)S(1)}, bf16[1024,100]{0,1:T(8,128)(2,1)}, u32[]{:S(2)}) copy-start(bf16[1024,100]{0,1:T(8,128)(2,1)} %param.15) | copy-start | bytes 614404
  0.7 6.2 %copy-start = (bf16[1024,2048]{1,0:T(8,128)(2,1)S(1)}, bf16[1024,2048]{1,0:T(8,128)(2,1)}, u32[]{:S(2)}) copy-start(bf16[1024,2048]{1,0:T(8,128)(2,1)} %kvw_ref.5) | copy-start | bytes 12582916
  2.1 6.3 %collective-permute-start = (bf16[64,1024]{1,0:T(8,128)(2,1)S(1)}, bf16[64,1024]{1,0:T(8,128)(2,1)S(1)}, u32[]{:S(2)}, u32[]{:S(2)}) collective-permute-start(bf16[64,1024]{1,0:T(8,128)(2,1)S(1)} %get-tuple-element.49), channel_id=1, source_target_pairs={{0,1},{1,0},{2,3},{3,2},{4,5},{5,4},{6,7},{7,6},{8,9},{9,8},{10,11... | collective-permute-start | bytes 393224 | tf_op jit(solution)/shard_map/ppermute | solution.py:353
  2.2 7.7 %collective-permute-start.1 = (bf16[64,1024]{1,0:T(8,128)(2,1)S(1)}, bf16[64,1024]{1,0:T(8,128)(2,1)S(1)}, u32[]{:S(2)}, u32[]{:S(2)}) collective-permute-start(bf16[64,1024]{1,0:T(8,128)(2,1)S(1)} %get-tuple-element.50), channel_id=1, source_target_pairs={{1,2},{2,1},{3,4},{4,3},{5,6},{6,5},{9,10},{10,9},{11,12},{12,11},... | collective-permute-start | bytes 393224 | tf_op jit(solution)/shard_map/ppermute | solution.py:354
  6.9 3.1 %copy-start.6 = (s32[3,256]{1,0:T(4,128)S(1)}, s32[3,256]{1,0:T(4,128)}, u32[]{:S(2)}) copy-start(s32[3,256]{1,0:T(4,128)} %src_ref.1) | copy-start | bytes 9220
  10.0 15.2 %copy-start.5 = (f32[100,256]{1,0:T(8,128)S(1)}, f32[100,256]{1,0:T(8,128)}, u32[]{:S(2)}) copy-start(f32[100,256]{1,0:T(8,128)} %refs_5_.1) | copy-start | bytes 307204
  14.9 7.2 %collective-permute-start.4 = (bf16[208,256]{1,0:T(8,128)(2,1)S(1)}, bf16[208,256]{1,0:T(8,128)(2,1)S(1)}, u32[]{:S(2)}, u32[]{:S(2)}) collective-permute-start(bf16[208,256]{1,0:T(8,128)(2,1)S(1)} %get-tuple-element.54), channel_id=1, source_target_pairs={{0,24},{8,16},{16,8},{24,0},{1,25},{9,17},{17,9},{25,1},{2,26},{10... | collective-permute-start | bytes 319496 | tf_op jit(solution)/shard_map/ppermute | solution.py:387
  19.3 5.8 %collective-permute-start.3 = (bf16[208,256]{1,0:T(8,128)(2,1)S(1)}, bf16[208,256]{1,0:T(8,128)(2,1)S(1)}, u32[]{:S(2)}, u32[]{:S(2)}) collective-permute-start(bf16[208,256]{1,0:T(8,128)(2,1)S(1)} %get-tuple-element.54), channel_id=1, source_target_pairs={{0,16},{8,24},{16,0},{24,8},{1,17},{9,25},{17,1},{25,9},{2,18},{10... | collective-permute-start | bytes 319496 | tf_op jit(solution)/shard_map/ppermute | solution.py:387
  19.3 5.8 %collective-permute-start.2 = (bf16[208,256]{1,0:T(8,128)(2,1)S(1)}, bf16[208,256]{1,0:T(8,128)(2,1)S(1)}, u32[]{:S(2)}, u32[]{:S(2)}) collective-permute-start(bf16[208,256]{1,0:T(8,128)(2,1)S(1)} %get-tuple-element.54), channel_id=1, source_target_pairs={{0,8},{8,0},{16,24},{24,16},{1,9},{9,1},{17,25},{25,17},{2,10},{10... | collective-permute-start | bytes 319496 | tf_op jit(solution)/shard_map/ppermute | solution.py:387
  26.9 3.4 %collective-permute-start.5 = (bf16[512,768]{1,0:T(8,128)(2,1)S(1)}, bf16[512,768]{1,0:T(8,128)(2,1)S(1)}, u32[]{:S(2)}, u32[]{:S(2)}) collective-permute-start(bf16[512,768]{1,0:T(8,128)(2,1)S(1)} %get-tuple-element.61), channel_id=1, source_target_pairs={{0,1},{1,0},{2,3},{3,2},{4,5},{5,4},{6,7},{7,6},{8,9},{9,8},{10,11... | collective-permute-start | bytes 2359304 | tf_op jit(solution)/shard_map/ppermute | solution.py:316
  29.7 2.5 %collective-permute-start.6 = (bf16[512,768]{1,0:T(8,128)(2,1)S(1)}, bf16[512,768]{1,0:T(8,128)(2,1)S(1)}, u32[]{:S(2)}, u32[]{:S(2)}) collective-permute-start(bf16[512,768]{1,0:T(8,128)(2,1)S(1)} %get-tuple-element.69), channel_id=1, source_target_pairs={{0,1},{1,0},{2,3},{3,2},{4,5},{5,4},{6,7},{7,6},{8,9},{9,8},{10,11... | collective-permute-start | bytes 2359304 | tf_op jit(solution)/shard_map/ppermute | solution.py:316
  30.3 3.0 %collective-permute-start.7 = (bf16[512,768]{1,0:T(8,128)(2,1)S(1)}, bf16[512,768]{1,0:T(8,128)(2,1)S(1)}, u32[]{:S(2)}, u32[]{:S(2)}) collective-permute-start(bf16[512,768]{1,0:T(8,128)(2,1)S(1)} %get-tuple-element.71), channel_id=1, source_target_pairs={{0,1},{1,0},{2,3},{3,2},{4,5},{5,4},{6,7},{7,6},{8,9},{9,8},{10,11... | collective-permute-start | bytes 2359304 | tf_op jit(solution)/shard_map/ppermute | solution.py:316
  33.5 13.4 %collective-permute-start.8 = (bf16[256,768]{1,0:T(8,128)(2,1)S(1)}, bf16[256,768]{1,0:T(8,128)(2,1)S(1)}, u32[]{:S(2)}, u32[]{:S(2)}) collective-permute-start(bf16[256,768]{1,0:T(8,128)(2,1)S(1)} %add_convert_fusion.2), channel_id=1, source_target_pairs={{0,2},{1,3},{2,0},{3,1},{4,6},{5,7},{6,4},{7,5},{8,10},{9,11},{10,... | collective-permute-start | bytes 1179656 | tf_op jit(solution)/shard_map/ppermute | solution.py:316
  37.8 10.0 %collective-permute-start.9 = (bf16[256,768]{1,0:T(8,128)(2,1)S(1)}, bf16[256,768]{1,0:T(8,128)(2,1)S(1)}, u32[]{:S(2)}, u32[]{:S(2)}) collective-permute-start(bf16[256,768]{1,0:T(8,128)(2,1)S(1)} %get-tuple-element.81), channel_id=1, source_target_pairs={{0,4},{1,5},{2,6},{3,7},{4,0},{5,1},{6,2},{7,3},{8,12},{9,13},{10,... | collective-permute-start | bytes 1179656 | tf_op jit(solution)/shard_map/ppermute | solution.py:316
  38.1 10.3 %collective-permute-start.10 = (bf16[256,768]{1,0:T(8,128)(2,1)S(1)}, bf16[256,768]{1,0:T(8,128)(2,1)S(1)}, u32[]{:S(2)}, u32[]{:S(2)}) collective-permute-start(bf16[256,768]{1,0:T(8,128)(2,1)S(1)} %get-tuple-element.82), channel_id=1, source_target_pairs={{0,8},{8,0},{16,24},{24,16},{1,9},{9,1},{17,25},{25,17},{2,10},{10... | collective-permute-start | bytes 1179656 | tf_op jit(solution)/shard_map/ppermute | solution.py:316
  48.5 5.2 %collective-permute-start.17 = (bf16[128,768]{1,0:T(8,128)(2,1)S(1)}, bf16[128,768]{1,0:T(8,128)(2,1)S(1)}, u32[]{:S(2)}, u32[]{:S(2)}) collective-permute-start(bf16[128,768]{1,0:T(8,128)(2,1)S(1)} %add_convert_fusion.3), channel_id=1, source_target_pairs={{0,2},{1,3},{2,0},{3,1},{4,6},{5,7},{6,4},{7,5},{8,10},{9,11},{10,... | collective-permute-start | bytes 589832 | tf_op jit(solution)/shard_map/ppermute | solution.py:316
  49.7 4.8 %collective-permute-start.15 = (bf16[128,768]{1,0:T(8,128)(2,1)S(1)}, bf16[128,768]{1,0:T(8,128)(2,1)S(1)}, u32[]{:S(2)}, u32[]{:S(2)}) collective-permute-start(bf16[128,768]{1,0:T(8,128)(2,1)S(1)} %add_convert_fusion.4), channel_id=1, source_target_pairs={{0,8},{8,0},{16,24},{24,16},{1,9},{9,1},{17,25},{25,17},{2,10},{10... | collective-permute-start | bytes 589832 | tf_op jit(solution)/shard_map/ppermute | solution.py:316
  49.8 5.6 %collective-permute-start.13 = (bf16[128,768]{1,0:T(8,128)(2,1)S(1)}, bf16[128,768]{1,0:T(8,128)(2,1)S(1)}, u32[]{:S(2)}, u32[]{:S(2)}) collective-permute-start(bf16[128,768]{1,0:T(8,128)(2,1)S(1)} %add_convert_fusion.5), channel_id=1, source_target_pairs={{0,4},{1,5},{2,6},{3,7},{4,0},{5,1},{6,2},{7,3},{8,12},{9,13},{10,... | collective-permute-start | bytes 589832 | tf_op jit(solution)/shard_map/ppermute | solution.py:316
  53.8 4.3 %collective-permute-start.18 = (bf16[64,768]{1,0:T(8,128)(2,1)S(1)}, bf16[64,768]{1,0:T(8,128)(2,1)S(1)}, u32[]{:S(2)}, u32[]{:S(2)}) collective-permute-start(bf16[64,768]{1,0:T(8,128)(2,1)S(1)} %add_convert_fusion.6), channel_id=1, source_target_pairs={{0,4},{1,5},{2,6},{3,7},{4,0},{5,1},{6,2},{7,3},{8,12},{9,13},{10,... | collective-permute-start | bytes 294920 | tf_op jit(solution)/shard_map/ppermute | solution.py:316
  54.5 3.6 %collective-permute-start.16 = (bf16[64,768]{1,0:T(8,128)(2,1)S(1)}, bf16[64,768]{1,0:T(8,128)(2,1)S(1)}, u32[]{:S(2)}, u32[]{:S(2)}) collective-permute-start(bf16[64,768]{1,0:T(8,128)(2,1)S(1)} %add_convert_fusion.7), channel_id=1, source_target_pairs={{0,2},{1,3},{2,0},{3,1},{4,6},{5,7},{6,4},{7,5},{8,10},{9,11},{10,... | collective-permute-start | bytes 294920 | tf_op jit(solution)/shard_map/ppermute | solution.py:316
  55.4 3.8 %collective-permute-start.14 = (bf16[64,768]{1,0:T(8,128)(2,1)S(1)}, bf16[64,768]{1,0:T(8,128)(2,1)S(1)}, u32[]{:S(2)}, u32[]{:S(2)}) collective-permute-start(bf16[64,768]{1,0:T(8,128)(2,1)S(1)} %add_convert_fusion.8), channel_id=1, source_target_pairs={{0,8},{8,0},{16,24},{24,16},{1,9},{9,1},{17,25},{25,17},{2,10},{10... | collective-permute-start | bytes 294920 | tf_op jit(solution)/shard_map/ppermute | solution.py:316
  59.4 15.8 %collective-permute-start.19 = (bf16[32,2304]{1,0:T(8,128)(2,1)S(1)}, bf16[32,2304]{1,0:T(8,128)(2,1)S(1)}, u32[]{:S(2)}, u32[]{:S(2)}) collective-permute-start(bf16[32,2304]{1,0:T(8,128)(2,1)S(1)} %slice.262), channel_id=1, source_target_pairs={{0,16},{8,24},{16,0},{24,8},{1,17},{9,25},{17,1},{25,9},{2,18},{10... | collective-permute-start | bytes 442376 | tf_op jit(solution)/shard_map/ppermute | solution.py:316
  61.2 8.1 %collective-permute-start.11 = (bf16[64,1024]{1,0:T(8,128)(2,1)S(1)}, bf16[64,1024]{1,0:T(8,128)(2,1)S(1)}, u32[]{:S(2)}, u32[]{:S(2)}) collective-permute-start(bf16[64,1024]{1,0:T(8,128)(2,1)S(1)} %get-tuple-element.85), channel_id=1, source_target_pairs={{0,1},{1,0},{2,3},{3,2},{4,5},{5,4},{6,7},{7,6},{8,9},{9,8},{10,11... | collective-permute-start | bytes 393224 | tf_op jit(solution)/shard_map/ppermute | solution.py:431
  67.3 6.8 %collective-permute-start.12 = (bf16[64,1024]{1,0:T(8,128)(2,1)S(1)}, bf16[64,1024]{1,0:T(8,128)(2,1)S(1)}, u32[]{:S(2)}, u32[]{:S(2)}) collective-permute-start(bf16[64,1024]{1,0:T(8,128)(2,1)S(1)} %get-tuple-element.86), channel_id=1, source_target_pairs={{1,2},{2,1},{3,4},{4,3},{5,6},{6,5},{9,10},{10,9},{11,12},{12,11},... | collective-permute-start | bytes 393224 | tf_op jit(solution)/shard_map/ppermute | solution.py:432

commit v6 on v5

--- a/solution.py
+++ b/solution.py
@@ -340,7 +340,7 @@
     chips = n_band // 2
     send_rows = -(-channels // 8) * 8
     mates = [(i, i ^ 1) for i in range(n_band)]
-    others = [(i, i + 1 if i % 2 else i - 1) for i in range(1, n_band - 1)]
+    others = [(i, (i + 1 if i % 2 else i - 1) % n_band) for i in range(n_band)]
 
     own_hidden, halo, for_mate, for_other = call(
         pick_body,
@@ -384,7 +384,7 @@
     )
 
     received = [
-        lax.ppermute(sent, "member", [(i, i ^ s) for i in range(n_member)]) for s in range(1, n_member)
+        lax.ppermute(sent, "member", [(i, i ^ s) for i in range(n_member)]) for s in range(n_member - 1, 0, -1)
     ]
 
     ext_t = call(
@@ -427,9 +427,9 @@
             )
         arrived = [swap(out, *turn[step], count[turn[step][0]]) for out, turn in zip(outgoing, turns)]
         if step == 0:
-            arrived, back_mate, back_other = lax.optimization_barrier((arrived, back_mate, back_other))
             from_mate = lax.ppermute(back_mate, "band", mates)
             from_other = lax.ppermute(back_other, "band", others)
+            arrived, from_mate, from_other = lax.optimization_barrier((arrived, from_mate, from_other))
         groups = [lower(terms) + [new] for terms, new in zip(groups, arrived)]
     hidden_grad = call(
         hidden_body,

time: 76.3 us -> 75.2 us (0.986)
  the two profiles are of different devices: /device:TPU:1 before, /device:TPU:0 now
where the time goes in v6:
time: 75.2 us; the launch traced here: 75.1 us
  waiting for transfers between devices  33.9 us (45%)
  starting transfers between devices  23.5 us (31%)
  Pallas kernels  15.8 us (21%)
  other arithmetic  0.91 us (1%)
  between operations  0.88 us (1%)
    ppermute x13, waiting for transfers between devices, swap(): return lax.ppermute(rows, axis, [(i, i ^ 1 << bit) for i in range(count)])  16.4 us
    pallas_call x9, Pallas kernels, call(): pl.pallas_call(body, out_shape=out_shape, in_specs=[pl.BlockSpec(memory_s...  15.8 us
    ppermute x13, starting transfers between devices, swap(): return lax.ppermute(rows, axis, [(i, i ^ 1 << bit) for i in range(count)])  13.8 us
    ppermute x3, waiting for transfers between devices, shards(): lax.ppermute(sent, 'member', [(i, i ^ s) for i in range(n_member)])  8.32 us
    ppermute x1, waiting for transfers between devices, shards(): from_other = lax.ppermute(back_other, 'band', others)  7.27 us
    ppermute x3, starting transfers between devices, shards(): lax.ppermute(sent, 'member', [(i, i ^ s) for i in range(n_member)])  4.58 us
    ppermute x1, starting transfers between devices, shards(): other = lax.ppermute(for_other, 'band', others)  3.56 us
    ppermute x1, waiting for transfers between devices, shards(): other = lax.ppermute(for_other, 'band', others)  1.65 us
  transfers between devices with their start and end apart: 20, of which 13 were waited for; matrix products, arithmetic and copies ran while one was open for 1% of the time, Pallas kernels for 9%

profile of v6, /device:TPU:0, one launch (start us, length us, event | category | flops | bytes accessed | tf_op | source)
XLA Modules:
  0.0 75.1 jit_solution(4640076222511325244)
XLA Ops:
  0.7 1.4 %shard_map.138 = (bf16[2,64,1024]{2,1,0:T(8,128)(2,1)S(1)}, s32[2,32]{1,0:T(2,128)S(1)}, bf16[64,1024]{1,0:T(8,128)(2,1)S(1)}, bf16[64,1024]{1,0:T(8,128)(2,1)S(1)}) custom-call(bf16[2,64,1024]{2,1,0:T(8,128)(2,1)} %hidden_hbm.1, s32[2,32]{1,0:T(2,128)} %halo_hbm.1), custom_call_target="tpu_custom_call" | custom-call | flops 10000000000 | bytes 1 | tf_op jit(solution)/shard_map/pallas_call | solution.py:28
  2.1 0.5 collective-permute-start
  2.6 3.6 %collective-permute-start.1 = (bf16[64,1024]{1,0:T(8,128)(2,1)S(1)}, bf16[64,1024]{1,0:T(8,128)(2,1)S(1)}, u32[]{:S(2)}, u32[]{:S(2)}) collective-permute-start(bf16[64,1024]{1,0:T(8,128)(2,1)S(1)} %get-tuple-element.50), channel_id=1, source_target_pairs={{0,7},{1,2},{2,1},{3,4},{4,3},{5,6},{6,5},{7,0},{8,15},{9,10},{10,... | collective-permute-start | bytes 393224 | tf_op jit(solution)/shard_map/ppermute | solution.py:354
  6.2 1.5 %shard_map.139 = (bf16[128,2048]{1,0:T(8,128)(2,1)S(1)}, bf16[1024,128]{1,0:T(8,128)(2,1)S(1)}, bf16[128,1024]{1,0:T(8,128)(2,1)S(1)}, f32[128,256]{1,0:T(8,128)S(1)}, f32[100,256]{1,0:T(8,128)S(1)}) custom-call(bf16[2,64,1024]{2,1,0:T(8,128)(2,1)S(1)} %get-tuple-element.51.hidden_ref, bf16[1024,1024]{1,0:T(8,128)(2,1)S(1)} %copy-done.1, ...), custom_call_target="tpu_custom_call" | custom-call | flops 1 | bytes 1 | tf_op jit(solution)/shard_map/pallas_call | solution.py:28
  7.8 1.6 %collective-permute-done.1.other_ref = bf16[64,1024]{1,0:T(8,128)(2,1)S(1)} collective-permute-done((bf16[64,1024]{1,0:T(8,128)(2,1)S(1)}, bf16[64,1024]{1,0:T(8,128)(2,1)S(1)}, u32[]{:S(2)}, u32[]{:S(2)}) %collective-permute-start.1) | collective-permute-done | bytes 131104 | tf_op jit(solution)/shard_map/ppermute | solution.py:354
  9.4 4.9 %shard_map.140 = (bf16[2,128,2048]{2,1,0:T(8,128)(2,1)S(1)}, bf16[8,2,256,256]{3,2,1,0:T(8,128)(2,1)S(1)}, bf16[8,2,256,256]{3,2,1,0:T(8,128)(2,1)S(1)}, bf16[2,...) custom-call(bf16[64,1024]{1,0:T(8,128)(2,1)S(1)} %collective-permute-done.mate_ref, ...), custom_call_target="tpu_custom_call" | custom-call | flops 1 | bytes 1 | tf_op jit(solution)/shard_map/pallas_call | solution.py:28
  14.4 2.0 %collective-permute-start.4 = (bf16[208,256]{1,0:T(8,128)(2,1)S(1)}, bf16[208,256]{1,0:T(8,128)(2,1)S(1)}, u32[]{:S(2)}, u32[]{:S(2)}) collective-permute-start(bf16[208,256]{1,0:T(8,128)(2,1)S(1)} %get-tuple-element.54), channel_id=1, source_target_pairs={{0,8},{8,0},{16,24},{24,16},{1,9},{9,1},{17,25},{25,17},{2,10},{10... | collective-permute-start | bytes 319496 | tf_op jit(solution)/shard_map/ppermute | solution.py:387
  16.3 2.6 %collective-permute-start.3 = (bf16[208,256]{1,0:T(8,128)(2,1)S(1)}, bf16[208,256]{1,0:T(8,128)(2,1)S(1)}, u32[]{:S(2)}, u32[]{:S(2)}) collective-permute-start(bf16[208,256]{1,0:T(8,128)(2,1)S(1)} %get-tuple-element.54), channel_id=1, source_target_pairs={{0,16},{8,24},{16,0},{24,8},{1,17},{9,25},{17,1},{25,9},{2,18},{10... | collective-permute-start | bytes 319496 | tf_op jit(solution)/shard_map/ppermute | solution.py:387
  18.9 0.3 shard_map.141.refs_9_.ext_ref
  19.2 0.4 collective-permute-done.4.refs_2_
  19.6 7.9 %collective-permute-done.3.refs_1_ = bf16[208,256]{1,0:T(8,128)(2,1)S(1)} collective-permute-done((bf16[208,256]{1,0:T(8,128)(2,1)S(1)}, bf16[208,256]{1,0:T(8,128)(2,1)S(1)}, u32[]{:S(2)}, u32[]{:S(2)}) %collective-permute-start.3) | collective-permute-done | bytes 106528 | tf_op jit(solution)/shard_map/ppermute | solution.py:387
  27.5 1.8 %shard_map.142 = (bf16[2,128,256]{2,1,0:T(8,128)(2,1)S(1)}, bf16[2,1024,256]{2,1,0:T(8,128)(2,1)S(1)}, bf16[256,1024]{1,0:T(8,128)(2,1)S(1)}, bf16[512,768]{1,0:T(8,128)(2,1)S(1)}, bf16[512,768]{1,0:T(8,128)(2,1)S(1)}) custom-call(bf16[208,256]{1,0:T(8,128)(2,1)S(1)} %collective-permute-done.2.refs_0_, bf16[208,256]{1,0:T(8,128)(2,1)S(1)} %collective-permute-done.3.refs_1_, ...), custom_call_target="tpu_custom_call" | custom-call | flops 1 | bytes 1 | tf_op jit(solution)/shard_map/pallas_call | solution.py:28
  29.3 0.1 collective-permute-start.5
  29.4 2.7 %shard_map.143 = (bf16[256,1024]{1,0:T(8,128)(2,1)S(1)}, bf16[512,768]{1,0:T(8,128)(2,1)S(1)}, bf16[512,768]{1,0:T(8,128)(2,1)S(1)}, bf16[512,768]{1,0:T(8,128)(2,1)S(1)}, bf16[512,768]{1,0:T(8,128)(2,1)S(1)}) custom-call(bf16[2,128,256]{2,1,0:T(8,128)(2,1)S(1)} %get-tuple-element.62.grad_ref, bf16[2,1024,256]{2,1,0:T(8,128)(2,1)S(1)} %get-tuple-element.63.dm_ref, ...), custom_call_target="tpu_custom_call" | custom-call | flops 1 | bytes 1 | tf_op jit(solution)/shard_map/pallas_call | solution.py:28
  32.1 0.6 collective-permute-start.6
  32.7 0.1 collective-permute-start.7
  32.7 0.1 add_convert_fusion.2
  32.8 1.7 %collective-permute-done.6 = bf16[512,768]{1,0:T(8,128)(2,1)S(1)} collective-permute-done((bf16[512,768]{1,0:T(8,128)(2,1)S(1)}, bf16[512,768]{1,0:T(8,128)(2,1)S(1)}, u32[]{:S(2)}, u32[]{:S(2)}) %collective-permute-start.6) | collective-permute-done | bytes 786464 | tf_op jit(solution)/shard_map/ppermute | solution.py:316
  34.6 1.1 %collective-permute-done.7 = bf16[512,768]{1,0:T(8,128)(2,1)S(1)} collective-permute-done((bf16[512,768]{1,0:T(8,128)(2,1)S(1)}, bf16[512,768]{1,0:T(8,128)(2,1)S(1)}, u32[]{:S(2)}, u32[]{:S(2)}) %collective-permute-start.7) | collective-permute-done | bytes 786464 | tf_op jit(solution)/shard_map/ppermute | solution.py:316
  35.7 0.2 add_convert_fusion
  35.9 0.5 collective-permute-start.8
  36.4 2.0 %collective-permute-start.9 = (bf16[256,768]{1,0:T(8,128)(2,1)S(1)}, bf16[256,768]{1,0:T(8,128)(2,1)S(1)}, u32[]{:S(2)}, u32[]{:S(2)}) collective-permute-start(bf16[256,768]{1,0:T(8,128)(2,1)S(1)} %get-tuple-element.81), channel_id=1, source_target_pairs={{0,4},{1,5},{2,6},{3,7},{4,0},{5,1},{6,2},{7,3},{8,12},{9,13},{10,... | collective-permute-start | bytes 1179656 | tf_op jit(solution)/shard_map/ppermute | solution.py:316
  38.3 2.1 %collective-permute-start.10 = (bf16[256,768]{1,0:T(8,128)(2,1)S(1)}, bf16[256,768]{1,0:T(8,128)(2,1)S(1)}, u32[]{:S(2)}, u32[]{:S(2)}) collective-permute-start(bf16[256,768]{1,0:T(8,128)(2,1)S(1)} %get-tuple-element.82), channel_id=1, source_target_pairs={{0,8},{8,0},{16,24},{24,16},{1,9},{9,1},{17,25},{25,17},{2,10},{10... | collective-permute-start | bytes 1179656 | tf_op jit(solution)/shard_map/ppermute | solution.py:316
  40.4 1.3 %shard_map.144 = (f32[2,64,1024]{2,1,0:T(8,128)S(1)}, bf16[64,1024]{1,0:T(8,128)(2,1)S(1)}, bf16[64,1024]{1,0:T(8,128)(2,1)S(1)}) custom-call(bf16[256,1024]{1,0:T(8,128)(2,1)S(1)} %get-tuple-element.78.ngk_ref, bf16[256,1024]{1,0:T(8,128)(2,1)S(1)} %get-tuple-element.67.ngv_ref, bf16[1024,2048]{1,0:T(8,128)(2,1)S(1)} %copy-done), custom_call_target="tpu_custom_call" | custom-call | flops 1 | bytes 1 | tf_op jit(solution)/shard_map/pallas_call | solution.py:28
  41.7 0.1 collective-permute-start.11
  41.8 1.0 %collective-permute-start.12 = (bf16[64,1024]{1,0:T(8,128)(2,1)S(1)}, bf16[64,1024]{1,0:T(8,128)(2,1)S(1)}, u32[]{:S(2)}, u32[]{:S(2)}) collective-permute-start(bf16[64,1024]{1,0:T(8,128)(2,1)S(1)} %get-tuple-element.84), channel_id=1, source_target_pairs={{0,7},{1,2},{2,1},{3,4},{4,3},{5,6},{6,5},{7,0},{8,15},{9,10},{10,... | collective-permute-start | bytes 393224 | tf_op jit(solution)/shard_map/ppermute | solution.py:431
  42.8 0.3 collective-permute-done.11.from_mate_ref
  43.1 7.3 %collective-permute-done.12.from_other_ref = bf16[64,1024]{1,0:T(8,128)(2,1)S(1)} collective-permute-done((bf16[64,1024]{1,0:T(8,128)(2,1)S(1)}, bf16[64,1024]{1,0:T(8,128)(2,1)S(1)}, u32[]{:S(2)}, u32[]{:S(2)}) %collective-permute-start.12) | collective-permute-done | bytes 131104 | tf_op jit(solution)/shard_map/ppermute | solution.py:431
  50.4 0.1 add_convert_fusion.4
  50.5 0.1 add_convert_fusion.3
  50.5 0.1 collective-permute-start.17
  50.6 1.8 %collective-permute-start.15 = (bf16[128,768]{1,0:T(8,128)(2,1)S(1)}, bf16[128,768]{1,0:T(8,128)(2,1)S(1)}, u32[]{:S(2)}, u32[]{:S(2)}) collective-permute-start(bf16[128,768]{1,0:T(8,128)(2,1)S(1)} %add_convert_fusion.4), channel_id=1, source_target_pairs={{0,8},{8,0},{16,24},{24,16},{1,9},{9,1},{17,25},{25,17},{2,10},{10... | collective-permute-start | bytes 589832 | tf_op jit(solution)/shard_map/ppermute | solution.py:316
  52.4 0.1 add_convert_fusion.5
  52.5 1.9 %collective-permute-start.13 = (bf16[128,768]{1,0:T(8,128)(2,1)S(1)}, bf16[128,768]{1,0:T(8,128)(2,1)S(1)}, u32[]{:S(2)}, u32[]{:S(2)}) collective-permute-start(bf16[128,768]{1,0:T(8,128)(2,1)S(1)} %add_convert_fusion.5), channel_id=1, source_target_pairs={{0,4},{1,5},{2,6},{3,7},{4,0},{5,1},{6,2},{7,3},{8,12},{9,13},{10,... | collective-permute-start | bytes 589832 | tf_op jit(solution)/shard_map/ppermute | solution.py:316
  54.4 2.9 %collective-permute-done.17 = bf16[128,768]{1,0:T(8,128)(2,1)S(1)} collective-permute-done((bf16[128,768]{1,0:T(8,128)(2,1)S(1)}, bf16[128,768]{1,0:T(8,128)(2,1)S(1)}, u32[]{:S(2)}, u32[]{:S(2)}) %collective-permute-start.17) | collective-permute-done | bytes 196640 | tf_op jit(solution)/shard_map/ppermute | solution.py:316
  57.4 1.1 %collective-permute-start.18 = (bf16[64,768]{1,0:T(8,128)(2,1)S(1)}, bf16[64,768]{1,0:T(8,128)(2,1)S(1)}, u32[]{:S(2)}, u32[]{:S(2)}) collective-permute-start(bf16[64,768]{1,0:T(8,128)(2,1)S(1)} %add_convert_fusion.6), channel_id=1, source_target_pairs={{0,4},{1,5},{2,6},{3,7},{4,0},{5,1},{6,2},{7,3},{8,12},{9,13},{10,... | collective-permute-start | bytes 294920 | tf_op jit(solution)/shard_map/ppermute | solution.py:316
  58.5 0.8 %collective-permute-start.16 = (bf16[64,768]{1,0:T(8,128)(2,1)S(1)}, bf16[64,768]{1,0:T(8,128)(2,1)S(1)}, u32[]{:S(2)}, u32[]{:S(2)}) collective-permute-start(bf16[64,768]{1,0:T(8,128)(2,1)S(1)} %add_convert_fusion.7), channel_id=1, source_target_pairs={{0,2},{1,3},{2,0},{3,1},{4,6},{5,7},{6,4},{7,5},{8,10},{9,11},{10,... | collective-permute-start | bytes 294920 | tf_op jit(solution)/shard_map/ppermute | solution.py:316
  59.4 0.8 %collective-permute-done.13 = bf16[128,768]{1,0:T(8,128)(2,1)S(1)} collective-permute-done((bf16[128,768]{1,0:T(8,128)(2,1)S(1)}, bf16[128,768]{1,0:T(8,128)(2,1)S(1)}, u32[]{:S(2)}, u32[]{:S(2)}) %collective-permute-start.13) | collective-permute-done | bytes 196640 | tf_op jit(solution)/shard_map/ppermute | solution.py:316
  60.2 1.0 %collective-permute-start.14 = (bf16[64,768]{1,0:T(8,128)(2,1)S(1)}, bf16[64,768]{1,0:T(8,128)(2,1)S(1)}, u32[]{:S(2)}, u32[]{:S(2)}) collective-permute-start(bf16[64,768]{1,0:T(8,128)(2,1)S(1)} %add_convert_fusion.8), channel_id=1, source_target_pairs={{0,8},{8,0},{16,24},{24,16},{1,9},{9,1},{17,25},{25,17},{2,10},{10... | collective-permute-start | bytes 294920 | tf_op jit(solution)/shard_map/ppermute | solution.py:316
  61.2 1.2 %collective-permute-done.18 = bf16[64,768]{1,0:T(8,128)(2,1)S(1)} collective-permute-done((bf16[64,768]{1,0:T(8,128)(2,1)S(1)}, bf16[64,768]{1,0:T(8,128)(2,1)S(1)}, u32[]{:S(2)}, u32[]{:S(2)}) %collective-permute-start.18) | collective-permute-done | bytes 98336 | tf_op jit(solution)/shard_map/ppermute | solution.py:316
  62.4 0.1 convert_add_fusion
  62.5 0.9 %collective-permute-done.16 = bf16[64,768]{1,0:T(8,128)(2,1)S(1)} collective-permute-done((bf16[64,768]{1,0:T(8,128)(2,1)S(1)}, bf16[64,768]{1,0:T(8,128)(2,1)S(1)}, u32[]{:S(2)}, u32[]{:S(2)}) %collective-permute-start.16) | collective-permute-done | bytes 98336 | tf_op jit(solution)/shard_map/ppermute | solution.py:316
  63.4 0.1 convert_add_fusion.1
  63.5 1.6 %collective-permute-done.14 = bf16[64,768]{1,0:T(8,128)(2,1)S(1)} collective-permute-done((bf16[64,768]{1,0:T(8,128)(2,1)S(1)}, bf16[64,768]{1,0:T(8,128)(2,1)S(1)}, u32[]{:S(2)}, u32[]{:S(2)}) %collective-permute-start.14) | collective-permute-done | bytes 98336 | tf_op jit(solution)/shard_map/ppermute | solution.py:316
  65.2 1.9 %collective-permute-start.19 = (bf16[32,2304]{1,0:T(8,128)(2,1)S(1)}, bf16[32,2304]{1,0:T(8,128)(2,1)S(1)}, u32[]{:S(2)}, u32[]{:S(2)}) collective-permute-start(bf16[32,2304]{1,0:T(8,128)(2,1)S(1)} %slice.262), channel_id=1, source_target_pairs={{0,16},{8,24},{16,0},{24,8},{1,17},{9,25},{17,1},{25,9},{2,18},{10... | collective-permute-start | bytes 442376 | tf_op jit(solution)/shard_map/ppermute | solution.py:316
  67.1 1.1 %shard_map.145 = f32[2,64,1024]{2,1,0:T(8,128)} custom-call(f32[2,64,1024]{2,1,0:T(8,128)S(1)} %get-tuple-element.79.own_ref, bf16[64,1024]{1,0:T(8,128)(2,1)S(1)} %collective-permute-done.11.from_mate_ref, bf16[64,1024]{1,0:T(8,128)(2,1)S(1)} %collective-permute-done.12.from_other_ref, s32[2,32]{1,0:T(2,128)S(1)} %get-tuple-element.87.halo_ref), custom_call_target="tpu_custom_call" | custom-call | flops 1 | bytes 1 | tf_op jit(solution)/shard_map/pallas_call | solution.py:28
  68.2 6.0 %collective-permute-done.19.arrived_ref = bf16[32,2304]{1,0:T(8,128)(2,1)S(1)} collective-permute-done((bf16[32,2304]{1,0:T(8,128)(2,1)S(1)}, bf16[32,2304]{1,0:T(8,128)(2,1)S(1)}, u32[]{:S(2)}, u32[]{:S(2)}) %collective-permute-start.19) | collective-permute-done | bytes 147488 | tf_op jit(solution)/shard_map/ppermute | solution.py:316
  74.2 0.9 %shard_map.146 = (f32[32,2048]{1,0:T(8,128)}, f32[32,1024]{1,0:T(8,128)}, f32[32,100]{1,0:T(8,128)}) custom-call(f32[32,2304]{1,0:T(8,128)S(1)} %slice.220.own_ref, bf16[32,2304]{1,0:T(8,128)(2,1)S(1)} %collective-permute-done.19.arrived_ref, bf16[100,1024]{1,0:T(8,128)(2,1)S(1)} %bitcast.4), custom_call_target="tpu_custom_call" | custom-call | flops 1 | bytes 1 | tf_op jit(solution)/shard_map/pallas_call | solution.py:28
  (33 shorter events, 0.4 us)
Async XLA Ops:
  0.6 5.5 %copy-start.2 = (bf16[256,1024]{1,0:T(8,128)(2,1)S(1)}, bf16[256,1024]{1,0:T(8,128)(2,1)}, u32[]{:S(2)}) copy-start(bf16[256,1024]{1,0:T(8,128)(2,1)} %q_ref.5) | copy-start | bytes 1572868
  0.6 5.5 %copy-start.1 = (bf16[1024,1024]{1,0:T(8,128)(2,1)S(1)}, bf16[1024,1024]{1,0:T(8,128)(2,1)}, u32[]{:S(2)}) copy-start(bf16[1024,1024]{1,0:T(8,128)(2,1)} %wo_ref.3) | copy-start | bytes 6291460
  0.7 5.5 %copy-start.8 = (f32[100]{0:T(128)S(1)}, f32[100]{0:T(128)}, u32[]{:S(2)}) copy-start(f32[100]{0:T(128)} %param.19) | copy-start | bytes 1204
  0.7 5.5 %copy-start.7 = (f32[256]{0:T(256)S(1)}, f32[256]{0:T(256)}, u32[]{:S(2)}) copy-start(f32[256]{0:T(256)} %param.18) | copy-start | bytes 3076
  0.7 5.5 %copy-start.4 = (f32[100,256]{1,0:T(8,128)S(1)}, f32[100,256]{1,0:T(8,128)}, u32[]{:S(2)}) copy-start(f32[100,256]{1,0:T(8,128)} %init_ref.1) | copy-start | bytes 307204
  0.7 5.5 %copy-start.3 = (bf16[1024,100]{0,1:T(8,128)(2,1)S(1)}, bf16[1024,100]{0,1:T(8,128)(2,1)}, u32[]{:S(2)}) copy-start(bf16[1024,100]{0,1:T(8,128)(2,1)} %param.15) | copy-start | bytes 614404
  0.7 5.5 %copy-start = (bf16[1024,2048]{1,0:T(8,128)(2,1)S(1)}, bf16[1024,2048]{1,0:T(8,128)(2,1)}, u32[]{:S(2)}) copy-start(bf16[1024,2048]{1,0:T(8,128)(2,1)} %kvw_ref.5) | copy-start | bytes 12582916
  2.1 5.7 %collective-permute-start = (bf16[64,1024]{1,0:T(8,128)(2,1)S(1)}, bf16[64,1024]{1,0:T(8,128)(2,1)S(1)}, u32[]{:S(2)}, u32[]{:S(2)}) collective-permute-start(bf16[64,1024]{1,0:T(8,128)(2,1)S(1)} %get-tuple-element.49), channel_id=1, source_target_pairs={{0,1},{1,0},{2,3},{3,2},{4,5},{5,4},{6,7},{7,6},{8,9},{9,8},{10,11... | collective-permute-start | bytes 393224 | tf_op jit(solution)/shard_map/ppermute | solution.py:353
  2.6 6.8 %collective-permute-start.1 = (bf16[64,1024]{1,0:T(8,128)(2,1)S(1)}, bf16[64,1024]{1,0:T(8,128)(2,1)S(1)}, u32[]{:S(2)}, u32[]{:S(2)}) collective-permute-start(bf16[64,1024]{1,0:T(8,128)(2,1)S(1)} %get-tuple-element.50), channel_id=1, source_target_pairs={{0,7},{1,2},{2,1},{3,4},{4,3},{5,6},{6,5},{7,0},{8,15},{9,10},{10,... | collective-permute-start | bytes 393224 | tf_op jit(solution)/shard_map/ppermute | solution.py:354
  6.2 3.2 %copy-start.6 = (s32[3,256]{1,0:T(4,128)S(1)}, s32[3,256]{1,0:T(4,128)}, u32[]{:S(2)}) copy-start(s32[3,256]{1,0:T(4,128)} %src_ref.1) | copy-start | bytes 9220
  9.4 18.1 %copy-start.5 = (f32[100,256]{1,0:T(8,128)S(1)}, f32[100,256]{1,0:T(8,128)}, u32[]{:S(2)}) copy-start(f32[100,256]{1,0:T(8,128)} %refs_5_.1) | copy-start | bytes 307204
  14.4 5.2 %collective-permute-start.4 = (bf16[208,256]{1,0:T(8,128)(2,1)S(1)}, bf16[208,256]{1,0:T(8,128)(2,1)S(1)}, u32[]{:S(2)}, u32[]{:S(2)}) collective-permute-start(bf16[208,256]{1,0:T(8,128)(2,1)S(1)} %get-tuple-element.54), channel_id=1, source_target_pairs={{0,8},{8,0},{16,24},{24,16},{1,9},{9,1},{17,25},{25,17},{2,10},{10... | collective-permute-start | bytes 319496 | tf_op jit(solution)/shard_map/ppermute | solution.py:387
  16.3 11.2 %collective-permute-start.3 = (bf16[208,256]{1,0:T(8,128)(2,1)S(1)}, bf16[208,256]{1,0:T(8,128)(2,1)S(1)}, u32[]{:S(2)}, u32[]{:S(2)}) collective-permute-start(bf16[208,256]{1,0:T(8,128)(2,1)S(1)} %get-tuple-element.54), channel_id=1, source_target_pairs={{0,16},{8,24},{16,0},{24,8},{1,17},{9,25},{17,1},{25,9},{2,18},{10... | collective-permute-start | bytes 319496 | tf_op jit(solution)/shard_map/ppermute | solution.py:387
  18.9 8.6 %collective-permute-start.2 = (bf16[208,256]{1,0:T(8,128)(2,1)S(1)}, bf16[208,256]{1,0:T(8,128)(2,1)S(1)}, u32[]{:S(2)}, u32[]{:S(2)}) collective-permute-start(bf16[208,256]{1,0:T(8,128)(2,1)S(1)} %get-tuple-element.54), channel_id=1, source_target_pairs={{0,24},{8,16},{16,8},{24,0},{1,25},{9,17},{17,9},{25,1},{2,26},{10... | collective-permute-start | bytes 319496 | tf_op jit(solution)/shard_map/ppermute | solution.py:387
  29.3 3.4 %collective-permute-start.5 = (bf16[512,768]{1,0:T(8,128)(2,1)S(1)}, bf16[512,768]{1,0:T(8,128)(2,1)S(1)}, u32[]{:S(2)}, u32[]{:S(2)}) collective-permute-start(bf16[512,768]{1,0:T(8,128)(2,1)S(1)} %get-tuple-element.61), channel_id=1, source_target_pairs={{0,1},{1,0},{2,3},{3,2},{4,5},{5,4},{6,7},{7,6},{8,9},{9,8},{10,11... | collective-permute-start | bytes 2359304 | tf_op jit(solution)/shard_map/ppermute | solution.py:316
  32.1 2.5 %collective-permute-start.6 = (bf16[512,768]{1,0:T(8,128)(2,1)S(1)}, bf16[512,768]{1,0:T(8,128)(2,1)S(1)}, u32[]{:S(2)}, u32[]{:S(2)}) collective-permute-start(bf16[512,768]{1,0:T(8,128)(2,1)S(1)} %get-tuple-element.69), channel_id=1, source_target_pairs={{0,1},{1,0},{2,3},{3,2},{4,5},{5,4},{6,7},{7,6},{8,9},{9,8},{10,11... | collective-permute-start | bytes 2359304 | tf_op jit(solution)/shard_map/ppermute | solution.py:316
  32.7 3.0 %collective-permute-start.7 = (bf16[512,768]{1,0:T(8,128)(2,1)S(1)}, bf16[512,768]{1,0:T(8,128)(2,1)S(1)}, u32[]{:S(2)}, u32[]{:S(2)}) collective-permute-start(bf16[512,768]{1,0:T(8,128)(2,1)S(1)} %get-tuple-element.71), channel_id=1, source_target_pairs={{0,1},{1,0},{2,3},{3,2},{4,5},{5,4},{6,7},{7,6},{8,9},{9,8},{10,11... | collective-permute-start | bytes 2359304 | tf_op jit(solution)/shard_map/ppermute | solution.py:316
  35.9 14.5 %collective-permute-start.8 = (bf16[256,768]{1,0:T(8,128)(2,1)S(1)}, bf16[256,768]{1,0:T(8,128)(2,1)S(1)}, u32[]{:S(2)}, u32[]{:S(2)}) collective-permute-start(bf16[256,768]{1,0:T(8,128)(2,1)S(1)} %add_convert_fusion.2), channel_id=1, source_target_pairs={{0,2},{1,3},{2,0},{3,1},{4,6},{5,7},{6,4},{7,5},{8,10},{9,11},{10,... | collective-permute-start | bytes 1179656 | tf_op jit(solution)/shard_map/ppermute | solution.py:316
  36.4 14.0 %collective-permute-start.9 = (bf16[256,768]{1,0:T(8,128)(2,1)S(1)}, bf16[256,768]{1,0:T(8,128)(2,1)S(1)}, u32[]{:S(2)}, u32[]{:S(2)}) collective-permute-start(bf16[256,768]{1,0:T(8,128)(2,1)S(1)} %get-tuple-element.81), channel_id=1, source_target_pairs={{0,4},{1,5},{2,6},{3,7},{4,0},{5,1},{6,2},{7,3},{8,12},{9,13},{10,... | collective-permute-start | bytes 1179656 | tf_op jit(solution)/shard_map/ppermute | solution.py:316
  38.3 12.0 %collective-permute-start.10 = (bf16[256,768]{1,0:T(8,128)(2,1)S(1)}, bf16[256,768]{1,0:T(8,128)(2,1)S(1)}, u32[]{:S(2)}, u32[]{:S(2)}) collective-permute-start(bf16[256,768]{1,0:T(8,128)(2,1)S(1)} %get-tuple-element.82), channel_id=1, source_target_pairs={{0,8},{8,0},{16,24},{24,16},{1,9},{9,1},{17,25},{25,17},{2,10},{10... | collective-permute-start | bytes 1179656 | tf_op jit(solution)/shard_map/ppermute | solution.py:316
  41.7 1.4 %collective-permute-start.11 = (bf16[64,1024]{1,0:T(8,128)(2,1)S(1)}, bf16[64,1024]{1,0:T(8,128)(2,1)S(1)}, u32[]{:S(2)}, u32[]{:S(2)}) collective-permute-start(bf16[64,1024]{1,0:T(8,128)(2,1)S(1)} %get-tuple-element.83), channel_id=1, source_target_pairs={{0,1},{1,0},{2,3},{3,2},{4,5},{5,4},{6,7},{7,6},{8,9},{9,8},{10,11... | collective-permute-start | bytes 393224 | tf_op jit(solution)/shard_map/ppermute | solution.py:430
  41.8 8.6 %collective-permute-start.12 = (bf16[64,1024]{1,0:T(8,128)(2,1)S(1)}, bf16[64,1024]{1,0:T(8,128)(2,1)S(1)}, u32[]{:S(2)}, u32[]{:S(2)}) collective-permute-start(bf16[64,1024]{1,0:T(8,128)(2,1)S(1)} %get-tuple-element.84), channel_id=1, source_target_pairs={{0,7},{1,2},{2,1},{3,4},{4,3},{5,6},{6,5},{7,0},{8,15},{9,10},{10,... | collective-permute-start | bytes 393224 | tf_op jit(solution)/shard_map/ppermute | solution.py:431
  50.5 6.8 %collective-permute-start.17 = (bf16[128,768]{1,0:T(8,128)(2,1)S(1)}, bf16[128,768]{1,0:T(8,128)(2,1)S(1)}, u32[]{:S(2)}, u32[]{:S(2)}) collective-permute-start(bf16[128,768]{1,0:T(8,128)(2,1)S(1)} %add_convert_fusion.3), channel_id=1, source_target_pairs={{0,2},{1,3},{2,0},{3,1},{4,6},{5,7},{6,4},{7,5},{8,10},{9,11},{10,... | collective-permute-start | bytes 589832 | tf_op jit(solution)/shard_map/ppermute | solution.py:316
  50.6 7.9 %collective-permute-start.15 = (bf16[128,768]{1,0:T(8,128)(2,1)S(1)}, bf16[128,768]{1,0:T(8,128)(2,1)S(1)}, u32[]{:S(2)}, u32[]{:S(2)}) collective-permute-start(bf16[128,768]{1,0:T(8,128)(2,1)S(1)} %add_convert_fusion.4), channel_id=1, source_target_pairs={{0,8},{8,0},{16,24},{24,16},{1,9},{9,1},{17,25},{25,17},{2,10},{10... | collective-permute-start | bytes 589832 | tf_op jit(solution)/shard_map/ppermute | solution.py:316
  52.5 7.7 %collective-permute-start.13 = (bf16[128,768]{1,0:T(8,128)(2,1)S(1)}, bf16[128,768]{1,0:T(8,128)(2,1)S(1)}, u32[]{:S(2)}, u32[]{:S(2)}) collective-permute-start(bf16[128,768]{1,0:T(8,128)(2,1)S(1)} %add_convert_fusion.5), channel_id=1, source_target_pairs={{0,4},{1,5},{2,6},{3,7},{4,0},{5,1},{6,2},{7,3},{8,12},{9,13},{10,... | collective-permute-start | bytes 589832 | tf_op jit(solution)/shard_map/ppermute | solution.py:316
  57.4 5.0 %collective-permute-start.18 = (bf16[64,768]{1,0:T(8,128)(2,1)S(1)}, bf16[64,768]{1,0:T(8,128)(2,1)S(1)}, u32[]{:S(2)}, u32[]{:S(2)}) collective-permute-start(bf16[64,768]{1,0:T(8,128)(2,1)S(1)} %add_convert_fusion.6), channel_id=1, source_target_pairs={{0,4},{1,5},{2,6},{3,7},{4,0},{5,1},{6,2},{7,3},{8,12},{9,13},{10,... | collective-permute-start | bytes 294920 | tf_op jit(solution)/shard_map/ppermute | solution.py:316
  58.5 4.9 %collective-permute-start.16 = (bf16[64,768]{1,0:T(8,128)(2,1)S(1)}, bf16[64,768]{1,0:T(8,128)(2,1)S(1)}, u32[]{:S(2)}, u32[]{:S(2)}) collective-permute-start(bf16[64,768]{1,0:T(8,128)(2,1)S(1)} %add_convert_fusion.7), channel_id=1, source_target_pairs={{0,2},{1,3},{2,0},{3,1},{4,6},{5,7},{6,4},{7,5},{8,10},{9,11},{10,... | collective-permute-start | bytes 294920 | tf_op jit(solution)/shard_map/ppermute | solution.py:316
  60.2 4.9 %collective-permute-start.14 = (bf16[64,768]{1,0:T(8,128)(2,1)S(1)}, bf16[64,768]{1,0:T(8,128)(2,1)S(1)}, u32[]{:S(2)}, u32[]{:S(2)}) collective-permute-start(bf16[64,768]{1,0:T(8,128)(2,1)S(1)} %add_convert_fusion.8), channel_id=1, source_target_pairs={{0,8},{8,0},{16,24},{24,16},{1,9},{9,1},{17,25},{25,17},{2,10},{10... | collective-permute-start | bytes 294920 | tf_op jit(solution)/shard_map/ppermute | solution.py:316
  65.2 9.0 %collective-permute-start.19 = (bf16[32,2304]{1,0:T(8,128)(2,1)S(1)}, bf16[32,2304]{1,0:T(8,128)(2,1)S(1)}, u32[]{:S(2)}, u32[]{:S(2)}) collective-permute-start(bf16[32,2304]{1,0:T(8,128)(2,1)S(1)} %slice.262), channel_id=1, source_target_pairs={{0,16},{8,24},{16,0},{24,8},{1,17},{9,25},{17,1},{25,9},{2,18},{10... | collective-permute-start | bytes 442376 | tf_op jit(solution)/shard_map/ppermute | solution.py:316

commit v7 on v6

--- a/solution.py
+++ b/solution.py
@@ -97,20 +97,26 @@
 
 
 def forward_body(
-    send_rows,
-    mate_ref, other_ref, own_ref, kvw_ref, q_ref, src_ref, p_ref,
-    kv_ref, gate_ref, slope_ref, merged_ref, part_ref, send_ref,
+    send_rows, mate_ref, other_ref, own_ref, kvw_ref, q_ref, src_ref, p_ref,
+    value_ref, gate_ref, slope_ref, merged_ref, part_ref, send_ref,
 ):
-    members, ext, width2 = kv_ref.shape
-    width = width2 // 2
+    members, ext, width = value_ref.shape
     points = q_ref.shape[0]
     nodes = own_ref.shape[0] // members
     rim = mate_ref.shape[0] // members
-    halo = mm(jnp.concatenate([mate_ref[...], other_ref[...]], axis=0), kvw_ref[...]).astype(BF)
-    for m in range(members):
-        kv_ref[m, 0:nodes, :] = own_ref[m * nodes : (m + 1) * nodes, :]
-        kv_ref[m, nodes : nodes + rim, :] = halo[m * rim : (m + 1) * rim]
-        kv_ref[m, nodes + rim : ext, :] = halo[(members + m) * rim : (members + m + 1) * rim]
+    step = 2 * LANES
+    halo_rows = jnp.concatenate([mate_ref[...], other_ref[...]], axis=0)
+
+    def project(start):
+        halo = mm(halo_rows, kvw_ref[:, start : start + step]).astype(BF)
+        result = []
+        for m in range(members):
+            own = own_ref[m * nodes : (m + 1) * nodes, start : start + step]
+            mate = halo[m * rim : (m + 1) * rim]
+            other = halo[(members + m) * rim : (members + m + 1) * rim]
+            result.append(jnp.concatenate([own, mate, other], axis=0))
+        return result
+
     rows = lax.broadcasted_iota(jnp.int32, (ext, points), 0)
     src = src_ref[...]
     even = lax.axis_index("band") % 2 == 0
@@ -119,19 +125,46 @@
     mask = rows == src[0:1, :]
     for e in range(1, src.shape[0]):
         mask = mask | (rows == src[e : e + 1, :])
-    mask = mask.astype(F32)
-    mask = jnp.concatenate([mask, mask], axis=0)
-    scale = HEAD_DIM ** (-0.5)
-    for pair in range(width // LANES):
-        cols = slice(pair * LANES, (pair + 1) * LANES)
-        vcols = slice(width + pair * LANES, width + (pair + 1) * LANES)
-        q = q_ref[:, cols]
-        for m in range(members):
-            th = jnp.tanh(mm(split_heads(kv_ref[m, :, cols]), q, NT) * (0.5 * scale))
-            gate = ((0.5 * th + 0.5) * mask).astype(BF)
-            gate_ref[pair, m] = gate
-            slope_ref[pair, m] = ((0.25 * scale) * mask * (1.0 - th * th)).astype(BF)
-            merged_ref[m, cols, :] = mm(split_heads(kv_ref[m, :, vcols]), gate, TN).astype(BF)
+    half_mask = jnp.where(mask, 0.5, 0.0).astype(F32)
+    half_mask = jnp.concatenate([half_mask, half_mask], axis=0)
+    half_scale = 0.5 * HEAD_DIM ** (-0.5)
+    low_rows = lax.broadcasted_iota(jnp.int32, (LANES, ext), 0) < HEAD_DIM
+
+    keys, values = {}, {}
+
+    def prepare(block):
+        start = block * step
+        for m, rows in enumerate(project(start)):
+            keys[block, m] = rows
+        for m, rows in enumerate(project(width + start)):
+            values[block, m] = rows
+            value_ref[m, :, start : start + step] = rows
+
+    def scores(pair, m):
+        block, at = pair * LANES // step, pair * LANES % step
+        q = (q_ref[:, pair * LANES : (pair + 1) * LANES].astype(F32) * half_scale).astype(BF)
+        return mm(split_heads(keys[block, m][:, at : at + LANES]), q, NT)
+
+    tasks = [(pair, m) for pair in range(width // LANES) for m in range(members)]
+    prepare(0)
+    ahead = scores(*tasks[0])
+    for i, (pair, m) in enumerate(tasks):
+        block, at = pair * LANES // step, pair * LANES % step
+        current = ahead
+        if at == 0 and m == 0 and (block + 1) * step < width:
+            prepare(block + 1)
+        if i + 1 < len(tasks):
+            ahead = scores(*tasks[i + 1])
+        value_t = values[block, m][:, at : at + LANES].astype(F32).T
+        zero = jnp.zeros_like(value_t)
+        value_t = jnp.concatenate(
+            [jnp.where(low_rows, value_t, zero), jnp.where(low_rows, zero, value_t)], axis=1
+        ).astype(BF)
+        gate = jnp.tanh(current) * half_mask + half_mask
+        rounded = gate.astype(BF)
+        gate_ref[pair, m] = rounded
+        slope_ref[pair, m] = (gate - gate * gate).astype(BF)
+        merged_ref[m, pair * LANES : (pair + 1) * LANES, :] = mm(value_t, rounded).astype(BF)
     sent = []
     for m in range(members):
         part = mm(p_ref[...], merged_ref[m])
@@ -243,36 +276,36 @@
 
 
 def key_body(
-    n_member, n_band, grad_ref, dm_ref, kv_ref, slope_ref, q_ref, merged_ref, wo_ref, ext_ref, ngv_ref,
+    n_member, n_band, width1, grad_ref, dm_ref, value_ref, slope_ref, q_ref, merged_ref, wo_ref, ext_ref, ngv_ref,
     ng_ref, *refs
 ):
     out_refs, turned = refs[:-1], refs[-1]
-    members, ext, width2 = kv_ref.shape
-    width = width2 // 2
-    group_width = out_refs[0].shape[1]
+    members, ext, width = value_ref.shape
+    scale = HEAD_DIM ** (-0.5)
     for pair in range(width // LANES):
         cols = slice(pair * LANES, (pair + 1) * LANES)
-        vcols = slice(width + pair * LANES, width + (pair + 1) * LANES)
         for m in range(members):
-            dgate = mm(split_heads(kv_ref[m, :, vcols]), dm_ref[m, cols, :])
+            dgate = mm(split_heads(value_ref[m, :, cols]), dm_ref[m, cols, :])
             dscore = (dgate * slope_ref[pair, m].astype(F32)).astype(BF)
-            ng_ref[m * ext : (m + 1) * ext, cols] = select_heads(mm(dscore, q_ref[:, cols])).astype(BF)
+            keys = select_heads(mm(dscore, q_ref[:, cols])) * scale
+            ng_ref[m * ext : (m + 1) * ext, cols] = keys.astype(BF)
     m_t = sum(mm(grad_ref[m], merged_ref[m], NT) for m in range(members))
     head_t = sum(mm(grad_ref[m], q_ref[...]) for m in range(members)) + mm(m_t.astype(BF), wo_ref[...])
     turned[...] = jnp.concatenate([m_t, head_t], axis=0).T
-    pieces = [(ngv_ref, group_width, width), (ng_ref, 0, width), (None, 0, 2 * LANES)]
-    at = group_width
+    pieces = [(ngv_ref, width1, width), (ng_ref, 0, width), (None, 0, 2 * LANES)]
+    group, offset = 0, 0
     for ref, first, last in pieces:
         while first < last:
-            group, offset = at // group_width, at % group_width
-            take = min(last - first, group_width - offset)
+            outs = out_refs[2 * group : 2 * group + 2]
+            take = min(last - first, outs[0].shape[1] - offset)
             if ref is None:
                 rows = reorder(turned, n_member, n_band)
             else:
                 rows = mm(ext_ref[...], ref[:, first : first + take])
-            outs = out_refs[2 * (group - 1) : 2 * group]
-            store_group(rows, group, n_member, n_band, offset, outs)
-            first, at = first + take, at + take
+            store_group(rows, group + 1, n_member, n_band, offset, outs)
+            first, offset = first + take, offset + take
+            if offset == outs[0].shape[1]:
+                group, offset = group + 1, 0
 
 
 def extended_grad_body(members, nodes, rim, ngk_ref, ngv_ref, kvw_ref, own_ref, mate_ref, other_ref):
@@ -340,7 +373,8 @@
     chips = n_band // 2
     send_rows = -(-channels // 8) * 8
     mates = [(i, i ^ 1) for i in range(n_band)]
-    others = [(i, (i + 1 if i % 2 else i - 1) % n_band) for i in range(n_band)]
+    others = [(0, 0), (n_band - 1, n_band - 1)]
+    others += [(i, i + 1 if i % 2 else i - 1) for i in range(1, n_band - 1)]
 
     own_hidden, halo, for_mate, for_other = call(
         pick_body,
@@ -370,10 +404,10 @@
         [pltpu.VMEM((8, LANES), F32), pltpu.VMEM((LANES, width), F32)],
     )
 
-    kv, gates, slopes, merged, part, sent = call(
+    value, gates, slopes, merged, part, sent = call(
         functools.partial(forward_body, send_rows),
         [
-            sds((members, ext, 2 * width), BF),
+            sds((members, ext, width), BF),
             sds((pairs, members, 2 * ext, points), BF),
             sds((pairs, members, 2 * ext, points), BF),
             sds((members, width, points), BF),
@@ -395,18 +429,20 @@
     )
 
     extra = 2 * LANES
-    group_width = (2 * width + extra) // GROUPS
+    third = (2 * width + extra) // LANES // GROUPS
+    widths = [(third - 1) * LANES, third * LANES]
+    widths.append(2 * width + extra - sum(widths))
     grad, dm, ng_value, send, keep = call(
         functools.partial(value_body, n_member, n_band),
         [sds((members, LANES, points), BF), sds((members, width, points), BF), sds((members * ext, width), BF)]
-        + [sds((width // 2, group_width), BF)] * 2,
+        + [sds((width // 2, widths[0]), BF)] * 2,
         (*received, part, base, truth, weight, pt, gates, ext_t),
     )
     groups = [[keep, swap(send, "band", 0, n_band)]]
     ng_key, *outs = call(
-        functools.partial(key_body, n_member, n_band),
-        [sds((members * ext, width), BF)] + [sds((width // 2, group_width), BF)] * (2 * (GROUPS - 1)),
-        (grad, dm, kv, slopes, queries, merged, out_weight, ext_t, ng_value),
+        functools.partial(key_body, n_member, n_band, widths[0]),
+        [sds((members * ext, width), BF)] + [sds((width // 2, w), BF) for w in widths[1:] for _ in range(2)],
+        (grad, dm, value, slopes, queries, merged, out_weight, ext_t, ng_value),
         [pltpu.VMEM((width, extra), F32)],
     )
     for i in range(GROUPS - 1):

time: 75.2 us -> 74.4 us (0.989)
  Pallas kernels: 15.8 us -> 14 us
  starting transfers between devices: 23.5 us -> 25.2 us
  waiting for transfers between devices: 33.9 us -> 32.8 us
    ppermute x13, waiting for transfers between devices: 16.4 us -> 24.6 us  [swap(): return lax.ppermute(rows, axis, [(i, i ^ 1 << bit) for i in range(count)])]
    ppermute x1, waiting for transfers between devices: 7.27 us -> 0.01 us  [shards(): from_other = lax.ppermute(back_other, 'band', others)]
    ppermute x13, starting transfers between devices: 13.8 us -> 17.4 us  [swap(): return lax.ppermute(rows, axis, [(i, i ^ 1 << bit) for i in range(count)])]
    ppermute x1, starting transfers between devices: 3.56 us -> 0.79 us  [shards(): other = lax.ppermute(for_other, 'band', others)]
    pallas_call x9, Pallas kernels: 15.8 us -> 14 us  [call(): pl.pallas_call(body, out_shape=out_shape, in_specs=[pl.BlockSpec(memory_s...]
    ppermute x1, waiting for transfers between devices: 1.65 us -> 0.01 us  [shards(): other = lax.ppermute(for_other, 'band', others)]
    ppermute x3, starting transfers between devices: 4.58 us -> 5.68 us  [shards(): lax.ppermute(sent, 'member', [(i, i ^ s) for i in range(n_member)])]
    ppermute x3, waiting for transfers between devices: 8.32 us -> 7.47 us  [shards(): lax.ppermute(sent, 'member', [(i, i ^ s) for i in range(n_member)])]
  transfers between devices with their start and end apart: 20 -> 20, of which waited for: 13 -> 12; matrix products, arithmetic and copies ran while one was open for 1% -> 1% of each run, Pallas kernels for 9% -> 6%
where the time goes in v7:
time: 74.4 us; the launch traced here: 74.2 us
  waiting for transfers between devices  32.8 us (44%)
  starting transfers between devices  25.2 us (34%)
  Pallas kernels  14 us (19%)
  between operations  0.93 us (1%)
  other arithmetic  0.91 us (1%)
    ppermute x13, waiting for transfers between devices, swap(): return lax.ppermute(rows, axis, [(i, i ^ 1 << bit) for i in range(count)])  24.6 us
    ppermute x13, starting transfers between devices, swap(): return lax.ppermute(rows, axis, [(i, i ^ 1 << bit) for i in range(count)])  17.4 us
    pallas_call x9, Pallas kernels, call(): pl.pallas_call(body, out_shape=out_shape, in_specs=[pl.BlockSpec(memory_s...  14 us
    ppermute x3, waiting for transfers between devices, shards(): lax.ppermute(sent, 'member', [(i, i ^ s) for i in range(n_member)])  7.47 us
    ppermute x3, starting transfers between devices, shards(): lax.ppermute(sent, 'member', [(i, i ^ s) for i in range(n_member)])  5.68 us
  transfers between devices with their start and end apart: 20, of which 12 were waited for; matrix products, arithmetic and copies ran while one was open for 1% of the time, Pallas kernels for 6%

profile of v7, /device:TPU:0, one launch (start us, length us, event | category | flops | bytes accessed | tf_op | source)
XLA Modules:
  0.0 74.2 jit_solution(14535443667513179219)
XLA Ops:
  0.7 1.4 %shard_map.138 = (bf16[2,64,1024]{2,1,0:T(8,128)(2,1)S(1)}, s32[2,32]{1,0:T(2,128)S(1)}, bf16[64,1024]{1,0:T(8,128)(2,1)S(1)}, bf16[64,1024]{1,0:T(8,128)(2,1)S(1)}) custom-call(bf16[2,64,1024]{2,1,0:T(8,128)(2,1)} %hidden_hbm.1, s32[2,32]{1,0:T(2,128)} %halo_hbm.1), custom_call_target="tpu_custom_call" | custom-call | flops 10000000000 | bytes 1 | tf_op jit(solution)/shard_map/pallas_call | solution.py:28
  2.1 0.5 collective-permute-start
  2.6 0.8 %collective-permute-start.1 = (bf16[64,1024]{1,0:T(8,128)(2,1)S(1)}, bf16[64,1024]{1,0:T(8,128)(2,1)S(1)}, u32[]{:S(2)}, u32[]{:S(2)}) collective-permute-start(bf16[64,1024]{1,0:T(8,128)(2,1)S(1)} %get-tuple-element.50), channel_id=1, source_target_pairs={{0,0},{7,7},{1,2},{2,1},{3,4},{4,3},{5,6},{6,5},{8,8},{15,15},{9,1... | collective-permute-start | bytes 393224 | tf_op jit(solution)/shard_map/ppermute | solution.py:388
  3.5 0.4 copy-done
  3.9 1.5 %shard_map.139 = (bf16[128,2048]{1,0:T(8,128)(2,1)S(1)}, bf16[1024,128]{1,0:T(8,128)(2,1)S(1)}, bf16[128,1024]{1,0:T(8,128)(2,1)S(1)}, f32[128,256]{1,0:T(8,128)S(1)}, f32[100,256]{1,0:T(8,128)S(1)}) custom-call(bf16[2,64,1024]{2,1,0:T(8,128)(2,1)S(1)} %get-tuple-element.51.hidden_ref, bf16[1024,1024]{1,0:T(8,128)(2,1)S(1)} %copy-done.1, ...), custom_call_target="tpu_custom_call" | custom-call | flops 1 | bytes 1 | tf_op jit(solution)/shard_map/pallas_call | solution.py:28
  5.4 2.9 %shard_map.140 = (bf16[2,128,1024]{2,1,0:T(8,128)(2,1)S(1)}, bf16[8,2,256,256]{3,2,1,0:T(8,128)(2,1)S(1)}, bf16[8,2,256,256]{3,2,1,0:T(8,128)(2,1)S(1)}, bf16[2,...) custom-call(bf16[64,1024]{1,0:T(8,128)(2,1)S(1)} %collective-permute-done.mate_ref, ...), custom_call_target="tpu_custom_call" | custom-call | flops 1 | bytes 1 | tf_op jit(solution)/shard_map/pallas_call | solution.py:28
  8.3 3.1 %collective-permute-start.4 = (bf16[208,256]{1,0:T(8,128)(2,1)S(1)}, bf16[208,256]{1,0:T(8,128)(2,1)S(1)}, u32[]{:S(2)}, u32[]{:S(2)}) collective-permute-start(bf16[208,256]{1,0:T(8,128)(2,1)S(1)} %get-tuple-element.54), channel_id=1, source_target_pairs={{0,8},{8,0},{16,24},{24,16},{1,9},{9,1},{17,25},{25,17},{2,10},{10... | collective-permute-start | bytes 319496 | tf_op jit(solution)/shard_map/ppermute | solution.py:421
  11.4 2.6 %collective-permute-start.3 = (bf16[208,256]{1,0:T(8,128)(2,1)S(1)}, bf16[208,256]{1,0:T(8,128)(2,1)S(1)}, u32[]{:S(2)}, u32[]{:S(2)}) collective-permute-start(bf16[208,256]{1,0:T(8,128)(2,1)S(1)} %get-tuple-element.54), channel_id=1, source_target_pairs={{0,16},{8,24},{16,0},{24,8},{1,17},{9,25},{17,1},{25,9},{2,18},{10... | collective-permute-start | bytes 319496 | tf_op jit(solution)/shard_map/ppermute | solution.py:421
  14.0 0.3 shard_map.141.refs_9_.ext_ref
  14.3 4.0 %collective-permute-done.3.refs_1_ = bf16[208,256]{1,0:T(8,128)(2,1)S(1)} collective-permute-done((bf16[208,256]{1,0:T(8,128)(2,1)S(1)}, bf16[208,256]{1,0:T(8,128)(2,1)S(1)}, u32[]{:S(2)}, u32[]{:S(2)}) %collective-permute-start.3) | collective-permute-done | bytes 106528 | tf_op jit(solution)/shard_map/ppermute | solution.py:421
  18.2 3.5 %collective-permute-done.2.refs_0_ = bf16[208,256]{1,0:T(8,128)(2,1)S(1)} collective-permute-done((bf16[208,256]{1,0:T(8,128)(2,1)S(1)}, bf16[208,256]{1,0:T(8,128)(2,1)S(1)}, u32[]{:S(2)}, u32[]{:S(2)}) %collective-permute-start.2) | collective-permute-done | bytes 106528 | tf_op jit(solution)/shard_map/ppermute | solution.py:421
  21.7 1.8 %shard_map.142 = (bf16[2,128,256]{2,1,0:T(8,128)(2,1)S(1)}, bf16[2,1024,256]{2,1,0:T(8,128)(2,1)S(1)}, bf16[256,1024]{1,0:T(8,128)(2,1)S(1)}, bf16[512,640]{1,0:T(8,128)(2,1)S(1)}, bf16[512,640]{1,0:T(8,128)(2,1)S(1)}) custom-call(bf16[208,256]{1,0:T(8,128)(2,1)S(1)} %collective-permute-done.2.refs_0_, bf16[208,256]{1,0:T(8,128)(2,1)S(1)} %collective-permute-done.3.refs_1_, ...), custom_call_target="tpu_custom_call" | custom-call | flops 1 | bytes 1 | tf_op jit(solution)/shard_map/pallas_call | solution.py:28
  23.5 3.0 %shard_map.143 = (bf16[256,1024]{1,0:T(8,128)(2,1)S(1)}, bf16[512,768]{1,0:T(8,128)(2,1)S(1)}, bf16[512,768]{1,0:T(8,128)(2,1)S(1)}, bf16[512,896]{1,0:T(8,128)(2,1)S(1)}, bf16[512,896]{1,0:T(8,128)(2,1)S(1)}) custom-call(bf16[2,128,256]{2,1,0:T(8,128)(2,1)S(1)} %get-tuple-element.62.grad_ref, bf16[2,1024,256]{2,1,0:T(8,128)(2,1)S(1)} %get-tuple-element.63.dm_ref, ...), custom_call_target="tpu_custom_call" | custom-call | flops 1 | bytes 1 | tf_op jit(solution)/shard_map/pallas_call | solution.py:28
  26.5 2.0 %collective-permute-start.7 = (bf16[512,896]{1,0:T(8,128)(2,1)S(1)}, bf16[512,896]{1,0:T(8,128)(2,1)S(1)}, u32[]{:S(2)}, u32[]{:S(2)}) collective-permute-start(bf16[512,896]{1,0:T(8,128)(2,1)S(1)} %get-tuple-element.71), channel_id=1, source_target_pairs={{0,1},{1,0},{2,3},{3,2},{4,5},{5,4},{6,7},{7,6},{8,9},{9,8},{10,11... | collective-permute-start | bytes 2752520 | tf_op jit(solution)/shard_map/ppermute | solution.py:349
  28.5 0.1 collective-permute-start.5
  28.6 0.4 collective-permute-start.6
  29.0 2.5 %collective-permute-done.5 = bf16[512,640]{1,0:T(8,128)(2,1)S(1)} collective-permute-done((bf16[512,640]{1,0:T(8,128)(2,1)S(1)}, bf16[512,640]{1,0:T(8,128)(2,1)S(1)}, u32[]{:S(2)}, u32[]{:S(2)}) %collective-permute-start.5) | collective-permute-done | bytes 655392 | tf_op jit(solution)/shard_map/ppermute | solution.py:349
  31.6 0.1 add_convert_fusion.2
  31.6 1.0 %collective-permute-done.6 = bf16[512,768]{1,0:T(8,128)(2,1)S(1)} collective-permute-done((bf16[512,768]{1,0:T(8,128)(2,1)S(1)}, bf16[512,768]{1,0:T(8,128)(2,1)S(1)}, u32[]{:S(2)}, u32[]{:S(2)}) %collective-permute-start.6) | collective-permute-done | bytes 786464 | tf_op jit(solution)/shard_map/ppermute | solution.py:349
  32.7 0.1 add_convert_fusion.1
  32.8 0.1 add_convert_fusion
  32.9 1.8 %collective-permute-start.10 = (bf16[256,896]{1,0:T(8,128)(2,1)S(1)}, bf16[256,896]{1,0:T(8,128)(2,1)S(1)}, u32[]{:S(2)}, u32[]{:S(2)}) collective-permute-start(bf16[256,896]{1,0:T(8,128)(2,1)S(1)} %add_convert_fusion), channel_id=1, source_target_pairs={{0,8},{8,0},{16,24},{24,16},{1,9},{9,1},{17,25},{25,17},{2,10},{10... | collective-permute-start | bytes 1376264 | tf_op jit(solution)/shard_map/ppermute | solution.py:349
  34.7 4.6 %collective-permute-start.9 = (bf16[256,768]{1,0:T(8,128)(2,1)S(1)}, bf16[256,768]{1,0:T(8,128)(2,1)S(1)}, u32[]{:S(2)}, u32[]{:S(2)}) collective-permute-start(bf16[256,768]{1,0:T(8,128)(2,1)S(1)} %add_convert_fusion.1), channel_id=1, source_target_pairs={{0,4},{1,5},{2,6},{3,7},{4,0},{5,1},{6,2},{7,3},{8,12},{9,13},{10,... | collective-permute-start | bytes 1179656 | tf_op jit(solution)/shard_map/ppermute | solution.py:349
  39.3 1.3 %shard_map.144 = (f32[2,64,1024]{2,1,0:T(8,128)S(1)}, bf16[64,1024]{1,0:T(8,128)(2,1)S(1)}, bf16[64,1024]{1,0:T(8,128)(2,1)S(1)}) custom-call(bf16[256,1024]{1,0:T(8,128)(2,1)S(1)} %get-tuple-element.78.ngk_ref, bf16[256,1024]{1,0:T(8,128)(2,1)S(1)} %get-tuple-element.67.ngv_ref, bf16[1024,2048]{1,0:T(8,128)(2,1)S(1)} %copy-done), custom_call_target="tpu_custom_call" | custom-call | flops 1 | bytes 1 | tf_op jit(solution)/shard_map/pallas_call | solution.py:28
  40.6 0.1 collective-permute-start.11
  40.7 0.7 collective-permute-start.12
  41.4 0.7 collective-permute-done.11.from_mate_ref
  42.0 7.9 %collective-permute-done.8 = bf16[256,640]{1,0:T(8,128)(2,1)S(1)} collective-permute-done((bf16[256,640]{1,0:T(8,128)(2,1)S(1)}, bf16[256,640]{1,0:T(8,128)(2,1)S(1)}, u32[]{:S(2)}, u32[]{:S(2)}) %collective-permute-start.8) | collective-permute-done | bytes 327712 | tf_op jit(solution)/shard_map/ppermute | solution.py:349
  49.9 0.1 add_convert_fusion.5
  50.0 1.7 %collective-permute-start.13 = (bf16[128,640]{1,0:T(8,128)(2,1)S(1)}, bf16[128,640]{1,0:T(8,128)(2,1)S(1)}, u32[]{:S(2)}, u32[]{:S(2)}) collective-permute-start(bf16[128,640]{1,0:T(8,128)(2,1)S(1)} %add_convert_fusion.5), channel_id=1, source_target_pairs={{0,4},{1,5},{2,6},{3,7},{4,0},{5,1},{6,2},{7,3},{8,12},{9,13},{10,... | collective-permute-start | bytes 491528 | tf_op jit(solution)/shard_map/ppermute | solution.py:349
  51.7 0.1 add_convert_fusion.4
  51.8 0.4 collective-permute-start.15
  52.2 0.1 add_convert_fusion.3
  52.3 1.2 %collective-permute-start.17 = (bf16[128,896]{1,0:T(8,128)(2,1)S(1)}, bf16[128,896]{1,0:T(8,128)(2,1)S(1)}, u32[]{:S(2)}, u32[]{:S(2)}) collective-permute-start(bf16[128,896]{1,0:T(8,128)(2,1)S(1)} %add_convert_fusion.3), channel_id=1, source_target_pairs={{0,2},{1,3},{2,0},{3,1},{4,6},{5,7},{6,4},{7,5},{8,10},{9,11},{10,... | collective-permute-start | bytes 688136 | tf_op jit(solution)/shard_map/ppermute | solution.py:349
  53.5 3.4 %collective-permute-done.13 = bf16[128,640]{1,0:T(8,128)(2,1)S(1)} collective-permute-done((bf16[128,640]{1,0:T(8,128)(2,1)S(1)}, bf16[128,640]{1,0:T(8,128)(2,1)S(1)}, u32[]{:S(2)}, u32[]{:S(2)}) %collective-permute-start.13) | collective-permute-done | bytes 163872 | tf_op jit(solution)/shard_map/ppermute | solution.py:349
  56.9 0.4 collective-permute-start.14
  57.4 0.9 %collective-permute-done.15 = bf16[128,768]{1,0:T(8,128)(2,1)S(1)} collective-permute-done((bf16[128,768]{1,0:T(8,128)(2,1)S(1)}, bf16[128,768]{1,0:T(8,128)(2,1)S(1)}, u32[]{:S(2)}, u32[]{:S(2)}) %collective-permute-start.15) | collective-permute-done | bytes 196640 | tf_op jit(solution)/shard_map/ppermute | solution.py:349
  58.3 1.8 %collective-permute-start.16 = (bf16[64,768]{1,0:T(8,128)(2,1)S(1)}, bf16[64,768]{1,0:T(8,128)(2,1)S(1)}, u32[]{:S(2)}, u32[]{:S(2)}) collective-permute-start(bf16[64,768]{1,0:T(8,128)(2,1)S(1)} %add_convert_fusion.7), channel_id=1, source_target_pairs={{0,2},{1,3},{2,0},{3,1},{4,6},{5,7},{6,4},{7,5},{8,10},{9,11},{10,... | collective-permute-start | bytes 294920 | tf_op jit(solution)/shard_map/ppermute | solution.py:349
  60.1 0.9 %collective-permute-start.18 = (bf16[64,896]{1,0:T(8,128)(2,1)S(1)}, bf16[64,896]{1,0:T(8,128)(2,1)S(1)}, u32[]{:S(2)}, u32[]{:S(2)}) collective-permute-start(bf16[64,896]{1,0:T(8,128)(2,1)S(1)} %add_convert_fusion.6), channel_id=1, source_target_pairs={{0,4},{1,5},{2,6},{3,7},{4,0},{5,1},{6,2},{7,3},{8,12},{9,13},{10,... | collective-permute-start | bytes 344072 | tf_op jit(solution)/shard_map/ppermute | solution.py:349
  61.0 0.7 collective-permute-done.14
  61.8 1.2 %collective-permute-done.16 = bf16[64,768]{1,0:T(8,128)(2,1)S(1)} collective-permute-done((bf16[64,768]{1,0:T(8,128)(2,1)S(1)}, bf16[64,768]{1,0:T(8,128)(2,1)S(1)}, u32[]{:S(2)}, u32[]{:S(2)}) %collective-permute-start.16) | collective-permute-done | bytes 98336 | tf_op jit(solution)/shard_map/ppermute | solution.py:349
  63.0 0.1 convert_add_fusion.1
  63.1 1.9 %collective-permute-done.18 = bf16[64,896]{1,0:T(8,128)(2,1)S(1)} collective-permute-done((bf16[64,896]{1,0:T(8,128)(2,1)S(1)}, bf16[64,896]{1,0:T(8,128)(2,1)S(1)}, u32[]{:S(2)}, u32[]{:S(2)}) %collective-permute-start.18) | collective-permute-done | bytes 114720 | tf_op jit(solution)/shard_map/ppermute | solution.py:349
  65.0 0.1 convert_add_fusion
  65.1 2.0 %collective-permute-start.19 = (bf16[32,2304]{1,0:T(8,128)(2,1)S(1)}, bf16[32,2304]{1,0:T(8,128)(2,1)S(1)}, u32[]{:S(2)}, u32[]{:S(2)}) collective-permute-start(bf16[32,2304]{1,0:T(8,128)(2,1)S(1)} %slice.262), channel_id=1, source_target_pairs={{0,16},{8,24},{16,0},{24,8},{1,17},{9,25},{17,1},{25,9},{2,18},{10... | collective-permute-start | bytes 442376 | tf_op jit(solution)/shard_map/ppermute | solution.py:349
  67.2 1.1 %shard_map.145 = f32[2,64,1024]{2,1,0:T(8,128)} custom-call(f32[2,64,1024]{2,1,0:T(8,128)S(1)} %get-tuple-element.79.own_ref, bf16[64,1024]{1,0:T(8,128)(2,1)S(1)} %collective-permute-done.11.from_mate_ref, bf16[64,1024]{1,0:T(8,128)(2,1)S(1)} %collective-permute-done.12.from_other_ref, s32[2,32]{1,0:T(2,128)S(1)} %get-tuple-element.87.halo_ref), custom_call_target="tpu_custom_call" | custom-call | flops 1 | bytes 1 | tf_op jit(solution)/shard_map/pallas_call | solution.py:28
  68.3 5.1 %collective-permute-done.19.arrived_ref = bf16[32,2304]{1,0:T(8,128)(2,1)S(1)} collective-permute-done((bf16[32,2304]{1,0:T(8,128)(2,1)S(1)}, bf16[32,2304]{1,0:T(8,128)(2,1)S(1)}, u32[]{:S(2)}, u32[]{:S(2)}) %collective-permute-start.19) | collective-permute-done | bytes 147488 | tf_op jit(solution)/shard_map/ppermute | solution.py:349
  73.4 0.9 %shard_map.146 = (f32[32,2048]{1,0:T(8,128)}, f32[32,1024]{1,0:T(8,128)}, f32[32,100]{1,0:T(8,128)}) custom-call(f32[32,2304]{1,0:T(8,128)S(1)} %slice.220.own_ref, bf16[32,2304]{1,0:T(8,128)(2,1)S(1)} %collective-permute-done.19.arrived_ref, bf16[100,1024]{1,0:T(8,128)(2,1)S(1)} %bitcast.4), custom_call_target="tpu_custom_call" | custom-call | flops 1 | bytes 1 | tf_op jit(solution)/shard_map/pallas_call | solution.py:28
  (34 shorter events, 0.4 us)
Async XLA Ops:
  0.6 2.8 %copy-start.2 = (bf16[256,1024]{1,0:T(8,128)(2,1)S(1)}, bf16[256,1024]{1,0:T(8,128)(2,1)}, u32[]{:S(2)}) copy-start(bf16[256,1024]{1,0:T(8,128)(2,1)} %q_ref.5) | copy-start | bytes 1572868
  0.6 2.8 %copy-start.1 = (bf16[1024,1024]{1,0:T(8,128)(2,1)S(1)}, bf16[1024,1024]{1,0:T(8,128)(2,1)}, u32[]{:S(2)}) copy-start(bf16[1024,1024]{1,0:T(8,128)(2,1)} %wo_ref.3) | copy-start | bytes 6291460
  0.7 2.8 %copy-start.8 = (f32[100]{0:T(128)S(1)}, f32[100]{0:T(128)}, u32[]{:S(2)}) copy-start(f32[100]{0:T(128)} %param.19) | copy-start | bytes 1204
  0.7 2.8 %copy-start.7 = (f32[256]{0:T(256)S(1)}, f32[256]{0:T(256)}, u32[]{:S(2)}) copy-start(f32[256]{0:T(256)} %param.18) | copy-start | bytes 3076
  0.7 2.8 %copy-start.4 = (f32[100,256]{1,0:T(8,128)S(1)}, f32[100,256]{1,0:T(8,128)}, u32[]{:S(2)}) copy-start(f32[100,256]{1,0:T(8,128)} %init_ref.1) | copy-start | bytes 307204
  0.7 2.8 %copy-start.3 = (bf16[1024,100]{0,1:T(8,128)(2,1)S(1)}, bf16[1024,100]{0,1:T(8,128)(2,1)}, u32[]{:S(2)}) copy-start(bf16[1024,100]{0,1:T(8,128)(2,1)} %param.15) | copy-start | bytes 614404
  0.7 3.2 %copy-start = (bf16[1024,2048]{1,0:T(8,128)(2,1)S(1)}, bf16[1024,2048]{1,0:T(8,128)(2,1)}, u32[]{:S(2)}) copy-start(bf16[1024,2048]{1,0:T(8,128)(2,1)} %kvw_ref.5) | copy-start | bytes 12582916
  2.1 3.3 %collective-permute-start = (bf16[64,1024]{1,0:T(8,128)(2,1)S(1)}, bf16[64,1024]{1,0:T(8,128)(2,1)S(1)}, u32[]{:S(2)}, u32[]{:S(2)}) collective-permute-start(bf16[64,1024]{1,0:T(8,128)(2,1)S(1)} %get-tuple-element.49), channel_id=1, source_target_pairs={{0,1},{1,0},{2,3},{3,2},{4,5},{5,4},{6,7},{7,6},{8,9},{9,8},{10,11... | collective-permute-start | bytes 393224 | tf_op jit(solution)/shard_map/ppermute | solution.py:387
  2.6 2.8 %collective-permute-start.1 = (bf16[64,1024]{1,0:T(8,128)(2,1)S(1)}, bf16[64,1024]{1,0:T(8,128)(2,1)S(1)}, u32[]{:S(2)}, u32[]{:S(2)}) collective-permute-start(bf16[64,1024]{1,0:T(8,128)(2,1)S(1)} %get-tuple-element.50), channel_id=1, source_target_pairs={{0,0},{7,7},{1,2},{2,1},{3,4},{4,3},{5,6},{6,5},{8,8},{15,15},{9,1... | collective-permute-start | bytes 393224 | tf_op jit(solution)/shard_map/ppermute | solution.py:388
  3.9 1.5 %copy-start.6 = (s32[3,256]{1,0:T(4,128)S(1)}, s32[3,256]{1,0:T(4,128)}, u32[]{:S(2)}) copy-start(s32[3,256]{1,0:T(4,128)} %src_ref.1) | copy-start | bytes 9220
  5.4 16.3 %copy-start.5 = (f32[100,256]{1,0:T(8,128)S(1)}, f32[100,256]{1,0:T(8,128)}, u32[]{:S(2)}) copy-start(f32[100,256]{1,0:T(8,128)} %refs_5_.1) | copy-start | bytes 307204
  8.3 6.0 %collective-permute-start.4 = (bf16[208,256]{1,0:T(8,128)(2,1)S(1)}, bf16[208,256]{1,0:T(8,128)(2,1)S(1)}, u32[]{:S(2)}, u32[]{:S(2)}) collective-permute-start(bf16[208,256]{1,0:T(8,128)(2,1)S(1)} %get-tuple-element.54), channel_id=1, source_target_pairs={{0,8},{8,0},{16,24},{24,16},{1,9},{9,1},{17,25},{25,17},{2,10},{10... | collective-permute-start | bytes 319496 | tf_op jit(solution)/shard_map/ppermute | solution.py:421
  11.4 6.9 %collective-permute-start.3 = (bf16[208,256]{1,0:T(8,128)(2,1)S(1)}, bf16[208,256]{1,0:T(8,128)(2,1)S(1)}, u32[]{:S(2)}, u32[]{:S(2)}) collective-permute-start(bf16[208,256]{1,0:T(8,128)(2,1)S(1)} %get-tuple-element.54), channel_id=1, source_target_pairs={{0,16},{8,24},{16,0},{24,8},{1,17},{9,25},{17,1},{25,9},{2,18},{10... | collective-permute-start | bytes 319496 | tf_op jit(solution)/shard_map/ppermute | solution.py:421
  14.0 7.7 %collective-permute-start.2 = (bf16[208,256]{1,0:T(8,128)(2,1)S(1)}, bf16[208,256]{1,0:T(8,128)(2,1)S(1)}, u32[]{:S(2)}, u32[]{:S(2)}) collective-permute-start(bf16[208,256]{1,0:T(8,128)(2,1)S(1)} %get-tuple-element.54), channel_id=1, source_target_pairs={{0,24},{8,16},{16,8},{24,0},{1,25},{9,17},{17,9},{25,1},{2,26},{10... | collective-permute-start | bytes 319496 | tf_op jit(solution)/shard_map/ppermute | solution.py:421
  26.5 6.2 %collective-permute-start.7 = (bf16[512,896]{1,0:T(8,128)(2,1)S(1)}, bf16[512,896]{1,0:T(8,128)(2,1)S(1)}, u32[]{:S(2)}, u32[]{:S(2)}) collective-permute-start(bf16[512,896]{1,0:T(8,128)(2,1)S(1)} %get-tuple-element.71), channel_id=1, source_target_pairs={{0,1},{1,0},{2,3},{3,2},{4,5},{5,4},{6,7},{7,6},{8,9},{9,8},{10,11... | collective-permute-start | bytes 2752520 | tf_op jit(solution)/shard_map/ppermute | solution.py:349
  28.5 3.0 %collective-permute-start.5 = (bf16[512,640]{1,0:T(8,128)(2,1)S(1)}, bf16[512,640]{1,0:T(8,128)(2,1)S(1)}, u32[]{:S(2)}, u32[]{:S(2)}) collective-permute-start(bf16[512,640]{1,0:T(8,128)(2,1)S(1)} %get-tuple-element.61), channel_id=1, source_target_pairs={{0,1},{1,0},{2,3},{3,2},{4,5},{5,4},{6,7},{7,6},{8,9},{9,8},{10,11... | collective-permute-start | bytes 1966088 | tf_op jit(solution)/shard_map/ppermute | solution.py:349
  28.6 4.1 %collective-permute-start.6 = (bf16[512,768]{1,0:T(8,128)(2,1)S(1)}, bf16[512,768]{1,0:T(8,128)(2,1)S(1)}, u32[]{:S(2)}, u32[]{:S(2)}) collective-permute-start(bf16[512,768]{1,0:T(8,128)(2,1)S(1)} %get-tuple-element.69), channel_id=1, source_target_pairs={{0,1},{1,0},{2,3},{3,2},{4,5},{5,4},{6,7},{7,6},{8,9},{9,8},{10,11... | collective-permute-start | bytes 2359304 | tf_op jit(solution)/shard_map/ppermute | solution.py:349
  32.9 17.0 %collective-permute-start.10 = (bf16[256,896]{1,0:T(8,128)(2,1)S(1)}, bf16[256,896]{1,0:T(8,128)(2,1)S(1)}, u32[]{:S(2)}, u32[]{:S(2)}) collective-permute-start(bf16[256,896]{1,0:T(8,128)(2,1)S(1)} %add_convert_fusion), channel_id=1, source_target_pairs={{0,8},{8,0},{16,24},{24,16},{1,9},{9,1},{17,25},{25,17},{2,10},{10... | collective-permute-start | bytes 1376264 | tf_op jit(solution)/shard_map/ppermute | solution.py:349
  34.7 15.2 %collective-permute-start.9 = (bf16[256,768]{1,0:T(8,128)(2,1)S(1)}, bf16[256,768]{1,0:T(8,128)(2,1)S(1)}, u32[]{:S(2)}, u32[]{:S(2)}) collective-permute-start(bf16[256,768]{1,0:T(8,128)(2,1)S(1)} %add_convert_fusion.1), channel_id=1, source_target_pairs={{0,4},{1,5},{2,6},{3,7},{4,0},{5,1},{6,2},{7,3},{8,12},{9,13},{10,... | collective-permute-start | bytes 1179656 | tf_op jit(solution)/shard_map/ppermute | solution.py:349
  39.3 10.6 %collective-permute-start.8 = (bf16[256,640]{1,0:T(8,128)(2,1)S(1)}, bf16[256,640]{1,0:T(8,128)(2,1)S(1)}, u32[]{:S(2)}, u32[]{:S(2)}) collective-permute-start(bf16[256,640]{1,0:T(8,128)(2,1)S(1)} %add_convert_fusion.2), channel_id=1, source_target_pairs={{0,2},{1,3},{2,0},{3,1},{4,6},{5,7},{6,4},{7,5},{8,10},{9,11},{10,... | collective-permute-start | bytes 983048 | tf_op jit(solution)/shard_map/ppermute | solution.py:349
  40.6 1.4 %collective-permute-start.11 = (bf16[64,1024]{1,0:T(8,128)(2,1)S(1)}, bf16[64,1024]{1,0:T(8,128)(2,1)S(1)}, u32[]{:S(2)}, u32[]{:S(2)}) collective-permute-start(bf16[64,1024]{1,0:T(8,128)(2,1)S(1)} %get-tuple-element.83), channel_id=1, source_target_pairs={{0,1},{1,0},{2,3},{3,2},{4,5},{5,4},{6,7},{7,6},{8,9},{9,8},{10,11... | collective-permute-start | bytes 393224 | tf_op jit(solution)/shard_map/ppermute | solution.py:466
  40.7 1.3 %collective-permute-start.12 = (bf16[64,1024]{1,0:T(8,128)(2,1)S(1)}, bf16[64,1024]{1,0:T(8,128)(2,1)S(1)}, u32[]{:S(2)}, u32[]{:S(2)}) collective-permute-start(bf16[64,1024]{1,0:T(8,128)(2,1)S(1)} %get-tuple-element.84), channel_id=1, source_target_pairs={{0,0},{7,7},{1,2},{2,1},{3,4},{4,3},{5,6},{6,5},{8,8},{15,15},{9,1... | collective-permute-start | bytes 393224 | tf_op jit(solution)/shard_map/ppermute | solution.py:467
  50.0 6.9 %collective-permute-start.13 = (bf16[128,640]{1,0:T(8,128)(2,1)S(1)}, bf16[128,640]{1,0:T(8,128)(2,1)S(1)}, u32[]{:S(2)}, u32[]{:S(2)}) collective-permute-start(bf16[128,640]{1,0:T(8,128)(2,1)S(1)} %add_convert_fusion.5), channel_id=1, source_target_pairs={{0,4},{1,5},{2,6},{3,7},{4,0},{5,1},{6,2},{7,3},{8,12},{9,13},{10,... | collective-permute-start | bytes 491528 | tf_op jit(solution)/shard_map/ppermute | solution.py:349
  51.8 6.4 %collective-permute-start.15 = (bf16[128,768]{1,0:T(8,128)(2,1)S(1)}, bf16[128,768]{1,0:T(8,128)(2,1)S(1)}, u32[]{:S(2)}, u32[]{:S(2)}) collective-permute-start(bf16[128,768]{1,0:T(8,128)(2,1)S(1)} %add_convert_fusion.4), channel_id=1, source_target_pairs={{0,8},{8,0},{16,24},{24,16},{1,9},{9,1},{17,25},{25,17},{2,10},{10... | collective-permute-start | bytes 589832 | tf_op jit(solution)/shard_map/ppermute | solution.py:349
  52.3 7.8 %collective-permute-start.17 = (bf16[128,896]{1,0:T(8,128)(2,1)S(1)}, bf16[128,896]{1,0:T(8,128)(2,1)S(1)}, u32[]{:S(2)}, u32[]{:S(2)}) collective-permute-start(bf16[128,896]{1,0:T(8,128)(2,1)S(1)} %add_convert_fusion.3), channel_id=1, source_target_pairs={{0,2},{1,3},{2,0},{3,1},{4,6},{5,7},{6,4},{7,5},{8,10},{9,11},{10,... | collective-permute-start | bytes 688136 | tf_op jit(solution)/shard_map/ppermute | solution.py:349
  56.9 4.8 %collective-permute-start.14 = (bf16[64,640]{1,0:T(8,128)(2,1)S(1)}, bf16[64,640]{1,0:T(8,128)(2,1)S(1)}, u32[]{:S(2)}, u32[]{:S(2)}) collective-permute-start(bf16[64,640]{1,0:T(8,128)(2,1)S(1)} %add_convert_fusion.8), channel_id=1, source_target_pairs={{0,8},{8,0},{16,24},{24,16},{1,9},{9,1},{17,25},{25,17},{2,10},{10... | collective-permute-start | bytes 245768 | tf_op jit(solution)/shard_map/ppermute | solution.py:349
  58.3 4.7 %collective-permute-start.16 = (bf16[64,768]{1,0:T(8,128)(2,1)S(1)}, bf16[64,768]{1,0:T(8,128)(2,1)S(1)}, u32[]{:S(2)}, u32[]{:S(2)}) collective-permute-start(bf16[64,768]{1,0:T(8,128)(2,1)S(1)} %add_convert_fusion.7), channel_id=1, source_target_pairs={{0,2},{1,3},{2,0},{3,1},{4,6},{5,7},{6,4},{7,5},{8,10},{9,11},{10,... | collective-permute-start | bytes 294920 | tf_op jit(solution)/shard_map/ppermute | solution.py:349
  60.1 4.9 %collective-permute-start.18 = (bf16[64,896]{1,0:T(8,128)(2,1)S(1)}, bf16[64,896]{1,0:T(8,128)(2,1)S(1)}, u32[]{:S(2)}, u32[]{:S(2)}) collective-permute-start(bf16[64,896]{1,0:T(8,128)(2,1)S(1)} %add_convert_fusion.6), channel_id=1, source_target_pairs={{0,4},{1,5},{2,6},{3,7},{4,0},{5,1},{6,2},{7,3},{8,12},{9,13},{10,... | collective-permute-start | bytes 344072 | tf_op jit(solution)/shard_map/ppermute | solution.py:349
  65.1 8.2 %collective-permute-start.19 = (bf16[32,2304]{1,0:T(8,128)(2,1)S(1)}, bf16[32,2304]{1,0:T(8,128)(2,1)S(1)}, u32[]{:S(2)}, u32[]{:S(2)}) collective-permute-start(bf16[32,2304]{1,0:T(8,128)(2,1)S(1)} %slice.262), channel_id=1, source_target_pairs={{0,16},{8,24},{16,0},{24,8},{1,17},{9,25},{17,1},{25,9},{2,18},{10... | collective-permute-start | bytes 442376 | tf_op jit(solution)/shard_map/ppermute | solution.py:349

commit v8 on v7

--- a/solution.py
+++ b/solution.py
@@ -275,43 +275,46 @@
     store_group(mm(ext_ref[...], ng_ref[:, 0:group_width]), 0, n_member, n_band, 0, out_refs)
 
 
-def key_body(
-    n_member, n_band, width1, grad_ref, dm_ref, value_ref, slope_ref, q_ref, merged_ref, wo_ref, ext_ref, ngv_ref,
-    ng_ref, *refs
-):
-    out_refs, turned = refs[:-1], refs[-1]
-    members, ext, width = value_ref.shape
+def key_gradients(pairs, dm_ref, value_ref, slope_ref, q_ref, ng_ref):
+    members, ext, _ = value_ref.shape
     scale = HEAD_DIM ** (-0.5)
-    for pair in range(width // LANES):
+    for place, pair in enumerate(pairs):
         cols = slice(pair * LANES, (pair + 1) * LANES)
         for m in range(members):
             dgate = mm(split_heads(value_ref[m, :, cols]), dm_ref[m, cols, :])
             dscore = (dgate * slope_ref[pair, m].astype(F32)).astype(BF)
             keys = select_heads(mm(dscore, q_ref[:, cols])) * scale
-            ng_ref[m * ext : (m + 1) * ext, cols] = keys.astype(BF)
+            ng_ref[m * ext : (m + 1) * ext, place * LANES : (place + 1) * LANES] = keys.astype(BF)
+
+
+def first_keys_body(
+    n_member, n_band, first_value, dm_ref, value_ref, slope_ref, q_ref, ext_ref, ngv_ref, ng_ref, *out_refs
+):
+    count = ng_ref.shape[1] // LANES
+    rest = mm(ext_ref[...], ngv_ref[:, first_value:])
+    store_group(rest, 1, n_member, n_band, 0, out_refs)
+    key_gradients(range(count), dm_ref, value_ref, slope_ref, q_ref, ng_ref)
+    store_group(mm(ext_ref[...], ng_ref[...]), 1, n_member, n_band, rest.shape[1], out_refs)
+
+
+def last_keys_body(
+    n_member, n_band, grad_ref, dm_ref, value_ref, slope_ref, q_ref, merged_ref, wo_ref, ext_ref, ng_ref, *refs
+):
+    out_refs, turned = refs[:-1], refs[-1]
+    members, _, width = value_ref.shape
+    count = ng_ref.shape[1] // LANES
+    key_gradients(range(width // LANES - count, width // LANES), dm_ref, value_ref, slope_ref, q_ref, ng_ref)
     m_t = sum(mm(grad_ref[m], merged_ref[m], NT) for m in range(members))
     head_t = sum(mm(grad_ref[m], q_ref[...]) for m in range(members)) + mm(m_t.astype(BF), wo_ref[...])
     turned[...] = jnp.concatenate([m_t, head_t], axis=0).T
-    pieces = [(ngv_ref, width1, width), (ng_ref, 0, width), (None, 0, 2 * LANES)]
-    group, offset = 0, 0
-    for ref, first, last in pieces:
-        while first < last:
-            outs = out_refs[2 * group : 2 * group + 2]
-            take = min(last - first, outs[0].shape[1] - offset)
-            if ref is None:
-                rows = reorder(turned, n_member, n_band)
-            else:
-                rows = mm(ext_ref[...], ref[:, first : first + take])
-            store_group(rows, group + 1, n_member, n_band, offset, outs)
-            first, offset = first + take, offset + take
-            if offset == outs[0].shape[1]:
-                group, offset = group + 1, 0
-
-
-def extended_grad_body(members, nodes, rim, ngk_ref, ngv_ref, kvw_ref, own_ref, mate_ref, other_ref):
+    store_group(mm(ext_ref[...], ng_ref[...]), 2, n_member, n_band, 0, out_refs)
+    store_group(reorder(turned, n_member, n_band), 2, n_member, n_band, ng_ref.shape[1], out_refs)
+
+
+def extended_grad_body(members, nodes, rim, first_ref, last_ref, ngv_ref, kvw_ref, own_ref, mate_ref, other_ref):
     ext = nodes + 2 * rim
-    width = kvw_ref.shape[0]
-    rows = mm(ngk_ref[...], kvw_ref[:, 0:width], NT) + mm(ngv_ref[...], kvw_ref[:, width:], NT)
+    grads = jnp.concatenate([first_ref[...], last_ref[...], ngv_ref[...]], axis=1)
+    rows = mm(grads, kvw_ref[...], NT)
     for m in range(members):
         at = m * ext
         own_ref[m] = rows[at : at + nodes]
@@ -373,8 +376,7 @@
     chips = n_band // 2
     send_rows = -(-channels // 8) * 8
     mates = [(i, i ^ 1) for i in range(n_band)]
-    others = [(0, 0), (n_band - 1, n_band - 1)]
-    others += [(i, i + 1 if i % 2 else i - 1) for i in range(1, n_band - 1)]
+    others = [(i, (i + 1 if i % 2 else i - 1) % n_band) for i in range(n_band)]
 
     own_hidden, halo, for_mate, for_other = call(
         pick_body,
@@ -429,40 +431,50 @@
     )
 
     extra = 2 * LANES
-    third = (2 * width + extra) // LANES // GROUPS
-    widths = [(third - 1) * LANES, third * LANES]
-    widths.append(2 * width + extra - sum(widths))
+    group_width = (2 * width + extra) // GROUPS
+    first_keys = 2 * group_width - width
+    group_shape = [sds((width // 2, group_width), BF)] * 2
     grad, dm, ng_value, send, keep = call(
         functools.partial(value_body, n_member, n_band),
         [sds((members, LANES, points), BF), sds((members, width, points), BF), sds((members * ext, width), BF)]
-        + [sds((width // 2, widths[0]), BF)] * 2,
+        + group_shape,
         (*received, part, base, truth, weight, pt, gates, ext_t),
     )
     groups = [[keep, swap(send, "band", 0, n_band)]]
-    ng_key, *outs = call(
-        functools.partial(key_body, n_member, n_band, widths[0]),
-        [sds((members * ext, width), BF)] + [sds((width // 2, w), BF) for w in widths[1:] for _ in range(2)],
-        (grad, dm, value, slopes, queries, merged, out_weight, ext_t, ng_value),
+    ng_first, send, keep = call(
+        functools.partial(first_keys_body, n_member, n_band, group_width),
+        [sds((members * ext, first_keys), BF)] + group_shape,
+        (dm, value, slopes, queries, ext_t, ng_value),
+    )
+    groups.append([keep, swap(send, "band", 0, n_band)])
+    ng_last, send, keep = call(
+        functools.partial(last_keys_body, n_member, n_band),
+        [sds((members * ext, width - first_keys), BF)] + group_shape,
+        (grad, dm, value, slopes, queries, merged, out_weight, ext_t),
         [pltpu.VMEM((width, extra), F32)],
     )
-    for i in range(GROUPS - 1):
-        groups.append([outs[2 * i + 1], swap(outs[2 * i], "band", 0, n_band)])
+    groups.append([keep, swap(send, "band", 0, n_band)])
 
     count = {"member": n_member, "band": n_band}
     turns, rest = halving_orders(n_member, n_band)
-    for step in range(len(turns[0])):
-        outgoing = [add_up(*upper(terms)).astype(BF) for terms in groups]
+    steps = len(turns[0])
+    for step in range(steps):
+        outgoing = []
+        for i in range(GROUPS):
+            outgoing.append(add_up(*upper(groups[i])).astype(BF))
+            if step == 0 and i + 1 < GROUPS:
+                outgoing[i], groups[i + 1] = lax.optimization_barrier((outgoing[i], groups[i + 1]))
         if step == 0:
-            outgoing[0], groups[1:] = lax.optimization_barrier((outgoing[0], groups[1:]))
-            outgoing[1:] = [add_up(*upper(terms)).astype(BF) for terms in groups[1:]]
-            outgoing, ng_key = lax.optimization_barrier((outgoing, ng_key))
+            outgoing, ng_last = lax.optimization_barrier((outgoing, ng_last))
             own_grad, back_mate, back_other = call(
                 functools.partial(extended_grad_body, members, nodes, rim),
                 [sds((members, nodes, width), F32)] + [sds((members * rim, width), BF)] * 2,
-                (ng_key, ng_value, kv_weight),
+                (ng_first, ng_last, ng_value, kv_weight),
             )
         arrived = [swap(out, *turn[step], count[turn[step][0]]) for out, turn in zip(outgoing, turns)]
         if step == 0:
+            arrived, back_mate, back_other = lax.optimization_barrier((arrived, back_mate, back_other))
+        if step == steps - 1:
             from_mate = lax.ppermute(back_mate, "band", mates)
             from_other = lax.ppermute(back_other, "band", others)
             arrived, from_mate, from_other = lax.optimization_barrier((arrived, from_mate, from_other))

time: 74.4 us -> 73.4 us (0.987)
    ppermute x1, starting transfers between devices: 0.79 us -> 3.56 us  [shards(): other = lax.ppermute(for_other, 'band', others)]
    ppermute x13, starting transfers between devices: 17.4 us -> 15.1 us  [swap(): return lax.ppermute(rows, axis, [(i, i ^ 1 << bit) for i in range(count)])]
    ppermute x13, waiting for transfers between devices: 24.6 us -> 22.3 us  [swap(): return lax.ppermute(rows, axis, [(i, i ^ 1 << bit) for i in range(count)])]
    ppermute x1, waiting for transfers between devices: 0.01 us -> 1.63 us  [shards(): other = lax.ppermute(for_other, 'band', others)]
    ppermute x3, starting transfers between devices: 5.68 us -> 4.58 us  [shards(): lax.ppermute(sent, 'member', [(i, i ^ s) for i in range(n_member)])]
    ppermute x3, waiting for transfers between devices: 7.47 us -> 8.32 us  [shards(): lax.ppermute(sent, 'member', [(i, i ^ s) for i in range(n_member)])]
    pallas_call x9 -> x10, Pallas kernels: 14 us -> 14.4 us  [call(): pl.pallas_call(body, out_shape=out_shape, in_specs=[pl.BlockSpec(memory_s...]
  transfers between devices with their start and end apart: 20 -> 20, of which waited for: 12 -> 12; matrix products, arithmetic and copies ran while one was open for 1% -> 1% of each run, Pallas kernels for 6% -> 10%
where the time goes in v8:
time: 73.4 us; the launch traced here: 73.3 us
  waiting for transfers between devices  32.3 us (44%)
  starting transfers between devices  24.7 us (34%)
  Pallas kernels  14.4 us (20%)
  other arithmetic  0.94 us (1%)
  between operations  0.89 us (1%)
    ppermute x13, waiting for transfers between devices, swap(): return lax.ppermute(rows, axis, [(i, i ^ 1 << bit) for i in range(count)])  22.3 us
    ppermute x13, starting transfers between devices, swap(): return lax.ppermute(rows, axis, [(i, i ^ 1 << bit) for i in range(count)])  15.1 us
    pallas_call x10, Pallas kernels, call(): pl.pallas_call(body, out_shape=out_shape, in_specs=[pl.BlockSpec(memory_s...  14.4 us
    ppermute x3, waiting for transfers between devices, shards(): lax.ppermute(sent, 'member', [(i, i ^ s) for i in range(n_member)])  8.32 us
    ppermute x3, starting transfers between devices, shards(): lax.ppermute(sent, 'member', [(i, i ^ s) for i in range(n_member)])  4.58 us
    ppermute x1, starting transfers between devices, shards(): other = lax.ppermute(for_other, 'band', others)  3.56 us
    ppermute x1, waiting for transfers between devices, shards(): other = lax.ppermute(for_other, 'band', others)  1.63 us
  transfers between devices with their start and end apart: 20, of which 12 were waited for; matrix products, arithmetic and copies ran while one was open for 1% of the time, Pallas kernels for 10%

profile of v8, /device:TPU:0, one launch (start us, length us, event | category | flops | bytes accessed | tf_op | source)
XLA Modules:
  0.0 73.3 jit_solution(8033917354288379077)
XLA Ops:
  0.7 1.4 %shard_map.138 = (bf16[2,64,1024]{2,1,0:T(8,128)(2,1)S(1)}, s32[2,32]{1,0:T(2,128)S(1)}, bf16[64,1024]{1,0:T(8,128)(2,1)S(1)}, bf16[64,1024]{1,0:T(8,128)(2,1)S(1)}) custom-call(bf16[2,64,1024]{2,1,0:T(8,128)(2,1)} %hidden_hbm.1, s32[2,32]{1,0:T(2,128)} %halo_hbm.1), custom_call_target="tpu_custom_call" | custom-call | flops 10000000000 | bytes 1 | tf_op jit(solution)/shard_map/pallas_call | solution.py:28
  2.1 0.5 collective-permute-start
  2.6 3.6 %collective-permute-start.1 = (bf16[64,1024]{1,0:T(8,128)(2,1)S(1)}, bf16[64,1024]{1,0:T(8,128)(2,1)S(1)}, u32[]{:S(2)}, u32[]{:S(2)}) collective-permute-start(bf16[64,1024]{1,0:T(8,128)(2,1)S(1)} %get-tuple-element.57), channel_id=1, source_target_pairs={{0,7},{1,2},{2,1},{3,4},{4,3},{5,6},{6,5},{7,0},{8,15},{9,10},{10,... | collective-permute-start | bytes 393224 | tf_op jit(solution)/shard_map/ppermute | solution.py:390
  6.2 1.5 %shard_map.139 = (bf16[128,2048]{1,0:T(8,128)(2,1)S(1)}, bf16[1024,128]{1,0:T(8,128)(2,1)S(1)}, bf16[128,1024]{1,0:T(8,128)(2,1)S(1)}, f32[128,256]{1,0:T(8,128)S(1)}, f32[100,256]{1,0:T(8,128)S(1)}) custom-call(bf16[2,64,1024]{2,1,0:T(8,128)(2,1)S(1)} %get-tuple-element.58.hidden_ref, bf16[1024,1024]{1,0:T(8,128)(2,1)S(1)} %copy-done.1, ...), custom_call_target="tpu_custom_call" | custom-call | flops 1 | bytes 1 | tf_op jit(solution)/shard_map/pallas_call | solution.py:28
  7.8 1.6 %collective-permute-done.1.other_ref = bf16[64,1024]{1,0:T(8,128)(2,1)S(1)} collective-permute-done((bf16[64,1024]{1,0:T(8,128)(2,1)S(1)}, bf16[64,1024]{1,0:T(8,128)(2,1)S(1)}, u32[]{:S(2)}, u32[]{:S(2)}) %collective-permute-start.1) | collective-permute-done | bytes 131104 | tf_op jit(solution)/shard_map/ppermute | solution.py:390
  9.4 2.9 %shard_map.140 = (bf16[2,128,1024]{2,1,0:T(8,128)(2,1)S(1)}, bf16[8,2,256,256]{3,2,1,0:T(8,128)(2,1)S(1)}, bf16[8,2,256,256]{3,2,1,0:T(8,128)(2,1)S(1)}, bf16[2,...) custom-call(bf16[64,1024]{1,0:T(8,128)(2,1)S(1)} %collective-permute-done.mate_ref, ...), custom_call_target="tpu_custom_call" | custom-call | flops 1 | bytes 1 | tf_op jit(solution)/shard_map/pallas_call | solution.py:28
  12.4 2.0 %collective-permute-start.4 = (bf16[208,256]{1,0:T(8,128)(2,1)S(1)}, bf16[208,256]{1,0:T(8,128)(2,1)S(1)}, u32[]{:S(2)}, u32[]{:S(2)}) collective-permute-start(bf16[208,256]{1,0:T(8,128)(2,1)S(1)} %get-tuple-element.61), channel_id=1, source_target_pairs={{0,8},{8,0},{16,24},{24,16},{1,9},{9,1},{17,25},{25,17},{2,10},{10... | collective-permute-start | bytes 319496 | tf_op jit(solution)/shard_map/ppermute | solution.py:423
  14.3 2.6 %collective-permute-start.3 = (bf16[208,256]{1,0:T(8,128)(2,1)S(1)}, bf16[208,256]{1,0:T(8,128)(2,1)S(1)}, u32[]{:S(2)}, u32[]{:S(2)}) collective-permute-start(bf16[208,256]{1,0:T(8,128)(2,1)S(1)} %get-tuple-element.61), channel_id=1, source_target_pairs={{0,16},{8,24},{16,0},{24,8},{1,17},{9,25},{17,1},{25,9},{2,18},{10... | collective-permute-start | bytes 319496 | tf_op jit(solution)/shard_map/ppermute | solution.py:423
  16.9 0.3 shard_map.141.refs_9_.ext_ref
  17.2 0.4 collective-permute-done.4.refs_2_
  17.6 7.9 %collective-permute-done.3.refs_1_ = bf16[208,256]{1,0:T(8,128)(2,1)S(1)} collective-permute-done((bf16[208,256]{1,0:T(8,128)(2,1)S(1)}, bf16[208,256]{1,0:T(8,128)(2,1)S(1)}, u32[]{:S(2)}, u32[]{:S(2)}) %collective-permute-start.3) | collective-permute-done | bytes 106528 | tf_op jit(solution)/shard_map/ppermute | solution.py:423
  25.5 1.8 %shard_map.142 = (bf16[2,128,256]{2,1,0:T(8,128)(2,1)S(1)}, bf16[2,1024,256]{2,1,0:T(8,128)(2,1)S(1)}, bf16[256,1024]{1,0:T(8,128)(2,1)S(1)}, bf16[512,768]{1,0:T(8,128)(2,1)S(1)}, bf16[512,768]{1,0:T(8,128)(2,1)S(1)}) custom-call(bf16[208,256]{1,0:T(8,128)(2,1)S(1)} %collective-permute-done.2.refs_0_, bf16[208,256]{1,0:T(8,128)(2,1)S(1)} %collective-permute-done.3.refs_1_, ...), custom_call_target="tpu_custom_call" | custom-call | flops 1 | bytes 1 | tf_op jit(solution)/shard_map/pallas_call | solution.py:28
  27.3 0.1 collective-permute-start.5
  27.4 1.5 %shard_map.143 = (bf16[256,512]{1,0:T(8,128)(2,1)S(1)}, bf16[512,768]{1,0:T(8,128)(2,1)S(1)}, bf16[512,768]{1,0:T(8,128)(2,1)S(1)}) custom-call(bf16[2,1024,256]{2,1,0:T(8,128)(2,1)S(1)} %get-tuple-element.67.dm_ref, bf16[2,128,1024]{2,1,0:T(8,128)(2,1)S(1)} %get-tuple-element.68.value_ref, bf16[8,2,256,256]{3,2,1,0:T(8,128)(2,1)S(1)} %get-tuple-element.69.slope_ref, ...), custom_call_target="tpu_custom_call" | custom-call | flops 1 | bytes 1 | tf_op jit(solution)/shard_map/pallas_call | solution.py:28
  28.9 0.6 collective-permute-start.6
  29.4 1.8 %shard_map.144 = (bf16[256,512]{1,0:T(8,128)(2,1)S(1)}, bf16[512,768]{1,0:T(8,128)(2,1)S(1)}, bf16[512,768]{1,0:T(8,128)(2,1)S(1)}) custom-call(bf16[2,128,256]{2,1,0:T(8,128)(2,1)S(1)} %get-tuple-element.79.grad_ref, bf16[2,1024,256]{2,1,0:T(8,128)(2,1)S(1)} %get-tuple-element.67.dm_ref, bf16[2,128,1024]{2,1,0:T(8,128)(2,1)S(1)} %get-tuple-element.68.value_ref, ...), custom_call_target="tpu_custom_call" | custom-call | flops 1 | bytes 1 | tf_op jit(solution)/shard_map/pallas_call | solution.py:28
  31.2 0.1 collective-permute-start.7
  31.3 0.1 add_convert_fusion.2
  31.4 0.1 add_convert_fusion.1
  31.5 2.0 %collective-permute-done.7 = bf16[512,768]{1,0:T(8,128)(2,1)S(1)} collective-permute-done((bf16[512,768]{1,0:T(8,128)(2,1)S(1)}, bf16[512,768]{1,0:T(8,128)(2,1)S(1)}, u32[]{:S(2)}, u32[]{:S(2)}) %collective-permute-start.7) | collective-permute-done | bytes 786464 | tf_op jit(solution)/shard_map/ppermute | solution.py:352
  33.6 0.1 add_convert_fusion
  33.7 0.2 collective-permute-start.8
  33.9 2.2 %collective-permute-start.9 = (bf16[256,768]{1,0:T(8,128)(2,1)S(1)}, bf16[256,768]{1,0:T(8,128)(2,1)S(1)}, u32[]{:S(2)}, u32[]{:S(2)}) collective-permute-start(bf16[256,768]{1,0:T(8,128)(2,1)S(1)} %add_convert_fusion.1), channel_id=1, source_target_pairs={{0,4},{1,5},{2,6},{3,7},{4,0},{5,1},{6,2},{7,3},{8,12},{9,13},{10,... | collective-permute-start | bytes 1179656 | tf_op jit(solution)/shard_map/ppermute | solution.py:352
  36.1 2.0 %collective-permute-start.10 = (bf16[256,768]{1,0:T(8,128)(2,1)S(1)}, bf16[256,768]{1,0:T(8,128)(2,1)S(1)}, u32[]{:S(2)}, u32[]{:S(2)}) collective-permute-start(bf16[256,768]{1,0:T(8,128)(2,1)S(1)} %add_convert_fusion), channel_id=1, source_target_pairs={{0,8},{8,0},{16,24},{24,16},{1,9},{9,1},{17,25},{25,17},{2,10},{10... | collective-permute-start | bytes 1179656 | tf_op jit(solution)/shard_map/ppermute | solution.py:352
  38.2 1.3 %shard_map.145 = (f32[2,64,1024]{2,1,0:T(8,128)S(1)}, bf16[64,1024]{1,0:T(8,128)(2,1)S(1)}, bf16[64,1024]{1,0:T(8,128)(2,1)S(1)}) custom-call(bf16[256,512]{1,0:T(8,128)(2,1)S(1)} %get-tuple-element.71.first_ref, bf16[256,512]{1,0:T(8,128)(2,1)S(1)} %get-tuple-element.87.last_ref, bf16[256,1024]{1,0:T(8,128)(2,1)S(1)} %get-tuple-element.70.ngv_ref, ...), custom_call_target="tpu_custom_call" | custom-call | flops 1 | bytes 1 | tf_op jit(solution)/shard_map/pallas_call | solution.py:28
  39.5 5.4 %collective-permute-done.8 = bf16[256,768]{1,0:T(8,128)(2,1)S(1)} collective-permute-done((bf16[256,768]{1,0:T(8,128)(2,1)S(1)}, bf16[256,768]{1,0:T(8,128)(2,1)S(1)}, u32[]{:S(2)}, u32[]{:S(2)}) %collective-permute-start.8) | collective-permute-done | bytes 393248 | tf_op jit(solution)/shard_map/ppermute | solution.py:352
  44.9 0.4 collective-permute-done.9
  45.3 1.8 %collective-permute-done.10 = bf16[256,768]{1,0:T(8,128)(2,1)S(1)} collective-permute-done((bf16[256,768]{1,0:T(8,128)(2,1)S(1)}, bf16[256,768]{1,0:T(8,128)(2,1)S(1)}, u32[]{:S(2)}, u32[]{:S(2)}) %collective-permute-start.10) | collective-permute-done | bytes 393248 | tf_op jit(solution)/shard_map/ppermute | solution.py:352
  47.0 1.0 %collective-permute-start.18 = (bf16[64,1024]{1,0:T(8,128)(2,1)S(1)}, bf16[64,1024]{1,0:T(8,128)(2,1)S(1)}, u32[]{:S(2)}, u32[]{:S(2)}) collective-permute-start(bf16[64,1024]{1,0:T(8,128)(2,1)S(1)} %get-tuple-element.98), channel_id=1, source_target_pairs={{0,7},{1,2},{2,1},{3,4},{4,3},{5,6},{6,5},{7,0},{8,15},{9,10},{10,... | collective-permute-start | bytes 393224 | tf_op jit(solution)/shard_map/ppermute | solution.py:479
  48.0 0.1 add_convert_fusion.4
  48.1 0.1 add_convert_fusion.3
  48.2 1.2 %collective-permute-start.15 = (bf16[128,768]{1,0:T(8,128)(2,1)S(1)}, bf16[128,768]{1,0:T(8,128)(2,1)S(1)}, u32[]{:S(2)}, u32[]{:S(2)}) collective-permute-start(bf16[128,768]{1,0:T(8,128)(2,1)S(1)} %add_convert_fusion.3), channel_id=1, source_target_pairs={{0,2},{1,3},{2,0},{3,1},{4,6},{5,7},{6,4},{7,5},{8,10},{9,11},{10,... | collective-permute-start | bytes 589832 | tf_op jit(solution)/shard_map/ppermute | solution.py:352
  49.4 1.7 %collective-permute-start.13 = (bf16[128,768]{1,0:T(8,128)(2,1)S(1)}, bf16[128,768]{1,0:T(8,128)(2,1)S(1)}, u32[]{:S(2)}, u32[]{:S(2)}) collective-permute-start(bf16[128,768]{1,0:T(8,128)(2,1)S(1)} %add_convert_fusion.4), channel_id=1, source_target_pairs={{0,8},{8,0},{16,24},{24,16},{1,9},{9,1},{17,25},{25,17},{2,10},{10... | collective-permute-start | bytes 589832 | tf_op jit(solution)/shard_map/ppermute | solution.py:352
  51.1 0.1 add_convert_fusion.5
  51.2 0.3 collective-permute-start.11
  51.6 5.2 %collective-permute-done.15 = bf16[128,768]{1,0:T(8,128)(2,1)S(1)} collective-permute-done((bf16[128,768]{1,0:T(8,128)(2,1)S(1)}, bf16[128,768]{1,0:T(8,128)(2,1)S(1)}, u32[]{:S(2)}, u32[]{:S(2)}) %collective-permute-start.15) | collective-permute-done | bytes 196640 | tf_op jit(solution)/shard_map/ppermute | solution.py:352
  56.8 0.9 %collective-permute-start.16 = (bf16[64,768]{1,0:T(8,128)(2,1)S(1)}, bf16[64,768]{1,0:T(8,128)(2,1)S(1)}, u32[]{:S(2)}, u32[]{:S(2)}) collective-permute-start(bf16[64,768]{1,0:T(8,128)(2,1)S(1)} %add_convert_fusion.6), channel_id=1, source_target_pairs={{0,4},{1,5},{2,6},{3,7},{4,0},{5,1},{6,2},{7,3},{8,12},{9,13},{10,... | collective-permute-start | bytes 294920 | tf_op jit(solution)/shard_map/ppermute | solution.py:352
  57.8 1.0 %collective-permute-start.14 = (bf16[64,768]{1,0:T(8,128)(2,1)S(1)}, bf16[64,768]{1,0:T(8,128)(2,1)S(1)}, u32[]{:S(2)}, u32[]{:S(2)}) collective-permute-start(bf16[64,768]{1,0:T(8,128)(2,1)S(1)} %add_convert_fusion.7), channel_id=1, source_target_pairs={{0,2},{1,3},{2,0},{3,1},{4,6},{5,7},{6,4},{7,5},{8,10},{9,11},{10,... | collective-permute-start | bytes 294920 | tf_op jit(solution)/shard_map/ppermute | solution.py:352
  58.8 1.8 %collective-permute-start.12 = (bf16[64,768]{1,0:T(8,128)(2,1)S(1)}, bf16[64,768]{1,0:T(8,128)(2,1)S(1)}, u32[]{:S(2)}, u32[]{:S(2)}) collective-permute-start(bf16[64,768]{1,0:T(8,128)(2,1)S(1)} %add_convert_fusion.8), channel_id=1, source_target_pairs={{0,8},{8,0},{16,24},{24,16},{1,9},{9,1},{17,25},{25,17},{2,10},{10... | collective-permute-start | bytes 294920 | tf_op jit(solution)/shard_map/ppermute | solution.py:352
  60.6 0.9 %collective-permute-done.16 = bf16[64,768]{1,0:T(8,128)(2,1)S(1)} collective-permute-done((bf16[64,768]{1,0:T(8,128)(2,1)S(1)}, bf16[64,768]{1,0:T(8,128)(2,1)S(1)}, u32[]{:S(2)}, u32[]{:S(2)}) %collective-permute-start.16) | collective-permute-done | bytes 98336 | tf_op jit(solution)/shard_map/ppermute | solution.py:352
  61.5 1.3 %collective-permute-done.14 = bf16[64,768]{1,0:T(8,128)(2,1)S(1)} collective-permute-done((bf16[64,768]{1,0:T(8,128)(2,1)S(1)}, bf16[64,768]{1,0:T(8,128)(2,1)S(1)}, u32[]{:S(2)}, u32[]{:S(2)}) %collective-permute-start.14) | collective-permute-done | bytes 98336 | tf_op jit(solution)/shard_map/ppermute | solution.py:352
  62.8 0.7 collective-permute-done.12
  63.5 0.1 convert_add_fusion.2
  63.5 0.1 convert_add_fusion
  63.7 2.9 %collective-permute-start.19 = (bf16[32,2304]{1,0:T(8,128)(2,1)S(1)}, bf16[32,2304]{1,0:T(8,128)(2,1)S(1)}, u32[]{:S(2)}, u32[]{:S(2)}) collective-permute-start(bf16[32,2304]{1,0:T(8,128)(2,1)S(1)} %slice.262), channel_id=1, source_target_pairs={{0,16},{8,24},{16,0},{24,8},{1,17},{9,25},{17,1},{25,9},{2,18},{10... | collective-permute-start | bytes 442376 | tf_op jit(solution)/shard_map/ppermute | solution.py:352
  66.6 1.1 %shard_map.146 = f32[2,64,1024]{2,1,0:T(8,128)} custom-call(f32[2,64,1024]{2,1,0:T(8,128)S(1)} %get-tuple-element.88.own_ref, bf16[64,1024]{1,0:T(8,128)(2,1)S(1)} %collective-permute-done.17.from_mate_ref, bf16[64,1024]{1,0:T(8,128)(2,1)S(1)} %collective-permute-done.18.from_other_ref, s32[2,32]{1,0:T(2,128)S(1)} %get-tuple-element.101.halo_ref), custom_call_target="tpu_custom_call" | custom-call | flops 1 | bytes 1 | tf_op jit(solution)/shard_map/pallas_call | solution.py:28
  67.7 4.7 %collective-permute-done.19.arrived_ref = bf16[32,2304]{1,0:T(8,128)(2,1)S(1)} collective-permute-done((bf16[32,2304]{1,0:T(8,128)(2,1)S(1)}, bf16[32,2304]{1,0:T(8,128)(2,1)S(1)}, u32[]{:S(2)}, u32[]{:S(2)}) %collective-permute-start.19) | collective-permute-done | bytes 147488 | tf_op jit(solution)/shard_map/ppermute | solution.py:352
  72.4 0.9 %shard_map.147 = (f32[32,2048]{1,0:T(8,128)}, f32[32,1024]{1,0:T(8,128)}, f32[32,100]{1,0:T(8,128)}) custom-call(f32[32,2304]{1,0:T(8,128)S(1)} %slice.220.own_ref, bf16[32,2304]{1,0:T(8,128)(2,1)S(1)} %collective-permute-done.19.arrived_ref, bf16[100,1024]{1,0:T(8,128)(2,1)S(1)} %bitcast.4), custom_call_target="tpu_custom_call" | custom-call | flops 1 | bytes 1 | tf_op jit(solution)/shard_map/pallas_call | solution.py:28
  (34 shorter events, 0.3 us)
Async XLA Ops:
  0.6 5.5 %copy-start.2 = (bf16[256,1024]{1,0:T(8,128)(2,1)S(1)}, bf16[256,1024]{1,0:T(8,128)(2,1)}, u32[]{:S(2)}) copy-start(bf16[256,1024]{1,0:T(8,128)(2,1)} %q_ref.7) | copy-start | bytes 1572868
  0.6 5.5 %copy-start.1 = (bf16[1024,1024]{1,0:T(8,128)(2,1)S(1)}, bf16[1024,1024]{1,0:T(8,128)(2,1)}, u32[]{:S(2)}) copy-start(bf16[1024,1024]{1,0:T(8,128)(2,1)} %wo_ref.3) | copy-start | bytes 6291460
  0.7 5.5 %copy-start.8 = (f32[100]{0:T(128)S(1)}, f32[100]{0:T(128)}, u32[]{:S(2)}) copy-start(f32[100]{0:T(128)} %param.19) | copy-start | bytes 1204
  0.7 5.5 %copy-start.7 = (f32[256]{0:T(256)S(1)}, f32[256]{0:T(256)}, u32[]{:S(2)}) copy-start(f32[256]{0:T(256)} %param.18) | copy-start | bytes 3076
  0.7 5.5 %copy-start.4 = (f32[100,256]{1,0:T(8,128)S(1)}, f32[100,256]{1,0:T(8,128)}, u32[]{:S(2)}) copy-start(f32[100,256]{1,0:T(8,128)} %init_ref.1) | copy-start | bytes 307204
  0.7 5.5 %copy-start.3 = (bf16[1024,100]{0,1:T(8,128)(2,1)S(1)}, bf16[1024,100]{0,1:T(8,128)(2,1)}, u32[]{:S(2)}) copy-start(bf16[1024,100]{0,1:T(8,128)(2,1)} %param.15) | copy-start | bytes 614404
  0.7 5.5 %copy-start = (bf16[1024,2048]{1,0:T(8,128)(2,1)S(1)}, bf16[1024,2048]{1,0:T(8,128)(2,1)}, u32[]{:S(2)}) copy-start(bf16[1024,2048]{1,0:T(8,128)(2,1)} %kvw_ref.5) | copy-start | bytes 12582916
  2.1 5.7 %collective-permute-start = (bf16[64,1024]{1,0:T(8,128)(2,1)S(1)}, bf16[64,1024]{1,0:T(8,128)(2,1)S(1)}, u32[]{:S(2)}, u32[]{:S(2)}) collective-permute-start(bf16[64,1024]{1,0:T(8,128)(2,1)S(1)} %get-tuple-element.56), channel_id=1, source_target_pairs={{0,1},{1,0},{2,3},{3,2},{4,5},{5,4},{6,7},{7,6},{8,9},{9,8},{10,11... | collective-permute-start | bytes 393224 | tf_op jit(solution)/shard_map/ppermute | solution.py:389
  2.6 6.8 %collective-permute-start.1 = (bf16[64,1024]{1,0:T(8,128)(2,1)S(1)}, bf16[64,1024]{1,0:T(8,128)(2,1)S(1)}, u32[]{:S(2)}, u32[]{:S(2)}) collective-permute-start(bf16[64,1024]{1,0:T(8,128)(2,1)S(1)} %get-tuple-element.57), channel_id=1, source_target_pairs={{0,7},{1,2},{2,1},{3,4},{4,3},{5,6},{6,5},{7,0},{8,15},{9,10},{10,... | collective-permute-start | bytes 393224 | tf_op jit(solution)/shard_map/ppermute | solution.py:390
  6.2 3.2 %copy-start.6 = (s32[3,256]{1,0:T(4,128)S(1)}, s32[3,256]{1,0:T(4,128)}, u32[]{:S(2)}) copy-start(s32[3,256]{1,0:T(4,128)} %src_ref.1) | copy-start | bytes 9220
  9.4 16.1 %copy-start.5 = (f32[100,256]{1,0:T(8,128)S(1)}, f32[100,256]{1,0:T(8,128)}, u32[]{:S(2)}) copy-start(f32[100,256]{1,0:T(8,128)} %refs_5_.1) | copy-start | bytes 307204
  12.4 5.2 %collective-permute-start.4 = (bf16[208,256]{1,0:T(8,128)(2,1)S(1)}, bf16[208,256]{1,0:T(8,128)(2,1)S(1)}, u32[]{:S(2)}, u32[]{:S(2)}) collective-permute-start(bf16[208,256]{1,0:T(8,128)(2,1)S(1)} %get-tuple-element.61), channel_id=1, source_target_pairs={{0,8},{8,0},{16,24},{24,16},{1,9},{9,1},{17,25},{25,17},{2,10},{10... | collective-permute-start | bytes 319496 | tf_op jit(solution)/shard_map/ppermute | solution.py:423
  14.3 11.2 %collective-permute-start.3 = (bf16[208,256]{1,0:T(8,128)(2,1)S(1)}, bf16[208,256]{1,0:T(8,128)(2,1)S(1)}, u32[]{:S(2)}, u32[]{:S(2)}) collective-permute-start(bf16[208,256]{1,0:T(8,128)(2,1)S(1)} %get-tuple-element.61), channel_id=1, source_target_pairs={{0,16},{8,24},{16,0},{24,8},{1,17},{9,25},{17,1},{25,9},{2,18},{10... | collective-permute-start | bytes 319496 | tf_op jit(solution)/shard_map/ppermute | solution.py:423
  16.9 8.6 %collective-permute-start.2 = (bf16[208,256]{1,0:T(8,128)(2,1)S(1)}, bf16[208,256]{1,0:T(8,128)(2,1)S(1)}, u32[]{:S(2)}, u32[]{:S(2)}) collective-permute-start(bf16[208,256]{1,0:T(8,128)(2,1)S(1)} %get-tuple-element.61), channel_id=1, source_target_pairs={{0,24},{8,16},{16,8},{24,0},{1,25},{9,17},{17,9},{25,1},{2,26},{10... | collective-permute-start | bytes 319496 | tf_op jit(solution)/shard_map/ppermute | solution.py:423
  27.3 4.0 %collective-permute-start.5 = (bf16[512,768]{1,0:T(8,128)(2,1)S(1)}, bf16[512,768]{1,0:T(8,128)(2,1)S(1)}, u32[]{:S(2)}, u32[]{:S(2)}) collective-permute-start(bf16[512,768]{1,0:T(8,128)(2,1)S(1)} %get-tuple-element.73), channel_id=1, source_target_pairs={{0,1},{1,0},{2,3},{3,2},{4,5},{5,4},{6,7},{7,6},{8,9},{9,8},{10,11... | collective-permute-start | bytes 2359304 | tf_op jit(solution)/shard_map/ppermute | solution.py:352
  28.9 2.5 %collective-permute-start.6 = (bf16[512,768]{1,0:T(8,128)(2,1)S(1)}, bf16[512,768]{1,0:T(8,128)(2,1)S(1)}, u32[]{:S(2)}, u32[]{:S(2)}) collective-permute-start(bf16[512,768]{1,0:T(8,128)(2,1)S(1)} %get-tuple-element.75), channel_id=1, source_target_pairs={{0,1},{1,0},{2,3},{3,2},{4,5},{5,4},{6,7},{7,6},{8,9},{9,8},{10,11... | collective-permute-start | bytes 2359304 | tf_op jit(solution)/shard_map/ppermute | solution.py:352
  31.2 2.4 %collective-permute-start.7 = (bf16[512,768]{1,0:T(8,128)(2,1)S(1)}, bf16[512,768]{1,0:T(8,128)(2,1)S(1)}, u32[]{:S(2)}, u32[]{:S(2)}) collective-permute-start(bf16[512,768]{1,0:T(8,128)(2,1)S(1)} %get-tuple-element.82), channel_id=1, source_target_pairs={{0,1},{1,0},{2,3},{3,2},{4,5},{5,4},{6,7},{7,6},{8,9},{9,8},{10,11... | collective-permute-start | bytes 2359304 | tf_op jit(solution)/shard_map/ppermute | solution.py:352
  33.7 11.2 %collective-permute-start.8 = (bf16[256,768]{1,0:T(8,128)(2,1)S(1)}, bf16[256,768]{1,0:T(8,128)(2,1)S(1)}, u32[]{:S(2)}, u32[]{:S(2)}) collective-permute-start(bf16[256,768]{1,0:T(8,128)(2,1)S(1)} %add_convert_fusion.2), channel_id=1, source_target_pairs={{0,2},{1,3},{2,0},{3,1},{4,6},{5,7},{6,4},{7,5},{8,10},{9,11},{10,... | collective-permute-start | bytes 1179656 | tf_op jit(solution)/shard_map/ppermute | solution.py:352
  33.9 11.3 %collective-permute-start.9 = (bf16[256,768]{1,0:T(8,128)(2,1)S(1)}, bf16[256,768]{1,0:T(8,128)(2,1)S(1)}, u32[]{:S(2)}, u32[]{:S(2)}) collective-permute-start(bf16[256,768]{1,0:T(8,128)(2,1)S(1)} %add_convert_fusion.1), channel_id=1, source_target_pairs={{0,4},{1,5},{2,6},{3,7},{4,0},{5,1},{6,2},{7,3},{8,12},{9,13},{10,... | collective-permute-start | bytes 1179656 | tf_op jit(solution)/shard_map/ppermute | solution.py:352
  36.1 10.9 %collective-permute-start.10 = (bf16[256,768]{1,0:T(8,128)(2,1)S(1)}, bf16[256,768]{1,0:T(8,128)(2,1)S(1)}, u32[]{:S(2)}, u32[]{:S(2)}) collective-permute-start(bf16[256,768]{1,0:T(8,128)(2,1)S(1)} %add_convert_fusion), channel_id=1, source_target_pairs={{0,8},{8,0},{16,24},{24,16},{1,9},{9,1},{17,25},{25,17},{2,10},{10... | collective-permute-start | bytes 1179656 | tf_op jit(solution)/shard_map/ppermute | solution.py:352
  47.0 13.6 %collective-permute-start.17 = (bf16[64,1024]{1,0:T(8,128)(2,1)S(1)}, bf16[64,1024]{1,0:T(8,128)(2,1)S(1)}, u32[]{:S(2)}, u32[]{:S(2)}) collective-permute-start(bf16[64,1024]{1,0:T(8,128)(2,1)S(1)} %get-tuple-element.97), channel_id=1, source_target_pairs={{0,1},{1,0},{2,3},{3,2},{4,5},{5,4},{6,7},{7,6},{8,9},{9,8},{10,11... | collective-permute-start | bytes 393224 | tf_op jit(solution)/shard_map/ppermute | solution.py:478
  47.0 13.6 %collective-permute-start.18 = (bf16[64,1024]{1,0:T(8,128)(2,1)S(1)}, bf16[64,1024]{1,0:T(8,128)(2,1)S(1)}, u32[]{:S(2)}, u32[]{:S(2)}) collective-permute-start(bf16[64,1024]{1,0:T(8,128)(2,1)S(1)} %get-tuple-element.98), channel_id=1, source_target_pairs={{0,7},{1,2},{2,1},{3,4},{4,3},{5,6},{6,5},{7,0},{8,15},{9,10},{10,... | collective-permute-start | bytes 393224 | tf_op jit(solution)/shard_map/ppermute | solution.py:479
  48.2 8.6 %collective-permute-start.15 = (bf16[128,768]{1,0:T(8,128)(2,1)S(1)}, bf16[128,768]{1,0:T(8,128)(2,1)S(1)}, u32[]{:S(2)}, u32[]{:S(2)}) collective-permute-start(bf16[128,768]{1,0:T(8,128)(2,1)S(1)} %add_convert_fusion.3), channel_id=1, source_target_pairs={{0,2},{1,3},{2,0},{3,1},{4,6},{5,7},{6,4},{7,5},{8,10},{9,11},{10,... | collective-permute-start | bytes 589832 | tf_op jit(solution)/shard_map/ppermute | solution.py:352
  49.4 8.3 %collective-permute-start.13 = (bf16[128,768]{1,0:T(8,128)(2,1)S(1)}, bf16[128,768]{1,0:T(8,128)(2,1)S(1)}, u32[]{:S(2)}, u32[]{:S(2)}) collective-permute-start(bf16[128,768]{1,0:T(8,128)(2,1)S(1)} %add_convert_fusion.4), channel_id=1, source_target_pairs={{0,8},{8,0},{16,24},{24,16},{1,9},{9,1},{17,25},{25,17},{2,10},{10... | collective-permute-start | bytes 589832 | tf_op jit(solution)/shard_map/ppermute | solution.py:352
  51.2 7.5 %collective-permute-start.11 = (bf16[128,768]{1,0:T(8,128)(2,1)S(1)}, bf16[128,768]{1,0:T(8,128)(2,1)S(1)}, u32[]{:S(2)}, u32[]{:S(2)}) collective-permute-start(bf16[128,768]{1,0:T(8,128)(2,1)S(1)} %add_convert_fusion.5), channel_id=1, source_target_pairs={{0,4},{1,5},{2,6},{3,7},{4,0},{5,1},{6,2},{7,3},{8,12},{9,13},{10,... | collective-permute-start | bytes 589832 | tf_op jit(solution)/shard_map/ppermute | solution.py:352
  56.8 4.7 %collective-permute-start.16 = (bf16[64,768]{1,0:T(8,128)(2,1)S(1)}, bf16[64,768]{1,0:T(8,128)(2,1)S(1)}, u32[]{:S(2)}, u32[]{:S(2)}) collective-permute-start(bf16[64,768]{1,0:T(8,128)(2,1)S(1)} %add_convert_fusion.6), channel_id=1, source_target_pairs={{0,4},{1,5},{2,6},{3,7},{4,0},{5,1},{6,2},{7,3},{8,12},{9,13},{10,... | collective-permute-start | bytes 294920 | tf_op jit(solution)/shard_map/ppermute | solution.py:352
  57.8 5.0 %collective-permute-start.14 = (bf16[64,768]{1,0:T(8,128)(2,1)S(1)}, bf16[64,768]{1,0:T(8,128)(2,1)S(1)}, u32[]{:S(2)}, u32[]{:S(2)}) collective-permute-start(bf16[64,768]{1,0:T(8,128)(2,1)S(1)} %add_convert_fusion.7), channel_id=1, source_target_pairs={{0,2},{1,3},{2,0},{3,1},{4,6},{5,7},{6,4},{7,5},{8,10},{9,11},{10,... | collective-permute-start | bytes 294920 | tf_op jit(solution)/shard_map/ppermute | solution.py:352
  58.8 4.7 %collective-permute-start.12 = (bf16[64,768]{1,0:T(8,128)(2,1)S(1)}, bf16[64,768]{1,0:T(8,128)(2,1)S(1)}, u32[]{:S(2)}, u32[]{:S(2)}) collective-permute-start(bf16[64,768]{1,0:T(8,128)(2,1)S(1)} %add_convert_fusion.8), channel_id=1, source_target_pairs={{0,8},{8,0},{16,24},{24,16},{1,9},{9,1},{17,25},{25,17},{2,10},{10... | collective-permute-start | bytes 294920 | tf_op jit(solution)/shard_map/ppermute | solution.py:352
  63.7 8.6 %collective-permute-start.19 = (bf16[32,2304]{1,0:T(8,128)(2,1)S(1)}, bf16[32,2304]{1,0:T(8,128)(2,1)S(1)}, u32[]{:S(2)}, u32[]{:S(2)}) collective-permute-start(bf16[32,2304]{1,0:T(8,128)(2,1)S(1)} %slice.262), channel_id=1, source_target_pairs={{0,16},{8,24},{16,0},{24,8},{1,17},{9,25},{17,1},{25,9},{2,18},{10... | collective-permute-start | bytes 442376 | tf_op jit(solution)/shard_map/ppermute | solution.py:352

commit v9 on v8

--- a/solution.py
+++ b/solution.py
@@ -473,11 +473,11 @@
             )
         arrived = [swap(out, *turn[step], count[turn[step][0]]) for out, turn in zip(outgoing, turns)]
         if step == 0:
-            arrived, back_mate, back_other = lax.optimization_barrier((arrived, back_mate, back_other))
+            from_mate = lax.ppermute(back_mate, "band", mates)
+            arrived, from_mate, back_other = lax.optimization_barrier((arrived, from_mate, back_other))
         if step == steps - 1:
-            from_mate = lax.ppermute(back_mate, "band", mates)
+            arrived, back_other = lax.optimization_barrier((arrived, back_other))
             from_other = lax.ppermute(back_other, "band", others)
-            arrived, from_mate, from_other = lax.optimization_barrier((arrived, from_mate, from_other))
         groups = [lower(terms) + [new] for terms, new in zip(groups, arrived)]
     hidden_grad = call(
         hidden_body,

time: 73.4 us -> 72 us (0.981)
  starting transfers between devices: 24.7 us -> 20.8 us
  waiting for transfers between devices: 32.3 us -> 34.8 us
    ppermute x1, waiting for transfers between devices: 0.01 us -> 5.91 us  [shards(): from_other = lax.ppermute(back_other, 'band', others)]
    ppermute x13, waiting for transfers between devices: 22.3 us -> 17.6 us  [swap(): return lax.ppermute(rows, axis, [(i, i ^ 1 << bit) for i in range(count)])]
    ppermute x13, starting transfers between devices: 15.1 us -> 12 us  [swap(): return lax.ppermute(rows, axis, [(i, i ^ 1 << bit) for i in range(count)])]
    ppermute x1, waiting for transfers between devices: 0.01 us -> 1.33 us  [shards(): from_mate = lax.ppermute(back_mate, 'band', mates)]
    ppermute x1, starting transfers between devices: 0.99 us -> 0.01 us  [shards(): from_other = lax.ppermute(back_other, 'band', others)]
  transfers between devices with their start and end apart: 20 -> 20, of which waited for: 12 -> 14; matrix products, arithmetic and copies ran while one was open for 1% -> 1% of each run, Pallas kernels for 10% -> 10%
where the time goes in v9:
time: 72 us; the launch traced here: 71.9 us
  waiting for transfers between devices  34.8 us (48%)
  starting transfers between devices  20.8 us (29%)
  Pallas kernels  14.4 us (20%)
  other arithmetic  0.96 us (1%)
  between operations  0.89 us (1%)
    ppermute x13, waiting for transfers between devices, swap(): return lax.ppermute(rows, axis, [(i, i ^ 1 << bit) for i in range(count)])  17.6 us
    pallas_call x10, Pallas kernels, call(): pl.pallas_call(body, out_shape=out_shape, in_specs=[pl.BlockSpec(memory_s...  14.4 us
    ppermute x13, starting transfers between devices, swap(): return lax.ppermute(rows, axis, [(i, i ^ 1 << bit) for i in range(count)])  12 us
    ppermute x3, waiting for transfers between devices, shards(): lax.ppermute(sent, 'member', [(i, i ^ s) for i in range(n_member)])  8.32 us
    ppermute x1, waiting for transfers between devices, shards(): from_other = lax.ppermute(back_other, 'band', others)  5.91 us
    ppermute x3, starting transfers between devices, shards(): lax.ppermute(sent, 'member', [(i, i ^ s) for i in range(n_member)])  4.58 us
    ppermute x1, starting transfers between devices, shards(): other = lax.ppermute(for_other, 'band', others)  3.56 us
    ppermute x1, waiting for transfers between devices, shards(): other = lax.ppermute(for_other, 'band', others)  1.63 us
  transfers between devices with their start and end apart: 20, of which 14 were waited for; matrix products, arithmetic and copies ran while one was open for 1% of the time, Pallas kernels for 10%

profile of v9, /device:TPU:0, one launch (start us, length us, event | category | flops | bytes accessed | tf_op | source)
XLA Modules:
  0.0 71.9 jit_solution(17839517549326171505)
XLA Ops:
  0.7 1.4 %shard_map.138 = (bf16[2,64,1024]{2,1,0:T(8,128)(2,1)S(1)}, s32[2,32]{1,0:T(2,128)S(1)}, bf16[64,1024]{1,0:T(8,128)(2,1)S(1)}, bf16[64,1024]{1,0:T(8,128)(2,1)S(1)}) custom-call(bf16[2,64,1024]{2,1,0:T(8,128)(2,1)} %hidden_hbm.1, s32[2,32]{1,0:T(2,128)} %halo_hbm.1), custom_call_target="tpu_custom_call" | custom-call | flops 10000000000 | bytes 1 | tf_op jit(solution)/shard_map/pallas_call | solution.py:28
  2.1 0.5 collective-permute-start
  2.6 3.6 %collective-permute-start.1 = (bf16[64,1024]{1,0:T(8,128)(2,1)S(1)}, bf16[64,1024]{1,0:T(8,128)(2,1)S(1)}, u32[]{:S(2)}, u32[]{:S(2)}) collective-permute-start(bf16[64,1024]{1,0:T(8,128)(2,1)S(1)} %get-tuple-element.56), channel_id=1, source_target_pairs={{0,7},{1,2},{2,1},{3,4},{4,3},{5,6},{6,5},{7,0},{8,15},{9,10},{10,... | collective-permute-start | bytes 393224 | tf_op jit(solution)/shard_map/ppermute | solution.py:390
  6.2 1.5 %shard_map.139 = (bf16[128,2048]{1,0:T(8,128)(2,1)S(1)}, bf16[1024,128]{1,0:T(8,128)(2,1)S(1)}, bf16[128,1024]{1,0:T(8,128)(2,1)S(1)}, f32[128,256]{1,0:T(8,128)S(1)}, f32[100,256]{1,0:T(8,128)S(1)}) custom-call(bf16[2,64,1024]{2,1,0:T(8,128)(2,1)S(1)} %get-tuple-element.57.hidden_ref, bf16[1024,1024]{1,0:T(8,128)(2,1)S(1)} %copy-done.1, ...), custom_call_target="tpu_custom_call" | custom-call | flops 1 | bytes 1 | tf_op jit(solution)/shard_map/pallas_call | solution.py:28
  7.8 1.6 %collective-permute-done.1.other_ref = bf16[64,1024]{1,0:T(8,128)(2,1)S(1)} collective-permute-done((bf16[64,1024]{1,0:T(8,128)(2,1)S(1)}, bf16[64,1024]{1,0:T(8,128)(2,1)S(1)}, u32[]{:S(2)}, u32[]{:S(2)}) %collective-permute-start.1) | collective-permute-done | bytes 131104 | tf_op jit(solution)/shard_map/ppermute | solution.py:390
  9.4 2.9 %shard_map.140 = (bf16[2,128,1024]{2,1,0:T(8,128)(2,1)S(1)}, bf16[8,2,256,256]{3,2,1,0:T(8,128)(2,1)S(1)}, bf16[8,2,256,256]{3,2,1,0:T(8,128)(2,1)S(1)}, bf16[2,...) custom-call(bf16[64,1024]{1,0:T(8,128)(2,1)S(1)} %collective-permute-done.mate_ref, ...), custom_call_target="tpu_custom_call" | custom-call | flops 1 | bytes 1 | tf_op jit(solution)/shard_map/pallas_call | solution.py:28
  12.4 2.0 %collective-permute-start.4 = (bf16[208,256]{1,0:T(8,128)(2,1)S(1)}, bf16[208,256]{1,0:T(8,128)(2,1)S(1)}, u32[]{:S(2)}, u32[]{:S(2)}) collective-permute-start(bf16[208,256]{1,0:T(8,128)(2,1)S(1)} %get-tuple-element.60), channel_id=1, source_target_pairs={{0,8},{8,0},{16,24},{24,16},{1,9},{9,1},{17,25},{25,17},{2,10},{10... | collective-permute-start | bytes 319496 | tf_op jit(solution)/shard_map/ppermute | solution.py:423
  14.3 2.6 %collective-permute-start.3 = (bf16[208,256]{1,0:T(8,128)(2,1)S(1)}, bf16[208,256]{1,0:T(8,128)(2,1)S(1)}, u32[]{:S(2)}, u32[]{:S(2)}) collective-permute-start(bf16[208,256]{1,0:T(8,128)(2,1)S(1)} %get-tuple-element.60), channel_id=1, source_target_pairs={{0,16},{8,24},{16,0},{24,8},{1,17},{9,25},{17,1},{25,9},{2,18},{10... | collective-permute-start | bytes 319496 | tf_op jit(solution)/shard_map/ppermute | solution.py:423
  16.9 0.3 shard_map.141.refs_9_.ext_ref
  17.2 0.4 collective-permute-done.4.refs_2_
  17.6 7.9 %collective-permute-done.3.refs_1_ = bf16[208,256]{1,0:T(8,128)(2,1)S(1)} collective-permute-done((bf16[208,256]{1,0:T(8,128)(2,1)S(1)}, bf16[208,256]{1,0:T(8,128)(2,1)S(1)}, u32[]{:S(2)}, u32[]{:S(2)}) %collective-permute-start.3) | collective-permute-done | bytes 106528 | tf_op jit(solution)/shard_map/ppermute | solution.py:423
  25.5 1.8 %shard_map.142 = (bf16[2,128,256]{2,1,0:T(8,128)(2,1)S(1)}, bf16[2,1024,256]{2,1,0:T(8,128)(2,1)S(1)}, bf16[256,1024]{1,0:T(8,128)(2,1)S(1)}, bf16[512,768]{1,0:T(8,128)(2,1)S(1)}, bf16[512,768]{1,0:T(8,128)(2,1)S(1)}) custom-call(bf16[208,256]{1,0:T(8,128)(2,1)S(1)} %collective-permute-done.2.refs_0_, bf16[208,256]{1,0:T(8,128)(2,1)S(1)} %collective-permute-done.3.refs_1_, ...), custom_call_target="tpu_custom_call" | custom-call | flops 1 | bytes 1 | tf_op jit(solution)/shard_map/pallas_call | solution.py:28
  27.3 0.1 collective-permute-start.5
  27.4 1.5 %shard_map.143 = (bf16[256,512]{1,0:T(8,128)(2,1)S(1)}, bf16[512,768]{1,0:T(8,128)(2,1)S(1)}, bf16[512,768]{1,0:T(8,128)(2,1)S(1)}) custom-call(bf16[2,1024,256]{2,1,0:T(8,128)(2,1)S(1)} %get-tuple-element.66.dm_ref, bf16[2,128,1024]{2,1,0:T(8,128)(2,1)S(1)} %get-tuple-element.67.value_ref, bf16[8,2,256,256]{3,2,1,0:T(8,128)(2,1)S(1)} %get-tuple-element.68.slope_ref, ...), custom_call_target="tpu_custom_call" | custom-call | flops 1 | bytes 1 | tf_op jit(solution)/shard_map/pallas_call | solution.py:28
  28.9 0.6 collective-permute-start.6
  29.4 1.8 %shard_map.144 = (bf16[256,512]{1,0:T(8,128)(2,1)S(1)}, bf16[512,768]{1,0:T(8,128)(2,1)S(1)}, bf16[512,768]{1,0:T(8,128)(2,1)S(1)}) custom-call(bf16[2,128,256]{2,1,0:T(8,128)(2,1)S(1)} %get-tuple-element.78.grad_ref, bf16[2,1024,256]{2,1,0:T(8,128)(2,1)S(1)} %get-tuple-element.66.dm_ref, bf16[2,128,1024]{2,1,0:T(8,128)(2,1)S(1)} %get-tuple-element.67.value_ref, ...), custom_call_target="tpu_custom_call" | custom-call | flops 1 | bytes 1 | tf_op jit(solution)/shard_map/pallas_call | solution.py:28
  31.2 0.1 collective-permute-start.7
  31.3 0.1 add_convert_fusion.2
  31.4 0.1 add_convert_fusion.1
  31.5 2.0 %collective-permute-done.7 = bf16[512,768]{1,0:T(8,128)(2,1)S(1)} collective-permute-done((bf16[512,768]{1,0:T(8,128)(2,1)S(1)}, bf16[512,768]{1,0:T(8,128)(2,1)S(1)}, u32[]{:S(2)}, u32[]{:S(2)}) %collective-permute-start.7) | collective-permute-done | bytes 786464 | tf_op jit(solution)/shard_map/ppermute | solution.py:352
  33.6 0.1 add_convert_fusion
  33.7 0.2 collective-permute-start.8
  33.9 2.2 %collective-permute-start.9 = (bf16[256,768]{1,0:T(8,128)(2,1)S(1)}, bf16[256,768]{1,0:T(8,128)(2,1)S(1)}, u32[]{:S(2)}, u32[]{:S(2)}) collective-permute-start(bf16[256,768]{1,0:T(8,128)(2,1)S(1)} %add_convert_fusion.1), channel_id=1, source_target_pairs={{0,4},{1,5},{2,6},{3,7},{4,0},{5,1},{6,2},{7,3},{8,12},{9,13},{10,... | collective-permute-start | bytes 1179656 | tf_op jit(solution)/shard_map/ppermute | solution.py:352
  36.1 2.0 %collective-permute-start.10 = (bf16[256,768]{1,0:T(8,128)(2,1)S(1)}, bf16[256,768]{1,0:T(8,128)(2,1)S(1)}, u32[]{:S(2)}, u32[]{:S(2)}) collective-permute-start(bf16[256,768]{1,0:T(8,128)(2,1)S(1)} %add_convert_fusion), channel_id=1, source_target_pairs={{0,8},{8,0},{16,24},{24,16},{1,9},{9,1},{17,25},{25,17},{2,10},{10... | collective-permute-start | bytes 1179656 | tf_op jit(solution)/shard_map/ppermute | solution.py:352
  38.2 1.3 %shard_map.145 = (f32[2,64,1024]{2,1,0:T(8,128)S(1)}, bf16[64,1024]{1,0:T(8,128)(2,1)S(1)}, bf16[64,1024]{1,0:T(8,128)(2,1)S(1)}) custom-call(bf16[256,512]{1,0:T(8,128)(2,1)S(1)} %get-tuple-element.70.first_ref, bf16[256,512]{1,0:T(8,128)(2,1)S(1)} %get-tuple-element.86.last_ref, bf16[256,1024]{1,0:T(8,128)(2,1)S(1)} %get-tuple-element.69.ngv_ref, ...), custom_call_target="tpu_custom_call" | custom-call | flops 1 | bytes 1 | tf_op jit(solution)/shard_map/pallas_call | solution.py:28
  39.6 1.3 %collective-permute-done.11.from_mate_ref = bf16[64,1024]{1,0:T(8,128)(2,1)S(1)} collective-permute-done((bf16[64,1024]{1,0:T(8,128)(2,1)S(1)}, bf16[64,1024]{1,0:T(8,128)(2,1)S(1)}, u32[]{:S(2)}, u32[]{:S(2)}) %collective-permute-start.11) | collective-permute-done | bytes 131104 | tf_op jit(solution)/shard_map/ppermute | solution.py:476
  40.9 4.0 %collective-permute-done.8 = bf16[256,768]{1,0:T(8,128)(2,1)S(1)} collective-permute-done((bf16[256,768]{1,0:T(8,128)(2,1)S(1)}, bf16[256,768]{1,0:T(8,128)(2,1)S(1)}, u32[]{:S(2)}, u32[]{:S(2)}) %collective-permute-start.8) | collective-permute-done | bytes 393248 | tf_op jit(solution)/shard_map/ppermute | solution.py:352
  44.9 0.4 collective-permute-done.9
  45.3 1.8 %collective-permute-done.10 = bf16[256,768]{1,0:T(8,128)(2,1)S(1)} collective-permute-done((bf16[256,768]{1,0:T(8,128)(2,1)S(1)}, bf16[256,768]{1,0:T(8,128)(2,1)S(1)}, u32[]{:S(2)}, u32[]{:S(2)}) %collective-permute-start.10) | collective-permute-done | bytes 393248 | tf_op jit(solution)/shard_map/ppermute | solution.py:352
  47.0 0.1 add_convert_fusion.4
  47.1 0.1 add_convert_fusion.3
  47.2 0.7 %collective-permute-start.16 = (bf16[128,768]{1,0:T(8,128)(2,1)S(1)}, bf16[128,768]{1,0:T(8,128)(2,1)S(1)}, u32[]{:S(2)}, u32[]{:S(2)}) collective-permute-start(bf16[128,768]{1,0:T(8,128)(2,1)S(1)} %add_convert_fusion.3), channel_id=1, source_target_pairs={{0,2},{1,3},{2,0},{3,1},{4,6},{5,7},{6,4},{7,5},{8,10},{9,11},{10,... | collective-permute-start | bytes 589832 | tf_op jit(solution)/shard_map/ppermute | solution.py:352
  47.9 1.7 %collective-permute-start.14 = (bf16[128,768]{1,0:T(8,128)(2,1)S(1)}, bf16[128,768]{1,0:T(8,128)(2,1)S(1)}, u32[]{:S(2)}, u32[]{:S(2)}) collective-permute-start(bf16[128,768]{1,0:T(8,128)(2,1)S(1)} %add_convert_fusion.4), channel_id=1, source_target_pairs={{0,8},{8,0},{16,24},{24,16},{1,9},{9,1},{17,25},{25,17},{2,10},{10... | collective-permute-start | bytes 589832 | tf_op jit(solution)/shard_map/ppermute | solution.py:352
  49.6 0.1 add_convert_fusion.5
  49.7 0.9 %collective-permute-start.12 = (bf16[128,768]{1,0:T(8,128)(2,1)S(1)}, bf16[128,768]{1,0:T(8,128)(2,1)S(1)}, u32[]{:S(2)}, u32[]{:S(2)}) collective-permute-start(bf16[128,768]{1,0:T(8,128)(2,1)S(1)} %add_convert_fusion.5), channel_id=1, source_target_pairs={{0,4},{1,5},{2,6},{3,7},{4,0},{5,1},{6,2},{7,3},{8,12},{9,13},{10,... | collective-permute-start | bytes 589832 | tf_op jit(solution)/shard_map/ppermute | solution.py:352
  50.6 2.5 %collective-permute-done.16 = bf16[128,768]{1,0:T(8,128)(2,1)S(1)} collective-permute-done((bf16[128,768]{1,0:T(8,128)(2,1)S(1)}, bf16[128,768]{1,0:T(8,128)(2,1)S(1)}, u32[]{:S(2)}, u32[]{:S(2)}) %collective-permute-start.16) | collective-permute-done | bytes 196640 | tf_op jit(solution)/shard_map/ppermute | solution.py:352
  53.1 0.7 collective-permute-start.17
  53.9 1.2 %collective-permute-start.15 = (bf16[64,768]{1,0:T(8,128)(2,1)S(1)}, bf16[64,768]{1,0:T(8,128)(2,1)S(1)}, u32[]{:S(2)}, u32[]{:S(2)}) collective-permute-start(bf16[64,768]{1,0:T(8,128)(2,1)S(1)} %add_convert_fusion.7), channel_id=1, source_target_pairs={{0,2},{1,3},{2,0},{3,1},{4,6},{5,7},{6,4},{7,5},{8,10},{9,11},{10,... | collective-permute-start | bytes 294920 | tf_op jit(solution)/shard_map/ppermute | solution.py:352
  55.1 1.4 %collective-permute-done.12 = bf16[128,768]{1,0:T(8,128)(2,1)S(1)} collective-permute-done((bf16[128,768]{1,0:T(8,128)(2,1)S(1)}, bf16[128,768]{1,0:T(8,128)(2,1)S(1)}, u32[]{:S(2)}, u32[]{:S(2)}) %collective-permute-start.12) | collective-permute-done | bytes 196640 | tf_op jit(solution)/shard_map/ppermute | solution.py:352
  56.5 0.4 collective-permute-start.13
  57.0 0.8 %collective-permute-done.17 = bf16[64,768]{1,0:T(8,128)(2,1)S(1)} collective-permute-done((bf16[64,768]{1,0:T(8,128)(2,1)S(1)}, bf16[64,768]{1,0:T(8,128)(2,1)S(1)}, u32[]{:S(2)}, u32[]{:S(2)}) %collective-permute-start.17) | collective-permute-done | bytes 98336 | tf_op jit(solution)/shard_map/ppermute | solution.py:352
  57.8 0.7 %collective-permute-done.15 = bf16[64,768]{1,0:T(8,128)(2,1)S(1)} collective-permute-done((bf16[64,768]{1,0:T(8,128)(2,1)S(1)}, bf16[64,768]{1,0:T(8,128)(2,1)S(1)}, u32[]{:S(2)}, u32[]{:S(2)}) %collective-permute-start.15) | collective-permute-done | bytes 98336 | tf_op jit(solution)/shard_map/ppermute | solution.py:352
  58.5 4.0 %collective-permute-done.13 = bf16[64,768]{1,0:T(8,128)(2,1)S(1)} collective-permute-done((bf16[64,768]{1,0:T(8,128)(2,1)S(1)}, bf16[64,768]{1,0:T(8,128)(2,1)S(1)}, u32[]{:S(2)}, u32[]{:S(2)}) %collective-permute-start.13) | collective-permute-done | bytes 98336 | tf_op jit(solution)/shard_map/ppermute | solution.py:352
  62.6 0.1 convert_add_fusion
  62.8 1.2 %collective-permute-start.19 = (bf16[32,2304]{1,0:T(8,128)(2,1)S(1)}, bf16[32,2304]{1,0:T(8,128)(2,1)S(1)}, u32[]{:S(2)}, u32[]{:S(2)}) collective-permute-start(bf16[32,2304]{1,0:T(8,128)(2,1)S(1)} %slice.262), channel_id=1, source_target_pairs={{0,16},{8,24},{16,0},{24,8},{1,17},{9,25},{17,1},{25,9},{2,18},{10... | collective-permute-start | bytes 442376 | tf_op jit(solution)/shard_map/ppermute | solution.py:352
  64.0 5.9 %collective-permute-done.18.from_other_ref = bf16[64,1024]{1,0:T(8,128)(2,1)S(1)} collective-permute-done((bf16[64,1024]{1,0:T(8,128)(2,1)S(1)}, bf16[64,1024]{1,0:T(8,128)(2,1)S(1)}, u32[]{:S(2)}, u32[]{:S(2)}) %collective-permute-start.18) | collective-permute-done | bytes 131104 | tf_op jit(solution)/shard_map/ppermute | solution.py:480
  69.9 1.1 %shard_map.146 = f32[2,64,1024]{2,1,0:T(8,128)} custom-call(f32[2,64,1024]{2,1,0:T(8,128)S(1)} %get-tuple-element.87.own_ref, bf16[64,1024]{1,0:T(8,128)(2,1)S(1)} %collective-permute-done.11.from_mate_ref, bf16[64,1024]{1,0:T(8,128)(2,1)S(1)} %collective-permute-done.18.from_other_ref, s32[2,32]{1,0:T(2,128)S(1)} %get-tuple-element.99.halo_ref), custom_call_target="tpu_custom_call" | custom-call | flops 1 | bytes 1 | tf_op jit(solution)/shard_map/pallas_call | solution.py:28
  71.0 0.9 %shard_map.147 = (f32[32,2048]{1,0:T(8,128)}, f32[32,1024]{1,0:T(8,128)}, f32[32,100]{1,0:T(8,128)}) custom-call(f32[32,2304]{1,0:T(8,128)S(1)} %slice.220.own_ref, bf16[32,2304]{1,0:T(8,128)(2,1)S(1)} %collective-permute-done.19.arrived_ref, bf16[100,1024]{1,0:T(8,128)(2,1)S(1)} %bitcast.4), custom_call_target="tpu_custom_call" | custom-call | flops 1 | bytes 1 | tf_op jit(solution)/shard_map/pallas_call | solution.py:28
  (34 shorter events, 0.4 us)
Async XLA Ops:
  0.6 5.5 %copy-start.2 = (bf16[256,1024]{1,0:T(8,128)(2,1)S(1)}, bf16[256,1024]{1,0:T(8,128)(2,1)}, u32[]{:S(2)}) copy-start(bf16[256,1024]{1,0:T(8,128)(2,1)} %q_ref.7) | copy-start | bytes 1572868
  0.6 5.5 %copy-start.1 = (bf16[1024,1024]{1,0:T(8,128)(2,1)S(1)}, bf16[1024,1024]{1,0:T(8,128)(2,1)}, u32[]{:S(2)}) copy-start(bf16[1024,1024]{1,0:T(8,128)(2,1)} %wo_ref.3) | copy-start | bytes 6291460
  0.7 5.5 %copy-start.8 = (f32[100]{0:T(128)S(1)}, f32[100]{0:T(128)}, u32[]{:S(2)}) copy-start(f32[100]{0:T(128)} %param.19) | copy-start | bytes 1204
  0.7 5.5 %copy-start.7 = (f32[256]{0:T(256)S(1)}, f32[256]{0:T(256)}, u32[]{:S(2)}) copy-start(f32[256]{0:T(256)} %param.18) | copy-start | bytes 3076
  0.7 5.5 %copy-start.4 = (f32[100,256]{1,0:T(8,128)S(1)}, f32[100,256]{1,0:T(8,128)}, u32[]{:S(2)}) copy-start(f32[100,256]{1,0:T(8,128)} %init_ref.1) | copy-start | bytes 307204
  0.7 5.5 %copy-start.3 = (bf16[1024,100]{0,1:T(8,128)(2,1)S(1)}, bf16[1024,100]{0,1:T(8,128)(2,1)}, u32[]{:S(2)}) copy-start(bf16[1024,100]{0,1:T(8,128)(2,1)} %param.15) | copy-start | bytes 614404
  0.7 5.5 %copy-start = (bf16[1024,2048]{1,0:T(8,128)(2,1)S(1)}, bf16[1024,2048]{1,0:T(8,128)(2,1)}, u32[]{:S(2)}) copy-start(bf16[1024,2048]{1,0:T(8,128)(2,1)} %kvw_ref.5) | copy-start | bytes 12582916
  2.1 5.7 %collective-permute-start = (bf16[64,1024]{1,0:T(8,128)(2,1)S(1)}, bf16[64,1024]{1,0:T(8,128)(2,1)S(1)}, u32[]{:S(2)}, u32[]{:S(2)}) collective-permute-start(bf16[64,1024]{1,0:T(8,128)(2,1)S(1)} %get-tuple-element.55), channel_id=1, source_target_pairs={{0,1},{1,0},{2,3},{3,2},{4,5},{5,4},{6,7},{7,6},{8,9},{9,8},{10,11... | collective-permute-start | bytes 393224 | tf_op jit(solution)/shard_map/ppermute | solution.py:389
  2.6 6.8 %collective-permute-start.1 = (bf16[64,1024]{1,0:T(8,128)(2,1)S(1)}, bf16[64,1024]{1,0:T(8,128)(2,1)S(1)}, u32[]{:S(2)}, u32[]{:S(2)}) collective-permute-start(bf16[64,1024]{1,0:T(8,128)(2,1)S(1)} %get-tuple-element.56), channel_id=1, source_target_pairs={{0,7},{1,2},{2,1},{3,4},{4,3},{5,6},{6,5},{7,0},{8,15},{9,10},{10,... | collective-permute-start | bytes 393224 | tf_op jit(solution)/shard_map/ppermute | solution.py:390
  6.2 3.2 %copy-start.6 = (s32[3,256]{1,0:T(4,128)S(1)}, s32[3,256]{1,0:T(4,128)}, u32[]{:S(2)}) copy-start(s32[3,256]{1,0:T(4,128)} %src_ref.1) | copy-start | bytes 9220
  9.4 16.1 %copy-start.5 = (f32[100,256]{1,0:T(8,128)S(1)}, f32[100,256]{1,0:T(8,128)}, u32[]{:S(2)}) copy-start(f32[100,256]{1,0:T(8,128)} %refs_5_.1) | copy-start | bytes 307204
  12.4 5.2 %collective-permute-start.4 = (bf16[208,256]{1,0:T(8,128)(2,1)S(1)}, bf16[208,256]{1,0:T(8,128)(2,1)S(1)}, u32[]{:S(2)}, u32[]{:S(2)}) collective-permute-start(bf16[208,256]{1,0:T(8,128)(2,1)S(1)} %get-tuple-element.60), channel_id=1, source_target_pairs={{0,8},{8,0},{16,24},{24,16},{1,9},{9,1},{17,25},{25,17},{2,10},{10... | collective-permute-start | bytes 319496 | tf_op jit(solution)/shard_map/ppermute | solution.py:423
  14.3 11.2 %collective-permute-start.3 = (bf16[208,256]{1,0:T(8,128)(2,1)S(1)}, bf16[208,256]{1,0:T(8,128)(2,1)S(1)}, u32[]{:S(2)}, u32[]{:S(2)}) collective-permute-start(bf16[208,256]{1,0:T(8,128)(2,1)S(1)} %get-tuple-element.60), channel_id=1, source_target_pairs={{0,16},{8,24},{16,0},{24,8},{1,17},{9,25},{17,1},{25,9},{2,18},{10... | collective-permute-start | bytes 319496 | tf_op jit(solution)/shard_map/ppermute | solution.py:423
  16.9 8.6 %collective-permute-start.2 = (bf16[208,256]{1,0:T(8,128)(2,1)S(1)}, bf16[208,256]{1,0:T(8,128)(2,1)S(1)}, u32[]{:S(2)}, u32[]{:S(2)}) collective-permute-start(bf16[208,256]{1,0:T(8,128)(2,1)S(1)} %get-tuple-element.60), channel_id=1, source_target_pairs={{0,24},{8,16},{16,8},{24,0},{1,25},{9,17},{17,9},{25,1},{2,26},{10... | collective-permute-start | bytes 319496 | tf_op jit(solution)/shard_map/ppermute | solution.py:423
  27.3 4.0 %collective-permute-start.5 = (bf16[512,768]{1,0:T(8,128)(2,1)S(1)}, bf16[512,768]{1,0:T(8,128)(2,1)S(1)}, u32[]{:S(2)}, u32[]{:S(2)}) collective-permute-start(bf16[512,768]{1,0:T(8,128)(2,1)S(1)} %get-tuple-element.72), channel_id=1, source_target_pairs={{0,1},{1,0},{2,3},{3,2},{4,5},{5,4},{6,7},{7,6},{8,9},{9,8},{10,11... | collective-permute-start | bytes 2359304 | tf_op jit(solution)/shard_map/ppermute | solution.py:352
  28.9 2.5 %collective-permute-start.6 = (bf16[512,768]{1,0:T(8,128)(2,1)S(1)}, bf16[512,768]{1,0:T(8,128)(2,1)S(1)}, u32[]{:S(2)}, u32[]{:S(2)}) collective-permute-start(bf16[512,768]{1,0:T(8,128)(2,1)S(1)} %get-tuple-element.74), channel_id=1, source_target_pairs={{0,1},{1,0},{2,3},{3,2},{4,5},{5,4},{6,7},{7,6},{8,9},{9,8},{10,11... | collective-permute-start | bytes 2359304 | tf_op jit(solution)/shard_map/ppermute | solution.py:352
  31.2 2.4 %collective-permute-start.7 = (bf16[512,768]{1,0:T(8,128)(2,1)S(1)}, bf16[512,768]{1,0:T(8,128)(2,1)S(1)}, u32[]{:S(2)}, u32[]{:S(2)}) collective-permute-start(bf16[512,768]{1,0:T(8,128)(2,1)S(1)} %get-tuple-element.81), channel_id=1, source_target_pairs={{0,1},{1,0},{2,3},{3,2},{4,5},{5,4},{6,7},{7,6},{8,9},{9,8},{10,11... | collective-permute-start | bytes 2359304 | tf_op jit(solution)/shard_map/ppermute | solution.py:352
  33.7 11.2 %collective-permute-start.8 = (bf16[256,768]{1,0:T(8,128)(2,1)S(1)}, bf16[256,768]{1,0:T(8,128)(2,1)S(1)}, u32[]{:S(2)}, u32[]{:S(2)}) collective-permute-start(bf16[256,768]{1,0:T(8,128)(2,1)S(1)} %add_convert_fusion.2), channel_id=1, source_target_pairs={{0,2},{1,3},{2,0},{3,1},{4,6},{5,7},{6,4},{7,5},{8,10},{9,11},{10,... | collective-permute-start | bytes 1179656 | tf_op jit(solution)/shard_map/ppermute | solution.py:352
  33.9 11.3 %collective-permute-start.9 = (bf16[256,768]{1,0:T(8,128)(2,1)S(1)}, bf16[256,768]{1,0:T(8,128)(2,1)S(1)}, u32[]{:S(2)}, u32[]{:S(2)}) collective-permute-start(bf16[256,768]{1,0:T(8,128)(2,1)S(1)} %add_convert_fusion.1), channel_id=1, source_target_pairs={{0,4},{1,5},{2,6},{3,7},{4,0},{5,1},{6,2},{7,3},{8,12},{9,13},{10,... | collective-permute-start | bytes 1179656 | tf_op jit(solution)/shard_map/ppermute | solution.py:352
  36.1 10.9 %collective-permute-start.10 = (bf16[256,768]{1,0:T(8,128)(2,1)S(1)}, bf16[256,768]{1,0:T(8,128)(2,1)S(1)}, u32[]{:S(2)}, u32[]{:S(2)}) collective-permute-start(bf16[256,768]{1,0:T(8,128)(2,1)S(1)} %add_convert_fusion), channel_id=1, source_target_pairs={{0,8},{8,0},{16,24},{24,16},{1,9},{9,1},{17,25},{25,17},{2,10},{10... | collective-permute-start | bytes 1179656 | tf_op jit(solution)/shard_map/ppermute | solution.py:352
  39.5 1.4 %collective-permute-start.11 = (bf16[64,1024]{1,0:T(8,128)(2,1)S(1)}, bf16[64,1024]{1,0:T(8,128)(2,1)S(1)}, u32[]{:S(2)}, u32[]{:S(2)}) collective-permute-start(bf16[64,1024]{1,0:T(8,128)(2,1)S(1)} %get-tuple-element.91), channel_id=1, source_target_pairs={{0,1},{1,0},{2,3},{3,2},{4,5},{5,4},{6,7},{7,6},{8,9},{9,8},{10,11... | collective-permute-start | bytes 393224 | tf_op jit(solution)/shard_map/ppermute | solution.py:476
  47.2 5.9 %collective-permute-start.16 = (bf16[128,768]{1,0:T(8,128)(2,1)S(1)}, bf16[128,768]{1,0:T(8,128)(2,1)S(1)}, u32[]{:S(2)}, u32[]{:S(2)}) collective-permute-start(bf16[128,768]{1,0:T(8,128)(2,1)S(1)} %add_convert_fusion.3), channel_id=1, source_target_pairs={{0,2},{1,3},{2,0},{3,1},{4,6},{5,7},{6,4},{7,5},{8,10},{9,11},{10,... | collective-permute-start | bytes 589832 | tf_op jit(solution)/shard_map/ppermute | solution.py:352
  47.9 5.9 %collective-permute-start.14 = (bf16[128,768]{1,0:T(8,128)(2,1)S(1)}, bf16[128,768]{1,0:T(8,128)(2,1)S(1)}, u32[]{:S(2)}, u32[]{:S(2)}) collective-permute-start(bf16[128,768]{1,0:T(8,128)(2,1)S(1)} %add_convert_fusion.4), channel_id=1, source_target_pairs={{0,8},{8,0},{16,24},{24,16},{1,9},{9,1},{17,25},{25,17},{2,10},{10... | collective-permute-start | bytes 589832 | tf_op jit(solution)/shard_map/ppermute | solution.py:352
  49.7 6.8 %collective-permute-start.12 = (bf16[128,768]{1,0:T(8,128)(2,1)S(1)}, bf16[128,768]{1,0:T(8,128)(2,1)S(1)}, u32[]{:S(2)}, u32[]{:S(2)}) collective-permute-start(bf16[128,768]{1,0:T(8,128)(2,1)S(1)} %add_convert_fusion.5), channel_id=1, source_target_pairs={{0,4},{1,5},{2,6},{3,7},{4,0},{5,1},{6,2},{7,3},{8,12},{9,13},{10,... | collective-permute-start | bytes 589832 | tf_op jit(solution)/shard_map/ppermute | solution.py:352
  53.1 4.7 %collective-permute-start.17 = (bf16[64,768]{1,0:T(8,128)(2,1)S(1)}, bf16[64,768]{1,0:T(8,128)(2,1)S(1)}, u32[]{:S(2)}, u32[]{:S(2)}) collective-permute-start(bf16[64,768]{1,0:T(8,128)(2,1)S(1)} %add_convert_fusion.6), channel_id=1, source_target_pairs={{0,4},{1,5},{2,6},{3,7},{4,0},{5,1},{6,2},{7,3},{8,12},{9,13},{10,... | collective-permute-start | bytes 294920 | tf_op jit(solution)/shard_map/ppermute | solution.py:352
  53.9 4.7 %collective-permute-start.15 = (bf16[64,768]{1,0:T(8,128)(2,1)S(1)}, bf16[64,768]{1,0:T(8,128)(2,1)S(1)}, u32[]{:S(2)}, u32[]{:S(2)}) collective-permute-start(bf16[64,768]{1,0:T(8,128)(2,1)S(1)} %add_convert_fusion.7), channel_id=1, source_target_pairs={{0,2},{1,3},{2,0},{3,1},{4,6},{5,7},{6,4},{7,5},{8,10},{9,11},{10,... | collective-permute-start | bytes 294920 | tf_op jit(solution)/shard_map/ppermute | solution.py:352
  56.5 6.0 %collective-permute-start.13 = (bf16[64,768]{1,0:T(8,128)(2,1)S(1)}, bf16[64,768]{1,0:T(8,128)(2,1)S(1)}, u32[]{:S(2)}, u32[]{:S(2)}) collective-permute-start(bf16[64,768]{1,0:T(8,128)(2,1)S(1)} %add_convert_fusion.8), channel_id=1, source_target_pairs={{0,8},{8,0},{16,24},{24,16},{1,9},{9,1},{17,25},{25,17},{2,10},{10... | collective-permute-start | bytes 294920 | tf_op jit(solution)/shard_map/ppermute | solution.py:352
  62.8 8.2 %collective-permute-start.19 = (bf16[32,2304]{1,0:T(8,128)(2,1)S(1)}, bf16[32,2304]{1,0:T(8,128)(2,1)S(1)}, u32[]{:S(2)}, u32[]{:S(2)}) collective-permute-start(bf16[32,2304]{1,0:T(8,128)(2,1)S(1)} %slice.262), channel_id=1, source_target_pairs={{0,16},{8,24},{16,0},{24,8},{1,17},{9,25},{17,1},{25,9},{2,18},{10... | collective-permute-start | bytes 442376 | tf_op jit(solution)/shard_map/ppermute | solution.py:352
  64.0 5.9 %collective-permute-start.18 = (bf16[64,1024]{1,0:T(8,128)(2,1)S(1)}, bf16[64,1024]{1,0:T(8,128)(2,1)S(1)}, u32[]{:S(2)}, u32[]{:S(2)}) collective-permute-start(bf16[64,1024]{1,0:T(8,128)(2,1)S(1)} %get-tuple-element.98), channel_id=1, source_target_pairs={{0,7},{1,2},{2,1},{3,4},{4,3},{5,6},{6,5},{7,0},{8,15},{9,10},{10,... | collective-permute-start | bytes 393224 | tf_op jit(solution)/shard_map/ppermute | solution.py:480

commit v10 on v9

--- a/solution.py
+++ b/solution.py
@@ -71,11 +71,69 @@
             out_ref[m * rim : (m + 1) * rim, :] = mm(hot, hidden_ref[m], TN).astype(BF)
 
 
-def prepare_body(
-    hidden_ref, wo_ref, hp_ref, q_ref, kvw_ref, init_ref, chw_ref, lat_ref,
-    kv_ref, pt_ref, p_ref, base_ref, weight_ref, chw_pad, hp_pad,
+def split_heads(block):
+    low = lax.broadcasted_iota(jnp.int32, block.shape, 1) < HEAD_DIM
+    zero = jnp.zeros_like(block)
+    return jnp.concatenate([jnp.where(low, block, zero), jnp.where(low, zero, block)], axis=0)
+
+
+def half_mask_of(src, first, count):
+    rows = lax.broadcasted_iota(jnp.int32, (count, src.shape[1]), 0) + first
+    mask = rows == src[0:1, :]
+    for e in range(1, src.shape[0]):
+        mask = mask | (rows == src[e : e + 1, :])
+    half = jnp.where(mask, 0.5, 0.0).astype(F32)
+    return jnp.concatenate([half, half], axis=0)
+
+
+def gate_rows(tasks, keys, values, q_ref, half_mask, gate_ref, slope_ref, store_merged):
+    half_scale = 0.5 * HEAD_DIM ** (-0.5)
+
+    def scores(pair, m):
+        q = (q_ref[:, pair * LANES : (pair + 1) * LANES].astype(F32) * half_scale).astype(BF)
+        return mm(split_heads(keys(pair, m)), q, NT)
+
+    ahead = scores(*tasks[0])
+    for i, (pair, m) in enumerate(tasks):
+        current = ahead
+        if i + 1 < len(tasks):
+            ahead = scores(*tasks[i + 1])
+        turned = split_heads(values(pair, m)).astype(F32).T.astype(BF)
+        gate = jnp.tanh(current) * half_mask + half_mask
+        rounded = gate.astype(BF)
+        gate_ref[pair, m] = rounded
+        slope_ref[pair, m] = (gate - gate * gate).astype(BF)
+        store_merged(pair, m, mm(turned, rounded))
+
+
+def tasks_of(width, members):
+    return [(pair, m) for pair in range(width // LANES) for m in range(members)]
+
+
+def own_body(
+    hidden_ref, wo_ref, hp_ref, q_ref, kvw_ref, init_ref, chw_ref, lat_ref, src_ref,
+    value_ref, gate_ref, slope_ref, merged_ref, pt_ref, p_ref, base_ref, weight_ref, chw_pad, hp_pad,
 ):
     channels = hp_ref.shape[0]
+    members, nodes, width = hidden_ref.shape
+    hidden = jnp.concatenate([hidden_ref[m] for m in range(members)], axis=0)
+    rows = mm(hidden, kvw_ref[...]).astype(BF)
+
+    def part(pair, m, first):
+        at = first + pair * LANES
+        return rows[m * nodes : (m + 1) * nodes, at : at + LANES]
+
+    def store_merged(pair, m, result):
+        merged_ref[m, pair * LANES : (pair + 1) * LANES, :] = result
+
+    for m in range(members):
+        value_ref[m] = rows[m * nodes : (m + 1) * nodes, width:]
+    gate_rows(
+        tasks_of(width, members),
+        lambda pair, m: part(pair, m, 0),
+        lambda pair, m: part(pair, m, width),
+        q_ref, half_mask_of(src_ref[...], 0, nodes), gate_ref, slope_ref, store_merged,
+    )
     hp_pad[...] = jnp.zeros_like(hp_pad)
     hp_pad[0:channels, :] = hp_ref[...].astype(F32)
     hp_t = hp_pad[...].astype(BF)
@@ -86,85 +144,47 @@
     p = mm(hp_t, wo_ref[...], NT)
     p_ref[...] = p.astype(BF)
     pt_ref[...] = p.T.astype(BF)
-    hidden = jnp.concatenate([hidden_ref[m] for m in range(hidden_ref.shape[0])], axis=0)
-    kv_ref[...] = mm(hidden, kvw_ref[...]).astype(BF)
-
-
-def split_heads(block):
-    low = lax.broadcasted_iota(jnp.int32, block.shape, 1) < HEAD_DIM
-    zero = jnp.zeros_like(block)
-    return jnp.concatenate([jnp.where(low, block, zero), jnp.where(low, zero, block)], axis=0)
-
-
-def forward_body(
-    send_rows, mate_ref, other_ref, own_ref, kvw_ref, q_ref, src_ref, p_ref,
+
+
+def halo_body(
+    send_rows, nodes, other_ref, mate_ref, own_ref, kvw_ref, q_ref, src_ref, p_ref,
     value_ref, gate_ref, slope_ref, merged_ref, part_ref, send_ref,
 ):
-    members, ext, width = value_ref.shape
+    members, count, width = value_ref.shape
     points = q_ref.shape[0]
-    nodes = own_ref.shape[0] // members
-    rim = mate_ref.shape[0] // members
+    rim = count // 2
     step = 2 * LANES
     halo_rows = jnp.concatenate([mate_ref[...], other_ref[...]], axis=0)
 
-    def project(start):
-        halo = mm(halo_rows, kvw_ref[:, start : start + step]).astype(BF)
-        result = []
-        for m in range(members):
-            own = own_ref[m * nodes : (m + 1) * nodes, start : start + step]
-            mate = halo[m * rim : (m + 1) * rim]
-            other = halo[(members + m) * rim : (members + m + 1) * rim]
-            result.append(jnp.concatenate([own, mate, other], axis=0))
-        return result
-
-    rows = lax.broadcasted_iota(jnp.int32, (ext, points), 0)
     src = src_ref[...]
     even = lax.axis_index("band") % 2 == 0
     shift = jnp.where(src >= nodes + rim, -rim, jnp.where(src >= nodes, rim, 0))
     src = src + jnp.where(even, shift, 0)
-    mask = rows == src[0:1, :]
-    for e in range(1, src.shape[0]):
-        mask = mask | (rows == src[e : e + 1, :])
-    half_mask = jnp.where(mask, 0.5, 0.0).astype(F32)
-    half_mask = jnp.concatenate([half_mask, half_mask], axis=0)
-    half_scale = 0.5 * HEAD_DIM ** (-0.5)
-    low_rows = lax.broadcasted_iota(jnp.int32, (LANES, ext), 0) < HEAD_DIM
-
-    keys, values = {}, {}
-
-    def prepare(block):
-        start = block * step
-        for m, rows in enumerate(project(start)):
-            keys[block, m] = rows
-        for m, rows in enumerate(project(width + start)):
-            values[block, m] = rows
-            value_ref[m, :, start : start + step] = rows
-
-    def scores(pair, m):
-        block, at = pair * LANES // step, pair * LANES % step
-        q = (q_ref[:, pair * LANES : (pair + 1) * LANES].astype(F32) * half_scale).astype(BF)
-        return mm(split_heads(keys[block, m][:, at : at + LANES]), q, NT)
-
-    tasks = [(pair, m) for pair in range(width // LANES) for m in range(members)]
-    prepare(0)
-    ahead = scores(*tasks[0])
-    for i, (pair, m) in enumerate(tasks):
-        block, at = pair * LANES // step, pair * LANES % step
-        current = ahead
-        if at == 0 and m == 0 and (block + 1) * step < width:
-            prepare(block + 1)
-        if i + 1 < len(tasks):
-            ahead = scores(*tasks[i + 1])
-        value_t = values[block, m][:, at : at + LANES].astype(F32).T
-        zero = jnp.zeros_like(value_t)
-        value_t = jnp.concatenate(
-            [jnp.where(low_rows, value_t, zero), jnp.where(low_rows, zero, value_t)], axis=1
-        ).astype(BF)
-        gate = jnp.tanh(current) * half_mask + half_mask
-        rounded = gate.astype(BF)
-        gate_ref[pair, m] = rounded
-        slope_ref[pair, m] = (gate - gate * gate).astype(BF)
-        merged_ref[m, pair * LANES : (pair + 1) * LANES, :] = mm(value_t, rounded).astype(BF)
+    held = {}
+
+    def rows(pair, m, first):
+        start = first + pair * LANES // step * step
+        if start not in held:
+            held[start] = mm(halo_rows, kvw_ref[:, start : start + step]).astype(BF)
+        at = pair * LANES % step
+        block = held[start][:, at : at + LANES]
+        mate = block[m * rim : (m + 1) * rim]
+        other = block[(members + m) * rim : (members + m + 1) * rim]
+        return jnp.concatenate([mate, other], axis=0)
+
+    def values(pair, m):
+        result = rows(pair, m, width)
+        value_ref[m, :, pair * LANES : (pair + 1) * LANES] = result
+        return result
+
+    def store_merged(pair, m, result):
+        cols = slice(pair * LANES, (pair + 1) * LANES)
+        merged_ref[m, cols, :] = (own_ref[m, cols, :] + result).astype(BF)
+
+    gate_rows(
+        tasks_of(width, members), lambda pair, m: rows(pair, m, 0), values,
+        q_ref, half_mask_of(src, nodes, count), gate_ref, slope_ref, store_merged,
+    )
     sent = []
     for m in range(members):
         part = mm(p_ref[...], merged_ref[m])
@@ -234,14 +254,23 @@
     return jnp.where(low, block[:half], block[half:])
 
 
+def joined(refs, pair, m):
+    return jnp.concatenate([ref[pair, m] for ref in refs], axis=0)
+
+
+def select_rows(block, own):
+    return jnp.concatenate([select_heads(block[: 2 * own]), select_heads(block[2 * own :])], axis=0)
+
+
 def soft_slope(v):
     return v * lax.rsqrt(v * v + SOFTENING * SOFTENING)
 
 
 def value_body(n_member, n_band, *refs):
     recv_refs = refs[: n_member - 1]
-    part_ref, base_ref, truth_ref, weight_ref, pt_ref, gate_ref, ext_ref = refs[n_member - 1 : n_member + 6]
-    grad_ref, dm_ref, ng_ref, *out_refs = refs[n_member + 6 :]
+    part_ref, base_ref, truth_ref, weight_ref, pt_ref, *gate_refs, ext_ref = refs[n_member - 1 : n_member + 7]
+    grad_ref, dm_ref, ng_ref, *out_refs = refs[n_member + 7 :]
+    own_rows = gate_refs[0].shape[2] // 2
     group_width = out_refs[0].shape[1]
     members, width, _ = dm_ref.shape
     ext = ng_ref.shape[0] // members
@@ -270,40 +299,46 @@
     for pair in range(width // LANES):
         cols = slice(pair * LANES, (pair + 1) * LANES)
         for m in range(members):
-            result = mm(gate_ref[pair, m], dm_ref[m, cols, :], NT)
-            ng_ref[m * ext : (m + 1) * ext, cols] = select_heads(result).astype(BF)
+            result = mm(joined(gate_refs, pair, m), dm_ref[m, cols, :], NT)
+            ng_ref[m * ext : (m + 1) * ext, cols] = select_rows(result, own_rows).astype(BF)
     store_group(mm(ext_ref[...], ng_ref[:, 0:group_width]), 0, n_member, n_band, 0, out_refs)
 
 
-def key_gradients(pairs, dm_ref, value_ref, slope_ref, q_ref, ng_ref):
-    members, ext, _ = value_ref.shape
+def key_gradients(pairs, dm_ref, value_refs, slope_refs, q_ref, ng_ref):
+    members = dm_ref.shape[0]
+    ext = ng_ref.shape[0] // members
     scale = HEAD_DIM ** (-0.5)
     for place, pair in enumerate(pairs):
         cols = slice(pair * LANES, (pair + 1) * LANES)
         for m in range(members):
-            dgate = mm(split_heads(value_ref[m, :, cols]), dm_ref[m, cols, :])
-            dscore = (dgate * slope_ref[pair, m].astype(F32)).astype(BF)
-            keys = select_heads(mm(dscore, q_ref[:, cols])) * scale
+            value = jnp.concatenate([split_heads(ref[m, :, cols]) for ref in value_refs], axis=0)
+            dgate = mm(value, dm_ref[m, cols, :])
+            dscore = (dgate * joined(slope_refs, pair, m).astype(F32)).astype(BF)
+            keys = select_rows(mm(dscore, q_ref[:, cols]), value_refs[0].shape[1]) * scale
             ng_ref[m * ext : (m + 1) * ext, place * LANES : (place + 1) * LANES] = keys.astype(BF)
 
 
 def first_keys_body(
-    n_member, n_band, first_value, dm_ref, value_ref, slope_ref, q_ref, ext_ref, ngv_ref, ng_ref, *out_refs
+    n_member, n_band, first_value, dm_ref, own_value_ref, halo_value_ref, own_slope_ref, halo_slope_ref,
+    q_ref, ext_ref, ngv_ref, ng_ref, *out_refs
 ):
     count = ng_ref.shape[1] // LANES
     rest = mm(ext_ref[...], ngv_ref[:, first_value:])
     store_group(rest, 1, n_member, n_band, 0, out_refs)
-    key_gradients(range(count), dm_ref, value_ref, slope_ref, q_ref, ng_ref)
+    value_refs, slope_refs = (own_value_ref, halo_value_ref), (own_slope_ref, halo_slope_ref)
+    key_gradients(range(count), dm_ref, value_refs, slope_refs, q_ref, ng_ref)
     store_group(mm(ext_ref[...], ng_ref[...]), 1, n_member, n_band, rest.shape[1], out_refs)
 
 
 def last_keys_body(
-    n_member, n_band, grad_ref, dm_ref, value_ref, slope_ref, q_ref, merged_ref, wo_ref, ext_ref, ng_ref, *refs
+    n_member, n_band, grad_ref, dm_ref, own_value_ref, halo_value_ref, own_slope_ref, halo_slope_ref,
+    q_ref, merged_ref, wo_ref, ext_ref, ng_ref, *refs
 ):
     out_refs, turned = refs[:-1], refs[-1]
-    members, _, width = value_ref.shape
+    members, width, _ = dm_ref.shape
     count = ng_ref.shape[1] // LANES
-    key_gradients(range(width // LANES - count, width // LANES), dm_ref, value_ref, slope_ref, q_ref, ng_ref)
+    value_refs, slope_refs = (own_value_ref, halo_value_ref), (own_slope_ref, halo_slope_ref)
+    key_gradients(range(width // LANES - count, width // LANES), dm_ref, value_refs, slope_refs, q_ref, ng_ref)
     m_t = sum(mm(grad_ref[m], merged_ref[m], NT) for m in range(members))
     head_t = sum(mm(grad_ref[m], q_ref[...]) for m in range(members)) + mm(m_t.astype(BF), wo_ref[...])
     turned[...] = jnp.concatenate([m_t, head_t], axis=0).T
@@ -386,14 +421,19 @@
         hbm=(0, 1),
         flops=10**10,
     )
+    other = lax.ppermute(for_other, "band", others)
     mate = lax.ppermute(for_mate, "band", mates)
-    other = lax.ppermute(for_other, "band", others)
 
     hp = head_projection.T
-    own_kv, pt, p, base, weight = call(
-        prepare_body,
-        [
-            sds((members * nodes, 2 * width), BF),
+
+    def gate_shapes(rows):
+        return [sds((members, rows, width), BF)] + [sds((pairs, members, 2 * rows, points), BF)] * 2
+
+    own_value, own_gates, own_slopes, own_merged, pt, p, base, weight = call(
+        own_body,
+        gate_shapes(nodes)
+        + [
+            sds((members, width, points), F32),
             sds((width, LANES), BF),
             sds((LANES, width), BF),
             sds((LANES, points), F32),
@@ -401,22 +441,20 @@
         ],
         (
             own_hidden, out_weight, hp, queries, kv_weight, initial_state,
-            channel_loss_weight[None, :], latitude_weight[None, :],
+            channel_loss_weight[None, :], latitude_weight[None, :], sources,
         ),
         [pltpu.VMEM((8, LANES), F32), pltpu.VMEM((LANES, width), F32)],
     )
 
-    value, gates, slopes, merged, part, sent = call(
-        functools.partial(forward_body, send_rows),
-        [
-            sds((members, ext, width), BF),
-            sds((pairs, members, 2 * ext, points), BF),
-            sds((pairs, members, 2 * ext, points), BF),
+    halo_value, halo_gates, halo_slopes, merged, part, sent = call(
+        functools.partial(halo_body, send_rows, nodes),
+        gate_shapes(2 * rim)
+        + [
             sds((members, width, points), BF),
             sds((members, LANES, points), F32),
             sds((-(-members * send_rows // 16) * 16, points), BF),
         ],
-        (mate, other, own_kv, kv_weight, queries, sources, p),
+        (other, mate, own_merged, kv_weight, queries, sources, p),
     )
 
     received = [
@@ -438,19 +476,19 @@
         functools.partial(value_body, n_member, n_band),
         [sds((members, LANES, points), BF), sds((members, width, points), BF), sds((members * ext, width), BF)]
         + group_shape,
-        (*received, part, base, truth, weight, pt, gates, ext_t),
+        (*received, part, base, truth, weight, pt, own_gates, halo_gates, ext_t),
     )
     groups = [[keep, swap(send, "band", 0, n_band)]]
     ng_first, send, keep = call(
         functools.partial(first_keys_body, n_member, n_band, group_width),
         [sds((members * ext, first_keys), BF)] + group_shape,
-        (dm, value, slopes, queries, ext_t, ng_value),
+        (dm, own_value, halo_value, own_slopes, halo_slopes, queries, ext_t, ng_value),
     )
     groups.append([keep, swap(send, "band", 0, n_band)])
     ng_last, send, keep = call(
         functools.partial(last_keys_body, n_member, n_band),
         [sds((members * ext, width - first_keys), BF)] + group_shape,
-        (grad, dm, value, slopes, queries, merged, out_weight, ext_t),
+        (grad, dm, own_value, halo_value, own_slopes, halo_slopes, queries, merged, out_weight, ext_t),
         [pltpu.VMEM((width, extra), F32)],
     )
     groups.append([keep, swap(send, "band", 0, n_band)])
@@ -479,20 +517,21 @@
             arrived, back_other = lax.optimization_barrier((arrived, back_other))
             from_other = lax.ppermute(back_other, "band", others)
         groups = [lower(terms) + [new] for terms, new in zip(groups, arrived)]
+    terms = [jnp.concatenate([add_up(*group) for group in groups], axis=1)]
+    for axis, bit in rest:
+        arrived = swap(add_up(*upper(terms)).astype(BF), axis, bit, count[axis])
+        terms = lower(terms) + [arrived]
+
+    kv_grad, out_grad, head_grad = call(
+        functools.partial(finish_body, devices),
+        [sds((rw, 2 * width), F32), sds((rw, width), F32), sds((rw, channels), F32)],
+        (add_up(*terms[:-1]), terms[-1], hp),
+    )
+    kv_grad, from_other = lax.optimization_barrier((kv_grad, from_other))
     hidden_grad = call(
         hidden_body,
         sds((members, nodes, width), F32),
         (own_grad, from_mate, from_other, halo),
-    )
-    terms = [jnp.concatenate([add_up(*group) for group in groups], axis=1)]
-    for axis, bit in rest:
-        arrived = swap(add_up(*upper(terms)).astype(BF), axis, bit, count[axis])
-        terms = lower(terms) + [arrived]
-
-    kv_grad, out_grad, head_grad = call(
-        functools.partial(finish_body, devices),
-        [sds((rw, 2 * width), F32), sds((rw, width), F32), sds((rw, channels), F32)],
-        (add_up(*terms[:-1]), terms[-1], hp),
     )
     return hidden_grad, kv_grad, out_grad, head_grad
 

time: 72 us -> 71.6 us (level)
  waiting for transfers between devices: 34.8 us -> 30.7 us
  starting transfers between devices: 20.8 us -> 23.2 us
  Pallas kernels: 14.4 us -> 15.7 us
    ppermute x1, waiting for transfers between devices: 5.91 us -> 0.01 us  [shards(): from_other = lax.ppermute(back_other, 'band', others)]
    ppermute x13, waiting for transfers between devices: 17.6 us -> 21.7 us  [swap(): return lax.ppermute(rows, axis, [(i, i ^ 1 << bit) for i in range(count)])]
    ppermute x13, starting transfers between devices: 12 us -> 14 us  [swap(): return lax.ppermute(rows, axis, [(i, i ^ 1 << bit) for i in range(count)])]
    ppermute x3, waiting for transfers between devices: 8.32 us -> 6.82 us  [shards(): lax.ppermute(sent, 'member', [(i, i ^ s) for i in range(n_member)])]
    pallas_call x10, Pallas kernels: 14.4 us -> 15.7 us  [call(): pl.pallas_call(body, out_shape=out_shape, in_specs=[pl.BlockSpec(memory_s...]
    ppermute x3, starting transfers between devices: 4.58 us -> 5.72 us  [shards(): lax.ppermute(sent, 'member', [(i, i ^ s) for i in range(n_member)])]
    ppermute x1, waiting for transfers between devices: 1.63 us -> 0.8 us  [shards(): other = lax.ppermute(for_other, 'band', others)]
  transfers between devices with their start and end apart: 20 -> 20, of which waited for: 14 -> 14; matrix products, arithmetic and copies ran while one was open for 1% -> 1% of each run, Pallas kernels for 10% -> 11%
where the time goes in v10:
time: 71.6 us; the launch traced here: 71.5 us
  waiting for transfers between devices  30.7 us (43%)
  starting transfers between devices  23.2 us (32%)
  Pallas kernels  15.7 us (22%)
  other arithmetic  0.95 us (1%)
  between operations  0.9 us (1%)
    ppermute x13, waiting for transfers between devices, swap(): return lax.ppermute(rows, axis, [(i, i ^ 1 << bit) for i in range(count)])  21.7 us
    pallas_call x10, Pallas kernels, call(): pl.pallas_call(body, out_shape=out_shape, in_specs=[pl.BlockSpec(memory_s...  15.7 us
    ppermute x13, starting transfers between devices, swap(): return lax.ppermute(rows, axis, [(i, i ^ 1 << bit) for i in range(count)])  14 us
    ppermute x3, waiting for transfers between devices, shards(): lax.ppermute(sent, 'member', [(i, i ^ s) for i in range(n_member)])  6.82 us
    ppermute x3, starting transfers between devices, shards(): lax.ppermute(sent, 'member', [(i, i ^ s) for i in range(n_member)])  5.72 us
    ppermute x1, starting transfers between devices, shards(): other = lax.ppermute(for_other, 'band', others)  3.4 us
  transfers between devices with their start and end apart: 20, of which 14 were waited for; matrix products, arithmetic and copies ran while one was open for 1% of the time, Pallas kernels for 11%

profile of v10, /device:TPU:0, one launch (start us, length us, event | category | flops | bytes accessed | tf_op | source)
XLA Modules:
  0.0 71.5 jit_solution(16440789571849896379)
XLA Ops:
  0.7 1.4 %shard_map.138 = (bf16[2,64,1024]{2,1,0:T(8,128)(2,1)S(1)}, s32[2,32]{1,0:T(2,128)S(1)}, bf16[64,1024]{1,0:T(8,128)(2,1)S(1)}, bf16[64,1024]{1,0:T(8,128)(2,1)S(1)}) custom-call(bf16[2,64,1024]{2,1,0:T(8,128)(2,1)} %hidden_hbm.1, s32[2,32]{1,0:T(2,128)} %halo_hbm.1), custom_call_target="tpu_custom_call" | custom-call | flops 10000000000 | bytes 1 | tf_op jit(solution)/shard_map/pallas_call | solution.py:28
  2.1 3.4 %collective-permute-start = (bf16[64,1024]{1,0:T(8,128)(2,1)S(1)}, bf16[64,1024]{1,0:T(8,128)(2,1)S(1)}, u32[]{:S(2)}, u32[]{:S(2)}) collective-permute-start(bf16[64,1024]{1,0:T(8,128)(2,1)S(1)} %get-tuple-element.60), channel_id=1, source_target_pairs={{0,7},{1,2},{2,1},{3,4},{4,3},{5,6},{6,5},{7,0},{8,15},{9,10},{10,... | collective-permute-start | bytes 393224 | tf_op jit(solution)/shard_map/ppermute | solution.py:424
  5.6 2.3 %shard_map.139 = (bf16[2,64,1024]{2,1,0:T(8,128)(2,1)S(1)}, bf16[8,2,128,256]{3,2,1,0:T(8,128)(2,1)S(1)}, bf16[8,2,128,256]{3,2,1,0:T(8,128)(2,1)S(1)}, f32[2,10...) custom-call(bf16[2,64,1024]{2,1,0:T(8,128)(2,1)S(1)} %get-tuple-elem, ...), custom_call_target="tpu_custom_call" | custom-call | flops 1 | bytes 1 | tf_op jit(solution)/shard_map/pallas_call | solution.py:28
  7.9 0.8 %collective-permute-done.other_ref = bf16[64,1024]{1,0:T(8,128)(2,1)S(1)} collective-permute-done((bf16[64,1024]{1,0:T(8,128)(2,1)S(1)}, bf16[64,1024]{1,0:T(8,128)(2,1)S(1)}, u32[]{:S(2)}, u32[]{:S(2)}) %collective-permute-start) | collective-permute-done | bytes 131104 | tf_op jit(solution)/shard_map/ppermute | solution.py:424
  8.7 3.4 %shard_map.140 = (bf16[2,64,1024]{2,1,0:T(8,128)(2,1)S(1)}, bf16[8,2,128,256]{3,2,1,0:T(8,128)(2,1)S(1)}, bf16[8,2,128,256]{3,2,1,0:T(8,128)(2,1)S(1)}, bf16[2,1...) custom-call(bf16[64,1024]{1,0:T(8,128)(2,1)S(1)} %collective-permute-done.other_ref, ...), custom_call_target="tpu_custom_call" | custom-call | flops 1 | bytes 1 | tf_op jit(solution)/shard_map/pallas_call | solution.py:28
  12.2 3.1 %collective-permute-start.4 = (bf16[208,256]{1,0:T(8,128)(2,1)S(1)}, bf16[208,256]{1,0:T(8,128)(2,1)S(1)}, u32[]{:S(2)}, u32[]{:S(2)}) collective-permute-start(bf16[208,256]{1,0:T(8,128)(2,1)S(1)} %get-tuple-element.65), channel_id=1, source_target_pairs={{0,8},{8,0},{16,24},{24,16},{1,9},{9,1},{17,25},{25,17},{2,10},{10... | collective-permute-start | bytes 319496 | tf_op jit(solution)/shard_map/ppermute | solution.py:461
  15.3 2.6 %collective-permute-start.3 = (bf16[208,256]{1,0:T(8,128)(2,1)S(1)}, bf16[208,256]{1,0:T(8,128)(2,1)S(1)}, u32[]{:S(2)}, u32[]{:S(2)}) collective-permute-start(bf16[208,256]{1,0:T(8,128)(2,1)S(1)} %get-tuple-element.65), channel_id=1, source_target_pairs={{0,16},{8,24},{16,0},{24,8},{1,17},{9,25},{17,1},{25,9},{2,18},{10... | collective-permute-start | bytes 319496 | tf_op jit(solution)/shard_map/ppermute | solution.py:461
  17.9 0.3 shard_map.141.refs_10_.ext_ref
  18.2 0.9 %collective-permute-done.4.refs_2_ = bf16[208,256]{1,0:T(8,128)(2,1)S(1)} collective-permute-done((bf16[208,256]{1,0:T(8,128)(2,1)S(1)}, bf16[208,256]{1,0:T(8,128)(2,1)S(1)}, u32[]{:S(2)}, u32[]{:S(2)}) %collective-permute-start.4) | collective-permute-done | bytes 106528 | tf_op jit(solution)/shard_map/ppermute | solution.py:461
  19.1 5.9 %collective-permute-done.3.refs_1_ = bf16[208,256]{1,0:T(8,128)(2,1)S(1)} collective-permute-done((bf16[208,256]{1,0:T(8,128)(2,1)S(1)}, bf16[208,256]{1,0:T(8,128)(2,1)S(1)}, u32[]{:S(2)}, u32[]{:S(2)}) %collective-permute-start.3) | collective-permute-done | bytes 106528 | tf_op jit(solution)/shard_map/ppermute | solution.py:461
  25.0 1.8 %shard_map.142 = (bf16[2,128,256]{2,1,0:T(8,128)(2,1)S(1)}, bf16[2,1024,256]{2,1,0:T(8,128)(2,1)S(1)}, bf16[256,1024]{1,0:T(8,128)(2,1)S(1)}, bf16[512,768]{1,0:T(8,128)(2,1)S(1)}, bf16[512,768]{1,0:T(8,128)(2,1)S(1)}) custom-call(bf16[208,256]{1,0:T(8,128)(2,1)S(1)} %collective-permute-done.2.refs_0_, bf16[208,256]{1,0:T(8,128)(2,1)S(1)} %collective-permute-done.3.refs_1_, ...), custom_call_target="tpu_custom_call" | custom-call | flops 1 | bytes 1 | tf_op jit(solution)/shard_map/pallas_call | solution.py:28
  26.8 0.1 collective-permute-start.5
  26.9 1.5 %shard_map.143 = (bf16[256,512]{1,0:T(8,128)(2,1)S(1)}, bf16[512,768]{1,0:T(8,128)(2,1)S(1)}, bf16[512,768]{1,0:T(8,128)(2,1)S(1)}) custom-call(bf16[2,1024,256]{2,1,0:T(8,128)(2,1)S(1)} %get-tuple-element.72.dm_ref, bf16[2,64,1024]{2,1,0:T(8,128)(2,1)S(1)} %get-tuple-element.73.own_value_ref, bf16[2,64,1024]{2,1,0:T(8,128)(2,1)S(1)} %get-tuple-element.74.halo_value_ref, ...), custom_call_target="tpu_custom_call" | custom-call | flops 1 | bytes 1 | tf_op jit(solution)/shard_map/pallas_call | solution.py:28
  28.3 0.6 collective-permute-start.6
  28.9 1.8 %shard_map.144 = (bf16[256,512]{1,0:T(8,128)(2,1)S(1)}, bf16[512,768]{1,0:T(8,128)(2,1)S(1)}, bf16[512,768]{1,0:T(8,128)(2,1)S(1)}) custom-call(bf16[2,128,256]{2,1,0:T(8,128)(2,1)S(1)} %get-tuple-element.86.grad_ref, bf16[2,1024,256]{2,1,0:T(8,128)(2,1)S(1)} %get-tuple-element.72.dm_ref, bf16[2,64,1024]{2,1,0:T(8,128)(2,1)S(1)} %get-tuple-element.73.own_value_ref, ...), custom_call_target="tpu_custom_call" | custom-call | flops 1 | bytes 1 | tf_op jit(solution)/shard_map/pallas_call | solution.py:28
  30.7 0.1 collective-permute-start.7
  30.8 0.1 add_convert_fusion.2
  30.9 0.1 add_convert_fusion.1
  31.0 2.0 %collective-permute-done.7 = bf16[512,768]{1,0:T(8,128)(2,1)S(1)} collective-permute-done((bf16[512,768]{1,0:T(8,128)(2,1)S(1)}, bf16[512,768]{1,0:T(8,128)(2,1)S(1)}, u32[]{:S(2)}, u32[]{:S(2)}) %collective-permute-start.7) | collective-permute-done | bytes 786464 | tf_op jit(solution)/shard_map/ppermute | solution.py:387
  33.0 0.1 add_convert_fusion
  33.1 1.2 %collective-permute-start.8 = (bf16[256,768]{1,0:T(8,128)(2,1)S(1)}, bf16[256,768]{1,0:T(8,128)(2,1)S(1)}, u32[]{:S(2)}, u32[]{:S(2)}) collective-permute-start(bf16[256,768]{1,0:T(8,128)(2,1)S(1)} %add_convert_fusion.2), channel_id=1, source_target_pairs={{0,2},{1,3},{2,0},{3,1},{4,6},{5,7},{6,4},{7,5},{8,10},{9,11},{10,... | collective-permute-start | bytes 1179656 | tf_op jit(solution)/shard_map/ppermute | solution.py:387
  34.3 2.4 %collective-permute-start.9 = (bf16[256,768]{1,0:T(8,128)(2,1)S(1)}, bf16[256,768]{1,0:T(8,128)(2,1)S(1)}, u32[]{:S(2)}, u32[]{:S(2)}) collective-permute-start(bf16[256,768]{1,0:T(8,128)(2,1)S(1)} %add_convert_fusion.1), channel_id=1, source_target_pairs={{0,4},{1,5},{2,6},{3,7},{4,0},{5,1},{6,2},{7,3},{8,12},{9,13},{10,... | collective-permute-start | bytes 1179656 | tf_op jit(solution)/shard_map/ppermute | solution.py:387
  36.7 1.7 %collective-permute-start.10 = (bf16[256,768]{1,0:T(8,128)(2,1)S(1)}, bf16[256,768]{1,0:T(8,128)(2,1)S(1)}, u32[]{:S(2)}, u32[]{:S(2)}) collective-permute-start(bf16[256,768]{1,0:T(8,128)(2,1)S(1)} %add_convert_fusion), channel_id=1, source_target_pairs={{0,8},{8,0},{16,24},{24,16},{1,9},{9,1},{17,25},{25,17},{2,10},{10... | collective-permute-start | bytes 1179656 | tf_op jit(solution)/shard_map/ppermute | solution.py:387
  38.4 1.3 %shard_map.145 = (f32[2,64,1024]{2,1,0:T(8,128)S(1)}, bf16[64,1024]{1,0:T(8,128)(2,1)S(1)}, bf16[64,1024]{1,0:T(8,128)(2,1)S(1)}) custom-call(bf16[256,512]{1,0:T(8,128)(2,1)S(1)} %get-tuple-element.78.first_ref, bf16[256,512]{1,0:T(8,128)(2,1)S(1)} %get-tuple-element.94.last_ref, bf16[256,1024]{1,0:T(8,128)(2,1)S(1)} %get-tuple-element.77.ngv_ref, ...), custom_call_target="tpu_custom_call" | custom-call | flops 1 | bytes 1 | tf_op jit(solution)/shard_map/pallas_call | solution.py:28
  39.7 0.1 collective-permute-start.11
  39.8 1.3 %collective-permute-done.11.from_mate_ref = bf16[64,1024]{1,0:T(8,128)(2,1)S(1)} collective-permute-done((bf16[64,1024]{1,0:T(8,128)(2,1)S(1)}, bf16[64,1024]{1,0:T(8,128)(2,1)S(1)}, u32[]{:S(2)}, u32[]{:S(2)}) %collective-permute-start.11) | collective-permute-done | bytes 131104 | tf_op jit(solution)/shard_map/ppermute | solution.py:514
  41.2 3.2 %collective-permute-done.8 = bf16[256,768]{1,0:T(8,128)(2,1)S(1)} collective-permute-done((bf16[256,768]{1,0:T(8,128)(2,1)S(1)}, bf16[256,768]{1,0:T(8,128)(2,1)S(1)}, u32[]{:S(2)}, u32[]{:S(2)}) %collective-permute-start.8) | collective-permute-done | bytes 393248 | tf_op jit(solution)/shard_map/ppermute | solution.py:387
  44.4 1.5 %collective-permute-done.9 = bf16[256,768]{1,0:T(8,128)(2,1)S(1)} collective-permute-done((bf16[256,768]{1,0:T(8,128)(2,1)S(1)}, bf16[256,768]{1,0:T(8,128)(2,1)S(1)}, u32[]{:S(2)}, u32[]{:S(2)}) %collective-permute-start.9) | collective-permute-done | bytes 393248 | tf_op jit(solution)/shard_map/ppermute | solution.py:387
  45.9 1.5 %collective-permute-done.10 = bf16[256,768]{1,0:T(8,128)(2,1)S(1)} collective-permute-done((bf16[256,768]{1,0:T(8,128)(2,1)S(1)}, bf16[256,768]{1,0:T(8,128)(2,1)S(1)}, u32[]{:S(2)}, u32[]{:S(2)}) %collective-permute-start.10) | collective-permute-done | bytes 393248 | tf_op jit(solution)/shard_map/ppermute | solution.py:387
  47.3 0.1 add_convert_fusion.4
  47.4 0.1 add_convert_fusion.3
  47.5 0.9 %collective-permute-start.16 = (bf16[128,768]{1,0:T(8,128)(2,1)S(1)}, bf16[128,768]{1,0:T(8,128)(2,1)S(1)}, u32[]{:S(2)}, u32[]{:S(2)}) collective-permute-start(bf16[128,768]{1,0:T(8,128)(2,1)S(1)} %add_convert_fusion.3), channel_id=1, source_target_pairs={{0,2},{1,3},{2,0},{3,1},{4,6},{5,7},{6,4},{7,5},{8,10},{9,11},{10,... | collective-permute-start | bytes 589832 | tf_op jit(solution)/shard_map/ppermute | solution.py:387
  48.4 1.7 %collective-permute-start.14 = (bf16[128,768]{1,0:T(8,128)(2,1)S(1)}, bf16[128,768]{1,0:T(8,128)(2,1)S(1)}, u32[]{:S(2)}, u32[]{:S(2)}) collective-permute-start(bf16[128,768]{1,0:T(8,128)(2,1)S(1)} %add_convert_fusion.4), channel_id=1, source_target_pairs={{0,8},{8,0},{16,24},{24,16},{1,9},{9,1},{17,25},{25,17},{2,10},{10... | collective-permute-start | bytes 589832 | tf_op jit(solution)/shard_map/ppermute | solution.py:387
  50.1 0.1 add_convert_fusion.5
  50.2 0.3 collective-permute-start.12
  50.5 2.7 %collective-permute-done.16 = bf16[128,768]{1,0:T(8,128)(2,1)S(1)} collective-permute-done((bf16[128,768]{1,0:T(8,128)(2,1)S(1)}, bf16[128,768]{1,0:T(8,128)(2,1)S(1)}, u32[]{:S(2)}, u32[]{:S(2)}) %collective-permute-start.16) | collective-permute-done | bytes 196640 | tf_op jit(solution)/shard_map/ppermute | solution.py:387
  53.3 0.9 %collective-permute-start.17 = (bf16[64,768]{1,0:T(8,128)(2,1)S(1)}, bf16[64,768]{1,0:T(8,128)(2,1)S(1)}, u32[]{:S(2)}, u32[]{:S(2)}) collective-permute-start(bf16[64,768]{1,0:T(8,128)(2,1)S(1)} %add_convert_fusion.6), channel_id=1, source_target_pairs={{0,4},{1,5},{2,6},{3,7},{4,0},{5,1},{6,2},{7,3},{8,12},{9,13},{10,... | collective-permute-start | bytes 294920 | tf_op jit(solution)/shard_map/ppermute | solution.py:387
  54.2 1.2 %collective-permute-start.15 = (bf16[64,768]{1,0:T(8,128)(2,1)S(1)}, bf16[64,768]{1,0:T(8,128)(2,1)S(1)}, u32[]{:S(2)}, u32[]{:S(2)}) collective-permute-start(bf16[64,768]{1,0:T(8,128)(2,1)S(1)} %add_convert_fusion.7), channel_id=1, source_target_pairs={{0,2},{1,3},{2,0},{3,1},{4,6},{5,7},{6,4},{7,5},{8,10},{9,11},{10,... | collective-permute-start | bytes 294920 | tf_op jit(solution)/shard_map/ppermute | solution.py:387
  55.4 1.2 %collective-permute-done.12 = bf16[128,768]{1,0:T(8,128)(2,1)S(1)} collective-permute-done((bf16[128,768]{1,0:T(8,128)(2,1)S(1)}, bf16[128,768]{1,0:T(8,128)(2,1)S(1)}, u32[]{:S(2)}, u32[]{:S(2)}) %collective-permute-start.12) | collective-permute-done | bytes 196640 | tf_op jit(solution)/shard_map/ppermute | solution.py:387
  56.7 0.7 %collective-permute-start.13 = (bf16[64,768]{1,0:T(8,128)(2,1)S(1)}, bf16[64,768]{1,0:T(8,128)(2,1)S(1)}, u32[]{:S(2)}, u32[]{:S(2)}) collective-permute-start(bf16[64,768]{1,0:T(8,128)(2,1)S(1)} %add_convert_fusion.8), channel_id=1, source_target_pairs={{0,8},{8,0},{16,24},{24,16},{1,9},{9,1},{17,25},{25,17},{2,10},{10... | collective-permute-start | bytes 294920 | tf_op jit(solution)/shard_map/ppermute | solution.py:387
  57.4 0.6 collective-permute-done.17
  58.0 0.9 %collective-permute-done.15 = bf16[64,768]{1,0:T(8,128)(2,1)S(1)} collective-permute-done((bf16[64,768]{1,0:T(8,128)(2,1)S(1)}, bf16[64,768]{1,0:T(8,128)(2,1)S(1)}, u32[]{:S(2)}, u32[]{:S(2)}) %collective-permute-start.15) | collective-permute-done | bytes 98336 | tf_op jit(solution)/shard_map/ppermute | solution.py:387
  58.9 3.0 %collective-permute-done.13 = bf16[64,768]{1,0:T(8,128)(2,1)S(1)} collective-permute-done((bf16[64,768]{1,0:T(8,128)(2,1)S(1)}, bf16[64,768]{1,0:T(8,128)(2,1)S(1)}, u32[]{:S(2)}, u32[]{:S(2)}) %collective-permute-start.13) | collective-permute-done | bytes 98336 | tf_op jit(solution)/shard_map/ppermute | solution.py:387
  61.9 0.1 convert_add_fusion
  62.1 2.3 %collective-permute-start.18 = (bf16[32,2304]{1,0:T(8,128)(2,1)S(1)}, bf16[32,2304]{1,0:T(8,128)(2,1)S(1)}, u32[]{:S(2)}, u32[]{:S(2)}) collective-permute-start(bf16[32,2304]{1,0:T(8,128)(2,1)S(1)} %slice.262), channel_id=1, source_target_pairs={{0,16},{8,24},{16,0},{24,8},{1,17},{9,25},{17,1},{25,9},{2,18},{10... | collective-permute-start | bytes 442376 | tf_op jit(solution)/shard_map/ppermute | solution.py:387
  64.4 5.1 %collective-permute-done.18.arrived_ref = bf16[32,2304]{1,0:T(8,128)(2,1)S(1)} collective-permute-done((bf16[32,2304]{1,0:T(8,128)(2,1)S(1)}, bf16[32,2304]{1,0:T(8,128)(2,1)S(1)}, u32[]{:S(2)}, u32[]{:S(2)}) %collective-permute-start.18) | collective-permute-done | bytes 147488 | tf_op jit(solution)/shard_map/ppermute | solution.py:387
  69.5 0.9 %shard_map.146 = (f32[32,2048]{1,0:T(8,128)}, f32[32,1024]{1,0:T(8,128)}, f32[32,100]{1,0:T(8,128)}) custom-call(f32[32,2304]{1,0:T(8,128)S(1)} %slice.220.own_ref, bf16[32,2304]{1,0:T(8,128)(2,1)S(1)} %collective-permute-done.18.arrived_ref, bf16[100,1024]{1,0:T(8,128)(2,1)S(1)} %bitcast.4), custom_call_target="tpu_custom_call" | custom-call | flops 1 | bytes 1 | tf_op jit(solution)/shard_map/pallas_call | solution.py:28
  70.4 1.1 %shard_map.147 = f32[2,64,1024]{2,1,0:T(8,128)} custom-call(f32[2,64,1024]{2,1,0:T(8,128)S(1)} %get-tuple-element.95.own_ref, bf16[64,1024]{1,0:T(8,128)(2,1)S(1)} %collective-permute-done.11.from_mate_ref, bf16[64,1024]{1,0:T(8,128)(2,1)S(1)} %collective-permute-done.19.from_other_ref, s32[2,32]{1,0:T(2,128)S(1)} %get-tuple-element.112.halo_ref), custom_call_target="tpu_custom_call" | custom-call | flops 1 | bytes 1 | tf_op jit(solution)/shard_map/pallas_call | solution.py:28
  (34 shorter events, 0.4 us)
Async XLA Ops:
  0.6 4.9 %copy-start.2 = (bf16[256,1024]{1,0:T(8,128)(2,1)S(1)}, bf16[256,1024]{1,0:T(8,128)(2,1)}, u32[]{:S(2)}) copy-start(bf16[256,1024]{1,0:T(8,128)(2,1)} %q_ref.7) | copy-start | bytes 1572868
  0.6 4.9 %copy-start.6 = (s32[3,256]{1,0:T(4,128)S(1)}, s32[3,256]{1,0:T(4,128)}, u32[]{:S(2)}) copy-start(s32[3,256]{1,0:T(4,128)} %src_ref.3) | copy-start | bytes 9220
  0.7 4.9 %copy-start.1 = (bf16[1024,1024]{1,0:T(8,128)(2,1)S(1)}, bf16[1024,1024]{1,0:T(8,128)(2,1)}, u32[]{:S(2)}) copy-start(bf16[1024,1024]{1,0:T(8,128)(2,1)} %wo_ref.3) | copy-start | bytes 6291460
  0.7 4.9 %copy-start.8 = (f32[100]{0:T(128)S(1)}, f32[100]{0:T(128)}, u32[]{:S(2)}) copy-start(f32[100]{0:T(128)} %param.19) | copy-start | bytes 1204
  0.7 4.9 %copy-start.7 = (f32[256]{0:T(256)S(1)}, f32[256]{0:T(256)}, u32[]{:S(2)}) copy-start(f32[256]{0:T(256)} %param.18) | copy-start | bytes 3076
  0.7 4.9 %copy-start.4 = (f32[100,256]{1,0:T(8,128)S(1)}, f32[100,256]{1,0:T(8,128)}, u32[]{:S(2)}) copy-start(f32[100,256]{1,0:T(8,128)} %init_ref.1) | copy-start | bytes 307204
  0.7 4.9 %copy-start.3 = (bf16[1024,100]{0,1:T(8,128)(2,1)S(1)}, bf16[1024,100]{0,1:T(8,128)(2,1)}, u32[]{:S(2)}) copy-start(bf16[1024,100]{0,1:T(8,128)(2,1)} %param.15) | copy-start | bytes 614404
  0.7 4.9 %copy-start = (bf16[1024,2048]{1,0:T(8,128)(2,1)S(1)}, bf16[1024,2048]{1,0:T(8,128)(2,1)}, u32[]{:S(2)}) copy-start(bf16[1024,2048]{1,0:T(8,128)(2,1)} %kvw_ref.5) | copy-start | bytes 12582916
  2.1 6.6 %collective-permute-start = (bf16[64,1024]{1,0:T(8,128)(2,1)S(1)}, bf16[64,1024]{1,0:T(8,128)(2,1)S(1)}, u32[]{:S(2)}, u32[]{:S(2)}) collective-permute-start(bf16[64,1024]{1,0:T(8,128)(2,1)S(1)} %get-tuple-element.60), channel_id=1, source_target_pairs={{0,7},{1,2},{2,1},{3,4},{4,3},{5,6},{6,5},{7,0},{8,15},{9,10},{10,... | collective-permute-start | bytes 393224 | tf_op jit(solution)/shard_map/ppermute | solution.py:424
  5.5 3.2 %collective-permute-start.1 = (bf16[64,1024]{1,0:T(8,128)(2,1)S(1)}, bf16[64,1024]{1,0:T(8,128)(2,1)S(1)}, u32[]{:S(2)}, u32[]{:S(2)}) collective-permute-start(bf16[64,1024]{1,0:T(8,128)(2,1)S(1)} %get-tuple-element.61), channel_id=1, source_target_pairs={{0,1},{1,0},{2,3},{3,2},{4,5},{5,4},{6,7},{7,6},{8,9},{9,8},{10,11... | collective-permute-start | bytes 393224 | tf_op jit(solution)/shard_map/ppermute | solution.py:425
  8.7 16.2 %copy-start.5 = (f32[100,256]{1,0:T(8,128)S(1)}, f32[100,256]{1,0:T(8,128)}, u32[]{:S(2)}) copy-start(f32[100,256]{1,0:T(8,128)} %refs_5_.1) | copy-start | bytes 307204
  12.2 6.9 %collective-permute-start.4 = (bf16[208,256]{1,0:T(8,128)(2,1)S(1)}, bf16[208,256]{1,0:T(8,128)(2,1)S(1)}, u32[]{:S(2)}, u32[]{:S(2)}) collective-permute-start(bf16[208,256]{1,0:T(8,128)(2,1)S(1)} %get-tuple-element.65), channel_id=1, source_target_pairs={{0,8},{8,0},{16,24},{24,16},{1,9},{9,1},{17,25},{25,17},{2,10},{10... | collective-permute-start | bytes 319496 | tf_op jit(solution)/shard_map/ppermute | solution.py:461
  15.3 9.7 %collective-permute-start.3 = (bf16[208,256]{1,0:T(8,128)(2,1)S(1)}, bf16[208,256]{1,0:T(8,128)(2,1)S(1)}, u32[]{:S(2)}, u32[]{:S(2)}) collective-permute-start(bf16[208,256]{1,0:T(8,128)(2,1)S(1)} %get-tuple-element.65), channel_id=1, source_target_pairs={{0,16},{8,24},{16,0},{24,8},{1,17},{9,25},{17,1},{25,9},{2,18},{10... | collective-permute-start | bytes 319496 | tf_op jit(solution)/shard_map/ppermute | solution.py:461
  17.9 7.1 %collective-permute-start.2 = (bf16[208,256]{1,0:T(8,128)(2,1)S(1)}, bf16[208,256]{1,0:T(8,128)(2,1)S(1)}, u32[]{:S(2)}, u32[]{:S(2)}) collective-permute-start(bf16[208,256]{1,0:T(8,128)(2,1)S(1)} %get-tuple-element.65), channel_id=1, source_target_pairs={{0,24},{8,16},{16,8},{24,0},{1,25},{9,17},{17,9},{25,1},{2,26},{10... | collective-permute-start | bytes 319496 | tf_op jit(solution)/shard_map/ppermute | solution.py:461
  26.8 4.0 %collective-permute-start.5 = (bf16[512,768]{1,0:T(8,128)(2,1)S(1)}, bf16[512,768]{1,0:T(8,128)(2,1)S(1)}, u32[]{:S(2)}, u32[]{:S(2)}) collective-permute-start(bf16[512,768]{1,0:T(8,128)(2,1)S(1)} %get-tuple-element.80), channel_id=1, source_target_pairs={{0,1},{1,0},{2,3},{3,2},{4,5},{5,4},{6,7},{7,6},{8,9},{9,8},{10,11... | collective-permute-start | bytes 2359304 | tf_op jit(solution)/shard_map/ppermute | solution.py:387
  28.3 2.5 %collective-permute-start.6 = (bf16[512,768]{1,0:T(8,128)(2,1)S(1)}, bf16[512,768]{1,0:T(8,128)(2,1)S(1)}, u32[]{:S(2)}, u32[]{:S(2)}) collective-permute-start(bf16[512,768]{1,0:T(8,128)(2,1)S(1)} %get-tuple-element.82), channel_id=1, source_target_pairs={{0,1},{1,0},{2,3},{3,2},{4,5},{5,4},{6,7},{7,6},{8,9},{9,8},{10,11... | collective-permute-start | bytes 2359304 | tf_op jit(solution)/shard_map/ppermute | solution.py:387
  30.7 2.4 %collective-permute-start.7 = (bf16[512,768]{1,0:T(8,128)(2,1)S(1)}, bf16[512,768]{1,0:T(8,128)(2,1)S(1)}, u32[]{:S(2)}, u32[]{:S(2)}) collective-permute-start(bf16[512,768]{1,0:T(8,128)(2,1)S(1)} %get-tuple-element.89), channel_id=1, source_target_pairs={{0,1},{1,0},{2,3},{3,2},{4,5},{5,4},{6,7},{7,6},{8,9},{9,8},{10,11... | collective-permute-start | bytes 2359304 | tf_op jit(solution)/shard_map/ppermute | solution.py:387
  33.1 11.2 %collective-permute-start.8 = (bf16[256,768]{1,0:T(8,128)(2,1)S(1)}, bf16[256,768]{1,0:T(8,128)(2,1)S(1)}, u32[]{:S(2)}, u32[]{:S(2)}) collective-permute-start(bf16[256,768]{1,0:T(8,128)(2,1)S(1)} %add_convert_fusion.2), channel_id=1, source_target_pairs={{0,2},{1,3},{2,0},{3,1},{4,6},{5,7},{6,4},{7,5},{8,10},{9,11},{10,... | collective-permute-start | bytes 1179656 | tf_op jit(solution)/shard_map/ppermute | solution.py:387
  34.3 11.5 %collective-permute-start.9 = (bf16[256,768]{1,0:T(8,128)(2,1)S(1)}, bf16[256,768]{1,0:T(8,128)(2,1)S(1)}, u32[]{:S(2)}, u32[]{:S(2)}) collective-permute-start(bf16[256,768]{1,0:T(8,128)(2,1)S(1)} %add_convert_fusion.1), channel_id=1, source_target_pairs={{0,4},{1,5},{2,6},{3,7},{4,0},{5,1},{6,2},{7,3},{8,12},{9,13},{10,... | collective-permute-start | bytes 1179656 | tf_op jit(solution)/shard_map/ppermute | solution.py:387
  36.7 10.6 %collective-permute-start.10 = (bf16[256,768]{1,0:T(8,128)(2,1)S(1)}, bf16[256,768]{1,0:T(8,128)(2,1)S(1)}, u32[]{:S(2)}, u32[]{:S(2)}) collective-permute-start(bf16[256,768]{1,0:T(8,128)(2,1)S(1)} %add_convert_fusion), channel_id=1, source_target_pairs={{0,8},{8,0},{16,24},{24,16},{1,9},{9,1},{17,25},{25,17},{2,10},{10... | collective-permute-start | bytes 1179656 | tf_op jit(solution)/shard_map/ppermute | solution.py:387
  39.7 1.4 %collective-permute-start.11 = (bf16[64,1024]{1,0:T(8,128)(2,1)S(1)}, bf16[64,1024]{1,0:T(8,128)(2,1)S(1)}, u32[]{:S(2)}, u32[]{:S(2)}) collective-permute-start(bf16[64,1024]{1,0:T(8,128)(2,1)S(1)} %get-tuple-element.99), channel_id=1, source_target_pairs={{0,1},{1,0},{2,3},{3,2},{4,5},{5,4},{6,7},{7,6},{8,9},{9,8},{10,11... | collective-permute-start | bytes 393224 | tf_op jit(solution)/shard_map/ppermute | solution.py:514
  47.5 5.7 %collective-permute-start.16 = (bf16[128,768]{1,0:T(8,128)(2,1)S(1)}, bf16[128,768]{1,0:T(8,128)(2,1)S(1)}, u32[]{:S(2)}, u32[]{:S(2)}) collective-permute-start(bf16[128,768]{1,0:T(8,128)(2,1)S(1)} %add_convert_fusion.3), channel_id=1, source_target_pairs={{0,2},{1,3},{2,0},{3,1},{4,6},{5,7},{6,4},{7,5},{8,10},{9,11},{10,... | collective-permute-start | bytes 589832 | tf_op jit(solution)/shard_map/ppermute | solution.py:387
  48.4 5.8 %collective-permute-start.14 = (bf16[128,768]{1,0:T(8,128)(2,1)S(1)}, bf16[128,768]{1,0:T(8,128)(2,1)S(1)}, u32[]{:S(2)}, u32[]{:S(2)}) collective-permute-start(bf16[128,768]{1,0:T(8,128)(2,1)S(1)} %add_convert_fusion.4), channel_id=1, source_target_pairs={{0,8},{8,0},{16,24},{24,16},{1,9},{9,1},{17,25},{25,17},{2,10},{10... | collective-permute-start | bytes 589832 | tf_op jit(solution)/shard_map/ppermute | solution.py:387
  50.2 6.4 %collective-permute-start.12 = (bf16[128,768]{1,0:T(8,128)(2,1)S(1)}, bf16[128,768]{1,0:T(8,128)(2,1)S(1)}, u32[]{:S(2)}, u32[]{:S(2)}) collective-permute-start(bf16[128,768]{1,0:T(8,128)(2,1)S(1)} %add_convert_fusion.5), channel_id=1, source_target_pairs={{0,4},{1,5},{2,6},{3,7},{4,0},{5,1},{6,2},{7,3},{8,12},{9,13},{10,... | collective-permute-start | bytes 589832 | tf_op jit(solution)/shard_map/ppermute | solution.py:387
  53.3 4.7 %collective-permute-start.17 = (bf16[64,768]{1,0:T(8,128)(2,1)S(1)}, bf16[64,768]{1,0:T(8,128)(2,1)S(1)}, u32[]{:S(2)}, u32[]{:S(2)}) collective-permute-start(bf16[64,768]{1,0:T(8,128)(2,1)S(1)} %add_convert_fusion.6), channel_id=1, source_target_pairs={{0,4},{1,5},{2,6},{3,7},{4,0},{5,1},{6,2},{7,3},{8,12},{9,13},{10,... | collective-permute-start | bytes 294920 | tf_op jit(solution)/shard_map/ppermute | solution.py:387
  54.2 4.7 %collective-permute-start.15 = (bf16[64,768]{1,0:T(8,128)(2,1)S(1)}, bf16[64,768]{1,0:T(8,128)(2,1)S(1)}, u32[]{:S(2)}, u32[]{:S(2)}) collective-permute-start(bf16[64,768]{1,0:T(8,128)(2,1)S(1)} %add_convert_fusion.7), channel_id=1, source_target_pairs={{0,2},{1,3},{2,0},{3,1},{4,6},{5,7},{6,4},{7,5},{8,10},{9,11},{10,... | collective-permute-start | bytes 294920 | tf_op jit(solution)/shard_map/ppermute | solution.py:387
  56.7 5.2 %collective-permute-start.13 = (bf16[64,768]{1,0:T(8,128)(2,1)S(1)}, bf16[64,768]{1,0:T(8,128)(2,1)S(1)}, u32[]{:S(2)}, u32[]{:S(2)}) collective-permute-start(bf16[64,768]{1,0:T(8,128)(2,1)S(1)} %add_convert_fusion.8), channel_id=1, source_target_pairs={{0,8},{8,0},{16,24},{24,16},{1,9},{9,1},{17,25},{25,17},{2,10},{10... | collective-permute-start | bytes 294920 | tf_op jit(solution)/shard_map/ppermute | solution.py:387
  62.1 7.4 %collective-permute-start.18 = (bf16[32,2304]{1,0:T(8,128)(2,1)S(1)}, bf16[32,2304]{1,0:T(8,128)(2,1)S(1)}, u32[]{:S(2)}, u32[]{:S(2)}) collective-permute-start(bf16[32,2304]{1,0:T(8,128)(2,1)S(1)} %slice.262), channel_id=1, source_target_pairs={{0,16},{8,24},{16,0},{24,8},{1,17},{9,25},{17,1},{25,9},{2,18},{10... | collective-permute-start | bytes 442376 | tf_op jit(solution)/shard_map/ppermute | solution.py:387
  64.4 6.0 %collective-permute-start.19 = (bf16[64,1024]{1,0:T(8,128)(2,1)S(1)}, bf16[64,1024]{1,0:T(8,128)(2,1)S(1)}, u32[]{:S(2)}, u32[]{:S(2)}) collective-permute-start(bf16[64,1024]{1,0:T(8,128)(2,1)S(1)} %get-tuple-element.110), channel_id=1, source_target_pairs={{0,7},{1,2},{2,1},{3,4},{4,3},{5,6},{6,5},{7,0},{8,15},{9,10},{10,... | collective-permute-start | bytes 393224 | tf_op jit(solution)/shard_map/ppermute | solution.py:518

commit v11 on v10

--- a/solution.py
+++ b/solution.py
@@ -86,7 +86,7 @@
     return jnp.concatenate([half, half], axis=0)
 
 
-def gate_rows(tasks, keys, values, q_ref, half_mask, gate_ref, slope_ref, store_merged):
+def gate_rows(tasks, keys, values, q_ref, half_mask, gate_ref, slope_ref, store_merged, prefetch=None):
     half_scale = 0.5 * HEAD_DIM ** (-0.5)
 
     def scores(pair, m):
@@ -96,6 +96,8 @@
     ahead = scores(*tasks[0])
     for i, (pair, m) in enumerate(tasks):
         current = ahead
+        if prefetch is not None:
+            prefetch(pair)
         if i + 1 < len(tasks):
             ahead = scores(*tasks[i + 1])
         turned = split_heads(values(pair, m)).astype(F32).T.astype(BF)
@@ -162,12 +164,17 @@
     src = src + jnp.where(even, shift, 0)
     held = {}
 
+    def prefetch(pair):
+        start = (pair * LANES // step + 1) * step
+        for first in (0, width):
+            if start < width and first + start not in held:
+                held[first + start] = mm(halo_rows, kvw_ref[:, first + start : first + start + step]).astype(BF)
+
+    prefetch(-1)
+
     def rows(pair, m, first):
-        start = first + pair * LANES // step * step
-        if start not in held:
-            held[start] = mm(halo_rows, kvw_ref[:, start : start + step]).astype(BF)
         at = pair * LANES % step
-        block = held[start][:, at : at + LANES]
+        block = held[first + pair * LANES - at][:, at : at + LANES]
         mate = block[m * rim : (m + 1) * rim]
         other = block[(members + m) * rim : (members + m + 1) * rim]
         return jnp.concatenate([mate, other], axis=0)
@@ -183,7 +190,7 @@
 
     gate_rows(
         tasks_of(width, members), lambda pair, m: rows(pair, m, 0), values,
-        q_ref, half_mask_of(src, nodes, count), gate_ref, slope_ref, store_merged,
+        q_ref, half_mask_of(src, nodes, count), gate_ref, slope_ref, store_merged, prefetch,
     )
     sent = []
     for m in range(members):
@@ -509,13 +516,15 @@
                 [sds((members, nodes, width), F32)] + [sds((members * rim, width), BF)] * 2,
                 (ng_first, ng_last, ng_value, kv_weight),
             )
+        if step == steps - 1:
+            outgoing[0], back_other = lax.optimization_barrier((outgoing[0], back_other))
+            from_other = lax.ppermute(back_other, "band", others)
         arrived = [swap(out, *turn[step], count[turn[step][0]]) for out, turn in zip(outgoing, turns)]
         if step == 0:
             from_mate = lax.ppermute(back_mate, "band", mates)
             arrived, from_mate, back_other = lax.optimization_barrier((arrived, from_mate, back_other))
         if step == steps - 1:
-            arrived, back_other = lax.optimization_barrier((arrived, back_other))
-            from_other = lax.ppermute(back_other, "band", others)
+            arrived, from_other = lax.optimization_barrier((arrived, from_other))
         groups = [lower(terms) + [new] for terms, new in zip(groups, arrived)]
     terms = [jnp.concatenate([add_up(*group) for group in groups], axis=1)]
     for axis, bit in rest:
@@ -527,7 +536,6 @@
         [sds((rw, 2 * width), F32), sds((rw, width), F32), sds((rw, channels), F32)],
         (add_up(*terms[:-1]), terms[-1], hp),
     )
-    kv_grad, from_other = lax.optimization_barrier((kv_grad, from_other))
     hidden_grad = call(
         hidden_body,
         sds((members, nodes, width), F32),

time: 71.6 us -> 73.1 us (1.021)
  waiting for transfers between devices: 30.7 us -> 33.8 us
  Pallas kernels: 15.7 us -> 14 us
    ppermute x13, waiting for transfers between devices: 21.7 us -> 24.9 us  [swap(): return lax.ppermute(rows, axis, [(i, i ^ 1 << bit) for i in range(count)])]
    pallas_call x10, Pallas kernels: 15.7 us -> 14 us  [call(): pl.pallas_call(body, out_shape=out_shape, in_specs=[pl.BlockSpec(memory_s...]
  transfers between devices with their start and end apart: 20 -> 20, of which waited for: 14 -> 12; matrix products, arithmetic and copies ran while one was open for 1% -> 1% of each run, Pallas kernels for 11% -> 11%
where the time goes in v11:
time: 73.1 us; the launch traced here: 73 us
  waiting for transfers between devices  33.8 us (46%)
  starting transfers between devices  23.2 us (32%)
  Pallas kernels  14 us (19%)
  other arithmetic  0.96 us (1%)
  between operations  0.91 us (1%)
    ppermute x13, waiting for transfers between devices, swap(): return lax.ppermute(rows, axis, [(i, i ^ 1 << bit) for i in range(count)])  24.9 us
    pallas_call x10, Pallas kernels, call(): pl.pallas_call(body, out_shape=out_shape, in_specs=[pl.BlockSpec(memory_s...  14 us
    ppermute x13, starting transfers between devices, swap(): return lax.ppermute(rows, axis, [(i, i ^ 1 << bit) for i in range(count)])  13.9 us
    ppermute x3, waiting for transfers between devices, shards(): lax.ppermute(sent, 'member', [(i, i ^ s) for i in range(n_member)])  6.82 us
    ppermute x3, starting transfers between devices, shards(): lax.ppermute(sent, 'member', [(i, i ^ s) for i in range(n_member)])  5.72 us
    ppermute x1, starting transfers between devices, shards(): other = lax.ppermute(for_other, 'band', others)  3.4 us
  transfers between devices with their start and end apart: 20, of which 12 were waited for; matrix products, arithmetic and copies ran while one was open for 1% of the time, Pallas kernels for 11%

profile of v11, /device:TPU:0, one launch (start us, length us, event | category | flops | bytes accessed | tf_op | source)
XLA Modules:
  0.0 73.0 jit_solution(14793448055718451752)
XLA Ops:
  0.7 1.4 %shard_map.138 = (bf16[2,64,1024]{2,1,0:T(8,128)(2,1)S(1)}, s32[2,32]{1,0:T(2,128)S(1)}, bf16[64,1024]{1,0:T(8,128)(2,1)S(1)}, bf16[64,1024]{1,0:T(8,128)(2,1)S(1)}) custom-call(bf16[2,64,1024]{2,1,0:T(8,128)(2,1)} %hidden_hbm.1, s32[2,32]{1,0:T(2,128)} %halo_hbm.1), custom_call_target="tpu_custom_call" | custom-call | flops 10000000000 | bytes 1 | tf_op jit(solution)/shard_map/pallas_call | solution.py:28
  2.1 3.4 %collective-permute-start = (bf16[64,1024]{1,0:T(8,128)(2,1)S(1)}, bf16[64,1024]{1,0:T(8,128)(2,1)S(1)}, u32[]{:S(2)}, u32[]{:S(2)}) collective-permute-start(bf16[64,1024]{1,0:T(8,128)(2,1)S(1)} %get-tuple-element.60), channel_id=1, source_target_pairs={{0,7},{1,2},{2,1},{3,4},{4,3},{5,6},{6,5},{7,0},{8,15},{9,10},{10,... | collective-permute-start | bytes 393224 | tf_op jit(solution)/shard_map/ppermute | solution.py:431
  5.6 2.3 %shard_map.139 = (bf16[2,64,1024]{2,1,0:T(8,128)(2,1)S(1)}, bf16[8,2,128,256]{3,2,1,0:T(8,128)(2,1)S(1)}, bf16[8,2,128,256]{3,2,1,0:T(8,128)(2,1)S(1)}, f32[2,10...) custom-call(bf16[2,64,1024]{2,1,0:T(8,128)(2,1)S(1)} %get-tuple-elem, ...), custom_call_target="tpu_custom_call" | custom-call | flops 1 | bytes 1 | tf_op jit(solution)/shard_map/pallas_call | solution.py:28
  7.9 0.8 %collective-permute-done.other_ref = bf16[64,1024]{1,0:T(8,128)(2,1)S(1)} collective-permute-done((bf16[64,1024]{1,0:T(8,128)(2,1)S(1)}, bf16[64,1024]{1,0:T(8,128)(2,1)S(1)}, u32[]{:S(2)}, u32[]{:S(2)}) %collective-permute-start) | collective-permute-done | bytes 131104 | tf_op jit(solution)/shard_map/ppermute | solution.py:431
  8.7 1.7 %shard_map.140 = (bf16[2,64,1024]{2,1,0:T(8,128)(2,1)S(1)}, bf16[8,2,128,256]{3,2,1,0:T(8,128)(2,1)S(1)}, bf16[8,2,128,256]{3,2,1,0:T(8,128)(2,1)S(1)}, bf16[2,1...) custom-call(bf16[64,1024]{1,0:T(8,128)(2,1)S(1)} %collective-permute-done.other_ref, ...), custom_call_target="tpu_custom_call" | custom-call | flops 1 | bytes 1 | tf_op jit(solution)/shard_map/pallas_call | solution.py:28
  10.5 3.1 %collective-permute-start.4 = (bf16[208,256]{1,0:T(8,128)(2,1)S(1)}, bf16[208,256]{1,0:T(8,128)(2,1)S(1)}, u32[]{:S(2)}, u32[]{:S(2)}) collective-permute-start(bf16[208,256]{1,0:T(8,128)(2,1)S(1)} %get-tuple-element.65), channel_id=1, source_target_pairs={{0,8},{8,0},{16,24},{24,16},{1,9},{9,1},{17,25},{25,17},{2,10},{10... | collective-permute-start | bytes 319496 | tf_op jit(solution)/shard_map/ppermute | solution.py:468
  13.6 2.6 %collective-permute-start.3 = (bf16[208,256]{1,0:T(8,128)(2,1)S(1)}, bf16[208,256]{1,0:T(8,128)(2,1)S(1)}, u32[]{:S(2)}, u32[]{:S(2)}) collective-permute-start(bf16[208,256]{1,0:T(8,128)(2,1)S(1)} %get-tuple-element.65), channel_id=1, source_target_pairs={{0,16},{8,24},{16,0},{24,8},{1,17},{9,25},{17,1},{25,9},{2,18},{10... | collective-permute-start | bytes 319496 | tf_op jit(solution)/shard_map/ppermute | solution.py:468
  16.2 0.3 shard_map.141.refs_10_.ext_ref
  16.4 0.9 %collective-permute-done.4.refs_2_ = bf16[208,256]{1,0:T(8,128)(2,1)S(1)} collective-permute-done((bf16[208,256]{1,0:T(8,128)(2,1)S(1)}, bf16[208,256]{1,0:T(8,128)(2,1)S(1)}, u32[]{:S(2)}, u32[]{:S(2)}) %collective-permute-start.4) | collective-permute-done | bytes 106528 | tf_op jit(solution)/shard_map/ppermute | solution.py:468
  17.3 5.9 %collective-permute-done.3.refs_1_ = bf16[208,256]{1,0:T(8,128)(2,1)S(1)} collective-permute-done((bf16[208,256]{1,0:T(8,128)(2,1)S(1)}, bf16[208,256]{1,0:T(8,128)(2,1)S(1)}, u32[]{:S(2)}, u32[]{:S(2)}) %collective-permute-start.3) | collective-permute-done | bytes 106528 | tf_op jit(solution)/shard_map/ppermute | solution.py:468
  23.3 1.8 %shard_map.142 = (bf16[2,128,256]{2,1,0:T(8,128)(2,1)S(1)}, bf16[2,1024,256]{2,1,0:T(8,128)(2,1)S(1)}, bf16[256,1024]{1,0:T(8,128)(2,1)S(1)}, bf16[512,768]{1,0:T(8,128)(2,1)S(1)}, bf16[512,768]{1,0:T(8,128)(2,1)S(1)}) custom-call(bf16[208,256]{1,0:T(8,128)(2,1)S(1)} %collective-permute-done.2.refs_0_, bf16[208,256]{1,0:T(8,128)(2,1)S(1)} %collective-permute-done.3.refs_1_, ...), custom_call_target="tpu_custom_call" | custom-call | flops 1 | bytes 1 | tf_op jit(solution)/shard_map/pallas_call | solution.py:28
  25.1 0.1 collective-permute-start.5
  25.1 1.5 %shard_map.143 = (bf16[256,512]{1,0:T(8,128)(2,1)S(1)}, bf16[512,768]{1,0:T(8,128)(2,1)S(1)}, bf16[512,768]{1,0:T(8,128)(2,1)S(1)}) custom-call(bf16[2,1024,256]{2,1,0:T(8,128)(2,1)S(1)} %get-tuple-element.72.dm_ref, bf16[2,64,1024]{2,1,0:T(8,128)(2,1)S(1)} %get-tuple-element.73.own_value_ref, bf16[2,64,1024]{2,1,0:T(8,128)(2,1)S(1)} %get-tuple-element.74.halo_value_ref, ...), custom_call_target="tpu_custom_call" | custom-call | flops 1 | bytes 1 | tf_op jit(solution)/shard_map/pallas_call | solution.py:28
  26.6 0.6 collective-permute-start.6
  27.2 1.8 %shard_map.144 = (bf16[256,512]{1,0:T(8,128)(2,1)S(1)}, bf16[512,768]{1,0:T(8,128)(2,1)S(1)}, bf16[512,768]{1,0:T(8,128)(2,1)S(1)}) custom-call(bf16[2,128,256]{2,1,0:T(8,128)(2,1)S(1)} %get-tuple-element.86.grad_ref, bf16[2,1024,256]{2,1,0:T(8,128)(2,1)S(1)} %get-tuple-element.72.dm_ref, bf16[2,64,1024]{2,1,0:T(8,128)(2,1)S(1)} %get-tuple-element.73.own_value_ref, ...), custom_call_target="tpu_custom_call" | custom-call | flops 1 | bytes 1 | tf_op jit(solution)/shard_map/pallas_call | solution.py:28
  29.0 0.1 collective-permute-start.7
  29.1 0.1 add_convert_fusion.2
  29.2 0.1 add_convert_fusion.1
  29.3 2.0 %collective-permute-done.7 = bf16[512,768]{1,0:T(8,128)(2,1)S(1)} collective-permute-done((bf16[512,768]{1,0:T(8,128)(2,1)S(1)}, bf16[512,768]{1,0:T(8,128)(2,1)S(1)}, u32[]{:S(2)}, u32[]{:S(2)}) %collective-permute-start.7) | collective-permute-done | bytes 786464 | tf_op jit(solution)/shard_map/ppermute | solution.py:394
  31.3 0.1 add_convert_fusion
  31.4 1.2 %collective-permute-start.8 = (bf16[256,768]{1,0:T(8,128)(2,1)S(1)}, bf16[256,768]{1,0:T(8,128)(2,1)S(1)}, u32[]{:S(2)}, u32[]{:S(2)}) collective-permute-start(bf16[256,768]{1,0:T(8,128)(2,1)S(1)} %add_convert_fusion.2), channel_id=1, source_target_pairs={{0,2},{1,3},{2,0},{3,1},{4,6},{5,7},{6,4},{7,5},{8,10},{9,11},{10,... | collective-permute-start | bytes 1179656 | tf_op jit(solution)/shard_map/ppermute | solution.py:394
  32.6 2.4 %collective-permute-start.9 = (bf16[256,768]{1,0:T(8,128)(2,1)S(1)}, bf16[256,768]{1,0:T(8,128)(2,1)S(1)}, u32[]{:S(2)}, u32[]{:S(2)}) collective-permute-start(bf16[256,768]{1,0:T(8,128)(2,1)S(1)} %add_convert_fusion.1), channel_id=1, source_target_pairs={{0,4},{1,5},{2,6},{3,7},{4,0},{5,1},{6,2},{7,3},{8,12},{9,13},{10,... | collective-permute-start | bytes 1179656 | tf_op jit(solution)/shard_map/ppermute | solution.py:394
  35.0 1.7 %collective-permute-start.10 = (bf16[256,768]{1,0:T(8,128)(2,1)S(1)}, bf16[256,768]{1,0:T(8,128)(2,1)S(1)}, u32[]{:S(2)}, u32[]{:S(2)}) collective-permute-start(bf16[256,768]{1,0:T(8,128)(2,1)S(1)} %add_convert_fusion), channel_id=1, source_target_pairs={{0,8},{8,0},{16,24},{24,16},{1,9},{9,1},{17,25},{25,17},{2,10},{10... | collective-permute-start | bytes 1179656 | tf_op jit(solution)/shard_map/ppermute | solution.py:394
  36.7 1.3 %shard_map.145 = (f32[2,64,1024]{2,1,0:T(8,128)S(1)}, bf16[64,1024]{1,0:T(8,128)(2,1)S(1)}, bf16[64,1024]{1,0:T(8,128)(2,1)S(1)}) custom-call(bf16[256,512]{1,0:T(8,128)(2,1)S(1)} %get-tuple-element.78.first_ref, bf16[256,512]{1,0:T(8,128)(2,1)S(1)} %get-tuple-element.94.last_ref, bf16[256,1024]{1,0:T(8,128)(2,1)S(1)} %get-tuple-element.77.ngv_ref, ...), custom_call_target="tpu_custom_call" | custom-call | flops 1 | bytes 1 | tf_op jit(solution)/shard_map/pallas_call | solution.py:28
  38.0 0.1 collective-permute-start.11
  38.1 1.3 %collective-permute-done.11.from_mate_ref = bf16[64,1024]{1,0:T(8,128)(2,1)S(1)} collective-permute-done((bf16[64,1024]{1,0:T(8,128)(2,1)S(1)}, bf16[64,1024]{1,0:T(8,128)(2,1)S(1)}, u32[]{:S(2)}, u32[]{:S(2)}) %collective-permute-start.11) | collective-permute-done | bytes 131104 | tf_op jit(solution)/shard_map/ppermute | solution.py:524
  39.4 3.2 %collective-permute-done.8 = bf16[256,768]{1,0:T(8,128)(2,1)S(1)} collective-permute-done((bf16[256,768]{1,0:T(8,128)(2,1)S(1)}, bf16[256,768]{1,0:T(8,128)(2,1)S(1)}, u32[]{:S(2)}, u32[]{:S(2)}) %collective-permute-start.8) | collective-permute-done | bytes 393248 | tf_op jit(solution)/shard_map/ppermute | solution.py:394
  42.6 1.5 %collective-permute-done.9 = bf16[256,768]{1,0:T(8,128)(2,1)S(1)} collective-permute-done((bf16[256,768]{1,0:T(8,128)(2,1)S(1)}, bf16[256,768]{1,0:T(8,128)(2,1)S(1)}, u32[]{:S(2)}, u32[]{:S(2)}) %collective-permute-start.9) | collective-permute-done | bytes 393248 | tf_op jit(solution)/shard_map/ppermute | solution.py:394
  44.1 1.5 %collective-permute-done.10 = bf16[256,768]{1,0:T(8,128)(2,1)S(1)} collective-permute-done((bf16[256,768]{1,0:T(8,128)(2,1)S(1)}, bf16[256,768]{1,0:T(8,128)(2,1)S(1)}, u32[]{:S(2)}, u32[]{:S(2)}) %collective-permute-start.10) | collective-permute-done | bytes 393248 | tf_op jit(solution)/shard_map/ppermute | solution.py:394
  45.6 0.1 add_convert_fusion.4
  45.7 0.1 add_convert_fusion.3
  45.8 0.9 %collective-permute-start.16 = (bf16[128,768]{1,0:T(8,128)(2,1)S(1)}, bf16[128,768]{1,0:T(8,128)(2,1)S(1)}, u32[]{:S(2)}, u32[]{:S(2)}) collective-permute-start(bf16[128,768]{1,0:T(8,128)(2,1)S(1)} %add_convert_fusion.3), channel_id=1, source_target_pairs={{0,2},{1,3},{2,0},{3,1},{4,6},{5,7},{6,4},{7,5},{8,10},{9,11},{10,... | collective-permute-start | bytes 589832 | tf_op jit(solution)/shard_map/ppermute | solution.py:394
  46.7 1.7 %collective-permute-start.14 = (bf16[128,768]{1,0:T(8,128)(2,1)S(1)}, bf16[128,768]{1,0:T(8,128)(2,1)S(1)}, u32[]{:S(2)}, u32[]{:S(2)}) collective-permute-start(bf16[128,768]{1,0:T(8,128)(2,1)S(1)} %add_convert_fusion.4), channel_id=1, source_target_pairs={{0,8},{8,0},{16,24},{24,16},{1,9},{9,1},{17,25},{25,17},{2,10},{10... | collective-permute-start | bytes 589832 | tf_op jit(solution)/shard_map/ppermute | solution.py:394
  48.4 0.1 add_convert_fusion.5
  48.5 0.3 collective-permute-start.12
  48.8 2.7 %collective-permute-done.16 = bf16[128,768]{1,0:T(8,128)(2,1)S(1)} collective-permute-done((bf16[128,768]{1,0:T(8,128)(2,1)S(1)}, bf16[128,768]{1,0:T(8,128)(2,1)S(1)}, u32[]{:S(2)}, u32[]{:S(2)}) %collective-permute-start.16) | collective-permute-done | bytes 196640 | tf_op jit(solution)/shard_map/ppermute | solution.py:394
  51.6 0.9 %collective-permute-start.17 = (bf16[64,768]{1,0:T(8,128)(2,1)S(1)}, bf16[64,768]{1,0:T(8,128)(2,1)S(1)}, u32[]{:S(2)}, u32[]{:S(2)}) collective-permute-start(bf16[64,768]{1,0:T(8,128)(2,1)S(1)} %add_convert_fusion.6), channel_id=1, source_target_pairs={{0,4},{1,5},{2,6},{3,7},{4,0},{5,1},{6,2},{7,3},{8,12},{9,13},{10,... | collective-permute-start | bytes 294920 | tf_op jit(solution)/shard_map/ppermute | solution.py:394
  52.4 2.5 %collective-permute-done.12 = bf16[128,768]{1,0:T(8,128)(2,1)S(1)} collective-permute-done((bf16[128,768]{1,0:T(8,128)(2,1)S(1)}, bf16[128,768]{1,0:T(8,128)(2,1)S(1)}, u32[]{:S(2)}, u32[]{:S(2)}) %collective-permute-start.12) | collective-permute-done | bytes 196640 | tf_op jit(solution)/shard_map/ppermute | solution.py:394
  54.9 0.1 collective-permute-start.18
  55.1 0.9 %collective-permute-start.15 = (bf16[64,768]{1,0:T(8,128)(2,1)S(1)}, bf16[64,768]{1,0:T(8,128)(2,1)S(1)}, u32[]{:S(2)}, u32[]{:S(2)}) collective-permute-start(bf16[64,768]{1,0:T(8,128)(2,1)S(1)} %add_convert_fusion.7), channel_id=1, source_target_pairs={{0,2},{1,3},{2,0},{3,1},{4,6},{5,7},{6,4},{7,5},{8,10},{9,11},{10,... | collective-permute-start | bytes 294920 | tf_op jit(solution)/shard_map/ppermute | solution.py:394
  56.0 1.0 %collective-permute-start.13 = (bf16[64,768]{1,0:T(8,128)(2,1)S(1)}, bf16[64,768]{1,0:T(8,128)(2,1)S(1)}, u32[]{:S(2)}, u32[]{:S(2)}) collective-permute-start(bf16[64,768]{1,0:T(8,128)(2,1)S(1)} %add_convert_fusion.8), channel_id=1, source_target_pairs={{0,8},{8,0},{16,24},{24,16},{1,9},{9,1},{17,25},{25,17},{2,10},{10... | collective-permute-start | bytes 294920 | tf_op jit(solution)/shard_map/ppermute | solution.py:394
  57.0 4.7 %collective-permute-done.15 = bf16[64,768]{1,0:T(8,128)(2,1)S(1)} collective-permute-done((bf16[64,768]{1,0:T(8,128)(2,1)S(1)}, bf16[64,768]{1,0:T(8,128)(2,1)S(1)}, u32[]{:S(2)}, u32[]{:S(2)}) %collective-permute-start.15) | collective-permute-done | bytes 98336 | tf_op jit(solution)/shard_map/ppermute | solution.py:394
  61.7 0.1 convert_add_fusion.2
  61.8 0.1 convert_add_fusion
  62.0 2.2 %collective-permute-start.19 = (bf16[32,2304]{1,0:T(8,128)(2,1)S(1)}, bf16[32,2304]{1,0:T(8,128)(2,1)S(1)}, u32[]{:S(2)}, u32[]{:S(2)}) collective-permute-start(bf16[32,2304]{1,0:T(8,128)(2,1)S(1)} %slice.262), channel_id=1, source_target_pairs={{0,16},{8,24},{16,0},{24,8},{1,17},{9,25},{17,1},{25,9},{2,18},{10... | collective-permute-start | bytes 442376 | tf_op jit(solution)/shard_map/ppermute | solution.py:394
  64.2 1.1 %shard_map.146 = f32[2,64,1024]{2,1,0:T(8,128)} custom-call(f32[2,64,1024]{2,1,0:T(8,128)S(1)} %get-tuple-element.95.own_ref, bf16[64,1024]{1,0:T(8,128)(2,1)S(1)} %collective-permute-done.11.from_mate_ref, bf16[64,1024]{1,0:T(8,128)(2,1)S(1)} %collective-permute-done.18.from_other_ref, s32[2,32]{1,0:T(2,128)S(1)} %get-tuple-element.109.halo_ref), custom_call_target="tpu_custom_call" | custom-call | flops 1 | bytes 1 | tf_op jit(solution)/shard_map/pallas_call | solution.py:28
  65.3 6.9 %collective-permute-done.19.arrived_ref = bf16[32,2304]{1,0:T(8,128)(2,1)S(1)} collective-permute-done((bf16[32,2304]{1,0:T(8,128)(2,1)S(1)}, bf16[32,2304]{1,0:T(8,128)(2,1)S(1)}, u32[]{:S(2)}, u32[]{:S(2)}) %collective-permute-start.19) | collective-permute-done | bytes 147488 | tf_op jit(solution)/shard_map/ppermute | solution.py:394
  72.1 0.9 %shard_map.147 = (f32[32,2048]{1,0:T(8,128)}, f32[32,1024]{1,0:T(8,128)}, f32[32,100]{1,0:T(8,128)}) custom-call(f32[32,2304]{1,0:T(8,128)S(1)} %slice.220.own_ref, bf16[32,2304]{1,0:T(8,128)(2,1)S(1)} %collective-permute-done.19.arrived_ref, bf16[100,1024]{1,0:T(8,128)(2,1)S(1)} %bitcast.4), custom_call_target="tpu_custom_call" | custom-call | flops 1 | bytes 1 | tf_op jit(solution)/shard_map/pallas_call | solution.py:28
  (34 shorter events, 0.3 us)
Async XLA Ops:
  0.6 4.9 %copy-start.2 = (bf16[256,1024]{1,0:T(8,128)(2,1)S(1)}, bf16[256,1024]{1,0:T(8,128)(2,1)}, u32[]{:S(2)}) copy-start(bf16[256,1024]{1,0:T(8,128)(2,1)} %q_ref.7) | copy-start | bytes 1572868
  0.6 4.9 %copy-start.6 = (s32[3,256]{1,0:T(4,128)S(1)}, s32[3,256]{1,0:T(4,128)}, u32[]{:S(2)}) copy-start(s32[3,256]{1,0:T(4,128)} %src_ref.3) | copy-start | bytes 9220
  0.7 4.9 %copy-start.1 = (bf16[1024,1024]{1,0:T(8,128)(2,1)S(1)}, bf16[1024,1024]{1,0:T(8,128)(2,1)}, u32[]{:S(2)}) copy-start(bf16[1024,1024]{1,0:T(8,128)(2,1)} %wo_ref.3) | copy-start | bytes 6291460
  0.7 4.9 %copy-start.8 = (f32[100]{0:T(128)S(1)}, f32[100]{0:T(128)}, u32[]{:S(2)}) copy-start(f32[100]{0:T(128)} %param.19) | copy-start | bytes 1204
  0.7 4.9 %copy-start.7 = (f32[256]{0:T(256)S(1)}, f32[256]{0:T(256)}, u32[]{:S(2)}) copy-start(f32[256]{0:T(256)} %param.18) | copy-start | bytes 3076
  0.7 4.9 %copy-start.4 = (f32[100,256]{1,0:T(8,128)S(1)}, f32[100,256]{1,0:T(8,128)}, u32[]{:S(2)}) copy-start(f32[100,256]{1,0:T(8,128)} %init_ref.1) | copy-start | bytes 307204
  0.7 4.9 %copy-start.3 = (bf16[1024,100]{0,1:T(8,128)(2,1)S(1)}, bf16[1024,100]{0,1:T(8,128)(2,1)}, u32[]{:S(2)}) copy-start(bf16[1024,100]{0,1:T(8,128)(2,1)} %param.15) | copy-start | bytes 614404
  0.7 4.9 %copy-start = (bf16[1024,2048]{1,0:T(8,128)(2,1)S(1)}, bf16[1024,2048]{1,0:T(8,128)(2,1)}, u32[]{:S(2)}) copy-start(bf16[1024,2048]{1,0:T(8,128)(2,1)} %kvw_ref.5) | copy-start | bytes 12582916
  2.1 6.6 %collective-permute-start = (bf16[64,1024]{1,0:T(8,128)(2,1)S(1)}, bf16[64,1024]{1,0:T(8,128)(2,1)S(1)}, u32[]{:S(2)}, u32[]{:S(2)}) collective-permute-start(bf16[64,1024]{1,0:T(8,128)(2,1)S(1)} %get-tuple-element.60), channel_id=1, source_target_pairs={{0,7},{1,2},{2,1},{3,4},{4,3},{5,6},{6,5},{7,0},{8,15},{9,10},{10,... | collective-permute-start | bytes 393224 | tf_op jit(solution)/shard_map/ppermute | solution.py:431
  5.5 3.2 %collective-permute-start.1 = (bf16[64,1024]{1,0:T(8,128)(2,1)S(1)}, bf16[64,1024]{1,0:T(8,128)(2,1)S(1)}, u32[]{:S(2)}, u32[]{:S(2)}) collective-permute-start(bf16[64,1024]{1,0:T(8,128)(2,1)S(1)} %get-tuple-element.61), channel_id=1, source_target_pairs={{0,1},{1,0},{2,3},{3,2},{4,5},{5,4},{6,7},{7,6},{8,9},{9,8},{10,11... | collective-permute-start | bytes 393224 | tf_op jit(solution)/shard_map/ppermute | solution.py:432
  8.7 14.5 %copy-start.5 = (f32[100,256]{1,0:T(8,128)S(1)}, f32[100,256]{1,0:T(8,128)}, u32[]{:S(2)}) copy-start(f32[100,256]{1,0:T(8,128)} %refs_5_.1) | copy-start | bytes 307204
  10.5 6.9 %collective-permute-start.4 = (bf16[208,256]{1,0:T(8,128)(2,1)S(1)}, bf16[208,256]{1,0:T(8,128)(2,1)S(1)}, u32[]{:S(2)}, u32[]{:S(2)}) collective-permute-start(bf16[208,256]{1,0:T(8,128)(2,1)S(1)} %get-tuple-element.65), channel_id=1, source_target_pairs={{0,8},{8,0},{16,24},{24,16},{1,9},{9,1},{17,25},{25,17},{2,10},{10... | collective-permute-start | bytes 319496 | tf_op jit(solution)/shard_map/ppermute | solution.py:468
  13.6 9.7 %collective-permute-start.3 = (bf16[208,256]{1,0:T(8,128)(2,1)S(1)}, bf16[208,256]{1,0:T(8,128)(2,1)S(1)}, u32[]{:S(2)}, u32[]{:S(2)}) collective-permute-start(bf16[208,256]{1,0:T(8,128)(2,1)S(1)} %get-tuple-element.65), channel_id=1, source_target_pairs={{0,16},{8,24},{16,0},{24,8},{1,17},{9,25},{17,1},{25,9},{2,18},{10... | collective-permute-start | bytes 319496 | tf_op jit(solution)/shard_map/ppermute | solution.py:468
  16.2 7.1 %collective-permute-start.2 = (bf16[208,256]{1,0:T(8,128)(2,1)S(1)}, bf16[208,256]{1,0:T(8,128)(2,1)S(1)}, u32[]{:S(2)}, u32[]{:S(2)}) collective-permute-start(bf16[208,256]{1,0:T(8,128)(2,1)S(1)} %get-tuple-element.65), channel_id=1, source_target_pairs={{0,24},{8,16},{16,8},{24,0},{1,25},{9,17},{17,9},{25,1},{2,26},{10... | collective-permute-start | bytes 319496 | tf_op jit(solution)/shard_map/ppermute | solution.py:468
  25.1 4.0 %collective-permute-start.5 = (bf16[512,768]{1,0:T(8,128)(2,1)S(1)}, bf16[512,768]{1,0:T(8,128)(2,1)S(1)}, u32[]{:S(2)}, u32[]{:S(2)}) collective-permute-start(bf16[512,768]{1,0:T(8,128)(2,1)S(1)} %get-tuple-element.80), channel_id=1, source_target_pairs={{0,1},{1,0},{2,3},{3,2},{4,5},{5,4},{6,7},{7,6},{8,9},{9,8},{10,11... | collective-permute-start | bytes 2359304 | tf_op jit(solution)/shard_map/ppermute | solution.py:394
  26.6 2.5 %collective-permute-start.6 = (bf16[512,768]{1,0:T(8,128)(2,1)S(1)}, bf16[512,768]{1,0:T(8,128)(2,1)S(1)}, u32[]{:S(2)}, u32[]{:S(2)}) collective-permute-start(bf16[512,768]{1,0:T(8,128)(2,1)S(1)} %get-tuple-element.82), channel_id=1, source_target_pairs={{0,1},{1,0},{2,3},{3,2},{4,5},{5,4},{6,7},{7,6},{8,9},{9,8},{10,11... | collective-permute-start | bytes 2359304 | tf_op jit(solution)/shard_map/ppermute | solution.py:394
  29.0 2.4 %collective-permute-start.7 = (bf16[512,768]{1,0:T(8,128)(2,1)S(1)}, bf16[512,768]{1,0:T(8,128)(2,1)S(1)}, u32[]{:S(2)}, u32[]{:S(2)}) collective-permute-start(bf16[512,768]{1,0:T(8,128)(2,1)S(1)} %get-tuple-element.89), channel_id=1, source_target_pairs={{0,1},{1,0},{2,3},{3,2},{4,5},{5,4},{6,7},{7,6},{8,9},{9,8},{10,11... | collective-permute-start | bytes 2359304 | tf_op jit(solution)/shard_map/ppermute | solution.py:394
  31.4 11.2 %collective-permute-start.8 = (bf16[256,768]{1,0:T(8,128)(2,1)S(1)}, bf16[256,768]{1,0:T(8,128)(2,1)S(1)}, u32[]{:S(2)}, u32[]{:S(2)}) collective-permute-start(bf16[256,768]{1,0:T(8,128)(2,1)S(1)} %add_convert_fusion.2), channel_id=1, source_target_pairs={{0,2},{1,3},{2,0},{3,1},{4,6},{5,7},{6,4},{7,5},{8,10},{9,11},{10,... | collective-permute-start | bytes 1179656 | tf_op jit(solution)/shard_map/ppermute | solution.py:394
  32.6 11.5 %collective-permute-start.9 = (bf16[256,768]{1,0:T(8,128)(2,1)S(1)}, bf16[256,768]{1,0:T(8,128)(2,1)S(1)}, u32[]{:S(2)}, u32[]{:S(2)}) collective-permute-start(bf16[256,768]{1,0:T(8,128)(2,1)S(1)} %add_convert_fusion.1), channel_id=1, source_target_pairs={{0,4},{1,5},{2,6},{3,7},{4,0},{5,1},{6,2},{7,3},{8,12},{9,13},{10,... | collective-permute-start | bytes 1179656 | tf_op jit(solution)/shard_map/ppermute | solution.py:394
  35.0 10.6 %collective-permute-start.10 = (bf16[256,768]{1,0:T(8,128)(2,1)S(1)}, bf16[256,768]{1,0:T(8,128)(2,1)S(1)}, u32[]{:S(2)}, u32[]{:S(2)}) collective-permute-start(bf16[256,768]{1,0:T(8,128)(2,1)S(1)} %add_convert_fusion), channel_id=1, source_target_pairs={{0,8},{8,0},{16,24},{24,16},{1,9},{9,1},{17,25},{25,17},{2,10},{10... | collective-permute-start | bytes 1179656 | tf_op jit(solution)/shard_map/ppermute | solution.py:394
  38.0 1.4 %collective-permute-start.11 = (bf16[64,1024]{1,0:T(8,128)(2,1)S(1)}, bf16[64,1024]{1,0:T(8,128)(2,1)S(1)}, u32[]{:S(2)}, u32[]{:S(2)}) collective-permute-start(bf16[64,1024]{1,0:T(8,128)(2,1)S(1)} %get-tuple-element.99), channel_id=1, source_target_pairs={{0,1},{1,0},{2,3},{3,2},{4,5},{5,4},{6,7},{7,6},{8,9},{9,8},{10,11... | collective-permute-start | bytes 393224 | tf_op jit(solution)/shard_map/ppermute | solution.py:524
  45.8 5.7 %collective-permute-start.16 = (bf16[128,768]{1,0:T(8,128)(2,1)S(1)}, bf16[128,768]{1,0:T(8,128)(2,1)S(1)}, u32[]{:S(2)}, u32[]{:S(2)}) collective-permute-start(bf16[128,768]{1,0:T(8,128)(2,1)S(1)} %add_convert_fusion.3), channel_id=1, source_target_pairs={{0,2},{1,3},{2,0},{3,1},{4,6},{5,7},{6,4},{7,5},{8,10},{9,11},{10,... | collective-permute-start | bytes 589832 | tf_op jit(solution)/shard_map/ppermute | solution.py:394
  46.7 8.4 %collective-permute-start.14 = (bf16[128,768]{1,0:T(8,128)(2,1)S(1)}, bf16[128,768]{1,0:T(8,128)(2,1)S(1)}, u32[]{:S(2)}, u32[]{:S(2)}) collective-permute-start(bf16[128,768]{1,0:T(8,128)(2,1)S(1)} %add_convert_fusion.4), channel_id=1, source_target_pairs={{0,8},{8,0},{16,24},{24,16},{1,9},{9,1},{17,25},{25,17},{2,10},{10... | collective-permute-start | bytes 589832 | tf_op jit(solution)/shard_map/ppermute | solution.py:394
  48.5 6.4 %collective-permute-start.12 = (bf16[128,768]{1,0:T(8,128)(2,1)S(1)}, bf16[128,768]{1,0:T(8,128)(2,1)S(1)}, u32[]{:S(2)}, u32[]{:S(2)}) collective-permute-start(bf16[128,768]{1,0:T(8,128)(2,1)S(1)} %add_convert_fusion.5), channel_id=1, source_target_pairs={{0,4},{1,5},{2,6},{3,7},{4,0},{5,1},{6,2},{7,3},{8,12},{9,13},{10,... | collective-permute-start | bytes 589832 | tf_op jit(solution)/shard_map/ppermute | solution.py:394
  51.6 5.5 %collective-permute-start.17 = (bf16[64,768]{1,0:T(8,128)(2,1)S(1)}, bf16[64,768]{1,0:T(8,128)(2,1)S(1)}, u32[]{:S(2)}, u32[]{:S(2)}) collective-permute-start(bf16[64,768]{1,0:T(8,128)(2,1)S(1)} %add_convert_fusion.6), channel_id=1, source_target_pairs={{0,4},{1,5},{2,6},{3,7},{4,0},{5,1},{6,2},{7,3},{8,12},{9,13},{10,... | collective-permute-start | bytes 294920 | tf_op jit(solution)/shard_map/ppermute | solution.py:394
  54.9 6.8 %collective-permute-start.18 = (bf16[64,1024]{1,0:T(8,128)(2,1)S(1)}, bf16[64,1024]{1,0:T(8,128)(2,1)S(1)}, u32[]{:S(2)}, u32[]{:S(2)}) collective-permute-start(bf16[64,1024]{1,0:T(8,128)(2,1)S(1)} %get-tuple-element.107), channel_id=1, source_target_pairs={{0,7},{1,2},{2,1},{3,4},{4,3},{5,6},{6,5},{7,0},{8,15},{9,10},{10,... | collective-permute-start | bytes 393224 | tf_op jit(solution)/shard_map/ppermute | solution.py:521
  55.1 6.6 %collective-permute-start.15 = (bf16[64,768]{1,0:T(8,128)(2,1)S(1)}, bf16[64,768]{1,0:T(8,128)(2,1)S(1)}, u32[]{:S(2)}, u32[]{:S(2)}) collective-permute-start(bf16[64,768]{1,0:T(8,128)(2,1)S(1)} %add_convert_fusion.7), channel_id=1, source_target_pairs={{0,2},{1,3},{2,0},{3,1},{4,6},{5,7},{6,4},{7,5},{8,10},{9,11},{10,... | collective-permute-start | bytes 294920 | tf_op jit(solution)/shard_map/ppermute | solution.py:394
  56.0 5.7 %collective-permute-start.13 = (bf16[64,768]{1,0:T(8,128)(2,1)S(1)}, bf16[64,768]{1,0:T(8,128)(2,1)S(1)}, u32[]{:S(2)}, u32[]{:S(2)}) collective-permute-start(bf16[64,768]{1,0:T(8,128)(2,1)S(1)} %add_convert_fusion.8), channel_id=1, source_target_pairs={{0,8},{8,0},{16,24},{24,16},{1,9},{9,1},{17,25},{25,17},{2,10},{10... | collective-permute-start | bytes 294920 | tf_op jit(solution)/shard_map/ppermute | solution.py:394
  62.0 10.1 %collective-permute-start.19 = (bf16[32,2304]{1,0:T(8,128)(2,1)S(1)}, bf16[32,2304]{1,0:T(8,128)(2,1)S(1)}, u32[]{:S(2)}, u32[]{:S(2)}) collective-permute-start(bf16[32,2304]{1,0:T(8,128)(2,1)S(1)} %slice.262), channel_id=1, source_target_pairs={{0,16},{8,24},{16,0},{24,8},{1,17},{9,25},{17,1},{25,9},{2,18},{10... | collective-permute-start | bytes 442376 | tf_op jit(solution)/shard_map/ppermute | solution.py:394

commit v12 on v11

--- a/solution.py
+++ b/solution.py
@@ -86,12 +86,9 @@
     return jnp.concatenate([half, half], axis=0)
 
 
-def gate_rows(tasks, keys, values, q_ref, half_mask, gate_ref, slope_ref, store_merged, prefetch=None):
-    half_scale = 0.5 * HEAD_DIM ** (-0.5)
-
+def gate_rows(tasks, keys, values, qt_ref, half_mask, gate_ref, slope_ref, store_merged, prefetch=None):
     def scores(pair, m):
-        q = (q_ref[:, pair * LANES : (pair + 1) * LANES].astype(F32) * half_scale).astype(BF)
-        return mm(split_heads(keys(pair, m)), q, NT)
+        return mm(split_heads(keys(pair, m)), qt_ref[pair * LANES : (pair + 1) * LANES, :])
 
     ahead = scores(*tasks[0])
     for i, (pair, m) in enumerate(tasks):
@@ -114,10 +111,12 @@
 
 def own_body(
     hidden_ref, wo_ref, hp_ref, q_ref, kvw_ref, init_ref, chw_ref, lat_ref, src_ref,
-    value_ref, gate_ref, slope_ref, merged_ref, pt_ref, p_ref, base_ref, weight_ref, chw_pad, hp_pad,
+    value_ref, gate_ref, slope_ref, merged_ref, qt_ref, pt_ref, p_ref, base_ref, weight_ref, chw_pad, hp_pad,
 ):
     channels = hp_ref.shape[0]
     members, nodes, width = hidden_ref.shape
+    half_scale = 0.5 * HEAD_DIM ** (-0.5)
+    qt_ref[...] = (q_ref[...].astype(F32) * half_scale).T.astype(BF)
     hidden = jnp.concatenate([hidden_ref[m] for m in range(members)], axis=0)
     rows = mm(hidden, kvw_ref[...]).astype(BF)
 
@@ -134,7 +133,7 @@
         tasks_of(width, members),
         lambda pair, m: part(pair, m, 0),
         lambda pair, m: part(pair, m, width),
-        q_ref, half_mask_of(src_ref[...], 0, nodes), gate_ref, slope_ref, store_merged,
+        qt_ref, half_mask_of(src_ref[...], 0, nodes), gate_ref, slope_ref, store_merged,
     )
     hp_pad[...] = jnp.zeros_like(hp_pad)
     hp_pad[0:channels, :] = hp_ref[...].astype(F32)
@@ -149,11 +148,11 @@
 
 
 def halo_body(
-    send_rows, nodes, other_ref, mate_ref, own_ref, kvw_ref, q_ref, src_ref, p_ref,
+    send_rows, nodes, other_ref, mate_ref, own_ref, kvw_ref, qt_ref, src_ref, p_ref,
     value_ref, gate_ref, slope_ref, merged_ref, part_ref, send_ref,
 ):
     members, count, width = value_ref.shape
-    points = q_ref.shape[0]
+    points = qt_ref.shape[1]
     rim = count // 2
     step = 2 * LANES
     halo_rows = jnp.concatenate([mate_ref[...], other_ref[...]], axis=0)
@@ -190,7 +189,7 @@
 
     gate_rows(
         tasks_of(width, members), lambda pair, m: rows(pair, m, 0), values,
-        q_ref, half_mask_of(src, nodes, count), gate_ref, slope_ref, store_merged, prefetch,
+        qt_ref, half_mask_of(src, nodes, count), gate_ref, slope_ref, store_merged, prefetch,
     )
     sent = []
     for m in range(members):
@@ -275,11 +274,10 @@
 
 def value_body(n_member, n_band, *refs):
     recv_refs = refs[: n_member - 1]
-    part_ref, base_ref, truth_ref, weight_ref, pt_ref, *gate_refs, ext_ref = refs[n_member - 1 : n_member + 7]
-    grad_ref, dm_ref, ng_ref, *out_refs = refs[n_member + 7 :]
+    part_ref, base_ref, truth_ref, weight_ref, p_ref, *gate_refs, ext_ref = refs[n_member - 1 : n_member + 7]
+    grad_ref, ng_ref, *out_refs = refs[n_member + 7 :]
     own_rows = gate_refs[0].shape[2] // 2
-    group_width = out_refs[0].shape[1]
-    members, width, _ = dm_ref.shape
+    members, width = grad_ref.shape[0], p_ref.shape[1]
     ext = ng_ref.shape[0] // members
     channels = truth_ref.shape[0]
     total = members * n_member
@@ -301,51 +299,61 @@
             slopes = slopes + soft_slope(own[m] - other)
         gap = soft_slope(own[m] + base_ref[0:channels, :] - truth_ref[...])
         grad_ref[m, 0:channels, :] = (weight_ref[...] * (gap / total - spread * slopes)).astype(BF)
-    for m in range(members):
-        dm_ref[m] = mm(pt_ref[...], grad_ref[m]).astype(BF)
+    dm = [mm(grad_ref[m].astype(F32).T.astype(BF), p_ref[...]).astype(BF) for m in range(members)]
     for pair in range(width // LANES):
         cols = slice(pair * LANES, (pair + 1) * LANES)
         for m in range(members):
-            result = mm(joined(gate_refs, pair, m), dm_ref[m, cols, :], NT)
+            result = mm(joined(gate_refs, pair, m), dm[m][:, cols])
             ng_ref[m * ext : (m + 1) * ext, cols] = select_rows(result, own_rows).astype(BF)
+    group_width = out_refs[0].shape[1]
     store_group(mm(ext_ref[...], ng_ref[:, 0:group_width]), 0, n_member, n_band, 0, out_refs)
 
 
-def key_gradients(pairs, dm_ref, value_refs, slope_refs, q_ref, ng_ref):
-    members = dm_ref.shape[0]
+def key_gradients(pairs, grad_ref, pt_ref, value_refs, slope_refs, q_ref, ng_ref):
+    members = grad_ref.shape[0]
     ext = ng_ref.shape[0] // members
+    own_rows = value_refs[0].shape[1]
     scale = HEAD_DIM ** (-0.5)
-    for place, pair in enumerate(pairs):
+    tasks = [(place, pair, m) for place, pair in enumerate(pairs) for m in range(members)]
+    first, count = pairs[0] * LANES, len(pairs) * LANES
+    dm = [mm(pt_ref[first : first + count, :], grad_ref[m]).astype(BF) for m in range(members)]
+
+    def gate_gradients(place, pair, m):
         cols = slice(pair * LANES, (pair + 1) * LANES)
-        for m in range(members):
-            value = jnp.concatenate([split_heads(ref[m, :, cols]) for ref in value_refs], axis=0)
-            dgate = mm(value, dm_ref[m, cols, :])
-            dscore = (dgate * joined(slope_refs, pair, m).astype(F32)).astype(BF)
-            keys = select_rows(mm(dscore, q_ref[:, cols]), value_refs[0].shape[1]) * scale
-            ng_ref[m * ext : (m + 1) * ext, place * LANES : (place + 1) * LANES] = keys.astype(BF)
+        value = jnp.concatenate([split_heads(ref[m, :, cols]) for ref in value_refs], axis=0)
+        return mm(value, dm[m][place * LANES : (place + 1) * LANES])
+
+    ahead = gate_gradients(*tasks[0])
+    for i, (place, pair, m) in enumerate(tasks):
+        current = ahead
+        if i + 1 < len(tasks):
+            ahead = gate_gradients(*tasks[i + 1])
+        dscore = (current * joined(slope_refs, pair, m).astype(F32)).astype(BF)
+        keys = select_rows(mm(dscore, q_ref[:, pair * LANES : (pair + 1) * LANES]), own_rows) * scale
+        ng_ref[m * ext : (m + 1) * ext, place * LANES : (place + 1) * LANES] = keys.astype(BF)
 
 
 def first_keys_body(
-    n_member, n_band, first_value, dm_ref, own_value_ref, halo_value_ref, own_slope_ref, halo_slope_ref,
-    q_ref, ext_ref, ngv_ref, ng_ref, *out_refs
+    n_member, n_band, first_value, grad_ref, pt_ref, own_value_ref, halo_value_ref, own_slope_ref,
+    halo_slope_ref, q_ref, ext_ref, ngv_ref, ng_ref, *out_refs
 ):
     count = ng_ref.shape[1] // LANES
     rest = mm(ext_ref[...], ngv_ref[:, first_value:])
     store_group(rest, 1, n_member, n_band, 0, out_refs)
     value_refs, slope_refs = (own_value_ref, halo_value_ref), (own_slope_ref, halo_slope_ref)
-    key_gradients(range(count), dm_ref, value_refs, slope_refs, q_ref, ng_ref)
+    key_gradients(range(count), grad_ref, pt_ref, value_refs, slope_refs, q_ref, ng_ref)
     store_group(mm(ext_ref[...], ng_ref[...]), 1, n_member, n_band, rest.shape[1], out_refs)
 
 
 def last_keys_body(
-    n_member, n_band, grad_ref, dm_ref, own_value_ref, halo_value_ref, own_slope_ref, halo_slope_ref,
+    n_member, n_band, grad_ref, pt_ref, own_value_ref, halo_value_ref, own_slope_ref, halo_slope_ref,
     q_ref, merged_ref, wo_ref, ext_ref, ng_ref, *refs
 ):
     out_refs, turned = refs[:-1], refs[-1]
-    members, width, _ = dm_ref.shape
-    count = ng_ref.shape[1] // LANES
+    members, width, _ = merged_ref.shape
+    pairs = range((width - ng_ref.shape[1]) // LANES, width // LANES)
     value_refs, slope_refs = (own_value_ref, halo_value_ref), (own_slope_ref, halo_slope_ref)
-    key_gradients(range(width // LANES - count, width // LANES), dm_ref, value_refs, slope_refs, q_ref, ng_ref)
+    key_gradients(pairs, grad_ref, pt_ref, value_refs, slope_refs, q_ref, ng_ref)
     m_t = sum(mm(grad_ref[m], merged_ref[m], NT) for m in range(members))
     head_t = sum(mm(grad_ref[m], q_ref[...]) for m in range(members)) + mm(m_t.astype(BF), wo_ref[...])
     turned[...] = jnp.concatenate([m_t, head_t], axis=0).T
@@ -436,11 +444,12 @@
     def gate_shapes(rows):
         return [sds((members, rows, width), BF)] + [sds((pairs, members, 2 * rows, points), BF)] * 2
 
-    own_value, own_gates, own_slopes, own_merged, pt, p, base, weight = call(
+    own_value, own_gates, own_slopes, own_merged, qt, pt, p, base, weight = call(
         own_body,
         gate_shapes(nodes)
         + [
             sds((members, width, points), F32),
+            sds((width, points), BF),
             sds((width, LANES), BF),
             sds((LANES, width), BF),
             sds((LANES, points), F32),
@@ -461,7 +470,7 @@
             sds((members, LANES, points), F32),
             sds((-(-members * send_rows // 16) * 16, points), BF),
         ],
-        (other, mate, own_merged, kv_weight, queries, sources, p),
+        (other, mate, own_merged, kv_weight, qt, sources, p),
     )
 
     received = [
@@ -479,23 +488,23 @@
     group_width = (2 * width + extra) // GROUPS
     first_keys = 2 * group_width - width
     group_shape = [sds((width // 2, group_width), BF)] * 2
-    grad, dm, ng_value, send, keep = call(
+    grad, ng_value, send, keep = call(
         functools.partial(value_body, n_member, n_band),
-        [sds((members, LANES, points), BF), sds((members, width, points), BF), sds((members * ext, width), BF)]
+        [sds((members, LANES, points), BF), sds((members * ext, width), BF)]
         + group_shape,
-        (*received, part, base, truth, weight, pt, own_gates, halo_gates, ext_t),
+        (*received, part, base, truth, weight, p, own_gates, halo_gates, ext_t),
     )
     groups = [[keep, swap(send, "band", 0, n_band)]]
     ng_first, send, keep = call(
         functools.partial(first_keys_body, n_member, n_band, group_width),
         [sds((members * ext, first_keys), BF)] + group_shape,
-        (dm, own_value, halo_value, own_slopes, halo_slopes, queries, ext_t, ng_value),
+        (grad, pt, own_value, halo_value, own_slopes, halo_slopes, queries, ext_t, ng_value),
     )
     groups.append([keep, swap(send, "band", 0, n_band)])
     ng_last, send, keep = call(
         functools.partial(last_keys_body, n_member, n_band),
         [sds((members * ext, width - first_keys), BF)] + group_shape,
-        (grad, dm, own_value, halo_value, own_slopes, halo_slopes, queries, merged, out_weight, ext_t),
+        (grad, pt, own_value, halo_value, own_slopes, halo_slopes, queries, merged, out_weight, ext_t),
         [pltpu.VMEM((width, extra), F32)],
     )
     groups.append([keep, swap(send, "band", 0, n_band)])
@@ -516,15 +525,13 @@
                 [sds((members, nodes, width), F32)] + [sds((members * rim, width), BF)] * 2,
                 (ng_first, ng_last, ng_value, kv_weight),
             )
-        if step == steps - 1:
-            outgoing[0], back_other = lax.optimization_barrier((outgoing[0], back_other))
-            from_other = lax.ppermute(back_other, "band", others)
         arrived = [swap(out, *turn[step], count[turn[step][0]]) for out, turn in zip(outgoing, turns)]
         if step == 0:
             from_mate = lax.ppermute(back_mate, "band", mates)
             arrived, from_mate, back_other = lax.optimization_barrier((arrived, from_mate, back_other))
         if step == steps - 1:
-            arrived, from_other = lax.optimization_barrier((arrived, from_other))
+            arrived, back_other = lax.optimization_barrier((arrived, back_other))
+            from_other = lax.ppermute(back_other, "band", others)
         groups = [lower(terms) + [new] for terms, new in zip(groups, arrived)]
     terms = [jnp.concatenate([add_up(*group) for group in groups], axis=1)]
     for axis, bit in rest:
@@ -536,6 +543,7 @@
         [sds((rw, 2 * width), F32), sds((rw, width), F32), sds((rw, channels), F32)],
         (add_up(*terms[:-1]), terms[-1], hp),
     )
+    kv_grad, from_other = lax.optimization_barrier((kv_grad, from_other))
     hidden_grad = call(
         hidden_body,
         sds((members, nodes, width), F32),

time: 73.1 us -> 69.4 us (0.949)
  waiting for transfers between devices: 33.8 us -> 29.6 us
    ppermute x13, waiting for transfers between devices: 24.9 us -> 20.4 us  [swap(): return lax.ppermute(rows, axis, [(i, i ^ 1 << bit) for i in range(count)])]
  transfers between devices with their start and end apart: 20 -> 20, of which waited for: 12 -> 15; matrix products, arithmetic and copies ran while one was open for 1% -> 1% of each run, Pallas kernels for 11% -> 12%
where the time goes in v12:
time: 69.4 us; the launch traced here: 69.2 us
  waiting for transfers between devices  29.6 us (43%)
  starting transfers between devices  23.4 us (34%)
  Pallas kernels  14.3 us (21%)
  other arithmetic  0.96 us (1%)
  between operations  0.91 us (1%)
    ppermute x13, waiting for transfers between devices, swap(): return lax.ppermute(rows, axis, [(i, i ^ 1 << bit) for i in range(count)])  20.4 us
    pallas_call x10, Pallas kernels, call(): pl.pallas_call(body, out_shape=out_shape, in_specs=[pl.BlockSpec(memory_s...  14.3 us
    ppermute x13, starting transfers between devices, swap(): return lax.ppermute(rows, axis, [(i, i ^ 1 << bit) for i in range(count)])  14.1 us
    ppermute x3, waiting for transfers between devices, shards(): lax.ppermute(sent, 'member', [(i, i ^ s) for i in range(n_member)])  6.7 us
    ppermute x3, starting transfers between devices, shards(): lax.ppermute(sent, 'member', [(i, i ^ s) for i in range(n_member)])  5.79 us
    ppermute x1, starting transfers between devices, shards(): other = lax.ppermute(for_other, 'band', others)  3.4 us
  transfers between devices with their start and end apart: 20, of which 15 were waited for; matrix products, arithmetic and copies ran while one was open for 1% of the time, Pallas kernels for 12%

profile of v12, /device:TPU:0, one launch (start us, length us, event | category | flops | bytes accessed | tf_op | source)
XLA Modules:
  0.0 69.2 jit_solution(13941081884258649570)
XLA Ops:
  0.7 1.4 %shard_map.138 = (bf16[2,64,1024]{2,1,0:T(8,128)(2,1)S(1)}, s32[2,32]{1,0:T(2,128)S(1)}, bf16[64,1024]{1,0:T(8,128)(2,1)S(1)}, bf16[64,1024]{1,0:T(8,128)(2,1)S(1)}) custom-call(bf16[2,64,1024]{2,1,0:T(8,128)(2,1)} %hidden_hbm.1, s32[2,32]{1,0:T(2,128)} %halo_hbm.1), custom_call_target="tpu_custom_call" | custom-call | flops 10000000000 | bytes 1 | tf_op jit(solution)/shard_map/pallas_call | solution.py:28
  2.1 3.4 %collective-permute-start = (bf16[64,1024]{1,0:T(8,128)(2,1)S(1)}, bf16[64,1024]{1,0:T(8,128)(2,1)S(1)}, u32[]{:S(2)}, u32[]{:S(2)}) collective-permute-start(bf16[64,1024]{1,0:T(8,128)(2,1)S(1)} %get-tuple-element.60), channel_id=1, source_target_pairs={{0,7},{1,2},{2,1},{3,4},{4,3},{5,6},{6,5},{7,0},{8,15},{9,10},{10,... | collective-permute-start | bytes 393224 | tf_op jit(solution)/shard_map/ppermute | solution.py:439
  5.6 2.4 %shard_map.139 = (bf16[2,64,1024]{2,1,0:T(8,128)(2,1)S(1)}, bf16[8,2,128,256]{3,2,1,0:T(8,128)(2,1)S(1)}, bf16[8,2,128,256]{3,2,1,0:T(8,128)(2,1)S(1)}, f32[2,10...) custom-call(bf16[2,64,1024]{2,1,0:T(8,128)(2,1)S(1)} %get-tuple-elem, ...), custom_call_target="tpu_custom_call" | custom-call | flops 1 | bytes 1 | tf_op jit(solution)/shard_map/pallas_call | solution.py:28
  8.0 0.7 %collective-permute-done.other_ref = bf16[64,1024]{1,0:T(8,128)(2,1)S(1)} collective-permute-done((bf16[64,1024]{1,0:T(8,128)(2,1)S(1)}, bf16[64,1024]{1,0:T(8,128)(2,1)S(1)}, u32[]{:S(2)}, u32[]{:S(2)}) %collective-permute-start) | collective-permute-done | bytes 131104 | tf_op jit(solution)/shard_map/ppermute | solution.py:439
  8.7 1.7 %shard_map.140 = (bf16[2,64,1024]{2,1,0:T(8,128)(2,1)S(1)}, bf16[8,2,128,256]{3,2,1,0:T(8,128)(2,1)S(1)}, bf16[8,2,128,256]{3,2,1,0:T(8,128)(2,1)S(1)}, bf16[2,1...) custom-call(bf16[64,1024]{1,0:T(8,128)(2,1)S(1)} %collective-permute-done.other_ref, ...), custom_call_target="tpu_custom_call" | custom-call | flops 1 | bytes 1 | tf_op jit(solution)/shard_map/pallas_call | solution.py:28
  10.4 5.2 %collective-permute-start.2 = (bf16[208,256]{1,0:T(8,128)(2,1)S(1)}, bf16[208,256]{1,0:T(8,128)(2,1)S(1)}, u32[]{:S(2)}, u32[]{:S(2)}) collective-permute-start(bf16[208,256]{1,0:T(8,128)(2,1)S(1)} %get-tuple-element.66), channel_id=1, source_target_pairs={{0,24},{8,16},{16,8},{24,0},{1,25},{9,17},{17,9},{25,1},{2,26},{10... | collective-permute-start | bytes 319496 | tf_op jit(solution)/shard_map/ppermute | solution.py:477
  15.6 0.6 collective-permute-start.4
  16.2 0.3 shard_map.141.refs_10_.ext_ref
  16.5 2.3 %collective-permute-done.2.refs_0_ = bf16[208,256]{1,0:T(8,128)(2,1)S(1)} collective-permute-done((bf16[208,256]{1,0:T(8,128)(2,1)S(1)}, bf16[208,256]{1,0:T(8,128)(2,1)S(1)}, u32[]{:S(2)}, u32[]{:S(2)}) %collective-permute-start.2) | collective-permute-done | bytes 106528 | tf_op jit(solution)/shard_map/ppermute | solution.py:477
  18.8 4.4 %collective-permute-done.3.refs_1_ = bf16[208,256]{1,0:T(8,128)(2,1)S(1)} collective-permute-done((bf16[208,256]{1,0:T(8,128)(2,1)S(1)}, bf16[208,256]{1,0:T(8,128)(2,1)S(1)}, u32[]{:S(2)}, u32[]{:S(2)}) %collective-permute-start.3) | collective-permute-done | bytes 106528 | tf_op jit(solution)/shard_map/ppermute | solution.py:477
  23.2 1.8 %shard_map.142 = (bf16[2,128,256]{2,1,0:T(8,128)(2,1)S(1)}, bf16[256,1024]{1,0:T(8,128)(2,1)S(1)}, bf16[512,768]{1,0:T(8,128)(2,1)S(1)}, bf16[512,768]{1,0:T(8,128)(2,1)S(1)}) custom-call(bf16[208,256]{1,0:T(8,128)(2,1)S(1)} %collective-permute-done.2.refs_0_, bf16[208,256]{1,0:T(8,128)(2,1)S(1)} %collective-permute-done.3.refs_1_, ...), custom_call_target="tpu_custom_call" | custom-call | flops 1 | bytes 1 | tf_op jit(solution)/shard_map/pallas_call | solution.py:28
  25.1 0.1 collective-permute-start.5
  25.1 1.5 %shard_map.143 = (bf16[256,512]{1,0:T(8,128)(2,1)S(1)}, bf16[512,768]{1,0:T(8,128)(2,1)S(1)}, bf16[512,768]{1,0:T(8,128)(2,1)S(1)}) custom-call(bf16[2,128,256]{2,1,0:T(8,128)(2,1)S(1)} %get-tuple-element.72.grad_ref, bf16[1024,128]{1,0:T(8,128)(2,1)S(1)} %get-tuple-element.73.pt_ref, bf16[2,64,1024]{2,1,0:T(8,128)(2,1)S(1)} %get-tuple-element.74.own_value_ref, ...), custom_call_target="tpu_custom_call" | custom-call | flops 1 | bytes 1 | tf_op jit(solution)/shard_map/pallas_call | solution.py:28
  26.6 0.6 collective-permute-start.6
  27.2 1.9 %shard_map.144 = (bf16[256,512]{1,0:T(8,128)(2,1)S(1)}, bf16[512,768]{1,0:T(8,128)(2,1)S(1)}, bf16[512,768]{1,0:T(8,128)(2,1)S(1)}) custom-call(bf16[2,128,256]{2,1,0:T(8,128)(2,1)S(1)} %get-tuple-element.72.grad_ref, bf16[1024,128]{1,0:T(8,128)(2,1)S(1)} %get-tuple-element.73.pt_ref, bf16[2,64,1024]{2,1,0:T(8,128)(2,1)S(1)} %get-tuple-element.74.own_value_ref, ...), custom_call_target="tpu_custom_call" | custom-call | flops 1 | bytes 1 | tf_op jit(solution)/shard_map/pallas_call | solution.py:28
  29.1 0.1 collective-permute-start.7
  29.2 0.1 add_convert_fusion.2
  29.3 0.1 add_convert_fusion.1
  29.4 2.0 %collective-permute-done.7 = bf16[512,768]{1,0:T(8,128)(2,1)S(1)} collective-permute-done((bf16[512,768]{1,0:T(8,128)(2,1)S(1)}, bf16[512,768]{1,0:T(8,128)(2,1)S(1)}, u32[]{:S(2)}, u32[]{:S(2)}) %collective-permute-start.7) | collective-permute-done | bytes 786464 | tf_op jit(solution)/shard_map/ppermute | solution.py:402
  31.5 0.1 add_convert_fusion
  31.6 0.4 collective-permute-start.10
  32.0 1.7 %collective-permute-start.8 = (bf16[256,768]{1,0:T(8,128)(2,1)S(1)}, bf16[256,768]{1,0:T(8,128)(2,1)S(1)}, u32[]{:S(2)}, u32[]{:S(2)}) collective-permute-start(bf16[256,768]{1,0:T(8,128)(2,1)S(1)} %add_convert_fusion.2), channel_id=1, source_target_pairs={{0,2},{1,3},{2,0},{3,1},{4,6},{5,7},{6,4},{7,5},{8,10},{9,11},{10,... | collective-permute-start | bytes 1179656 | tf_op jit(solution)/shard_map/ppermute | solution.py:402
  33.7 1.8 %collective-permute-start.9 = (bf16[256,768]{1,0:T(8,128)(2,1)S(1)}, bf16[256,768]{1,0:T(8,128)(2,1)S(1)}, u32[]{:S(2)}, u32[]{:S(2)}) collective-permute-start(bf16[256,768]{1,0:T(8,128)(2,1)S(1)} %add_convert_fusion.1), channel_id=1, source_target_pairs={{0,4},{1,5},{2,6},{3,7},{4,0},{5,1},{6,2},{7,3},{8,12},{9,13},{10,... | collective-permute-start | bytes 1179656 | tf_op jit(solution)/shard_map/ppermute | solution.py:402
  35.5 1.3 %shard_map.145 = (f32[2,64,1024]{2,1,0:T(8,128)S(1)}, bf16[64,1024]{1,0:T(8,128)(2,1)S(1)}, bf16[64,1024]{1,0:T(8,128)(2,1)S(1)}) custom-call(bf16[256,512]{1,0:T(8,128)(2,1)S(1)} %get-tuple-element.79.first_ref, bf16[256,512]{1,0:T(8,128)(2,1)S(1)} %get-tuple-element.94.last_ref, bf16[256,1024]{1,0:T(8,128)(2,1)S(1)} %get-tuple-element.78.ngv_ref, ...), custom_call_target="tpu_custom_call" | custom-call | flops 1 | bytes 1 | tf_op jit(solution)/shard_map/pallas_call | solution.py:28
  36.9 1.3 %collective-permute-done.11.from_mate_ref = bf16[64,1024]{1,0:T(8,128)(2,1)S(1)} collective-permute-done((bf16[64,1024]{1,0:T(8,128)(2,1)S(1)}, bf16[64,1024]{1,0:T(8,128)(2,1)S(1)}, u32[]{:S(2)}, u32[]{:S(2)}) %collective-permute-start.11) | collective-permute-done | bytes 131104 | tf_op jit(solution)/shard_map/ppermute | solution.py:530
  38.2 4.6 %collective-permute-done.10 = bf16[256,768]{1,0:T(8,128)(2,1)S(1)} collective-permute-done((bf16[256,768]{1,0:T(8,128)(2,1)S(1)}, bf16[256,768]{1,0:T(8,128)(2,1)S(1)}, u32[]{:S(2)}, u32[]{:S(2)}) %collective-permute-start.10) | collective-permute-done | bytes 393248 | tf_op jit(solution)/shard_map/ppermute | solution.py:402
  42.8 0.3 collective-permute-done.8
  43.0 1.5 %collective-permute-done.9 = bf16[256,768]{1,0:T(8,128)(2,1)S(1)} collective-permute-done((bf16[256,768]{1,0:T(8,128)(2,1)S(1)}, bf16[256,768]{1,0:T(8,128)(2,1)S(1)}, u32[]{:S(2)}, u32[]{:S(2)}) %collective-permute-start.9) | collective-permute-done | bytes 393248 | tf_op jit(solution)/shard_map/ppermute | solution.py:402
  44.5 0.1 add_convert_fusion.3
  44.6 0.7 %collective-permute-start.16 = (bf16[128,768]{1,0:T(8,128)(2,1)S(1)}, bf16[128,768]{1,0:T(8,128)(2,1)S(1)}, u32[]{:S(2)}, u32[]{:S(2)}) collective-permute-start(bf16[128,768]{1,0:T(8,128)(2,1)S(1)} %add_convert_fusion.3), channel_id=1, source_target_pairs={{0,2},{1,3},{2,0},{3,1},{4,6},{5,7},{6,4},{7,5},{8,10},{9,11},{10,... | collective-permute-start | bytes 589832 | tf_op jit(solution)/shard_map/ppermute | solution.py:402
  45.3 0.1 add_convert_fusion.4
  45.4 1.7 %collective-permute-start.14 = (bf16[128,768]{1,0:T(8,128)(2,1)S(1)}, bf16[128,768]{1,0:T(8,128)(2,1)S(1)}, u32[]{:S(2)}, u32[]{:S(2)}) collective-permute-start(bf16[128,768]{1,0:T(8,128)(2,1)S(1)} %add_convert_fusion.4), channel_id=1, source_target_pairs={{0,8},{8,0},{16,24},{24,16},{1,9},{9,1},{17,25},{25,17},{2,10},{10... | collective-permute-start | bytes 589832 | tf_op jit(solution)/shard_map/ppermute | solution.py:402
  47.2 0.1 add_convert_fusion.5
  47.2 1.8 %collective-permute-start.12 = (bf16[128,768]{1,0:T(8,128)(2,1)S(1)}, bf16[128,768]{1,0:T(8,128)(2,1)S(1)}, u32[]{:S(2)}, u32[]{:S(2)}) collective-permute-start(bf16[128,768]{1,0:T(8,128)(2,1)S(1)} %add_convert_fusion.5), channel_id=1, source_target_pairs={{0,4},{1,5},{2,6},{3,7},{4,0},{5,1},{6,2},{7,3},{8,12},{9,13},{10,... | collective-permute-start | bytes 589832 | tf_op jit(solution)/shard_map/ppermute | solution.py:402
  49.0 1.4 %collective-permute-done.16 = bf16[128,768]{1,0:T(8,128)(2,1)S(1)} collective-permute-done((bf16[128,768]{1,0:T(8,128)(2,1)S(1)}, bf16[128,768]{1,0:T(8,128)(2,1)S(1)}, u32[]{:S(2)}, u32[]{:S(2)}) %collective-permute-start.16) | collective-permute-done | bytes 196640 | tf_op jit(solution)/shard_map/ppermute | solution.py:402
  50.5 1.6 %collective-permute-start.17 = (bf16[64,768]{1,0:T(8,128)(2,1)S(1)}, bf16[64,768]{1,0:T(8,128)(2,1)S(1)}, u32[]{:S(2)}, u32[]{:S(2)}) collective-permute-start(bf16[64,768]{1,0:T(8,128)(2,1)S(1)} %add_convert_fusion.6), channel_id=1, source_target_pairs={{0,4},{1,5},{2,6},{3,7},{4,0},{5,1},{6,2},{7,3},{8,12},{9,13},{10,... | collective-permute-start | bytes 294920 | tf_op jit(solution)/shard_map/ppermute | solution.py:402
  52.1 0.9 %collective-permute-start.15 = (bf16[64,768]{1,0:T(8,128)(2,1)S(1)}, bf16[64,768]{1,0:T(8,128)(2,1)S(1)}, u32[]{:S(2)}, u32[]{:S(2)}) collective-permute-start(bf16[64,768]{1,0:T(8,128)(2,1)S(1)} %add_convert_fusion.7), channel_id=1, source_target_pairs={{0,2},{1,3},{2,0},{3,1},{4,6},{5,7},{6,4},{7,5},{8,10},{9,11},{10,... | collective-permute-start | bytes 294920 | tf_op jit(solution)/shard_map/ppermute | solution.py:402
  53.0 1.0 %collective-permute-done.12 = bf16[128,768]{1,0:T(8,128)(2,1)S(1)} collective-permute-done((bf16[128,768]{1,0:T(8,128)(2,1)S(1)}, bf16[128,768]{1,0:T(8,128)(2,1)S(1)}, u32[]{:S(2)}, u32[]{:S(2)}) %collective-permute-start.12) | collective-permute-done | bytes 196640 | tf_op jit(solution)/shard_map/ppermute | solution.py:402
  54.0 0.7 %collective-permute-start.13 = (bf16[64,768]{1,0:T(8,128)(2,1)S(1)}, bf16[64,768]{1,0:T(8,128)(2,1)S(1)}, u32[]{:S(2)}, u32[]{:S(2)}) collective-permute-start(bf16[64,768]{1,0:T(8,128)(2,1)S(1)} %add_convert_fusion.8), channel_id=1, source_target_pairs={{0,8},{8,0},{16,24},{24,16},{1,9},{9,1},{17,25},{25,17},{2,10},{10... | collective-permute-start | bytes 294920 | tf_op jit(solution)/shard_map/ppermute | solution.py:402
  54.8 0.3 collective-permute-done.17
  55.1 1.6 %collective-permute-done.15 = bf16[64,768]{1,0:T(8,128)(2,1)S(1)} collective-permute-done((bf16[64,768]{1,0:T(8,128)(2,1)S(1)}, bf16[64,768]{1,0:T(8,128)(2,1)S(1)}, u32[]{:S(2)}, u32[]{:S(2)}) %collective-permute-start.15) | collective-permute-done | bytes 98336 | tf_op jit(solution)/shard_map/ppermute | solution.py:402
  56.8 2.7 %collective-permute-done.13 = bf16[64,768]{1,0:T(8,128)(2,1)S(1)} collective-permute-done((bf16[64,768]{1,0:T(8,128)(2,1)S(1)}, bf16[64,768]{1,0:T(8,128)(2,1)S(1)}, u32[]{:S(2)}, u32[]{:S(2)}) %collective-permute-start.13) | collective-permute-done | bytes 98336 | tf_op jit(solution)/shard_map/ppermute | solution.py:402
  59.5 0.1 convert_add_fusion
  59.8 2.0 %collective-permute-start.18 = (bf16[32,2304]{1,0:T(8,128)(2,1)S(1)}, bf16[32,2304]{1,0:T(8,128)(2,1)S(1)}, u32[]{:S(2)}, u32[]{:S(2)}) collective-permute-start(bf16[32,2304]{1,0:T(8,128)(2,1)S(1)} %slice.262), channel_id=1, source_target_pairs={{0,16},{8,24},{16,0},{24,8},{1,17},{9,25},{17,1},{25,9},{2,18},{10... | collective-permute-start | bytes 442376 | tf_op jit(solution)/shard_map/ppermute | solution.py:402
  61.8 5.0 %collective-permute-done.18.arrived_ref = bf16[32,2304]{1,0:T(8,128)(2,1)S(1)} collective-permute-done((bf16[32,2304]{1,0:T(8,128)(2,1)S(1)}, bf16[32,2304]{1,0:T(8,128)(2,1)S(1)}, u32[]{:S(2)}, u32[]{:S(2)}) %collective-permute-start.18) | collective-permute-done | bytes 147488 | tf_op jit(solution)/shard_map/ppermute | solution.py:402
  66.9 0.9 %shard_map.146 = (f32[32,2048]{1,0:T(8,128)}, f32[32,1024]{1,0:T(8,128)}, f32[32,100]{1,0:T(8,128)}) custom-call(f32[32,2304]{1,0:T(8,128)S(1)} %slice.220.own_ref, bf16[32,2304]{1,0:T(8,128)(2,1)S(1)} %collective-permute-done.18.arrived_ref, bf16[100,1024]{1,0:T(8,128)(2,1)S(1)} %bitcast.4), custom_call_target="tpu_custom_call" | custom-call | flops 1 | bytes 1 | tf_op jit(solution)/shard_map/pallas_call | solution.py:28
  67.7 0.4 collective-permute-done.19.from_other_ref
  68.1 1.1 %shard_map.147 = f32[2,64,1024]{2,1,0:T(8,128)} custom-call(f32[2,64,1024]{2,1,0:T(8,128)S(1)} %get-tuple-element.95.own_ref, bf16[64,1024]{1,0:T(8,128)(2,1)S(1)} %collective-permute-done.11.from_mate_ref, bf16[64,1024]{1,0:T(8,128)(2,1)S(1)} %collective-permute-done.19.from_other_ref, s32[2,32]{1,0:T(2,128)S(1)} %get-tuple-element.112.halo_ref), custom_call_target="tpu_custom_call" | custom-call | flops 1 | bytes 1 | tf_op jit(solution)/shard_map/pallas_call | solution.py:28
  (34 shorter events, 0.4 us)
Async XLA Ops:
  0.6 4.9 %copy-start.3 = (bf16[1024,100]{0,1:T(8,128)(2,1)S(1)}, bf16[1024,100]{0,1:T(8,128)(2,1)}, u32[]{:S(2)}) copy-start(bf16[1024,100]{0,1:T(8,128)(2,1)} %param.15) | copy-start | bytes 614404
  0.6 4.9 %copy-start.8 = (f32[100]{0:T(128)S(1)}, f32[100]{0:T(128)}, u32[]{:S(2)}) copy-start(f32[100]{0:T(128)} %param.19) | copy-start | bytes 1204
  0.7 4.9 %copy-start.7 = (f32[256]{0:T(256)S(1)}, f32[256]{0:T(256)}, u32[]{:S(2)}) copy-start(f32[256]{0:T(256)} %param.18) | copy-start | bytes 3076
  0.7 4.9 %copy-start.2 = (bf16[256,1024]{1,0:T(8,128)(2,1)S(1)}, bf16[256,1024]{1,0:T(8,128)(2,1)}, u32[]{:S(2)}) copy-start(bf16[256,1024]{1,0:T(8,128)(2,1)} %q_ref.5) | copy-start | bytes 1572868
  0.7 4.9 %copy-start.1 = (bf16[1024,1024]{1,0:T(8,128)(2,1)S(1)}, bf16[1024,1024]{1,0:T(8,128)(2,1)}, u32[]{:S(2)}) copy-start(bf16[1024,1024]{1,0:T(8,128)(2,1)} %wo_ref.3) | copy-start | bytes 6291460
  0.7 4.9 %copy-start.4 = (f32[100,256]{1,0:T(8,128)S(1)}, f32[100,256]{1,0:T(8,128)}, u32[]{:S(2)}) copy-start(f32[100,256]{1,0:T(8,128)} %init_ref.1) | copy-start | bytes 307204
  0.7 4.9 %copy-start.6 = (s32[3,256]{1,0:T(4,128)S(1)}, s32[3,256]{1,0:T(4,128)}, u32[]{:S(2)}) copy-start(s32[3,256]{1,0:T(4,128)} %src_ref.3) | copy-start | bytes 9220
  0.7 4.9 %copy-start = (bf16[1024,2048]{1,0:T(8,128)(2,1)S(1)}, bf16[1024,2048]{1,0:T(8,128)(2,1)}, u32[]{:S(2)}) copy-start(bf16[1024,2048]{1,0:T(8,128)(2,1)} %kvw_ref.5) | copy-start | bytes 12582916
  2.1 6.6 %collective-permute-start = (bf16[64,1024]{1,0:T(8,128)(2,1)S(1)}, bf16[64,1024]{1,0:T(8,128)(2,1)S(1)}, u32[]{:S(2)}, u32[]{:S(2)}) collective-permute-start(bf16[64,1024]{1,0:T(8,128)(2,1)S(1)} %get-tuple-element.60), channel_id=1, source_target_pairs={{0,7},{1,2},{2,1},{3,4},{4,3},{5,6},{6,5},{7,0},{8,15},{9,10},{10,... | collective-permute-start | bytes 393224 | tf_op jit(solution)/shard_map/ppermute | solution.py:439
  5.5 3.2 %collective-permute-start.1 = (bf16[64,1024]{1,0:T(8,128)(2,1)S(1)}, bf16[64,1024]{1,0:T(8,128)(2,1)S(1)}, u32[]{:S(2)}, u32[]{:S(2)}) collective-permute-start(bf16[64,1024]{1,0:T(8,128)(2,1)S(1)} %get-tuple-element.61), channel_id=1, source_target_pairs={{0,1},{1,0},{2,3},{3,2},{4,5},{5,4},{6,7},{7,6},{8,9},{9,8},{10,11... | collective-permute-start | bytes 393224 | tf_op jit(solution)/shard_map/ppermute | solution.py:440
  8.7 14.5 %copy-start.5 = (f32[100,256]{1,0:T(8,128)S(1)}, f32[100,256]{1,0:T(8,128)}, u32[]{:S(2)}) copy-start(f32[100,256]{1,0:T(8,128)} %refs_5_.1) | copy-start | bytes 307204
  10.4 8.3 %collective-permute-start.2 = (bf16[208,256]{1,0:T(8,128)(2,1)S(1)}, bf16[208,256]{1,0:T(8,128)(2,1)S(1)}, u32[]{:S(2)}, u32[]{:S(2)}) collective-permute-start(bf16[208,256]{1,0:T(8,128)(2,1)S(1)} %get-tuple-element.66), channel_id=1, source_target_pairs={{0,24},{8,16},{16,8},{24,0},{1,25},{9,17},{17,9},{25,1},{2,26},{10... | collective-permute-start | bytes 319496 | tf_op jit(solution)/shard_map/ppermute | solution.py:477
  15.6 7.6 %collective-permute-start.3 = (bf16[208,256]{1,0:T(8,128)(2,1)S(1)}, bf16[208,256]{1,0:T(8,128)(2,1)S(1)}, u32[]{:S(2)}, u32[]{:S(2)}) collective-permute-start(bf16[208,256]{1,0:T(8,128)(2,1)S(1)} %get-tuple-element.66), channel_id=1, source_target_pairs={{0,16},{8,24},{16,0},{24,8},{1,17},{9,25},{17,1},{25,9},{2,18},{10... | collective-permute-start | bytes 319496 | tf_op jit(solution)/shard_map/ppermute | solution.py:477
  15.6 7.6 %collective-permute-start.4 = (bf16[208,256]{1,0:T(8,128)(2,1)S(1)}, bf16[208,256]{1,0:T(8,128)(2,1)S(1)}, u32[]{:S(2)}, u32[]{:S(2)}) collective-permute-start(bf16[208,256]{1,0:T(8,128)(2,1)S(1)} %get-tuple-element.66), channel_id=1, source_target_pairs={{0,8},{8,0},{16,24},{24,16},{1,9},{9,1},{17,25},{25,17},{2,10},{10... | collective-permute-start | bytes 319496 | tf_op jit(solution)/shard_map/ppermute | solution.py:477
  25.1 4.1 %collective-permute-start.5 = (bf16[512,768]{1,0:T(8,128)(2,1)S(1)}, bf16[512,768]{1,0:T(8,128)(2,1)S(1)}, u32[]{:S(2)}, u32[]{:S(2)}) collective-permute-start(bf16[512,768]{1,0:T(8,128)(2,1)S(1)} %get-tuple-element.81), channel_id=1, source_target_pairs={{0,1},{1,0},{2,3},{3,2},{4,5},{5,4},{6,7},{7,6},{8,9},{9,8},{10,11... | collective-permute-start | bytes 2359304 | tf_op jit(solution)/shard_map/ppermute | solution.py:402
  26.6 2.7 %collective-permute-start.6 = (bf16[512,768]{1,0:T(8,128)(2,1)S(1)}, bf16[512,768]{1,0:T(8,128)(2,1)S(1)}, u32[]{:S(2)}, u32[]{:S(2)}) collective-permute-start(bf16[512,768]{1,0:T(8,128)(2,1)S(1)} %get-tuple-element.83), channel_id=1, source_target_pairs={{0,1},{1,0},{2,3},{3,2},{4,5},{5,4},{6,7},{7,6},{8,9},{9,8},{10,11... | collective-permute-start | bytes 2359304 | tf_op jit(solution)/shard_map/ppermute | solution.py:402
  29.1 2.4 %collective-permute-start.7 = (bf16[512,768]{1,0:T(8,128)(2,1)S(1)}, bf16[512,768]{1,0:T(8,128)(2,1)S(1)}, u32[]{:S(2)}, u32[]{:S(2)}) collective-permute-start(bf16[512,768]{1,0:T(8,128)(2,1)S(1)} %get-tuple-element.89), channel_id=1, source_target_pairs={{0,1},{1,0},{2,3},{3,2},{4,5},{5,4},{6,7},{7,6},{8,9},{9,8},{10,11... | collective-permute-start | bytes 2359304 | tf_op jit(solution)/shard_map/ppermute | solution.py:402
  31.6 11.2 %collective-permute-start.10 = (bf16[256,768]{1,0:T(8,128)(2,1)S(1)}, bf16[256,768]{1,0:T(8,128)(2,1)S(1)}, u32[]{:S(2)}, u32[]{:S(2)}) collective-permute-start(bf16[256,768]{1,0:T(8,128)(2,1)S(1)} %add_convert_fusion), channel_id=1, source_target_pairs={{0,8},{8,0},{16,24},{24,16},{1,9},{9,1},{17,25},{25,17},{2,10},{10... | collective-permute-start | bytes 1179656 | tf_op jit(solution)/shard_map/ppermute | solution.py:402
  32.0 11.1 %collective-permute-start.8 = (bf16[256,768]{1,0:T(8,128)(2,1)S(1)}, bf16[256,768]{1,0:T(8,128)(2,1)S(1)}, u32[]{:S(2)}, u32[]{:S(2)}) collective-permute-start(bf16[256,768]{1,0:T(8,128)(2,1)S(1)} %add_convert_fusion.2), channel_id=1, source_target_pairs={{0,2},{1,3},{2,0},{3,1},{4,6},{5,7},{6,4},{7,5},{8,10},{9,11},{10,... | collective-permute-start | bytes 1179656 | tf_op jit(solution)/shard_map/ppermute | solution.py:402
  33.7 10.8 %collective-permute-start.9 = (bf16[256,768]{1,0:T(8,128)(2,1)S(1)}, bf16[256,768]{1,0:T(8,128)(2,1)S(1)}, u32[]{:S(2)}, u32[]{:S(2)}) collective-permute-start(bf16[256,768]{1,0:T(8,128)(2,1)S(1)} %add_convert_fusion.1), channel_id=1, source_target_pairs={{0,4},{1,5},{2,6},{3,7},{4,0},{5,1},{6,2},{7,3},{8,12},{9,13},{10,... | collective-permute-start | bytes 1179656 | tf_op jit(solution)/shard_map/ppermute | solution.py:402
  36.8 1.4 %collective-permute-start.11 = (bf16[64,1024]{1,0:T(8,128)(2,1)S(1)}, bf16[64,1024]{1,0:T(8,128)(2,1)S(1)}, u32[]{:S(2)}, u32[]{:S(2)}) collective-permute-start(bf16[64,1024]{1,0:T(8,128)(2,1)S(1)} %get-tuple-element.99), channel_id=1, source_target_pairs={{0,1},{1,0},{2,3},{3,2},{4,5},{5,4},{6,7},{7,6},{8,9},{9,8},{10,11... | collective-permute-start | bytes 393224 | tf_op jit(solution)/shard_map/ppermute | solution.py:530
  44.6 5.8 %collective-permute-start.16 = (bf16[128,768]{1,0:T(8,128)(2,1)S(1)}, bf16[128,768]{1,0:T(8,128)(2,1)S(1)}, u32[]{:S(2)}, u32[]{:S(2)}) collective-permute-start(bf16[128,768]{1,0:T(8,128)(2,1)S(1)} %add_convert_fusion.3), channel_id=1, source_target_pairs={{0,2},{1,3},{2,0},{3,1},{4,6},{5,7},{6,4},{7,5},{8,10},{9,11},{10,... | collective-permute-start | bytes 589832 | tf_op jit(solution)/shard_map/ppermute | solution.py:402
  45.4 6.6 %collective-permute-start.14 = (bf16[128,768]{1,0:T(8,128)(2,1)S(1)}, bf16[128,768]{1,0:T(8,128)(2,1)S(1)}, u32[]{:S(2)}, u32[]{:S(2)}) collective-permute-start(bf16[128,768]{1,0:T(8,128)(2,1)S(1)} %add_convert_fusion.4), channel_id=1, source_target_pairs={{0,8},{8,0},{16,24},{24,16},{1,9},{9,1},{17,25},{25,17},{2,10},{10... | collective-permute-start | bytes 589832 | tf_op jit(solution)/shard_map/ppermute | solution.py:402
  47.2 6.8 %collective-permute-start.12 = (bf16[128,768]{1,0:T(8,128)(2,1)S(1)}, bf16[128,768]{1,0:T(8,128)(2,1)S(1)}, u32[]{:S(2)}, u32[]{:S(2)}) collective-permute-start(bf16[128,768]{1,0:T(8,128)(2,1)S(1)} %add_convert_fusion.5), channel_id=1, source_target_pairs={{0,4},{1,5},{2,6},{3,7},{4,0},{5,1},{6,2},{7,3},{8,12},{9,13},{10,... | collective-permute-start | bytes 589832 | tf_op jit(solution)/shard_map/ppermute | solution.py:402
  50.5 4.7 %collective-permute-start.17 = (bf16[64,768]{1,0:T(8,128)(2,1)S(1)}, bf16[64,768]{1,0:T(8,128)(2,1)S(1)}, u32[]{:S(2)}, u32[]{:S(2)}) collective-permute-start(bf16[64,768]{1,0:T(8,128)(2,1)S(1)} %add_convert_fusion.6), channel_id=1, source_target_pairs={{0,4},{1,5},{2,6},{3,7},{4,0},{5,1},{6,2},{7,3},{8,12},{9,13},{10,... | collective-permute-start | bytes 294920 | tf_op jit(solution)/shard_map/ppermute | solution.py:402
  52.1 4.7 %collective-permute-start.15 = (bf16[64,768]{1,0:T(8,128)(2,1)S(1)}, bf16[64,768]{1,0:T(8,128)(2,1)S(1)}, u32[]{:S(2)}, u32[]{:S(2)}) collective-permute-start(bf16[64,768]{1,0:T(8,128)(2,1)S(1)} %add_convert_fusion.7), channel_id=1, source_target_pairs={{0,2},{1,3},{2,0},{3,1},{4,6},{5,7},{6,4},{7,5},{8,10},{9,11},{10,... | collective-permute-start | bytes 294920 | tf_op jit(solution)/shard_map/ppermute | solution.py:402
  54.0 5.4 %collective-permute-start.13 = (bf16[64,768]{1,0:T(8,128)(2,1)S(1)}, bf16[64,768]{1,0:T(8,128)(2,1)S(1)}, u32[]{:S(2)}, u32[]{:S(2)}) collective-permute-start(bf16[64,768]{1,0:T(8,128)(2,1)S(1)} %add_convert_fusion.8), channel_id=1, source_target_pairs={{0,8},{8,0},{16,24},{24,16},{1,9},{9,1},{17,25},{25,17},{2,10},{10... | collective-permute-start | bytes 294920 | tf_op jit(solution)/shard_map/ppermute | solution.py:402
  59.8 7.1 %collective-permute-start.18 = (bf16[32,2304]{1,0:T(8,128)(2,1)S(1)}, bf16[32,2304]{1,0:T(8,128)(2,1)S(1)}, u32[]{:S(2)}, u32[]{:S(2)}) collective-permute-start(bf16[32,2304]{1,0:T(8,128)(2,1)S(1)} %slice.262), channel_id=1, source_target_pairs={{0,16},{8,24},{16,0},{24,8},{1,17},{9,25},{17,1},{25,9},{2,18},{10... | collective-permute-start | bytes 442376 | tf_op jit(solution)/shard_map/ppermute | solution.py:402
  61.8 6.3 %collective-permute-start.19 = (bf16[64,1024]{1,0:T(8,128)(2,1)S(1)}, bf16[64,1024]{1,0:T(8,128)(2,1)S(1)}, u32[]{:S(2)}, u32[]{:S(2)}) collective-permute-start(bf16[64,1024]{1,0:T(8,128)(2,1)S(1)} %get-tuple-element.110), channel_id=1, source_target_pairs={{0,7},{1,2},{2,1},{3,4},{4,3},{5,6},{6,5},{7,0},{8,15},{9,10},{10,... | collective-permute-start | bytes 393224 | tf_op jit(solution)/shard_map/ppermute | solution.py:534

commit v13 on v12

--- a/solution.py
+++ b/solution.py
@@ -148,7 +148,7 @@
 
 
 def halo_body(
-    send_rows, nodes, other_ref, mate_ref, own_ref, kvw_ref, qt_ref, src_ref, p_ref,
+    channels, nodes, other_ref, mate_ref, own_ref, kvw_ref, qt_ref, src_ref, p_ref,
     value_ref, gate_ref, slope_ref, merged_ref, part_ref, send_ref,
 ):
     members, count, width = value_ref.shape
@@ -195,10 +195,7 @@
     for m in range(members):
         part = mm(p_ref[...], merged_ref[m])
         part_ref[m] = part
-        sent.append(part[0:send_rows])
-    filler = send_ref.shape[0] - members * send_rows
-    if filler:
-        sent.append(jnp.zeros((filler, points), F32))
+        sent.append(part[0:channels])
     send_ref[...] = jnp.concatenate(sent, axis=0).astype(BF)
 
 
@@ -285,11 +282,10 @@
 
     grad_ref[...] = jnp.zeros_like(grad_ref)
     own = [part_ref[m, 0:channels, :] for m in range(members)]
-    sent_rows = -(-channels // 8) * 8
     others = []
     for ref in recv_refs:
         rows = ref[...].astype(F32)
-        others += [rows[k * sent_rows : k * sent_rows + channels] for k in range(members)]
+        others += [rows[k * channels : (k + 1) * channels] for k in range(members)]
     for m in range(members):
         slopes = jnp.zeros_like(own[m])
         for k in range(members):
@@ -372,16 +368,17 @@
         other_ref[m * rim : (m + 1) * rim, :] = rows[at + nodes + rim : at + ext].astype(BF)
 
 
-def hidden_body(own_ref, from_mate_ref, from_other_ref, halo_ref, out_ref):
-    members, nodes, _ = own_ref.shape
+def finish_body(
+    devices, own_hidden_ref, mate_ref, other_ref, halo_ref, own_ref, arrived_ref, hp_ref,
+    hidden_ref, kv_ref, out_ref, head_ref,
+):
+    members, nodes, _ = own_hidden_ref.shape
     rim = halo_ref.shape[1]
     mate, other = [one_hot_rows(rows, nodes) for rows in halo_lists(halo_ref)]
     for m in range(members):
         rows = slice(m * rim, (m + 1) * rim)
-        out_ref[m] = own_ref[m] + mm(mate, from_mate_ref[rows, :]) + mm(other, from_other_ref[rows, :])
-
-
-def finish_body(devices, own_ref, arrived_ref, hp_ref, kv_ref, out_ref, head_ref):
+        back = mm(mate, mate_ref[rows, :]) + mm(other, other_ref[rows, :])
+        hidden_ref[m] = own_hidden_ref[m] + back
     width = kv_ref.shape[1] // 2
     channels = hp_ref.shape[0]
     total = (own_ref[...] + arrived_ref[...].astype(F32)) * (1.0 / devices)
@@ -424,7 +421,6 @@
     devices = n_member * n_band
     rw = width // devices
     chips = n_band // 2
-    send_rows = -(-channels // 8) * 8
     mates = [(i, i ^ 1) for i in range(n_band)]
     others = [(i, (i + 1 if i % 2 else i - 1) % n_band) for i in range(n_band)]
 
@@ -463,12 +459,12 @@
     )
 
     halo_value, halo_gates, halo_slopes, merged, part, sent = call(
-        functools.partial(halo_body, send_rows, nodes),
+        functools.partial(halo_body, channels, nodes),
         gate_shapes(2 * rim)
         + [
             sds((members, width, points), BF),
             sds((members, LANES, points), F32),
-            sds((-(-members * send_rows // 16) * 16, points), BF),
+            sds((members * channels, points), BF),
         ],
         (other, mate, own_merged, kv_weight, qt, sources, p),
     )
@@ -538,18 +534,16 @@
         arrived = swap(add_up(*upper(terms)).astype(BF), axis, bit, count[axis])
         terms = lower(terms) + [arrived]
 
-    kv_grad, out_grad, head_grad = call(
+    return call(
         functools.partial(finish_body, devices),
-        [sds((rw, 2 * width), F32), sds((rw, width), F32), sds((rw, channels), F32)],
-        (add_up(*terms[:-1]), terms[-1], hp),
-    )
-    kv_grad, from_other = lax.optimization_barrier((kv_grad, from_other))
-    hidden_grad = call(
-        hidden_body,
-        sds((members, nodes, width), F32),
-        (own_grad, from_mate, from_other, halo),
-    )
-    return hidden_grad, kv_grad, out_grad, head_grad
+        [
+            sds((members, nodes, width), F32),
+            sds((rw, 2 * width), F32),
+            sds((rw, width), F32),
+            sds((rw, channels), F32),
+        ],
+        (own_grad, from_mate, from_other, halo, add_up(*terms[:-1]), terms[-1], hp),
+    )
 
 
 def solution(mesh):

time: 69.4 us -> 69.2 us (level)
  Pallas kernels: 14.3 us -> 13.5 us
    ppermute x1, waiting for transfers between devices: 0.42 us -> 6.33 us  [shards(): from_other = lax.ppermute(back_other, 'band', others)]
    ppermute x13, waiting for transfers between devices: 20.4 us -> 15.3 us  [swap(): return lax.ppermute(rows, axis, [(i, i ^ 1 << bit) for i in range(count)])]
    pallas_call x10 -> x9, Pallas kernels: 14.3 us -> 13.5 us  [call(): pl.pallas_call(body, out_shape=out_shape, in_specs=[pl.BlockSpec(memory_s...]
  transfers between devices with their start and end apart: 20 -> 20, of which waited for: 15 -> 14; matrix products, arithmetic and copies ran while one was open for 1% -> 1% of each run, Pallas kernels for 12% -> 11%
where the time goes in v13:
time: 69.2 us; the launch traced here: 69.1 us
  waiting for transfers between devices  30.1 us (43%)
  starting transfers between devices  23.5 us (34%)
  Pallas kernels  13.5 us (20%)
  other arithmetic  0.96 us (1%)
  between operations  0.9 us (1%)
    ppermute x13, waiting for transfers between devices, swap(): return lax.ppermute(rows, axis, [(i, i ^ 1 << bit) for i in range(count)])  15.3 us
    ppermute x13, starting transfers between devices, swap(): return lax.ppermute(rows, axis, [(i, i ^ 1 << bit) for i in range(count)])  14.3 us
    pallas_call x9, Pallas kernels, call(): pl.pallas_call(body, out_shape=out_shape, in_specs=[pl.BlockSpec(memory_s...  13.5 us
    ppermute x3, waiting for transfers between devices, shards(): lax.ppermute(sent, 'member', [(i, i ^ s) for i in range(n_member)])  6.35 us
    ppermute x1, waiting for transfers between devices, shards(): from_other = lax.ppermute(back_other, 'band', others)  6.33 us
    ppermute x3, starting transfers between devices, shards(): lax.ppermute(sent, 'member', [(i, i ^ s) for i in range(n_member)])  5.79 us
    ppermute x1, starting transfers between devices, shards(): other = lax.ppermute(for_other, 'band', others)  3.4 us
  transfers between devices with their start and end apart: 20, of which 14 were waited for; matrix products, arithmetic and copies ran while one was open for 1% of the time, Pallas kernels for 11%

profile of v13, /device:TPU:0, one launch (start us, length us, event | category | flops | bytes accessed | tf_op | source)
XLA Modules:
  0.0 69.1 jit_solution(3608123210188500824)
XLA Ops:
  0.7 1.4 %shard_map.138 = (bf16[2,64,1024]{2,1,0:T(8,128)(2,1)S(1)}, s32[2,32]{1,0:T(2,128)S(1)}, bf16[64,1024]{1,0:T(8,128)(2,1)S(1)}, bf16[64,1024]{1,0:T(8,128)(2,1)S(1)}) custom-call(bf16[2,64,1024]{2,1,0:T(8,128)(2,1)} %hidden_hbm.1, s32[2,32]{1,0:T(2,128)} %halo_hbm.1), custom_call_target="tpu_custom_call" | custom-call | flops 10000000000 | bytes 1 | tf_op jit(solution)/shard_map/pallas_call | solution.py:28
  2.1 3.4 %collective-permute-start = (bf16[64,1024]{1,0:T(8,128)(2,1)S(1)}, bf16[64,1024]{1,0:T(8,128)(2,1)S(1)}, u32[]{:S(2)}, u32[]{:S(2)}) collective-permute-start(bf16[64,1024]{1,0:T(8,128)(2,1)S(1)} %get-tuple-element.55), channel_id=1, source_target_pairs={{0,7},{1,2},{2,1},{3,4},{4,3},{5,6},{6,5},{7,0},{8,15},{9,10},{10,... | collective-permute-start | bytes 393224 | tf_op jit(solution)/shard_map/ppermute | solution.py:435
  5.6 2.4 %shard_map.139 = (bf16[2,64,1024]{2,1,0:T(8,128)(2,1)S(1)}, bf16[8,2,128,256]{3,2,1,0:T(8,128)(2,1)S(1)}, bf16[8,2,128,256]{3,2,1,0:T(8,128)(2,1)S(1)}, f32[2,10...) custom-call(bf16[2,64,1024]{2,1,0:T(8,128)(2,1)S(1)} %get-tuple-elem, ...), custom_call_target="tpu_custom_call" | custom-call | flops 1 | bytes 1 | tf_op jit(solution)/shard_map/pallas_call | solution.py:28
  8.0 0.7 %collective-permute-done.other_ref = bf16[64,1024]{1,0:T(8,128)(2,1)S(1)} collective-permute-done((bf16[64,1024]{1,0:T(8,128)(2,1)S(1)}, bf16[64,1024]{1,0:T(8,128)(2,1)S(1)}, u32[]{:S(2)}, u32[]{:S(2)}) %collective-permute-start) | collective-permute-done | bytes 131104 | tf_op jit(solution)/shard_map/ppermute | solution.py:435
  8.7 1.7 %shard_map.140 = (bf16[2,64,1024]{2,1,0:T(8,128)(2,1)S(1)}, bf16[8,2,128,256]{3,2,1,0:T(8,128)(2,1)S(1)}, bf16[8,2,128,256]{3,2,1,0:T(8,128)(2,1)S(1)}, bf16[2,1...) custom-call(bf16[64,1024]{1,0:T(8,128)(2,1)S(1)} %collective-permute-done.other_ref, ...), custom_call_target="tpu_custom_call" | custom-call | flops 1 | bytes 1 | tf_op jit(solution)/shard_map/pallas_call | solution.py:28
  10.4 5.2 %collective-permute-start.2 = (bf16[200,256]{1,0:T(8,128)(2,1)S(1)}, bf16[200,256]{1,0:T(8,128)(2,1)S(1)}, u32[]{:S(2)}, u32[]{:S(2)}) collective-permute-start(bf16[200,256]{1,0:T(8,128)(2,1)S(1)} %get-tuple-element.61), channel_id=1, source_target_pairs={{0,24},{8,16},{16,8},{24,0},{1,25},{9,17},{17,9},{25,1},{2,26},{10... | collective-permute-start | bytes 307208 | tf_op jit(solution)/shard_map/ppermute | solution.py:473
  15.6 0.6 collective-permute-start.4
  16.2 0.3 shard_map.141.refs_10_.ext_ref
  16.5 2.1 %collective-permute-done.2.refs_0_ = bf16[200,256]{1,0:T(8,128)(2,1)S(1)} collective-permute-done((bf16[200,256]{1,0:T(8,128)(2,1)S(1)}, bf16[200,256]{1,0:T(8,128)(2,1)S(1)}, u32[]{:S(2)}, u32[]{:S(2)}) %collective-permute-start.2) | collective-permute-done | bytes 102432 | tf_op jit(solution)/shard_map/ppermute | solution.py:473
  18.6 4.2 %collective-permute-done.3.refs_1_ = bf16[200,256]{1,0:T(8,128)(2,1)S(1)} collective-permute-done((bf16[200,256]{1,0:T(8,128)(2,1)S(1)}, bf16[200,256]{1,0:T(8,128)(2,1)S(1)}, u32[]{:S(2)}, u32[]{:S(2)}) %collective-permute-start.3) | collective-permute-done | bytes 102432 | tf_op jit(solution)/shard_map/ppermute | solution.py:473
  22.9 1.9 %shard_map.142 = (bf16[2,128,256]{2,1,0:T(8,128)(2,1)S(1)}, bf16[256,1024]{1,0:T(8,128)(2,1)S(1)}, bf16[512,768]{1,0:T(8,128)(2,1)S(1)}, bf16[512,768]{1,0:T(8,128)(2,1)S(1)}) custom-call(bf16[200,256]{1,0:T(8,128)(2,1)S(1)} %collective-permute-done.2.refs_0_, bf16[200,256]{1,0:T(8,128)(2,1)S(1)} %collective-permute-done.3.refs_1_, ...), custom_call_target="tpu_custom_call" | custom-call | flops 1 | bytes 1 | tf_op jit(solution)/shard_map/pallas_call | solution.py:28
  24.7 0.1 collective-permute-start.5
  24.8 1.5 %shard_map.143 = (bf16[256,512]{1,0:T(8,128)(2,1)S(1)}, bf16[512,768]{1,0:T(8,128)(2,1)S(1)}, bf16[512,768]{1,0:T(8,128)(2,1)S(1)}) custom-call(bf16[2,128,256]{2,1,0:T(8,128)(2,1)S(1)} %get-tuple-element.67.grad_ref, bf16[1024,128]{1,0:T(8,128)(2,1)S(1)} %get-tuple-element.68.pt_ref, bf16[2,64,1024]{2,1,0:T(8,128)(2,1)S(1)} %get-tuple-element.69.own_value_ref, ...), custom_call_target="tpu_custom_call" | custom-call | flops 1 | bytes 1 | tf_op jit(solution)/shard_map/pallas_call | solution.py:28
  26.3 0.6 collective-permute-start.6
  26.8 1.9 %shard_map.144 = (bf16[256,512]{1,0:T(8,128)(2,1)S(1)}, bf16[512,768]{1,0:T(8,128)(2,1)S(1)}, bf16[512,768]{1,0:T(8,128)(2,1)S(1)}) custom-call(bf16[2,128,256]{2,1,0:T(8,128)(2,1)S(1)} %get-tuple-element.67.grad_ref, bf16[1024,128]{1,0:T(8,128)(2,1)S(1)} %get-tuple-element.68.pt_ref, bf16[2,64,1024]{2,1,0:T(8,128)(2,1)S(1)} %get-tuple-element.69.own_value_ref, ...), custom_call_target="tpu_custom_call" | custom-call | flops 1 | bytes 1 | tf_op jit(solution)/shard_map/pallas_call | solution.py:28
  28.8 0.1 collective-permute-start.7
  28.9 0.1 add_convert_fusion.2
  29.0 0.1 add_convert_fusion.1
  29.1 2.0 %collective-permute-done.7 = bf16[512,768]{1,0:T(8,128)(2,1)S(1)} collective-permute-done((bf16[512,768]{1,0:T(8,128)(2,1)S(1)}, bf16[512,768]{1,0:T(8,128)(2,1)S(1)}, u32[]{:S(2)}, u32[]{:S(2)}) %collective-permute-start.7) | collective-permute-done | bytes 786464 | tf_op jit(solution)/shard_map/ppermute | solution.py:399
  31.1 0.1 add_convert_fusion
  31.2 0.5 collective-permute-start.10
  31.8 1.7 %collective-permute-start.8 = (bf16[256,768]{1,0:T(8,128)(2,1)S(1)}, bf16[256,768]{1,0:T(8,128)(2,1)S(1)}, u32[]{:S(2)}, u32[]{:S(2)}) collective-permute-start(bf16[256,768]{1,0:T(8,128)(2,1)S(1)} %add_convert_fusion.2), channel_id=1, source_target_pairs={{0,2},{1,3},{2,0},{3,1},{4,6},{5,7},{6,4},{7,5},{8,10},{9,11},{10,... | collective-permute-start | bytes 1179656 | tf_op jit(solution)/shard_map/ppermute | solution.py:399
  33.4 1.8 %collective-permute-start.9 = (bf16[256,768]{1,0:T(8,128)(2,1)S(1)}, bf16[256,768]{1,0:T(8,128)(2,1)S(1)}, u32[]{:S(2)}, u32[]{:S(2)}) collective-permute-start(bf16[256,768]{1,0:T(8,128)(2,1)S(1)} %add_convert_fusion.1), channel_id=1, source_target_pairs={{0,4},{1,5},{2,6},{3,7},{4,0},{5,1},{6,2},{7,3},{8,12},{9,13},{10,... | collective-permute-start | bytes 1179656 | tf_op jit(solution)/shard_map/ppermute | solution.py:399
  35.3 1.3 %shard_map.145 = (f32[2,64,1024]{2,1,0:T(8,128)S(1)}, bf16[64,1024]{1,0:T(8,128)(2,1)S(1)}, bf16[64,1024]{1,0:T(8,128)(2,1)S(1)}) custom-call(bf16[256,512]{1,0:T(8,128)(2,1)S(1)} %get-tuple-element.74.first_ref, bf16[256,512]{1,0:T(8,128)(2,1)S(1)} %get-tuple-element.89.last_ref, bf16[256,1024]{1,0:T(8,128)(2,1)S(1)} %get-tuple-element.73.ngv_ref, ...), custom_call_target="tpu_custom_call" | custom-call | flops 1 | bytes 1 | tf_op jit(solution)/shard_map/pallas_call | solution.py:28
  36.6 0.1 collective-permute-start.11
  36.7 1.3 %collective-permute-done.11.mate_ref = bf16[64,1024]{1,0:T(8,128)(2,1)S(1)} collective-permute-done((bf16[64,1024]{1,0:T(8,128)(2,1)S(1)}, bf16[64,1024]{1,0:T(8,128)(2,1)S(1)}, u32[]{:S(2)}, u32[]{:S(2)}) %collective-permute-start.11) | collective-permute-done | bytes 131104 | tf_op jit(solution)/shard_map/ppermute | solution.py:526
  38.0 4.5 %collective-permute-done.10 = bf16[256,768]{1,0:T(8,128)(2,1)S(1)} collective-permute-done((bf16[256,768]{1,0:T(8,128)(2,1)S(1)}, bf16[256,768]{1,0:T(8,128)(2,1)S(1)}, u32[]{:S(2)}, u32[]{:S(2)}) %collective-permute-start.10) | collective-permute-done | bytes 393248 | tf_op jit(solution)/shard_map/ppermute | solution.py:399
  42.5 0.3 collective-permute-done.8
  42.8 1.5 %collective-permute-done.9 = bf16[256,768]{1,0:T(8,128)(2,1)S(1)} collective-permute-done((bf16[256,768]{1,0:T(8,128)(2,1)S(1)}, bf16[256,768]{1,0:T(8,128)(2,1)S(1)}, u32[]{:S(2)}, u32[]{:S(2)}) %collective-permute-start.9) | collective-permute-done | bytes 393248 | tf_op jit(solution)/shard_map/ppermute | solution.py:399
  44.3 0.1 add_convert_fusion.3
  44.3 0.8 %collective-permute-start.16 = (bf16[128,768]{1,0:T(8,128)(2,1)S(1)}, bf16[128,768]{1,0:T(8,128)(2,1)S(1)}, u32[]{:S(2)}, u32[]{:S(2)}) collective-permute-start(bf16[128,768]{1,0:T(8,128)(2,1)S(1)} %add_convert_fusion.3), channel_id=1, source_target_pairs={{0,2},{1,3},{2,0},{3,1},{4,6},{5,7},{6,4},{7,5},{8,10},{9,11},{10,... | collective-permute-start | bytes 589832 | tf_op jit(solution)/shard_map/ppermute | solution.py:399
  45.1 0.1 add_convert_fusion.4
  45.2 1.7 %collective-permute-start.14 = (bf16[128,768]{1,0:T(8,128)(2,1)S(1)}, bf16[128,768]{1,0:T(8,128)(2,1)S(1)}, u32[]{:S(2)}, u32[]{:S(2)}) collective-permute-start(bf16[128,768]{1,0:T(8,128)(2,1)S(1)} %add_convert_fusion.4), channel_id=1, source_target_pairs={{0,8},{8,0},{16,24},{24,16},{1,9},{9,1},{17,25},{25,17},{2,10},{10... | collective-permute-start | bytes 589832 | tf_op jit(solution)/shard_map/ppermute | solution.py:399
  46.9 0.1 add_convert_fusion.5
  46.9 1.8 %collective-permute-start.12 = (bf16[128,768]{1,0:T(8,128)(2,1)S(1)}, bf16[128,768]{1,0:T(8,128)(2,1)S(1)}, u32[]{:S(2)}, u32[]{:S(2)}) collective-permute-start(bf16[128,768]{1,0:T(8,128)(2,1)S(1)} %add_convert_fusion.5), channel_id=1, source_target_pairs={{0,4},{1,5},{2,6},{3,7},{4,0},{5,1},{6,2},{7,3},{8,12},{9,13},{10,... | collective-permute-start | bytes 589832 | tf_op jit(solution)/shard_map/ppermute | solution.py:399
  48.8 1.4 %collective-permute-done.16 = bf16[128,768]{1,0:T(8,128)(2,1)S(1)} collective-permute-done((bf16[128,768]{1,0:T(8,128)(2,1)S(1)}, bf16[128,768]{1,0:T(8,128)(2,1)S(1)}, u32[]{:S(2)}, u32[]{:S(2)}) %collective-permute-start.16) | collective-permute-done | bytes 196640 | tf_op jit(solution)/shard_map/ppermute | solution.py:399
  50.2 1.6 %collective-permute-start.17 = (bf16[64,768]{1,0:T(8,128)(2,1)S(1)}, bf16[64,768]{1,0:T(8,128)(2,1)S(1)}, u32[]{:S(2)}, u32[]{:S(2)}) collective-permute-start(bf16[64,768]{1,0:T(8,128)(2,1)S(1)} %add_convert_fusion.6), channel_id=1, source_target_pairs={{0,4},{1,5},{2,6},{3,7},{4,0},{5,1},{6,2},{7,3},{8,12},{9,13},{10,... | collective-permute-start | bytes 294920 | tf_op jit(solution)/shard_map/ppermute | solution.py:399
  51.9 0.9 %collective-permute-start.15 = (bf16[64,768]{1,0:T(8,128)(2,1)S(1)}, bf16[64,768]{1,0:T(8,128)(2,1)S(1)}, u32[]{:S(2)}, u32[]{:S(2)}) collective-permute-start(bf16[64,768]{1,0:T(8,128)(2,1)S(1)} %add_convert_fusion.7), channel_id=1, source_target_pairs={{0,2},{1,3},{2,0},{3,1},{4,6},{5,7},{6,4},{7,5},{8,10},{9,11},{10,... | collective-permute-start | bytes 294920 | tf_op jit(solution)/shard_map/ppermute | solution.py:399
  52.8 1.0 %collective-permute-done.12 = bf16[128,768]{1,0:T(8,128)(2,1)S(1)} collective-permute-done((bf16[128,768]{1,0:T(8,128)(2,1)S(1)}, bf16[128,768]{1,0:T(8,128)(2,1)S(1)}, u32[]{:S(2)}, u32[]{:S(2)}) %collective-permute-start.12) | collective-permute-done | bytes 196640 | tf_op jit(solution)/shard_map/ppermute | solution.py:399
  53.8 0.7 %collective-permute-start.13 = (bf16[64,768]{1,0:T(8,128)(2,1)S(1)}, bf16[64,768]{1,0:T(8,128)(2,1)S(1)}, u32[]{:S(2)}, u32[]{:S(2)}) collective-permute-start(bf16[64,768]{1,0:T(8,128)(2,1)S(1)} %add_convert_fusion.8), channel_id=1, source_target_pairs={{0,8},{8,0},{16,24},{24,16},{1,9},{9,1},{17,25},{25,17},{2,10},{10... | collective-permute-start | bytes 294920 | tf_op jit(solution)/shard_map/ppermute | solution.py:399
  54.5 0.4 collective-permute-done.17
  54.9 1.7 %collective-permute-done.15 = bf16[64,768]{1,0:T(8,128)(2,1)S(1)} collective-permute-done((bf16[64,768]{1,0:T(8,128)(2,1)S(1)}, bf16[64,768]{1,0:T(8,128)(2,1)S(1)}, u32[]{:S(2)}, u32[]{:S(2)}) %collective-permute-start.15) | collective-permute-done | bytes 98336 | tf_op jit(solution)/shard_map/ppermute | solution.py:399
  56.6 2.6 %collective-permute-done.13 = bf16[64,768]{1,0:T(8,128)(2,1)S(1)} collective-permute-done((bf16[64,768]{1,0:T(8,128)(2,1)S(1)}, bf16[64,768]{1,0:T(8,128)(2,1)S(1)}, u32[]{:S(2)}, u32[]{:S(2)}) %collective-permute-start.13) | collective-permute-done | bytes 98336 | tf_op jit(solution)/shard_map/ppermute | solution.py:399
  59.2 0.1 convert_add_fusion.2
  59.3 0.1 convert_add_fusion
  59.5 2.0 %collective-permute-start.19 = (bf16[32,2304]{1,0:T(8,128)(2,1)S(1)}, bf16[32,2304]{1,0:T(8,128)(2,1)S(1)}, u32[]{:S(2)}, u32[]{:S(2)}) collective-permute-start(bf16[32,2304]{1,0:T(8,128)(2,1)S(1)} %slice.262), channel_id=1, source_target_pairs={{0,16},{8,24},{16,0},{24,8},{1,17},{9,25},{17,1},{25,9},{2,18},{10... | collective-permute-start | bytes 442376 | tf_op jit(solution)/shard_map/ppermute | solution.py:399
  61.5 6.3 %collective-permute-done.18.other_ref = bf16[64,1024]{1,0:T(8,128)(2,1)S(1)} collective-permute-done((bf16[64,1024]{1,0:T(8,128)(2,1)S(1)}, bf16[64,1024]{1,0:T(8,128)(2,1)S(1)}, u32[]{:S(2)}, u32[]{:S(2)}) %collective-permute-start.18) | collective-permute-done | bytes 131104 | tf_op jit(solution)/shard_map/ppermute | solution.py:530
  67.9 1.2 %shard_map.146 = (f32[2,64,1024]{2,1,0:T(8,128)}, f32[32,2048]{1,0:T(8,128)}, f32[32,1024]{1,0:T(8,128)}, f32[32,100]{1,0:T(8,128)}) custom-call(f32[2,64,1024]{2,1,0:T(8,128)S(1)} %get-tuple-element.90.own_hidden_ref, bf16[64,1024]{1,0:T(8,128)(2,1)S(1)} %collective-permute-done.11.mate_ref, bf16[64,1024]{1,0:T(8,128)(2,1)S(1)} %collective-permute-done.18.other_ref, ...), custom_call_target="tpu_custom_call" | custom-call | flops 1 | bytes 1 | tf_op jit(solution)/shard_map/pallas_call | solution.py:28
  (33 shorter events, 0.3 us)
Async XLA Ops:
  0.6 4.9 %copy-start.3 = (bf16[1024,100]{0,1:T(8,128)(2,1)S(1)}, bf16[1024,100]{0,1:T(8,128)(2,1)}, u32[]{:S(2)}) copy-start(bf16[1024,100]{0,1:T(8,128)(2,1)} %param.15) | copy-start | bytes 614404
  0.6 4.9 %copy-start.8 = (f32[100]{0:T(128)S(1)}, f32[100]{0:T(128)}, u32[]{:S(2)}) copy-start(f32[100]{0:T(128)} %param.19) | copy-start | bytes 1204
  0.7 4.9 %copy-start.7 = (f32[256]{0:T(256)S(1)}, f32[256]{0:T(256)}, u32[]{:S(2)}) copy-start(f32[256]{0:T(256)} %param.18) | copy-start | bytes 3076
  0.7 4.9 %copy-start.2 = (bf16[256,1024]{1,0:T(8,128)(2,1)S(1)}, bf16[256,1024]{1,0:T(8,128)(2,1)}, u32[]{:S(2)}) copy-start(bf16[256,1024]{1,0:T(8,128)(2,1)} %q_ref.5) | copy-start | bytes 1572868
  0.7 4.9 %copy-start.1 = (bf16[1024,1024]{1,0:T(8,128)(2,1)S(1)}, bf16[1024,1024]{1,0:T(8,128)(2,1)}, u32[]{:S(2)}) copy-start(bf16[1024,1024]{1,0:T(8,128)(2,1)} %wo_ref.3) | copy-start | bytes 6291460
  0.7 4.9 %copy-start.5 = (f32[100,256]{1,0:T(8,128)S(1)}, f32[100,256]{1,0:T(8,128)}, u32[]{:S(2)}) copy-start(f32[100,256]{1,0:T(8,128)} %init_ref.1) | copy-start | bytes 307204
  0.7 4.9 %copy-start.6 = (s32[3,256]{1,0:T(4,128)S(1)}, s32[3,256]{1,0:T(4,128)}, u32[]{:S(2)}) copy-start(s32[3,256]{1,0:T(4,128)} %src_ref.3) | copy-start | bytes 9220
  0.7 4.9 %copy-start = (bf16[1024,2048]{1,0:T(8,128)(2,1)S(1)}, bf16[1024,2048]{1,0:T(8,128)(2,1)}, u32[]{:S(2)}) copy-start(bf16[1024,2048]{1,0:T(8,128)(2,1)} %kvw_ref.5) | copy-start | bytes 12582916
  2.1 6.6 %collective-permute-start = (bf16[64,1024]{1,0:T(8,128)(2,1)S(1)}, bf16[64,1024]{1,0:T(8,128)(2,1)S(1)}, u32[]{:S(2)}, u32[]{:S(2)}) collective-permute-start(bf16[64,1024]{1,0:T(8,128)(2,1)S(1)} %get-tuple-element.55), channel_id=1, source_target_pairs={{0,7},{1,2},{2,1},{3,4},{4,3},{5,6},{6,5},{7,0},{8,15},{9,10},{10,... | collective-permute-start | bytes 393224 | tf_op jit(solution)/shard_map/ppermute | solution.py:435
  5.5 3.2 %collective-permute-start.1 = (bf16[64,1024]{1,0:T(8,128)(2,1)S(1)}, bf16[64,1024]{1,0:T(8,128)(2,1)S(1)}, u32[]{:S(2)}, u32[]{:S(2)}) collective-permute-start(bf16[64,1024]{1,0:T(8,128)(2,1)S(1)} %get-tuple-element.56), channel_id=1, source_target_pairs={{0,1},{1,0},{2,3},{3,2},{4,5},{5,4},{6,7},{7,6},{8,9},{9,8},{10,11... | collective-permute-start | bytes 393224 | tf_op jit(solution)/shard_map/ppermute | solution.py:436
  8.7 14.1 %copy-start.4 = (f32[100,256]{1,0:T(8,128)S(1)}, f32[100,256]{1,0:T(8,128)}, u32[]{:S(2)}) copy-start(f32[100,256]{1,0:T(8,128)} %refs_5_.1) | copy-start | bytes 307204
  10.4 8.2 %collective-permute-start.2 = (bf16[200,256]{1,0:T(8,128)(2,1)S(1)}, bf16[200,256]{1,0:T(8,128)(2,1)S(1)}, u32[]{:S(2)}, u32[]{:S(2)}) collective-permute-start(bf16[200,256]{1,0:T(8,128)(2,1)S(1)} %get-tuple-element.61), channel_id=1, source_target_pairs={{0,24},{8,16},{16,8},{24,0},{1,25},{9,17},{17,9},{25,1},{2,26},{10... | collective-permute-start | bytes 307208 | tf_op jit(solution)/shard_map/ppermute | solution.py:473
  15.6 7.3 %collective-permute-start.3 = (bf16[200,256]{1,0:T(8,128)(2,1)S(1)}, bf16[200,256]{1,0:T(8,128)(2,1)S(1)}, u32[]{:S(2)}, u32[]{:S(2)}) collective-permute-start(bf16[200,256]{1,0:T(8,128)(2,1)S(1)} %get-tuple-element.61), channel_id=1, source_target_pairs={{0,16},{8,24},{16,0},{24,8},{1,17},{9,25},{17,1},{25,9},{2,18},{10... | collective-permute-start | bytes 307208 | tf_op jit(solution)/shard_map/ppermute | solution.py:473
  15.6 7.3 %collective-permute-start.4 = (bf16[200,256]{1,0:T(8,128)(2,1)S(1)}, bf16[200,256]{1,0:T(8,128)(2,1)S(1)}, u32[]{:S(2)}, u32[]{:S(2)}) collective-permute-start(bf16[200,256]{1,0:T(8,128)(2,1)S(1)} %get-tuple-element.61), channel_id=1, source_target_pairs={{0,8},{8,0},{16,24},{24,16},{1,9},{9,1},{17,25},{25,17},{2,10},{10... | collective-permute-start | bytes 307208 | tf_op jit(solution)/shard_map/ppermute | solution.py:473
  24.7 4.1 %collective-permute-start.5 = (bf16[512,768]{1,0:T(8,128)(2,1)S(1)}, bf16[512,768]{1,0:T(8,128)(2,1)S(1)}, u32[]{:S(2)}, u32[]{:S(2)}) collective-permute-start(bf16[512,768]{1,0:T(8,128)(2,1)S(1)} %get-tuple-element.76), channel_id=1, source_target_pairs={{0,1},{1,0},{2,3},{3,2},{4,5},{5,4},{6,7},{7,6},{8,9},{9,8},{10,11... | collective-permute-start | bytes 2359304 | tf_op jit(solution)/shard_map/ppermute | solution.py:399
  26.3 2.7 %collective-permute-start.6 = (bf16[512,768]{1,0:T(8,128)(2,1)S(1)}, bf16[512,768]{1,0:T(8,128)(2,1)S(1)}, u32[]{:S(2)}, u32[]{:S(2)}) collective-permute-start(bf16[512,768]{1,0:T(8,128)(2,1)S(1)} %get-tuple-element.78), channel_id=1, source_target_pairs={{0,1},{1,0},{2,3},{3,2},{4,5},{5,4},{6,7},{7,6},{8,9},{9,8},{10,11... | collective-permute-start | bytes 2359304 | tf_op jit(solution)/shard_map/ppermute | solution.py:399
  28.8 2.4 %collective-permute-start.7 = (bf16[512,768]{1,0:T(8,128)(2,1)S(1)}, bf16[512,768]{1,0:T(8,128)(2,1)S(1)}, u32[]{:S(2)}, u32[]{:S(2)}) collective-permute-start(bf16[512,768]{1,0:T(8,128)(2,1)S(1)} %get-tuple-element.84), channel_id=1, source_target_pairs={{0,1},{1,0},{2,3},{3,2},{4,5},{5,4},{6,7},{7,6},{8,9},{9,8},{10,11... | collective-permute-start | bytes 2359304 | tf_op jit(solution)/shard_map/ppermute | solution.py:399
  31.2 11.2 %collective-permute-start.10 = (bf16[256,768]{1,0:T(8,128)(2,1)S(1)}, bf16[256,768]{1,0:T(8,128)(2,1)S(1)}, u32[]{:S(2)}, u32[]{:S(2)}) collective-permute-start(bf16[256,768]{1,0:T(8,128)(2,1)S(1)} %add_convert_fusion), channel_id=1, source_target_pairs={{0,8},{8,0},{16,24},{24,16},{1,9},{9,1},{17,25},{25,17},{2,10},{10... | collective-permute-start | bytes 1179656 | tf_op jit(solution)/shard_map/ppermute | solution.py:399
  31.8 11.0 %collective-permute-start.8 = (bf16[256,768]{1,0:T(8,128)(2,1)S(1)}, bf16[256,768]{1,0:T(8,128)(2,1)S(1)}, u32[]{:S(2)}, u32[]{:S(2)}) collective-permute-start(bf16[256,768]{1,0:T(8,128)(2,1)S(1)} %add_convert_fusion.2), channel_id=1, source_target_pairs={{0,2},{1,3},{2,0},{3,1},{4,6},{5,7},{6,4},{7,5},{8,10},{9,11},{10,... | collective-permute-start | bytes 1179656 | tf_op jit(solution)/shard_map/ppermute | solution.py:399
  33.4 10.8 %collective-permute-start.9 = (bf16[256,768]{1,0:T(8,128)(2,1)S(1)}, bf16[256,768]{1,0:T(8,128)(2,1)S(1)}, u32[]{:S(2)}, u32[]{:S(2)}) collective-permute-start(bf16[256,768]{1,0:T(8,128)(2,1)S(1)} %add_convert_fusion.1), channel_id=1, source_target_pairs={{0,4},{1,5},{2,6},{3,7},{4,0},{5,1},{6,2},{7,3},{8,12},{9,13},{10,... | collective-permute-start | bytes 1179656 | tf_op jit(solution)/shard_map/ppermute | solution.py:399
  36.6 1.4 %collective-permute-start.11 = (bf16[64,1024]{1,0:T(8,128)(2,1)S(1)}, bf16[64,1024]{1,0:T(8,128)(2,1)S(1)}, u32[]{:S(2)}, u32[]{:S(2)}) collective-permute-start(bf16[64,1024]{1,0:T(8,128)(2,1)S(1)} %get-tuple-element.94), channel_id=1, source_target_pairs={{0,1},{1,0},{2,3},{3,2},{4,5},{5,4},{6,7},{7,6},{8,9},{9,8},{10,11... | collective-permute-start | bytes 393224 | tf_op jit(solution)/shard_map/ppermute | solution.py:526
  44.3 5.8 %collective-permute-start.16 = (bf16[128,768]{1,0:T(8,128)(2,1)S(1)}, bf16[128,768]{1,0:T(8,128)(2,1)S(1)}, u32[]{:S(2)}, u32[]{:S(2)}) collective-permute-start(bf16[128,768]{1,0:T(8,128)(2,1)S(1)} %add_convert_fusion.3), channel_id=1, source_target_pairs={{0,2},{1,3},{2,0},{3,1},{4,6},{5,7},{6,4},{7,5},{8,10},{9,11},{10,... | collective-permute-start | bytes 589832 | tf_op jit(solution)/shard_map/ppermute | solution.py:399
  45.2 6.6 %collective-permute-start.14 = (bf16[128,768]{1,0:T(8,128)(2,1)S(1)}, bf16[128,768]{1,0:T(8,128)(2,1)S(1)}, u32[]{:S(2)}, u32[]{:S(2)}) collective-permute-start(bf16[128,768]{1,0:T(8,128)(2,1)S(1)} %add_convert_fusion.4), channel_id=1, source_target_pairs={{0,8},{8,0},{16,24},{24,16},{1,9},{9,1},{17,25},{25,17},{2,10},{10... | collective-permute-start | bytes 589832 | tf_op jit(solution)/shard_map/ppermute | solution.py:399
  46.9 6.8 %collective-permute-start.12 = (bf16[128,768]{1,0:T(8,128)(2,1)S(1)}, bf16[128,768]{1,0:T(8,128)(2,1)S(1)}, u32[]{:S(2)}, u32[]{:S(2)}) collective-permute-start(bf16[128,768]{1,0:T(8,128)(2,1)S(1)} %add_convert_fusion.5), channel_id=1, source_target_pairs={{0,4},{1,5},{2,6},{3,7},{4,0},{5,1},{6,2},{7,3},{8,12},{9,13},{10,... | collective-permute-start | bytes 589832 | tf_op jit(solution)/shard_map/ppermute | solution.py:399
  50.2 4.7 %collective-permute-start.17 = (bf16[64,768]{1,0:T(8,128)(2,1)S(1)}, bf16[64,768]{1,0:T(8,128)(2,1)S(1)}, u32[]{:S(2)}, u32[]{:S(2)}) collective-permute-start(bf16[64,768]{1,0:T(8,128)(2,1)S(1)} %add_convert_fusion.6), channel_id=1, source_target_pairs={{0,4},{1,5},{2,6},{3,7},{4,0},{5,1},{6,2},{7,3},{8,12},{9,13},{10,... | collective-permute-start | bytes 294920 | tf_op jit(solution)/shard_map/ppermute | solution.py:399
  51.9 4.7 %collective-permute-start.15 = (bf16[64,768]{1,0:T(8,128)(2,1)S(1)}, bf16[64,768]{1,0:T(8,128)(2,1)S(1)}, u32[]{:S(2)}, u32[]{:S(2)}) collective-permute-start(bf16[64,768]{1,0:T(8,128)(2,1)S(1)} %add_convert_fusion.7), channel_id=1, source_target_pairs={{0,2},{1,3},{2,0},{3,1},{4,6},{5,7},{6,4},{7,5},{8,10},{9,11},{10,... | collective-permute-start | bytes 294920 | tf_op jit(solution)/shard_map/ppermute | solution.py:399
  53.8 5.4 %collective-permute-start.13 = (bf16[64,768]{1,0:T(8,128)(2,1)S(1)}, bf16[64,768]{1,0:T(8,128)(2,1)S(1)}, u32[]{:S(2)}, u32[]{:S(2)}) collective-permute-start(bf16[64,768]{1,0:T(8,128)(2,1)S(1)} %add_convert_fusion.8), channel_id=1, source_target_pairs={{0,8},{8,0},{16,24},{24,16},{1,9},{9,1},{17,25},{25,17},{2,10},{10... | collective-permute-start | bytes 294920 | tf_op jit(solution)/shard_map/ppermute | solution.py:399
  59.5 8.4 %collective-permute-start.19 = (bf16[32,2304]{1,0:T(8,128)(2,1)S(1)}, bf16[32,2304]{1,0:T(8,128)(2,1)S(1)}, u32[]{:S(2)}, u32[]{:S(2)}) collective-permute-start(bf16[32,2304]{1,0:T(8,128)(2,1)S(1)} %slice.262), channel_id=1, source_target_pairs={{0,16},{8,24},{16,0},{24,8},{1,17},{9,25},{17,1},{25,9},{2,18},{10... | collective-permute-start | bytes 442376 | tf_op jit(solution)/shard_map/ppermute | solution.py:399
  61.5 6.4 %collective-permute-start.18 = (bf16[64,1024]{1,0:T(8,128)(2,1)S(1)}, bf16[64,1024]{1,0:T(8,128)(2,1)S(1)}, u32[]{:S(2)}, u32[]{:S(2)}) collective-permute-start(bf16[64,1024]{1,0:T(8,128)(2,1)S(1)} %get-tuple-element.101), channel_id=1, source_target_pairs={{0,7},{1,2},{2,1},{3,4},{4,3},{5,6},{6,5},{7,0},{8,15},{9,10},{10,... | collective-permute-start | bytes 393224 | tf_op jit(solution)/shard_map/ppermute | solution.py:530

commit v14 on v13

--- a/solution.py
+++ b/solution.py
@@ -357,15 +357,17 @@
     store_group(reorder(turned, n_member, n_band), 2, n_member, n_band, ng_ref.shape[1], out_refs)
 
 
-def extended_grad_body(members, nodes, rim, first_ref, last_ref, ngv_ref, kvw_ref, own_ref, mate_ref, other_ref):
+def extended_grad_body(members, nodes, rim, first_ref, last_ref, ngv_ref, kvw_ref, own_ref, back_ref):
     ext = nodes + 2 * rim
     grads = jnp.concatenate([first_ref[...], last_ref[...], ngv_ref[...]], axis=1)
     rows = mm(grads, kvw_ref[...], NT)
     for m in range(members):
         at = m * ext
         own_ref[m] = rows[at : at + nodes]
-        mate_ref[m * rim : (m + 1) * rim, :] = rows[at + nodes : at + nodes + rim].astype(BF)
-        other_ref[m * rim : (m + 1) * rim, :] = rows[at + nodes + rim : at + ext].astype(BF)
+        for side in range(2):
+            first = (side * members + m) * rim
+            start = at + nodes + side * rim
+            back_ref[first : first + rim, :] = rows[start : start + rim].astype(BF)
 
 
 def finish_body(
@@ -516,18 +518,20 @@
                 outgoing[i], groups[i + 1] = lax.optimization_barrier((outgoing[i], groups[i + 1]))
         if step == 0:
             outgoing, ng_last = lax.optimization_barrier((outgoing, ng_last))
-            own_grad, back_mate, back_other = call(
+            own_grad, back = call(
                 functools.partial(extended_grad_body, members, nodes, rim),
-                [sds((members, nodes, width), F32)] + [sds((members * rim, width), BF)] * 2,
+                [sds((members, nodes, width), F32), sds((2 * members * rim, width), BF)],
                 (ng_first, ng_last, ng_value, kv_weight),
             )
         arrived = [swap(out, *turn[step], count[turn[step][0]]) for out, turn in zip(outgoing, turns)]
         if step == 0:
-            from_mate = lax.ppermute(back_mate, "band", mates)
-            arrived, from_mate, back_other = lax.optimization_barrier((arrived, from_mate, back_other))
+            from_mate = lax.ppermute(back, "band", mates)
+            arrived, from_mate = lax.optimization_barrier((arrived, from_mate))
         if step == steps - 1:
-            arrived, back_other = lax.optimization_barrier((arrived, back_other))
-            from_other = lax.ppermute(back_other, "band", others)
+            onward = lower([from_mate])[0]
+            arrived, onward = lax.optimization_barrier((arrived, onward))
+            chips_on = [(i, (i + 2 - i % 2 * 4) % n_band) for i in range(n_band)]
+            from_other = lax.ppermute(onward, "band", chips_on)
         groups = [lower(terms) + [new] for terms, new in zip(groups, arrived)]
     terms = [jnp.concatenate([add_up(*group) for group in groups], axis=1)]
     for axis, bit in rest:

time: 69.2 us -> 68.7 us (level)
  waiting for transfers between devices: 30.1 us -> 28.3 us
  starting transfers between devices: 23.5 us -> 24.7 us
    ppermute x2, waiting for transfers between devices: 7.67 us -> 6.15 us  [the longest x1 4.63 us: shards(): from_other = lax.ppermute(onward, 'band', chips_on)]
    ppermute x2, starting transfers between devices: 0.07 us -> 1.28 us  [the longest x1 1.21 us: shards(): from_other = lax.ppermute(onward, 'band', chips_on)]
where the time goes in v14:
time: 68.7 us; the launch traced here: 68.6 us
  waiting for transfers between devices  28.3 us (41%)
  starting transfers between devices  24.7 us (36%)
  Pallas kernels  13.6 us (20%)
  other arithmetic  0.96 us (1%)
  between operations  0.9 us (1%)
    ppermute x13, waiting for transfers between devices, swap(): return lax.ppermute(rows, axis, [(i, i ^ 1 << bit) for i in range(count)])  15.1 us
    ppermute x13, starting transfers between devices, swap(): return lax.ppermute(rows, axis, [(i, i ^ 1 << bit) for i in range(count)])  14.3 us
    pallas_call x9, Pallas kernels, call(): pl.pallas_call(body, out_shape=out_shape, in_specs=[pl.BlockSpec(memory_s...  13.6 us
    ppermute x3, waiting for transfers between devices, shards(): lax.ppermute(sent, 'member', [(i, i ^ s) for i in range(n_member)])  6.35 us
    ppermute x3, starting transfers between devices, shards(): lax.ppermute(sent, 'member', [(i, i ^ s) for i in range(n_member)])  5.79 us
    ppermute x1, waiting for transfers between devices, shards(): from_other = lax.ppermute(onward, 'band', chips_on)  4.63 us
    ppermute x1, starting transfers between devices, shards(): other = lax.ppermute(for_other, 'band', others)  3.4 us
    ppermute x1, waiting for transfers between devices, shards(): from_mate = lax.ppermute(back, 'band', mates)  1.52 us
  transfers between devices with their start and end apart: 20, of which 14 were waited for; matrix products, arithmetic and copies ran while one was open for 1% of the time, Pallas kernels for 11%

profile of v14, /device:TPU:0, one launch (start us, length us, event | category | flops | bytes accessed | tf_op | source)
XLA Modules:
  0.0 68.6 jit_solution(5978835852589471252)
XLA Ops:
  0.7 1.4 %shard_map.138 = (bf16[2,64,1024]{2,1,0:T(8,128)(2,1)S(1)}, s32[2,32]{1,0:T(2,128)S(1)}, bf16[64,1024]{1,0:T(8,128)(2,1)S(1)}, bf16[64,1024]{1,0:T(8,128)(2,1)S(1)}) custom-call(bf16[2,64,1024]{2,1,0:T(8,128)(2,1)} %hidden_hbm.1, s32[2,32]{1,0:T(2,128)} %halo_hbm.1), custom_call_target="tpu_custom_call" | custom-call | flops 10000000000 | bytes 1 | tf_op jit(solution)/shard_map/pallas_call | solution.py:28
  2.1 3.4 %collective-permute-start = (bf16[64,1024]{1,0:T(8,128)(2,1)S(1)}, bf16[64,1024]{1,0:T(8,128)(2,1)S(1)}, u32[]{:S(2)}, u32[]{:S(2)}) collective-permute-start(bf16[64,1024]{1,0:T(8,128)(2,1)S(1)} %get-tuple-element.53), channel_id=1, source_target_pairs={{0,7},{1,2},{2,1},{3,4},{4,3},{5,6},{6,5},{7,0},{8,15},{9,10},{10,... | collective-permute-start | bytes 393224 | tf_op jit(solution)/shard_map/ppermute | solution.py:437
  5.6 2.4 %shard_map.139 = (bf16[2,64,1024]{2,1,0:T(8,128)(2,1)S(1)}, bf16[8,2,128,256]{3,2,1,0:T(8,128)(2,1)S(1)}, bf16[8,2,128,256]{3,2,1,0:T(8,128)(2,1)S(1)}, f32[2,10...) custom-call(bf16[2,64,1024]{2,1,0:T(8,128)(2,1)S(1)} %get-tuple-elem, ...), custom_call_target="tpu_custom_call" | custom-call | flops 1 | bytes 1 | tf_op jit(solution)/shard_map/pallas_call | solution.py:28
  8.0 0.7 %collective-permute-done.other_ref = bf16[64,1024]{1,0:T(8,128)(2,1)S(1)} collective-permute-done((bf16[64,1024]{1,0:T(8,128)(2,1)S(1)}, bf16[64,1024]{1,0:T(8,128)(2,1)S(1)}, u32[]{:S(2)}, u32[]{:S(2)}) %collective-permute-start) | collective-permute-done | bytes 131104 | tf_op jit(solution)/shard_map/ppermute | solution.py:437
  8.7 1.7 %shard_map.140 = (bf16[2,64,1024]{2,1,0:T(8,128)(2,1)S(1)}, bf16[8,2,128,256]{3,2,1,0:T(8,128)(2,1)S(1)}, bf16[8,2,128,256]{3,2,1,0:T(8,128)(2,1)S(1)}, bf16[2,1...) custom-call(bf16[64,1024]{1,0:T(8,128)(2,1)S(1)} %collective-permute-done.other_ref, ...), custom_call_target="tpu_custom_call" | custom-call | flops 1 | bytes 1 | tf_op jit(solution)/shard_map/pallas_call | solution.py:28
  10.4 5.2 %collective-permute-start.2 = (bf16[200,256]{1,0:T(8,128)(2,1)S(1)}, bf16[200,256]{1,0:T(8,128)(2,1)S(1)}, u32[]{:S(2)}, u32[]{:S(2)}) collective-permute-start(bf16[200,256]{1,0:T(8,128)(2,1)S(1)} %get-tuple-element.59), channel_id=1, source_target_pairs={{0,24},{8,16},{16,8},{24,0},{1,25},{9,17},{17,9},{25,1},{2,26},{10... | collective-permute-start | bytes 307208 | tf_op jit(solution)/shard_map/ppermute | solution.py:475
  15.6 0.6 collective-permute-start.4
  16.2 0.3 shard_map.141.refs_10_.ext_ref
  16.5 2.1 %collective-permute-done.2.refs_0_ = bf16[200,256]{1,0:T(8,128)(2,1)S(1)} collective-permute-done((bf16[200,256]{1,0:T(8,128)(2,1)S(1)}, bf16[200,256]{1,0:T(8,128)(2,1)S(1)}, u32[]{:S(2)}, u32[]{:S(2)}) %collective-permute-start.2) | collective-permute-done | bytes 102432 | tf_op jit(solution)/shard_map/ppermute | solution.py:475
  18.6 4.2 %collective-permute-done.3.refs_1_ = bf16[200,256]{1,0:T(8,128)(2,1)S(1)} collective-permute-done((bf16[200,256]{1,0:T(8,128)(2,1)S(1)}, bf16[200,256]{1,0:T(8,128)(2,1)S(1)}, u32[]{:S(2)}, u32[]{:S(2)}) %collective-permute-start.3) | collective-permute-done | bytes 102432 | tf_op jit(solution)/shard_map/ppermute | solution.py:475
  22.9 1.9 %shard_map.142 = (bf16[2,128,256]{2,1,0:T(8,128)(2,1)S(1)}, bf16[256,1024]{1,0:T(8,128)(2,1)S(1)}, bf16[512,768]{1,0:T(8,128)(2,1)S(1)}, bf16[512,768]{1,0:T(8,128)(2,1)S(1)}) custom-call(bf16[200,256]{1,0:T(8,128)(2,1)S(1)} %collective-permute-done.2.refs_0_, bf16[200,256]{1,0:T(8,128)(2,1)S(1)} %collective-permute-done.3.refs_1_, ...), custom_call_target="tpu_custom_call" | custom-call | flops 1 | bytes 1 | tf_op jit(solution)/shard_map/pallas_call | solution.py:28
  24.7 0.1 collective-permute-start.5
  24.8 1.5 %shard_map.143 = (bf16[256,512]{1,0:T(8,128)(2,1)S(1)}, bf16[512,768]{1,0:T(8,128)(2,1)S(1)}, bf16[512,768]{1,0:T(8,128)(2,1)S(1)}) custom-call(bf16[2,128,256]{2,1,0:T(8,128)(2,1)S(1)} %get-tuple-element.65.grad_ref, bf16[1024,128]{1,0:T(8,128)(2,1)S(1)} %get-tuple-element.66.pt_ref, bf16[2,64,1024]{2,1,0:T(8,128)(2,1)S(1)} %get-tuple-element.67.own_value_ref, ...), custom_call_target="tpu_custom_call" | custom-call | flops 1 | bytes 1 | tf_op jit(solution)/shard_map/pallas_call | solution.py:28
  26.3 0.6 collective-permute-start.6
  26.8 1.9 %shard_map.144 = (bf16[256,512]{1,0:T(8,128)(2,1)S(1)}, bf16[512,768]{1,0:T(8,128)(2,1)S(1)}, bf16[512,768]{1,0:T(8,128)(2,1)S(1)}) custom-call(bf16[2,128,256]{2,1,0:T(8,128)(2,1)S(1)} %get-tuple-element.65.grad_ref, bf16[1024,128]{1,0:T(8,128)(2,1)S(1)} %get-tuple-element.66.pt_ref, bf16[2,64,1024]{2,1,0:T(8,128)(2,1)S(1)} %get-tuple-element.67.own_value_ref, ...), custom_call_target="tpu_custom_call" | custom-call | flops 1 | bytes 1 | tf_op jit(solution)/shard_map/pallas_call | solution.py:28
  28.8 0.1 collective-permute-start.7
  28.9 0.1 add_convert_fusion.2
  29.0 0.1 add_convert_fusion.1
  29.1 2.0 %collective-permute-done.7 = bf16[512,768]{1,0:T(8,128)(2,1)S(1)} collective-permute-done((bf16[512,768]{1,0:T(8,128)(2,1)S(1)}, bf16[512,768]{1,0:T(8,128)(2,1)S(1)}, u32[]{:S(2)}, u32[]{:S(2)}) %collective-permute-start.7) | collective-permute-done | bytes 786464 | tf_op jit(solution)/shard_map/ppermute | solution.py:401
  31.1 0.1 add_convert_fusion
  31.2 0.5 collective-permute-start.10
  31.8 1.7 %collective-permute-start.8 = (bf16[256,768]{1,0:T(8,128)(2,1)S(1)}, bf16[256,768]{1,0:T(8,128)(2,1)S(1)}, u32[]{:S(2)}, u32[]{:S(2)}) collective-permute-start(bf16[256,768]{1,0:T(8,128)(2,1)S(1)} %add_convert_fusion.2), channel_id=1, source_target_pairs={{0,2},{1,3},{2,0},{3,1},{4,6},{5,7},{6,4},{7,5},{8,10},{9,11},{10,... | collective-permute-start | bytes 1179656 | tf_op jit(solution)/shard_map/ppermute | solution.py:401
  33.4 1.8 %collective-permute-start.9 = (bf16[256,768]{1,0:T(8,128)(2,1)S(1)}, bf16[256,768]{1,0:T(8,128)(2,1)S(1)}, u32[]{:S(2)}, u32[]{:S(2)}) collective-permute-start(bf16[256,768]{1,0:T(8,128)(2,1)S(1)} %add_convert_fusion.1), channel_id=1, source_target_pairs={{0,4},{1,5},{2,6},{3,7},{4,0},{5,1},{6,2},{7,3},{8,12},{9,13},{10,... | collective-permute-start | bytes 1179656 | tf_op jit(solution)/shard_map/ppermute | solution.py:401
  35.3 1.3 %shard_map.145 = (f32[2,64,1024]{2,1,0:T(8,128)S(1)}, bf16[128,1024]{1,0:T(8,128)(2,1)S(1)}) custom-call(bf16[256,512]{1,0:T(8,128)(2,1)S(1)} %get-tuple-element.72.first_ref, bf16[256,512]{1,0:T(8,128)(2,1)S(1)} %get-tuple-element.87.last_ref, bf16[256,1024]{1,0:T(8,128)(2,1)S(1)} %get-tuple-element.71.ngv_ref, bf16[1024,2048]{1,0:T(8,128)(2,1)S(1)} %copy-done), custom_call_target="tpu_custom_call" | custom-call | flops 1 | bytes 1 | tf_op jit(solution)/shard_map/pallas_call | solution.py:28
  36.6 0.1 collective-permute-start.11
  36.7 1.5 %collective-permute-done.11.mate_ref = bf16[128,1024]{1,0:T(8,128)(2,1)S(1)} collective-permute-done((bf16[128,1024]{1,0:T(8,128)(2,1)S(1)}, bf16[128,1024]{1,0:T(8,128)(2,1)S(1)}, u32[]{:S(2)}, u32[]{:S(2)}) %collective-permute-start.11) | collective-permute-done | bytes 262176 | tf_op jit(solution)/shard_map/ppermute | solution.py:528
  38.2 4.3 %collective-permute-done.10 = bf16[256,768]{1,0:T(8,128)(2,1)S(1)} collective-permute-done((bf16[256,768]{1,0:T(8,128)(2,1)S(1)}, bf16[256,768]{1,0:T(8,128)(2,1)S(1)}, u32[]{:S(2)}, u32[]{:S(2)}) %collective-permute-start.10) | collective-permute-done | bytes 393248 | tf_op jit(solution)/shard_map/ppermute | solution.py:401
  42.5 0.3 collective-permute-done.8
  42.8 1.5 %collective-permute-done.9 = bf16[256,768]{1,0:T(8,128)(2,1)S(1)} collective-permute-done((bf16[256,768]{1,0:T(8,128)(2,1)S(1)}, bf16[256,768]{1,0:T(8,128)(2,1)S(1)}, u32[]{:S(2)}, u32[]{:S(2)}) %collective-permute-start.9) | collective-permute-done | bytes 393248 | tf_op jit(solution)/shard_map/ppermute | solution.py:401
  44.3 0.1 add_convert_fusion.3
  44.3 0.8 %collective-permute-start.16 = (bf16[128,768]{1,0:T(8,128)(2,1)S(1)}, bf16[128,768]{1,0:T(8,128)(2,1)S(1)}, u32[]{:S(2)}, u32[]{:S(2)}) collective-permute-start(bf16[128,768]{1,0:T(8,128)(2,1)S(1)} %add_convert_fusion.3), channel_id=1, source_target_pairs={{0,2},{1,3},{2,0},{3,1},{4,6},{5,7},{6,4},{7,5},{8,10},{9,11},{10,... | collective-permute-start | bytes 589832 | tf_op jit(solution)/shard_map/ppermute | solution.py:401
  45.1 0.1 add_convert_fusion.4
  45.2 1.7 %collective-permute-start.14 = (bf16[128,768]{1,0:T(8,128)(2,1)S(1)}, bf16[128,768]{1,0:T(8,128)(2,1)S(1)}, u32[]{:S(2)}, u32[]{:S(2)}) collective-permute-start(bf16[128,768]{1,0:T(8,128)(2,1)S(1)} %add_convert_fusion.4), channel_id=1, source_target_pairs={{0,8},{8,0},{16,24},{24,16},{1,9},{9,1},{17,25},{25,17},{2,10},{10... | collective-permute-start | bytes 589832 | tf_op jit(solution)/shard_map/ppermute | solution.py:401
  46.9 0.1 add_convert_fusion.5
  46.9 1.8 %collective-permute-start.12 = (bf16[128,768]{1,0:T(8,128)(2,1)S(1)}, bf16[128,768]{1,0:T(8,128)(2,1)S(1)}, u32[]{:S(2)}, u32[]{:S(2)}) collective-permute-start(bf16[128,768]{1,0:T(8,128)(2,1)S(1)} %add_convert_fusion.5), channel_id=1, source_target_pairs={{0,4},{1,5},{2,6},{3,7},{4,0},{5,1},{6,2},{7,3},{8,12},{9,13},{10,... | collective-permute-start | bytes 589832 | tf_op jit(solution)/shard_map/ppermute | solution.py:401
  48.8 1.4 %collective-permute-done.16 = bf16[128,768]{1,0:T(8,128)(2,1)S(1)} collective-permute-done((bf16[128,768]{1,0:T(8,128)(2,1)S(1)}, bf16[128,768]{1,0:T(8,128)(2,1)S(1)}, u32[]{:S(2)}, u32[]{:S(2)}) %collective-permute-start.16) | collective-permute-done | bytes 196640 | tf_op jit(solution)/shard_map/ppermute | solution.py:401
  50.2 1.6 %collective-permute-start.17 = (bf16[64,768]{1,0:T(8,128)(2,1)S(1)}, bf16[64,768]{1,0:T(8,128)(2,1)S(1)}, u32[]{:S(2)}, u32[]{:S(2)}) collective-permute-start(bf16[64,768]{1,0:T(8,128)(2,1)S(1)} %add_convert_fusion.6), channel_id=1, source_target_pairs={{0,4},{1,5},{2,6},{3,7},{4,0},{5,1},{6,2},{7,3},{8,12},{9,13},{10,... | collective-permute-start | bytes 294920 | tf_op jit(solution)/shard_map/ppermute | solution.py:401
  51.9 0.9 %collective-permute-start.15 = (bf16[64,768]{1,0:T(8,128)(2,1)S(1)}, bf16[64,768]{1,0:T(8,128)(2,1)S(1)}, u32[]{:S(2)}, u32[]{:S(2)}) collective-permute-start(bf16[64,768]{1,0:T(8,128)(2,1)S(1)} %add_convert_fusion.7), channel_id=1, source_target_pairs={{0,2},{1,3},{2,0},{3,1},{4,6},{5,7},{6,4},{7,5},{8,10},{9,11},{10,... | collective-permute-start | bytes 294920 | tf_op jit(solution)/shard_map/ppermute | solution.py:401
  52.8 1.0 %collective-permute-done.12 = bf16[128,768]{1,0:T(8,128)(2,1)S(1)} collective-permute-done((bf16[128,768]{1,0:T(8,128)(2,1)S(1)}, bf16[128,768]{1,0:T(8,128)(2,1)S(1)}, u32[]{:S(2)}, u32[]{:S(2)}) %collective-permute-start.12) | collective-permute-done | bytes 196640 | tf_op jit(solution)/shard_map/ppermute | solution.py:401
  53.8 0.7 %collective-permute-start.13 = (bf16[64,768]{1,0:T(8,128)(2,1)S(1)}, bf16[64,768]{1,0:T(8,128)(2,1)S(1)}, u32[]{:S(2)}, u32[]{:S(2)}) collective-permute-start(bf16[64,768]{1,0:T(8,128)(2,1)S(1)} %add_convert_fusion.8), channel_id=1, source_target_pairs={{0,8},{8,0},{16,24},{24,16},{1,9},{9,1},{17,25},{25,17},{2,10},{10... | collective-permute-start | bytes 294920 | tf_op jit(solution)/shard_map/ppermute | solution.py:401
  54.5 0.4 collective-permute-done.17
  54.9 1.7 %collective-permute-done.15 = bf16[64,768]{1,0:T(8,128)(2,1)S(1)} collective-permute-done((bf16[64,768]{1,0:T(8,128)(2,1)S(1)}, bf16[64,768]{1,0:T(8,128)(2,1)S(1)}, u32[]{:S(2)}, u32[]{:S(2)}) %collective-permute-start.15) | collective-permute-done | bytes 98336 | tf_op jit(solution)/shard_map/ppermute | solution.py:401
  56.6 2.6 %collective-permute-done.13 = bf16[64,768]{1,0:T(8,128)(2,1)S(1)} collective-permute-done((bf16[64,768]{1,0:T(8,128)(2,1)S(1)}, bf16[64,768]{1,0:T(8,128)(2,1)S(1)}, u32[]{:S(2)}, u32[]{:S(2)}) %collective-permute-start.13) | collective-permute-done | bytes 98336 | tf_op jit(solution)/shard_map/ppermute | solution.py:401
  59.3 0.1 convert_add_fusion
  59.5 2.0 %collective-permute-start.19 = (bf16[32,2304]{1,0:T(8,128)(2,1)S(1)}, bf16[32,2304]{1,0:T(8,128)(2,1)S(1)}, u32[]{:S(2)}, u32[]{:S(2)}) collective-permute-start(bf16[32,2304]{1,0:T(8,128)(2,1)S(1)} %slice.266), channel_id=1, source_target_pairs={{0,16},{8,24},{16,0},{24,8},{1,17},{9,25},{17,1},{25,9},{2,18},{10... | collective-permute-start | bytes 442376 | tf_op jit(solution)/shard_map/ppermute | solution.py:401
  61.5 1.2 %collective-permute-start.18 = (bf16[64,1024]{1,0:T(8,128)(2,1)S(1)}, bf16[64,1024]{1,0:T(8,128)(2,1)S(1)}, u32[]{:S(2)}, u32[]{:S(2)}) collective-permute-start(bf16[64,1024]{1,0:T(8,128)(2,1)S(1)} %slice.199), channel_id=1, source_target_pairs={{0,2},{1,7},{2,4},{3,1},{4,6},{5,3},{6,0},{7,5},{8,10},{9,15},{10,... | collective-permute-start | bytes 393224 | tf_op jit(solution)/shard_map/ppermute | solution.py:534
  62.7 4.6 %collective-permute-done.18.other_ref = bf16[64,1024]{1,0:T(8,128)(2,1)S(1)} collective-permute-done((bf16[64,1024]{1,0:T(8,128)(2,1)S(1)}, bf16[64,1024]{1,0:T(8,128)(2,1)S(1)}, u32[]{:S(2)}, u32[]{:S(2)}) %collective-permute-start.18) | collective-permute-done | bytes 131104 | tf_op jit(solution)/shard_map/ppermute | solution.py:534
  67.4 1.2 %shard_map.146 = (f32[2,64,1024]{2,1,0:T(8,128)}, f32[32,2048]{1,0:T(8,128)}, f32[32,1024]{1,0:T(8,128)}, f32[32,100]{1,0:T(8,128)}) custom-call(f32[2,64,1024]{2,1,0:T(8,128)S(1)} %get-tuple-element.88.own_hidden_ref, bf16[128,1024]{1,0:T(8,128)(2,1)S(1)} %collective-permute-done.11.mate_ref, bf16[64,1024]{1,0:T(8,128)(2,1)S(1)} %collective-permute-done.18.other_ref, ...), custom_call_target="tpu_custom_call" | custom-call | flops 1 | bytes 1 | tf_op jit(solution)/shard_map/pallas_call | solution.py:28
  (34 shorter events, 0.4 us)
Async XLA Ops:
  0.6 4.9 %copy-start.3 = (bf16[1024,100]{0,1:T(8,128)(2,1)S(1)}, bf16[1024,100]{0,1:T(8,128)(2,1)}, u32[]{:S(2)}) copy-start(bf16[1024,100]{0,1:T(8,128)(2,1)} %param.15) | copy-start | bytes 614404
  0.6 4.9 %copy-start.8 = (f32[100]{0:T(128)S(1)}, f32[100]{0:T(128)}, u32[]{:S(2)}) copy-start(f32[100]{0:T(128)} %param.19) | copy-start | bytes 1204
  0.7 4.9 %copy-start.7 = (f32[256]{0:T(256)S(1)}, f32[256]{0:T(256)}, u32[]{:S(2)}) copy-start(f32[256]{0:T(256)} %param.18) | copy-start | bytes 3076
  0.7 4.9 %copy-start.2 = (bf16[256,1024]{1,0:T(8,128)(2,1)S(1)}, bf16[256,1024]{1,0:T(8,128)(2,1)}, u32[]{:S(2)}) copy-start(bf16[256,1024]{1,0:T(8,128)(2,1)} %q_ref.5) | copy-start | bytes 1572868
  0.7 4.9 %copy-start.1 = (bf16[1024,1024]{1,0:T(8,128)(2,1)S(1)}, bf16[1024,1024]{1,0:T(8,128)(2,1)}, u32[]{:S(2)}) copy-start(bf16[1024,1024]{1,0:T(8,128)(2,1)} %wo_ref.3) | copy-start | bytes 6291460
  0.7 4.9 %copy-start.5 = (f32[100,256]{1,0:T(8,128)S(1)}, f32[100,256]{1,0:T(8,128)}, u32[]{:S(2)}) copy-start(f32[100,256]{1,0:T(8,128)} %init_ref.1) | copy-start | bytes 307204
  0.7 4.9 %copy-start.6 = (s32[3,256]{1,0:T(4,128)S(1)}, s32[3,256]{1,0:T(4,128)}, u32[]{:S(2)}) copy-start(s32[3,256]{1,0:T(4,128)} %src_ref.3) | copy-start | bytes 9220
  0.7 4.9 %copy-start = (bf16[1024,2048]{1,0:T(8,128)(2,1)S(1)}, bf16[1024,2048]{1,0:T(8,128)(2,1)}, u32[]{:S(2)}) copy-start(bf16[1024,2048]{1,0:T(8,128)(2,1)} %kvw_ref.5) | copy-start | bytes 12582916
  2.1 6.6 %collective-permute-start = (bf16[64,1024]{1,0:T(8,128)(2,1)S(1)}, bf16[64,1024]{1,0:T(8,128)(2,1)S(1)}, u32[]{:S(2)}, u32[]{:S(2)}) collective-permute-start(bf16[64,1024]{1,0:T(8,128)(2,1)S(1)} %get-tuple-element.53), channel_id=1, source_target_pairs={{0,7},{1,2},{2,1},{3,4},{4,3},{5,6},{6,5},{7,0},{8,15},{9,10},{10,... | collective-permute-start | bytes 393224 | tf_op jit(solution)/shard_map/ppermute | solution.py:437
  5.5 3.2 %collective-permute-start.1 = (bf16[64,1024]{1,0:T(8,128)(2,1)S(1)}, bf16[64,1024]{1,0:T(8,128)(2,1)S(1)}, u32[]{:S(2)}, u32[]{:S(2)}) collective-permute-start(bf16[64,1024]{1,0:T(8,128)(2,1)S(1)} %get-tuple-element.54), channel_id=1, source_target_pairs={{0,1},{1,0},{2,3},{3,2},{4,5},{5,4},{6,7},{7,6},{8,9},{9,8},{10,11... | collective-permute-start | bytes 393224 | tf_op jit(solution)/shard_map/ppermute | solution.py:438
  8.7 14.1 %copy-start.4 = (f32[100,256]{1,0:T(8,128)S(1)}, f32[100,256]{1,0:T(8,128)}, u32[]{:S(2)}) copy-start(f32[100,256]{1,0:T(8,128)} %refs_5_.1) | copy-start | bytes 307204
  10.4 8.2 %collective-permute-start.2 = (bf16[200,256]{1,0:T(8,128)(2,1)S(1)}, bf16[200,256]{1,0:T(8,128)(2,1)S(1)}, u32[]{:S(2)}, u32[]{:S(2)}) collective-permute-start(bf16[200,256]{1,0:T(8,128)(2,1)S(1)} %get-tuple-element.59), channel_id=1, source_target_pairs={{0,24},{8,16},{16,8},{24,0},{1,25},{9,17},{17,9},{25,1},{2,26},{10... | collective-permute-start | bytes 307208 | tf_op jit(solution)/shard_map/ppermute | solution.py:475
  15.6 7.3 %collective-permute-start.3 = (bf16[200,256]{1,0:T(8,128)(2,1)S(1)}, bf16[200,256]{1,0:T(8,128)(2,1)S(1)}, u32[]{:S(2)}, u32[]{:S(2)}) collective-permute-start(bf16[200,256]{1,0:T(8,128)(2,1)S(1)} %get-tuple-element.59), channel_id=1, source_target_pairs={{0,16},{8,24},{16,0},{24,8},{1,17},{9,25},{17,1},{25,9},{2,18},{10... | collective-permute-start | bytes 307208 | tf_op jit(solution)/shard_map/ppermute | solution.py:475
  15.6 7.3 %collective-permute-start.4 = (bf16[200,256]{1,0:T(8,128)(2,1)S(1)}, bf16[200,256]{1,0:T(8,128)(2,1)S(1)}, u32[]{:S(2)}, u32[]{:S(2)}) collective-permute-start(bf16[200,256]{1,0:T(8,128)(2,1)S(1)} %get-tuple-element.59), channel_id=1, source_target_pairs={{0,8},{8,0},{16,24},{24,16},{1,9},{9,1},{17,25},{25,17},{2,10},{10... | collective-permute-start | bytes 307208 | tf_op jit(solution)/shard_map/ppermute | solution.py:475
  24.7 4.1 %collective-permute-start.5 = (bf16[512,768]{1,0:T(8,128)(2,1)S(1)}, bf16[512,768]{1,0:T(8,128)(2,1)S(1)}, u32[]{:S(2)}, u32[]{:S(2)}) collective-permute-start(bf16[512,768]{1,0:T(8,128)(2,1)S(1)} %get-tuple-element.74), channel_id=1, source_target_pairs={{0,1},{1,0},{2,3},{3,2},{4,5},{5,4},{6,7},{7,6},{8,9},{9,8},{10,11... | collective-permute-start | bytes 2359304 | tf_op jit(solution)/shard_map/ppermute | solution.py:401
  26.3 2.7 %collective-permute-start.6 = (bf16[512,768]{1,0:T(8,128)(2,1)S(1)}, bf16[512,768]{1,0:T(8,128)(2,1)S(1)}, u32[]{:S(2)}, u32[]{:S(2)}) collective-permute-start(bf16[512,768]{1,0:T(8,128)(2,1)S(1)} %get-tuple-element.76), channel_id=1, source_target_pairs={{0,1},{1,0},{2,3},{3,2},{4,5},{5,4},{6,7},{7,6},{8,9},{9,8},{10,11... | collective-permute-start | bytes 2359304 | tf_op jit(solution)/shard_map/ppermute | solution.py:401
  28.8 2.4 %collective-permute-start.7 = (bf16[512,768]{1,0:T(8,128)(2,1)S(1)}, bf16[512,768]{1,0:T(8,128)(2,1)S(1)}, u32[]{:S(2)}, u32[]{:S(2)}) collective-permute-start(bf16[512,768]{1,0:T(8,128)(2,1)S(1)} %get-tuple-element.82), channel_id=1, source_target_pairs={{0,1},{1,0},{2,3},{3,2},{4,5},{5,4},{6,7},{7,6},{8,9},{9,8},{10,11... | collective-permute-start | bytes 2359304 | tf_op jit(solution)/shard_map/ppermute | solution.py:401
  31.2 11.2 %collective-permute-start.10 = (bf16[256,768]{1,0:T(8,128)(2,1)S(1)}, bf16[256,768]{1,0:T(8,128)(2,1)S(1)}, u32[]{:S(2)}, u32[]{:S(2)}) collective-permute-start(bf16[256,768]{1,0:T(8,128)(2,1)S(1)} %add_convert_fusion), channel_id=1, source_target_pairs={{0,8},{8,0},{16,24},{24,16},{1,9},{9,1},{17,25},{25,17},{2,10},{10... | collective-permute-start | bytes 1179656 | tf_op jit(solution)/shard_map/ppermute | solution.py:401
  31.8 11.0 %collective-permute-start.8 = (bf16[256,768]{1,0:T(8,128)(2,1)S(1)}, bf16[256,768]{1,0:T(8,128)(2,1)S(1)}, u32[]{:S(2)}, u32[]{:S(2)}) collective-permute-start(bf16[256,768]{1,0:T(8,128)(2,1)S(1)} %add_convert_fusion.2), channel_id=1, source_target_pairs={{0,2},{1,3},{2,0},{3,1},{4,6},{5,7},{6,4},{7,5},{8,10},{9,11},{10,... | collective-permute-start | bytes 1179656 | tf_op jit(solution)/shard_map/ppermute | solution.py:401
  33.4 10.8 %collective-permute-start.9 = (bf16[256,768]{1,0:T(8,128)(2,1)S(1)}, bf16[256,768]{1,0:T(8,128)(2,1)S(1)}, u32[]{:S(2)}, u32[]{:S(2)}) collective-permute-start(bf16[256,768]{1,0:T(8,128)(2,1)S(1)} %add_convert_fusion.1), channel_id=1, source_target_pairs={{0,4},{1,5},{2,6},{3,7},{4,0},{5,1},{6,2},{7,3},{8,12},{9,13},{10,... | collective-permute-start | bytes 1179656 | tf_op jit(solution)/shard_map/ppermute | solution.py:401
  36.6 1.6 %collective-permute-start.11 = (bf16[128,1024]{1,0:T(8,128)(2,1)S(1)}, bf16[128,1024]{1,0:T(8,128)(2,1)S(1)}, u32[]{:S(2)}, u32[]{:S(2)}) collective-permute-start(bf16[128,1024]{1,0:T(8,128)(2,1)S(1)} %get-tuple-element.92), channel_id=1, source_target_pairs={{0,1},{1,0},{2,3},{3,2},{4,5},{5,4},{6,7},{7,6},{8,9},{9,8},{10,11... | collective-permute-start | bytes 786440 | tf_op jit(solution)/shard_map/ppermute | solution.py:528
  44.3 5.8 %collective-permute-start.16 = (bf16[128,768]{1,0:T(8,128)(2,1)S(1)}, bf16[128,768]{1,0:T(8,128)(2,1)S(1)}, u32[]{:S(2)}, u32[]{:S(2)}) collective-permute-start(bf16[128,768]{1,0:T(8,128)(2,1)S(1)} %add_convert_fusion.3), channel_id=1, source_target_pairs={{0,2},{1,3},{2,0},{3,1},{4,6},{5,7},{6,4},{7,5},{8,10},{9,11},{10,... | collective-permute-start | bytes 589832 | tf_op jit(solution)/shard_map/ppermute | solution.py:401
  45.2 6.6 %collective-permute-start.14 = (bf16[128,768]{1,0:T(8,128)(2,1)S(1)}, bf16[128,768]{1,0:T(8,128)(2,1)S(1)}, u32[]{:S(2)}, u32[]{:S(2)}) collective-permute-start(bf16[128,768]{1,0:T(8,128)(2,1)S(1)} %add_convert_fusion.4), channel_id=1, source_target_pairs={{0,8},{8,0},{16,24},{24,16},{1,9},{9,1},{17,25},{25,17},{2,10},{10... | collective-permute-start | bytes 589832 | tf_op jit(solution)/shard_map/ppermute | solution.py:401
  46.9 6.8 %collective-permute-start.12 = (bf16[128,768]{1,0:T(8,128)(2,1)S(1)}, bf16[128,768]{1,0:T(8,128)(2,1)S(1)}, u32[]{:S(2)}, u32[]{:S(2)}) collective-permute-start(bf16[128,768]{1,0:T(8,128)(2,1)S(1)} %add_convert_fusion.5), channel_id=1, source_target_pairs={{0,4},{1,5},{2,6},{3,7},{4,0},{5,1},{6,2},{7,3},{8,12},{9,13},{10,... | collective-permute-start | bytes 589832 | tf_op jit(solution)/shard_map/ppermute | solution.py:401
  50.2 4.7 %collective-permute-start.17 = (bf16[64,768]{1,0:T(8,128)(2,1)S(1)}, bf16[64,768]{1,0:T(8,128)(2,1)S(1)}, u32[]{:S(2)}, u32[]{:S(2)}) collective-permute-start(bf16[64,768]{1,0:T(8,128)(2,1)S(1)} %add_convert_fusion.6), channel_id=1, source_target_pairs={{0,4},{1,5},{2,6},{3,7},{4,0},{5,1},{6,2},{7,3},{8,12},{9,13},{10,... | collective-permute-start | bytes 294920 | tf_op jit(solution)/shard_map/ppermute | solution.py:401
  51.9 4.7 %collective-permute-start.15 = (bf16[64,768]{1,0:T(8,128)(2,1)S(1)}, bf16[64,768]{1,0:T(8,128)(2,1)S(1)}, u32[]{:S(2)}, u32[]{:S(2)}) collective-permute-start(bf16[64,768]{1,0:T(8,128)(2,1)S(1)} %add_convert_fusion.7), channel_id=1, source_target_pairs={{0,2},{1,3},{2,0},{3,1},{4,6},{5,7},{6,4},{7,5},{8,10},{9,11},{10,... | collective-permute-start | bytes 294920 | tf_op jit(solution)/shard_map/ppermute | solution.py:401
  53.8 5.4 %collective-permute-start.13 = (bf16[64,768]{1,0:T(8,128)(2,1)S(1)}, bf16[64,768]{1,0:T(8,128)(2,1)S(1)}, u32[]{:S(2)}, u32[]{:S(2)}) collective-permute-start(bf16[64,768]{1,0:T(8,128)(2,1)S(1)} %add_convert_fusion.8), channel_id=1, source_target_pairs={{0,8},{8,0},{16,24},{24,16},{1,9},{9,1},{17,25},{25,17},{2,10},{10... | collective-permute-start | bytes 294920 | tf_op jit(solution)/shard_map/ppermute | solution.py:401
  59.5 7.9 %collective-permute-start.19 = (bf16[32,2304]{1,0:T(8,128)(2,1)S(1)}, bf16[32,2304]{1,0:T(8,128)(2,1)S(1)}, u32[]{:S(2)}, u32[]{:S(2)}) collective-permute-start(bf16[32,2304]{1,0:T(8,128)(2,1)S(1)} %slice.266), channel_id=1, source_target_pairs={{0,16},{8,24},{16,0},{24,8},{1,17},{9,25},{17,1},{25,9},{2,18},{10... | collective-permute-start | bytes 442376 | tf_op jit(solution)/shard_map/ppermute | solution.py:401
  61.5 5.9 %collective-permute-start.18 = (bf16[64,1024]{1,0:T(8,128)(2,1)S(1)}, bf16[64,1024]{1,0:T(8,128)(2,1)S(1)}, u32[]{:S(2)}, u32[]{:S(2)}) collective-permute-start(bf16[64,1024]{1,0:T(8,128)(2,1)S(1)} %slice.199), channel_id=1, source_target_pairs={{0,2},{1,7},{2,4},{3,1},{4,6},{5,3},{6,0},{7,5},{8,10},{9,15},{10,... | collective-permute-start | bytes 393224 | tf_op jit(solution)/shard_map/ppermute | solution.py:534

commit v15 on v14

--- a/solution.py
+++ b/solution.py
@@ -371,8 +371,8 @@
 
 
 def finish_body(
-    devices, own_hidden_ref, mate_ref, other_ref, halo_ref, own_ref, arrived_ref, hp_ref,
-    hidden_ref, kv_ref, out_ref, head_ref,
+    devices, own_hidden_ref, mate_ref, other_ref, halo_ref, hp_ref, late_ref, late_arrived_ref, early_ref,
+    early_arrived_ref, hidden_ref, kv_ref, out_ref, head_ref,
 ):
     members, nodes, _ = own_hidden_ref.shape
     rim = halo_ref.shape[1]
@@ -383,7 +383,9 @@
         hidden_ref[m] = own_hidden_ref[m] + back
     width = kv_ref.shape[1] // 2
     channels = hp_ref.shape[0]
-    total = (own_ref[...] + arrived_ref[...].astype(F32)) * (1.0 / devices)
+    late = late_ref[...] + late_arrived_ref[...].astype(F32)
+    early = early_ref[...] + early_arrived_ref[...].astype(F32)
+    total = jnp.concatenate([late, early], axis=1) * (1.0 / devices)
     kv_ref[:, width:] = total[:, 0:width]
     kv_ref[:, 0:width] = total[:, width : 2 * width]
     m_rows = total[:, 2 * width : 2 * width + channels]
@@ -527,16 +529,19 @@
         if step == 0:
             from_mate = lax.ppermute(back, "band", mates)
             arrived, from_mate = lax.optimization_barrier((arrived, from_mate))
-        if step == steps - 1:
-            onward = lower([from_mate])[0]
-            arrived, onward = lax.optimization_barrier((arrived, onward))
-            chips_on = [(i, (i + 2 - i % 2 * 4) % n_band) for i in range(n_band)]
-            from_other = lax.ppermute(onward, "band", chips_on)
         groups = [lower(terms) + [new] for terms, new in zip(groups, arrived)]
-    terms = [jnp.concatenate([add_up(*group) for group in groups], axis=1)]
+    late = [add_up(*groups[0])]
+    early = [jnp.concatenate([add_up(*group) for group in groups[1:]], axis=1)]
+    onward = lower([from_mate])[0]
+    early, onward = lax.optimization_barrier((early, onward))
+    from_other = lax.ppermute(onward, "band", [(i, (i + 2 - i % 2 * 4) % n_band) for i in range(n_band)])
     for axis, bit in rest:
-        arrived = swap(add_up(*upper(terms)).astype(BF), axis, bit, count[axis])
-        terms = lower(terms) + [arrived]
+        arrived = swap(add_up(*upper(early)).astype(BF), axis, bit, count[axis])
+        early = lower(early) + [arrived]
+        outgoing = add_up(*upper(late)).astype(BF)
+        arrived, outgoing = lax.optimization_barrier((arrived, outgoing))
+        early[-1] = arrived
+        late = lower(late) + [swap(outgoing, axis, bit, count[axis])]
 
     return call(
         functools.partial(finish_body, devices),
@@ -546,7 +551,10 @@
             sds((rw, width), F32),
             sds((rw, channels), F32),
         ],
-        (own_grad, from_mate, from_other, halo, add_up(*terms[:-1]), terms[-1], hp),
+        (
+            own_grad, from_mate, from_other, halo, hp,
+            add_up(*late[:-1]), late[-1], add_up(*early[:-1]), early[-1],
+        ),
     )
 
 

time: 68.7 us -> 73.1 us (1.064)
  waiting for transfers between devices: 28.3 us -> 32.1 us
    ppermute x13 -> x14, waiting for transfers between devices: 15.1 us -> 23.2 us  [swap(): return lax.ppermute(rows, axis, [(i, i ^ 1 << bit) for i in range(count)])]
    ppermute x1, waiting for transfers between devices: 4.63 us -> 0.22 us  [shards(): lax.ppermute(onward, 'band', [(i, (i + 2 - i % 2 * 4) % n_band) for i in...]
    ppermute x1, starting transfers between devices: 1.21 us -> 2.7 us  [shards(): lax.ppermute(onward, 'band', [(i, (i + 2 - i % 2 * 4) % n_band) for i in...]
    ppermute x13 -> x14, starting transfers between devices: 14.3 us -> 13.4 us  [swap(): return lax.ppermute(rows, axis, [(i, i ^ 1 << bit) for i in range(count)])]
  transfers between devices with their start and end apart: 20 -> 21, of which waited for: 14 -> 16; matrix products, arithmetic and copies ran while one was open for 1% -> 1% of each run, Pallas kernels for 11% -> 10%
where the time goes in v15:
time: 73.1 us; the launch traced here: 72.9 us
  waiting for transfers between devices  32.1 us (44%)
  starting transfers between devices  25.4 us (35%)
  Pallas kernels  13.6 us (19%)
  other arithmetic  0.94 us (1%)
  between operations  0.92 us (1%)
    ppermute x14, waiting for transfers between devices, swap(): return lax.ppermute(rows, axis, [(i, i ^ 1 << bit) for i in range(count)])  23.2 us
    pallas_call x9, Pallas kernels, call(): pl.pallas_call(body, out_shape=out_shape, in_specs=[pl.BlockSpec(memory_s...  13.6 us
    ppermute x14, starting transfers between devices, swap(): return lax.ppermute(rows, axis, [(i, i ^ 1 << bit) for i in range(count)])  13.4 us
    ppermute x3, waiting for transfers between devices, shards(): lax.ppermute(sent, 'member', [(i, i ^ s) for i in range(n_member)])  6.35 us
    ppermute x3, starting transfers between devices, shards(): lax.ppermute(sent, 'member', [(i, i ^ s) for i in range(n_member)])  5.79 us
    ppermute x1, starting transfers between devices, shards(): other = lax.ppermute(for_other, 'band', others)  3.4 us
    ppermute x1, starting transfers between devices, shards(): lax.ppermute(onward, 'band', [(i, (i + 2 - i % 2 * 4) % n_band) for i in...  2.7 us
    ppermute x1, waiting for transfers between devices, shards(): from_mate = lax.ppermute(back, 'band', mates)  1.52 us
  transfers between devices with their start and end apart: 21, of which 16 were waited for; matrix products, arithmetic and copies ran while one was open for 1% of the time, Pallas kernels for 10%

profile of v15, /device:TPU:0, one launch (start us, length us, event | category | flops | bytes accessed | tf_op | source)
XLA Modules:
  0.0 72.9 jit_solution(9013442616398784648)
XLA Ops:
  0.7 1.4 %shard_map.138 = (bf16[2,64,1024]{2,1,0:T(8,128)(2,1)S(1)}, s32[2,32]{1,0:T(2,128)S(1)}, bf16[64,1024]{1,0:T(8,128)(2,1)S(1)}, bf16[64,1024]{1,0:T(8,128)(2,1)S(1)}) custom-call(bf16[2,64,1024]{2,1,0:T(8,128)(2,1)} %hidden_hbm.1, s32[2,32]{1,0:T(2,128)} %halo_hbm.1), custom_call_target="tpu_custom_call" | custom-call | flops 10000000000 | bytes 1 | tf_op jit(solution)/shard_map/pallas_call | solution.py:28
  2.1 3.4 %collective-permute-start = (bf16[64,1024]{1,0:T(8,128)(2,1)S(1)}, bf16[64,1024]{1,0:T(8,128)(2,1)S(1)}, u32[]{:S(2)}, u32[]{:S(2)}) collective-permute-start(bf16[64,1024]{1,0:T(8,128)(2,1)S(1)} %get-tuple-element.53), channel_id=1, source_target_pairs={{0,7},{1,2},{2,1},{3,4},{4,3},{5,6},{6,5},{7,0},{8,15},{9,10},{10,... | collective-permute-start | bytes 393224 | tf_op jit(solution)/shard_map/ppermute | solution.py:439
  5.6 2.4 %shard_map.139 = (bf16[2,64,1024]{2,1,0:T(8,128)(2,1)S(1)}, bf16[8,2,128,256]{3,2,1,0:T(8,128)(2,1)S(1)}, bf16[8,2,128,256]{3,2,1,0:T(8,128)(2,1)S(1)}, f32[2,10...) custom-call(bf16[2,64,1024]{2,1,0:T(8,128)(2,1)S(1)} %get-tuple-elem, ...), custom_call_target="tpu_custom_call" | custom-call | flops 1 | bytes 1 | tf_op jit(solution)/shard_map/pallas_call | solution.py:28
  8.0 0.7 collective-permute-done.other_ref
  8.7 1.7 %shard_map.140 = (bf16[2,64,1024]{2,1,0:T(8,128)(2,1)S(1)}, bf16[8,2,128,256]{3,2,1,0:T(8,128)(2,1)S(1)}, bf16[8,2,128,256]{3,2,1,0:T(8,128)(2,1)S(1)}, bf16[2,1...) custom-call(bf16[64,1024]{1,0:T(8,128)(2,1)S(1)} %collective-permute-done.other_ref, ...), custom_call_target="tpu_custom_call" | custom-call | flops 1 | bytes 1 | tf_op jit(solution)/shard_map/pallas_call | solution.py:28
  10.4 5.2 %collective-permute-start.2 = (bf16[200,256]{1,0:T(8,128)(2,1)S(1)}, bf16[200,256]{1,0:T(8,128)(2,1)S(1)}, u32[]{:S(2)}, u32[]{:S(2)}) collective-permute-start(bf16[200,256]{1,0:T(8,128)(2,1)S(1)} %get-tuple-element.59), channel_id=1, source_target_pairs={{0,24},{8,16},{16,8},{24,0},{1,25},{9,17},{17,9},{25,1},{2,26},{10... | collective-permute-start | bytes 307208 | tf_op jit(solution)/shard_map/ppermute | solution.py:477
  15.6 0.6 collective-permute-start.4
  16.2 0.3 shard_map.141.refs_10_.ext_ref
  16.5 2.1 %collective-permute-done.2.refs_0_ = bf16[200,256]{1,0:T(8,128)(2,1)S(1)} collective-permute-done((bf16[200,256]{1,0:T(8,128)(2,1)S(1)}, bf16[200,256]{1,0:T(8,128)(2,1)S(1)}, u32[]{:S(2)}, u32[]{:S(2)}) %collective-permute-start.2) | collective-permute-done | bytes 102432 | tf_op jit(solution)/shard_map/ppermute | solution.py:477
  18.6 4.2 %collective-permute-done.3.refs_1_ = bf16[200,256]{1,0:T(8,128)(2,1)S(1)} collective-permute-done((bf16[200,256]{1,0:T(8,128)(2,1)S(1)}, bf16[200,256]{1,0:T(8,128)(2,1)S(1)}, u32[]{:S(2)}, u32[]{:S(2)}) %collective-permute-start.3) | collective-permute-done | bytes 102432 | tf_op jit(solution)/shard_map/ppermute | solution.py:477
  22.9 1.9 %shard_map.142 = (bf16[2,128,256]{2,1,0:T(8,128)(2,1)S(1)}, bf16[256,1024]{1,0:T(8,128)(2,1)S(1)}, bf16[512,768]{1,0:T(8,128)(2,1)S(1)}, bf16[512,768]{1,0:T(8,128)(2,1)S(1)}) custom-call(bf16[200,256]{1,0:T(8,128)(2,1)S(1)} %collective-permute-done.2.refs_0_, bf16[200,256]{1,0:T(8,128)(2,1)S(1)} %collective-permute-done.3.refs_1_, ...), custom_call_target="tpu_custom_call" | custom-call | flops 1 | bytes 1 | tf_op jit(solution)/shard_map/pallas_call | solution.py:28
  24.8 1.5 %shard_map.143 = (bf16[256,512]{1,0:T(8,128)(2,1)S(1)}, bf16[512,768]{1,0:T(8,128)(2,1)S(1)}, bf16[512,768]{1,0:T(8,128)(2,1)S(1)}) custom-call(bf16[2,128,256]{2,1,0:T(8,128)(2,1)S(1)} %get-tuple-element.65.grad_ref, bf16[1024,128]{1,0:T(8,128)(2,1)S(1)} %get-tuple-element.66.pt_ref, bf16[2,64,1024]{2,1,0:T(8,128)(2,1)S(1)} %get-tuple-element.67.own_value_ref, ...), custom_call_target="tpu_custom_call" | custom-call | flops 1 | bytes 1 | tf_op jit(solution)/shard_map/pallas_call | solution.py:28
  26.3 0.6 collective-permute-start.6
  26.8 1.9 %shard_map.144 = (bf16[256,512]{1,0:T(8,128)(2,1)S(1)}, bf16[512,768]{1,0:T(8,128)(2,1)S(1)}, bf16[512,768]{1,0:T(8,128)(2,1)S(1)}) custom-call(bf16[2,128,256]{2,1,0:T(8,128)(2,1)S(1)} %get-tuple-element.65.grad_ref, bf16[1024,128]{1,0:T(8,128)(2,1)S(1)} %get-tuple-element.66.pt_ref, bf16[2,64,1024]{2,1,0:T(8,128)(2,1)S(1)} %get-tuple-element.67.own_value_ref, ...), custom_call_target="tpu_custom_call" | custom-call | flops 1 | bytes 1 | tf_op jit(solution)/shard_map/pallas_call | solution.py:28
  28.8 0.1 collective-permute-start.7
  28.9 0.1 add_convert_fusion.2
  29.0 0.1 add_convert_fusion.1
  29.1 2.0 %collective-permute-done.7 = bf16[512,768]{1,0:T(8,128)(2,1)S(1)} collective-permute-done((bf16[512,768]{1,0:T(8,128)(2,1)S(1)}, bf16[512,768]{1,0:T(8,128)(2,1)S(1)}, u32[]{:S(2)}, u32[]{:S(2)}) %collective-permute-start.7) | collective-permute-done | bytes 786464 | tf_op jit(solution)/shard_map/ppermute | solution.py:403
  31.1 0.1 add_convert_fusion
  31.2 0.5 collective-permute-start.10
  31.8 1.7 %collective-permute-start.8 = (bf16[256,768]{1,0:T(8,128)(2,1)S(1)}, bf16[256,768]{1,0:T(8,128)(2,1)S(1)}, u32[]{:S(2)}, u32[]{:S(2)}) collective-permute-start(bf16[256,768]{1,0:T(8,128)(2,1)S(1)} %add_convert_fusion.2), channel_id=1, source_target_pairs={{0,2},{1,3},{2,0},{3,1},{4,6},{5,7},{6,4},{7,5},{8,10},{9,11},{10,... | collective-permute-start | bytes 1179656 | tf_op jit(solution)/shard_map/ppermute | solution.py:403
  33.4 1.8 %collective-permute-start.9 = (bf16[256,768]{1,0:T(8,128)(2,1)S(1)}, bf16[256,768]{1,0:T(8,128)(2,1)S(1)}, u32[]{:S(2)}, u32[]{:S(2)}) collective-permute-start(bf16[256,768]{1,0:T(8,128)(2,1)S(1)} %add_convert_fusion.1), channel_id=1, source_target_pairs={{0,4},{1,5},{2,6},{3,7},{4,0},{5,1},{6,2},{7,3},{8,12},{9,13},{10,... | collective-permute-start | bytes 1179656 | tf_op jit(solution)/shard_map/ppermute | solution.py:403
  35.3 1.3 %shard_map.145 = (f32[2,64,1024]{2,1,0:T(8,128)S(1)}, bf16[128,1024]{1,0:T(8,128)(2,1)S(1)}) custom-call(bf16[256,512]{1,0:T(8,128)(2,1)S(1)} %get-tuple-element.72.first_ref, bf16[256,512]{1,0:T(8,128)(2,1)S(1)} %get-tuple-element.87.last_ref, bf16[256,1024]{1,0:T(8,128)(2,1)S(1)} %get-tuple-element.71.ngv_ref, bf16[1024,2048]{1,0:T(8,128)(2,1)S(1)} %copy-done), custom_call_target="tpu_custom_call" | custom-call | flops 1 | bytes 1 | tf_op jit(solution)/shard_map/pallas_call | solution.py:28
  36.7 1.5 %collective-permute-done.11.mate_ref = bf16[128,1024]{1,0:T(8,128)(2,1)S(1)} collective-permute-done((bf16[128,1024]{1,0:T(8,128)(2,1)S(1)}, bf16[128,1024]{1,0:T(8,128)(2,1)S(1)}, u32[]{:S(2)}, u32[]{:S(2)}) %collective-permute-start.11) | collective-permute-done | bytes 262176 | tf_op jit(solution)/shard_map/ppermute | solution.py:530
  38.2 4.3 %collective-permute-done.10 = bf16[256,768]{1,0:T(8,128)(2,1)S(1)} collective-permute-done((bf16[256,768]{1,0:T(8,128)(2,1)S(1)}, bf16[256,768]{1,0:T(8,128)(2,1)S(1)}, u32[]{:S(2)}, u32[]{:S(2)}) %collective-permute-start.10) | collective-permute-done | bytes 393248 | tf_op jit(solution)/shard_map/ppermute | solution.py:403
  42.5 0.3 collective-permute-done.8
  42.8 1.5 %collective-permute-done.9 = bf16[256,768]{1,0:T(8,128)(2,1)S(1)} collective-permute-done((bf16[256,768]{1,0:T(8,128)(2,1)S(1)}, bf16[256,768]{1,0:T(8,128)(2,1)S(1)}, u32[]{:S(2)}, u32[]{:S(2)}) %collective-permute-start.9) | collective-permute-done | bytes 393248 | tf_op jit(solution)/shard_map/ppermute | solution.py:403
  44.3 0.1 add_convert_fusion.3
  44.3 1.7 %collective-permute-start.17 = (bf16[128,768]{1,0:T(8,128)(2,1)S(1)}, bf16[128,768]{1,0:T(8,128)(2,1)S(1)}, u32[]{:S(2)}, u32[]{:S(2)}) collective-permute-start(bf16[128,768]{1,0:T(8,128)(2,1)S(1)} %add_convert_fusion.3), channel_id=1, source_target_pairs={{0,4},{1,5},{2,6},{3,7},{4,0},{5,1},{6,2},{7,3},{8,12},{9,13},{10,... | collective-permute-start | bytes 589832 | tf_op jit(solution)/shard_map/ppermute | solution.py:403
  46.0 0.1 add_convert_fusion.5
  46.1 1.7 %collective-permute-start.12 = (bf16[128,768]{1,0:T(8,128)(2,1)S(1)}, bf16[128,768]{1,0:T(8,128)(2,1)S(1)}, u32[]{:S(2)}, u32[]{:S(2)}) collective-permute-start(bf16[128,768]{1,0:T(8,128)(2,1)S(1)} %add_convert_fusion.5), channel_id=1, source_target_pairs={{0,8},{8,0},{16,24},{24,16},{1,9},{9,1},{17,25},{25,17},{2,10},{10... | collective-permute-start | bytes 589832 | tf_op jit(solution)/shard_map/ppermute | solution.py:403
  47.8 0.1 add_convert_fusion.4
  47.9 0.9 %collective-permute-start.14 = (bf16[128,768]{1,0:T(8,128)(2,1)S(1)}, bf16[128,768]{1,0:T(8,128)(2,1)S(1)}, u32[]{:S(2)}, u32[]{:S(2)}) collective-permute-start(bf16[128,768]{1,0:T(8,128)(2,1)S(1)} %add_convert_fusion.4), channel_id=1, source_target_pairs={{0,2},{1,3},{2,0},{3,1},{4,6},{5,7},{6,4},{7,5},{8,10},{9,11},{10,... | collective-permute-start | bytes 589832 | tf_op jit(solution)/shard_map/ppermute | solution.py:403
  48.8 1.4 %collective-permute-done.17 = bf16[128,768]{1,0:T(8,128)(2,1)S(1)} collective-permute-done((bf16[128,768]{1,0:T(8,128)(2,1)S(1)}, bf16[128,768]{1,0:T(8,128)(2,1)S(1)}, u32[]{:S(2)}, u32[]{:S(2)}) %collective-permute-start.17) | collective-permute-done | bytes 196640 | tf_op jit(solution)/shard_map/ppermute | solution.py:403
  50.2 1.7 %collective-permute-start.18 = (bf16[64,768]{1,0:T(8,128)(2,1)S(1)}, bf16[64,768]{1,0:T(8,128)(2,1)S(1)}, u32[]{:S(2)}, u32[]{:S(2)}) collective-permute-start(bf16[64,768]{1,0:T(8,128)(2,1)S(1)} %add_convert_fusion.6), channel_id=1, source_target_pairs={{0,8},{8,0},{16,24},{24,16},{1,9},{9,1},{17,25},{25,17},{2,10},{10... | collective-permute-start | bytes 294920 | tf_op jit(solution)/shard_map/ppermute | solution.py:403
  51.9 1.0 %collective-permute-done.12 = bf16[128,768]{1,0:T(8,128)(2,1)S(1)} collective-permute-done((bf16[128,768]{1,0:T(8,128)(2,1)S(1)}, bf16[128,768]{1,0:T(8,128)(2,1)S(1)}, u32[]{:S(2)}, u32[]{:S(2)}) %collective-permute-start.12) | collective-permute-done | bytes 196640 | tf_op jit(solution)/shard_map/ppermute | solution.py:403
  52.9 0.7 %collective-permute-start.13 = (bf16[64,768]{1,0:T(8,128)(2,1)S(1)}, bf16[64,768]{1,0:T(8,128)(2,1)S(1)}, u32[]{:S(2)}, u32[]{:S(2)}) collective-permute-start(bf16[64,768]{1,0:T(8,128)(2,1)S(1)} %add_convert_fusion.8), channel_id=1, source_target_pairs={{0,2},{1,3},{2,0},{3,1},{4,6},{5,7},{6,4},{7,5},{8,10},{9,11},{10,... | collective-permute-start | bytes 294920 | tf_op jit(solution)/shard_map/ppermute | solution.py:403
  53.7 1.0 %collective-permute-done.14 = bf16[128,768]{1,0:T(8,128)(2,1)S(1)} collective-permute-done((bf16[128,768]{1,0:T(8,128)(2,1)S(1)}, bf16[128,768]{1,0:T(8,128)(2,1)S(1)}, u32[]{:S(2)}, u32[]{:S(2)}) %collective-permute-start.14) | collective-permute-done | bytes 196640 | tf_op jit(solution)/shard_map/ppermute | solution.py:403
  54.7 0.1 collective-permute-start.15
  54.8 2.8 %collective-permute-done.13 = bf16[64,768]{1,0:T(8,128)(2,1)S(1)} collective-permute-done((bf16[64,768]{1,0:T(8,128)(2,1)S(1)}, bf16[64,768]{1,0:T(8,128)(2,1)S(1)}, u32[]{:S(2)}, u32[]{:S(2)}) %collective-permute-start.13) | collective-permute-done | bytes 98336 | tf_op jit(solution)/shard_map/ppermute | solution.py:403
  57.7 1.7 %collective-permute-done.15 = bf16[64,768]{1,0:T(8,128)(2,1)S(1)} collective-permute-done((bf16[64,768]{1,0:T(8,128)(2,1)S(1)}, bf16[64,768]{1,0:T(8,128)(2,1)S(1)}, u32[]{:S(2)}, u32[]{:S(2)}) %collective-permute-start.15) | collective-permute-done | bytes 98336 | tf_op jit(solution)/shard_map/ppermute | solution.py:403
  59.5 1.8 %collective-permute-start.19 = (bf16[32,1536]{1,0:T(8,128)(2,1)S(1)}, bf16[32,1536]{1,0:T(8,128)(2,1)S(1)}, u32[]{:S(2)}, u32[]{:S(2)}) collective-permute-start(bf16[32,1536]{1,0:T(8,128)(2,1)S(1)} %slice.277), channel_id=1, source_target_pairs={{0,16},{8,24},{16,0},{24,8},{1,17},{9,25},{17,1},{25,9},{2,18},{10... | collective-permute-start | bytes 294920 | tf_op jit(solution)/shard_map/ppermute | solution.py:403
  61.3 2.7 %collective-permute-start.16 = (bf16[64,1024]{1,0:T(8,128)(2,1)S(1)}, bf16[64,1024]{1,0:T(8,128)(2,1)S(1)}, u32[]{:S(2)}, u32[]{:S(2)}) collective-permute-start(bf16[64,1024]{1,0:T(8,128)(2,1)S(1)} %slice.207), channel_id=1, source_target_pairs={{0,2},{1,7},{2,4},{3,1},{4,6},{5,3},{6,0},{7,5},{8,10},{9,15},{10,... | collective-permute-start | bytes 393224 | tf_op jit(solution)/shard_map/ppermute | solution.py:537
  64.1 2.7 %collective-permute-done.19.early_arrived_ref = bf16[32,1536]{1,0:T(8,128)(2,1)S(1)} collective-permute-done((bf16[32,1536]{1,0:T(8,128)(2,1)S(1)}, bf16[32,1536]{1,0:T(8,128)(2,1)S(1)}, u32[]{:S(2)}, u32[]{:S(2)}) %collective-permute-start.19) | collective-permute-done | bytes 98336 | tf_op jit(solution)/shard_map/ppermute | solution.py:403
  66.7 0.2 collective-permute-start.20
  66.9 0.2 collective-permute-done.16.other_ref
  67.1 4.6 %collective-permute-done.20.late_arrived_ref = bf16[32,768]{1,0:T(8,128)(2,1)S(1)} collective-permute-done((bf16[32,768]{1,0:T(8,128)(2,1)S(1)}, bf16[32,768]{1,0:T(8,128)(2,1)S(1)}, u32[]{:S(2)}, u32[]{:S(2)}) %collective-permute-start.20) | collective-permute-done | bytes 49184 | tf_op jit(solution)/shard_map/ppermute | solution.py:403
  71.7 1.2 %shard_map.146 = (f32[2,64,1024]{2,1,0:T(8,128)}, f32[32,2048]{1,0:T(8,128)}, f32[32,1024]{1,0:T(8,128)}, f32[32,100]{1,0:T(8,128)}) custom-call(f32[2,64,1024]{2,1,0:T(8,128)S(1)} %get-tuple-element.88.own_hidden_ref, bf16[128,1024]{1,0:T(8,128)(2,1)S(1)} %collective-permute-done.11.mate_ref, bf16[64,1024]{1,0:T(8,128)(2,1)S(1)} %collective-permute-done.16.other_ref, ...), custom_call_target="tpu_custom_call" | custom-call | flops 1 | bytes 1 | tf_op jit(solution)/shard_map/pallas_call | solution.py:28
  (39 shorter events, 0.6 us)
Async XLA Ops:
  0.6 4.9 %copy-start.3 = (bf16[1024,100]{0,1:T(8,128)(2,1)S(1)}, bf16[1024,100]{0,1:T(8,128)(2,1)}, u32[]{:S(2)}) copy-start(bf16[1024,100]{0,1:T(8,128)(2,1)} %param.15) | copy-start | bytes 614404
  0.6 4.9 %copy-start.8 = (f32[100]{0:T(128)S(1)}, f32[100]{0:T(128)}, u32[]{:S(2)}) copy-start(f32[100]{0:T(128)} %param.19) | copy-start | bytes 1204
  0.7 4.9 %copy-start.7 = (f32[256]{0:T(256)S(1)}, f32[256]{0:T(256)}, u32[]{:S(2)}) copy-start(f32[256]{0:T(256)} %param.18) | copy-start | bytes 3076
  0.7 4.9 %copy-start.2 = (bf16[256,1024]{1,0:T(8,128)(2,1)S(1)}, bf16[256,1024]{1,0:T(8,128)(2,1)}, u32[]{:S(2)}) copy-start(bf16[256,1024]{1,0:T(8,128)(2,1)} %q_ref.5) | copy-start | bytes 1572868
  0.7 4.9 %copy-start.1 = (bf16[1024,1024]{1,0:T(8,128)(2,1)S(1)}, bf16[1024,1024]{1,0:T(8,128)(2,1)}, u32[]{:S(2)}) copy-start(bf16[1024,1024]{1,0:T(8,128)(2,1)} %wo_ref.3) | copy-start | bytes 6291460
  0.7 4.9 %copy-start.5 = (f32[100,256]{1,0:T(8,128)S(1)}, f32[100,256]{1,0:T(8,128)}, u32[]{:S(2)}) copy-start(f32[100,256]{1,0:T(8,128)} %init_ref.1) | copy-start | bytes 307204
  0.7 4.9 %copy-start.6 = (s32[3,256]{1,0:T(4,128)S(1)}, s32[3,256]{1,0:T(4,128)}, u32[]{:S(2)}) copy-start(s32[3,256]{1,0:T(4,128)} %src_ref.3) | copy-start | bytes 9220
  0.7 4.9 %copy-start = (bf16[1024,2048]{1,0:T(8,128)(2,1)S(1)}, bf16[1024,2048]{1,0:T(8,128)(2,1)}, u32[]{:S(2)}) copy-start(bf16[1024,2048]{1,0:T(8,128)(2,1)} %kvw_ref.5) | copy-start | bytes 12582916
  2.1 6.6 %collective-permute-start = (bf16[64,1024]{1,0:T(8,128)(2,1)S(1)}, bf16[64,1024]{1,0:T(8,128)(2,1)S(1)}, u32[]{:S(2)}, u32[]{:S(2)}) collective-permute-start(bf16[64,1024]{1,0:T(8,128)(2,1)S(1)} %get-tuple-element.53), channel_id=1, source_target_pairs={{0,7},{1,2},{2,1},{3,4},{4,3},{5,6},{6,5},{7,0},{8,15},{9,10},{10,... | collective-permute-start | bytes 393224 | tf_op jit(solution)/shard_map/ppermute | solution.py:439
  5.5 3.2 %collective-permute-start.1 = (bf16[64,1024]{1,0:T(8,128)(2,1)S(1)}, bf16[64,1024]{1,0:T(8,128)(2,1)S(1)}, u32[]{:S(2)}, u32[]{:S(2)}) collective-permute-start(bf16[64,1024]{1,0:T(8,128)(2,1)S(1)} %get-tuple-element.54), channel_id=1, source_target_pairs={{0,1},{1,0},{2,3},{3,2},{4,5},{5,4},{6,7},{7,6},{8,9},{9,8},{10,11... | collective-permute-start | bytes 393224 | tf_op jit(solution)/shard_map/ppermute | solution.py:440
  8.7 14.1 %copy-start.4 = (f32[100,256]{1,0:T(8,128)S(1)}, f32[100,256]{1,0:T(8,128)}, u32[]{:S(2)}) copy-start(f32[100,256]{1,0:T(8,128)} %refs_5_.1) | copy-start | bytes 307204
  10.4 8.2 %collective-permute-start.2 = (bf16[200,256]{1,0:T(8,128)(2,1)S(1)}, bf16[200,256]{1,0:T(8,128)(2,1)S(1)}, u32[]{:S(2)}, u32[]{:S(2)}) collective-permute-start(bf16[200,256]{1,0:T(8,128)(2,1)S(1)} %get-tuple-element.59), channel_id=1, source_target_pairs={{0,24},{8,16},{16,8},{24,0},{1,25},{9,17},{17,9},{25,1},{2,26},{10... | collective-permute-start | bytes 307208 | tf_op jit(solution)/shard_map/ppermute | solution.py:477
  15.6 7.3 %collective-permute-start.3 = (bf16[200,256]{1,0:T(8,128)(2,1)S(1)}, bf16[200,256]{1,0:T(8,128)(2,1)S(1)}, u32[]{:S(2)}, u32[]{:S(2)}) collective-permute-start(bf16[200,256]{1,0:T(8,128)(2,1)S(1)} %get-tuple-element.59), channel_id=1, source_target_pairs={{0,16},{8,24},{16,0},{24,8},{1,17},{9,25},{17,1},{25,9},{2,18},{10... | collective-permute-start | bytes 307208 | tf_op jit(solution)/shard_map/ppermute | solution.py:477
  15.6 7.3 %collective-permute-start.4 = (bf16[200,256]{1,0:T(8,128)(2,1)S(1)}, bf16[200,256]{1,0:T(8,128)(2,1)S(1)}, u32[]{:S(2)}, u32[]{:S(2)}) collective-permute-start(bf16[200,256]{1,0:T(8,128)(2,1)S(1)} %get-tuple-element.59), channel_id=1, source_target_pairs={{0,8},{8,0},{16,24},{24,16},{1,9},{9,1},{17,25},{25,17},{2,10},{10... | collective-permute-start | bytes 307208 | tf_op jit(solution)/shard_map/ppermute | solution.py:477
  24.7 4.1 %collective-permute-start.5 = (bf16[512,768]{1,0:T(8,128)(2,1)S(1)}, bf16[512,768]{1,0:T(8,128)(2,1)S(1)}, u32[]{:S(2)}, u32[]{:S(2)}) collective-permute-start(bf16[512,768]{1,0:T(8,128)(2,1)S(1)} %get-tuple-element.74), channel_id=1, source_target_pairs={{0,1},{1,0},{2,3},{3,2},{4,5},{5,4},{6,7},{7,6},{8,9},{9,8},{10,11... | collective-permute-start | bytes 2359304 | tf_op jit(solution)/shard_map/ppermute | solution.py:403
  26.3 2.7 %collective-permute-start.6 = (bf16[512,768]{1,0:T(8,128)(2,1)S(1)}, bf16[512,768]{1,0:T(8,128)(2,1)S(1)}, u32[]{:S(2)}, u32[]{:S(2)}) collective-permute-start(bf16[512,768]{1,0:T(8,128)(2,1)S(1)} %get-tuple-element.76), channel_id=1, source_target_pairs={{0,1},{1,0},{2,3},{3,2},{4,5},{5,4},{6,7},{7,6},{8,9},{9,8},{10,11... | collective-permute-start | bytes 2359304 | tf_op jit(solution)/shard_map/ppermute | solution.py:403
  28.8 2.4 %collective-permute-start.7 = (bf16[512,768]{1,0:T(8,128)(2,1)S(1)}, bf16[512,768]{1,0:T(8,128)(2,1)S(1)}, u32[]{:S(2)}, u32[]{:S(2)}) collective-permute-start(bf16[512,768]{1,0:T(8,128)(2,1)S(1)} %get-tuple-element.82), channel_id=1, source_target_pairs={{0,1},{1,0},{2,3},{3,2},{4,5},{5,4},{6,7},{7,6},{8,9},{9,8},{10,11... | collective-permute-start | bytes 2359304 | tf_op jit(solution)/shard_map/ppermute | solution.py:403
  31.2 11.2 %collective-permute-start.10 = (bf16[256,768]{1,0:T(8,128)(2,1)S(1)}, bf16[256,768]{1,0:T(8,128)(2,1)S(1)}, u32[]{:S(2)}, u32[]{:S(2)}) collective-permute-start(bf16[256,768]{1,0:T(8,128)(2,1)S(1)} %add_convert_fusion), channel_id=1, source_target_pairs={{0,8},{8,0},{16,24},{24,16},{1,9},{9,1},{17,25},{25,17},{2,10},{10... | collective-permute-start | bytes 1179656 | tf_op jit(solution)/shard_map/ppermute | solution.py:403
  31.8 11.0 %collective-permute-start.8 = (bf16[256,768]{1,0:T(8,128)(2,1)S(1)}, bf16[256,768]{1,0:T(8,128)(2,1)S(1)}, u32[]{:S(2)}, u32[]{:S(2)}) collective-permute-start(bf16[256,768]{1,0:T(8,128)(2,1)S(1)} %add_convert_fusion.2), channel_id=1, source_target_pairs={{0,2},{1,3},{2,0},{3,1},{4,6},{5,7},{6,4},{7,5},{8,10},{9,11},{10,... | collective-permute-start | bytes 1179656 | tf_op jit(solution)/shard_map/ppermute | solution.py:403
  33.4 10.8 %collective-permute-start.9 = (bf16[256,768]{1,0:T(8,128)(2,1)S(1)}, bf16[256,768]{1,0:T(8,128)(2,1)S(1)}, u32[]{:S(2)}, u32[]{:S(2)}) collective-permute-start(bf16[256,768]{1,0:T(8,128)(2,1)S(1)} %add_convert_fusion.1), channel_id=1, source_target_pairs={{0,4},{1,5},{2,6},{3,7},{4,0},{5,1},{6,2},{7,3},{8,12},{9,13},{10,... | collective-permute-start | bytes 1179656 | tf_op jit(solution)/shard_map/ppermute | solution.py:403
  36.6 1.6 %collective-permute-start.11 = (bf16[128,1024]{1,0:T(8,128)(2,1)S(1)}, bf16[128,1024]{1,0:T(8,128)(2,1)S(1)}, u32[]{:S(2)}, u32[]{:S(2)}) collective-permute-start(bf16[128,1024]{1,0:T(8,128)(2,1)S(1)} %get-tuple-element.92), channel_id=1, source_target_pairs={{0,1},{1,0},{2,3},{3,2},{4,5},{5,4},{6,7},{7,6},{8,9},{9,8},{10,11... | collective-permute-start | bytes 786440 | tf_op jit(solution)/shard_map/ppermute | solution.py:530
  44.3 5.8 %collective-permute-start.17 = (bf16[128,768]{1,0:T(8,128)(2,1)S(1)}, bf16[128,768]{1,0:T(8,128)(2,1)S(1)}, u32[]{:S(2)}, u32[]{:S(2)}) collective-permute-start(bf16[128,768]{1,0:T(8,128)(2,1)S(1)} %add_convert_fusion.3), channel_id=1, source_target_pairs={{0,4},{1,5},{2,6},{3,7},{4,0},{5,1},{6,2},{7,3},{8,12},{9,13},{10,... | collective-permute-start | bytes 589832 | tf_op jit(solution)/shard_map/ppermute | solution.py:403
  46.1 6.8 %collective-permute-start.12 = (bf16[128,768]{1,0:T(8,128)(2,1)S(1)}, bf16[128,768]{1,0:T(8,128)(2,1)S(1)}, u32[]{:S(2)}, u32[]{:S(2)}) collective-permute-start(bf16[128,768]{1,0:T(8,128)(2,1)S(1)} %add_convert_fusion.5), channel_id=1, source_target_pairs={{0,8},{8,0},{16,24},{24,16},{1,9},{9,1},{17,25},{25,17},{2,10},{10... | collective-permute-start | bytes 589832 | tf_op jit(solution)/shard_map/ppermute | solution.py:403
  47.9 6.8 %collective-permute-start.14 = (bf16[128,768]{1,0:T(8,128)(2,1)S(1)}, bf16[128,768]{1,0:T(8,128)(2,1)S(1)}, u32[]{:S(2)}, u32[]{:S(2)}) collective-permute-start(bf16[128,768]{1,0:T(8,128)(2,1)S(1)} %add_convert_fusion.4), channel_id=1, source_target_pairs={{0,2},{1,3},{2,0},{3,1},{4,6},{5,7},{6,4},{7,5},{8,10},{9,11},{10,... | collective-permute-start | bytes 589832 | tf_op jit(solution)/shard_map/ppermute | solution.py:403
  50.2 13.8 %collective-permute-start.18 = (bf16[64,768]{1,0:T(8,128)(2,1)S(1)}, bf16[64,768]{1,0:T(8,128)(2,1)S(1)}, u32[]{:S(2)}, u32[]{:S(2)}) collective-permute-start(bf16[64,768]{1,0:T(8,128)(2,1)S(1)} %add_convert_fusion.6), channel_id=1, source_target_pairs={{0,8},{8,0},{16,24},{24,16},{1,9},{9,1},{17,25},{25,17},{2,10},{10... | collective-permute-start | bytes 294920 | tf_op jit(solution)/shard_map/ppermute | solution.py:403
  52.9 4.7 %collective-permute-start.13 = (bf16[64,768]{1,0:T(8,128)(2,1)S(1)}, bf16[64,768]{1,0:T(8,128)(2,1)S(1)}, u32[]{:S(2)}, u32[]{:S(2)}) collective-permute-start(bf16[64,768]{1,0:T(8,128)(2,1)S(1)} %add_convert_fusion.8), channel_id=1, source_target_pairs={{0,2},{1,3},{2,0},{3,1},{4,6},{5,7},{6,4},{7,5},{8,10},{9,11},{10,... | collective-permute-start | bytes 294920 | tf_op jit(solution)/shard_map/ppermute | solution.py:403
  54.7 4.7 %collective-permute-start.15 = (bf16[64,768]{1,0:T(8,128)(2,1)S(1)}, bf16[64,768]{1,0:T(8,128)(2,1)S(1)}, u32[]{:S(2)}, u32[]{:S(2)}) collective-permute-start(bf16[64,768]{1,0:T(8,128)(2,1)S(1)} %add_convert_fusion.7), channel_id=1, source_target_pairs={{0,4},{1,5},{2,6},{3,7},{4,0},{5,1},{6,2},{7,3},{8,12},{9,13},{10,... | collective-permute-start | bytes 294920 | tf_op jit(solution)/shard_map/ppermute | solution.py:403
  59.5 7.2 %collective-permute-start.19 = (bf16[32,1536]{1,0:T(8,128)(2,1)S(1)}, bf16[32,1536]{1,0:T(8,128)(2,1)S(1)}, u32[]{:S(2)}, u32[]{:S(2)}) collective-permute-start(bf16[32,1536]{1,0:T(8,128)(2,1)S(1)} %slice.277), channel_id=1, source_target_pairs={{0,16},{8,24},{16,0},{24,8},{1,17},{9,25},{17,1},{25,9},{2,18},{10... | collective-permute-start | bytes 294920 | tf_op jit(solution)/shard_map/ppermute | solution.py:403
  61.3 5.9 %collective-permute-start.16 = (bf16[64,1024]{1,0:T(8,128)(2,1)S(1)}, bf16[64,1024]{1,0:T(8,128)(2,1)S(1)}, u32[]{:S(2)}, u32[]{:S(2)}) collective-permute-start(bf16[64,1024]{1,0:T(8,128)(2,1)S(1)} %slice.207), channel_id=1, source_target_pairs={{0,2},{1,7},{2,4},{3,1},{4,6},{5,3},{6,0},{7,5},{8,10},{9,15},{10,... | collective-permute-start | bytes 393224 | tf_op jit(solution)/shard_map/ppermute | solution.py:537
  66.7 5.0 %collective-permute-start.20 = (bf16[32,768]{1,0:T(8,128)(2,1)S(1)}, bf16[32,768]{1,0:T(8,128)(2,1)S(1)}, u32[]{:S(2)}, u32[]{:S(2)}) collective-permute-start(bf16[32,768]{1,0:T(8,128)(2,1)S(1)} %slice.278), channel_id=1, source_target_pairs={{0,16},{8,24},{16,0},{24,8},{1,17},{9,25},{17,1},{25,9},{2,18},{10... | collective-permute-start | bytes 147464 | tf_op jit(solution)/shard_map/ppermute | solution.py:403

commit v16 on v14

--- a/solution.py
+++ b/solution.py
@@ -514,7 +514,7 @@
         outgoing = []
         for i in range(GROUPS):
             outgoing.append(add_up(*upper(groups[i])).astype(BF))
-            if step == 0 and i + 1 < GROUPS:
+            if step <= 1 and i + 1 < GROUPS:
                 outgoing[i], groups[i + 1] = lax.optimization_barrier((outgoing[i], groups[i + 1]))
         if step == 0:
             outgoing, ng_last = lax.optimization_barrier((outgoing, ng_last))
@@ -526,7 +526,7 @@
         arrived = [swap(out, *turn[step], count[turn[step][0]]) for out, turn in zip(outgoing, turns)]
         if step == 0:
             from_mate = lax.ppermute(back, "band", mates)
-            arrived, from_mate = lax.optimization_barrier((arrived, from_mate))
+            arrived[-1], from_mate = lax.optimization_barrier((arrived[-1], from_mate))
         if step == steps - 1:
             onward = lower([from_mate])[0]
             arrived, onward = lax.optimization_barrier((arrived, onward))

time: 68.7 us -> 69.3 us (level)
  waiting for transfers between devices: 28.3 us -> 30.2 us
  starting transfers between devices: 24.7 us -> 23.3 us
    ppermute x13, waiting for transfers between devices: 15.1 us -> 18.6 us  [swap(): return lax.ppermute(rows, axis, [(i, i ^ 1 << bit) for i in range(count)])]
    ppermute x1, waiting for transfers between devices: 1.52 us -> 0.01 us  [shards(): from_mate = lax.ppermute(back, 'band', mates)]
    ppermute x13, starting transfers between devices: 14.3 us -> 12.8 us  [swap(): return lax.ppermute(rows, axis, [(i, i ^ 1 << bit) for i in range(count)])]
where the time goes in v16:
time: 69.3 us; the launch traced here: 69.1 us
  waiting for transfers between devices  30.2 us (44%)
  starting transfers between devices  23.3 us (34%)
  Pallas kernels  13.6 us (20%)
  between operations  0.94 us (1%)
  other arithmetic  0.92 us (1%)
    ppermute x13, waiting for transfers between devices, swap(): return lax.ppermute(rows, axis, [(i, i ^ 1 << bit) for i in range(count)])  18.6 us
    pallas_call x9, Pallas kernels, call(): pl.pallas_call(body, out_shape=out_shape, in_specs=[pl.BlockSpec(memory_s...  13.6 us
    ppermute x13, starting transfers between devices, swap(): return lax.ppermute(rows, axis, [(i, i ^ 1 << bit) for i in range(count)])  12.8 us
    ppermute x3, waiting for transfers between devices, shards(): lax.ppermute(sent, 'member', [(i, i ^ s) for i in range(n_member)])  6.35 us
    ppermute x3, starting transfers between devices, shards(): lax.ppermute(sent, 'member', [(i, i ^ s) for i in range(n_member)])  5.79 us
    ppermute x1, waiting for transfers between devices, shards(): from_other = lax.ppermute(onward, 'band', chips_on)  4.57 us
    ppermute x1, starting transfers between devices, shards(): other = lax.ppermute(for_other, 'band', others)  3.4 us
  transfers between devices with their start and end apart: 20, of which 14 were waited for; matrix products, arithmetic and copies ran while one was open for 1% of the time, Pallas kernels for 11%

profile of v16, /device:TPU:0, one launch (start us, length us, event | category | flops | bytes accessed | tf_op | source)
XLA Modules:
  0.0 69.1 jit_solution(8650769217106425171)
XLA Ops:
  0.7 1.4 %shard_map.138 = (bf16[2,64,1024]{2,1,0:T(8,128)(2,1)S(1)}, s32[2,32]{1,0:T(2,128)S(1)}, bf16[64,1024]{1,0:T(8,128)(2,1)S(1)}, bf16[64,1024]{1,0:T(8,128)(2,1)S(1)}) custom-call(bf16[2,64,1024]{2,1,0:T(8,128)(2,1)} %hidden_hbm.1, s32[2,32]{1,0:T(2,128)} %halo_hbm.1), custom_call_target="tpu_custom_call" | custom-call | flops 10000000000 | bytes 1 | tf_op jit(solution)/shard_map/pallas_call | solution.py:28
  2.1 3.4 %collective-permute-start = (bf16[64,1024]{1,0:T(8,128)(2,1)S(1)}, bf16[64,1024]{1,0:T(8,128)(2,1)S(1)}, u32[]{:S(2)}, u32[]{:S(2)}) collective-permute-start(bf16[64,1024]{1,0:T(8,128)(2,1)S(1)} %get-tuple-element.59), channel_id=1, source_target_pairs={{0,7},{1,2},{2,1},{3,4},{4,3},{5,6},{6,5},{7,0},{8,15},{9,10},{10,... | collective-permute-start | bytes 393224 | tf_op jit(solution)/shard_map/ppermute | solution.py:437
  5.6 2.4 %shard_map.139 = (bf16[2,64,1024]{2,1,0:T(8,128)(2,1)S(1)}, bf16[8,2,128,256]{3,2,1,0:T(8,128)(2,1)S(1)}, bf16[8,2,128,256]{3,2,1,0:T(8,128)(2,1)S(1)}, f32[2,10...) custom-call(bf16[2,64,1024]{2,1,0:T(8,128)(2,1)S(1)} %get-tuple-elem, ...), custom_call_target="tpu_custom_call" | custom-call | flops 1 | bytes 1 | tf_op jit(solution)/shard_map/pallas_call | solution.py:28
  8.0 0.7 %collective-permute-done.other_ref = bf16[64,1024]{1,0:T(8,128)(2,1)S(1)} collective-permute-done((bf16[64,1024]{1,0:T(8,128)(2,1)S(1)}, bf16[64,1024]{1,0:T(8,128)(2,1)S(1)}, u32[]{:S(2)}, u32[]{:S(2)}) %collective-permute-start) | collective-permute-done | bytes 131104 | tf_op jit(solution)/shard_map/ppermute | solution.py:437
  8.7 1.7 %shard_map.140 = (bf16[2,64,1024]{2,1,0:T(8,128)(2,1)S(1)}, bf16[8,2,128,256]{3,2,1,0:T(8,128)(2,1)S(1)}, bf16[8,2,128,256]{3,2,1,0:T(8,128)(2,1)S(1)}, bf16[2,1...) custom-call(bf16[64,1024]{1,0:T(8,128)(2,1)S(1)} %collective-permute-done.other_ref, ...), custom_call_target="tpu_custom_call" | custom-call | flops 1 | bytes 1 | tf_op jit(solution)/shard_map/pallas_call | solution.py:28
  10.4 5.2 %collective-permute-start.2 = (bf16[200,256]{1,0:T(8,128)(2,1)S(1)}, bf16[200,256]{1,0:T(8,128)(2,1)S(1)}, u32[]{:S(2)}, u32[]{:S(2)}) collective-permute-start(bf16[200,256]{1,0:T(8,128)(2,1)S(1)} %get-tuple-element.65), channel_id=1, source_target_pairs={{0,24},{8,16},{16,8},{24,0},{1,25},{9,17},{17,9},{25,1},{2,26},{10... | collective-permute-start | bytes 307208 | tf_op jit(solution)/shard_map/ppermute | solution.py:475
  15.6 0.6 collective-permute-start.4
  16.2 0.3 shard_map.141.refs_10_.ext_ref
  16.5 2.1 %collective-permute-done.2.refs_0_ = bf16[200,256]{1,0:T(8,128)(2,1)S(1)} collective-permute-done((bf16[200,256]{1,0:T(8,128)(2,1)S(1)}, bf16[200,256]{1,0:T(8,128)(2,1)S(1)}, u32[]{:S(2)}, u32[]{:S(2)}) %collective-permute-start.2) | collective-permute-done | bytes 102432 | tf_op jit(solution)/shard_map/ppermute | solution.py:475
  18.6 4.2 %collective-permute-done.3.refs_1_ = bf16[200,256]{1,0:T(8,128)(2,1)S(1)} collective-permute-done((bf16[200,256]{1,0:T(8,128)(2,1)S(1)}, bf16[200,256]{1,0:T(8,128)(2,1)S(1)}, u32[]{:S(2)}, u32[]{:S(2)}) %collective-permute-start.3) | collective-permute-done | bytes 102432 | tf_op jit(solution)/shard_map/ppermute | solution.py:475
  22.9 1.9 %shard_map.142 = (bf16[2,128,256]{2,1,0:T(8,128)(2,1)S(1)}, bf16[256,1024]{1,0:T(8,128)(2,1)S(1)}, bf16[512,768]{1,0:T(8,128)(2,1)S(1)}, bf16[512,768]{1,0:T(8,128)(2,1)S(1)}) custom-call(bf16[200,256]{1,0:T(8,128)(2,1)S(1)} %collective-permute-done.2.refs_0_, bf16[200,256]{1,0:T(8,128)(2,1)S(1)} %collective-permute-done.3.refs_1_, ...), custom_call_target="tpu_custom_call" | custom-call | flops 1 | bytes 1 | tf_op jit(solution)/shard_map/pallas_call | solution.py:28
  24.7 0.1 collective-permute-start.5
  24.8 1.5 %shard_map.143 = (bf16[256,512]{1,0:T(8,128)(2,1)S(1)}, bf16[512,768]{1,0:T(8,128)(2,1)S(1)}, bf16[512,768]{1,0:T(8,128)(2,1)S(1)}) custom-call(bf16[2,128,256]{2,1,0:T(8,128)(2,1)S(1)} %get-tuple-element.71.grad_ref, bf16[1024,128]{1,0:T(8,128)(2,1)S(1)} %get-tuple-element.72.pt_ref, bf16[2,64,1024]{2,1,0:T(8,128)(2,1)S(1)} %get-tuple-element.73.own_value_ref, ...), custom_call_target="tpu_custom_call" | custom-call | flops 1 | bytes 1 | tf_op jit(solution)/shard_map/pallas_call | solution.py:28
  26.3 0.6 collective-permute-start.6
  26.8 1.9 %shard_map.144 = (bf16[256,512]{1,0:T(8,128)(2,1)S(1)}, bf16[512,768]{1,0:T(8,128)(2,1)S(1)}, bf16[512,768]{1,0:T(8,128)(2,1)S(1)}) custom-call(bf16[2,128,256]{2,1,0:T(8,128)(2,1)S(1)} %get-tuple-element.71.grad_ref, bf16[1024,128]{1,0:T(8,128)(2,1)S(1)} %get-tuple-element.72.pt_ref, bf16[2,64,1024]{2,1,0:T(8,128)(2,1)S(1)} %get-tuple-element.73.own_value_ref, ...), custom_call_target="tpu_custom_call" | custom-call | flops 1 | bytes 1 | tf_op jit(solution)/shard_map/pallas_call | solution.py:28
  28.8 0.1 collective-permute-start.7
  28.9 0.1 add_convert_fusion.2
  29.0 0.1 add_convert_fusion.1
  29.1 2.0 %collective-permute-done.7 = bf16[512,768]{1,0:T(8,128)(2,1)S(1)} collective-permute-done((bf16[512,768]{1,0:T(8,128)(2,1)S(1)}, bf16[512,768]{1,0:T(8,128)(2,1)S(1)}, u32[]{:S(2)}, u32[]{:S(2)}) %collective-permute-start.7) | collective-permute-done | bytes 786464 | tf_op jit(solution)/shard_map/ppermute | solution.py:401
  31.1 0.1 add_convert_fusion
  31.2 1.8 %collective-permute-start.10 = (bf16[256,768]{1,0:T(8,128)(2,1)S(1)}, bf16[256,768]{1,0:T(8,128)(2,1)S(1)}, u32[]{:S(2)}, u32[]{:S(2)}) collective-permute-start(bf16[256,768]{1,0:T(8,128)(2,1)S(1)} %add_convert_fusion.2), channel_id=1, source_target_pairs={{0,2},{1,3},{2,0},{3,1},{4,6},{5,7},{6,4},{7,5},{8,10},{9,11},{10,... | collective-permute-start | bytes 1179656 | tf_op jit(solution)/shard_map/ppermute | solution.py:401
  33.0 1.8 %collective-permute-start.11 = (bf16[256,768]{1,0:T(8,128)(2,1)S(1)}, bf16[256,768]{1,0:T(8,128)(2,1)S(1)}, u32[]{:S(2)}, u32[]{:S(2)}) collective-permute-start(bf16[256,768]{1,0:T(8,128)(2,1)S(1)} %add_convert_fusion.1), channel_id=1, source_target_pairs={{0,4},{1,5},{2,6},{3,7},{4,0},{5,1},{6,2},{7,3},{8,12},{9,13},{10,... | collective-permute-start | bytes 1179656 | tf_op jit(solution)/shard_map/ppermute | solution.py:401
  34.8 0.4 collective-permute-start.8
  35.3 1.3 %shard_map.145 = (f32[2,64,1024]{2,1,0:T(8,128)S(1)}, bf16[128,1024]{1,0:T(8,128)(2,1)S(1)}) custom-call(bf16[256,512]{1,0:T(8,128)(2,1)S(1)} %get-tuple-element.78.first_ref, bf16[256,512]{1,0:T(8,128)(2,1)S(1)} %get-tuple-element.93.last_ref, bf16[256,1024]{1,0:T(8,128)(2,1)S(1)} %get-tuple-element.77.ngv_ref, bf16[1024,2048]{1,0:T(8,128)(2,1)S(1)} %copy-done), custom_call_target="tpu_custom_call" | custom-call | flops 1 | bytes 1 | tf_op jit(solution)/shard_map/pallas_call | solution.py:28
  36.6 0.1 collective-permute-start.9
  36.8 5.8 %collective-permute-done.10 = bf16[256,768]{1,0:T(8,128)(2,1)S(1)} collective-permute-done((bf16[256,768]{1,0:T(8,128)(2,1)S(1)}, bf16[256,768]{1,0:T(8,128)(2,1)S(1)}, u32[]{:S(2)}, u32[]{:S(2)}) %collective-permute-start.10) | collective-permute-done | bytes 393248 | tf_op jit(solution)/shard_map/ppermute | solution.py:401
  42.6 0.1 add_convert_fusion.5
  42.7 1.4 %collective-permute-done.11 = bf16[256,768]{1,0:T(8,128)(2,1)S(1)} collective-permute-done((bf16[256,768]{1,0:T(8,128)(2,1)S(1)}, bf16[256,768]{1,0:T(8,128)(2,1)S(1)}, u32[]{:S(2)}, u32[]{:S(2)}) %collective-permute-start.11) | collective-permute-done | bytes 393248 | tf_op jit(solution)/shard_map/ppermute | solution.py:401
  44.1 1.3 %collective-permute-done.8 = bf16[256,768]{1,0:T(8,128)(2,1)S(1)} collective-permute-done((bf16[256,768]{1,0:T(8,128)(2,1)S(1)}, bf16[256,768]{1,0:T(8,128)(2,1)S(1)}, u32[]{:S(2)}, u32[]{:S(2)}) %collective-permute-start.8) | collective-permute-done | bytes 393248 | tf_op jit(solution)/shard_map/ppermute | solution.py:401
  45.4 0.1 add_convert_fusion.4
  45.5 0.1 add_convert_fusion.3
  45.6 0.9 %collective-permute-start.16 = (bf16[128,768]{1,0:T(8,128)(2,1)S(1)}, bf16[128,768]{1,0:T(8,128)(2,1)S(1)}, u32[]{:S(2)}, u32[]{:S(2)}) collective-permute-start(bf16[128,768]{1,0:T(8,128)(2,1)S(1)} %add_convert_fusion.3), channel_id=1, source_target_pairs={{0,2},{1,3},{2,0},{3,1},{4,6},{5,7},{6,4},{7,5},{8,10},{9,11},{10,... | collective-permute-start | bytes 589832 | tf_op jit(solution)/shard_map/ppermute | solution.py:401
  46.5 0.4 collective-permute-start.14
  46.9 0.3 collective-permute-start.12
  47.2 4.1 %collective-permute-done.16 = bf16[128,768]{1,0:T(8,128)(2,1)S(1)} collective-permute-done((bf16[128,768]{1,0:T(8,128)(2,1)S(1)}, bf16[128,768]{1,0:T(8,128)(2,1)S(1)}, u32[]{:S(2)}, u32[]{:S(2)}) %collective-permute-start.16) | collective-permute-done | bytes 196640 | tf_op jit(solution)/shard_map/ppermute | solution.py:401
  51.4 0.5 collective-permute-start.17
  51.9 0.2 collective-permute-done.14
  52.2 1.3 %collective-permute-start.15 = (bf16[64,768]{1,0:T(8,128)(2,1)S(1)}, bf16[64,768]{1,0:T(8,128)(2,1)S(1)}, u32[]{:S(2)}, u32[]{:S(2)}) collective-permute-start(bf16[64,768]{1,0:T(8,128)(2,1)S(1)} %add_convert_fusion.7), channel_id=1, source_target_pairs={{0,2},{1,3},{2,0},{3,1},{4,6},{5,7},{6,4},{7,5},{8,10},{9,11},{10,... | collective-permute-start | bytes 294920 | tf_op jit(solution)/shard_map/ppermute | solution.py:401
  53.5 0.1 collective-permute-done.12
  53.6 1.6 %collective-permute-start.13 = (bf16[64,768]{1,0:T(8,128)(2,1)S(1)}, bf16[64,768]{1,0:T(8,128)(2,1)S(1)}, u32[]{:S(2)}, u32[]{:S(2)}) collective-permute-start(bf16[64,768]{1,0:T(8,128)(2,1)S(1)} %add_convert_fusion.8), channel_id=1, source_target_pairs={{0,8},{8,0},{16,24},{24,16},{1,9},{9,1},{17,25},{25,17},{2,10},{10... | collective-permute-start | bytes 294920 | tf_op jit(solution)/shard_map/ppermute | solution.py:401
  55.3 0.8 %collective-permute-done.17 = bf16[64,768]{1,0:T(8,128)(2,1)S(1)} collective-permute-done((bf16[64,768]{1,0:T(8,128)(2,1)S(1)}, bf16[64,768]{1,0:T(8,128)(2,1)S(1)}, u32[]{:S(2)}, u32[]{:S(2)}) %collective-permute-start.17) | collective-permute-done | bytes 98336 | tf_op jit(solution)/shard_map/ppermute | solution.py:401
  56.1 0.8 %collective-permute-done.15 = bf16[64,768]{1,0:T(8,128)(2,1)S(1)} collective-permute-done((bf16[64,768]{1,0:T(8,128)(2,1)S(1)}, bf16[64,768]{1,0:T(8,128)(2,1)S(1)}, u32[]{:S(2)}, u32[]{:S(2)}) %collective-permute-start.15) | collective-permute-done | bytes 98336 | tf_op jit(solution)/shard_map/ppermute | solution.py:401
  56.9 1.9 %collective-permute-done.13 = bf16[64,768]{1,0:T(8,128)(2,1)S(1)} collective-permute-done((bf16[64,768]{1,0:T(8,128)(2,1)S(1)}, bf16[64,768]{1,0:T(8,128)(2,1)S(1)}, u32[]{:S(2)}, u32[]{:S(2)}) %collective-permute-start.13) | collective-permute-done | bytes 98336 | tf_op jit(solution)/shard_map/ppermute | solution.py:401
  58.8 0.1 convert_add_fusion
  59.1 3.0 %collective-permute-start.19 = (bf16[32,2304]{1,0:T(8,128)(2,1)S(1)}, bf16[32,2304]{1,0:T(8,128)(2,1)S(1)}, u32[]{:S(2)}, u32[]{:S(2)}) collective-permute-start(bf16[32,2304]{1,0:T(8,128)(2,1)S(1)} %slice.273), channel_id=1, source_target_pairs={{0,16},{8,24},{16,0},{24,8},{1,17},{9,25},{17,1},{25,9},{2,18},{10... | collective-permute-start | bytes 442376 | tf_op jit(solution)/shard_map/ppermute | solution.py:401
  62.1 1.3 %collective-permute-start.18 = (bf16[64,1024]{1,0:T(8,128)(2,1)S(1)}, bf16[64,1024]{1,0:T(8,128)(2,1)S(1)}, u32[]{:S(2)}, u32[]{:S(2)}) collective-permute-start(bf16[64,1024]{1,0:T(8,128)(2,1)S(1)} %slice.203), channel_id=1, source_target_pairs={{0,2},{1,7},{2,4},{3,1},{4,6},{5,3},{6,0},{7,5},{8,10},{9,15},{10,... | collective-permute-start | bytes 393224 | tf_op jit(solution)/shard_map/ppermute | solution.py:534
  63.4 4.6 %collective-permute-done.18.other_ref = bf16[64,1024]{1,0:T(8,128)(2,1)S(1)} collective-permute-done((bf16[64,1024]{1,0:T(8,128)(2,1)S(1)}, bf16[64,1024]{1,0:T(8,128)(2,1)S(1)}, u32[]{:S(2)}, u32[]{:S(2)}) %collective-permute-start.18) | collective-permute-done | bytes 131104 | tf_op jit(solution)/shard_map/ppermute | solution.py:534
  67.9 1.2 %shard_map.146 = (f32[2,64,1024]{2,1,0:T(8,128)}, f32[32,2048]{1,0:T(8,128)}, f32[32,1024]{1,0:T(8,128)}, f32[32,100]{1,0:T(8,128)}) custom-call(f32[2,64,1024]{2,1,0:T(8,128)S(1)} %get-tuple-element.94.own_hidden_ref, bf16[128,1024]{1,0:T(8,128)(2,1)S(1)} %collective-permute-done.9.mate_ref, bf16[64,1024]{1,0:T(8,128)(2,1)S(1)} %collective-permute-done.18.other_ref, ...), custom_call_target="tpu_custom_call" | custom-call | flops 1 | bytes 1 | tf_op jit(solution)/shard_map/pallas_call | solution.py:28
  (38 shorter events, 0.5 us)
Async XLA Ops:
  0.6 4.9 %copy-start.3 = (bf16[1024,100]{0,1:T(8,128)(2,1)S(1)}, bf16[1024,100]{0,1:T(8,128)(2,1)}, u32[]{:S(2)}) copy-start(bf16[1024,100]{0,1:T(8,128)(2,1)} %param.15) | copy-start | bytes 614404
  0.6 4.9 %copy-start.8 = (f32[100]{0:T(128)S(1)}, f32[100]{0:T(128)}, u32[]{:S(2)}) copy-start(f32[100]{0:T(128)} %param.19) | copy-start | bytes 1204
  0.7 4.9 %copy-start.7 = (f32[256]{0:T(256)S(1)}, f32[256]{0:T(256)}, u32[]{:S(2)}) copy-start(f32[256]{0:T(256)} %param.18) | copy-start | bytes 3076
  0.7 4.9 %copy-start.2 = (bf16[256,1024]{1,0:T(8,128)(2,1)S(1)}, bf16[256,1024]{1,0:T(8,128)(2,1)}, u32[]{:S(2)}) copy-start(bf16[256,1024]{1,0:T(8,128)(2,1)} %q_ref.5) | copy-start | bytes 1572868
  0.7 4.9 %copy-start.1 = (bf16[1024,1024]{1,0:T(8,128)(2,1)S(1)}, bf16[1024,1024]{1,0:T(8,128)(2,1)}, u32[]{:S(2)}) copy-start(bf16[1024,1024]{1,0:T(8,128)(2,1)} %wo_ref.3) | copy-start | bytes 6291460
  0.7 4.9 %copy-start.5 = (f32[100,256]{1,0:T(8,128)S(1)}, f32[100,256]{1,0:T(8,128)}, u32[]{:S(2)}) copy-start(f32[100,256]{1,0:T(8,128)} %init_ref.1) | copy-start | bytes 307204
  0.7 4.9 %copy-start.6 = (s32[3,256]{1,0:T(4,128)S(1)}, s32[3,256]{1,0:T(4,128)}, u32[]{:S(2)}) copy-start(s32[3,256]{1,0:T(4,128)} %src_ref.3) | copy-start | bytes 9220
  0.7 4.9 %copy-start = (bf16[1024,2048]{1,0:T(8,128)(2,1)S(1)}, bf16[1024,2048]{1,0:T(8,128)(2,1)}, u32[]{:S(2)}) copy-start(bf16[1024,2048]{1,0:T(8,128)(2,1)} %kvw_ref.5) | copy-start | bytes 12582916
  2.1 6.6 %collective-permute-start = (bf16[64,1024]{1,0:T(8,128)(2,1)S(1)}, bf16[64,1024]{1,0:T(8,128)(2,1)S(1)}, u32[]{:S(2)}, u32[]{:S(2)}) collective-permute-start(bf16[64,1024]{1,0:T(8,128)(2,1)S(1)} %get-tuple-element.59), channel_id=1, source_target_pairs={{0,7},{1,2},{2,1},{3,4},{4,3},{5,6},{6,5},{7,0},{8,15},{9,10},{10,... | collective-permute-start | bytes 393224 | tf_op jit(solution)/shard_map/ppermute | solution.py:437
  5.5 3.2 %collective-permute-start.1 = (bf16[64,1024]{1,0:T(8,128)(2,1)S(1)}, bf16[64,1024]{1,0:T(8,128)(2,1)S(1)}, u32[]{:S(2)}, u32[]{:S(2)}) collective-permute-start(bf16[64,1024]{1,0:T(8,128)(2,1)S(1)} %get-tuple-element.60), channel_id=1, source_target_pairs={{0,1},{1,0},{2,3},{3,2},{4,5},{5,4},{6,7},{7,6},{8,9},{9,8},{10,11... | collective-permute-start | bytes 393224 | tf_op jit(solution)/shard_map/ppermute | solution.py:438
  8.7 14.1 %copy-start.4 = (f32[100,256]{1,0:T(8,128)S(1)}, f32[100,256]{1,0:T(8,128)}, u32[]{:S(2)}) copy-start(f32[100,256]{1,0:T(8,128)} %refs_5_.1) | copy-start | bytes 307204
  10.4 8.2 %collective-permute-start.2 = (bf16[200,256]{1,0:T(8,128)(2,1)S(1)}, bf16[200,256]{1,0:T(8,128)(2,1)S(1)}, u32[]{:S(2)}, u32[]{:S(2)}) collective-permute-start(bf16[200,256]{1,0:T(8,128)(2,1)S(1)} %get-tuple-element.65), channel_id=1, source_target_pairs={{0,24},{8,16},{16,8},{24,0},{1,25},{9,17},{17,9},{25,1},{2,26},{10... | collective-permute-start | bytes 307208 | tf_op jit(solution)/shard_map/ppermute | solution.py:475
  15.6 7.3 %collective-permute-start.3 = (bf16[200,256]{1,0:T(8,128)(2,1)S(1)}, bf16[200,256]{1,0:T(8,128)(2,1)S(1)}, u32[]{:S(2)}, u32[]{:S(2)}) collective-permute-start(bf16[200,256]{1,0:T(8,128)(2,1)S(1)} %get-tuple-element.65), channel_id=1, source_target_pairs={{0,16},{8,24},{16,0},{24,8},{1,17},{9,25},{17,1},{25,9},{2,18},{10... | collective-permute-start | bytes 307208 | tf_op jit(solution)/shard_map/ppermute | solution.py:475
  15.6 7.3 %collective-permute-start.4 = (bf16[200,256]{1,0:T(8,128)(2,1)S(1)}, bf16[200,256]{1,0:T(8,128)(2,1)S(1)}, u32[]{:S(2)}, u32[]{:S(2)}) collective-permute-start(bf16[200,256]{1,0:T(8,128)(2,1)S(1)} %get-tuple-element.65), channel_id=1, source_target_pairs={{0,8},{8,0},{16,24},{24,16},{1,9},{9,1},{17,25},{25,17},{2,10},{10... | collective-permute-start | bytes 307208 | tf_op jit(solution)/shard_map/ppermute | solution.py:475
  24.7 4.1 %collective-permute-start.5 = (bf16[512,768]{1,0:T(8,128)(2,1)S(1)}, bf16[512,768]{1,0:T(8,128)(2,1)S(1)}, u32[]{:S(2)}, u32[]{:S(2)}) collective-permute-start(bf16[512,768]{1,0:T(8,128)(2,1)S(1)} %get-tuple-element.80), channel_id=1, source_target_pairs={{0,1},{1,0},{2,3},{3,2},{4,5},{5,4},{6,7},{7,6},{8,9},{9,8},{10,11... | collective-permute-start | bytes 2359304 | tf_op jit(solution)/shard_map/ppermute | solution.py:401
  26.3 2.7 %collective-permute-start.6 = (bf16[512,768]{1,0:T(8,128)(2,1)S(1)}, bf16[512,768]{1,0:T(8,128)(2,1)S(1)}, u32[]{:S(2)}, u32[]{:S(2)}) collective-permute-start(bf16[512,768]{1,0:T(8,128)(2,1)S(1)} %get-tuple-element.82), channel_id=1, source_target_pairs={{0,1},{1,0},{2,3},{3,2},{4,5},{5,4},{6,7},{7,6},{8,9},{9,8},{10,11... | collective-permute-start | bytes 2359304 | tf_op jit(solution)/shard_map/ppermute | solution.py:401
  28.8 2.4 %collective-permute-start.7 = (bf16[512,768]{1,0:T(8,128)(2,1)S(1)}, bf16[512,768]{1,0:T(8,128)(2,1)S(1)}, u32[]{:S(2)}, u32[]{:S(2)}) collective-permute-start(bf16[512,768]{1,0:T(8,128)(2,1)S(1)} %get-tuple-element.88), channel_id=1, source_target_pairs={{0,1},{1,0},{2,3},{3,2},{4,5},{5,4},{6,7},{7,6},{8,9},{9,8},{10,11... | collective-permute-start | bytes 2359304 | tf_op jit(solution)/shard_map/ppermute | solution.py:401
  31.2 11.4 %collective-permute-start.10 = (bf16[256,768]{1,0:T(8,128)(2,1)S(1)}, bf16[256,768]{1,0:T(8,128)(2,1)S(1)}, u32[]{:S(2)}, u32[]{:S(2)}) collective-permute-start(bf16[256,768]{1,0:T(8,128)(2,1)S(1)} %add_convert_fusion.2), channel_id=1, source_target_pairs={{0,2},{1,3},{2,0},{3,1},{4,6},{5,7},{6,4},{7,5},{8,10},{9,11},{10,... | collective-permute-start | bytes 1179656 | tf_op jit(solution)/shard_map/ppermute | solution.py:401
  33.0 11.1 %collective-permute-start.11 = (bf16[256,768]{1,0:T(8,128)(2,1)S(1)}, bf16[256,768]{1,0:T(8,128)(2,1)S(1)}, u32[]{:S(2)}, u32[]{:S(2)}) collective-permute-start(bf16[256,768]{1,0:T(8,128)(2,1)S(1)} %add_convert_fusion.1), channel_id=1, source_target_pairs={{0,4},{1,5},{2,6},{3,7},{4,0},{5,1},{6,2},{7,3},{8,12},{9,13},{10,... | collective-permute-start | bytes 1179656 | tf_op jit(solution)/shard_map/ppermute | solution.py:401
  34.8 10.6 %collective-permute-start.8 = (bf16[256,768]{1,0:T(8,128)(2,1)S(1)}, bf16[256,768]{1,0:T(8,128)(2,1)S(1)}, u32[]{:S(2)}, u32[]{:S(2)}) collective-permute-start(bf16[256,768]{1,0:T(8,128)(2,1)S(1)} %add_convert_fusion), channel_id=1, source_target_pairs={{0,8},{8,0},{16,24},{24,16},{1,9},{9,1},{17,25},{25,17},{2,10},{10... | collective-permute-start | bytes 1179656 | tf_op jit(solution)/shard_map/ppermute | solution.py:401
  36.6 7.5 %collective-permute-start.9 = (bf16[128,1024]{1,0:T(8,128)(2,1)S(1)}, bf16[128,1024]{1,0:T(8,128)(2,1)S(1)}, u32[]{:S(2)}, u32[]{:S(2)}) collective-permute-start(bf16[128,1024]{1,0:T(8,128)(2,1)S(1)} %get-tuple-element.96), channel_id=1, source_target_pairs={{0,1},{1,0},{2,3},{3,2},{4,5},{5,4},{6,7},{7,6},{8,9},{9,8},{10,11... | collective-permute-start | bytes 786440 | tf_op jit(solution)/shard_map/ppermute | solution.py:528
  45.6 5.7 %collective-permute-start.16 = (bf16[128,768]{1,0:T(8,128)(2,1)S(1)}, bf16[128,768]{1,0:T(8,128)(2,1)S(1)}, u32[]{:S(2)}, u32[]{:S(2)}) collective-permute-start(bf16[128,768]{1,0:T(8,128)(2,1)S(1)} %add_convert_fusion.3), channel_id=1, source_target_pairs={{0,2},{1,3},{2,0},{3,1},{4,6},{5,7},{6,4},{7,5},{8,10},{9,11},{10,... | collective-permute-start | bytes 589832 | tf_op jit(solution)/shard_map/ppermute | solution.py:401
  46.5 5.7 %collective-permute-start.14 = (bf16[128,768]{1,0:T(8,128)(2,1)S(1)}, bf16[128,768]{1,0:T(8,128)(2,1)S(1)}, u32[]{:S(2)}, u32[]{:S(2)}) collective-permute-start(bf16[128,768]{1,0:T(8,128)(2,1)S(1)} %add_convert_fusion.4), channel_id=1, source_target_pairs={{0,8},{8,0},{16,24},{24,16},{1,9},{9,1},{17,25},{25,17},{2,10},{10... | collective-permute-start | bytes 589832 | tf_op jit(solution)/shard_map/ppermute | solution.py:401
  46.9 6.7 %collective-permute-start.12 = (bf16[128,768]{1,0:T(8,128)(2,1)S(1)}, bf16[128,768]{1,0:T(8,128)(2,1)S(1)}, u32[]{:S(2)}, u32[]{:S(2)}) collective-permute-start(bf16[128,768]{1,0:T(8,128)(2,1)S(1)} %add_convert_fusion.5), channel_id=1, source_target_pairs={{0,4},{1,5},{2,6},{3,7},{4,0},{5,1},{6,2},{7,3},{8,12},{9,13},{10,... | collective-permute-start | bytes 589832 | tf_op jit(solution)/shard_map/ppermute | solution.py:401
  51.4 4.7 %collective-permute-start.17 = (bf16[64,768]{1,0:T(8,128)(2,1)S(1)}, bf16[64,768]{1,0:T(8,128)(2,1)S(1)}, u32[]{:S(2)}, u32[]{:S(2)}) collective-permute-start(bf16[64,768]{1,0:T(8,128)(2,1)S(1)} %add_convert_fusion.6), channel_id=1, source_target_pairs={{0,4},{1,5},{2,6},{3,7},{4,0},{5,1},{6,2},{7,3},{8,12},{9,13},{10,... | collective-permute-start | bytes 294920 | tf_op jit(solution)/shard_map/ppermute | solution.py:401
  52.2 4.7 %collective-permute-start.15 = (bf16[64,768]{1,0:T(8,128)(2,1)S(1)}, bf16[64,768]{1,0:T(8,128)(2,1)S(1)}, u32[]{:S(2)}, u32[]{:S(2)}) collective-permute-start(bf16[64,768]{1,0:T(8,128)(2,1)S(1)} %add_convert_fusion.7), channel_id=1, source_target_pairs={{0,2},{1,3},{2,0},{3,1},{4,6},{5,7},{6,4},{7,5},{8,10},{9,11},{10,... | collective-permute-start | bytes 294920 | tf_op jit(solution)/shard_map/ppermute | solution.py:401
  53.6 5.1 %collective-permute-start.13 = (bf16[64,768]{1,0:T(8,128)(2,1)S(1)}, bf16[64,768]{1,0:T(8,128)(2,1)S(1)}, u32[]{:S(2)}, u32[]{:S(2)}) collective-permute-start(bf16[64,768]{1,0:T(8,128)(2,1)S(1)} %add_convert_fusion.8), channel_id=1, source_target_pairs={{0,8},{8,0},{16,24},{24,16},{1,9},{9,1},{17,25},{25,17},{2,10},{10... | collective-permute-start | bytes 294920 | tf_op jit(solution)/shard_map/ppermute | solution.py:401
  59.1 8.9 %collective-permute-start.19 = (bf16[32,2304]{1,0:T(8,128)(2,1)S(1)}, bf16[32,2304]{1,0:T(8,128)(2,1)S(1)}, u32[]{:S(2)}, u32[]{:S(2)}) collective-permute-start(bf16[32,2304]{1,0:T(8,128)(2,1)S(1)} %slice.273), channel_id=1, source_target_pairs={{0,16},{8,24},{16,0},{24,8},{1,17},{9,25},{17,1},{25,9},{2,18},{10... | collective-permute-start | bytes 442376 | tf_op jit(solution)/shard_map/ppermute | solution.py:401
  62.1 5.9 %collective-permute-start.18 = (bf16[64,1024]{1,0:T(8,128)(2,1)S(1)}, bf16[64,1024]{1,0:T(8,128)(2,1)S(1)}, u32[]{:S(2)}, u32[]{:S(2)}) collective-permute-start(bf16[64,1024]{1,0:T(8,128)(2,1)S(1)} %slice.203), channel_id=1, source_target_pairs={{0,2},{1,7},{2,4},{3,1},{4,6},{5,3},{6,0},{7,5},{8,10},{9,15},{10,... | collective-permute-start | bytes 393224 | tf_op jit(solution)/shard_map/ppermute | solution.py:534

commit v17 on v16

--- a/solution.py
+++ b/solution.py
@@ -343,18 +343,22 @@
 
 def last_keys_body(
     n_member, n_band, grad_ref, pt_ref, own_value_ref, halo_value_ref, own_slope_ref, halo_slope_ref,
-    q_ref, merged_ref, wo_ref, ext_ref, ng_ref, *refs
+    q_ref, ext_ref, ng_ref, *out_refs
 ):
-    out_refs, turned = refs[:-1], refs[-1]
-    members, width, _ = merged_ref.shape
+    width = q_ref.shape[1]
     pairs = range((width - ng_ref.shape[1]) // LANES, width // LANES)
     value_refs, slope_refs = (own_value_ref, halo_value_ref), (own_slope_ref, halo_slope_ref)
     key_gradients(pairs, grad_ref, pt_ref, value_refs, slope_refs, q_ref, ng_ref)
+    store_group(mm(ext_ref[...], ng_ref[...]), 2, n_member, n_band, 0, out_refs)
+
+
+def small_body(n_member, n_band, grad_ref, q_ref, merged_ref, wo_ref, *refs):
+    out_refs, turned = refs[:-1], refs[-1]
+    members = grad_ref.shape[0]
     m_t = sum(mm(grad_ref[m], merged_ref[m], NT) for m in range(members))
     head_t = sum(mm(grad_ref[m], q_ref[...]) for m in range(members)) + mm(m_t.astype(BF), wo_ref[...])
     turned[...] = jnp.concatenate([m_t, head_t], axis=0).T
-    store_group(mm(ext_ref[...], ng_ref[...]), 2, n_member, n_band, 0, out_refs)
-    store_group(reorder(turned, n_member, n_band), 2, n_member, n_band, ng_ref.shape[1], out_refs)
+    store_group(reorder(turned, n_member, n_band), 2, n_member, n_band, 0, out_refs)
 
 
 def extended_grad_body(members, nodes, rim, first_ref, last_ref, ngv_ref, kvw_ref, own_ref, back_ref):
@@ -409,6 +413,14 @@
     return [t[t.shape[0] // 2 :] for t in terms]
 
 
+def summed(pieces, half):
+    return jnp.concatenate([add_up(*half(terms)) for terms in pieces], axis=1)
+
+
+def remaining(pieces):
+    return lower(pieces[0]) if len(pieces) == 1 else [summed(pieces, lower)]
+
+
 def shards(
     n_member, n_band,
     hidden, queries, kv_weight, out_weight, head_projection, initial_state, truth,
@@ -492,20 +504,27 @@
         + group_shape,
         (*received, part, base, truth, weight, p, own_gates, halo_gates, ext_t),
     )
-    groups = [[keep, swap(send, "band", 0, n_band)]]
+    groups = [[[keep, swap(send, "band", 0, n_band)]]]
     ng_first, send, keep = call(
         functools.partial(first_keys_body, n_member, n_band, group_width),
         [sds((members * ext, first_keys), BF)] + group_shape,
         (grad, pt, own_value, halo_value, own_slopes, halo_slopes, queries, ext_t, ng_value),
     )
-    groups.append([keep, swap(send, "band", 0, n_band)])
+    groups.append([[keep, swap(send, "band", 0, n_band)]])
+    last_keys = width - first_keys
     ng_last, send, keep = call(
         functools.partial(last_keys_body, n_member, n_band),
-        [sds((members * ext, width - first_keys), BF)] + group_shape,
-        (grad, pt, own_value, halo_value, own_slopes, halo_slopes, queries, merged, out_weight, ext_t),
+        [sds((members * ext, last_keys), BF)] + [sds((width // 2, last_keys), BF)] * 2,
+        (grad, pt, own_value, halo_value, own_slopes, halo_slopes, queries, ext_t),
+    )
+    groups.append([[keep, swap(send, "band", 0, n_band)]])
+    send, keep = call(
+        functools.partial(small_body, n_member, n_band),
+        [sds((width // 2, extra), BF)] * 2,
+        (grad, queries, merged, out_weight),
         [pltpu.VMEM((width, extra), F32)],
     )
-    groups.append([keep, swap(send, "band", 0, n_band)])
+    groups[-1].append([keep, swap(send, "band", 0, n_band)])
 
     count = {"member": n_member, "band": n_band}
     turns, rest = halving_orders(n_member, n_band)
@@ -513,7 +532,7 @@
     for step in range(steps):
         outgoing = []
         for i in range(GROUPS):
-            outgoing.append(add_up(*upper(groups[i])).astype(BF))
+            outgoing.append(summed(groups[i], upper).astype(BF))
             if step <= 1 and i + 1 < GROUPS:
                 outgoing[i], groups[i + 1] = lax.optimization_barrier((outgoing[i], groups[i + 1]))
         if step == 0:
@@ -532,8 +551,8 @@
             arrived, onward = lax.optimization_barrier((arrived, onward))
             chips_on = [(i, (i + 2 - i % 2 * 4) % n_band) for i in range(n_band)]
             from_other = lax.ppermute(onward, "band", chips_on)
-        groups = [lower(terms) + [new] for terms, new in zip(groups, arrived)]
-    terms = [jnp.concatenate([add_up(*group) for group in groups], axis=1)]
+        groups = [[remaining(pieces) + [new]] for pieces, new in zip(groups, arrived)]
+    terms = [jnp.concatenate([add_up(*group[0]) for group in groups], axis=1)]
     for axis, bit in rest:
         arrived = swap(add_up(*upper(terms)).astype(BF), axis, bit, count[axis])
         terms = lower(terms) + [arrived]

time: 69.3 us -> 69.6 us (level)
  waiting for transfers between devices: 30.2 us -> 28.4 us
  starting transfers between devices: 23.3 us -> 24.9 us
    ppermute x13 -> x14, waiting for transfers between devices: 18.6 us -> 16.8 us  [swap(): return lax.ppermute(rows, axis, [(i, i ^ 1 << bit) for i in range(count)])]
    ppermute x13 -> x14, starting transfers between devices: 12.8 us -> 14.3 us  [swap(): return lax.ppermute(rows, axis, [(i, i ^ 1 << bit) for i in range(count)])]
    pallas_call x9 -> x10, Pallas kernels: 13.6 us -> 14.1 us  [call(): pl.pallas_call(body, out_shape=out_shape, in_specs=[pl.BlockSpec(memory_s...]
  transfers between devices with their start and end apart: 20 -> 21, of which waited for: 14 -> 13; matrix products, arithmetic and copies ran while one was open for 1% -> 1% of each run, Pallas kernels for 11% -> 11%
where the time goes in v17:
time: 69.6 us; the launch traced here: 69.4 us
  waiting for transfers between devices  28.4 us (41%)
  starting transfers between devices  24.9 us (36%)
  Pallas kernels  14.1 us (20%)
  other arithmetic  1 us (1%)
  between operations  0.96 us (1%)
    ppermute x14, waiting for transfers between devices, swap(): return lax.ppermute(rows, axis, [(i, i ^ 1 << bit) for i in range(count)])  16.8 us
    ppermute x14, starting transfers between devices, swap(): return lax.ppermute(rows, axis, [(i, i ^ 1 << bit) for i in range(count)])  14.3 us
    pallas_call x10, Pallas kernels, call(): pl.pallas_call(body, out_shape=out_shape, in_specs=[pl.BlockSpec(memory_s...  14.1 us
    ppermute x3, waiting for transfers between devices, shards(): lax.ppermute(sent, 'member', [(i, i ^ s) for i in range(n_member)])  6.35 us
    ppermute x3, starting transfers between devices, shards(): lax.ppermute(sent, 'member', [(i, i ^ s) for i in range(n_member)])  5.79 us
    ppermute x1, waiting for transfers between devices, shards(): from_other = lax.ppermute(onward, 'band', chips_on)  4.46 us
    ppermute x1, starting transfers between devices, shards(): other = lax.ppermute(for_other, 'band', others)  3.4 us
  transfers between devices with their start and end apart: 21, of which 13 were waited for; matrix products, arithmetic and copies ran while one was open for 1% of the time, Pallas kernels for 11%

profile of v17, /device:TPU:0, one launch (start us, length us, event | category | flops | bytes accessed | tf_op | source)
XLA Modules:
  0.0 69.4 jit_solution(14302059908354871838)
XLA Ops:
  0.7 1.4 %shard_map.138 = (bf16[2,64,1024]{2,1,0:T(8,128)(2,1)S(1)}, s32[2,32]{1,0:T(2,128)S(1)}, bf16[64,1024]{1,0:T(8,128)(2,1)S(1)}, bf16[64,1024]{1,0:T(8,128)(2,1)S(1)}) custom-call(bf16[2,64,1024]{2,1,0:T(8,128)(2,1)} %hidden_hbm.1, s32[2,32]{1,0:T(2,128)} %halo_hbm.1), custom_call_target="tpu_custom_call" | custom-call | flops 10000000000 | bytes 1 | tf_op jit(solution)/shard_map/pallas_call | solution.py:28
  2.1 3.4 %collective-permute-start = (bf16[64,1024]{1,0:T(8,128)(2,1)S(1)}, bf16[64,1024]{1,0:T(8,128)(2,1)S(1)}, u32[]{:S(2)}, u32[]{:S(2)}) collective-permute-start(bf16[64,1024]{1,0:T(8,128)(2,1)S(1)} %get-tuple-element.62), channel_id=1, source_target_pairs={{0,7},{1,2},{2,1},{3,4},{4,3},{5,6},{6,5},{7,0},{8,15},{9,10},{10,... | collective-permute-start | bytes 393224 | tf_op jit(solution)/shard_map/ppermute | solution.py:449
  5.6 2.5 %shard_map.139 = (bf16[2,64,1024]{2,1,0:T(8,128)(2,1)S(1)}, bf16[8,2,128,256]{3,2,1,0:T(8,128)(2,1)S(1)}, bf16[8,2,128,256]{3,2,1,0:T(8,128)(2,1)S(1)}, f32[2,10...) custom-call(bf16[2,64,1024]{2,1,0:T(8,128)(2,1)S(1)} %get-tuple-elem, ...), custom_call_target="tpu_custom_call" | custom-call | flops 1 | bytes 1 | tf_op jit(solution)/shard_map/pallas_call | solution.py:28
  8.0 0.7 collective-permute-done.other_ref
  8.7 1.7 %shard_map.140 = (bf16[2,64,1024]{2,1,0:T(8,128)(2,1)S(1)}, bf16[8,2,128,256]{3,2,1,0:T(8,128)(2,1)S(1)}, bf16[8,2,128,256]{3,2,1,0:T(8,128)(2,1)S(1)}, bf16[2,1...) custom-call(bf16[64,1024]{1,0:T(8,128)(2,1)S(1)} %collective-permute-done.other_ref, ...), custom_call_target="tpu_custom_call" | custom-call | flops 1 | bytes 1 | tf_op jit(solution)/shard_map/pallas_call | solution.py:28
  10.5 5.2 %collective-permute-start.2 = (bf16[200,256]{1,0:T(8,128)(2,1)S(1)}, bf16[200,256]{1,0:T(8,128)(2,1)S(1)}, u32[]{:S(2)}, u32[]{:S(2)}) collective-permute-start(bf16[200,256]{1,0:T(8,128)(2,1)S(1)} %get-tuple-element.68), channel_id=1, source_target_pairs={{0,24},{8,16},{16,8},{24,0},{1,25},{9,17},{17,9},{25,1},{2,26},{10... | collective-permute-start | bytes 307208 | tf_op jit(solution)/shard_map/ppermute | solution.py:487
  15.6 0.6 collective-permute-start.4
  16.3 0.3 shard_map.141.refs_10_.ext_ref
  16.5 2.1 %collective-permute-done.2.refs_0_ = bf16[200,256]{1,0:T(8,128)(2,1)S(1)} collective-permute-done((bf16[200,256]{1,0:T(8,128)(2,1)S(1)}, bf16[200,256]{1,0:T(8,128)(2,1)S(1)}, u32[]{:S(2)}, u32[]{:S(2)}) %collective-permute-start.2) | collective-permute-done | bytes 102432 | tf_op jit(solution)/shard_map/ppermute | solution.py:487
  18.6 4.2 %collective-permute-done.3.refs_1_ = bf16[200,256]{1,0:T(8,128)(2,1)S(1)} collective-permute-done((bf16[200,256]{1,0:T(8,128)(2,1)S(1)}, bf16[200,256]{1,0:T(8,128)(2,1)S(1)}, u32[]{:S(2)}, u32[]{:S(2)}) %collective-permute-start.3) | collective-permute-done | bytes 102432 | tf_op jit(solution)/shard_map/ppermute | solution.py:487
  22.9 1.9 %shard_map.142 = (bf16[2,128,256]{2,1,0:T(8,128)(2,1)S(1)}, bf16[256,1024]{1,0:T(8,128)(2,1)S(1)}, bf16[512,768]{1,0:T(8,128)(2,1)S(1)}, bf16[512,768]{1,0:T(8,128)(2,1)S(1)}) custom-call(bf16[200,256]{1,0:T(8,128)(2,1)S(1)} %collective-permute-done.2.refs_0_, bf16[200,256]{1,0:T(8,128)(2,1)S(1)} %collective-permute-done.3.refs_1_, ...), custom_call_target="tpu_custom_call" | custom-call | flops 1 | bytes 1 | tf_op jit(solution)/shard_map/pallas_call | solution.py:28
  24.7 0.1 collective-permute-start.5
  24.8 1.5 %shard_map.143 = (bf16[256,512]{1,0:T(8,128)(2,1)S(1)}, bf16[512,768]{1,0:T(8,128)(2,1)S(1)}, bf16[512,768]{1,0:T(8,128)(2,1)S(1)}) custom-call(bf16[2,128,256]{2,1,0:T(8,128)(2,1)S(1)} %get-tuple-element.74.grad_ref, bf16[1024,128]{1,0:T(8,128)(2,1)S(1)} %get-tuple-element.75.pt_ref, bf16[2,64,1024]{2,1,0:T(8,128)(2,1)S(1)} %get-tuple-element.76.own_value_ref, ...), custom_call_target="tpu_custom_call" | custom-call | flops 1 | bytes 1 | tf_op jit(solution)/shard_map/pallas_call | solution.py:28
  26.3 0.6 collective-permute-start.6
  26.8 1.4 %shard_map.144 = (bf16[256,512]{1,0:T(8,128)(2,1)S(1)}, bf16[512,512]{1,0:T(8,128)(2,1)S(1)}, bf16[512,512]{1,0:T(8,128)(2,1)S(1)}) custom-call(bf16[2,128,256]{2,1,0:T(8,128)(2,1)S(1)} %get-tuple-element.74.grad_ref, bf16[1024,128]{1,0:T(8,128)(2,1)S(1)} %get-tuple-element.75.pt_ref, bf16[2,64,1024]{2,1,0:T(8,128)(2,1)S(1)} %get-tuple-element.76.own_value_ref, ...), custom_call_target="tpu_custom_call" | custom-call | flops 1 | bytes 1 | tf_op jit(solution)/shard_map/pallas_call | solution.py:28
  28.2 0.1 collective-permute-start.7
  28.3 1.1 %shard_map.145 = (bf16[512,256]{1,0:T(8,128)(2,1)S(1)}, bf16[512,256]{1,0:T(8,128)(2,1)S(1)}) custom-call(bf16[2,128,256]{2,1,0:T(8,128)(2,1)S(1)} %get-tuple-element.74.grad_ref, bf16[256,1024]{1,0:T(8,128)(2,1)S(1)} %copy-done.2, bf16[2,1024,256]{2,1,0:T(8,128)(2,1)S(1)} %get-tuple-element.91.merged_ref, bf16[1024,1024]{1,0:T(8,128)(2,1)S(1)} %copy-done.1), custom_call_target="tpu_custom_call" | custom-call | flops 1 | bytes 1 | tf_op jit(solution)/shard_map/pallas_call | solution.py:28
  29.4 0.6 collective-permute-start.8
  29.9 0.1 add_convert_fusion.1
  30.0 0.1 add_convert_fusion
  30.1 0.9 %collective-permute-done.8 = bf16[512,256]{1,0:T(8,128)(2,1)S(1)} collective-permute-done((bf16[512,256]{1,0:T(8,128)(2,1)S(1)}, bf16[512,256]{1,0:T(8,128)(2,1)S(1)}, u32[]{:S(2)}, u32[]{:S(2)}) %collective-permute-start.8) | collective-permute-done | bytes 262176 | tf_op jit(solution)/shard_map/ppermute | solution.py:405
  31.1 0.1 convert_add_fusion
  31.3 2.0 %collective-permute-start.11 = (bf16[256,768]{1,0:T(8,128)(2,1)S(1)}, bf16[256,768]{1,0:T(8,128)(2,1)S(1)}, u32[]{:S(2)}, u32[]{:S(2)}) collective-permute-start(bf16[256,768]{1,0:T(8,128)(2,1)S(1)} %add_convert_fusion.1), channel_id=1, source_target_pairs={{0,2},{1,3},{2,0},{3,1},{4,6},{5,7},{6,4},{7,5},{8,10},{9,11},{10,... | collective-permute-start | bytes 1179656 | tf_op jit(solution)/shard_map/ppermute | solution.py:405
  33.3 1.6 %collective-permute-start.12 = (bf16[256,768]{1,0:T(8,128)(2,1)S(1)}, bf16[256,768]{1,0:T(8,128)(2,1)S(1)}, u32[]{:S(2)}, u32[]{:S(2)}) collective-permute-start(bf16[256,768]{1,0:T(8,128)(2,1)S(1)} %add_convert_fusion), channel_id=1, source_target_pairs={{0,4},{1,5},{2,6},{3,7},{4,0},{5,1},{6,2},{7,3},{8,12},{9,13},{10,... | collective-permute-start | bytes 1179656 | tf_op jit(solution)/shard_map/ppermute | solution.py:405
  34.9 0.4 collective-permute-start.9
  35.3 1.3 %shard_map.146 = (f32[2,64,1024]{2,1,0:T(8,128)S(1)}, bf16[128,1024]{1,0:T(8,128)(2,1)S(1)}) custom-call(bf16[256,512]{1,0:T(8,128)(2,1)S(1)} %get-tuple-element.81.first_ref, bf16[256,512]{1,0:T(8,128)(2,1)S(1)} %get-tuple-element.100.last_ref, bf16[256,1024]{1,0:T(8,128)(2,1)S(1)} %get-tuple-element.80.ngv_ref, bf16[1024,2048]{1,0:T(8,128)(2,1)S(1)} %copy-done), custom_call_target="tpu_custom_call" | custom-call | flops 1 | bytes 1 | tf_op jit(solution)/shard_map/pallas_call | solution.py:28
  36.7 0.1 collective-permute-start.10
  36.9 5.9 %collective-permute-done.11 = bf16[256,768]{1,0:T(8,128)(2,1)S(1)} collective-permute-done((bf16[256,768]{1,0:T(8,128)(2,1)S(1)}, bf16[256,768]{1,0:T(8,128)(2,1)S(1)}, u32[]{:S(2)}, u32[]{:S(2)}) %collective-permute-start.11) | collective-permute-done | bytes 393248 | tf_op jit(solution)/shard_map/ppermute | solution.py:405
  42.8 0.1 add_convert_fusion.5
  42.9 1.4 %collective-permute-done.12 = bf16[256,768]{1,0:T(8,128)(2,1)S(1)} collective-permute-done((bf16[256,768]{1,0:T(8,128)(2,1)S(1)}, bf16[256,768]{1,0:T(8,128)(2,1)S(1)}, u32[]{:S(2)}, u32[]{:S(2)}) %collective-permute-start.12) | collective-permute-done | bytes 393248 | tf_op jit(solution)/shard_map/ppermute | solution.py:405
  44.3 1.5 %collective-permute-done.9 = bf16[256,768]{1,0:T(8,128)(2,1)S(1)} collective-permute-done((bf16[256,768]{1,0:T(8,128)(2,1)S(1)}, bf16[256,768]{1,0:T(8,128)(2,1)S(1)}, u32[]{:S(2)}, u32[]{:S(2)}) %collective-permute-start.9) | collective-permute-done | bytes 393248 | tf_op jit(solution)/shard_map/ppermute | solution.py:405
  45.7 0.1 add_convert_fusion.4
  45.8 0.9 %collective-permute-start.17 = (bf16[128,768]{1,0:T(8,128)(2,1)S(1)}, bf16[128,768]{1,0:T(8,128)(2,1)S(1)}, u32[]{:S(2)}, u32[]{:S(2)}) collective-permute-start(bf16[128,768]{1,0:T(8,128)(2,1)S(1)} %add_convert_fusion.3), channel_id=1, source_target_pairs={{0,2},{1,3},{2,0},{3,1},{4,6},{5,7},{6,4},{7,5},{8,10},{9,11},{10,... | collective-permute-start | bytes 589832 | tf_op jit(solution)/shard_map/ppermute | solution.py:405
  46.7 0.4 collective-permute-start.15
  47.2 0.3 collective-permute-start.13
  47.5 4.2 %collective-permute-done.17 = bf16[128,768]{1,0:T(8,128)(2,1)S(1)} collective-permute-done((bf16[128,768]{1,0:T(8,128)(2,1)S(1)}, bf16[128,768]{1,0:T(8,128)(2,1)S(1)}, u32[]{:S(2)}, u32[]{:S(2)}) %collective-permute-start.17) | collective-permute-done | bytes 196640 | tf_op jit(solution)/shard_map/ppermute | solution.py:405
  51.7 0.7 collective-permute-start.18
  52.3 0.1 collective-permute-done.15
  52.5 1.3 %collective-permute-start.16 = (bf16[64,768]{1,0:T(8,128)(2,1)S(1)}, bf16[64,768]{1,0:T(8,128)(2,1)S(1)}, u32[]{:S(2)}, u32[]{:S(2)}) collective-permute-start(bf16[64,768]{1,0:T(8,128)(2,1)S(1)} %add_convert_fusion.8), channel_id=1, source_target_pairs={{0,2},{1,3},{2,0},{3,1},{4,6},{5,7},{6,4},{7,5},{8,10},{9,11},{10,... | collective-permute-start | bytes 294920 | tf_op jit(solution)/shard_map/ppermute | solution.py:405
  53.8 1.8 %collective-permute-start.14 = (bf16[64,768]{1,0:T(8,128)(2,1)S(1)}, bf16[64,768]{1,0:T(8,128)(2,1)S(1)}, u32[]{:S(2)}, u32[]{:S(2)}) collective-permute-start(bf16[64,768]{1,0:T(8,128)(2,1)S(1)} %add_convert_fusion.9), channel_id=1, source_target_pairs={{0,8},{8,0},{16,24},{24,16},{1,9},{9,1},{17,25},{25,17},{2,10},{10... | collective-permute-start | bytes 294920 | tf_op jit(solution)/shard_map/ppermute | solution.py:405
  55.6 0.7 %collective-permute-done.18 = bf16[64,768]{1,0:T(8,128)(2,1)S(1)} collective-permute-done((bf16[64,768]{1,0:T(8,128)(2,1)S(1)}, bf16[64,768]{1,0:T(8,128)(2,1)S(1)}, u32[]{:S(2)}, u32[]{:S(2)}) %collective-permute-start.18) | collective-permute-done | bytes 98336 | tf_op jit(solution)/shard_map/ppermute | solution.py:405
  56.4 0.8 %collective-permute-done.16 = bf16[64,768]{1,0:T(8,128)(2,1)S(1)} collective-permute-done((bf16[64,768]{1,0:T(8,128)(2,1)S(1)}, bf16[64,768]{1,0:T(8,128)(2,1)S(1)}, u32[]{:S(2)}, u32[]{:S(2)}) %collective-permute-start.16) | collective-permute-done | bytes 98336 | tf_op jit(solution)/shard_map/ppermute | solution.py:405
  57.1 1.4 %collective-permute-done.14 = bf16[64,768]{1,0:T(8,128)(2,1)S(1)} collective-permute-done((bf16[64,768]{1,0:T(8,128)(2,1)S(1)}, bf16[64,768]{1,0:T(8,128)(2,1)S(1)}, u32[]{:S(2)}, u32[]{:S(2)}) %collective-permute-start.14) | collective-permute-done | bytes 98336 | tf_op jit(solution)/shard_map/ppermute | solution.py:405
  58.6 0.1 convert_add_fusion.2
  58.8 3.6 %collective-permute-start.20 = (bf16[32,2304]{1,0:T(8,128)(2,1)S(1)}, bf16[32,2304]{1,0:T(8,128)(2,1)S(1)}, u32[]{:S(2)}, u32[]{:S(2)}) collective-permute-start(bf16[32,2304]{1,0:T(8,128)(2,1)S(1)} %slice.277), channel_id=1, source_target_pairs={{0,16},{8,24},{16,0},{24,8},{1,17},{9,25},{17,1},{25,9},{2,18},{10... | collective-permute-start | bytes 442376 | tf_op jit(solution)/shard_map/ppermute | solution.py:405
  62.4 1.4 %collective-permute-start.19 = (bf16[64,1024]{1,0:T(8,128)(2,1)S(1)}, bf16[64,1024]{1,0:T(8,128)(2,1)S(1)}, u32[]{:S(2)}, u32[]{:S(2)}) collective-permute-start(bf16[64,1024]{1,0:T(8,128)(2,1)S(1)} %slice.205), channel_id=1, source_target_pairs={{0,2},{1,7},{2,4},{3,1},{4,6},{5,3},{6,0},{7,5},{8,10},{9,15},{10,... | collective-permute-start | bytes 393224 | tf_op jit(solution)/shard_map/ppermute | solution.py:553
  63.8 4.5 %collective-permute-done.19.other_ref = bf16[64,1024]{1,0:T(8,128)(2,1)S(1)} collective-permute-done((bf16[64,1024]{1,0:T(8,128)(2,1)S(1)}, bf16[64,1024]{1,0:T(8,128)(2,1)S(1)}, u32[]{:S(2)}, u32[]{:S(2)}) %collective-permute-start.19) | collective-permute-done | bytes 131104 | tf_op jit(solution)/shard_map/ppermute | solution.py:553
  68.2 1.2 %shard_map.147 = (f32[2,64,1024]{2,1,0:T(8,128)}, f32[32,2048]{1,0:T(8,128)}, f32[32,1024]{1,0:T(8,128)}, f32[32,100]{1,0:T(8,128)}) custom-call(f32[2,64,1024]{2,1,0:T(8,128)S(1)} %get-tuple-element.101.own_hidden_ref, bf16[128,1024]{1,0:T(8,128)(2,1)S(1)} %collective-permute-done.10.mate_ref, bf16[64,1024]{1,0:T(8,128)(2,1)S(1)} %collective-permute-done.19.other_ref, ...), custom_call_target="tpu_custom_call" | custom-call | flops 1 | bytes 1 | tf_op jit(solution)/shard_map/pallas_call | solution.py:28
  (42 shorter events, 0.6 us)
Async XLA Ops:
  0.6 4.9 %copy-start.3 = (bf16[1024,100]{0,1:T(8,128)(2,1)S(1)}, bf16[1024,100]{0,1:T(8,128)(2,1)}, u32[]{:S(2)}) copy-start(bf16[1024,100]{0,1:T(8,128)(2,1)} %param.15) | copy-start | bytes 614404
  0.6 4.9 %copy-start.8 = (f32[100]{0:T(128)S(1)}, f32[100]{0:T(128)}, u32[]{:S(2)}) copy-start(f32[100]{0:T(128)} %param.19) | copy-start | bytes 1204
  0.7 4.9 %copy-start.7 = (f32[256]{0:T(256)S(1)}, f32[256]{0:T(256)}, u32[]{:S(2)}) copy-start(f32[256]{0:T(256)} %param.18) | copy-start | bytes 3076
  0.7 4.9 %copy-start.2 = (bf16[256,1024]{1,0:T(8,128)(2,1)S(1)}, bf16[256,1024]{1,0:T(8,128)(2,1)}, u32[]{:S(2)}) copy-start(bf16[256,1024]{1,0:T(8,128)(2,1)} %q_ref.7) | copy-start | bytes 1572868
  0.7 4.9 %copy-start.1 = (bf16[1024,1024]{1,0:T(8,128)(2,1)S(1)}, bf16[1024,1024]{1,0:T(8,128)(2,1)}, u32[]{:S(2)}) copy-start(bf16[1024,1024]{1,0:T(8,128)(2,1)} %wo_ref.3) | copy-start | bytes 6291460
  0.7 4.9 %copy-start.5 = (f32[100,256]{1,0:T(8,128)S(1)}, f32[100,256]{1,0:T(8,128)}, u32[]{:S(2)}) copy-start(f32[100,256]{1,0:T(8,128)} %init_ref.1) | copy-start | bytes 307204
  0.7 4.9 %copy-start.6 = (s32[3,256]{1,0:T(4,128)S(1)}, s32[3,256]{1,0:T(4,128)}, u32[]{:S(2)}) copy-start(s32[3,256]{1,0:T(4,128)} %src_ref.3) | copy-start | bytes 9220
  0.7 4.9 %copy-start = (bf16[1024,2048]{1,0:T(8,128)(2,1)S(1)}, bf16[1024,2048]{1,0:T(8,128)(2,1)}, u32[]{:S(2)}) copy-start(bf16[1024,2048]{1,0:T(8,128)(2,1)} %kvw_ref.5) | copy-start | bytes 12582916
  2.1 6.6 %collective-permute-start = (bf16[64,1024]{1,0:T(8,128)(2,1)S(1)}, bf16[64,1024]{1,0:T(8,128)(2,1)S(1)}, u32[]{:S(2)}, u32[]{:S(2)}) collective-permute-start(bf16[64,1024]{1,0:T(8,128)(2,1)S(1)} %get-tuple-element.62), channel_id=1, source_target_pairs={{0,7},{1,2},{2,1},{3,4},{4,3},{5,6},{6,5},{7,0},{8,15},{9,10},{10,... | collective-permute-start | bytes 393224 | tf_op jit(solution)/shard_map/ppermute | solution.py:449
  5.5 3.2 %collective-permute-start.1 = (bf16[64,1024]{1,0:T(8,128)(2,1)S(1)}, bf16[64,1024]{1,0:T(8,128)(2,1)S(1)}, u32[]{:S(2)}, u32[]{:S(2)}) collective-permute-start(bf16[64,1024]{1,0:T(8,128)(2,1)S(1)} %get-tuple-element.63), channel_id=1, source_target_pairs={{0,1},{1,0},{2,3},{3,2},{4,5},{5,4},{6,7},{7,6},{8,9},{9,8},{10,11... | collective-permute-start | bytes 393224 | tf_op jit(solution)/shard_map/ppermute | solution.py:450
  8.7 14.1 %copy-start.4 = (f32[100,256]{1,0:T(8,128)S(1)}, f32[100,256]{1,0:T(8,128)}, u32[]{:S(2)}) copy-start(f32[100,256]{1,0:T(8,128)} %refs_5_.1) | copy-start | bytes 307204
  10.5 8.2 %collective-permute-start.2 = (bf16[200,256]{1,0:T(8,128)(2,1)S(1)}, bf16[200,256]{1,0:T(8,128)(2,1)S(1)}, u32[]{:S(2)}, u32[]{:S(2)}) collective-permute-start(bf16[200,256]{1,0:T(8,128)(2,1)S(1)} %get-tuple-element.68), channel_id=1, source_target_pairs={{0,24},{8,16},{16,8},{24,0},{1,25},{9,17},{17,9},{25,1},{2,26},{10... | collective-permute-start | bytes 307208 | tf_op jit(solution)/shard_map/ppermute | solution.py:487
  15.6 7.3 %collective-permute-start.3 = (bf16[200,256]{1,0:T(8,128)(2,1)S(1)}, bf16[200,256]{1,0:T(8,128)(2,1)S(1)}, u32[]{:S(2)}, u32[]{:S(2)}) collective-permute-start(bf16[200,256]{1,0:T(8,128)(2,1)S(1)} %get-tuple-element.68), channel_id=1, source_target_pairs={{0,16},{8,24},{16,0},{24,8},{1,17},{9,25},{17,1},{25,9},{2,18},{10... | collective-permute-start | bytes 307208 | tf_op jit(solution)/shard_map/ppermute | solution.py:487
  15.6 7.3 %collective-permute-start.4 = (bf16[200,256]{1,0:T(8,128)(2,1)S(1)}, bf16[200,256]{1,0:T(8,128)(2,1)S(1)}, u32[]{:S(2)}, u32[]{:S(2)}) collective-permute-start(bf16[200,256]{1,0:T(8,128)(2,1)S(1)} %get-tuple-element.68), channel_id=1, source_target_pairs={{0,8},{8,0},{16,24},{24,16},{1,9},{9,1},{17,25},{25,17},{2,10},{10... | collective-permute-start | bytes 307208 | tf_op jit(solution)/shard_map/ppermute | solution.py:487
  24.7 5.2 %collective-permute-start.5 = (bf16[512,768]{1,0:T(8,128)(2,1)S(1)}, bf16[512,768]{1,0:T(8,128)(2,1)S(1)}, u32[]{:S(2)}, u32[]{:S(2)}) collective-permute-start(bf16[512,768]{1,0:T(8,128)(2,1)S(1)} %get-tuple-element.83), channel_id=1, source_target_pairs={{0,1},{1,0},{2,3},{3,2},{4,5},{5,4},{6,7},{7,6},{8,9},{9,8},{10,11... | collective-permute-start | bytes 2359304 | tf_op jit(solution)/shard_map/ppermute | solution.py:405
  26.3 3.7 %collective-permute-start.6 = (bf16[512,768]{1,0:T(8,128)(2,1)S(1)}, bf16[512,768]{1,0:T(8,128)(2,1)S(1)}, u32[]{:S(2)}, u32[]{:S(2)}) collective-permute-start(bf16[512,768]{1,0:T(8,128)(2,1)S(1)} %get-tuple-element.85), channel_id=1, source_target_pairs={{0,1},{1,0},{2,3},{3,2},{4,5},{5,4},{6,7},{7,6},{8,9},{9,8},{10,11... | collective-permute-start | bytes 2359304 | tf_op jit(solution)/shard_map/ppermute | solution.py:405
  28.2 2.9 %collective-permute-start.7 = (bf16[512,512]{1,0:T(8,128)(2,1)S(1)}, bf16[512,512]{1,0:T(8,128)(2,1)S(1)}, u32[]{:S(2)}, u32[]{:S(2)}) collective-permute-start(bf16[512,512]{1,0:T(8,128)(2,1)S(1)} %get-tuple-element.90), channel_id=1, source_target_pairs={{0,1},{1,0},{2,3},{3,2},{4,5},{5,4},{6,7},{7,6},{8,9},{9,8},{10,11... | collective-permute-start | bytes 1572872 | tf_op jit(solution)/shard_map/ppermute | solution.py:405
  29.4 1.7 %collective-permute-start.8 = (bf16[512,256]{1,0:T(8,128)(2,1)S(1)}, bf16[512,256]{1,0:T(8,128)(2,1)S(1)}, u32[]{:S(2)}, u32[]{:S(2)}) collective-permute-start(bf16[512,256]{1,0:T(8,128)(2,1)S(1)} %get-tuple-element.93), channel_id=1, source_target_pairs={{0,1},{1,0},{2,3},{3,2},{4,5},{5,4},{6,7},{7,6},{8,9},{9,8},{10,11... | collective-permute-start | bytes 786440 | tf_op jit(solution)/shard_map/ppermute | solution.py:405
  31.3 11.5 %collective-permute-start.11 = (bf16[256,768]{1,0:T(8,128)(2,1)S(1)}, bf16[256,768]{1,0:T(8,128)(2,1)S(1)}, u32[]{:S(2)}, u32[]{:S(2)}) collective-permute-start(bf16[256,768]{1,0:T(8,128)(2,1)S(1)} %add_convert_fusion.1), channel_id=1, source_target_pairs={{0,2},{1,3},{2,0},{3,1},{4,6},{5,7},{6,4},{7,5},{8,10},{9,11},{10,... | collective-permute-start | bytes 1179656 | tf_op jit(solution)/shard_map/ppermute | solution.py:405
  33.3 11.0 %collective-permute-start.12 = (bf16[256,768]{1,0:T(8,128)(2,1)S(1)}, bf16[256,768]{1,0:T(8,128)(2,1)S(1)}, u32[]{:S(2)}, u32[]{:S(2)}) collective-permute-start(bf16[256,768]{1,0:T(8,128)(2,1)S(1)} %add_convert_fusion), channel_id=1, source_target_pairs={{0,4},{1,5},{2,6},{3,7},{4,0},{5,1},{6,2},{7,3},{8,12},{9,13},{10,... | collective-permute-start | bytes 1179656 | tf_op jit(solution)/shard_map/ppermute | solution.py:405
  34.9 10.8 %collective-permute-start.9 = (bf16[256,768]{1,0:T(8,128)(2,1)S(1)}, bf16[256,768]{1,0:T(8,128)(2,1)S(1)}, u32[]{:S(2)}, u32[]{:S(2)}) collective-permute-start(bf16[256,768]{1,0:T(8,128)(2,1)S(1)} %pad_maximum_fusion.2), channel_id=1, source_target_pairs={{0,8},{8,0},{16,24},{24,16},{1,9},{9,1},{17,25},{25,17},{2,10},{10... | collective-permute-start | bytes 1179656 | tf_op jit(solution)/shard_map/ppermute | solution.py:405
  36.7 7.6 %collective-permute-start.10 = (bf16[128,1024]{1,0:T(8,128)(2,1)S(1)}, bf16[128,1024]{1,0:T(8,128)(2,1)S(1)}, u32[]{:S(2)}, u32[]{:S(2)}) collective-permute-start(bf16[128,1024]{1,0:T(8,128)(2,1)S(1)} %get-tuple-element.103), channel_id=1, source_target_pairs={{0,1},{1,0},{2,3},{3,2},{4,5},{5,4},{6,7},{7,6},{8,9},{9,8},{10,11... | collective-permute-start | bytes 786440 | tf_op jit(solution)/shard_map/ppermute | solution.py:547
  45.8 5.8 %collective-permute-start.17 = (bf16[128,768]{1,0:T(8,128)(2,1)S(1)}, bf16[128,768]{1,0:T(8,128)(2,1)S(1)}, u32[]{:S(2)}, u32[]{:S(2)}) collective-permute-start(bf16[128,768]{1,0:T(8,128)(2,1)S(1)} %add_convert_fusion.3), channel_id=1, source_target_pairs={{0,2},{1,3},{2,0},{3,1},{4,6},{5,7},{6,4},{7,5},{8,10},{9,11},{10,... | collective-permute-start | bytes 589832 | tf_op jit(solution)/shard_map/ppermute | solution.py:405
  46.7 5.7 %collective-permute-start.15 = (bf16[128,768]{1,0:T(8,128)(2,1)S(1)}, bf16[128,768]{1,0:T(8,128)(2,1)S(1)}, u32[]{:S(2)}, u32[]{:S(2)}) collective-permute-start(bf16[128,768]{1,0:T(8,128)(2,1)S(1)} %add_convert_fusion.4), channel_id=1, source_target_pairs={{0,8},{8,0},{16,24},{24,16},{1,9},{9,1},{17,25},{25,17},{2,10},{10... | collective-permute-start | bytes 589832 | tf_op jit(solution)/shard_map/ppermute | solution.py:405
  47.2 6.5 %collective-permute-start.13 = (bf16[128,768]{1,0:T(8,128)(2,1)S(1)}, bf16[128,768]{1,0:T(8,128)(2,1)S(1)}, u32[]{:S(2)}, u32[]{:S(2)}) collective-permute-start(bf16[128,768]{1,0:T(8,128)(2,1)S(1)} %add_convert_fusion.5), channel_id=1, source_target_pairs={{0,4},{1,5},{2,6},{3,7},{4,0},{5,1},{6,2},{7,3},{8,12},{9,13},{10,... | collective-permute-start | bytes 589832 | tf_op jit(solution)/shard_map/ppermute | solution.py:405
  51.7 4.7 %collective-permute-start.18 = (bf16[64,768]{1,0:T(8,128)(2,1)S(1)}, bf16[64,768]{1,0:T(8,128)(2,1)S(1)}, u32[]{:S(2)}, u32[]{:S(2)}) collective-permute-start(bf16[64,768]{1,0:T(8,128)(2,1)S(1)} %add_convert_fusion.7), channel_id=1, source_target_pairs={{0,4},{1,5},{2,6},{3,7},{4,0},{5,1},{6,2},{7,3},{8,12},{9,13},{10,... | collective-permute-start | bytes 294920 | tf_op jit(solution)/shard_map/ppermute | solution.py:405
  52.5 4.7 %collective-permute-start.16 = (bf16[64,768]{1,0:T(8,128)(2,1)S(1)}, bf16[64,768]{1,0:T(8,128)(2,1)S(1)}, u32[]{:S(2)}, u32[]{:S(2)}) collective-permute-start(bf16[64,768]{1,0:T(8,128)(2,1)S(1)} %add_convert_fusion.8), channel_id=1, source_target_pairs={{0,2},{1,3},{2,0},{3,1},{4,6},{5,7},{6,4},{7,5},{8,10},{9,11},{10,... | collective-permute-start | bytes 294920 | tf_op jit(solution)/shard_map/ppermute | solution.py:405
  53.8 4.7 %collective-permute-start.14 = (bf16[64,768]{1,0:T(8,128)(2,1)S(1)}, bf16[64,768]{1,0:T(8,128)(2,1)S(1)}, u32[]{:S(2)}, u32[]{:S(2)}) collective-permute-start(bf16[64,768]{1,0:T(8,128)(2,1)S(1)} %add_convert_fusion.9), channel_id=1, source_target_pairs={{0,8},{8,0},{16,24},{24,16},{1,9},{9,1},{17,25},{25,17},{2,10},{10... | collective-permute-start | bytes 294920 | tf_op jit(solution)/shard_map/ppermute | solution.py:405
  58.8 9.5 %collective-permute-start.20 = (bf16[32,2304]{1,0:T(8,128)(2,1)S(1)}, bf16[32,2304]{1,0:T(8,128)(2,1)S(1)}, u32[]{:S(2)}, u32[]{:S(2)}) collective-permute-start(bf16[32,2304]{1,0:T(8,128)(2,1)S(1)} %slice.277), channel_id=1, source_target_pairs={{0,16},{8,24},{16,0},{24,8},{1,17},{9,25},{17,1},{25,9},{2,18},{10... | collective-permute-start | bytes 442376 | tf_op jit(solution)/shard_map/ppermute | solution.py:405
  62.4 5.9 %collective-permute-start.19 = (bf16[64,1024]{1,0:T(8,128)(2,1)S(1)}, bf16[64,1024]{1,0:T(8,128)(2,1)S(1)}, u32[]{:S(2)}, u32[]{:S(2)}) collective-permute-start(bf16[64,1024]{1,0:T(8,128)(2,1)S(1)} %slice.205), channel_id=1, source_target_pairs={{0,2},{1,7},{2,4},{3,1},{4,6},{5,3},{6,0},{7,5},{8,10},{9,15},{10,... | collective-permute-start | bytes 393224 | tf_op jit(solution)/shard_map/ppermute | solution.py:553

commit v18 on v14

--- a/solution.py
+++ b/solution.py
@@ -523,15 +523,17 @@
                 [sds((members, nodes, width), F32), sds((2 * members * rim, width), BF)],
                 (ng_first, ng_last, ng_value, kv_weight),
             )
+        if step == steps - 1:
+            onward = lower([from_mate])[0]
+            outgoing[0], onward = lax.optimization_barrier((outgoing[0], onward))
+            chips_on = [(i, (i + 2 - i % 2 * 4) % n_band) for i in range(n_band)]
+            from_other = lax.ppermute(onward, "band", chips_on)
         arrived = [swap(out, *turn[step], count[turn[step][0]]) for out, turn in zip(outgoing, turns)]
         if step == 0:
             from_mate = lax.ppermute(back, "band", mates)
             arrived, from_mate = lax.optimization_barrier((arrived, from_mate))
         if step == steps - 1:
-            onward = lower([from_mate])[0]
-            arrived, onward = lax.optimization_barrier((arrived, onward))
-            chips_on = [(i, (i + 2 - i % 2 * 4) % n_band) for i in range(n_band)]
-            from_other = lax.ppermute(onward, "band", chips_on)
+            arrived, from_other = lax.optimization_barrier((arrived, from_other))
         groups = [lower(terms) + [new] for terms, new in zip(groups, arrived)]
     terms = [jnp.concatenate([add_up(*group) for group in groups], axis=1)]
     for axis, bit in rest:

time: 68.7 us -> 70.7 us (1.029)
  waiting for transfers between devices: 28.3 us -> 29.5 us
  starting transfers between devices: 24.7 us -> 25.5 us
    ppermute x13, waiting for transfers between devices: 15.1 us -> 20.9 us  [swap(): return lax.ppermute(rows, axis, [(i, i ^ 1 << bit) for i in range(count)])]
    ppermute x1, waiting for transfers between devices: 4.63 us -> 0.01 us  [shards(): from_other = lax.ppermute(onward, 'band', chips_on)]
    ppermute x13, starting transfers between devices: 14.3 us -> 15.1 us  [swap(): return lax.ppermute(rows, axis, [(i, i ^ 1 << bit) for i in range(count)])]
  transfers between devices with their start and end apart: 20 -> 20, of which waited for: 14 -> 13; matrix products, arithmetic and copies ran while one was open for 1% -> 1% of each run, Pallas kernels for 11% -> 10%
where the time goes in v18:
time: 70.7 us; the launch traced here: 70.6 us
  waiting for transfers between devices  29.5 us (42%)
  starting transfers between devices  25.5 us (36%)
  Pallas kernels  13.5 us (19%)
  other arithmetic  0.96 us (1%)
  between operations  0.9 us (1%)
    ppermute x13, waiting for transfers between devices, swap(): return lax.ppermute(rows, axis, [(i, i ^ 1 << bit) for i in range(count)])  20.9 us
    ppermute x13, starting transfers between devices, swap(): return lax.ppermute(rows, axis, [(i, i ^ 1 << bit) for i in range(count)])  15.1 us
    pallas_call x9, Pallas kernels, call(): pl.pallas_call(body, out_shape=out_shape, in_specs=[pl.BlockSpec(memory_s...  13.5 us
    ppermute x3, waiting for transfers between devices, shards(): lax.ppermute(sent, 'member', [(i, i ^ s) for i in range(n_member)])  6.35 us
    ppermute x3, starting transfers between devices, shards(): lax.ppermute(sent, 'member', [(i, i ^ s) for i in range(n_member)])  5.79 us
    ppermute x1, starting transfers between devices, shards(): other = lax.ppermute(for_other, 'band', others)  3.4 us
    ppermute x1, waiting for transfers between devices, shards(): from_mate = lax.ppermute(back, 'band', mates)  1.52 us
  transfers between devices with their start and end apart: 20, of which 13 were waited for; matrix products, arithmetic and copies ran while one was open for 1% of the time, Pallas kernels for 10%

profile of v18, /device:TPU:0, one launch (start us, length us, event | category | flops | bytes accessed | tf_op | source)
XLA Modules:
  0.0 70.6 jit_solution(1218588061776776338)
XLA Ops:
  0.7 1.4 %shard_map.138 = (bf16[2,64,1024]{2,1,0:T(8,128)(2,1)S(1)}, s32[2,32]{1,0:T(2,128)S(1)}, bf16[64,1024]{1,0:T(8,128)(2,1)S(1)}, bf16[64,1024]{1,0:T(8,128)(2,1)S(1)}) custom-call(bf16[2,64,1024]{2,1,0:T(8,128)(2,1)} %hidden_hbm.1, s32[2,32]{1,0:T(2,128)} %halo_hbm.1), custom_call_target="tpu_custom_call" | custom-call | flops 10000000000 | bytes 1 | tf_op jit(solution)/shard_map/pallas_call | solution.py:28
  2.1 3.4 %collective-permute-start = (bf16[64,1024]{1,0:T(8,128)(2,1)S(1)}, bf16[64,1024]{1,0:T(8,128)(2,1)S(1)}, u32[]{:S(2)}, u32[]{:S(2)}) collective-permute-start(bf16[64,1024]{1,0:T(8,128)(2,1)S(1)} %get-tuple-element.55), channel_id=1, source_target_pairs={{0,7},{1,2},{2,1},{3,4},{4,3},{5,6},{6,5},{7,0},{8,15},{9,10},{10,... | collective-permute-start | bytes 393224 | tf_op jit(solution)/shard_map/ppermute | solution.py:437
  5.6 2.4 %shard_map.139 = (bf16[2,64,1024]{2,1,0:T(8,128)(2,1)S(1)}, bf16[8,2,128,256]{3,2,1,0:T(8,128)(2,1)S(1)}, bf16[8,2,128,256]{3,2,1,0:T(8,128)(2,1)S(1)}, f32[2,10...) custom-call(bf16[2,64,1024]{2,1,0:T(8,128)(2,1)S(1)} %get-tuple-elem, ...), custom_call_target="tpu_custom_call" | custom-call | flops 1 | bytes 1 | tf_op jit(solution)/shard_map/pallas_call | solution.py:28
  8.0 0.7 %collective-permute-done.other_ref = bf16[64,1024]{1,0:T(8,128)(2,1)S(1)} collective-permute-done((bf16[64,1024]{1,0:T(8,128)(2,1)S(1)}, bf16[64,1024]{1,0:T(8,128)(2,1)S(1)}, u32[]{:S(2)}, u32[]{:S(2)}) %collective-permute-start) | collective-permute-done | bytes 131104 | tf_op jit(solution)/shard_map/ppermute | solution.py:437
  8.7 1.7 %shard_map.140 = (bf16[2,64,1024]{2,1,0:T(8,128)(2,1)S(1)}, bf16[8,2,128,256]{3,2,1,0:T(8,128)(2,1)S(1)}, bf16[8,2,128,256]{3,2,1,0:T(8,128)(2,1)S(1)}, bf16[2,1...) custom-call(bf16[64,1024]{1,0:T(8,128)(2,1)S(1)} %collective-permute-done.other_ref, ...), custom_call_target="tpu_custom_call" | custom-call | flops 1 | bytes 1 | tf_op jit(solution)/shard_map/pallas_call | solution.py:28
  10.4 5.2 %collective-permute-start.2 = (bf16[200,256]{1,0:T(8,128)(2,1)S(1)}, bf16[200,256]{1,0:T(8,128)(2,1)S(1)}, u32[]{:S(2)}, u32[]{:S(2)}) collective-permute-start(bf16[200,256]{1,0:T(8,128)(2,1)S(1)} %get-tuple-element.61), channel_id=1, source_target_pairs={{0,24},{8,16},{16,8},{24,0},{1,25},{9,17},{17,9},{25,1},{2,26},{10... | collective-permute-start | bytes 307208 | tf_op jit(solution)/shard_map/ppermute | solution.py:475
  15.6 0.6 collective-permute-start.4
  16.2 0.3 shard_map.141.refs_10_.ext_ref
  16.5 2.1 %collective-permute-done.2.refs_0_ = bf16[200,256]{1,0:T(8,128)(2,1)S(1)} collective-permute-done((bf16[200,256]{1,0:T(8,128)(2,1)S(1)}, bf16[200,256]{1,0:T(8,128)(2,1)S(1)}, u32[]{:S(2)}, u32[]{:S(2)}) %collective-permute-start.2) | collective-permute-done | bytes 102432 | tf_op jit(solution)/shard_map/ppermute | solution.py:475
  18.6 4.2 %collective-permute-done.3.refs_1_ = bf16[200,256]{1,0:T(8,128)(2,1)S(1)} collective-permute-done((bf16[200,256]{1,0:T(8,128)(2,1)S(1)}, bf16[200,256]{1,0:T(8,128)(2,1)S(1)}, u32[]{:S(2)}, u32[]{:S(2)}) %collective-permute-start.3) | collective-permute-done | bytes 102432 | tf_op jit(solution)/shard_map/ppermute | solution.py:475
  22.9 1.9 %shard_map.142 = (bf16[2,128,256]{2,1,0:T(8,128)(2,1)S(1)}, bf16[256,1024]{1,0:T(8,128)(2,1)S(1)}, bf16[512,768]{1,0:T(8,128)(2,1)S(1)}, bf16[512,768]{1,0:T(8,128)(2,1)S(1)}) custom-call(bf16[200,256]{1,0:T(8,128)(2,1)S(1)} %collective-permute-done.2.refs_0_, bf16[200,256]{1,0:T(8,128)(2,1)S(1)} %collective-permute-done.3.refs_1_, ...), custom_call_target="tpu_custom_call" | custom-call | flops 1 | bytes 1 | tf_op jit(solution)/shard_map/pallas_call | solution.py:28
  24.7 0.1 collective-permute-start.5
  24.8 1.5 %shard_map.143 = (bf16[256,512]{1,0:T(8,128)(2,1)S(1)}, bf16[512,768]{1,0:T(8,128)(2,1)S(1)}, bf16[512,768]{1,0:T(8,128)(2,1)S(1)}) custom-call(bf16[2,128,256]{2,1,0:T(8,128)(2,1)S(1)} %get-tuple-element.67.grad_ref, bf16[1024,128]{1,0:T(8,128)(2,1)S(1)} %get-tuple-element.68.pt_ref, bf16[2,64,1024]{2,1,0:T(8,128)(2,1)S(1)} %get-tuple-element.69.own_value_ref, ...), custom_call_target="tpu_custom_call" | custom-call | flops 1 | bytes 1 | tf_op jit(solution)/shard_map/pallas_call | solution.py:28
  26.3 0.6 collective-permute-start.6
  26.8 1.9 %shard_map.144 = (bf16[256,512]{1,0:T(8,128)(2,1)S(1)}, bf16[512,768]{1,0:T(8,128)(2,1)S(1)}, bf16[512,768]{1,0:T(8,128)(2,1)S(1)}) custom-call(bf16[2,128,256]{2,1,0:T(8,128)(2,1)S(1)} %get-tuple-element.67.grad_ref, bf16[1024,128]{1,0:T(8,128)(2,1)S(1)} %get-tuple-element.68.pt_ref, bf16[2,64,1024]{2,1,0:T(8,128)(2,1)S(1)} %get-tuple-element.69.own_value_ref, ...), custom_call_target="tpu_custom_call" | custom-call | flops 1 | bytes 1 | tf_op jit(solution)/shard_map/pallas_call | solution.py:28
  28.8 0.1 collective-permute-start.7
  28.9 0.1 add_convert_fusion.2
  29.0 0.1 add_convert_fusion.1
  29.1 2.0 %collective-permute-done.7 = bf16[512,768]{1,0:T(8,128)(2,1)S(1)} collective-permute-done((bf16[512,768]{1,0:T(8,128)(2,1)S(1)}, bf16[512,768]{1,0:T(8,128)(2,1)S(1)}, u32[]{:S(2)}, u32[]{:S(2)}) %collective-permute-start.7) | collective-permute-done | bytes 786464 | tf_op jit(solution)/shard_map/ppermute | solution.py:401
  31.1 0.1 add_convert_fusion
  31.2 0.5 collective-permute-start.10
  31.8 1.7 %collective-permute-start.8 = (bf16[256,768]{1,0:T(8,128)(2,1)S(1)}, bf16[256,768]{1,0:T(8,128)(2,1)S(1)}, u32[]{:S(2)}, u32[]{:S(2)}) collective-permute-start(bf16[256,768]{1,0:T(8,128)(2,1)S(1)} %add_convert_fusion.2), channel_id=1, source_target_pairs={{0,2},{1,3},{2,0},{3,1},{4,6},{5,7},{6,4},{7,5},{8,10},{9,11},{10,... | collective-permute-start | bytes 1179656 | tf_op jit(solution)/shard_map/ppermute | solution.py:401
  33.4 1.8 %collective-permute-start.9 = (bf16[256,768]{1,0:T(8,128)(2,1)S(1)}, bf16[256,768]{1,0:T(8,128)(2,1)S(1)}, u32[]{:S(2)}, u32[]{:S(2)}) collective-permute-start(bf16[256,768]{1,0:T(8,128)(2,1)S(1)} %add_convert_fusion.1), channel_id=1, source_target_pairs={{0,4},{1,5},{2,6},{3,7},{4,0},{5,1},{6,2},{7,3},{8,12},{9,13},{10,... | collective-permute-start | bytes 1179656 | tf_op jit(solution)/shard_map/ppermute | solution.py:401
  35.3 1.3 %shard_map.145 = (f32[2,64,1024]{2,1,0:T(8,128)S(1)}, bf16[128,1024]{1,0:T(8,128)(2,1)S(1)}) custom-call(bf16[256,512]{1,0:T(8,128)(2,1)S(1)} %get-tuple-element.74.first_ref, bf16[256,512]{1,0:T(8,128)(2,1)S(1)} %get-tuple-element.89.last_ref, bf16[256,1024]{1,0:T(8,128)(2,1)S(1)} %get-tuple-element.73.ngv_ref, bf16[1024,2048]{1,0:T(8,128)(2,1)S(1)} %copy-done), custom_call_target="tpu_custom_call" | custom-call | flops 1 | bytes 1 | tf_op jit(solution)/shard_map/pallas_call | solution.py:28
  36.6 0.1 collective-permute-start.11
  36.7 1.5 %collective-permute-done.11.mate_ref = bf16[128,1024]{1,0:T(8,128)(2,1)S(1)} collective-permute-done((bf16[128,1024]{1,0:T(8,128)(2,1)S(1)}, bf16[128,1024]{1,0:T(8,128)(2,1)S(1)}, u32[]{:S(2)}, u32[]{:S(2)}) %collective-permute-start.11) | collective-permute-done | bytes 262176 | tf_op jit(solution)/shard_map/ppermute | solution.py:533
  38.2 4.3 %collective-permute-done.10 = bf16[256,768]{1,0:T(8,128)(2,1)S(1)} collective-permute-done((bf16[256,768]{1,0:T(8,128)(2,1)S(1)}, bf16[256,768]{1,0:T(8,128)(2,1)S(1)}, u32[]{:S(2)}, u32[]{:S(2)}) %collective-permute-start.10) | collective-permute-done | bytes 393248 | tf_op jit(solution)/shard_map/ppermute | solution.py:401
  42.5 0.3 collective-permute-done.8
  42.8 1.5 %collective-permute-done.9 = bf16[256,768]{1,0:T(8,128)(2,1)S(1)} collective-permute-done((bf16[256,768]{1,0:T(8,128)(2,1)S(1)}, bf16[256,768]{1,0:T(8,128)(2,1)S(1)}, u32[]{:S(2)}, u32[]{:S(2)}) %collective-permute-start.9) | collective-permute-done | bytes 393248 | tf_op jit(solution)/shard_map/ppermute | solution.py:401
  44.3 0.1 add_convert_fusion.3
  44.3 0.8 %collective-permute-start.16 = (bf16[128,768]{1,0:T(8,128)(2,1)S(1)}, bf16[128,768]{1,0:T(8,128)(2,1)S(1)}, u32[]{:S(2)}, u32[]{:S(2)}) collective-permute-start(bf16[128,768]{1,0:T(8,128)(2,1)S(1)} %add_convert_fusion.3), channel_id=1, source_target_pairs={{0,2},{1,3},{2,0},{3,1},{4,6},{5,7},{6,4},{7,5},{8,10},{9,11},{10,... | collective-permute-start | bytes 589832 | tf_op jit(solution)/shard_map/ppermute | solution.py:401
  45.1 0.1 add_convert_fusion.4
  45.2 1.7 %collective-permute-start.14 = (bf16[128,768]{1,0:T(8,128)(2,1)S(1)}, bf16[128,768]{1,0:T(8,128)(2,1)S(1)}, u32[]{:S(2)}, u32[]{:S(2)}) collective-permute-start(bf16[128,768]{1,0:T(8,128)(2,1)S(1)} %add_convert_fusion.4), channel_id=1, source_target_pairs={{0,8},{8,0},{16,24},{24,16},{1,9},{9,1},{17,25},{25,17},{2,10},{10... | collective-permute-start | bytes 589832 | tf_op jit(solution)/shard_map/ppermute | solution.py:401
  46.9 0.1 add_convert_fusion.5
  46.9 1.8 %collective-permute-start.12 = (bf16[128,768]{1,0:T(8,128)(2,1)S(1)}, bf16[128,768]{1,0:T(8,128)(2,1)S(1)}, u32[]{:S(2)}, u32[]{:S(2)}) collective-permute-start(bf16[128,768]{1,0:T(8,128)(2,1)S(1)} %add_convert_fusion.5), channel_id=1, source_target_pairs={{0,4},{1,5},{2,6},{3,7},{4,0},{5,1},{6,2},{7,3},{8,12},{9,13},{10,... | collective-permute-start | bytes 589832 | tf_op jit(solution)/shard_map/ppermute | solution.py:401
  48.8 1.4 %collective-permute-done.16 = bf16[128,768]{1,0:T(8,128)(2,1)S(1)} collective-permute-done((bf16[128,768]{1,0:T(8,128)(2,1)S(1)}, bf16[128,768]{1,0:T(8,128)(2,1)S(1)}, u32[]{:S(2)}, u32[]{:S(2)}) %collective-permute-start.16) | collective-permute-done | bytes 196640 | tf_op jit(solution)/shard_map/ppermute | solution.py:401
  50.2 1.6 %collective-permute-start.17 = (bf16[64,768]{1,0:T(8,128)(2,1)S(1)}, bf16[64,768]{1,0:T(8,128)(2,1)S(1)}, u32[]{:S(2)}, u32[]{:S(2)}) collective-permute-start(bf16[64,768]{1,0:T(8,128)(2,1)S(1)} %add_convert_fusion.6), channel_id=1, source_target_pairs={{0,4},{1,5},{2,6},{3,7},{4,0},{5,1},{6,2},{7,3},{8,12},{9,13},{10,... | collective-permute-start | bytes 294920 | tf_op jit(solution)/shard_map/ppermute | solution.py:401
  51.8 1.9 %collective-permute-done.12 = bf16[128,768]{1,0:T(8,128)(2,1)S(1)} collective-permute-done((bf16[128,768]{1,0:T(8,128)(2,1)S(1)}, bf16[128,768]{1,0:T(8,128)(2,1)S(1)}, u32[]{:S(2)}, u32[]{:S(2)}) %collective-permute-start.12) | collective-permute-done | bytes 196640 | tf_op jit(solution)/shard_map/ppermute | solution.py:401
  53.8 1.2 %collective-permute-start.18 = (bf16[64,1024]{1,0:T(8,128)(2,1)S(1)}, bf16[64,1024]{1,0:T(8,128)(2,1)S(1)}, u32[]{:S(2)}, u32[]{:S(2)}) collective-permute-start(bf16[64,1024]{1,0:T(8,128)(2,1)S(1)} %slice.185), channel_id=1, source_target_pairs={{0,2},{1,7},{2,4},{3,1},{4,6},{5,3},{6,0},{7,5},{8,10},{9,15},{10,... | collective-permute-start | bytes 393224 | tf_op jit(solution)/shard_map/ppermute | solution.py:530
  55.1 1.7 %collective-permute-start.15 = (bf16[64,768]{1,0:T(8,128)(2,1)S(1)}, bf16[64,768]{1,0:T(8,128)(2,1)S(1)}, u32[]{:S(2)}, u32[]{:S(2)}) collective-permute-start(bf16[64,768]{1,0:T(8,128)(2,1)S(1)} %add_convert_fusion.7), channel_id=1, source_target_pairs={{0,2},{1,3},{2,0},{3,1},{4,6},{5,7},{6,4},{7,5},{8,10},{9,11},{10,... | collective-permute-start | bytes 294920 | tf_op jit(solution)/shard_map/ppermute | solution.py:401
  56.8 0.8 %collective-permute-start.13 = (bf16[64,768]{1,0:T(8,128)(2,1)S(1)}, bf16[64,768]{1,0:T(8,128)(2,1)S(1)}, u32[]{:S(2)}, u32[]{:S(2)}) collective-permute-start(bf16[64,768]{1,0:T(8,128)(2,1)S(1)} %add_convert_fusion.8), channel_id=1, source_target_pairs={{0,8},{8,0},{16,24},{24,16},{1,9},{9,1},{17,25},{25,17},{2,10},{10... | collective-permute-start | bytes 294920 | tf_op jit(solution)/shard_map/ppermute | solution.py:401
  57.6 3.1 %collective-permute-done.15 = bf16[64,768]{1,0:T(8,128)(2,1)S(1)} collective-permute-done((bf16[64,768]{1,0:T(8,128)(2,1)S(1)}, bf16[64,768]{1,0:T(8,128)(2,1)S(1)}, u32[]{:S(2)}, u32[]{:S(2)}) %collective-permute-start.15) | collective-permute-done | bytes 98336 | tf_op jit(solution)/shard_map/ppermute | solution.py:401
  60.6 0.7 %collective-permute-done.13 = bf16[64,768]{1,0:T(8,128)(2,1)S(1)} collective-permute-done((bf16[64,768]{1,0:T(8,128)(2,1)S(1)}, bf16[64,768]{1,0:T(8,128)(2,1)S(1)}, u32[]{:S(2)}, u32[]{:S(2)}) %collective-permute-start.13) | collective-permute-done | bytes 98336 | tf_op jit(solution)/shard_map/ppermute | solution.py:401
  61.4 0.1 convert_add_fusion.2
  61.5 0.1 convert_add_fusion
  61.7 1.9 %collective-permute-start.19 = (bf16[32,2304]{1,0:T(8,128)(2,1)S(1)}, bf16[32,2304]{1,0:T(8,128)(2,1)S(1)}, u32[]{:S(2)}, u32[]{:S(2)}) collective-permute-start(bf16[32,2304]{1,0:T(8,128)(2,1)S(1)} %slice.266), channel_id=1, source_target_pairs={{0,16},{8,24},{16,0},{24,8},{1,17},{9,25},{17,1},{25,9},{2,18},{10... | collective-permute-start | bytes 442376 | tf_op jit(solution)/shard_map/ppermute | solution.py:401
  63.6 5.8 %collective-permute-done.19.arrived_ref = bf16[32,2304]{1,0:T(8,128)(2,1)S(1)} collective-permute-done((bf16[32,2304]{1,0:T(8,128)(2,1)S(1)}, bf16[32,2304]{1,0:T(8,128)(2,1)S(1)}, u32[]{:S(2)}, u32[]{:S(2)}) %collective-permute-start.19) | collective-permute-done | bytes 147488 | tf_op jit(solution)/shard_map/ppermute | solution.py:401
  69.4 1.2 %shard_map.146 = (f32[2,64,1024]{2,1,0:T(8,128)}, f32[32,2048]{1,0:T(8,128)}, f32[32,1024]{1,0:T(8,128)}, f32[32,100]{1,0:T(8,128)}) custom-call(f32[2,64,1024]{2,1,0:T(8,128)S(1)} %get-tuple-element.90.own_hidden_ref, bf16[128,1024]{1,0:T(8,128)(2,1)S(1)} %collective-permute-done.11.mate_ref, bf16[64,1024]{1,0:T(8,128)(2,1)S(1)} %collective-permute-done.18.other_ref, ...), custom_call_target="tpu_custom_call" | custom-call | flops 1 | bytes 1 | tf_op jit(solution)/shard_map/pallas_call | solution.py:28
  (34 shorter events, 0.3 us)
Async XLA Ops:
  0.6 4.9 %copy-start.3 = (bf16[1024,100]{0,1:T(8,128)(2,1)S(1)}, bf16[1024,100]{0,1:T(8,128)(2,1)}, u32[]{:S(2)}) copy-start(bf16[1024,100]{0,1:T(8,128)(2,1)} %param.15) | copy-start | bytes 614404
  0.6 4.9 %copy-start.8 = (f32[100]{0:T(128)S(1)}, f32[100]{0:T(128)}, u32[]{:S(2)}) copy-start(f32[100]{0:T(128)} %param.19) | copy-start | bytes 1204
  0.7 4.9 %copy-start.7 = (f32[256]{0:T(256)S(1)}, f32[256]{0:T(256)}, u32[]{:S(2)}) copy-start(f32[256]{0:T(256)} %param.18) | copy-start | bytes 3076
  0.7 4.9 %copy-start.2 = (bf16[256,1024]{1,0:T(8,128)(2,1)S(1)}, bf16[256,1024]{1,0:T(8,128)(2,1)}, u32[]{:S(2)}) copy-start(bf16[256,1024]{1,0:T(8,128)(2,1)} %q_ref.5) | copy-start | bytes 1572868
  0.7 4.9 %copy-start.1 = (bf16[1024,1024]{1,0:T(8,128)(2,1)S(1)}, bf16[1024,1024]{1,0:T(8,128)(2,1)}, u32[]{:S(2)}) copy-start(bf16[1024,1024]{1,0:T(8,128)(2,1)} %wo_ref.3) | copy-start | bytes 6291460
  0.7 4.9 %copy-start.5 = (f32[100,256]{1,0:T(8,128)S(1)}, f32[100,256]{1,0:T(8,128)}, u32[]{:S(2)}) copy-start(f32[100,256]{1,0:T(8,128)} %init_ref.1) | copy-start | bytes 307204
  0.7 4.9 %copy-start.6 = (s32[3,256]{1,0:T(4,128)S(1)}, s32[3,256]{1,0:T(4,128)}, u32[]{:S(2)}) copy-start(s32[3,256]{1,0:T(4,128)} %src_ref.3) | copy-start | bytes 9220
  0.7 4.9 %copy-start = (bf16[1024,2048]{1,0:T(8,128)(2,1)S(1)}, bf16[1024,2048]{1,0:T(8,128)(2,1)}, u32[]{:S(2)}) copy-start(bf16[1024,2048]{1,0:T(8,128)(2,1)} %kvw_ref.5) | copy-start | bytes 12582916
  2.1 6.6 %collective-permute-start = (bf16[64,1024]{1,0:T(8,128)(2,1)S(1)}, bf16[64,1024]{1,0:T(8,128)(2,1)S(1)}, u32[]{:S(2)}, u32[]{:S(2)}) collective-permute-start(bf16[64,1024]{1,0:T(8,128)(2,1)S(1)} %get-tuple-element.55), channel_id=1, source_target_pairs={{0,7},{1,2},{2,1},{3,4},{4,3},{5,6},{6,5},{7,0},{8,15},{9,10},{10,... | collective-permute-start | bytes 393224 | tf_op jit(solution)/shard_map/ppermute | solution.py:437
  5.5 3.2 %collective-permute-start.1 = (bf16[64,1024]{1,0:T(8,128)(2,1)S(1)}, bf16[64,1024]{1,0:T(8,128)(2,1)S(1)}, u32[]{:S(2)}, u32[]{:S(2)}) collective-permute-start(bf16[64,1024]{1,0:T(8,128)(2,1)S(1)} %get-tuple-element.56), channel_id=1, source_target_pairs={{0,1},{1,0},{2,3},{3,2},{4,5},{5,4},{6,7},{7,6},{8,9},{9,8},{10,11... | collective-permute-start | bytes 393224 | tf_op jit(solution)/shard_map/ppermute | solution.py:438
  8.7 14.1 %copy-start.4 = (f32[100,256]{1,0:T(8,128)S(1)}, f32[100,256]{1,0:T(8,128)}, u32[]{:S(2)}) copy-start(f32[100,256]{1,0:T(8,128)} %refs_5_.1) | copy-start | bytes 307204
  10.4 8.2 %collective-permute-start.2 = (bf16[200,256]{1,0:T(8,128)(2,1)S(1)}, bf16[200,256]{1,0:T(8,128)(2,1)S(1)}, u32[]{:S(2)}, u32[]{:S(2)}) collective-permute-start(bf16[200,256]{1,0:T(8,128)(2,1)S(1)} %get-tuple-element.61), channel_id=1, source_target_pairs={{0,24},{8,16},{16,8},{24,0},{1,25},{9,17},{17,9},{25,1},{2,26},{10... | collective-permute-start | bytes 307208 | tf_op jit(solution)/shard_map/ppermute | solution.py:475
  15.6 7.3 %collective-permute-start.3 = (bf16[200,256]{1,0:T(8,128)(2,1)S(1)}, bf16[200,256]{1,0:T(8,128)(2,1)S(1)}, u32[]{:S(2)}, u32[]{:S(2)}) collective-permute-start(bf16[200,256]{1,0:T(8,128)(2,1)S(1)} %get-tuple-element.61), channel_id=1, source_target_pairs={{0,16},{8,24},{16,0},{24,8},{1,17},{9,25},{17,1},{25,9},{2,18},{10... | collective-permute-start | bytes 307208 | tf_op jit(solution)/shard_map/ppermute | solution.py:475
  15.6 7.3 %collective-permute-start.4 = (bf16[200,256]{1,0:T(8,128)(2,1)S(1)}, bf16[200,256]{1,0:T(8,128)(2,1)S(1)}, u32[]{:S(2)}, u32[]{:S(2)}) collective-permute-start(bf16[200,256]{1,0:T(8,128)(2,1)S(1)} %get-tuple-element.61), channel_id=1, source_target_pairs={{0,8},{8,0},{16,24},{24,16},{1,9},{9,1},{17,25},{25,17},{2,10},{10... | collective-permute-start | bytes 307208 | tf_op jit(solution)/shard_map/ppermute | solution.py:475
  24.7 4.1 %collective-permute-start.5 = (bf16[512,768]{1,0:T(8,128)(2,1)S(1)}, bf16[512,768]{1,0:T(8,128)(2,1)S(1)}, u32[]{:S(2)}, u32[]{:S(2)}) collective-permute-start(bf16[512,768]{1,0:T(8,128)(2,1)S(1)} %get-tuple-element.76), channel_id=1, source_target_pairs={{0,1},{1,0},{2,3},{3,2},{4,5},{5,4},{6,7},{7,6},{8,9},{9,8},{10,11... | collective-permute-start | bytes 2359304 | tf_op jit(solution)/shard_map/ppermute | solution.py:401
  26.3 2.7 %collective-permute-start.6 = (bf16[512,768]{1,0:T(8,128)(2,1)S(1)}, bf16[512,768]{1,0:T(8,128)(2,1)S(1)}, u32[]{:S(2)}, u32[]{:S(2)}) collective-permute-start(bf16[512,768]{1,0:T(8,128)(2,1)S(1)} %get-tuple-element.78), channel_id=1, source_target_pairs={{0,1},{1,0},{2,3},{3,2},{4,5},{5,4},{6,7},{7,6},{8,9},{9,8},{10,11... | collective-permute-start | bytes 2359304 | tf_op jit(solution)/shard_map/ppermute | solution.py:401
  28.8 2.4 %collective-permute-start.7 = (bf16[512,768]{1,0:T(8,128)(2,1)S(1)}, bf16[512,768]{1,0:T(8,128)(2,1)S(1)}, u32[]{:S(2)}, u32[]{:S(2)}) collective-permute-start(bf16[512,768]{1,0:T(8,128)(2,1)S(1)} %get-tuple-element.84), channel_id=1, source_target_pairs={{0,1},{1,0},{2,3},{3,2},{4,5},{5,4},{6,7},{7,6},{8,9},{9,8},{10,11... | collective-permute-start | bytes 2359304 | tf_op jit(solution)/shard_map/ppermute | solution.py:401
  31.2 11.2 %collective-permute-start.10 = (bf16[256,768]{1,0:T(8,128)(2,1)S(1)}, bf16[256,768]{1,0:T(8,128)(2,1)S(1)}, u32[]{:S(2)}, u32[]{:S(2)}) collective-permute-start(bf16[256,768]{1,0:T(8,128)(2,1)S(1)} %add_convert_fusion), channel_id=1, source_target_pairs={{0,8},{8,0},{16,24},{24,16},{1,9},{9,1},{17,25},{25,17},{2,10},{10... | collective-permute-start | bytes 1179656 | tf_op jit(solution)/shard_map/ppermute | solution.py:401
  31.8 11.0 %collective-permute-start.8 = (bf16[256,768]{1,0:T(8,128)(2,1)S(1)}, bf16[256,768]{1,0:T(8,128)(2,1)S(1)}, u32[]{:S(2)}, u32[]{:S(2)}) collective-permute-start(bf16[256,768]{1,0:T(8,128)(2,1)S(1)} %add_convert_fusion.2), channel_id=1, source_target_pairs={{0,2},{1,3},{2,0},{3,1},{4,6},{5,7},{6,4},{7,5},{8,10},{9,11},{10,... | collective-permute-start | bytes 1179656 | tf_op jit(solution)/shard_map/ppermute | solution.py:401
  33.4 10.8 %collective-permute-start.9 = (bf16[256,768]{1,0:T(8,128)(2,1)S(1)}, bf16[256,768]{1,0:T(8,128)(2,1)S(1)}, u32[]{:S(2)}, u32[]{:S(2)}) collective-permute-start(bf16[256,768]{1,0:T(8,128)(2,1)S(1)} %add_convert_fusion.1), channel_id=1, source_target_pairs={{0,4},{1,5},{2,6},{3,7},{4,0},{5,1},{6,2},{7,3},{8,12},{9,13},{10,... | collective-permute-start | bytes 1179656 | tf_op jit(solution)/shard_map/ppermute | solution.py:401
  36.6 1.6 %collective-permute-start.11 = (bf16[128,1024]{1,0:T(8,128)(2,1)S(1)}, bf16[128,1024]{1,0:T(8,128)(2,1)S(1)}, u32[]{:S(2)}, u32[]{:S(2)}) collective-permute-start(bf16[128,1024]{1,0:T(8,128)(2,1)S(1)} %get-tuple-element.94), channel_id=1, source_target_pairs={{0,1},{1,0},{2,3},{3,2},{4,5},{5,4},{6,7},{7,6},{8,9},{9,8},{10,11... | collective-permute-start | bytes 786440 | tf_op jit(solution)/shard_map/ppermute | solution.py:533
  44.3 5.8 %collective-permute-start.16 = (bf16[128,768]{1,0:T(8,128)(2,1)S(1)}, bf16[128,768]{1,0:T(8,128)(2,1)S(1)}, u32[]{:S(2)}, u32[]{:S(2)}) collective-permute-start(bf16[128,768]{1,0:T(8,128)(2,1)S(1)} %add_convert_fusion.3), channel_id=1, source_target_pairs={{0,2},{1,3},{2,0},{3,1},{4,6},{5,7},{6,4},{7,5},{8,10},{9,11},{10,... | collective-permute-start | bytes 589832 | tf_op jit(solution)/shard_map/ppermute | solution.py:401
  45.2 9.8 %collective-permute-start.14 = (bf16[128,768]{1,0:T(8,128)(2,1)S(1)}, bf16[128,768]{1,0:T(8,128)(2,1)S(1)}, u32[]{:S(2)}, u32[]{:S(2)}) collective-permute-start(bf16[128,768]{1,0:T(8,128)(2,1)S(1)} %add_convert_fusion.4), channel_id=1, source_target_pairs={{0,8},{8,0},{16,24},{24,16},{1,9},{9,1},{17,25},{25,17},{2,10},{10... | collective-permute-start | bytes 589832 | tf_op jit(solution)/shard_map/ppermute | solution.py:401
  46.9 6.8 %collective-permute-start.12 = (bf16[128,768]{1,0:T(8,128)(2,1)S(1)}, bf16[128,768]{1,0:T(8,128)(2,1)S(1)}, u32[]{:S(2)}, u32[]{:S(2)}) collective-permute-start(bf16[128,768]{1,0:T(8,128)(2,1)S(1)} %add_convert_fusion.5), channel_id=1, source_target_pairs={{0,4},{1,5},{2,6},{3,7},{4,0},{5,1},{6,2},{7,3},{8,12},{9,13},{10,... | collective-permute-start | bytes 589832 | tf_op jit(solution)/shard_map/ppermute | solution.py:401
  50.2 7.4 %collective-permute-start.17 = (bf16[64,768]{1,0:T(8,128)(2,1)S(1)}, bf16[64,768]{1,0:T(8,128)(2,1)S(1)}, u32[]{:S(2)}, u32[]{:S(2)}) collective-permute-start(bf16[64,768]{1,0:T(8,128)(2,1)S(1)} %add_convert_fusion.6), channel_id=1, source_target_pairs={{0,4},{1,5},{2,6},{3,7},{4,0},{5,1},{6,2},{7,3},{8,12},{9,13},{10,... | collective-permute-start | bytes 294920 | tf_op jit(solution)/shard_map/ppermute | solution.py:401
  53.8 7.6 %collective-permute-start.18 = (bf16[64,1024]{1,0:T(8,128)(2,1)S(1)}, bf16[64,1024]{1,0:T(8,128)(2,1)S(1)}, u32[]{:S(2)}, u32[]{:S(2)}) collective-permute-start(bf16[64,1024]{1,0:T(8,128)(2,1)S(1)} %slice.185), channel_id=1, source_target_pairs={{0,2},{1,7},{2,4},{3,1},{4,6},{5,3},{6,0},{7,5},{8,10},{9,15},{10,... | collective-permute-start | bytes 393224 | tf_op jit(solution)/shard_map/ppermute | solution.py:530
  55.1 5.6 %collective-permute-start.15 = (bf16[64,768]{1,0:T(8,128)(2,1)S(1)}, bf16[64,768]{1,0:T(8,128)(2,1)S(1)}, u32[]{:S(2)}, u32[]{:S(2)}) collective-permute-start(bf16[64,768]{1,0:T(8,128)(2,1)S(1)} %add_convert_fusion.7), channel_id=1, source_target_pairs={{0,2},{1,3},{2,0},{3,1},{4,6},{5,7},{6,4},{7,5},{8,10},{9,11},{10,... | collective-permute-start | bytes 294920 | tf_op jit(solution)/shard_map/ppermute | solution.py:401
  56.8 4.6 %collective-permute-start.13 = (bf16[64,768]{1,0:T(8,128)(2,1)S(1)}, bf16[64,768]{1,0:T(8,128)(2,1)S(1)}, u32[]{:S(2)}, u32[]{:S(2)}) collective-permute-start(bf16[64,768]{1,0:T(8,128)(2,1)S(1)} %add_convert_fusion.8), channel_id=1, source_target_pairs={{0,8},{8,0},{16,24},{24,16},{1,9},{9,1},{17,25},{25,17},{2,10},{10... | collective-permute-start | bytes 294920 | tf_op jit(solution)/shard_map/ppermute | solution.py:401
  61.7 7.7 %collective-permute-start.19 = (bf16[32,2304]{1,0:T(8,128)(2,1)S(1)}, bf16[32,2304]{1,0:T(8,128)(2,1)S(1)}, u32[]{:S(2)}, u32[]{:S(2)}) collective-permute-start(bf16[32,2304]{1,0:T(8,128)(2,1)S(1)} %slice.266), channel_id=1, source_target_pairs={{0,16},{8,24},{16,0},{24,8},{1,17},{9,25},{17,1},{25,9},{2,18},{10... | collective-permute-start | bytes 442376 | tf_op jit(solution)/shard_map/ppermute | solution.py:401

commit v19 on v14

--- a/solution.py
+++ b/solution.py
@@ -484,24 +484,25 @@
 
     extra = 2 * LANES
     group_width = (2 * width + extra) // GROUPS
-    first_keys = 2 * group_width - width
-    group_shape = [sds((width // 2, group_width), BF)] * 2
+    widths = [group_width, group_width - LANES, group_width + LANES]
+    first_keys = widths[0] + widths[1] - width
+    group_shapes = [[sds((width // 2, w), BF)] * 2 for w in widths]
     grad, ng_value, send, keep = call(
         functools.partial(value_body, n_member, n_band),
         [sds((members, LANES, points), BF), sds((members * ext, width), BF)]
-        + group_shape,
+        + group_shapes[0],
         (*received, part, base, truth, weight, p, own_gates, halo_gates, ext_t),
     )
     groups = [[keep, swap(send, "band", 0, n_band)]]
     ng_first, send, keep = call(
         functools.partial(first_keys_body, n_member, n_band, group_width),
-        [sds((members * ext, first_keys), BF)] + group_shape,
+        [sds((members * ext, first_keys), BF)] + group_shapes[1],
         (grad, pt, own_value, halo_value, own_slopes, halo_slopes, queries, ext_t, ng_value),
     )
     groups.append([keep, swap(send, "band", 0, n_band)])
     ng_last, send, keep = call(
         functools.partial(last_keys_body, n_member, n_band),
-        [sds((members * ext, width - first_keys), BF)] + group_shape,
+        [sds((members * ext, width - first_keys), BF)] + group_shapes[2],
         (grad, pt, own_value, halo_value, own_slopes, halo_slopes, queries, merged, out_weight, ext_t),
         [pltpu.VMEM((width, extra), F32)],
     )

time: 68.7 us -> 69.8 us (1.016)
  transfers between devices with their start and end apart: 20 -> 20, of which waited for: 14 -> 10; matrix products, arithmetic and copies ran while one was open for 1% -> 1% of each run, Pallas kernels for 11% -> 11%
where the time goes in v19:
time: 69.8 us; the launch traced here: 69.6 us
  waiting for transfers between devices  28.9 us (41%)
  starting transfers between devices  24.7 us (35%)
  Pallas kernels  14.2 us (20%)
  other arithmetic  0.93 us (1%)
  between operations  0.91 us (1%)
    ppermute x13, waiting for transfers between devices, swap(): return lax.ppermute(rows, axis, [(i, i ^ 1 << bit) for i in range(count)])  15.2 us
    ppermute x13, starting transfers between devices, swap(): return lax.ppermute(rows, axis, [(i, i ^ 1 << bit) for i in range(count)])  14.7 us
    pallas_call x9, Pallas kernels, call(): pl.pallas_call(body, out_shape=out_shape, in_specs=[pl.BlockSpec(memory_s...  14.2 us
    ppermute x3, waiting for transfers between devices, shards(): lax.ppermute(sent, 'member', [(i, i ^ s) for i in range(n_member)])  6.35 us
    ppermute x3, starting transfers between devices, shards(): lax.ppermute(sent, 'member', [(i, i ^ s) for i in range(n_member)])  5.79 us
    ppermute x1, waiting for transfers between devices, shards(): from_other = lax.ppermute(onward, 'band', chips_on)  5.09 us
    ppermute x1, starting transfers between devices, shards(): other = lax.ppermute(for_other, 'band', others)  3.4 us
    ppermute x1, waiting for transfers between devices, shards(): from_mate = lax.ppermute(back, 'band', mates)  1.52 us
  transfers between devices with their start and end apart: 20, of which 10 were waited for; matrix products, arithmetic and copies ran while one was open for 1% of the time, Pallas kernels for 11%

profile of v19, /device:TPU:0, one launch (start us, length us, event | category | flops | bytes accessed | tf_op | source)
XLA Modules:
  0.0 69.6 jit_solution(806271261084374654)
XLA Ops:
  0.7 1.4 %shard_map.138 = (bf16[2,64,1024]{2,1,0:T(8,128)(2,1)S(1)}, s32[2,32]{1,0:T(2,128)S(1)}, bf16[64,1024]{1,0:T(8,128)(2,1)S(1)}, bf16[64,1024]{1,0:T(8,128)(2,1)S(1)}) custom-call(bf16[2,64,1024]{2,1,0:T(8,128)(2,1)} %hidden_hbm.1, s32[2,32]{1,0:T(2,128)} %halo_hbm.1), custom_call_target="tpu_custom_call" | custom-call | flops 10000000000 | bytes 1 | tf_op jit(solution)/shard_map/pallas_call | solution.py:28
  2.1 3.4 %collective-permute-start = (bf16[64,1024]{1,0:T(8,128)(2,1)S(1)}, bf16[64,1024]{1,0:T(8,128)(2,1)S(1)}, u32[]{:S(2)}, u32[]{:S(2)}) collective-permute-start(bf16[64,1024]{1,0:T(8,128)(2,1)S(1)} %get-tuple-element.53), channel_id=1, source_target_pairs={{0,7},{1,2},{2,1},{3,4},{4,3},{5,6},{6,5},{7,0},{8,15},{9,10},{10,... | collective-permute-start | bytes 393224 | tf_op jit(solution)/shard_map/ppermute | solution.py:437
  5.6 2.4 %shard_map.139 = (bf16[2,64,1024]{2,1,0:T(8,128)(2,1)S(1)}, bf16[8,2,128,256]{3,2,1,0:T(8,128)(2,1)S(1)}, bf16[8,2,128,256]{3,2,1,0:T(8,128)(2,1)S(1)}, f32[2,10...) custom-call(bf16[2,64,1024]{2,1,0:T(8,128)(2,1)S(1)} %get-tuple-elem, ...), custom_call_target="tpu_custom_call" | custom-call | flops 1 | bytes 1 | tf_op jit(solution)/shard_map/pallas_call | solution.py:28
  8.0 0.7 collective-permute-done.other_ref
  8.7 1.7 %shard_map.140 = (bf16[2,64,1024]{2,1,0:T(8,128)(2,1)S(1)}, bf16[8,2,128,256]{3,2,1,0:T(8,128)(2,1)S(1)}, bf16[8,2,128,256]{3,2,1,0:T(8,128)(2,1)S(1)}, bf16[2,1...) custom-call(bf16[64,1024]{1,0:T(8,128)(2,1)S(1)} %collective-permute-done.other_ref, ...), custom_call_target="tpu_custom_call" | custom-call | flops 1 | bytes 1 | tf_op jit(solution)/shard_map/pallas_call | solution.py:28
  10.5 5.1 %collective-permute-start.2 = (bf16[200,256]{1,0:T(8,128)(2,1)S(1)}, bf16[200,256]{1,0:T(8,128)(2,1)S(1)}, u32[]{:S(2)}, u32[]{:S(2)}) collective-permute-start(bf16[200,256]{1,0:T(8,128)(2,1)S(1)} %get-tuple-element.59), channel_id=1, source_target_pairs={{0,24},{8,16},{16,8},{24,0},{1,25},{9,17},{17,9},{25,1},{2,26},{10... | collective-permute-start | bytes 307208 | tf_op jit(solution)/shard_map/ppermute | solution.py:475
  15.6 0.6 collective-permute-start.4
  16.3 0.3 shard_map.141.refs_10_.ext_ref
  16.5 2.1 %collective-permute-done.2.refs_0_ = bf16[200,256]{1,0:T(8,128)(2,1)S(1)} collective-permute-done((bf16[200,256]{1,0:T(8,128)(2,1)S(1)}, bf16[200,256]{1,0:T(8,128)(2,1)S(1)}, u32[]{:S(2)}, u32[]{:S(2)}) %collective-permute-start.2) | collective-permute-done | bytes 102432 | tf_op jit(solution)/shard_map/ppermute | solution.py:475
  18.7 4.2 %collective-permute-done.3.refs_1_ = bf16[200,256]{1,0:T(8,128)(2,1)S(1)} collective-permute-done((bf16[200,256]{1,0:T(8,128)(2,1)S(1)}, bf16[200,256]{1,0:T(8,128)(2,1)S(1)}, u32[]{:S(2)}, u32[]{:S(2)}) %collective-permute-start.3) | collective-permute-done | bytes 102432 | tf_op jit(solution)/shard_map/ppermute | solution.py:475
  22.9 1.9 %shard_map.142 = (bf16[2,128,256]{2,1,0:T(8,128)(2,1)S(1)}, bf16[256,1024]{1,0:T(8,128)(2,1)S(1)}, bf16[512,768]{1,0:T(8,128)(2,1)S(1)}, bf16[512,768]{1,0:T(8,128)(2,1)S(1)}) custom-call(bf16[200,256]{1,0:T(8,128)(2,1)S(1)} %collective-permute-done.2.refs_0_, bf16[200,256]{1,0:T(8,128)(2,1)S(1)} %collective-permute-done.3.refs_1_, ...), custom_call_target="tpu_custom_call" | custom-call | flops 1 | bytes 1 | tf_op jit(solution)/shard_map/pallas_call | solution.py:28
  24.8 0.1 collective-permute-start.5
  24.8 2.4 %shard_map.144 = (bf16[256,640]{1,0:T(8,128)(2,1)S(1)}, bf16[512,896]{1,0:T(8,128)(2,1)S(1)}, bf16[512,896]{1,0:T(8,128)(2,1)S(1)}) custom-call(bf16[2,128,256]{2,1,0:T(8,128)(2,1)S(1)} %get-tuple-element.65.grad_ref, bf16[1024,128]{1,0:T(8,128)(2,1)S(1)} %get-tuple-element.66.pt_ref, bf16[2,64,1024]{2,1,0:T(8,128)(2,1)S(1)} %get-tuple-element.67.own_value_ref, ...), custom_call_target="tpu_custom_call" | custom-call | flops 1 | bytes 1 | tf_op jit(solution)/shard_map/pallas_call | solution.py:28
  27.3 0.6 collective-permute-start.7
  27.8 1.5 %shard_map.143 = (bf16[256,384]{1,0:T(8,128)(2,1)S(1)}, bf16[512,640]{1,0:T(8,128)(2,1)S(1)}, bf16[512,640]{1,0:T(8,128)(2,1)S(1)}) custom-call(bf16[2,128,256]{2,1,0:T(8,128)(2,1)S(1)} %get-tuple-element.65.grad_ref, bf16[1024,128]{1,0:T(8,128)(2,1)S(1)} %get-tuple-element.66.pt_ref, bf16[2,64,1024]{2,1,0:T(8,128)(2,1)S(1)} %get-tuple-element.67.own_value_ref, ...), custom_call_target="tpu_custom_call" | custom-call | flops 1 | bytes 1 | tf_op jit(solution)/shard_map/pallas_call | solution.py:28
  29.4 0.1 collective-permute-start.6
  29.5 0.1 add_convert_fusion.1
  29.6 2.0 %collective-permute-done.6 = bf16[512,640]{1,0:T(8,128)(2,1)S(1)} collective-permute-done((bf16[512,640]{1,0:T(8,128)(2,1)S(1)}, bf16[512,640]{1,0:T(8,128)(2,1)S(1)}, u32[]{:S(2)}, u32[]{:S(2)}) %collective-permute-start.6) | collective-permute-done | bytes 655392 | tf_op jit(solution)/shard_map/ppermute | solution.py:401
  31.5 0.1 add_convert_fusion.2
  31.6 0.1 add_convert_fusion
  31.7 0.5 collective-permute-start.10
  32.2 1.7 %collective-permute-start.8 = (bf16[256,768]{1,0:T(8,128)(2,1)S(1)}, bf16[256,768]{1,0:T(8,128)(2,1)S(1)}, u32[]{:S(2)}, u32[]{:S(2)}) collective-permute-start(bf16[256,768]{1,0:T(8,128)(2,1)S(1)} %add_convert_fusion.1), channel_id=1, source_target_pairs={{0,2},{1,3},{2,0},{3,1},{4,6},{5,7},{6,4},{7,5},{8,10},{9,11},{10,... | collective-permute-start | bytes 1179656 | tf_op jit(solution)/shard_map/ppermute | solution.py:401
  33.9 1.8 %collective-permute-start.9 = (bf16[256,640]{1,0:T(8,128)(2,1)S(1)}, bf16[256,640]{1,0:T(8,128)(2,1)S(1)}, u32[]{:S(2)}, u32[]{:S(2)}) collective-permute-start(bf16[256,640]{1,0:T(8,128)(2,1)S(1)} %add_convert_fusion.2), channel_id=1, source_target_pairs={{0,4},{1,5},{2,6},{3,7},{4,0},{5,1},{6,2},{7,3},{8,12},{9,13},{10,... | collective-permute-start | bytes 983048 | tf_op jit(solution)/shard_map/ppermute | solution.py:401
  35.8 1.3 %shard_map.145 = (f32[2,64,1024]{2,1,0:T(8,128)S(1)}, bf16[128,1024]{1,0:T(8,128)(2,1)S(1)}) custom-call(bf16[256,384]{1,0:T(8,128)(2,1)S(1)} %get-tuple-element.72.first_ref, bf16[256,640]{1,0:T(8,128)(2,1)S(1)} %get-tuple-element.87.last_ref, bf16[256,1024]{1,0:T(8,128)(2,1)S(1)} %get-tuple-element.71.ngv_ref, bf16[1024,2048]{1,0:T(8,128)(2,1)S(1)} %copy-done), custom_call_target="tpu_custom_call" | custom-call | flops 1 | bytes 1 | tf_op jit(solution)/shard_map/pallas_call | solution.py:28
  37.1 0.1 collective-permute-start.11
  37.1 1.5 %collective-permute-done.11.mate_ref = bf16[128,1024]{1,0:T(8,128)(2,1)S(1)} collective-permute-done((bf16[128,1024]{1,0:T(8,128)(2,1)S(1)}, bf16[128,1024]{1,0:T(8,128)(2,1)S(1)}, u32[]{:S(2)}, u32[]{:S(2)}) %collective-permute-start.11) | collective-permute-done | bytes 262176 | tf_op jit(solution)/shard_map/ppermute | solution.py:529
  38.7 4.7 %collective-permute-done.9 = bf16[256,640]{1,0:T(8,128)(2,1)S(1)} collective-permute-done((bf16[256,640]{1,0:T(8,128)(2,1)S(1)}, bf16[256,640]{1,0:T(8,128)(2,1)S(1)}, u32[]{:S(2)}, u32[]{:S(2)}) %collective-permute-start.9) | collective-permute-done | bytes 327712 | tf_op jit(solution)/shard_map/ppermute | solution.py:401
  43.4 1.0 %collective-permute-done.10 = bf16[256,896]{1,0:T(8,128)(2,1)S(1)} collective-permute-done((bf16[256,896]{1,0:T(8,128)(2,1)S(1)}, bf16[256,896]{1,0:T(8,128)(2,1)S(1)}, u32[]{:S(2)}, u32[]{:S(2)}) %collective-permute-start.10) | collective-permute-done | bytes 458784 | tf_op jit(solution)/shard_map/ppermute | solution.py:401
  44.4 0.1 add_convert_fusion.3
  44.5 2.0 %collective-permute-start.16 = (bf16[128,896]{1,0:T(8,128)(2,1)S(1)}, bf16[128,896]{1,0:T(8,128)(2,1)S(1)}, u32[]{:S(2)}, u32[]{:S(2)}) collective-permute-start(bf16[128,896]{1,0:T(8,128)(2,1)S(1)} %add_convert_fusion.3), channel_id=1, source_target_pairs={{0,2},{1,3},{2,0},{3,1},{4,6},{5,7},{6,4},{7,5},{8,10},{9,11},{10,... | collective-permute-start | bytes 688136 | tf_op jit(solution)/shard_map/ppermute | solution.py:401
  46.4 0.1 add_convert_fusion.4
  46.5 1.7 %collective-permute-start.12 = (bf16[128,768]{1,0:T(8,128)(2,1)S(1)}, bf16[128,768]{1,0:T(8,128)(2,1)S(1)}, u32[]{:S(2)}, u32[]{:S(2)}) collective-permute-start(bf16[128,768]{1,0:T(8,128)(2,1)S(1)} %add_convert_fusion.4), channel_id=1, source_target_pairs={{0,4},{1,5},{2,6},{3,7},{4,0},{5,1},{6,2},{7,3},{8,12},{9,13},{10,... | collective-permute-start | bytes 589832 | tf_op jit(solution)/shard_map/ppermute | solution.py:401
  48.2 0.1 add_convert_fusion.5
  48.3 0.5 collective-permute-start.14
  48.8 3.9 %collective-permute-done.12 = bf16[128,768]{1,0:T(8,128)(2,1)S(1)} collective-permute-done((bf16[128,768]{1,0:T(8,128)(2,1)S(1)}, bf16[128,768]{1,0:T(8,128)(2,1)S(1)}, u32[]{:S(2)}, u32[]{:S(2)}) %collective-permute-start.12) | collective-permute-done | bytes 196640 | tf_op jit(solution)/shard_map/ppermute | solution.py:401
  52.7 0.1 add_convert_fusion.7
  52.7 0.5 collective-permute-start.13
  53.2 0.1 add_convert_fusion.6
  53.3 1.4 %collective-permute-start.17 = (bf16[64,896]{1,0:T(8,128)(2,1)S(1)}, bf16[64,896]{1,0:T(8,128)(2,1)S(1)}, u32[]{:S(2)}, u32[]{:S(2)}) collective-permute-start(bf16[64,896]{1,0:T(8,128)(2,1)S(1)} %add_convert_fusion.6), channel_id=1, source_target_pairs={{0,4},{1,5},{2,6},{3,7},{4,0},{5,1},{6,2},{7,3},{8,12},{9,13},{10,... | collective-permute-start | bytes 344072 | tf_op jit(solution)/shard_map/ppermute | solution.py:401
  54.8 0.9 %collective-permute-start.15 = (bf16[64,640]{1,0:T(8,128)(2,1)S(1)}, bf16[64,640]{1,0:T(8,128)(2,1)S(1)}, u32[]{:S(2)}, u32[]{:S(2)}) collective-permute-start(bf16[64,640]{1,0:T(8,128)(2,1)S(1)} %add_convert_fusion.8), channel_id=1, source_target_pairs={{0,2},{1,3},{2,0},{3,1},{4,6},{5,7},{6,4},{7,5},{8,10},{9,11},{10,... | collective-permute-start | bytes 245768 | tf_op jit(solution)/shard_map/ppermute | solution.py:401
  55.7 3.6 %collective-permute-done.15 = bf16[64,640]{1,0:T(8,128)(2,1)S(1)} collective-permute-done((bf16[64,640]{1,0:T(8,128)(2,1)S(1)}, bf16[64,640]{1,0:T(8,128)(2,1)S(1)}, u32[]{:S(2)}, u32[]{:S(2)}) %collective-permute-start.15) | collective-permute-done | bytes 81952 | tf_op jit(solution)/shard_map/ppermute | solution.py:401
  59.3 0.1 convert_add_fusion.1
  59.3 0.1 convert_add_fusion.2
  59.4 0.1 convert_add_fusion
  59.6 3.0 %collective-permute-start.19 = (bf16[32,2304]{1,0:T(8,128)(2,1)S(1)}, bf16[32,2304]{1,0:T(8,128)(2,1)S(1)}, u32[]{:S(2)}, u32[]{:S(2)}) collective-permute-start(bf16[32,2304]{1,0:T(8,128)(2,1)S(1)} %slice.266), channel_id=1, source_target_pairs={{0,16},{8,24},{16,0},{24,8},{1,17},{9,25},{17,1},{25,9},{2,18},{10... | collective-permute-start | bytes 442376 | tf_op jit(solution)/shard_map/ppermute | solution.py:401
  62.6 0.8 %collective-permute-start.18 = (bf16[64,1024]{1,0:T(8,128)(2,1)S(1)}, bf16[64,1024]{1,0:T(8,128)(2,1)S(1)}, u32[]{:S(2)}, u32[]{:S(2)}) collective-permute-start(bf16[64,1024]{1,0:T(8,128)(2,1)S(1)} %slice.199), channel_id=1, source_target_pairs={{0,2},{1,7},{2,4},{3,1},{4,6},{5,3},{6,0},{7,5},{8,10},{9,15},{10,... | collective-permute-start | bytes 393224 | tf_op jit(solution)/shard_map/ppermute | solution.py:535
  63.3 5.1 %collective-permute-done.18.other_ref = bf16[64,1024]{1,0:T(8,128)(2,1)S(1)} collective-permute-done((bf16[64,1024]{1,0:T(8,128)(2,1)S(1)}, bf16[64,1024]{1,0:T(8,128)(2,1)S(1)}, u32[]{:S(2)}, u32[]{:S(2)}) %collective-permute-start.18) | collective-permute-done | bytes 131104 | tf_op jit(solution)/shard_map/ppermute | solution.py:535
  68.4 1.2 %shard_map.146 = (f32[2,64,1024]{2,1,0:T(8,128)}, f32[32,2048]{1,0:T(8,128)}, f32[32,1024]{1,0:T(8,128)}, f32[32,100]{1,0:T(8,128)}) custom-call(f32[2,64,1024]{2,1,0:T(8,128)S(1)} %get-tuple-element.88.own_hidden_ref, bf16[128,1024]{1,0:T(8,128)(2,1)S(1)} %collective-permute-done.11.mate_ref, bf16[64,1024]{1,0:T(8,128)(2,1)S(1)} %collective-permute-done.18.other_ref, ...), custom_call_target="tpu_custom_call" | custom-call | flops 1 | bytes 1 | tf_op jit(solution)/shard_map/pallas_call | solution.py:28
  (35 shorter events, 0.2 us)
Async XLA Ops:
  0.6 4.9 %copy-start.3 = (bf16[1024,100]{0,1:T(8,128)(2,1)S(1)}, bf16[1024,100]{0,1:T(8,128)(2,1)}, u32[]{:S(2)}) copy-start(bf16[1024,100]{0,1:T(8,128)(2,1)} %param.15) | copy-start | bytes 614404
  0.6 4.9 %copy-start.8 = (f32[100]{0:T(128)S(1)}, f32[100]{0:T(128)}, u32[]{:S(2)}) copy-start(f32[100]{0:T(128)} %param.19) | copy-start | bytes 1204
  0.7 4.9 %copy-start.7 = (f32[256]{0:T(256)S(1)}, f32[256]{0:T(256)}, u32[]{:S(2)}) copy-start(f32[256]{0:T(256)} %param.18) | copy-start | bytes 3076
  0.7 4.9 %copy-start.2 = (bf16[256,1024]{1,0:T(8,128)(2,1)S(1)}, bf16[256,1024]{1,0:T(8,128)(2,1)}, u32[]{:S(2)}) copy-start(bf16[256,1024]{1,0:T(8,128)(2,1)} %q_ref.5) | copy-start | bytes 1572868
  0.7 4.9 %copy-start.1 = (bf16[1024,1024]{1,0:T(8,128)(2,1)S(1)}, bf16[1024,1024]{1,0:T(8,128)(2,1)}, u32[]{:S(2)}) copy-start(bf16[1024,1024]{1,0:T(8,128)(2,1)} %wo_ref.3) | copy-start | bytes 6291460
  0.7 4.9 %copy-start.5 = (f32[100,256]{1,0:T(8,128)S(1)}, f32[100,256]{1,0:T(8,128)}, u32[]{:S(2)}) copy-start(f32[100,256]{1,0:T(8,128)} %init_ref.1) | copy-start | bytes 307204
  0.7 4.9 %copy-start.6 = (s32[3,256]{1,0:T(4,128)S(1)}, s32[3,256]{1,0:T(4,128)}, u32[]{:S(2)}) copy-start(s32[3,256]{1,0:T(4,128)} %src_ref.3) | copy-start | bytes 9220
  0.7 4.9 %copy-start = (bf16[1024,2048]{1,0:T(8,128)(2,1)S(1)}, bf16[1024,2048]{1,0:T(8,128)(2,1)}, u32[]{:S(2)}) copy-start(bf16[1024,2048]{1,0:T(8,128)(2,1)} %kvw_ref.5) | copy-start | bytes 12582916
  2.1 6.6 %collective-permute-start = (bf16[64,1024]{1,0:T(8,128)(2,1)S(1)}, bf16[64,1024]{1,0:T(8,128)(2,1)S(1)}, u32[]{:S(2)}, u32[]{:S(2)}) collective-permute-start(bf16[64,1024]{1,0:T(8,128)(2,1)S(1)} %get-tuple-element.53), channel_id=1, source_target_pairs={{0,7},{1,2},{2,1},{3,4},{4,3},{5,6},{6,5},{7,0},{8,15},{9,10},{10,... | collective-permute-start | bytes 393224 | tf_op jit(solution)/shard_map/ppermute | solution.py:437
  5.5 3.2 %collective-permute-start.1 = (bf16[64,1024]{1,0:T(8,128)(2,1)S(1)}, bf16[64,1024]{1,0:T(8,128)(2,1)S(1)}, u32[]{:S(2)}, u32[]{:S(2)}) collective-permute-start(bf16[64,1024]{1,0:T(8,128)(2,1)S(1)} %get-tuple-element.54), channel_id=1, source_target_pairs={{0,1},{1,0},{2,3},{3,2},{4,5},{5,4},{6,7},{7,6},{8,9},{9,8},{10,11... | collective-permute-start | bytes 393224 | tf_op jit(solution)/shard_map/ppermute | solution.py:438
  8.7 14.2 %copy-start.4 = (f32[100,256]{1,0:T(8,128)S(1)}, f32[100,256]{1,0:T(8,128)}, u32[]{:S(2)}) copy-start(f32[100,256]{1,0:T(8,128)} %refs_5_.1) | copy-start | bytes 307204
  10.5 8.2 %collective-permute-start.2 = (bf16[200,256]{1,0:T(8,128)(2,1)S(1)}, bf16[200,256]{1,0:T(8,128)(2,1)S(1)}, u32[]{:S(2)}, u32[]{:S(2)}) collective-permute-start(bf16[200,256]{1,0:T(8,128)(2,1)S(1)} %get-tuple-element.59), channel_id=1, source_target_pairs={{0,24},{8,16},{16,8},{24,0},{1,25},{9,17},{17,9},{25,1},{2,26},{10... | collective-permute-start | bytes 307208 | tf_op jit(solution)/shard_map/ppermute | solution.py:475
  15.6 7.3 %collective-permute-start.3 = (bf16[200,256]{1,0:T(8,128)(2,1)S(1)}, bf16[200,256]{1,0:T(8,128)(2,1)S(1)}, u32[]{:S(2)}, u32[]{:S(2)}) collective-permute-start(bf16[200,256]{1,0:T(8,128)(2,1)S(1)} %get-tuple-element.59), channel_id=1, source_target_pairs={{0,16},{8,24},{16,0},{24,8},{1,17},{9,25},{17,1},{25,9},{2,18},{10... | collective-permute-start | bytes 307208 | tf_op jit(solution)/shard_map/ppermute | solution.py:475
  15.6 7.3 %collective-permute-start.4 = (bf16[200,256]{1,0:T(8,128)(2,1)S(1)}, bf16[200,256]{1,0:T(8,128)(2,1)S(1)}, u32[]{:S(2)}, u32[]{:S(2)}) collective-permute-start(bf16[200,256]{1,0:T(8,128)(2,1)S(1)} %get-tuple-element.59), channel_id=1, source_target_pairs={{0,8},{8,0},{16,24},{24,16},{1,9},{9,1},{17,25},{25,17},{2,10},{10... | collective-permute-start | bytes 307208 | tf_op jit(solution)/shard_map/ppermute | solution.py:475
  24.8 4.7 %collective-permute-start.5 = (bf16[512,768]{1,0:T(8,128)(2,1)S(1)}, bf16[512,768]{1,0:T(8,128)(2,1)S(1)}, u32[]{:S(2)}, u32[]{:S(2)}) collective-permute-start(bf16[512,768]{1,0:T(8,128)(2,1)S(1)} %get-tuple-element.74), channel_id=1, source_target_pairs={{0,1},{1,0},{2,3},{3,2},{4,5},{5,4},{6,7},{7,6},{8,9},{9,8},{10,11... | collective-permute-start | bytes 2359304 | tf_op jit(solution)/shard_map/ppermute | solution.py:401
  27.3 4.4 %collective-permute-start.7 = (bf16[512,896]{1,0:T(8,128)(2,1)S(1)}, bf16[512,896]{1,0:T(8,128)(2,1)S(1)}, u32[]{:S(2)}, u32[]{:S(2)}) collective-permute-start(bf16[512,896]{1,0:T(8,128)(2,1)S(1)} %get-tuple-element.82), channel_id=1, source_target_pairs={{0,1},{1,0},{2,3},{3,2},{4,5},{5,4},{6,7},{7,6},{8,9},{9,8},{10,11... | collective-permute-start | bytes 2752520 | tf_op jit(solution)/shard_map/ppermute | solution.py:401
  29.4 2.2 %collective-permute-start.6 = (bf16[512,640]{1,0:T(8,128)(2,1)S(1)}, bf16[512,640]{1,0:T(8,128)(2,1)S(1)}, u32[]{:S(2)}, u32[]{:S(2)}) collective-permute-start(bf16[512,640]{1,0:T(8,128)(2,1)S(1)} %get-tuple-element.76), channel_id=1, source_target_pairs={{0,1},{1,0},{2,3},{3,2},{4,5},{5,4},{6,7},{7,6},{8,9},{9,8},{10,11... | collective-permute-start | bytes 1966088 | tf_op jit(solution)/shard_map/ppermute | solution.py:401
  31.7 12.6 %collective-permute-start.10 = (bf16[256,896]{1,0:T(8,128)(2,1)S(1)}, bf16[256,896]{1,0:T(8,128)(2,1)S(1)}, u32[]{:S(2)}, u32[]{:S(2)}) collective-permute-start(bf16[256,896]{1,0:T(8,128)(2,1)S(1)} %add_convert_fusion), channel_id=1, source_target_pairs={{0,8},{8,0},{16,24},{24,16},{1,9},{9,1},{17,25},{25,17},{2,10},{10... | collective-permute-start | bytes 1376264 | tf_op jit(solution)/shard_map/ppermute | solution.py:401
  32.2 11.1 %collective-permute-start.8 = (bf16[256,768]{1,0:T(8,128)(2,1)S(1)}, bf16[256,768]{1,0:T(8,128)(2,1)S(1)}, u32[]{:S(2)}, u32[]{:S(2)}) collective-permute-start(bf16[256,768]{1,0:T(8,128)(2,1)S(1)} %add_convert_fusion.1), channel_id=1, source_target_pairs={{0,2},{1,3},{2,0},{3,1},{4,6},{5,7},{6,4},{7,5},{8,10},{9,11},{10,... | collective-permute-start | bytes 1179656 | tf_op jit(solution)/shard_map/ppermute | solution.py:401
  33.9 9.4 %collective-permute-start.9 = (bf16[256,640]{1,0:T(8,128)(2,1)S(1)}, bf16[256,640]{1,0:T(8,128)(2,1)S(1)}, u32[]{:S(2)}, u32[]{:S(2)}) collective-permute-start(bf16[256,640]{1,0:T(8,128)(2,1)S(1)} %add_convert_fusion.2), channel_id=1, source_target_pairs={{0,4},{1,5},{2,6},{3,7},{4,0},{5,1},{6,2},{7,3},{8,12},{9,13},{10,... | collective-permute-start | bytes 983048 | tf_op jit(solution)/shard_map/ppermute | solution.py:401
  37.1 1.6 %collective-permute-start.11 = (bf16[128,1024]{1,0:T(8,128)(2,1)S(1)}, bf16[128,1024]{1,0:T(8,128)(2,1)S(1)}, u32[]{:S(2)}, u32[]{:S(2)}) collective-permute-start(bf16[128,1024]{1,0:T(8,128)(2,1)S(1)} %get-tuple-element.92), channel_id=1, source_target_pairs={{0,1},{1,0},{2,3},{3,2},{4,5},{5,4},{6,7},{7,6},{8,9},{9,8},{10,11... | collective-permute-start | bytes 786440 | tf_op jit(solution)/shard_map/ppermute | solution.py:529
  44.5 8.8 %collective-permute-start.16 = (bf16[128,896]{1,0:T(8,128)(2,1)S(1)}, bf16[128,896]{1,0:T(8,128)(2,1)S(1)}, u32[]{:S(2)}, u32[]{:S(2)}) collective-permute-start(bf16[128,896]{1,0:T(8,128)(2,1)S(1)} %add_convert_fusion.3), channel_id=1, source_target_pairs={{0,2},{1,3},{2,0},{3,1},{4,6},{5,7},{6,4},{7,5},{8,10},{9,11},{10,... | collective-permute-start | bytes 688136 | tf_op jit(solution)/shard_map/ppermute | solution.py:401
  46.5 6.1 %collective-permute-start.12 = (bf16[128,768]{1,0:T(8,128)(2,1)S(1)}, bf16[128,768]{1,0:T(8,128)(2,1)S(1)}, u32[]{:S(2)}, u32[]{:S(2)}) collective-permute-start(bf16[128,768]{1,0:T(8,128)(2,1)S(1)} %add_convert_fusion.4), channel_id=1, source_target_pairs={{0,4},{1,5},{2,6},{3,7},{4,0},{5,1},{6,2},{7,3},{8,12},{9,13},{10,... | collective-permute-start | bytes 589832 | tf_op jit(solution)/shard_map/ppermute | solution.py:401
  48.3 6.5 %collective-permute-start.14 = (bf16[128,640]{1,0:T(8,128)(2,1)S(1)}, bf16[128,640]{1,0:T(8,128)(2,1)S(1)}, u32[]{:S(2)}, u32[]{:S(2)}) collective-permute-start(bf16[128,640]{1,0:T(8,128)(2,1)S(1)} %add_convert_fusion.5), channel_id=1, source_target_pairs={{0,8},{8,0},{16,24},{24,16},{1,9},{9,1},{17,25},{25,17},{2,10},{10... | collective-permute-start | bytes 491528 | tf_op jit(solution)/shard_map/ppermute | solution.py:401
  52.7 6.6 %collective-permute-start.13 = (bf16[64,768]{1,0:T(8,128)(2,1)S(1)}, bf16[64,768]{1,0:T(8,128)(2,1)S(1)}, u32[]{:S(2)}, u32[]{:S(2)}) collective-permute-start(bf16[64,768]{1,0:T(8,128)(2,1)S(1)} %add_convert_fusion.7), channel_id=1, source_target_pairs={{0,8},{8,0},{16,24},{24,16},{1,9},{9,1},{17,25},{25,17},{2,10},{10... | collective-permute-start | bytes 294920 | tf_op jit(solution)/shard_map/ppermute | solution.py:401
  53.3 6.0 %collective-permute-start.17 = (bf16[64,896]{1,0:T(8,128)(2,1)S(1)}, bf16[64,896]{1,0:T(8,128)(2,1)S(1)}, u32[]{:S(2)}, u32[]{:S(2)}) collective-permute-start(bf16[64,896]{1,0:T(8,128)(2,1)S(1)} %add_convert_fusion.6), channel_id=1, source_target_pairs={{0,4},{1,5},{2,6},{3,7},{4,0},{5,1},{6,2},{7,3},{8,12},{9,13},{10,... | collective-permute-start | bytes 344072 | tf_op jit(solution)/shard_map/ppermute | solution.py:401
  54.8 4.5 %collective-permute-start.15 = (bf16[64,640]{1,0:T(8,128)(2,1)S(1)}, bf16[64,640]{1,0:T(8,128)(2,1)S(1)}, u32[]{:S(2)}, u32[]{:S(2)}) collective-permute-start(bf16[64,640]{1,0:T(8,128)(2,1)S(1)} %add_convert_fusion.8), channel_id=1, source_target_pairs={{0,2},{1,3},{2,0},{3,1},{4,6},{5,7},{6,4},{7,5},{8,10},{9,11},{10,... | collective-permute-start | bytes 245768 | tf_op jit(solution)/shard_map/ppermute | solution.py:401
  59.6 8.9 %collective-permute-start.19 = (bf16[32,2304]{1,0:T(8,128)(2,1)S(1)}, bf16[32,2304]{1,0:T(8,128)(2,1)S(1)}, u32[]{:S(2)}, u32[]{:S(2)}) collective-permute-start(bf16[32,2304]{1,0:T(8,128)(2,1)S(1)} %slice.266), channel_id=1, source_target_pairs={{0,16},{8,24},{16,0},{24,8},{1,17},{9,25},{17,1},{25,9},{2,18},{10... | collective-permute-start | bytes 442376 | tf_op jit(solution)/shard_map/ppermute | solution.py:401
  62.6 5.9 %collective-permute-start.18 = (bf16[64,1024]{1,0:T(8,128)(2,1)S(1)}, bf16[64,1024]{1,0:T(8,128)(2,1)S(1)}, u32[]{:S(2)}, u32[]{:S(2)}) collective-permute-start(bf16[64,1024]{1,0:T(8,128)(2,1)S(1)} %slice.199), channel_id=1, source_target_pairs={{0,2},{1,7},{2,4},{3,1},{4,6},{5,3},{6,0},{7,5},{8,10},{9,15},{10,... | collective-permute-start | bytes 393224 | tf_op jit(solution)/shard_map/ppermute | solution.py:535
